TPU v7x, 128 devices: a whole 4x4x4 slice. The times are simulated.
128 devices in a mesh: seq: 64 (over x, z, y_lo, core), head: 2 (over y_hi).
Axes of the slice: x: 4, y: 4 (y_hi: 2, y_lo: 2; y = y_hi * 2 + y_lo), z: 4, core: 2. Of those that a mesh axis runs over, the one named last changes fastest.
Arguments:
- dna_bases: int32 [1048576], P('seq'), may hold values from 0 to 3
- stem_weight: bfloat16 [256, 1536], replicated, may hold values from -1 to 1
- encoder_weight: bfloat16 [3, 1536, 1536], P(None, None, 'head'), may hold values from -0.09375 to 0.09375
- norm_gain: float32 [1536], replicated, may hold values from 0.25 to 1.75
- attention_weight: bfloat16 [3, 1536, 1536], P(None, None, 'head'), may hold values from -0.15625 to 0.15625
- logit_scale: float32 [8], P('head'), may hold values from 8 to 400
- out_weight: bfloat16 [1536, 1536], P('head'), may hold values from -1.25 to 1.25
- decoder_weight: bfloat16 [3, 1536, 1536], P(None, 'head'), may hold values from -0.09375 to 0.09375
- grad_out: bfloat16 [16384, 1536], P('seq'), may hold values from -6 to 6
Outputs:
- decoded: bfloat16 [16384, 1536], P('seq', 'head')
- bins_grad: bfloat16 [8192, 1536], P('seq', 'head')
Inputs may be any that keep to these rules, and one draw needn't show every extreme that they name: `dna_bases`: each entry names one of four bases.
All inputs are finite; a program needn't handle non-finite values.
Results may differ from a plain program's by a relative error of at most 0.034.
The roundings to bfloat16 on the way count: a program that leaves them out, or rounds other values in their place, can miss the bound.
Values may be sent and summed in bfloat16 or wider, within the bound.
No kernel may reach another device: no remote copies, remote signals or barrier semaphores. Data moves between devices by JAX's collectives and lax.ppermute only.
A program may use at most 192 MiB of HBM per device.

v0:
```python
import jax
import jax.numpy as jnp
from jax import lax
from jax.sharding import PartitionSpec as P


def extended(block, sides, width):
    for axis, dim in sides:
        count = lax.axis_size(axis)
        forward = [(i, i + 1) for i in range(count - 1)]
        backward = [(target, source) for source, target in forward]
        low = lax.ppermute(
            lax.slice_in_dim(block, block.shape[dim] - width, None, axis=dim), axis, forward
        )
        high = lax.ppermute(lax.slice_in_dim(block, 0, width, axis=dim), axis, backward)
        block = jnp.concatenate([low, block, high], axis=dim)
    return block


def embed_bases(dna_bases, stem_weight):
    patch_len = stem_weight.shape[0] // 4
    grouped = dna_bases.reshape(-1, patch_len)
    letters = jnp.arange(4, dtype=jnp.int32)
    onehot = (
        (grouped[:, :, None] == letters)
        .astype(jnp.bfloat16)
        .reshape(grouped.shape[0], 4 * patch_len)
    )
    return jnp.dot(onehot, stem_weight, preferred_element_type=jnp.float32).astype(jnp.bfloat16)


def conv_forward(padded, weight, rows_here):
    result = jnp.dot(padded[0:rows_here], weight[0], preferred_element_type=jnp.float32)
    for tap in range(1, weight.shape[0]):
        result = result + jnp.dot(
            padded[tap : tap + rows_here], weight[tap], preferred_element_type=jnp.float32
        )
    return result


def conv_backward(padded, weight, rows_here):
    margin = weight.shape[0] // 2
    result = None
    for tap in range(weight.shape[0]):
        begin = 2 * margin - tap
        term = lax.dot_general(
            padded[begin : begin + rows_here],
            weight[tap],
            (((1,), (1,)), ((), ())),
            preferred_element_type=jnp.float32,
        )
        result = term if result is None else result + term
    return result


def gelu_grad(pre_act, cotangent):
    return jax.vjp(jax.nn.gelu, pre_act)[1](cotangent)[0]


def head_scores(query_heads, factor, key_piece, heads_here, head_size):
    key_heads = key_piece.reshape(key_piece.shape[0], heads_here, head_size)
    key_inv = lax.rsqrt(jnp.mean(jnp.square(key_heads.astype(jnp.float32)), axis=2) + 1e-06)
    raw_dot = jnp.einsum("qhd,khd->hqk", query_heads, key_heads, preferred_element_type=jnp.float32)
    return raw_dot * factor.T[:, :, None] * key_inv.T[:, None, :]


def per_device(
    dna_bases,
    stem_weight,
    encoder_weight,
    norm_gain,
    attention_weight,
    logit_scale,
    out_weight,
    decoder_weight,
    grad_out,
):
    margin = encoder_weight.shape[0] // 2
    rows_here = grad_out.shape[0]
    features = stem_weight.shape[1]
    half_width = encoder_weight.shape[2]
    column = lax.axis_index("head") * half_width
    embedded = embed_bases(dna_bases, stem_weight)
    padded = extended(embedded, (("seq", 0),), margin)
    encoder_pre = conv_forward(padded, encoder_weight, rows_here)
    embed_half = lax.dynamic_slice_in_dim(embedded, column, half_width, 1)
    encoded_half = (embed_half.astype(jnp.float32) + jax.nn.gelu(encoder_pre)).astype(jnp.bfloat16)
    encoded = lax.all_gather(encoded_half, "head", axis=1, tiled=True)
    binned = jnp.mean(encoded.astype(jnp.float32).reshape(rows_here // 2, 2, features), axis=1)
    normed = (
        binned * lax.rsqrt(jnp.mean(jnp.square(binned), axis=1, keepdims=True) + 1e-06) * norm_gain
    ).astype(jnp.bfloat16)
    queries = jnp.dot(normed, attention_weight[0], preferred_element_type=jnp.float32).astype(
        jnp.bfloat16
    )
    keys = jnp.dot(normed, attention_weight[1], preferred_element_type=jnp.float32).astype(
        jnp.bfloat16
    )
    values = jnp.dot(normed, attention_weight[2], preferred_element_type=jnp.float32).astype(
        jnp.bfloat16
    )
    bin_rows = queries.shape[0]
    heads_here = logit_scale.shape[0]
    head_size = queries.shape[1] // heads_here
    query_heads = queries.reshape(bin_rows, heads_here, head_size)
    query_inv = lax.rsqrt(jnp.mean(jnp.square(query_heads.astype(jnp.float32)), axis=2) + 1e-06)
    factor = query_inv * (logit_scale / head_size)[None, :]
    keys_all, values_all = (
        lax.all_gather(keys, "seq", axis=0, tiled=True),
        lax.all_gather(values, "seq", axis=0, tiled=True),
    )
    scores = head_scores(query_heads, factor, keys_all, heads_here, head_size)
    row_max = jnp.max(scores, axis=2, keepdims=True)
    exps = jnp.exp(scores - row_max)
    row_sum = jnp.sum(exps, axis=2)
    value_heads = values_all.reshape(values_all.shape[0], heads_here, head_size)
    weighted = jnp.einsum(
        "hqk,khd->hqd", exps.astype(jnp.bfloat16), value_heads, preferred_element_type=jnp.float32
    )
    mixed_heads = (weighted / row_sum[:, :, None]).transpose(1, 0, 2)
    attended = mixed_heads.reshape(bin_rows, heads_here * head_size).astype(jnp.bfloat16)
    partial_proj = jnp.dot(attended, out_weight, preferred_element_type=jnp.float32)
    projected = lax.psum(partial_proj.astype(jnp.bfloat16), "head").astype(jnp.float32)
    block_out = (binned + projected).astype(jnp.bfloat16)
    decoder_in = (
        jnp.repeat(block_out, 2, axis=0).astype(jnp.float32) + encoded.astype(jnp.float32)
    ).astype(jnp.bfloat16)
    decoder_half = lax.dynamic_slice_in_dim(decoder_in, column, half_width, 1)
    decoder_pad = extended(decoder_half, (("seq", 0),), margin)
    partials = conv_forward(decoder_pad, decoder_weight, rows_here)
    cotangent = grad_out.astype(jnp.float32)
    cotangent_half = lax.dynamic_slice_in_dim(cotangent, column, half_width, 1)
    decoder_pre = lax.psum(partials.astype(jnp.bfloat16), "head").astype(jnp.float32)
    pre_half = lax.dynamic_slice_in_dim(decoder_pre, column, half_width, 1)
    decoded = (decoder_half.astype(jnp.float32) + jax.nn.gelu(pre_half)).astype(jnp.bfloat16)
    slope_grad = gelu_grad(decoder_pre, cotangent).astype(jnp.bfloat16)
    slope_pad = extended(slope_grad, (("seq", 0),), margin)
    input_grad = cotangent_half + conv_backward(slope_pad, decoder_weight, rows_here)
    bins_grad = jnp.sum(input_grad.reshape(rows_here // 2, 2, half_width), axis=1).astype(
        jnp.bfloat16
    )
    return (decoded, bins_grad)


def solution(mesh):
    in_specs = (
        P("seq"),
        P(),
        P(None, None, "head"),
        P(),
        P(None, None, "head"),
        P("head"),
        P("head", None),
        P(None, "head", None),
        P("seq", None),
    )
    out_specs = (P("seq", "head"), P("seq", "head"))
    return jax.shard_map(
        per_device, mesh=mesh, in_specs=in_specs, out_specs=out_specs, check_vma=False
    )
```

profile of v0, /device:TPU:0, one launch (start us, length us, event | category | flops | bytes accessed | tf_op | source)
XLA Modules:
  0.0 439.7 jit_solution(14010668326207469725)
XLA Ops:
  7.2 0.0 all-gather.3.cloned.1.call-start
  7.2 1.1 eq.22
  8.3 0.1 copy.14
  8.4 0.1 eq.24
  8.6 0.1 eq.26
  8.7 1.6 convolution_convert_fusion
  10.3 1.3 collective-permute-start.1
  11.6 3.0 collective-permute-start
  14.6 3.3 fusion.29
  18.0 2.5 fusion.27
  20.5 2.7 fusion.97
  23.2 13.9 %all_gather.9 = bf16[256,1536]{1,0:T(8,128)(2,1)S(1)} all-gather(bf16[256,768]{1,0:T(8,128)(2,1)S(1)} %fusion.97), channel_id=1, replica_groups=mesh['seq'=64,'head'=2] {'head'}, dimensions={1}, use_global_device_ids=true | all-gather | bytes 1179648 | tf_op jit(solution)/shard_map/all_gather | solution.py:88
  37.0 0.9 copy-done.2
  37.9 2.1 reshape.41
  40.1 3.3 reduce_sum.54
  43.3 0.2 multiply_reduce_fusion.1
  43.5 0.1 multiply_convert_fusion
  43.7 2.8 fusion.73
  46.5 0.0 all-gather.3.cloned.1.call-update
  46.5 0.0 all-gather.5.cloned.1.call-start
  46.6 2.8 fusion.76
  49.4 0.0 all-gather.5.cloned.1.call-update
  49.4 0.2 all-reduce.3.cloned.1.call-start
  49.7 2.8 fusion.70
  52.5 1.1 copy.15
  53.6 0.1 multiply_reduce_fusion.2
  53.7 0.1 multiply_bitcast_fusion
  53.7 114.2 %all-gather.3.cloned.1.call-done = bf16[8192,768]{1,0:T(8,128)(2,1)} async-done(((bf16[128,768]{1,0:T(8,128)(2,1)}), bf16[8192,768]{1,0:T(8,128)(2,1)}) %all-gather.3.cloned.1.call-update) | async-done | bytes 12582928 | tf_op jit(solution)/shard_map/all_gather | solution.py:109
  168.0 15.7 %copy.16 = bf16[8192,768]{0,1:T(8,128)(2,1)} copy(bf16[8192,768]{1,0:T(8,128)(2,1)} %all-gather.3.cloned.1.call-done) | data formatting | bytes 25165824 | tf_op jit(solution)/shard_map/all_gather | solution.py:109
  183.7 7.4 %multiply_reduce_fusion = f32[8192,4]{0,1:T(4,128)S(1)} fusion(bf16[8192,4,192]{0,2,1:T(8,128)(2,1)} %bitcast.84), kind=kLoop, calls=%fused_computation | loop fusion | flops 18841600 | bytes 12713984 | tf_op jit(solution)/shard_map/reduce_sum | solution.py:62
  191.1 0.1 rsqrt_bitcast_fusion
  191.2 6.5 %fusion = (f32[4,128]{1,0:T(4,128)S(1)}, f32[4,128,8192]{2,1,0:T(8,128)S(1)}) fusion(f32[4,8192]{1,0:T(4,128)S(1)} %rsqrt_bitcast_fusion, f32[4,128]{1,0:T(4,128)S(1)} %multiply_bitcast_fusion, bf16[128,4,192]{0,2,1:T(8,128)(2,1)S(1)} %bitcast.88, bf16[8192,4,192]{0,2,1:T(8,128)(2,1)} %bitcast.85), kind=kOutput, calls=%fused_computation.3 | convolution fusion | flops 1623195136 | bytes 29691904 | tf_op jit(solution)/shard_map/qhd,khd->hqk/dot_general | solution.py:63
  197.6 5.7 %copy-done.1 = f32[4,128,8192]{2,1,0:T(8,128)} copy-done((f32[4,128,8192]{2,1,0:T(8,128)}, f32[4,128,8192]{2,1,0:T(8,128)S(1)}, u32[]{:S(2)}) %copy-start.1) | copy-done | bytes 16777240
  203.4 4.1 fusion.1
  207.5 80.1 %all-gather.5.cloned.1.call-done = bf16[8192,768]{1,0:T(8,128)(2,1)} async-done(((bf16[128,768]{1,0:T(8,128)(2,1)}), bf16[8192,768]{1,0:T(8,128)(2,1)}) %all-gather.5.cloned.1.call-update) | async-done | bytes 12582928 | tf_op jit(solution)/shard_map/all_gather | solution.py:110
  287.6 15.6 %copy.17 = bf16[8192,768]{0,1:T(8,128)(2,1)} copy(bf16[8192,768]{1,0:T(8,128)(2,1)} %all-gather.5.cloned.1.call-done) | data formatting | bytes 25165824 | tf_op jit(solution)/shard_map/all_gather | solution.py:110
  303.2 11.4 %fusion.82 = bf16[128,4,192]{0,2,1:T(8,128)(2,1)S(1)} fusion(bf16[8192,4,192]{0,2,1:T(8,128)(2,1)} %bitcast.86, f32[4,128,8192]{2,1,0:T(8,128)} %copy-done.1, f32[4,128]{1,0:T(4,128)S(1)} %get-tuple-element.8, f32[4,8192]{1,0:T(4,128)S(1)} %rsqrt_bitcast_fusion, f32[4,128]{1,0:T(4,128)S(1)} %multiply_bitcast_fusion, f32[128,4]{0,1:T(4,128)S(1)} %bitcast.90), kind=kOutput, calls=%fused_computation.71 | convolution fusion | flops 1627586560 | bytes 29693952 | tf_op jit(solution)/shard_map/hqk,khd->hqd/dot_general | solution.py:117
  314.7 1.2 convolution_convert_fusion.1
  315.9 0.0 all-reduce.3.cloned.1.call-update
  315.9 0.0 all-reduce.5.cloned.1.call-start
  316.0 2.5 convert_element_type.84
  318.5 30.4 %all-reduce.3.cloned.1.call-done = bf16[128,1536]{1,0:T(8,128)(2,1)} async-done(((bf16[128,1536]{1,0:T(8,128)(2,1)}), bf16[128,1536]{1,0:T(8,128)(2,1)}) %all-reduce.3.cloned.1.call-update) | async-done | bytes 393232 | tf_op jit(solution)/shard_map/psum | solution.py:123
  348.9 1.1 fusion.114
  350.0 1.7 broadcast_in_dim.2
  351.7 3.2 convert_element_type.98
  354.8 1.4 fusion.111
  356.3 1.3 collective-permute-start.3
  357.6 2.4 fusion.16
  360.0 3.3 collective-permute-start.2
  363.3 2.4 fusion.12
  365.8 3.4 fusion.9
  369.2 0.0 all-reduce.5.cloned.1.call-update
  369.2 1.3 convert_element_type.104
  370.6 44.1 %all-reduce.5.cloned.1.call-done = bf16[256,1536]{1,0:T(8,128)(2,1)} async-done(((bf16[256,1536]{1,0:T(8,128)(2,1)}), bf16[256,1536]{1,0:T(8,128)(2,1)}) %all-reduce.5.cloned.1.call-update) | async-done | bytes 786448 | tf_op jit(solution)/shard_map/psum | solution.py:133
  414.7 2.3 fusion.51
  417.0 2.5 fusion.14
  419.6 1.7 collective-permute-start.5
  421.3 1.3 collective-permute-start.4
  422.6 0.2 convert_element_type.102
  422.8 1.0 fusion.108
  423.9 2.6 fusion.10
  426.5 3.4 fusion.64
  429.9 1.6 reshape.45
  431.5 1.7 reduce_sum.59
  (29 shorter events, 0.2 us)
Async XLA Ops:
  7.2 307.5 %copy-start = (bf16[768,1536]{1,0:T(8,128)(2,1)S(1)}, bf16[768,1536]{1,0:T(8,128)(2,1)}, u32[]{:S(2)}) copy-start(bf16[768,1536]{1,0:T(8,128)(2,1)} %param.15) | copy-start | bytes 7077892
  7.2 160.8 %all-gather.3.cloned.1.call-start = ((), (), s32[]{:S(2)}) async-start(), calls=%async_computation | async-start | bytes 12779520 | tf_op jit(solution)/shard_map/all_gather | solution.py:109
  10.3 7.7 %collective-permute-start.1 = (bf16[1,1536]{1,0:T(2,128)(2,1)S(1)}, bf16[1,1536]{1,0:T(2,128)(2,1)S(1)}, u32[]{:S(2)}, u32[]{:S(2)}) collective-permute-start(bf16[1,1536]{1,0:T(2,128)(2,1)S(1)} %get-tuple-element.5), channel_id=1, source_target_pairs={{2,0},{4,2},{6,4},{8,6},{10,8},{12,10},{14,12},{16,14},{18,16},{20... | collective-permute-start | bytes 9224 | tf_op jit(solution)/shard_map/ppermute | solution.py:15
  11.6 8.9 %collective-permute-start = (bf16[1,1536]{1,0:T(2,128)(2,1)S(1)}, bf16[1,1536]{1,0:T(2,128)(2,1)S(1)}, u32[]{:S(2)}, u32[]{:S(2)}) collective-permute-start(bf16[1,1536]{1,0:T(2,128)(2,1)S(1)} %get-tuple-element.4), channel_id=1, source_target_pairs={{0,2},{2,4},{4,6},{6,8},{8,10},{10,12},{12,14},{14,16},{16,18},{18... | collective-permute-start | bytes 9224 | tf_op jit(solution)/shard_map/ppermute | solution.py:12
  18.0 2.5 copy-start.8
  37.0 0.9 copy-start.2
  37.9 5.6 %copy-start.6 = (f32[1536]{0:T(1024)S(1)}, f32[1536]{0:T(1024)}, u32[]{:S(2)}) copy-start(f32[1536]{0:T(1024)} %param.12) | copy-start | bytes 18436
  46.5 3.2 copy-start.7
  46.5 241.1 %all-gather.5.cloned.1.call-start = ((), (), s32[]{:S(2)}) async-start(), calls=%async_computation.1 | async-start | bytes 12779520 | tf_op jit(solution)/shard_map/all_gather | solution.py:110
  49.4 299.5 %all-reduce.3.cloned.1.call-start = ((), (), s32[]{:S(2)}) async-start(), calls=%async_computation.2 | async-start | bytes 786432 | tf_op jit(solution)/shard_map/psum | solution.py:123
  197.6 5.7 %copy-start.1 = (f32[4,128,8192]{2,1,0:T(8,128)}, f32[4,128,8192]{2,1,0:T(8,128)S(1)}, u32[]{:S(2)}) copy-start(f32[4,128,8192]{2,1,0:T(8,128)S(1)} %get-tuple-element.9) | copy-start | bytes 50331652
  315.9 98.8 %all-reduce.5.cloned.1.call-start = ((), (), s32[]{:S(2)}) async-start(), calls=%async_computation.3 | async-start | bytes 1572864 | tf_op jit(solution)/shard_map/psum | solution.py:133
  356.3 7.0 %collective-permute-start.3 = (bf16[1,768]{1,0:T(2,128)(2,1)S(1)}, bf16[1,768]{1,0:T(2,128)(2,1)S(1)}, u32[]{:S(2)}, u32[]{:S(2)}) collective-permute-start(bf16[1,768]{1,0:T(2,128)(2,1)S(1)} %get-tuple-element.7), channel_id=1, source_target_pairs={{2,0},{4,2},{6,4},{8,6},{10,8},{12,10},{14,12},{16,14},{18,16},{20... | collective-permute-start | bytes 4616 | tf_op jit(solution)/shard_map/ppermute | solution.py:15
  360.0 5.7 %collective-permute-start.2 = (bf16[1,768]{1,0:T(2,128)(2,1)S(1)}, bf16[1,768]{1,0:T(2,128)(2,1)S(1)}, u32[]{:S(2)}, u32[]{:S(2)}) collective-permute-start(bf16[1,768]{1,0:T(2,128)(2,1)S(1)} %get-tuple-element.6), channel_id=1, source_target_pairs={{0,2},{2,4},{4,6},{6,8},{8,10},{10,12},{12,14},{14,16},{16,18},{18... | collective-permute-start | bytes 4616 | tf_op jit(solution)/shard_map/ppermute | solution.py:12
  365.7 3.5 copy-start.3
  417.0 5.6 %copy-start.4 = (bf16[256,1536]{1,0:T(8,128)(2,1)S(1)}, bf16[256,1536]{1,0:T(8,128)(2,1)}, u32[]{:S(2)}) copy-start(bf16[256,1536]{1,0:T(8,128)(2,1)} %all-reduce.5.cloned.1.call-done) | copy-start | bytes 2359300
  419.6 4.3 collective-permute-start.5
  421.3 5.2 %collective-permute-start.4 = (bf16[1,1536]{1,0:T(2,128)(2,1)S(1)}, bf16[1,1536]{1,0:T(2,128)(2,1)S(1)}, u32[]{:S(2)}, u32[]{:S(2)}) collective-permute-start(bf16[1,1536]{1,0:T(2,128)(2,1)S(1)} %get-tuple-element.2), channel_id=1, source_target_pairs={{2,0},{4,2},{6,4},{8,6},{10,8},{12,10},{14,12},{16,14},{18,16},{20... | collective-permute-start | bytes 9224 | tf_op jit(solution)/shard_map/ppermute | solution.py:15
  423.9 2.6 copy-start.5
Sparse Core Ops, SparseCore 0:
  46.6 121.2 all-gather.2
  170.2 117.3 all-gather.4
  316.1 32.7 all-reduce.2
  369.3 45.3 all-reduce.4
where the time goes:
time: 447 us; the launch traced here: 440 us
  waiting for transfers between devices  269 us (60%)
  matrix products  54.6 us (12%)
  local copies, waits for them, and re-layouts  49.1 us (11%)
  other arithmetic  26.8 us (6%)
  between operations  14.1 us (3%)
  blocking collectives  13.9 us (3%)
  starting transfers between devices  12.2 us (3%)
    all_gather x1, waiting for transfers between devices, per_device(): lax.all_gather(keys, 'seq', axis=0, tiled=True)  114 us
    all_gather x1, waiting for transfers between devices, per_device(): lax.all_gather(values, 'seq', axis=0, tiled=True)  80.1 us
    psum x1, waiting for transfers between devices, per_device(): lax.psum(partials.astype(jnp.bfloat16), 'head').astype(jnp.float32)  44.1 us
    psum x1, waiting for transfers between devices, per_device(): lax.psum(partial_proj.astype(jnp.bfloat16), 'head').astype(jnp.float32)  30.4 us
    all_gather x1, local copies, waits for them, and re-layouts, per_device(): lax.all_gather(keys, 'seq', axis=0, tiled=True)  15.7 us
    all_gather x1, local copies, waits for them, and re-layouts, per_device(): lax.all_gather(values, 'seq', axis=0, tiled=True)  15.6 us
    all_gather x1, blocking collectives, per_device(): encoded = lax.all_gather(encoded_half, 'head', axis=1, tiled=True)  13.9 us
    dot_general x1, matrix products, per_device(): jnp.einsum('hqk,khd->hqd', exps.astype(jnp.bfloat16), value_heads, prefer...  11.4 us
  transfers between devices with their start and end apart: 10, of which 4 were waited for; matrix products, arithmetic and copies ran while one was open for 13% of the time, Pallas kernels for 0%

commit v1 on v0

v1 whole, which is shorter than its diff:
```python
import functools

import jax
import jax.numpy as jnp
from jax import lax
from jax.experimental import pallas as pl
from jax.experimental.pallas import tpu as pltpu
from jax.sharding import PartitionSpec as P

BF16 = jnp.bfloat16
F32 = jnp.float32
ROWS = 136
OWN = 128
TILE = 256
HEAD = 192
EPS = 1e-06
VMEM = 56 * 1024 * 1024


def params():
    return pltpu.CompilerParams(vmem_limit_bytes=VMEM)


def dot(a, b):
    return jnp.dot(a, b, preferred_element_type=F32)


def dot_t(a, b):
    return lax.dot_general(a, b, (((1,), (1,)), ((), ())), preferred_element_type=F32)


def cost(flops, nbytes):
    return pl.CostEstimate(flops=int(flops), bytes_accessed=int(nbytes), transcendentals=0)


def shape(dims, dtype):
    return jax.ShapeDtypeStruct(dims, dtype)


def whole(dims):
    return pl.BlockSpec(dims, lambda *_: (0,) * len(dims))


def above(rows):
    return pltpu.roll(rows, 1, 0)


def below(rows):
    return pltpu.roll(rows, ROWS - 1, 0)


def gelu_parts(x):
    inner = 0.7978845608028654 * (x + 0.044715 * (x * x * x))
    return inner, jnp.tanh(inner)


def conv_taps(rows, weight):
    first, mid, last = (dot(rows, weight(t)) for t in range(3))
    even = above(first[ROWS:]) + mid[:ROWS] + last[ROWS:]
    odd = first[:ROWS] + mid[ROWS:] + below(last[:ROWS])
    return even, odd


def encoder_kernel(ids, codes, stem, weight, encoded, squares, embedded):
    step = pl.program_id(0)

    @pl.when(step == 0)
    def _():
        patch = stem.shape[0] // 4
        row = lax.broadcasted_iota(jnp.int32, (2 * patch, 4 * patch), 0)
        col = lax.broadcasted_iota(jnp.int32, (2 * patch, 4 * patch), 1)
        code = codes[...]
        spread = [
            dot(code, (row == col // 4 + offset).astype(F32).astype(BF16))
            for offset in (0, patch)
        ]
        spread = jnp.concatenate(spread, axis=0)
        base = lax.broadcasted_iota(jnp.int32, spread.shape, 1) % 4 + 1
        onehot = (spread == base.astype(F32)).astype(F32).astype(BF16)
        embedded[...] = dot(onehot, stem[...]).astype(BF16)
        squares[...] = jnp.zeros_like(squares)

    even, odd = conv_taps(embedded[...], lambda t: weight[t])
    column = ids[0] * (3 * TILE) + step * TILE
    mine = embedded[:, pl.ds(pl.multiple_of(column, TILE), TILE)].astype(F32)
    pre = jnp.concatenate([even, odd], axis=0)
    _, tanh = gelu_parts(pre)
    out = (mine + 0.5 * pre * (1.0 + tanh)).astype(BF16)
    encoded[...] = out
    out = out.astype(F32)
    binned = (out[:ROWS] + out[ROWS:]) * 0.5
    squares[...] += jnp.broadcast_to(
        jnp.sum(binned * binned, axis=1, keepdims=True), squares.shape
    )


def encode(ids, codes, stem, weight):
    half = weight.shape[2]
    feats = stem.shape[1]
    return pl.pallas_call(
        encoder_kernel,
        grid_spec=pltpu.PrefetchScalarGridSpec(
            num_scalar_prefetch=1,
            grid=(half // TILE,),
            in_specs=[
                whole(codes.shape),
                whole(stem.shape),
                pl.BlockSpec((3, feats, TILE), lambda i, ids: (0, 0, i)),
            ],
            out_specs=[
                pl.BlockSpec((2 * ROWS, TILE), lambda i, ids: (0, i)),
                whole((ROWS, 128)),
            ],
            scratch_shapes=[pltpu.VMEM((2 * ROWS, feats), BF16)],
        ),
        out_shape=[shape((2 * ROWS, half), BF16), shape((ROWS, 128), F32)],
        compiler_params=params(),
        cost_estimate=cost(2 * 2 * ROWS * 3 * feats * half, weight.size * 2),
        name="encode",
    )(ids, codes, stem, weight)


def norm_kernel(ids, encoded, mine, theirs, gain, out):
    enc = encoded[...].astype(F32)
    binned = (enc[:ROWS] + enc[ROWS:]) * 0.5
    mean = (mine[:, 0:1] + theirs[:, 0:1]) * (1.0 / (2 * encoded.shape[1]))
    out[...] = (binned * lax.rsqrt(mean + EPS) * gain[...]).astype(BF16)


def normalize(ids, encoded, mine, theirs, gain):
    half = encoded.shape[1]
    return pl.pallas_call(
        norm_kernel,
        grid_spec=pltpu.PrefetchScalarGridSpec(
            num_scalar_prefetch=1,
            grid=(1,),
            in_specs=[
                whole(encoded.shape),
                whole(mine.shape),
                whole(theirs.shape),
                pl.BlockSpec((1, half), lambda i, ids: (0, ids[0])),
            ],
            out_specs=whole((ROWS, half)),
        ),
        out_shape=shape((ROWS, half), BF16),
        compiler_params=params(),
        cost_estimate=cost(8 * ROWS * half, encoded.size * 2),
        name="normalize",
    )(ids, encoded, mine, theirs, gain)


def project_kernel(ids, mine, theirs, weight, queries, keyvals):
    half = mine.shape[1]
    near = pl.ds(pl.multiple_of(ids[0] * half, half), half)
    far = pl.ds(pl.multiple_of((1 - ids[0]) * half, half), half)
    rows = []
    for kind in range(3):
        both = dot(mine[...], weight[kind, near, :]) + dot(theirs[...], weight[kind, far, :])
        both = both.astype(BF16).astype(F32)
        rows.append((both, pltpu.roll(both, 2 * HEAD - 64, 1)))
    low = lax.broadcasted_iota(jnp.int32, (ROWS, 128), 1) < 64
    for head in range(2):
        query, key, value = (
            (r[0][:, :128], r[0][:, 128:256]) if head == 0 else (r[1][:, 128:256], r[1][:, 256:384])
            for r in rows
        )
        queries[head, :, :128] = query[0].astype(BF16)
        queries[head, :, 128:] = jnp.where(low, query[1], 0.0).astype(BF16)
        keyvals[head, :, :128] = key[0][:OWN].astype(BF16)
        keyvals[head, :, 128:256] = value[0][:OWN].astype(BF16)
        tail = jnp.where(low, key[1], pltpu.roll(value[1], 64, 1))
        keyvals[head, :, 256:] = tail[:OWN].astype(BF16)


def project(ids, mine, theirs, weight):
    feats = weight.shape[1]
    return pl.pallas_call(
        project_kernel,
        grid_spec=pltpu.PrefetchScalarGridSpec(
            num_scalar_prefetch=1,
            grid=(2,),
            in_specs=[
                whole(mine.shape),
                whole(theirs.shape),
                pl.BlockSpec((3, feats, 2 * HEAD), lambda i, ids: (0, 0, i)),
            ],
            out_specs=[
                pl.BlockSpec((2, ROWS, 256), lambda i, ids: (i, 0, 0)),
                pl.BlockSpec((2, OWN, 384), lambda i, ids: (i, 0, 0)),
            ],
        ),
        out_shape=[shape((4, ROWS, 256), BF16), shape((4, OWN, 384), BF16)],
        compiler_params=params(),
        cost_estimate=cost(2 * ROWS * weight.size, weight.size * 2),
        name="project",
    )(ids, mine, theirs, weight)


def attend_kernel(scale, q0, q1, q2, q3, k0, k1, k2, k3, o0, o1, o2, o3, inverse):
    chunk = k0.shape[0]
    lane = lax.broadcasted_iota(jnp.int32, (8, 256), 1)
    ones = (lane < HEAD).astype(F32).astype(BF16)
    pieces = (k0, k1, k2, k3)

    def keys(ref):
        return jnp.concatenate([ref[:, :128], ref[:, 256:]], axis=1)

    @pl.when(pl.program_id(0) == 0)
    def _():
        for at, ref in enumerate(pieces):
            key = keys(ref).astype(F32)
            square = key * key
            high = square.astype(BF16)
            rest = (square - high.astype(F32)).astype(BF16)
            total = dot_t(ones, high) + dot_t(ones, rest)
            inverse[:, at * chunk : (at + 1) * chunk] = lax.rsqrt(total * (1.0 / HEAD) + EPS)

    for query_ref, out in ((q0, o0), (q1, o1), (q2, o2), (q3, o3)):
        query = query_ref[...]
        wide = query.astype(F32)
        own = lax.rsqrt(jnp.sum(wide * wide, axis=1, keepdims=True) * (1.0 / HEAD) + EPS)
        factor = own * (scale[0] * (1.0 / HEAD))
        scores = []
        peak = None
        for at, ref in enumerate(pieces):
            part = dot_t(query, keys(ref)) * factor
            part = part * inverse[0:1, at * chunk : (at + 1) * chunk]
            top = jnp.max(part, axis=1, keepdims=True)
            peak = top if peak is None else jnp.maximum(peak, top)
            scores.append(part)
        total, mixed = None, None
        for part, ref in zip(scores, pieces):
            exps = jnp.exp(part - peak)
            count = jnp.sum(exps, axis=1, keepdims=True)
            values = jnp.concatenate([ref[:, 128:256], ref[:, 256:]], axis=1)
            term = dot(exps.astype(BF16), values)
            total = count if total is None else total + count
            mixed = term if mixed is None else mixed + term
        mixed = mixed / total
        weight = peak + jnp.log(total)
        high = weight.astype(BF16).astype(F32)
        rest = weight - high
        mid = rest.astype(BF16).astype(F32)
        place = lax.broadcasted_iota(jnp.int32, mixed.shape, 1)
        mixed = jnp.where(place == 128, high, mixed)
        mixed = jnp.where(place == 129, mid, mixed)
        mixed = jnp.where(place == 130, rest - mid, mixed)
        out[...] = mixed.astype(BF16)


def attend(scale, queries, keyvals):
    rows = queries[0].shape[0]
    block = rows // 2
    keys = 4 * keyvals[0].shape[0]
    return pl.pallas_call(
        attend_kernel,
        grid=(2,),
        in_specs=[pl.BlockSpec(memory_space=pltpu.SMEM)]
        + [pl.BlockSpec((block, 256), lambda i: (i, 0))] * 4
        + [whole(keyvals[0].shape)] * 4,
        out_specs=[pl.BlockSpec((block, 256), lambda i: (i, 0))] * 4,
        out_shape=[shape((rows, 256), BF16)] * 4,
        scratch_shapes=[pltpu.VMEM((8, keys), F32)],
        compiler_params=params(),
        cost_estimate=cost(4 * 4 * rows * keys * 256, 4 * (rows + 512) * 1024),
        name="attend",
    )(scale, *queries, *keyvals)


def merge_kernel(a0, a1, a2, a3, out):
    parts = [ref[...].astype(F32) for ref in (a0, a1, a2, a3)]
    logs = [p[:, 128:129] + p[:, 129:130] + p[:, 130:131] for p in parts]
    peak = functools.reduce(jnp.maximum, logs)
    shares = [jnp.exp(log - peak) for log in logs]
    total = sum(shares)
    mixed = sum(p * (share / total) for p, share in zip(parts, shares))
    out[:, :128] = mixed[:, :128].astype(BF16)
    out[:, 128:] = pltpu.roll(mixed[:, 128:], 64, 1).astype(BF16)


def merge(parts):
    return pl.pallas_call(
        merge_kernel,
        out_shape=shape(parts[0].shape, BF16),
        compiler_params=params(),
        cost_estimate=cost(20 * parts[0].size, 10 * parts[0].size),
        name="merge",
    )(*parts)


def output_kernel(ids, a0, a1, a2, a3, weight, out):
    total = None
    for distance, ref in enumerate((a0, a1, a2, a3)):
        head = lax.rem(ids[1] + distance, 4)
        rows = weight[pl.ds(pl.multiple_of(head * HEAD, HEAD), HEAD), :]
        term = dot(ref[:, :HEAD], rows)
        total = term if total is None else total + term
    out[...] = total.astype(out.dtype)


def output(ids, parts, weight, mine, dtype):
    half = weight.shape[1] // 2
    return pl.pallas_call(
        output_kernel,
        grid_spec=pltpu.PrefetchScalarGridSpec(
            num_scalar_prefetch=1,
            grid=(half // TILE,),
            in_specs=[whole(parts[0].shape)] * 4
            + [
                pl.BlockSpec(
                    (weight.shape[0], TILE),
                    lambda i, ids: (0, 3 * (ids[0] if mine else 1 - ids[0]) + i),
                )
            ],
            out_specs=pl.BlockSpec((ROWS, TILE), lambda i, ids: (0, i)),
        ),
        out_shape=shape((ROWS, half), dtype),
        compiler_params=params(),
        cost_estimate=cost(2 * ROWS * weight.size // 2, weight.size),
        name="output",
    )(ids, *parts, weight)


def decode_send_kernel(ids, own, other, encoded, weight, inputs, out):
    @pl.when(pl.program_id(0) == 0)
    def _():
        enc = encoded[...].astype(F32)
        even, odd = enc[:ROWS], enc[ROWS:]
        binned = (even + odd) * 0.5
        block = (binned + (own[...] + other[...].astype(F32))).astype(BF16).astype(F32)
        row = lax.broadcasted_iota(jnp.int32, block.shape, 0)
        outside = ((ids[2] == 0) & (row == ROWS - 1)) | ((ids[2] == 63) & (row == OWN))
        even = jnp.where(outside, 0.0, block + even)
        odd = jnp.where(outside, 0.0, block + odd)
        inputs[...] = jnp.concatenate([even, odd], axis=0).astype(BF16)

    even, odd = conv_taps(inputs[...], lambda t: weight[t])
    out[...] = jnp.concatenate([even, odd], axis=0).astype(BF16)


def decode_send(ids, own, other, encoded, weight):
    half = weight.shape[1]
    return pl.pallas_call(
        decode_send_kernel,
        grid_spec=pltpu.PrefetchScalarGridSpec(
            num_scalar_prefetch=1,
            grid=(half // TILE,),
            in_specs=[
                whole(own.shape),
                whole(other.shape),
                whole(encoded.shape),
                pl.BlockSpec((3, half, TILE), lambda i, ids: (0, 0, 3 * (1 - ids[0]) + i)),
            ],
            out_specs=[
                whole((2 * ROWS, half)),
                pl.BlockSpec((2 * ROWS, TILE), lambda i, ids: (0, i)),
            ],
        ),
        out_shape=[shape((2 * ROWS, half), BF16)] * 2,
        compiler_params=params(),
        cost_estimate=cost(2 * 2 * ROWS * weight.size // 2, weight.size),
        name="decode_send",
    )(ids, own, other, encoded, weight)


def decode_own_kernel(ids, inputs, weight, out):
    even, odd = conv_taps(inputs[...], lambda t: weight[t])
    out[...] = jnp.concatenate([even, odd], axis=0)


def decode_own(ids, inputs, weight):
    half = weight.shape[1]
    return pl.pallas_call(
        decode_own_kernel,
        grid_spec=pltpu.PrefetchScalarGridSpec(
            num_scalar_prefetch=1,
            grid=(half // TILE,),
            in_specs=[
                whole(inputs.shape),
                pl.BlockSpec((3, half, TILE), lambda i, ids: (0, 0, 3 * ids[0] + i)),
            ],
            out_specs=pl.BlockSpec((2 * ROWS, TILE), lambda i, ids: (0, i)),
        ),
        out_shape=shape((2 * ROWS, half), F32),
        compiler_params=params(),
        cost_estimate=cost(2 * 2 * ROWS * weight.size // 2, weight.size),
        name="decode_own",
    )(ids, inputs, weight)


def slope_kernel(ids, own, other, inputs, grad, edges, decoded, slope, paired, wide):
    pre = own[...] + other[...].astype(F32)
    _, tanh = gelu_parts(pre)
    result = inputs[...].astype(F32) + 0.5 * pre * (1.0 + tanh)
    halves = (slice(0, 128), slice(128, TILE))
    for lanes in halves:
        wide[pl.ds(0, OWN, 2), :] = result[:OWN, lanes]
        wide[pl.ds(1, OWN, 2), :] = result[ROWS : ROWS + OWN, lanes]
        decoded[:, lanes] = wide[...].astype(BF16)
    slant = 0.5 * (1.0 + tanh) + (0.5 * 0.7978845608028654) * pre * (1.0 - tanh * tanh) * (
        1.0 + (3 * 0.044715) * (pre * pre)
    )
    evens, odds = [], []
    for lanes in halves:
        wide[...] = grad[:, lanes].astype(F32)
        evens.append(wide[pl.ds(0, OWN, 2), :])
        odds.append(wide[pl.ds(1, OWN, 2), :])
    even = jnp.concatenate(evens, axis=1)
    odd = jnp.concatenate(odds, axis=1)
    paired[...] = even + odd
    edge = edges[...].astype(F32)
    row = lax.broadcasted_iota(jnp.int32, (ROWS - OWN, even.shape[1]), 0)
    even_edge = jnp.where(row == 0, edge[1:2], 0.0)
    odd_edge = jnp.where(row == ROWS - OWN - 1, edge[0:1], 0.0)
    cotangent = jnp.concatenate([even, even_edge, odd, odd_edge], axis=0)
    slope[...] = (cotangent * slant).astype(BF16)


def slopes(ids, own, other, inputs, grad, edges):
    half = own.shape[1]

    def tile(rows):
        return pl.BlockSpec((rows, TILE), lambda i, ids: (0, i))

    def mine(rows):
        return pl.BlockSpec((rows, TILE), lambda i, ids: (0, 3 * ids[0] + i))

    return pl.pallas_call(
        slope_kernel,
        grid_spec=pltpu.PrefetchScalarGridSpec(
            num_scalar_prefetch=1,
            grid=(half // TILE,),
            in_specs=[tile(2 * ROWS)] * 3 + [mine(2 * OWN), mine(8)],
            out_specs=[tile(2 * OWN), tile(2 * ROWS), tile(OWN)],
            scratch_shapes=[pltpu.VMEM((2 * OWN, 128), F32)],
        ),
        out_shape=[
            shape((2 * OWN, half), BF16),
            shape((2 * ROWS, half), BF16),
            shape((OWN, half), F32),
        ],
        compiler_params=params(),
        cost_estimate=cost(30 * own.size, 14 * own.size),
        name="slopes",
    )(ids, own, other, inputs, grad, edges)


def backward_kernel(ids, slope, start, weight, out, level, lower, upper):
    step = pl.program_id(0)
    first, mid, last = (dot_t(slope[...], weight[t]) for t in range(3))
    flat = first[ROWS:] + mid[:ROWS] + mid[ROWS:] + last[:ROWS]

    @pl.when(step == 0)
    def _():
        level[...] = flat
        lower[...] = first[:ROWS]
        upper[...] = last[ROWS:]

    @pl.when(step > 0)
    def _():
        level[...] += flat
        lower[...] += first[:ROWS]
        upper[...] += last[ROWS:]

    @pl.when(step == pl.num_programs(0) - 1)
    def _():
        total = level[...] + below(lower[...]) + above(upper[...])
        out[...] = (start[...] + total[:OWN]).astype(out.dtype)


def backward(ids, slope, start, weight, mine, dtype):
    half = weight.shape[1]
    return pl.pallas_call(
        backward_kernel,
        grid_spec=pltpu.PrefetchScalarGridSpec(
            num_scalar_prefetch=1,
            grid=(half // TILE,),
            in_specs=[
                pl.BlockSpec((2 * ROWS, TILE), lambda i, ids: (0, i)),
                whole(start.shape),
                pl.BlockSpec(
                    (3, half, TILE),
                    lambda i, ids: (0, 0, 3 * (ids[0] if mine else 1 - ids[0]) + i),
                ),
            ],
            out_specs=whole((OWN, half)),
            scratch_shapes=[pltpu.VMEM((ROWS, half), F32)] * 3,
        ),
        out_shape=shape((OWN, half), dtype),
        compiler_params=params(),
        cost_estimate=cost(2 * 2 * ROWS * weight.size // 2, weight.size),
        name="backward",
    )(ids, slope, start, weight)


def place(at):
    return at // 16, at // 4 % 4, at // 2 % 2, at % 2


def moves(dx=0, dz=0, dy=0, dc=0):
    pairs = []
    for at in range(64):
        x, z, y, c = place(at)
        pairs.append((at, (x + dx) % 4 * 16 + (z + dz) % 4 * 4 + (y ^ dy) * 2 + (c ^ dc)))
    return pairs


def swap(value):
    return lax.ppermute(value, "head", [(0, 1), (1, 0)])


def send(value, **step):
    return lax.ppermute(value, "seq", moves(**step))


def per_device(
    dna_bases,
    stem_weight,
    encoder_weight,
    norm_gain,
    attention_weight,
    logit_scale,
    out_weight,
    decoder_weight,
    grad_out,
):
    at = lax.axis_index("seq")
    x = at // 16
    ids = jnp.stack([lax.axis_index("head"), x, at]).astype(jnp.int32)

    codes = (dna_bases + 1).astype(BF16).reshape(OWN, 128)
    forward = [(i, i + 1) for i in range(63)]
    backwards = [(i + 1, i) for i in range(63)]
    feats = grad_out.shape[1]
    last = jnp.concatenate([codes[-2:].reshape(1, 256), grad_out[-1:]], axis=1)
    first = jnp.concatenate([codes[:2].reshape(1, 256), grad_out[:1]], axis=1)
    before = lax.ppermute(last, "seq", forward)
    after = lax.ppermute(first, "seq", backwards)
    gap = jnp.zeros((ROWS - OWN - 4, 128), BF16)
    ring = jnp.concatenate(
        [codes, after[:, :256].reshape(2, 128), gap, before[:, :256].reshape(2, 128)], axis=0
    )
    edges = jnp.concatenate(
        [before[:, 256:], after[:, 256:], jnp.zeros((6, feats), BF16)], axis=0
    )

    encoded, squares = encode(ids, ring, stem_weight, encoder_weight)
    normed = normalize(ids, encoded, squares, swap(squares), norm_gain.reshape(1, feats))
    queries, keyvals = project(ids, normed, swap(normed), attention_weight)

    def pick(stack, distance):
        return lax.dynamic_index_in_dim(stack, (x + distance) % 4, 0, keepdims=False)

    def regroup(stack):
        return jnp.concatenate(
            [pick(stack, 0)] + [send(pick(stack, d), dx=d) for d in (1, 3, 2)], axis=0
        )

    keyvals = regroup(keyvals)
    queries = regroup(queries)
    turns = ({"dc": 1}, {"dy": 1}, {"dy": 1, "dc": 1})
    all_keys = [keyvals] + [send(keyvals, dz=d) for d in (1, 3, 2)]
    all_queries = [queries] + [send(queries, **turn) for turn in turns]
    scale = lax.dynamic_slice_in_dim(logit_scale, x, 1)
    parts = attend(scale, all_queries, all_keys)
    mixed = merge([parts[0]] + [send(part, **turn) for part, turn in zip(parts[1:], turns)])
    mixed = mixed.reshape(4, ROWS, 256)
    back = [send(mixed[i], dx=-d) for i, d in ((1, 1), (2, 3), (3, 2))]
    heads = [mixed[0], back[0], back[2], back[1]]

    sent = swap(output(ids, heads, out_weight, False, BF16))
    kept = output(ids, heads, out_weight, True, F32)
    inputs, sent = decode_send(ids, kept, sent, encoded, decoder_weight)
    sent = swap(sent)
    kept = decode_own(ids, inputs, decoder_weight)
    decoded, slope, paired = slopes(ids, kept, sent, inputs, grad_out, edges)
    sent = swap(slope)
    partial = backward(ids, slope, paired, decoder_weight, True, F32)
    bins_grad = backward(ids, sent, partial, decoder_weight, False, BF16)
    return decoded, bins_grad


def solution(mesh):
    in_specs = (
        P("seq"),
        P(),
        P(None, None, "head"),
        P(),
        P(None, None, "head"),
        P("head"),
        P("head", None),
        P(None, "head", None),
        P("seq", None),
    )
    out_specs = (P("seq", "head"), P("seq", "head"))
    return jax.shard_map(
        per_device, mesh=mesh, in_specs=in_specs, out_specs=out_specs, check_vma=False
    )
```

time: 447 us -> 178 us (0.40); the launches traced: 440 us -> 177 us
  waiting for transfers between devices: 269 us -> 50.2 us
  Pallas kernels: 0 us -> 64.4 us
  matrix products: 54.6 us -> 0 us
  local copies, waits for them, and re-layouts: 49.1 us -> 12.4 us
  starting transfers between devices: 12.2 us -> 44.9 us
  other arithmetic: 26.8 us -> 3.77 us
  blocking collectives: 13.9 us -> 0 us
  between operations: 14.1 us -> 0.91 us
    all_gather x2 -> x0, waiting for transfers between devices: 194 us -> none  [the longest x1 114 us: per_device(): lax.all_gather(keys, 'seq', axis=0, tiled=True)]
    psum x2 -> x0, waiting for transfers between devices: 74.6 us -> none  [the longest x1 44.1 us: per_device(): lax.psum(partials.astype(jnp.bfloat16), 'head').astype(jnp.float32)]
    pallas_call x0 -> x12, Pallas kernels: none -> 64.4 us  [the longest x1 11.5 us: attend(): pl.pallas_call(attend_kernel, grid=(2,), in_specs=[pl.BlockSpec(memory_sp...]
    dot_general x16 -> x0, matrix products: 54.6 us -> none  [the longest x1 11.4 us: per_device(): jnp.einsum('hqk,khd->hqd', exps.astype(jnp.bfloat16), value_heads, prefer...]
    ppermute x6 -> x25, waiting for transfers between devices: 0.02 us -> 50.2 us  [the longest x18 34.8 us: send(): return lax.ppermute(value, 'seq', moves(**step))]
    ppermute x6 -> x25, starting transfers between devices: 11.9 us -> 44.9 us  [the longest x18 25.1 us: send(): return lax.ppermute(value, 'seq', moves(**step))]
    all_gather x2 -> x0, local copies, waits for them, and re-layouts: 31.4 us -> none  [the longest x1 15.7 us: per_device(): lax.all_gather(keys, 'seq', axis=0, tiled=True)]
    reduce_sum x6 -> x0, other arithmetic: 16.7 us -> none  [the longest x1 7.4 us: head_scores(): jnp.mean(jnp.square(key_heads.astype(jnp.float32)), axis=2) + 1e-06]
  transfers between devices with their start and end apart: 10 -> 25, of which waited for: 4 -> 16; matrix products, arithmetic and copies ran while one was open for 13% -> 3% of each run, Pallas kernels for 0% -> 8%
where the time goes in v1:
time: 178 us; the launch traced here: 177 us
  Pallas kernels  64.4 us (36%)
  waiting for transfers between devices  50.2 us (28%)
  starting transfers between devices  44.9 us (25%)
  local copies, waits for them, and re-layouts  12.4 us (7%)
  other arithmetic  3.77 us (2%)
    ppermute x18, waiting for transfers between devices, send(): return lax.ppermute(value, 'seq', moves(**step))  34.8 us
    ppermute x18, starting transfers between devices, send(): return lax.ppermute(value, 'seq', moves(**step))  25.1 us
    ppermute x5, starting transfers between devices, swap(): return lax.ppermute(value, 'head', [(0, 1), (1, 0)])  15.4 us
    ppermute x5, waiting for transfers between devices, swap(): return lax.ppermute(value, 'head', [(0, 1), (1, 0)])  15.3 us
    pallas_call x1, Pallas kernels, attend(): pl.pallas_call(attend_kernel, grid=(2,), in_specs=[pl.BlockSpec(memory_sp...  11.5 us
    pallas_call x2, Pallas kernels, backward(): pl.pallas_call(backward_kernel, grid_spec=pltpu.PrefetchScalarGridSpec(nu...  11.1 us
    pallas_call x2, Pallas kernels, output(): pl.pallas_call(output_kernel, grid_spec=pltpu.PrefetchScalarGridSpec(num_...  8.07 us
    pallas_call x1, Pallas kernels, encode(): pl.pallas_call(encoder_kernel, grid_spec=pltpu.PrefetchScalarGridSpec(num...  7.36 us
  transfers between devices with their start and end apart: 25, of which 16 were waited for; matrix products, arithmetic and copies ran while one was open for 3% of the time, Pallas kernels for 8%

profile of v1, /device:TPU:0, one launch (start us, length us, event | category | flops | bytes accessed | tf_op | source)
XLA Modules:
  0.0 176.6 jit_solution(8537564548255592260)
XLA Ops:
  0.6 0.9 add_convert_fusion
  1.5 0.8 fusion
  2.3 1.3 collective-permute-start
  3.6 3.0 %collective-permute-start.1 = (bf16[1,1792]{1,0:T(2,128)(2,1)S(1)}, bf16[1,1792]{1,0:T(2,128)(2,1)S(1)}, u32[]{:S(2)}, u32[]{:S(2)}) collective-permute-start(bf16[1,1792]{1,0:T(2,128)(2,1)S(1)} %pad_maximum_fusion.4), channel_id=1, source_target_pairs={{0,2},{2,4},{4,6},{6,8},{8,10},{10,12},{12,14},{14,16},{16,18},{18... | collective-permute-start | bytes 10760 | tf_op jit(solution)/shard_map/ppermute | solution.py:537
  6.7 0.9 fusion.3
  7.6 0.6 pad_add_fusion.ids
  8.3 0.7 pad_maximum_fusion.2.codes
  9.0 7.4 %encode.1 = (bf16[272,768]{1,0:T(8,128)(2,1)}, f32[136,128]{1,0:T(8,128)}) custom-call(s32[3]{0:T(128)} %pad_add_fusion.ids, bf16[136,128]{1,0:T(8,128)(2,1)} %pad_maximum_fusion.2.codes, bf16[256,1536]{1,0:T(8,128)(2,1)} %stem.1, bf16[3,1536,768]{2,1,0:T(8,128)(2,1)} %weight.8), custom_call_target="tpu_custom_call" | custom-call | flops 1925185536 | bytes 7077888 | tf_op jit(solution)/shard_map/encode/pallas_call | solution.py:100
  16.4 3.3 %collective-permute-start.2 = (f32[136,128]{1,0:T(8,128)}, f32[136,128]{1,0:T(8,128)S(1)}, u32[]{:S(2)}, u32[]{:S(2)}) collective-permute-start(f32[136,128]{1,0:T(8,128)} %get-tuple-element.16.mine), channel_id=1, source_target_pairs={{0,1},{1,0},{2,3},{3,2},{4,5},{5,4},{6,7},{7,6},{8,9},{9,8},{10,11... | collective-permute-start | bytes 208904 | tf_op jit(solution)/shard_map/ppermute | solution.py:509
  19.6 0.6 reshape.40.gain
  20.2 2.6 %collective-permute-done.2.theirs = f32[136,128]{1,0:T(8,128)S(1)} collective-permute-done((f32[136,128]{1,0:T(8,128)}, f32[136,128]{1,0:T(8,128)S(1)}, u32[]{:S(2)}, u32[]{:S(2)}) %collective-permute-start.2) | collective-permute-done | bytes 69664 | tf_op jit(solution)/shard_map/ppermute | solution.py:509
  22.8 0.6 copy-done.12
  23.5 2.5 %normalize.1.mine = bf16[136,768]{1,0:T(8,128)(2,1)} custom-call(s32[3]{0:T(128)} %pad_add_fusion.ids, bf16[272,768]{1,0:T(8,128)(2,1)} %get-tuple-element.15.encoded, f32[136,128]{1,0:T(8,128)} %get-tuple-element.16.mine, f32[136,128]{1,0:T(8,128)} %copy-done.12, f32[1,1536]{1,0:T(1,128)} %reshape.40.gain), custom_call_target="tpu_custom_call" | custom-call | flops 835584 | bytes 417792 | tf_op jit(solution)/shard_map/normalize/pallas_call | solution.py:132
  26.0 3.5 %collective-permute-start.3 = (bf16[136,768]{1,0:T(8,128)(2,1)}, bf16[136,768]{1,0:T(8,128)(2,1)S(1)}, u32[]{:S(2)}, u32[]{:S(2)}) collective-permute-start(bf16[136,768]{1,0:T(8,128)(2,1)} %normalize.1.mine), channel_id=1, source_target_pairs={{0,1},{1,0},{2,3},{3,2},{4,5},{5,4},{6,7},{7,6},{8,9},{9,8},{10,11... | collective-permute-start | bytes 626696 | tf_op jit(solution)/shard_map/ppermute | solution.py:509
  29.5 5.7 %collective-permute-done.3.theirs = bf16[136,768]{1,0:T(8,128)(2,1)S(1)} collective-permute-done((bf16[136,768]{1,0:T(8,128)(2,1)}, bf16[136,768]{1,0:T(8,128)(2,1)S(1)}, u32[]{:S(2)}, u32[]{:S(2)}) %collective-permute-start.3) | collective-permute-done | bytes 208928 | tf_op jit(solution)/shard_map/ppermute | solution.py:509
  35.1 0.7 copy-done.10
  35.8 5.6 %project.1 = (bf16[4,136,256]{2,1,0:T(8,128)(2,1)}, bf16[4,128,384]{2,1,0:T(8,128)(2,1)}) custom-call(s32[3]{0:T(128)} %pad_add_fusion.ids, bf16[136,768]{1,0:T(8,128)(2,1)} %normalize.1.mine, bf16[136,768]{1,0:T(8,128)(2,1)} %copy-done.10, bf16[3,1536,768]{2,1,0:T(8,128)(2,1)} %weight.9), custom_call_target="tpu_custom_call" | custom-call | flops 962592768 | bytes 7077888 | tf_op jit(solution)/shard_map/project/pallas_call | solution.py:177
  41.4 1.0 dynamic-slice_bitcast_fusion.7
  42.4 8.0 %collective-permute-start.4 = (bf16[136,256]{1,0:T(8,128)(2,1)S(1)}, bf16[136,256]{1,0:T(8,128)(2,1)S(1)}, u32[]{:S(2)}, u32[]{:S(2)}) collective-permute-start(bf16[136,256]{1,0:T(8,128)(2,1)S(1)} %get-tuple-element.41), channel_id=1, source_target_pairs={{0,32},{2,34},{4,36},{6,38},{8,40},{10,42},{12,44},{14,46},{16,48}... | collective-permute-start | bytes 208904 | tf_op jit(solution)/shard_map/ppermute | solution.py:513
  50.4 1.7 collective-permute-start.5
  52.1 1.9 %collective-permute-start.6 = (bf16[136,256]{1,0:T(8,128)(2,1)S(1)}, bf16[136,256]{1,0:T(8,128)(2,1)S(1)}, u32[]{:S(2)}, u32[]{:S(2)}) collective-permute-start(bf16[136,256]{1,0:T(8,128)(2,1)S(1)} %get-tuple-element.39), channel_id=1, source_target_pairs={{0,64},{2,66},{4,68},{6,70},{8,72},{10,74},{12,76},{14,78},{16,80}... | collective-permute-start | bytes 208904 | tf_op jit(solution)/shard_map/ppermute | solution.py:513
  54.0 1.1 dynamic-slice_bitcast_fusion.3
  55.0 1.0 collective-permute-start.10
  56.0 2.3 %collective-permute-start.11 = (bf16[128,384]{1,0:T(8,128)(2,1)S(1)}, bf16[128,384]{1,0:T(8,128)(2,1)S(1)}, u32[]{:S(2)}, u32[]{:S(2)}) collective-permute-start(bf16[128,384]{1,0:T(8,128)(2,1)S(1)} %get-tuple-element.32), channel_id=1, source_target_pairs={{0,96},{2,98},{4,100},{6,102},{8,104},{10,106},{12,108},{14,110},{... | collective-permute-start | bytes 294920 | tf_op jit(solution)/shard_map/ppermute | solution.py:513
  58.9 2.0 %collective-permute-done.10 = bf16[128,384]{1,0:T(8,128)(2,1)S(1)} collective-permute-done((bf16[128,384]{1,0:T(8,128)(2,1)S(1)}, bf16[128,384]{1,0:T(8,128)(2,1)S(1)}, u32[]{:S(2)}, u32[]{:S(2)}) %collective-permute-start.10) | collective-permute-done | bytes 98336 | tf_op jit(solution)/shard_map/ppermute | solution.py:513
  60.9 0.6 collective-permute-done.11
  61.6 2.9 %collective-permute-done.12 = bf16[128,384]{1,0:T(8,128)(2,1)S(1)} collective-permute-done((bf16[128,384]{1,0:T(8,128)(2,1)S(1)}, bf16[128,384]{1,0:T(8,128)(2,1)S(1)}, u32[]{:S(2)}, u32[]{:S(2)}) %collective-permute-start.12) | collective-permute-done | bytes 98336 | tf_op jit(solution)/shard_map/ppermute | solution.py:513
  64.6 3.2 %collective-permute-start.14 = (bf16[512,384]{1,0:T(8,128)(2,1)S(1)}, bf16[512,384]{1,0:T(8,128)(2,1)S(1)}, u32[]{:S(2)}, u32[]{:S(2)}) collective-permute-start(bf16[512,384]{1,0:T(8,128)(2,1)S(1)} %pad_maximum_fusion.k0), channel_id=1, source_target_pairs={{0,24},{2,26},{4,28},{6,30},{8,0},{10,2},{12,4},{14,6},{16,8},{18,... | collective-permute-start | bytes 1179656 | tf_op jit(solution)/shard_map/ppermute | solution.py:513
  68.2 0.6 dynamic_slice.29.scale
  68.7 8.3 %collective-permute-done.8.q2 = bf16[544,256]{1,0:T(8,128)(2,1)S(1)} collective-permute-done((bf16[544,256]{1,0:T(8,128)(2,1)S(1)}, bf16[544,256]{1,0:T(8,128)(2,1)S(1)}, u32[]{:S(2)}, u32[]{:S(2)}) %collective-permute-start.8) | collective-permute-done | bytes 278560 | tf_op jit(solution)/shard_map/ppermute | solution.py:513
  77.1 0.8 collective-permute-done.9.q3
  77.9 2.6 %collective-permute-done.13.k1 = bf16[512,384]{1,0:T(8,128)(2,1)S(1)} collective-permute-done((bf16[512,384]{1,0:T(8,128)(2,1)S(1)}, bf16[512,384]{1,0:T(8,128)(2,1)S(1)}, u32[]{:S(2)}, u32[]{:S(2)}) %collective-permute-start.13) | collective-permute-done | bytes 393248 | tf_op jit(solution)/shard_map/ppermute | solution.py:513
  80.5 0.7 copy-done.16
  81.4 0.7 copy-done.18
  82.1 11.5 %attend.1 = (bf16[544,256]{1,0:T(8,128)(2,1)}, bf16[544,256]{1,0:T(8,128)(2,1)}, bf16[544,256]{1,0:T(8,128)(2,1)}, bf16[544,256]{1,0:T(8,128)(2,1)}) custom-call(f32[1]{0:T(128)} %dynamic_slice.29.scale, bf16[544,256]{1,0:T(8,128)(2,1)} %copy-done.6, bf16[544,256]{1,0:T(8,128)(2,1)} %copy-done.19, bf16[544,256]{1,0:T(8,128)(2,1)} %copy-done.20, ...), custom_call_target="tpu_custom_call" | custom-call | flops 4563402752 | bytes 4325376 | tf_op jit(solution)/shard_map/attend/pallas_call | solution.py:255
  93.8 1.7 collective-permute-start.18
  95.6 7.9 %collective-permute-done.17.a2 = bf16[544,256]{1,0:T(8,128)(2,1)S(1)} collective-permute-done((bf16[544,256]{1,0:T(8,128)(2,1)}, bf16[544,256]{1,0:T(8,128)(2,1)S(1)}, u32[]{:S(2)}, u32[]{:S(2)}) %collective-permute-start.17) | collective-permute-done | bytes 278560 | tf_op jit(solution)/shard_map/ppermute | solution.py:513
  103.5 5.0 %collective-permute-done.18.a3 = bf16[544,256]{1,0:T(8,128)(2,1)S(1)} collective-permute-done((bf16[544,256]{1,0:T(8,128)(2,1)}, bf16[544,256]{1,0:T(8,128)(2,1)S(1)}, u32[]{:S(2)}, u32[]{:S(2)}) %collective-permute-start.18) | collective-permute-done | bytes 278560 | tf_op jit(solution)/shard_map/ppermute | solution.py:513
  108.5 0.7 copy-done.9
  109.2 3.0 %merge.1 = bf16[544,256]{1,0:T(8,128)(2,1)} custom-call(bf16[544,256]{1,0:T(8,128)(2,1)} %get-tuple-element.19.a0, bf16[544,256]{1,0:T(8,128)(2,1)} %copy-done.7, bf16[544,256]{1,0:T(8,128)(2,1)} %copy-done.8, bf16[544,256]{1,0:T(8,128)(2,1)} %copy-done.9), custom_call_target="tpu_custom_call" | custom-call | flops 2785280 | bytes 1392640 | tf_op jit(solution)/shard_map/merge/pallas_call | solution.py:282
  112.2 1.6 fusion.1
  113.8 1.7 collective-permute-start.19
  115.5 1.2 collective-permute-start.20
  116.7 1.4 collective-permute-start.21
  118.2 3.7 %collective-permute-done.20.a2 = bf16[136,256]{1,0:T(8,128)(2,1)S(1)} collective-permute-done((bf16[136,256]{1,0:T(8,128)(2,1)S(1)}, bf16[136,256]{1,0:T(8,128)(2,1)S(1)}, u32[]{:S(2)}, u32[]{:S(2)}) %collective-permute-start.20) | collective-permute-done | bytes 69664 | tf_op jit(solution)/shard_map/ppermute | solution.py:513
  121.9 0.9 collective-permute-done.21.a3
  122.7 0.6 copy-done.5
  123.4 3.9 %output.3 = bf16[136,768]{1,0:T(8,128)(2,1)} custom-call(s32[3]{0:T(128)} %pad_add_fusion.ids, bf16[136,256]{1,0:T(8,128)(2,1)} %get-tuple-element.37.a0, bf16[136,256]{1,0:T(8,128)(2,1)} %copy-done.3, bf16[136,256]{1,0:T(8,128)(2,1)} %copy-done.4, bf16[136,256]{1,0:T(8,128)(2,1)} %copy-done.5, bf16[768,1536]{1,0:T(8,128)(2,1)} %weight.11), custom_call_target="tpu_custom_call" | custom-call | flops 160432128 | bytes 1179648 | tf_op jit(solution)/shard_map/output/pallas_call | solution.py:303
  127.3 2.9 %collective-permute-start.22 = (bf16[136,768]{1,0:T(8,128)(2,1)}, bf16[136,768]{1,0:T(8,128)(2,1)S(1)}, u32[]{:S(2)}, u32[]{:S(2)}) collective-permute-start(bf16[136,768]{1,0:T(8,128)(2,1)} %output.3), channel_id=1, source_target_pairs={{0,1},{1,0},{2,3},{3,2},{4,5},{5,4},{6,7},{7,6},{8,9},{9,8},{10,11... | collective-permute-start | bytes 626696 | tf_op jit(solution)/shard_map/ppermute | solution.py:509
  130.3 4.1 %output.2.own = f32[136,768]{1,0:T(8,128)} custom-call(s32[3]{0:T(128)} %pad_add_fusion.ids, bf16[136,256]{1,0:T(8,128)(2,1)} %get-tuple-element.37.a0, bf16[136,256]{1,0:T(8,128)(2,1)} %copy-done.3, bf16[136,256]{1,0:T(8,128)(2,1)} %copy-done.4, bf16[136,256]{1,0:T(8,128)(2,1)} %copy-done.5, bf16[768,1536]{1,0:T(8,128)(2,1)} %weight.11), custom_call_target="tpu_custom_call" | custom-call | flops 160432128 | bytes 1179648 | tf_op jit(solution)/shard_map/output/pallas_call | solution.py:303
  134.4 1.3 collective-permute-done.22.other
  135.7 0.7 copy-done.11
  136.4 5.5 %decode_send.1 = (bf16[272,768]{1,0:T(8,128)(2,1)}, bf16[272,768]{1,0:T(8,128)(2,1)}) custom-call(s32[3]{0:T(128)} %pad_add_fusion.ids, f32[136,768]{1,0:T(8,128)} %output.2.own, bf16[136,768]{1,0:T(8,128)(2,1)} %copy-done.11, bf16[272,768]{1,0:T(8,128)(2,1)} %get-tuple-element.15.encoded, bf16[3,768,1536]{2,1,0:T(8,128)(2,1)} %weight.15), custom_call_target="tpu_custom_call" | custom-call | flops 962592768 | bytes 3538944 | tf_op jit(solution)/shard_map/decode_send/pallas_call | solution.py:343
  141.9 2.9 %collective-permute-start.23 = (bf16[272,768]{1,0:T(8,128)(2,1)}, bf16[272,768]{1,0:T(8,128)(2,1)S(1)}, u32[]{:S(2)}, u32[]{:S(2)}) collective-permute-start(bf16[272,768]{1,0:T(8,128)(2,1)} %get-tuple-element.24), channel_id=1, source_target_pairs={{0,1},{1,0},{2,3},{3,2},{4,5},{5,4},{6,7},{7,6},{8,9},{9,8},{10,11... | collective-permute-start | bytes 1253384 | tf_op jit(solution)/shard_map/ppermute | solution.py:509
  144.8 0.7 maximum_maximum_fusion.edges
  145.4 5.2 %decode_own.1.own = f32[272,768]{1,0:T(8,128)} custom-call(s32[3]{0:T(128)} %pad_add_fusion.ids, bf16[272,768]{1,0:T(8,128)(2,1)} %get-tuple-element.23.inputs, bf16[3,768,1536]{2,1,0:T(8,128)(2,1)} %weight.15), custom_call_target="tpu_custom_call" | custom-call | flops 962592768 | bytes 3538944 | tf_op jit(solution)/shard_map/decode_own/pallas_call | solution.py:373
  150.6 3.2 %collective-permute-done.23.other = bf16[272,768]{1,0:T(8,128)(2,1)S(1)} collective-permute-done((bf16[272,768]{1,0:T(8,128)(2,1)}, bf16[272,768]{1,0:T(8,128)(2,1)S(1)}, u32[]{:S(2)}, u32[]{:S(2)}) %collective-permute-start.23) | collective-permute-done | bytes 417824 | tf_op jit(solution)/shard_map/ppermute | solution.py:509
  153.8 0.8 copy-done.1
  154.6 4.6 %slopes.1 = (bf16[256,768]{1,0:T(8,128)(2,1)}, bf16[272,768]{1,0:T(8,128)(2,1)}, f32[128,768]{1,0:T(8,128)}) custom-call(s32[3]{0:T(128)} %pad_add_fusion.ids, f32[272,768]{1,0:T(8,128)} %decode_own.1.own, bf16[272,768]{1,0:T(8,128)(2,1)} %copy-done.1, bf16[272,768]{1,0:T(8,128)(2,1)} %get-tuple-element.23.inputs, bf16[256,1536]{1,0:T(8,128)(2,1)} %grad.1, ...), custom_call_target="tpu_custom_call" | custom-call | flops 6266880 | bytes 2924544 | tf_op jit(solution)/shard_map/slopes/pallas_call | solution.py:428
  159.2 2.9 %collective-permute-start.24 = (bf16[272,768]{1,0:T(8,128)(2,1)}, bf16[272,768]{1,0:T(8,128)(2,1)S(1)}, u32[]{:S(2)}, u32[]{:S(2)}) collective-permute-start(bf16[272,768]{1,0:T(8,128)(2,1)} %get-tuple-element.26.slope), channel_id=1, source_target_pairs={{0,1},{1,0},{2,3},{3,2},{4,5},{5,4},{6,7},{7,6},{8,9},{9,8},{10,11... | collective-permute-start | bytes 1253384 | tf_op jit(solution)/shard_map/ppermute | solution.py:509
  162.1 5.6 %backward.2.start = f32[128,768]{1,0:T(8,128)} custom-call(s32[3]{0:T(128)} %pad_add_fusion.ids, bf16[272,768]{1,0:T(8,128)(2,1)} %get-tuple-element.26.slope, f32[128,768]{1,0:T(8,128)} %get-tuple-element.27.start, bf16[3,768,1536]{2,1,0:T(8,128)(2,1)} %weight.15), custom_call_target="tpu_custom_call" | custom-call | flops 962592768 | bytes 3538944 | tf_op jit(solution)/shard_map/backward/pallas_call | solution.py:473
  167.7 2.6 %collective-permute-done.24.slope = bf16[272,768]{1,0:T(8,128)(2,1)S(1)} collective-permute-done((bf16[272,768]{1,0:T(8,128)(2,1)}, bf16[272,768]{1,0:T(8,128)(2,1)S(1)}, u32[]{:S(2)}, u32[]{:S(2)}) %collective-permute-start.24) | collective-permute-done | bytes 417824 | tf_op jit(solution)/shard_map/ppermute | solution.py:509
  170.3 0.8 copy-done
  171.1 5.5 %backward.3 = bf16[128,768]{1,0:T(8,128)(2,1)} custom-call(s32[3]{0:T(128)} %pad_add_fusion.ids, bf16[272,768]{1,0:T(8,128)(2,1)} %copy-done, f32[128,768]{1,0:T(8,128)} %backward.2.start, bf16[3,768,1536]{2,1,0:T(8,128)(2,1)} %weight.15), custom_call_target="tpu_custom_call" | custom-call | flops 962592768 | bytes 3538944 | tf_op jit(solution)/shard_map/backward/pallas_call | solution.py:473
  (72 shorter events, 1.6 us)
Async XLA Ops:
  0.6 19.0 %copy-start.15 = (f32[1536]{0:T(1024)S(1)}, f32[1536]{0:T(1024)}, u32[]{:S(2)}) copy-start(f32[1536]{0:T(1024)} %param.12) | copy-start | bytes 18436
  2.3 5.9 %collective-permute-start = (bf16[1,1792]{1,0:T(2,128)(2,1)S(1)}, bf16[1,1792]{1,0:T(2,128)(2,1)S(1)}, u32[]{:S(2)}, u32[]{:S(2)}) collective-permute-start(bf16[1,1792]{1,0:T(2,128)(2,1)S(1)} %pad_maximum_fusion.3), channel_id=1, source_target_pairs={{2,0},{4,2},{6,4},{8,6},{10,8},{12,10},{14,12},{16,14},{18,16},{20... | collective-permute-start | bytes 10760 | tf_op jit(solution)/shard_map/ppermute | solution.py:538
  3.6 4.6 %collective-permute-start.1 = (bf16[1,1792]{1,0:T(2,128)(2,1)S(1)}, bf16[1,1792]{1,0:T(2,128)(2,1)S(1)}, u32[]{:S(2)}, u32[]{:S(2)}) collective-permute-start(bf16[1,1792]{1,0:T(2,128)(2,1)S(1)} %pad_maximum_fusion.4), channel_id=1, source_target_pairs={{0,2},{2,4},{4,6},{6,8},{8,10},{10,12},{12,14},{14,16},{16,18},{18... | collective-permute-start | bytes 10760 | tf_op jit(solution)/shard_map/ppermute | solution.py:537
  8.2 122.0 %copy-start.14 = (bf16[1,1792]{1,0:T(2,128)(2,1)}, bf16[1,1792]{1,0:T(2,128)(2,1)S(1)}, u32[]{:S(2)}) copy-start(bf16[1,1792]{1,0:T(2,128)(2,1)S(1)} %collective-permute-done) | copy-start | bytes 10756
  8.3 122.0 %copy-start.13 = (bf16[1,1792]{1,0:T(2,128)(2,1)}, bf16[1,1792]{1,0:T(2,128)(2,1)S(1)}, u32[]{:S(2)}) copy-start(bf16[1,1792]{1,0:T(2,128)(2,1)S(1)} %collective-permute-done.1) | copy-start | bytes 10756
  16.4 51.8 %copy-start.22 = (f32[4]{0:T(128)S(1)}, f32[4]{0:T(128)}, u32[]{:S(2)}) copy-start(f32[4]{0:T(128)} %param.14) | copy-start | bytes 52
  16.4 6.5 %collective-permute-start.2 = (f32[136,128]{1,0:T(8,128)}, f32[136,128]{1,0:T(8,128)S(1)}, u32[]{:S(2)}, u32[]{:S(2)}) collective-permute-start(f32[136,128]{1,0:T(8,128)} %get-tuple-element.16.mine), channel_id=1, source_target_pairs={{0,1},{1,0},{2,3},{3,2},{4,5},{5,4},{6,7},{7,6},{8,9},{9,8},{10,11... | collective-permute-start | bytes 208904 | tf_op jit(solution)/shard_map/ppermute | solution.py:509
  22.8 0.6 copy-start.12
  26.0 9.1 %collective-permute-start.3 = (bf16[136,768]{1,0:T(8,128)(2,1)}, bf16[136,768]{1,0:T(8,128)(2,1)S(1)}, u32[]{:S(2)}, u32[]{:S(2)}) collective-permute-start(bf16[136,768]{1,0:T(8,128)(2,1)} %normalize.1.mine), channel_id=1, source_target_pairs={{0,1},{1,0},{2,3},{3,2},{4,5},{5,4},{6,7},{7,6},{8,9},{9,8},{10,11... | collective-permute-start | bytes 626696 | tf_op jit(solution)/shard_map/ppermute | solution.py:509
  35.1 0.7 copy-start.10
  42.4 16.0 %collective-permute-start.4 = (bf16[136,256]{1,0:T(8,128)(2,1)S(1)}, bf16[136,256]{1,0:T(8,128)(2,1)S(1)}, u32[]{:S(2)}, u32[]{:S(2)}) collective-permute-start(bf16[136,256]{1,0:T(8,128)(2,1)S(1)} %get-tuple-element.41), channel_id=1, source_target_pairs={{0,32},{2,34},{4,36},{6,38},{8,40},{10,42},{12,44},{14,46},{16,48}... | collective-permute-start | bytes 208904 | tf_op jit(solution)/shard_map/ppermute | solution.py:513
  50.4 8.4 %collective-permute-start.5 = (bf16[136,256]{1,0:T(8,128)(2,1)S(1)}, bf16[136,256]{1,0:T(8,128)(2,1)S(1)}, u32[]{:S(2)}, u32[]{:S(2)}) collective-permute-start(bf16[136,256]{1,0:T(8,128)(2,1)S(1)} %get-tuple-element.40), channel_id=1, source_target_pairs={{0,96},{2,98},{4,100},{6,102},{8,104},{10,106},{12,108},{14,110},{... | collective-permute-start | bytes 208904 | tf_op jit(solution)/shard_map/ppermute | solution.py:513
  52.1 6.7 %collective-permute-start.6 = (bf16[136,256]{1,0:T(8,128)(2,1)S(1)}, bf16[136,256]{1,0:T(8,128)(2,1)S(1)}, u32[]{:S(2)}, u32[]{:S(2)}) collective-permute-start(bf16[136,256]{1,0:T(8,128)(2,1)S(1)} %get-tuple-element.39), channel_id=1, source_target_pairs={{0,64},{2,66},{4,68},{6,70},{8,72},{10,74},{12,76},{14,78},{16,80}... | collective-permute-start | bytes 208904 | tf_op jit(solution)/shard_map/ppermute | solution.py:513
  55.0 5.9 %collective-permute-start.10 = (bf16[128,384]{1,0:T(8,128)(2,1)S(1)}, bf16[128,384]{1,0:T(8,128)(2,1)S(1)}, u32[]{:S(2)}, u32[]{:S(2)}) collective-permute-start(bf16[128,384]{1,0:T(8,128)(2,1)S(1)} %get-tuple-element.33), channel_id=1, source_target_pairs={{0,32},{2,34},{4,36},{6,38},{8,40},{10,42},{12,44},{14,46},{16,48}... | collective-permute-start | bytes 294920 | tf_op jit(solution)/shard_map/ppermute | solution.py:513
  56.0 5.6 %collective-permute-start.11 = (bf16[128,384]{1,0:T(8,128)(2,1)S(1)}, bf16[128,384]{1,0:T(8,128)(2,1)S(1)}, u32[]{:S(2)}, u32[]{:S(2)}) collective-permute-start(bf16[128,384]{1,0:T(8,128)(2,1)S(1)} %get-tuple-element.32), channel_id=1, source_target_pairs={{0,96},{2,98},{4,100},{6,102},{8,104},{10,106},{12,108},{14,110},{... | collective-permute-start | bytes 294920 | tf_op jit(solution)/shard_map/ppermute | solution.py:513
  58.4 6.1 %collective-permute-start.12 = (bf16[128,384]{1,0:T(8,128)(2,1)S(1)}, bf16[128,384]{1,0:T(8,128)(2,1)S(1)}, u32[]{:S(2)}, u32[]{:S(2)}) collective-permute-start(bf16[128,384]{1,0:T(8,128)(2,1)S(1)} %get-tuple-element.31), channel_id=1, source_target_pairs={{0,64},{2,66},{4,68},{6,70},{8,72},{10,74},{12,76},{14,78},{16,80}... | collective-permute-start | bytes 294920 | tf_op jit(solution)/shard_map/ppermute | solution.py:513
  58.8 21.7 %copy-start.6 = (bf16[544,256]{1,0:T(8,128)(2,1)}, bf16[544,256]{1,0:T(8,128)(2,1)S(1)}, u32[]{:S(2)}) copy-start(bf16[544,256]{1,0:T(8,128)(2,1)S(1)} %pad_maximum_fusion.1.q0) | copy-start | bytes 835588
  58.8 9.0 %collective-permute-start.7 = (bf16[544,256]{1,0:T(8,128)(2,1)S(1)}, bf16[544,256]{1,0:T(8,128)(2,1)S(1)}, u32[]{:S(2)}, u32[]{:S(2)}) collective-permute-start(bf16[544,256]{1,0:T(8,128)(2,1)S(1)} %pad_maximum_fusion.1.q0), channel_id=1, source_target_pairs={{0,2},{2,0},{4,6},{6,4},{8,10},{10,8},{12,14},{14,12},{16,18},{18,... | collective-permute-start | bytes 835592 | tf_op jit(solution)/shard_map/ppermute | solution.py:513
  64.5 15.9 %copy-start.2 = (bf16[512,384]{1,0:T(8,128)(2,1)}, bf16[512,384]{1,0:T(8,128)(2,1)S(1)}, u32[]{:S(2)}) copy-start(bf16[512,384]{1,0:T(8,128)(2,1)S(1)} %pad_maximum_fusion.k0) | copy-start | bytes 1179652
  64.5 15.9 %collective-permute-start.13 = (bf16[512,384]{1,0:T(8,128)(2,1)S(1)}, bf16[512,384]{1,0:T(8,128)(2,1)S(1)}, u32[]{:S(2)}, u32[]{:S(2)}) collective-permute-start(bf16[512,384]{1,0:T(8,128)(2,1)S(1)} %pad_maximum_fusion.k0), channel_id=1, source_target_pairs={{0,8},{2,10},{4,12},{6,14},{8,16},{10,18},{12,20},{14,22},{16,24},... | collective-permute-start | bytes 1179656 | tf_op jit(solution)/shard_map/ppermute | solution.py:513
  64.6 15.8 %collective-permute-start.14 = (bf16[512,384]{1,0:T(8,128)(2,1)S(1)}, bf16[512,384]{1,0:T(8,128)(2,1)S(1)}, u32[]{:S(2)}, u32[]{:S(2)}) collective-permute-start(bf16[512,384]{1,0:T(8,128)(2,1)S(1)} %pad_maximum_fusion.k0), channel_id=1, source_target_pairs={{0,24},{2,26},{4,28},{6,30},{8,0},{10,2},{12,4},{14,6},{16,8},{18,... | collective-permute-start | bytes 1179656 | tf_op jit(solution)/shard_map/ppermute | solution.py:513
  67.8 12.6 %collective-permute-start.15 = (bf16[512,384]{1,0:T(8,128)(2,1)S(1)}, bf16[512,384]{1,0:T(8,128)(2,1)S(1)}, u32[]{:S(2)}, u32[]{:S(2)}) collective-permute-start(bf16[512,384]{1,0:T(8,128)(2,1)S(1)} %pad_maximum_fusion.k0), channel_id=1, source_target_pairs={{0,16},{2,18},{4,20},{6,22},{8,24},{10,26},{12,28},{14,30},{16,0},... | collective-permute-start | bytes 1179656 | tf_op jit(solution)/shard_map/ppermute | solution.py:513
  67.8 9.2 %collective-permute-start.8 = (bf16[544,256]{1,0:T(8,128)(2,1)S(1)}, bf16[544,256]{1,0:T(8,128)(2,1)S(1)}, u32[]{:S(2)}, u32[]{:S(2)}) collective-permute-start(bf16[544,256]{1,0:T(8,128)(2,1)S(1)} %pad_maximum_fusion.1.q0), channel_id=1, source_target_pairs={{0,4},{2,6},{4,0},{6,2},{8,12},{10,14},{12,8},{14,10},{16,20},{18,... | collective-permute-start | bytes 835592 | tf_op jit(solution)/shard_map/ppermute | solution.py:513
  67.8 12.6 %copy-start.19 = (bf16[544,256]{1,0:T(8,128)(2,1)}, bf16[544,256]{1,0:T(8,128)(2,1)S(1)}, u32[]{:S(2)}) copy-start(bf16[544,256]{1,0:T(8,128)(2,1)S(1)} %collective-permute-done.7.q1) | copy-start | bytes 835588
  67.9 10.0 %collective-permute-start.9 = (bf16[544,256]{1,0:T(8,128)(2,1)S(1)}, bf16[544,256]{1,0:T(8,128)(2,1)S(1)}, u32[]{:S(2)}, u32[]{:S(2)}) collective-permute-start(bf16[544,256]{1,0:T(8,128)(2,1)S(1)} %pad_maximum_fusion.1.q0), channel_id=1, source_target_pairs={{0,6},{2,4},{4,2},{6,0},{8,14},{10,12},{12,10},{14,8},{16,22},{18,... | collective-permute-start | bytes 835592 | tf_op jit(solution)/shard_map/ppermute | solution.py:513
  77.1 3.4 %copy-start.20 = (bf16[544,256]{1,0:T(8,128)(2,1)}, bf16[544,256]{1,0:T(8,128)(2,1)S(1)}, u32[]{:S(2)}) copy-start(bf16[544,256]{1,0:T(8,128)(2,1)S(1)} %collective-permute-done.8.q2) | copy-start | bytes 835588
  77.9 2.6 %copy-start.21 = (bf16[544,256]{1,0:T(8,128)(2,1)}, bf16[544,256]{1,0:T(8,128)(2,1)S(1)}, u32[]{:S(2)}) copy-start(bf16[544,256]{1,0:T(8,128)(2,1)S(1)} %collective-permute-done.9.q3) | copy-start | bytes 835588
  80.4 0.8 copy-start.16
  80.4 0.9 copy-start.17
  81.4 0.7 copy-start.18
  93.7 1.9 %collective-permute-start.16 = (bf16[544,256]{1,0:T(8,128)(2,1)}, bf16[544,256]{1,0:T(8,128)(2,1)S(1)}, u32[]{:S(2)}, u32[]{:S(2)}) collective-permute-start(bf16[544,256]{1,0:T(8,128)(2,1)} %get-tuple-element.20), channel_id=1, source_target_pairs={{0,2},{2,0},{4,6},{6,4},{8,10},{10,8},{12,14},{14,12},{16,18},{18,... | collective-permute-start | bytes 835592 | tf_op jit(solution)/shard_map/ppermute | solution.py:513
  93.7 9.8 %collective-permute-start.17 = (bf16[544,256]{1,0:T(8,128)(2,1)}, bf16[544,256]{1,0:T(8,128)(2,1)S(1)}, u32[]{:S(2)}, u32[]{:S(2)}) collective-permute-start(bf16[544,256]{1,0:T(8,128)(2,1)} %get-tuple-element.21), channel_id=1, source_target_pairs={{0,4},{2,6},{4,0},{6,2},{8,12},{10,14},{12,8},{14,10},{16,20},{18,... | collective-permute-start | bytes 835592 | tf_op jit(solution)/shard_map/ppermute | solution.py:513
  93.8 14.6 %collective-permute-start.18 = (bf16[544,256]{1,0:T(8,128)(2,1)}, bf16[544,256]{1,0:T(8,128)(2,1)S(1)}, u32[]{:S(2)}, u32[]{:S(2)}) collective-permute-start(bf16[544,256]{1,0:T(8,128)(2,1)} %get-tuple-element.22), channel_id=1, source_target_pairs={{0,6},{2,4},{4,2},{6,0},{8,14},{10,12},{12,10},{14,8},{16,22},{18,... | collective-permute-start | bytes 835592 | tf_op jit(solution)/shard_map/ppermute | solution.py:513
  95.6 12.9 %copy-start.7 = (bf16[544,256]{1,0:T(8,128)(2,1)}, bf16[544,256]{1,0:T(8,128)(2,1)S(1)}, u32[]{:S(2)}) copy-start(bf16[544,256]{1,0:T(8,128)(2,1)S(1)} %collective-permute-done.16.a1) | copy-start | bytes 835588
  103.5 5.0 %copy-start.8 = (bf16[544,256]{1,0:T(8,128)(2,1)}, bf16[544,256]{1,0:T(8,128)(2,1)S(1)}, u32[]{:S(2)}) copy-start(bf16[544,256]{1,0:T(8,128)(2,1)S(1)} %collective-permute-done.17.a2) | copy-start | bytes 835588
  108.5 0.7 copy-start.9
  113.8 4.4 %collective-permute-start.19 = (bf16[136,256]{1,0:T(8,128)(2,1)S(1)}, bf16[136,256]{1,0:T(8,128)(2,1)S(1)}, u32[]{:S(2)}, u32[]{:S(2)}) collective-permute-start(bf16[136,256]{1,0:T(8,128)(2,1)S(1)} %get-tuple-element.36), channel_id=1, source_target_pairs={{0,96},{2,98},{4,100},{6,102},{8,104},{10,106},{12,108},{14,110},{... | collective-permute-start | bytes 208904 | tf_op jit(solution)/shard_map/ppermute | solution.py:513
  115.5 6.4 %collective-permute-start.20 = (bf16[136,256]{1,0:T(8,128)(2,1)S(1)}, bf16[136,256]{1,0:T(8,128)(2,1)S(1)}, u32[]{:S(2)}, u32[]{:S(2)}) collective-permute-start(bf16[136,256]{1,0:T(8,128)(2,1)S(1)} %get-tuple-element.35), channel_id=1, source_target_pairs={{0,64},{2,66},{4,68},{6,70},{8,72},{10,74},{12,76},{14,78},{16,80}... | collective-permute-start | bytes 208904 | tf_op jit(solution)/shard_map/ppermute | solution.py:513
  116.7 6.1 %collective-permute-start.21 = (bf16[136,256]{1,0:T(8,128)(2,1)S(1)}, bf16[136,256]{1,0:T(8,128)(2,1)S(1)}, u32[]{:S(2)}, u32[]{:S(2)}) collective-permute-start(bf16[136,256]{1,0:T(8,128)(2,1)S(1)} %get-tuple-element.34), channel_id=1, source_target_pairs={{0,32},{2,34},{4,36},{6,38},{8,40},{10,42},{12,44},{14,46},{16,48}... | collective-permute-start | bytes 208904 | tf_op jit(solution)/shard_map/ppermute | solution.py:513
  118.2 4.6 %copy-start.3 = (bf16[136,256]{1,0:T(8,128)(2,1)}, bf16[136,256]{1,0:T(8,128)(2,1)S(1)}, u32[]{:S(2)}) copy-start(bf16[136,256]{1,0:T(8,128)(2,1)S(1)} %collective-permute-done.19.a1) | copy-start | bytes 208900
  121.9 0.9 copy-start.4
  122.7 0.6 copy-start.5
  127.3 8.4 %collective-permute-start.22 = (bf16[136,768]{1,0:T(8,128)(2,1)}, bf16[136,768]{1,0:T(8,128)(2,1)S(1)}, u32[]{:S(2)}, u32[]{:S(2)}) collective-permute-start(bf16[136,768]{1,0:T(8,128)(2,1)} %output.3), channel_id=1, source_target_pairs={{0,1},{1,0},{2,3},{3,2},{4,5},{5,4},{6,7},{7,6},{8,9},{9,8},{10,11... | collective-permute-start | bytes 626696 | tf_op jit(solution)/shard_map/ppermute | solution.py:509
  130.3 14.5 %slice-start = ((bf16[1,1792]{1,0:T(2,128)(2,1)}), bf16[1,1536]{1,0:T(2,128)(2,1)S(1)}, s32[]{:S(2)}) async-start(bf16[1,1792]{1,0:T(2,128)(2,1)} %copy-done.13), calls=%async_computation | async-start | bytes 12288 | tf_op jit(solution)/shard_map/slice | solution.py:544
  130.3 14.5 %slice-start.1 = ((bf16[1,1792]{1,0:T(2,128)(2,1)}), bf16[1,1536]{1,0:T(2,128)(2,1)S(1)}, s32[]{:S(2)}) async-start(bf16[1,1792]{1,0:T(2,128)(2,1)} %copy-done.14), calls=%async_computation.1 | async-start | bytes 12288 | tf_op jit(solution)/shard_map/slice | solution.py:544
  135.7 0.7 copy-start.11
  141.9 12.0 %collective-permute-start.23 = (bf16[272,768]{1,0:T(8,128)(2,1)}, bf16[272,768]{1,0:T(8,128)(2,1)S(1)}, u32[]{:S(2)}, u32[]{:S(2)}) collective-permute-start(bf16[272,768]{1,0:T(8,128)(2,1)} %get-tuple-element.24), channel_id=1, source_target_pairs={{0,1},{1,0},{2,3},{3,2},{4,5},{5,4},{6,7},{7,6},{8,9},{9,8},{10,11... | collective-permute-start | bytes 1253384 | tf_op jit(solution)/shard_map/ppermute | solution.py:509
  153.8 0.8 copy-start.1
  159.2 11.1 %collective-permute-start.24 = (bf16[272,768]{1,0:T(8,128)(2,1)}, bf16[272,768]{1,0:T(8,128)(2,1)S(1)}, u32[]{:S(2)}, u32[]{:S(2)}) collective-permute-start(bf16[272,768]{1,0:T(8,128)(2,1)} %get-tuple-element.26.slope), channel_id=1, source_target_pairs={{0,1},{1,0},{2,3},{3,2},{4,5},{5,4},{6,7},{7,6},{8,9},{9,8},{10,11... | collective-permute-start | bytes 1253384 | tf_op jit(solution)/shard_map/ppermute | solution.py:509
  170.3 0.8 copy-start

commit v2 on v1

--- a/solution.py
+++ b/solution.py
@@ -14,11 +14,11 @@
 TILE = 256
 HEAD = 192
 EPS = 1e-06
-VMEM = 56 * 1024 * 1024
-
-
-def params():
-    return pltpu.CompilerParams(vmem_limit_bytes=VMEM)
+MIB = 1024 * 1024
+
+
+def params(mib):
+    return pltpu.CompilerParams(vmem_limit_bytes=mib * MIB)
 
 
 def dot(a, b):
@@ -114,7 +114,7 @@
             scratch_shapes=[pltpu.VMEM((2 * ROWS, feats), BF16)],
         ),
         out_shape=[shape((2 * ROWS, half), BF16), shape((ROWS, 128), F32)],
-        compiler_params=params(),
+        compiler_params=params(16),
         cost_estimate=cost(2 * 2 * ROWS * 3 * feats * half, weight.size * 2),
         name="encode",
     )(ids, codes, stem, weight)
@@ -143,7 +143,7 @@
             out_specs=whole((ROWS, half)),
         ),
         out_shape=shape((ROWS, half), BF16),
-        compiler_params=params(),
+        compiler_params=params(4),
         cost_estimate=cost(8 * ROWS * half, encoded.size * 2),
         name="normalize",
     )(ids, encoded, mine, theirs, gain)
@@ -190,7 +190,7 @@
             ],
         ),
         out_shape=[shape((4, ROWS, 256), BF16), shape((4, OWN, 384), BF16)],
-        compiler_params=params(),
+        compiler_params=params(12),
         cost_estimate=cost(2 * ROWS * weight.size, weight.size * 2),
         name="project",
     )(ids, mine, theirs, weight)
@@ -261,7 +261,7 @@
         out_specs=[pl.BlockSpec((block, 256), lambda i: (i, 0))] * 4,
         out_shape=[shape((rows, 256), BF16)] * 4,
         scratch_shapes=[pltpu.VMEM((8, keys), F32)],
-        compiler_params=params(),
+        compiler_params=params(24),
         cost_estimate=cost(4 * 4 * rows * keys * 256, 4 * (rows + 512) * 1024),
         name="attend",
     )(scale, *queries, *keyvals)
@@ -282,7 +282,7 @@
     return pl.pallas_call(
         merge_kernel,
         out_shape=shape(parts[0].shape, BF16),
-        compiler_params=params(),
+        compiler_params=params(8),
         cost_estimate=cost(20 * parts[0].size, 10 * parts[0].size),
         name="merge",
     )(*parts)
@@ -315,7 +315,7 @@
             out_specs=pl.BlockSpec((ROWS, TILE), lambda i, ids: (0, i)),
         ),
         out_shape=shape((ROWS, half), dtype),
-        compiler_params=params(),
+        compiler_params=params(6),
         cost_estimate=cost(2 * ROWS * weight.size // 2, weight.size),
         name="output",
     )(ids, *parts, weight)
@@ -357,7 +357,7 @@
             ],
         ),
         out_shape=[shape((2 * ROWS, half), BF16)] * 2,
-        compiler_params=params(),
+        compiler_params=params(8),
         cost_estimate=cost(2 * 2 * ROWS * weight.size // 2, weight.size),
         name="decode_send",
     )(ids, own, other, encoded, weight)
@@ -382,7 +382,7 @@
             out_specs=pl.BlockSpec((2 * ROWS, TILE), lambda i, ids: (0, i)),
         ),
         out_shape=shape((2 * ROWS, half), F32),
-        compiler_params=params(),
+        compiler_params=params(8),
         cost_estimate=cost(2 * 2 * ROWS * weight.size // 2, weight.size),
         name="decode_own",
     )(ids, inputs, weight)
@@ -439,7 +439,7 @@
             shape((2 * ROWS, half), BF16),
             shape((OWN, half), F32),
         ],
-        compiler_params=params(),
+        compiler_params=params(6),
         cost_estimate=cost(30 * own.size, 14 * own.size),
         name="slopes",
     )(ids, own, other, inputs, grad, edges)
@@ -487,7 +487,7 @@
             scratch_shapes=[pltpu.VMEM((ROWS, half), F32)] * 3,
         ),
         out_shape=shape((OWN, half), dtype),
-        compiler_params=params(),
+        compiler_params=params(10),
         cost_estimate=cost(2 * 2 * ROWS * weight.size // 2, weight.size),
         name="backward",
     )(ids, slope, start, weight)

time: 178 us -> 154 us (0.87)
  Pallas kernels: 64.4 us -> 36.6 us
  waiting for transfers between devices: 50.2 us -> 58.3 us
  local copies, waits for them, and re-layouts: 12.4 us -> 8.87 us
    ppermute x5, waiting for transfers between devices: 15.3 us -> 23.4 us  [swap(): return lax.ppermute(value, 'head', [(0, 1), (1, 0)])]
    pallas_call x2, Pallas kernels: 8.07 us -> 2.96 us  [output(): pl.pallas_call(output_kernel, grid_spec=pltpu.PrefetchScalarGridSpec(num_...]
    pallas_call x2, Pallas kernels: 11.1 us -> 6.49 us  [backward(): pl.pallas_call(backward_kernel, grid_spec=pltpu.PrefetchScalarGridSpec(nu...]
    pallas_call x1, Pallas kernels: 5.47 us -> 2.61 us  [decode_send(): pl.pallas_call(decode_send_kernel, grid_spec=pltpu.PrefetchScalarGridSpec...]
    pallas_call x1, Pallas kernels: 7.36 us -> 4.57 us  [encode(): pl.pallas_call(encoder_kernel, grid_spec=pltpu.PrefetchScalarGridSpec(num...]
    pallas_call x1, Pallas kernels: 5.17 us -> 2.42 us  [decode_own(): pl.pallas_call(decode_own_kernel, grid_spec=pltpu.PrefetchScalarGridSpec(...]
    pallas_call x1, Pallas kernels: 5.59 us -> 3.34 us  [project(): pl.pallas_call(project_kernel, grid_spec=pltpu.PrefetchScalarGridSpec(num...]
    pallas_call x1, Pallas kernels: 4.64 us -> 2.47 us  [slopes(): pl.pallas_call(slope_kernel, grid_spec=pltpu.PrefetchScalarGridSpec(num_s...]
  transfers between devices with their start and end apart: 25 -> 25, of which waited for: 16 -> 17; matrix products, arithmetic and copies ran while one was open for 3% -> 1% of each run, Pallas kernels for 8% -> 4%
where the time goes in v2:
time: 154 us; the launch traced here: 153 us
  waiting for transfers between devices  58.3 us (38%)
  starting transfers between devices  46.4 us (30%)
  Pallas kernels  36.6 us (24%)
  local copies, waits for them, and re-layouts  8.87 us (6%)
  other arithmetic  2.03 us (1%)
    ppermute x18, waiting for transfers between devices, send(): return lax.ppermute(value, 'seq', moves(**step))  34.9 us
    ppermute x18, starting transfers between devices, send(): return lax.ppermute(value, 'seq', moves(**step))  26.3 us
    ppermute x5, waiting for transfers between devices, swap(): return lax.ppermute(value, 'head', [(0, 1), (1, 0)])  23.4 us
    ppermute x5, starting transfers between devices, swap(): return lax.ppermute(value, 'head', [(0, 1), (1, 0)])  15.8 us
    pallas_call x1, Pallas kernels, attend(): pl.pallas_call(attend_kernel, grid=(2,), in_specs=[pl.BlockSpec(memory_sp...  9.99 us
    unnamed x22, local copies, waits for them, and re-layouts  7.21 us
    pallas_call x2, Pallas kernels, backward(): pl.pallas_call(backward_kernel, grid_spec=pltpu.PrefetchScalarGridSpec(nu...  6.49 us
    pallas_call x1, Pallas kernels, encode(): pl.pallas_call(encoder_kernel, grid_spec=pltpu.PrefetchScalarGridSpec(num...  4.57 us
  transfers between devices with their start and end apart: 25, of which 17 were waited for; matrix products, arithmetic and copies ran while one was open for 1% of the time, Pallas kernels for 4%

profile of v2, /device:TPU:0, one launch (start us, length us, event | category | flops | bytes accessed | tf_op | source)
XLA Modules:
  0.0 153.1 jit_solution(7859967410766531379)
XLA Ops:
  0.6 0.9 add_convert_fusion
  1.5 0.8 fusion
  2.3 1.3 collective-permute-start
  3.6 3.0 %collective-permute-start.1 = (bf16[1,1792]{1,0:T(2,128)(2,1)S(1)}, bf16[1,1792]{1,0:T(2,128)(2,1)S(1)}, u32[]{:S(2)}, u32[]{:S(2)}) collective-permute-start(bf16[1,1792]{1,0:T(2,128)(2,1)S(1)} %pad_maximum_fusion.4), channel_id=1, source_target_pairs={{0,2},{2,4},{4,6},{6,8},{8,10},{10,12},{12,14},{14,16},{16,18},{18... | collective-permute-start | bytes 10760 | tf_op jit(solution)/shard_map/ppermute | solution.py:537
  6.7 0.9 fusion.3
  7.6 0.1 pad_add_fusion.ids
  7.6 0.1 pad.13.clone
  7.8 0.1 pad_maximum_fusion.2.codes
  7.9 3.0 %copy-done.1 = bf16[3,1536,768]{2,1,0:T(8,128)(2,1)S(1)} copy-done((bf16[3,1536,768]{2,1,0:T(8,128)(2,1)S(1)}, bf16[3,1536,768]{2,1,0:T(8,128)(2,1)}, u32[]{:S(2)}) %copy-start.1) | copy-done | bytes 7077912
  10.9 1.1 copy-done.4
  12.0 4.6 %encode.1 = (bf16[272,768]{1,0:T(8,128)(2,1)S(1)}, f32[136,128]{1,0:T(8,128)S(1)}) custom-call(s32[3]{0:T(128)S(1)} %pad_add_fusion.ids, bf16[136,128]{1,0:T(8,128)(2,1)S(1)} %pad_maximum_fusion.2.codes, bf16[256,1536]{1,0:T(8,128)(2,1)S(1)} %copy-done.4, bf16[3,1536,768]{2,1,0:T(8,128)(2,1)S(1)} %copy-done.1), custom_call_target="tpu_custom_call" | custom-call | flops 1925185536 | bytes 7077888 | tf_op jit(solution)/shard_map/encode/pallas_call | solution.py:100
  16.6 3.4 %collective-permute-start.2 = (f32[136,128]{1,0:T(8,128)S(1)}, f32[136,128]{1,0:T(8,128)S(1)}, u32[]{:S(2)}, u32[]{:S(2)}) collective-permute-start(f32[136,128]{1,0:T(8,128)S(1)} %get-tuple-element.16.mine), channel_id=1, source_target_pairs={{0,1},{1,0},{2,3},{3,2},{4,5},{5,4},{6,7},{7,6},{8,9},{9,8},{10,11... | collective-permute-start | bytes 208904 | tf_op jit(solution)/shard_map/ppermute | solution.py:509
  20.0 3.0 %collective-permute-done.2.theirs = f32[136,128]{1,0:T(8,128)S(1)} collective-permute-done((f32[136,128]{1,0:T(8,128)S(1)}, f32[136,128]{1,0:T(8,128)S(1)}, u32[]{:S(2)}, u32[]{:S(2)}) %collective-permute-start.2) | collective-permute-done | bytes 69664 | tf_op jit(solution)/shard_map/ppermute | solution.py:509
  23.0 0.7 normalize.1.mine
  23.6 3.6 %collective-permute-start.3 = (bf16[136,768]{1,0:T(8,128)(2,1)S(1)}, bf16[136,768]{1,0:T(8,128)(2,1)S(1)}, u32[]{:S(2)}, u32[]{:S(2)}) collective-permute-start(bf16[136,768]{1,0:T(8,128)(2,1)S(1)} %normalize.1.mine), channel_id=1, source_target_pairs={{0,1},{1,0},{2,3},{3,2},{4,5},{5,4},{6,7},{7,6},{8,9},{9,8},{10,11... | collective-permute-start | bytes 626696 | tf_op jit(solution)/shard_map/ppermute | solution.py:509
  27.2 5.4 %collective-permute-done.3.theirs = bf16[136,768]{1,0:T(8,128)(2,1)S(1)} collective-permute-done((bf16[136,768]{1,0:T(8,128)(2,1)S(1)}, bf16[136,768]{1,0:T(8,128)(2,1)S(1)}, u32[]{:S(2)}, u32[]{:S(2)}) %collective-permute-start.3) | collective-permute-done | bytes 208928 | tf_op jit(solution)/shard_map/ppermute | solution.py:509
  32.6 3.0 %copy-done.2 = bf16[3,1536,768]{2,1,0:T(8,128)(2,1)S(1)} copy-done((bf16[3,1536,768]{2,1,0:T(8,128)(2,1)S(1)}, bf16[3,1536,768]{2,1,0:T(8,128)(2,1)}, u32[]{:S(2)}) %copy-start.2) | copy-done | bytes 7077912
  35.6 3.3 %project.1 = (bf16[4,136,256]{2,1,0:T(8,128)(2,1)S(1)}, bf16[4,128,384]{2,1,0:T(8,128)(2,1)S(1)}) custom-call(s32[3]{0:T(128)S(1)} %pad_add_fusion.ids, bf16[136,768]{1,0:T(8,128)(2,1)S(1)} %normalize.1.mine, bf16[136,768]{1,0:T(8,128)(2,1)S(1)} %collective-permute-done.3.theirs, bf16[3,1536,768]{2,1,0:T(8,128)(2,1)S(1)} %copy-done.2), custom_call_target="tpu_custom_call" | custom-call | flops 962592768 | bytes 7077888 | tf_op jit(solution)/shard_map/project/pallas_call | solution.py:177
  39.0 9.2 %collective-permute-start.4 = (bf16[136,256]{1,0:T(8,128)(2,1)S(1)}, bf16[136,256]{1,0:T(8,128)(2,1)S(1)}, u32[]{:S(2)}, u32[]{:S(2)}) collective-permute-start(bf16[136,256]{1,0:T(8,128)(2,1)S(1)} %get-tuple-element.41), channel_id=1, source_target_pairs={{0,32},{2,34},{4,36},{6,38},{8,40},{10,42},{12,44},{14,46},{16,48}... | collective-permute-start | bytes 208904 | tf_op jit(solution)/shard_map/ppermute | solution.py:513
  48.2 1.7 %collective-permute-start.5 = (bf16[136,256]{1,0:T(8,128)(2,1)S(1)}, bf16[136,256]{1,0:T(8,128)(2,1)S(1)}, u32[]{:S(2)}, u32[]{:S(2)}) collective-permute-start(bf16[136,256]{1,0:T(8,128)(2,1)S(1)} %get-tuple-element.40), channel_id=1, source_target_pairs={{0,96},{2,98},{4,100},{6,102},{8,104},{10,106},{12,108},{14,110},{... | collective-permute-start | bytes 208904 | tf_op jit(solution)/shard_map/ppermute | solution.py:513
  49.9 1.9 %collective-permute-start.6 = (bf16[136,256]{1,0:T(8,128)(2,1)S(1)}, bf16[136,256]{1,0:T(8,128)(2,1)S(1)}, u32[]{:S(2)}, u32[]{:S(2)}) collective-permute-start(bf16[136,256]{1,0:T(8,128)(2,1)S(1)} %get-tuple-element.39), channel_id=1, source_target_pairs={{0,64},{2,66},{4,68},{6,70},{8,72},{10,74},{12,76},{14,78},{16,80}... | collective-permute-start | bytes 208904 | tf_op jit(solution)/shard_map/ppermute | solution.py:513
  51.8 1.0 collective-permute-start.10
  52.8 2.3 %collective-permute-start.11 = (bf16[128,384]{1,0:T(8,128)(2,1)S(1)}, bf16[128,384]{1,0:T(8,128)(2,1)S(1)}, u32[]{:S(2)}, u32[]{:S(2)}) collective-permute-start(bf16[128,384]{1,0:T(8,128)(2,1)S(1)} %get-tuple-element.32), channel_id=1, source_target_pairs={{0,96},{2,98},{4,100},{6,102},{8,104},{10,106},{12,108},{14,110},{... | collective-permute-start | bytes 294920 | tf_op jit(solution)/shard_map/ppermute | solution.py:513
  55.1 0.4 collective-permute-start.12
  55.5 0.1 collective-permute-done.6
  55.7 0.1 collective-permute-start.7
  55.8 1.9 %collective-permute-done.10 = bf16[128,384]{1,0:T(8,128)(2,1)S(1)} collective-permute-done((bf16[128,384]{1,0:T(8,128)(2,1)S(1)}, bf16[128,384]{1,0:T(8,128)(2,1)S(1)}, u32[]{:S(2)}, u32[]{:S(2)}) %collective-permute-start.10) | collective-permute-done | bytes 98336 | tf_op jit(solution)/shard_map/ppermute | solution.py:513
  57.7 0.6 collective-permute-done.11
  58.3 2.9 %collective-permute-done.12 = bf16[128,384]{1,0:T(8,128)(2,1)S(1)} collective-permute-done((bf16[128,384]{1,0:T(8,128)(2,1)S(1)}, bf16[128,384]{1,0:T(8,128)(2,1)S(1)}, u32[]{:S(2)}, u32[]{:S(2)}) %collective-permute-start.12) | collective-permute-done | bytes 98336 | tf_op jit(solution)/shard_map/ppermute | solution.py:513
  61.3 0.1 collective-permute-start.13
  61.4 3.2 %collective-permute-start.14 = (bf16[512,384]{1,0:T(8,128)(2,1)S(1)}, bf16[512,384]{1,0:T(8,128)(2,1)S(1)}, u32[]{:S(2)}, u32[]{:S(2)}) collective-permute-start(bf16[512,384]{1,0:T(8,128)(2,1)S(1)} %pad_maximum_fusion.k0), channel_id=1, source_target_pairs={{0,24},{2,26},{4,28},{6,30},{8,0},{10,2},{12,4},{14,6},{16,8},{18,... | collective-permute-start | bytes 1179656 | tf_op jit(solution)/shard_map/ppermute | solution.py:513
  64.6 0.3 collective-permute-start.9
  64.9 0.6 dynamic_slice.29.scale
  65.5 8.3 %collective-permute-done.8.q2 = bf16[544,256]{1,0:T(8,128)(2,1)S(1)} collective-permute-done((bf16[544,256]{1,0:T(8,128)(2,1)S(1)}, bf16[544,256]{1,0:T(8,128)(2,1)S(1)}, u32[]{:S(2)}, u32[]{:S(2)}) %collective-permute-start.8) | collective-permute-done | bytes 278560 | tf_op jit(solution)/shard_map/ppermute | solution.py:513
  73.8 0.8 collective-permute-done.9.q3
  74.6 2.7 %collective-permute-done.13.k1 = bf16[512,384]{1,0:T(8,128)(2,1)S(1)} collective-permute-done((bf16[512,384]{1,0:T(8,128)(2,1)S(1)}, bf16[512,384]{1,0:T(8,128)(2,1)S(1)}, u32[]{:S(2)}, u32[]{:S(2)}) %collective-permute-start.13) | collective-permute-done | bytes 393248 | tf_op jit(solution)/shard_map/ppermute | solution.py:513
  77.3 10.0 %attend.1 = (bf16[544,256]{1,0:T(8,128)(2,1)S(1)}, bf16[544,256]{1,0:T(8,128)(2,1)S(1)}, bf16[544,256]{1,0:T(8,128)(2,1)S(1)}, bf16[544,256]{1,0:T(8,128)(2,1)S(1)}) custom-call(f32[1]{0:T(128)} %dynamic_slice.29.scale, bf16[544,256]{1,0:T(8,128)(2,1)S(1)} %pad_maximum_fusion.1.q0, bf16[544,256]{1,0:T(8,128)(2,1)S(1)} %collective-permute-done.7.q1, ...), custom_call_target="tpu_custom_call" | custom-call | flops 4563402752 | bytes 4325376 | tf_op jit(solution)/shard_map/attend/pallas_call | solution.py:255
  87.3 0.1 collective-permute-start.16
  87.4 0.1 collective-permute-start.17
  87.5 1.8 %collective-permute-start.18 = (bf16[544,256]{1,0:T(8,128)(2,1)S(1)}, bf16[544,256]{1,0:T(8,128)(2,1)S(1)}, u32[]{:S(2)}, u32[]{:S(2)}) collective-permute-start(bf16[544,256]{1,0:T(8,128)(2,1)S(1)} %get-tuple-element.22), channel_id=1, source_target_pairs={{0,6},{2,4},{4,2},{6,0},{8,14},{10,12},{12,10},{14,8},{16,22},{18,... | collective-permute-start | bytes 835592 | tf_op jit(solution)/shard_map/ppermute | solution.py:513
  89.3 7.7 %collective-permute-done.17.a2 = bf16[544,256]{1,0:T(8,128)(2,1)S(1)} collective-permute-done((bf16[544,256]{1,0:T(8,128)(2,1)S(1)}, bf16[544,256]{1,0:T(8,128)(2,1)S(1)}, u32[]{:S(2)}, u32[]{:S(2)}) %collective-permute-start.17) | collective-permute-done | bytes 278560 | tf_op jit(solution)/shard_map/ppermute | solution.py:513
  97.0 5.0 %collective-permute-done.18.a3 = bf16[544,256]{1,0:T(8,128)(2,1)S(1)} collective-permute-done((bf16[544,256]{1,0:T(8,128)(2,1)S(1)}, bf16[544,256]{1,0:T(8,128)(2,1)S(1)}, u32[]{:S(2)}, u32[]{:S(2)}) %collective-permute-start.18) | collective-permute-done | bytes 278560 | tf_op jit(solution)/shard_map/ppermute | solution.py:513
  102.0 1.1 merge.1
  103.1 1.8 %collective-permute-start.19 = (bf16[136,256]{1,0:T(8,128)(2,1)S(1)}, bf16[136,256]{1,0:T(8,128)(2,1)S(1)}, u32[]{:S(2)}, u32[]{:S(2)}) collective-permute-start(bf16[136,256]{1,0:T(8,128)(2,1)S(1)} %get-tuple-element.36), channel_id=1, source_target_pairs={{0,96},{2,98},{4,100},{6,102},{8,104},{10,106},{12,108},{14,110},{... | collective-permute-start | bytes 208904 | tf_op jit(solution)/shard_map/ppermute | solution.py:513
  104.9 1.1 collective-permute-start.20
  106.0 1.3 collective-permute-start.21
  107.3 0.2 collective-permute-done.19.a1
  107.5 3.7 %collective-permute-done.20.a2 = bf16[136,256]{1,0:T(8,128)(2,1)S(1)} collective-permute-done((bf16[136,256]{1,0:T(8,128)(2,1)S(1)}, bf16[136,256]{1,0:T(8,128)(2,1)S(1)}, u32[]{:S(2)}, u32[]{:S(2)}) %collective-permute-start.20) | collective-permute-done | bytes 69664 | tf_op jit(solution)/shard_map/ppermute | solution.py:513
  111.2 0.8 collective-permute-done.21.a3
  112.1 1.5 output.3
  113.6 3.0 %collective-permute-start.22 = (bf16[136,768]{1,0:T(8,128)(2,1)S(1)}, bf16[136,768]{1,0:T(8,128)(2,1)S(1)}, u32[]{:S(2)}, u32[]{:S(2)}) collective-permute-start(bf16[136,768]{1,0:T(8,128)(2,1)S(1)} %output.3), channel_id=1, source_target_pairs={{0,1},{1,0},{2,3},{3,2},{4,5},{5,4},{6,7},{7,6},{8,9},{9,8},{10,11... | collective-permute-start | bytes 626696 | tf_op jit(solution)/shard_map/ppermute | solution.py:509
  116.5 0.1 pad.2.clone
  116.6 1.5 output.2.own
  118.1 3.7 %collective-permute-done.22.other = bf16[136,768]{1,0:T(8,128)(2,1)S(1)} collective-permute-done((bf16[136,768]{1,0:T(8,128)(2,1)S(1)}, bf16[136,768]{1,0:T(8,128)(2,1)S(1)}, u32[]{:S(2)}, u32[]{:S(2)}) %collective-permute-start.22) | collective-permute-done | bytes 208928 | tf_op jit(solution)/shard_map/ppermute | solution.py:509
  121.8 2.6 %decode_send.1 = (bf16[272,768]{1,0:T(8,128)(2,1)S(1)}, bf16[272,768]{1,0:T(8,128)(2,1)S(1)}) custom-call(s32[3]{0:T(128)S(1)} %pad_add_fusion.ids, f32[136,768]{1,0:T(8,128)S(1)} %output.2.own, bf16[136,768]{1,0:T(8,128)(2,1)S(1)} %collective-permute-done.22.other, bf16[272,768]{1,0:T(8,128)(2,1)S(1)} %get-tuple-element.15.encoded, ...), custom_call_target="tpu_custom_call" | custom-call | flops 962592768 | bytes 3538944 | tf_op jit(solution)/shard_map/decode_send/pallas_call | solution.py:343
  124.4 3.0 %collective-permute-start.23 = (bf16[272,768]{1,0:T(8,128)(2,1)S(1)}, bf16[272,768]{1,0:T(8,128)(2,1)S(1)}, u32[]{:S(2)}, u32[]{:S(2)}) collective-permute-start(bf16[272,768]{1,0:T(8,128)(2,1)S(1)} %get-tuple-element.24), channel_id=1, source_target_pairs={{0,1},{1,0},{2,3},{3,2},{4,5},{5,4},{6,7},{7,6},{8,9},{9,8},{10,11... | collective-permute-start | bytes 1253384 | tf_op jit(solution)/shard_map/ppermute | solution.py:509
  127.4 0.1 maximum_maximum_fusion.edges
  127.5 2.4 %decode_own.1.own = f32[272,768]{1,0:T(8,128)S(1)} custom-call(s32[3]{0:T(128)S(1)} %pad_add_fusion.ids, bf16[272,768]{1,0:T(8,128)(2,1)S(1)} %get-tuple-element.23.inputs, bf16[3,768,1536]{2,1,0:T(8,128)(2,1)S(1)} %bitcast.24), custom_call_target="tpu_custom_call" | custom-call | flops 962592768 | bytes 3538944 | tf_op jit(solution)/shard_map/decode_own/pallas_call | solution.py:373
  129.9 6.3 %collective-permute-done.23.other = bf16[272,768]{1,0:T(8,128)(2,1)S(1)} collective-permute-done((bf16[272,768]{1,0:T(8,128)(2,1)S(1)}, bf16[272,768]{1,0:T(8,128)(2,1)S(1)}, u32[]{:S(2)}, u32[]{:S(2)}) %collective-permute-start.23) | collective-permute-done | bytes 417824 | tf_op jit(solution)/shard_map/ppermute | solution.py:509
  136.2 2.5 %slopes.1 = (bf16[256,768]{1,0:T(8,128)(2,1)}, bf16[272,768]{1,0:T(8,128)(2,1)S(1)}, f32[128,768]{1,0:T(8,128)S(1)}) custom-call(s32[3]{0:T(128)S(1)} %pad_add_fusion.ids, f32[272,768]{1,0:T(8,128)S(1)} %decode_own.1.own, bf16[272,768]{1,0:T(8,128)(2,1)S(1)} %collective-permute-done.23.other, bf16[272,768]{1,0:T(8,128)(2,1)S(1)} %get-tuple-element.23.inputs, ...), custom_call_target="tpu_custom_call" | custom-call | flops 6266880 | bytes 2924544 | tf_op jit(solution)/shard_map/slopes/pallas_call | solution.py:428
  138.7 2.9 %collective-permute-start.24 = (bf16[272,768]{1,0:T(8,128)(2,1)S(1)}, bf16[272,768]{1,0:T(8,128)(2,1)S(1)}, u32[]{:S(2)}, u32[]{:S(2)}) collective-permute-start(bf16[272,768]{1,0:T(8,128)(2,1)S(1)} %get-tuple-element.26.slope), channel_id=1, source_target_pairs={{0,1},{1,0},{2,3},{3,2},{4,5},{5,4},{6,7},{7,6},{8,9},{9,8},{10,11... | collective-permute-start | bytes 1253384 | tf_op jit(solution)/shard_map/ppermute | solution.py:509
  141.6 2.9 %backward.2.start = f32[128,768]{1,0:T(8,128)S(1)} custom-call(s32[3]{0:T(128)S(1)} %pad_add_fusion.ids, bf16[272,768]{1,0:T(8,128)(2,1)S(1)} %get-tuple-element.26.slope, f32[128,768]{1,0:T(8,128)S(1)} %get-tuple-element.27.start, bf16[3,768,1536]{2,1,0:T(8,128)(2,1)S(1)} %bitcast.24), custom_call_target="tpu_custom_call" | custom-call | flops 962592768 | bytes 3538944 | tf_op jit(solution)/shard_map/backward/pallas_call | solution.py:473
  144.5 5.0 %collective-permute-done.24.slope = bf16[272,768]{1,0:T(8,128)(2,1)S(1)} collective-permute-done((bf16[272,768]{1,0:T(8,128)(2,1)S(1)}, bf16[272,768]{1,0:T(8,128)(2,1)S(1)}, u32[]{:S(2)}, u32[]{:S(2)}) %collective-permute-start.24) | collective-permute-done | bytes 417824 | tf_op jit(solution)/shard_map/ppermute | solution.py:509
  149.5 3.6 %backward.3 = bf16[128,768]{1,0:T(8,128)(2,1)} custom-call(s32[3]{0:T(128)S(1)} %pad_add_fusion.ids, bf16[272,768]{1,0:T(8,128)(2,1)S(1)} %collective-permute-done.24.slope, f32[128,768]{1,0:T(8,128)S(1)} %backward.2.start, bf16[3,768,1536]{2,1,0:T(8,128)(2,1)S(1)} %bitcast.24), custom_call_target="tpu_custom_call" | custom-call | flops 962592768 | bytes 3538944 | tf_op jit(solution)/shard_map/backward/pallas_call | solution.py:473
  (49 shorter events, 0.3 us)
Async XLA Ops:
  0.6 19.4 %copy-start.7 = (f32[1536]{0:T(1024)S(1)}, f32[1536]{0:T(1024)}, u32[]{:S(2)}) copy-start(f32[1536]{0:T(1024)} %param.12) | copy-start | bytes 18436
  2.3 5.4 %collective-permute-start = (bf16[1,1792]{1,0:T(2,128)(2,1)S(1)}, bf16[1,1792]{1,0:T(2,128)(2,1)S(1)}, u32[]{:S(2)}, u32[]{:S(2)}) collective-permute-start(bf16[1,1792]{1,0:T(2,128)(2,1)S(1)} %pad_maximum_fusion.3), channel_id=1, source_target_pairs={{2,0},{4,2},{6,4},{8,6},{10,8},{12,10},{14,12},{16,14},{18,16},{20... | collective-permute-start | bytes 10760 | tf_op jit(solution)/shard_map/ppermute | solution.py:538
  3.6 4.1 %collective-permute-start.1 = (bf16[1,1792]{1,0:T(2,128)(2,1)S(1)}, bf16[1,1792]{1,0:T(2,128)(2,1)S(1)}, u32[]{:S(2)}, u32[]{:S(2)}) collective-permute-start(bf16[1,1792]{1,0:T(2,128)(2,1)S(1)} %pad_maximum_fusion.4), channel_id=1, source_target_pairs={{0,2},{2,4},{4,6},{6,8},{8,10},{10,12},{12,14},{14,16},{16,18},{18... | collective-permute-start | bytes 10760 | tf_op jit(solution)/shard_map/ppermute | solution.py:537
  7.7 108.9 %copy-start.6 = (bf16[1,1792]{1,0:T(2,128)(2,1)}, bf16[1,1792]{1,0:T(2,128)(2,1)S(1)}, u32[]{:S(2)}) copy-start(bf16[1,1792]{1,0:T(2,128)(2,1)S(1)} %collective-permute-done) | copy-start | bytes 10756
  7.7 108.9 %copy-start.5 = (bf16[1,1792]{1,0:T(2,128)(2,1)}, bf16[1,1792]{1,0:T(2,128)(2,1)S(1)}, u32[]{:S(2)}) copy-start(bf16[1,1792]{1,0:T(2,128)(2,1)S(1)} %collective-permute-done.1) | copy-start | bytes 10756
  7.9 3.0 %copy-start.1 = (bf16[3,1536,768]{2,1,0:T(8,128)(2,1)S(1)}, bf16[3,1536,768]{2,1,0:T(8,128)(2,1)}, u32[]{:S(2)}) copy-start(bf16[3,1536,768]{2,1,0:T(8,128)(2,1)} %weight.8) | copy-start | bytes 21233668
  10.9 1.1 copy-start.4
  16.6 48.3 %copy-start.8 = (f32[4]{0:T(128)S(1)}, f32[4]{0:T(128)}, u32[]{:S(2)}) copy-start(f32[4]{0:T(128)} %param.14) | copy-start | bytes 52
  16.6 6.3 %collective-permute-start.2 = (f32[136,128]{1,0:T(8,128)S(1)}, f32[136,128]{1,0:T(8,128)S(1)}, u32[]{:S(2)}, u32[]{:S(2)}) collective-permute-start(f32[136,128]{1,0:T(8,128)S(1)} %get-tuple-element.16.mine), channel_id=1, source_target_pairs={{0,1},{1,0},{2,3},{3,2},{4,5},{5,4},{6,7},{7,6},{8,9},{9,8},{10,11... | collective-permute-start | bytes 208904 | tf_op jit(solution)/shard_map/ppermute | solution.py:509
  23.6 9.0 %collective-permute-start.3 = (bf16[136,768]{1,0:T(8,128)(2,1)S(1)}, bf16[136,768]{1,0:T(8,128)(2,1)S(1)}, u32[]{:S(2)}, u32[]{:S(2)}) collective-permute-start(bf16[136,768]{1,0:T(8,128)(2,1)S(1)} %normalize.1.mine), channel_id=1, source_target_pairs={{0,1},{1,0},{2,3},{3,2},{4,5},{5,4},{6,7},{7,6},{8,9},{9,8},{10,11... | collective-permute-start | bytes 626696 | tf_op jit(solution)/shard_map/ppermute | solution.py:509
  32.6 3.0 %copy-start.2 = (bf16[3,1536,768]{2,1,0:T(8,128)(2,1)S(1)}, bf16[3,1536,768]{2,1,0:T(8,128)(2,1)}, u32[]{:S(2)}) copy-start(bf16[3,1536,768]{2,1,0:T(8,128)(2,1)} %weight.9) | copy-start | bytes 21233668
  39.0 16.1 %collective-permute-start.4 = (bf16[136,256]{1,0:T(8,128)(2,1)S(1)}, bf16[136,256]{1,0:T(8,128)(2,1)S(1)}, u32[]{:S(2)}, u32[]{:S(2)}) collective-permute-start(bf16[136,256]{1,0:T(8,128)(2,1)S(1)} %get-tuple-element.41), channel_id=1, source_target_pairs={{0,32},{2,34},{4,36},{6,38},{8,40},{10,42},{12,44},{14,46},{16,48}... | collective-permute-start | bytes 208904 | tf_op jit(solution)/shard_map/ppermute | solution.py:513
  48.2 7.3 %collective-permute-start.5 = (bf16[136,256]{1,0:T(8,128)(2,1)S(1)}, bf16[136,256]{1,0:T(8,128)(2,1)S(1)}, u32[]{:S(2)}, u32[]{:S(2)}) collective-permute-start(bf16[136,256]{1,0:T(8,128)(2,1)S(1)} %get-tuple-element.40), channel_id=1, source_target_pairs={{0,96},{2,98},{4,100},{6,102},{8,104},{10,106},{12,108},{14,110},{... | collective-permute-start | bytes 208904 | tf_op jit(solution)/shard_map/ppermute | solution.py:513
  49.9 5.8 %collective-permute-start.6 = (bf16[136,256]{1,0:T(8,128)(2,1)S(1)}, bf16[136,256]{1,0:T(8,128)(2,1)S(1)}, u32[]{:S(2)}, u32[]{:S(2)}) collective-permute-start(bf16[136,256]{1,0:T(8,128)(2,1)S(1)} %get-tuple-element.39), channel_id=1, source_target_pairs={{0,64},{2,66},{4,68},{6,70},{8,72},{10,74},{12,76},{14,78},{16,80}... | collective-permute-start | bytes 208904 | tf_op jit(solution)/shard_map/ppermute | solution.py:513
  51.8 5.9 %collective-permute-start.10 = (bf16[128,384]{1,0:T(8,128)(2,1)S(1)}, bf16[128,384]{1,0:T(8,128)(2,1)S(1)}, u32[]{:S(2)}, u32[]{:S(2)}) collective-permute-start(bf16[128,384]{1,0:T(8,128)(2,1)S(1)} %get-tuple-element.33), channel_id=1, source_target_pairs={{0,32},{2,34},{4,36},{6,38},{8,40},{10,42},{12,44},{14,46},{16,48}... | collective-permute-start | bytes 294920 | tf_op jit(solution)/shard_map/ppermute | solution.py:513
  52.8 5.6 %collective-permute-start.11 = (bf16[128,384]{1,0:T(8,128)(2,1)S(1)}, bf16[128,384]{1,0:T(8,128)(2,1)S(1)}, u32[]{:S(2)}, u32[]{:S(2)}) collective-permute-start(bf16[128,384]{1,0:T(8,128)(2,1)S(1)} %get-tuple-element.32), channel_id=1, source_target_pairs={{0,96},{2,98},{4,100},{6,102},{8,104},{10,106},{12,108},{14,110},{... | collective-permute-start | bytes 294920 | tf_op jit(solution)/shard_map/ppermute | solution.py:513
  55.1 6.1 %collective-permute-start.12 = (bf16[128,384]{1,0:T(8,128)(2,1)S(1)}, bf16[128,384]{1,0:T(8,128)(2,1)S(1)}, u32[]{:S(2)}, u32[]{:S(2)}) collective-permute-start(bf16[128,384]{1,0:T(8,128)(2,1)S(1)} %get-tuple-element.31), channel_id=1, source_target_pairs={{0,64},{2,66},{4,68},{6,70},{8,72},{10,74},{12,76},{14,78},{16,80}... | collective-permute-start | bytes 294920 | tf_op jit(solution)/shard_map/ppermute | solution.py:513
  55.7 8.9 %collective-permute-start.7 = (bf16[544,256]{1,0:T(8,128)(2,1)S(1)}, bf16[544,256]{1,0:T(8,128)(2,1)S(1)}, u32[]{:S(2)}, u32[]{:S(2)}) collective-permute-start(bf16[544,256]{1,0:T(8,128)(2,1)S(1)} %pad_maximum_fusion.1.q0), channel_id=1, source_target_pairs={{0,2},{2,0},{4,6},{6,4},{8,10},{10,8},{12,14},{14,12},{16,18},{18,... | collective-permute-start | bytes 835592 | tf_op jit(solution)/shard_map/ppermute | solution.py:513
  61.3 16.0 %collective-permute-start.13 = (bf16[512,384]{1,0:T(8,128)(2,1)S(1)}, bf16[512,384]{1,0:T(8,128)(2,1)S(1)}, u32[]{:S(2)}, u32[]{:S(2)}) collective-permute-start(bf16[512,384]{1,0:T(8,128)(2,1)S(1)} %pad_maximum_fusion.k0), channel_id=1, source_target_pairs={{0,8},{2,10},{4,12},{6,14},{8,16},{10,18},{12,20},{14,22},{16,24},... | collective-permute-start | bytes 1179656 | tf_op jit(solution)/shard_map/ppermute | solution.py:513
  61.4 15.9 %collective-permute-start.14 = (bf16[512,384]{1,0:T(8,128)(2,1)S(1)}, bf16[512,384]{1,0:T(8,128)(2,1)S(1)}, u32[]{:S(2)}, u32[]{:S(2)}) collective-permute-start(bf16[512,384]{1,0:T(8,128)(2,1)S(1)} %pad_maximum_fusion.k0), channel_id=1, source_target_pairs={{0,24},{2,26},{4,28},{6,30},{8,0},{10,2},{12,4},{14,6},{16,8},{18,... | collective-permute-start | bytes 1179656 | tf_op jit(solution)/shard_map/ppermute | solution.py:513
  64.6 12.7 %collective-permute-start.15 = (bf16[512,384]{1,0:T(8,128)(2,1)S(1)}, bf16[512,384]{1,0:T(8,128)(2,1)S(1)}, u32[]{:S(2)}, u32[]{:S(2)}) collective-permute-start(bf16[512,384]{1,0:T(8,128)(2,1)S(1)} %pad_maximum_fusion.k0), channel_id=1, source_target_pairs={{0,16},{2,18},{4,20},{6,22},{8,24},{10,26},{12,28},{14,30},{16,0},... | collective-permute-start | bytes 1179656 | tf_op jit(solution)/shard_map/ppermute | solution.py:513
  64.6 9.2 %collective-permute-start.8 = (bf16[544,256]{1,0:T(8,128)(2,1)S(1)}, bf16[544,256]{1,0:T(8,128)(2,1)S(1)}, u32[]{:S(2)}, u32[]{:S(2)}) collective-permute-start(bf16[544,256]{1,0:T(8,128)(2,1)S(1)} %pad_maximum_fusion.1.q0), channel_id=1, source_target_pairs={{0,4},{2,6},{4,0},{6,2},{8,12},{10,14},{12,8},{14,10},{16,20},{18,... | collective-permute-start | bytes 835592 | tf_op jit(solution)/shard_map/ppermute | solution.py:513
  64.6 10.0 %collective-permute-start.9 = (bf16[544,256]{1,0:T(8,128)(2,1)S(1)}, bf16[544,256]{1,0:T(8,128)(2,1)S(1)}, u32[]{:S(2)}, u32[]{:S(2)}) collective-permute-start(bf16[544,256]{1,0:T(8,128)(2,1)S(1)} %pad_maximum_fusion.1.q0), channel_id=1, source_target_pairs={{0,6},{2,4},{4,2},{6,0},{8,14},{10,12},{12,10},{14,8},{16,22},{18,... | collective-permute-start | bytes 835592 | tf_op jit(solution)/shard_map/ppermute | solution.py:513
  64.9 56.9 %slice-start = ((s8[7077888]{0:T(1024)(128)(4,1)}), s8[4194304]{0:T(1024)(128)(4,1)S(1)}, s32[]{:S(2)}) async-start(s8[7077888]{0:T(1024)(128)(4,1)} %bitcast.23), calls=%async_computation | async-start | bytes 8388608
  65.5 46.6 %copy-start = (bf16[768,1536]{1,0:T(8,128)(2,1)S(1)}, bf16[768,1536]{1,0:T(8,128)(2,1)}, u32[]{:S(2)}) copy-start(bf16[768,1536]{1,0:T(8,128)(2,1)} %weight.11) | copy-start | bytes 7077892
  65.5 56.3 %slice-start.1 = ((s8[7077888]{0:T(1024)(128)(4,1)}), s8[2883584]{0:T(1024)(128)(4,1)S(1)}, s32[]{:S(2)}) async-start(s8[7077888]{0:T(1024)(128)(4,1)} %bitcast.23), calls=%async_computation.1 | async-start | bytes 5767168
  87.3 2.0 %collective-permute-start.16 = (bf16[544,256]{1,0:T(8,128)(2,1)S(1)}, bf16[544,256]{1,0:T(8,128)(2,1)S(1)}, u32[]{:S(2)}, u32[]{:S(2)}) collective-permute-start(bf16[544,256]{1,0:T(8,128)(2,1)S(1)} %get-tuple-element.20), channel_id=1, source_target_pairs={{0,2},{2,0},{4,6},{6,4},{8,10},{10,8},{12,14},{14,12},{16,18},{18,... | collective-permute-start | bytes 835592 | tf_op jit(solution)/shard_map/ppermute | solution.py:513
  87.4 9.5 %collective-permute-start.17 = (bf16[544,256]{1,0:T(8,128)(2,1)S(1)}, bf16[544,256]{1,0:T(8,128)(2,1)S(1)}, u32[]{:S(2)}, u32[]{:S(2)}) collective-permute-start(bf16[544,256]{1,0:T(8,128)(2,1)S(1)} %get-tuple-element.21), channel_id=1, source_target_pairs={{0,4},{2,6},{4,0},{6,2},{8,12},{10,14},{12,8},{14,10},{16,20},{18,... | collective-permute-start | bytes 835592 | tf_op jit(solution)/shard_map/ppermute | solution.py:513
  87.5 14.5 %collective-permute-start.18 = (bf16[544,256]{1,0:T(8,128)(2,1)S(1)}, bf16[544,256]{1,0:T(8,128)(2,1)S(1)}, u32[]{:S(2)}, u32[]{:S(2)}) collective-permute-start(bf16[544,256]{1,0:T(8,128)(2,1)S(1)} %get-tuple-element.22), channel_id=1, source_target_pairs={{0,6},{2,4},{4,2},{6,0},{8,14},{10,12},{12,10},{14,8},{16,22},{18,... | collective-permute-start | bytes 835592 | tf_op jit(solution)/shard_map/ppermute | solution.py:513
  103.1 4.5 %collective-permute-start.19 = (bf16[136,256]{1,0:T(8,128)(2,1)S(1)}, bf16[136,256]{1,0:T(8,128)(2,1)S(1)}, u32[]{:S(2)}, u32[]{:S(2)}) collective-permute-start(bf16[136,256]{1,0:T(8,128)(2,1)S(1)} %get-tuple-element.36), channel_id=1, source_target_pairs={{0,96},{2,98},{4,100},{6,102},{8,104},{10,106},{12,108},{14,110},{... | collective-permute-start | bytes 208904 | tf_op jit(solution)/shard_map/ppermute | solution.py:513
  104.9 6.4 %collective-permute-start.20 = (bf16[136,256]{1,0:T(8,128)(2,1)S(1)}, bf16[136,256]{1,0:T(8,128)(2,1)S(1)}, u32[]{:S(2)}, u32[]{:S(2)}) collective-permute-start(bf16[136,256]{1,0:T(8,128)(2,1)S(1)} %get-tuple-element.35), channel_id=1, source_target_pairs={{0,64},{2,66},{4,68},{6,70},{8,72},{10,74},{12,76},{14,78},{16,80}... | collective-permute-start | bytes 208904 | tf_op jit(solution)/shard_map/ppermute | solution.py:513
  106.0 6.1 %collective-permute-start.21 = (bf16[136,256]{1,0:T(8,128)(2,1)S(1)}, bf16[136,256]{1,0:T(8,128)(2,1)S(1)}, u32[]{:S(2)}, u32[]{:S(2)}) collective-permute-start(bf16[136,256]{1,0:T(8,128)(2,1)S(1)} %get-tuple-element.34), channel_id=1, source_target_pairs={{0,32},{2,34},{4,36},{6,38},{8,40},{10,42},{12,44},{14,46},{16,48}... | collective-permute-start | bytes 208904 | tf_op jit(solution)/shard_map/ppermute | solution.py:513
  113.6 8.2 %collective-permute-start.22 = (bf16[136,768]{1,0:T(8,128)(2,1)S(1)}, bf16[136,768]{1,0:T(8,128)(2,1)S(1)}, u32[]{:S(2)}, u32[]{:S(2)}) collective-permute-start(bf16[136,768]{1,0:T(8,128)(2,1)S(1)} %output.3), channel_id=1, source_target_pairs={{0,1},{1,0},{2,3},{3,2},{4,5},{5,4},{6,7},{7,6},{8,9},{9,8},{10,11... | collective-permute-start | bytes 626696 | tf_op jit(solution)/shard_map/ppermute | solution.py:509
  116.6 10.8 %slice-start.2 = ((bf16[1,1792]{1,0:T(2,128)(2,1)}), bf16[1,1536]{1,0:T(2,128)(2,1)S(1)}, s32[]{:S(2)}) async-start(bf16[1,1792]{1,0:T(2,128)(2,1)} %copy-done.5), calls=%async_computation.2 | async-start | bytes 12288 | tf_op jit(solution)/shard_map/slice | solution.py:544
  116.6 10.8 %slice-start.3 = ((bf16[1,1792]{1,0:T(2,128)(2,1)}), bf16[1,1536]{1,0:T(2,128)(2,1)S(1)}, s32[]{:S(2)}) async-start(bf16[1,1792]{1,0:T(2,128)(2,1)} %copy-done.6), calls=%async_computation.3 | async-start | bytes 12288 | tf_op jit(solution)/shard_map/slice | solution.py:544
  118.1 18.1 %copy-start.3 = (bf16[256,1536]{1,0:T(8,128)(2,1)S(1)}, bf16[256,1536]{1,0:T(8,128)(2,1)}, u32[]{:S(2)}) copy-start(bf16[256,1536]{1,0:T(8,128)(2,1)} %grad.1) | copy-start | bytes 2359300
  124.4 11.8 %collective-permute-start.23 = (bf16[272,768]{1,0:T(8,128)(2,1)S(1)}, bf16[272,768]{1,0:T(8,128)(2,1)S(1)}, u32[]{:S(2)}, u32[]{:S(2)}) collective-permute-start(bf16[272,768]{1,0:T(8,128)(2,1)S(1)} %get-tuple-element.24), channel_id=1, source_target_pairs={{0,1},{1,0},{2,3},{3,2},{4,5},{5,4},{6,7},{7,6},{8,9},{9,8},{10,11... | collective-permute-start | bytes 1253384 | tf_op jit(solution)/shard_map/ppermute | solution.py:509
  138.7 10.8 %collective-permute-start.24 = (bf16[272,768]{1,0:T(8,128)(2,1)S(1)}, bf16[272,768]{1,0:T(8,128)(2,1)S(1)}, u32[]{:S(2)}, u32[]{:S(2)}) collective-permute-start(bf16[272,768]{1,0:T(8,128)(2,1)S(1)} %get-tuple-element.26.slope), channel_id=1, source_target_pairs={{0,1},{1,0},{2,3},{3,2},{4,5},{5,4},{6,7},{7,6},{8,9},{9,8},{10,11... | collective-permute-start | bytes 1253384 | tf_op jit(solution)/shard_map/ppermute | solution.py:509

commit v3 on v0

v3 whole, which is shorter than its diff:
```python
import functools

import jax
import jax.numpy as jnp
from jax import lax
from jax.experimental import pallas as pl
from jax.experimental.pallas import tpu as pltpu
from jax.sharding import PartitionSpec as P

BF16 = jnp.bfloat16
F32 = jnp.float32
ROWS = 136
OWN = 128
TILE = 256
HEAD = 192
EPS = 1e-06
MIB = 1024 * 1024


def params(mib):
    return pltpu.CompilerParams(vmem_limit_bytes=mib * MIB)


def dot(a, b):
    return jnp.dot(a, b, preferred_element_type=F32)


def dot_t(a, b):
    return lax.dot_general(a, b, (((1,), (1,)), ((), ())), preferred_element_type=F32)


def cost(flops, nbytes):
    return pl.CostEstimate(flops=int(flops), bytes_accessed=int(nbytes), transcendentals=0)


def shape(dims, dtype):
    return jax.ShapeDtypeStruct(dims, dtype)


VM = pl.BlockSpec(memory_space=pltpu.VMEM)
SM = pl.BlockSpec(memory_space=pltpu.SMEM)
HBM = pl.BlockSpec(memory_space=pltpu.HBM)


def above(rows):
    return pltpu.roll(rows, 1, 0)


def below(rows):
    return pltpu.roll(rows, ROWS - 1, 0)


def lanes(at, size):
    return pl.ds(pl.multiple_of(at, size), size)


def tiles(count, body):
    lax.fori_loop(0, count, lambda i, carry: (body(i), carry)[1], 0)


def gelu_tanh(x):
    return jnp.tanh(0.7978845608028654 * (x + 0.044715 * (x * x * x)))


def conv_taps(rows, weight):
    first, mid, last = (dot(rows, weight(t)) for t in range(3))
    even = above(first[ROWS:]) + mid[:ROWS] + last[ROWS:]
    odd = first[:ROWS] + mid[ROWS:] + below(last[:ROWS])
    return jnp.concatenate([even, odd], axis=0)


def prepare_kernel(bases, grad, weight, codes, last, first, loaded, sem):
    copy = pltpu.make_async_copy(weight, loaded, sem)
    copy.start()
    code = (bases[...] + 1).astype(F32)
    codes[...] = code.astype(BF16)
    feats = grad.shape[1]
    last[:, :feats] = grad[2 * OWN - 16 :, :].astype(F32)[8:].astype(BF16)
    last[:, feats:] = code[OWN - 8 :].astype(BF16)
    first[:, :feats] = grad[:16, :].astype(F32)[:8].astype(BF16)
    first[:, feats:] = code[:8].astype(BF16)
    copy.wait()


def prepare(bases, grad, weight):
    width = grad.shape[1] + 128
    return pl.pallas_call(
        prepare_kernel,
        in_specs=[VM, VM, HBM],
        out_specs=[VM] * 4,
        out_shape=[
            shape((OWN, 128), BF16),
            shape((8, width), BF16),
            shape((8, width), BF16),
            pltpu.VMEM(weight.shape, BF16),
        ],
        scratch_shapes=[pltpu.SemaphoreType.DMA(())],
        compiler_params=params(8),
        cost_estimate=cost(10**6, weight.size * 2),
        name="prepare",
    )(bases, grad, pltpu.with_memory_space_constraint(weight, pltpu.HBM))


def encode_kernel(ids, codes, before, after, stem, weight, ahead, encoded, loaded, embedded, sem):
    copy = pltpu.make_async_copy(ahead, loaded, sem)
    copy.start()
    patch = stem.shape[0] // 4
    feats = stem.shape[1]
    half = weight.shape[2]
    row = lax.broadcasted_iota(jnp.int32, (2 * patch, 4 * patch), 0)
    col = lax.broadcasted_iota(jnp.int32, (2 * patch, 4 * patch), 1)
    place = lax.broadcasted_iota(jnp.int32, (ROWS - OWN, 128), 0)
    halo = jnp.where(place >= 6, before[:, feats:].astype(F32), 0.0)
    halo = jnp.where(place < 2, after[:, feats:].astype(F32), halo)
    code = jnp.concatenate([codes[...].astype(F32), halo], axis=0).astype(BF16)
    spread = [
        dot(code, (row == col // 4 + offset).astype(F32).astype(BF16)) for offset in (0, patch)
    ]
    spread = jnp.concatenate(spread, axis=0)
    base = lax.broadcasted_iota(jnp.int32, spread.shape, 1) % 4 + 1
    onehot = (spread == base.astype(F32)).astype(F32).astype(BF16)

    def embed(i):
        at = lanes(i * TILE, TILE)
        embedded[:, at] = dot(onehot, stem[:, at]).astype(BF16)

    tiles(feats // TILE, embed)

    def convolve(i):
        at = lanes(i * TILE, TILE)
        pre = conv_taps(embedded[...], lambda t: weight[t, :, at])
        mine = embedded[:, lanes(ids[0] * half + i * TILE, TILE)].astype(F32)
        encoded[:, at] = (mine + 0.5 * pre * (1.0 + gelu_tanh(pre))).astype(BF16)

    tiles(half // TILE, convolve)
    copy.wait()


def encode(ids, codes, before, after, stem, weight, ahead):
    half = weight.shape[2]
    feats = stem.shape[1]
    return pl.pallas_call(
        encode_kernel,
        in_specs=[SM, VM, VM, VM, VM, VM, HBM],
        out_specs=[VM, VM],
        out_shape=[shape((2 * ROWS, half), BF16), pltpu.VMEM(ahead.shape, BF16)],
        scratch_shapes=[pltpu.VMEM((2 * ROWS, feats), BF16), pltpu.SemaphoreType.DMA(())],
        compiler_params=params(12),
        cost_estimate=cost(2 * 2 * ROWS * 3 * feats * half, weight.size * 4),
        name="encode",
    )(ids, codes, before, after, stem, weight, pltpu.with_memory_space_constraint(ahead, pltpu.HBM))


def project_kernel(ids, mine, theirs, gain, weight, queries, keyvals):
    half = mine.shape[1]
    near = lanes(ids[0] * half, half)
    far = lanes((1 - ids[0]) * half, half)

    def pairs(ref):
        enc = ref[...].astype(F32)
        return (enc[:ROWS] + enc[ROWS:]) * 0.5

    binned = pairs(mine), pairs(theirs)
    total = sum(jnp.sum(part * part, axis=1, keepdims=True) for part in binned)
    inverse = lax.rsqrt(total * (1.0 / (2 * half)) + EPS)
    here = (binned[0] * inverse * gain[:, near]).astype(BF16)
    there = (binned[1] * inverse * gain[:, far]).astype(BF16)
    low = lax.broadcasted_iota(jnp.int32, (ROWS, 128), 1) < 64
    for pair in range(2):
        at = slice(pair * 2 * HEAD, (pair + 1) * 2 * HEAD)
        rows = []
        for kind in range(3):
            both = dot(here, weight[kind, near, at]) + dot(there, weight[kind, far, at])
            both = both.astype(BF16).astype(F32)
            rows.append((both, pltpu.roll(both, 2 * HEAD - 64, 1)))
        for side in range(2):
            head = 2 * pair + side
            query, key, value = (
                (r[0][:, :128], r[0][:, 128:256]) if side == 0 else (r[1][:, 128:256], r[1][:, 256:384])
                for r in rows
            )
            queries[head, :, :128] = query[0].astype(BF16)
            queries[head, :, 128:] = jnp.where(low, query[1], 0.0).astype(BF16)
            keyvals[head, :, :128] = key[0][:OWN].astype(BF16)
            keyvals[head, :, 128:256] = value[0][:OWN].astype(BF16)
            tail = jnp.where(low, key[1], pltpu.roll(value[1], 64, 1))
            keyvals[head, :, 256:] = tail[:OWN].astype(BF16)


def project(ids, mine, theirs, gain, weight):
    return pl.pallas_call(
        project_kernel,
        in_specs=[SM, VM, VM, VM, VM],
        out_specs=[VM, VM],
        out_shape=[shape((4, ROWS, 256), BF16), shape((4, OWN, 384), BF16)],
        compiler_params=params(12),
        cost_estimate=cost(2 * ROWS * weight.size, weight.size * 2),
        name="project",
    )(ids, mine, theirs, gain, weight)


BLOCK = 2 * ROWS


def attend_kernel(count, resumed, final, scale, *refs):
    queries, refs = refs[:2], refs[2:]
    pieces, refs = refs[:count], refs[count:]
    if resumed:
        (old_mixed, old_stats), refs = refs[:2], refs[2:]
    outs, inverse = refs[:2], refs[2]
    chunk = pieces[0].shape[0]
    lane = lax.broadcasted_iota(jnp.int32, (8, 256), 1)
    ones = (lane < HEAD).astype(F32).astype(BF16)

    def keys(ref):
        return jnp.concatenate([ref[:, :128], ref[:, 256:]], axis=1)

    for at, ref in enumerate(pieces):
        key = keys(ref).astype(F32)
        square = key * key
        high = square.astype(BF16)
        rest = (square - high.astype(F32)).astype(BF16)
        total = dot_t(ones, high) + dot_t(ones, rest)
        inverse[:, at * chunk : (at + 1) * chunk] = lax.rsqrt(total * (1.0 / HEAD) + EPS)

    def block(i):
        for side, query_ref in enumerate(queries):
            span = query_ref.shape[0]
            rows = lanes(i * BLOCK, BLOCK)
            state = lanes(side * span + i * BLOCK, BLOCK)
            query = query_ref[rows, :]
            wide = query.astype(F32)
            own = lax.rsqrt(jnp.sum(wide * wide, axis=1, keepdims=True) * (1.0 / HEAD) + EPS)
            factor = own * (scale[0] * (1.0 / HEAD))
            scores = []
            peak = old_stats[state, 0:1] if resumed else None
            before = peak
            for at, ref in enumerate(pieces):
                part = dot_t(query, keys(ref)) * factor
                part = part * inverse[0:1, at * chunk : (at + 1) * chunk]
                top = jnp.max(part, axis=1, keepdims=True)
                peak = top if peak is None else jnp.maximum(peak, top)
                scores.append(part)
            total, mixed = None, None
            if resumed:
                shrink = jnp.exp(before - peak)
                total = old_stats[state, 64:65] * shrink
                mixed = old_mixed[state, :] * shrink
            for part, ref in zip(scores, pieces):
                exps = jnp.exp(part - peak)
                sums = jnp.sum(exps, axis=1, keepdims=True)
                values = jnp.concatenate([ref[:, 128:256], ref[:, 256:]], axis=1)
                term = dot(exps.astype(BF16), values)
                total = sums if total is None else total + sums
                mixed = term if mixed is None else mixed + term
            if not final:
                outs[0][state, :] = mixed
                half = lax.broadcasted_iota(jnp.int32, (BLOCK, 128), 1) < 64
                outs[1][state, :] = jnp.where(half, peak, total)
                continue
            mixed = mixed / total
            weight = peak + jnp.log(total)
            high = weight.astype(BF16).astype(F32)
            rest = weight - high
            mid = rest.astype(BF16).astype(F32)
            place = lax.broadcasted_iota(jnp.int32, mixed.shape, 1)
            mixed = jnp.where(place == 128, high, mixed)
            mixed = jnp.where(place == 129, mid, mixed)
            mixed = jnp.where(place == 130, rest - mid, mixed)
            outs[side][rows, :] = mixed.astype(BF16)

    tiles(queries[0].shape[0] // BLOCK, block)


def attend(scale, queries, pieces, state, final):
    rows = queries[0].shape[0]
    keys = len(pieces) * pieces[0].shape[0]
    if final:
        outs = [shape((rows, 256), BF16)] * 2
    else:
        outs = [shape((2 * rows, 256), F32), shape((2 * rows, 128), F32)]
    return pl.pallas_call(
        functools.partial(attend_kernel, len(pieces), bool(state), final),
        in_specs=[SM] + [VM] * (2 + len(pieces) + len(state)),
        out_specs=[VM] * 2,
        out_shape=outs,
        scratch_shapes=[pltpu.VMEM((8, keys), F32)],
        compiler_params=params(20),
        cost_estimate=cost(4 * 2 * rows * keys * 256, 8 * rows * 1024),
        name="attend",
    )(scale, *queries, *pieces, *state)


def merge_kernel(a0, a1, out):
    parts = [ref[...].astype(F32) for ref in (a0, a1)]
    logs = [p[:, 128:129] + p[:, 129:130] + p[:, 130:131] for p in parts]
    peak = functools.reduce(jnp.maximum, logs)
    shares = [jnp.exp(log - peak) for log in logs]
    total = sum(shares)
    mixed = sum(p * (share / total) for p, share in zip(parts, shares))
    mixed = jnp.concatenate([mixed[:, :128], pltpu.roll(mixed[:, 128:], 64, 1)], axis=1)
    for block in range(4):
        out[block] = mixed[block * ROWS : (block + 1) * ROWS].astype(BF16)


def merge(parts):
    return pl.pallas_call(
        merge_kernel,
        in_specs=[VM] * 2,
        out_specs=VM,
        out_shape=shape((4, ROWS, 256), BF16),
        compiler_params=params(8),
        cost_estimate=cost(20 * parts[0].size, 10 * parts[0].size),
        name="merge",
    )(*parts)


def output_kernel(mine, ids, heads, weight, out):
    half = out.shape[1]
    side = ids[0] if mine else 1 - ids[0]

    def tile(i):
        at = lanes(side * half + i * TILE, TILE)
        total = None
        for head in range(4):
            rows = weight[head * HEAD : (head + 1) * HEAD, at]
            term = dot(heads[head, :, :HEAD], rows)
            total = term if total is None else total + term
        out[:, lanes(i * TILE, TILE)] = total.astype(out.dtype)

    tiles(half // TILE, tile)


def output(ids, heads, weight, mine, dtype):
    half = weight.shape[1] // 2
    return pl.pallas_call(
        functools.partial(output_kernel, mine),
        in_specs=[SM, VM, VM],
        out_specs=VM,
        out_shape=shape((ROWS, half), dtype),
        compiler_params=params(6),
        cost_estimate=cost(2 * ROWS * weight.size // 2, weight.size),
        name="output",
    )(ids, heads, weight)


def decode_send_kernel(ids, own, other, encoded, weight, inputs, out):
    half = out.shape[1]

    def mix(i):
        at = lanes(i * TILE, TILE)
        enc = encoded[:, at].astype(F32)
        even, odd = enc[:ROWS], enc[ROWS:]
        binned = (even + odd) * 0.5
        block = (binned + (own[:, at] + other[:, at].astype(F32))).astype(BF16).astype(F32)
        row = lax.broadcasted_iota(jnp.int32, block.shape, 0)
        outside = ((ids[2] == 0) & (row == ROWS - 1)) | ((ids[2] == 63) & (row == OWN))
        even = jnp.where(outside, 0.0, block + even)
        odd = jnp.where(outside, 0.0, block + odd)
        inputs[:, at] = jnp.concatenate([even, odd], axis=0).astype(BF16)

    tiles(half // TILE, mix)

    def tile(i):
        at = lanes((1 - ids[0]) * half + i * TILE, TILE)
        out[:, lanes(i * TILE, TILE)] = conv_taps(inputs[...], lambda t: weight[t, :, at]).astype(BF16)

    tiles(half // TILE, tile)


def decode_send(ids, own, other, encoded, weight):
    half = weight.shape[1]
    return pl.pallas_call(
        decode_send_kernel,
        in_specs=[SM] + [VM] * 4,
        out_specs=[VM] * 2,
        out_shape=[shape((2 * ROWS, half), BF16)] * 2,
        compiler_params=params(8),
        cost_estimate=cost(2 * 2 * ROWS * weight.size // 2, weight.size),
        name="decode_send",
    )(ids, own, other, encoded, weight)


def decode_own_kernel(ids, inputs, weight, out):
    half = out.shape[1]

    def tile(i):
        at = lanes(ids[0] * half + i * TILE, TILE)
        out[:, lanes(i * TILE, TILE)] = conv_taps(inputs[...], lambda t: weight[t, :, at])

    tiles(half // TILE, tile)


def decode_own(ids, inputs, weight):
    half = weight.shape[1]
    return pl.pallas_call(
        decode_own_kernel,
        in_specs=[SM, VM, VM],
        out_specs=VM,
        out_shape=shape((2 * ROWS, half), F32),
        compiler_params=params(8),
        cost_estimate=cost(2 * 2 * ROWS * weight.size // 2, weight.size),
        name="decode_own",
    )(ids, inputs, weight)


def slope_kernel(ids, own, other, inputs, grad, before, after, decoded, slope, paired, wide):
    half = own.shape[1]

    def tile(i):
        at = lanes(i * 128, 128)
        column = lanes(ids[0] * half + i * 128, 128)
        pre = own[:, at] + other[:, at].astype(F32)
        tanh = gelu_tanh(pre)
        result = inputs[:, at].astype(F32) + 0.5 * pre * (1.0 + tanh)
        wide[0, pl.ds(0, OWN, 2), :] = result[:OWN]
        wide[0, pl.ds(1, OWN, 2), :] = result[ROWS : ROWS + OWN]
        decoded[:, at] = wide[0].astype(BF16)
        slant = 0.5 * (1.0 + tanh) + (0.5 * 0.7978845608028654) * pre * (1.0 - tanh * tanh) * (
            1.0 + (3 * 0.044715) * (pre * pre)
        )
        wide[1] = grad[:, column].astype(F32)
        even = wide[1, pl.ds(0, OWN, 2), :]
        odd = wide[1, pl.ds(1, OWN, 2), :]
        paired[:, at] = even + odd
        row = lax.broadcasted_iota(jnp.int32, (ROWS - OWN, 128), 0)
        even_edge = jnp.where(row == 0, after[:, column].astype(F32), 0.0)
        odd_edge = jnp.where(row == ROWS - OWN - 1, before[:, column].astype(F32), 0.0)
        cotangent = jnp.concatenate([even, even_edge, odd, odd_edge], axis=0)
        slope[:, at] = (cotangent * slant).astype(BF16)

    tiles(half // 128, tile)


def slopes(ids, own, other, inputs, grad, before, after):
    half = own.shape[1]
    return pl.pallas_call(
        slope_kernel,
        in_specs=[SM] + [VM] * 6,
        out_specs=[VM] * 3,
        out_shape=[
            shape((2 * OWN, half), BF16),
            shape((2 * ROWS, half), BF16),
            shape((OWN, half), F32),
        ],
        scratch_shapes=[pltpu.VMEM((2, 2 * OWN, 128), F32)],
        compiler_params=params(6),
        cost_estimate=cost(30 * own.size, 14 * own.size),
        name="slopes",
    )(ids, own, other, inputs, grad, before, after)


def backward_kernel(mine, ids, slope, start, weight, out, level, lower, upper):
    half = slope.shape[1]
    side = ids[0] if mine else 1 - ids[0]
    level[...] = jnp.zeros_like(level)
    lower[...] = jnp.zeros_like(lower)
    upper[...] = jnp.zeros_like(upper)

    def tile(i):
        at = lanes(side * half + i * TILE, TILE)
        part = slope[:, lanes(i * TILE, TILE)]
        first, mid, last = (dot_t(part, weight[t, :, at]) for t in range(3))
        level[...] += first[ROWS:] + mid[:ROWS] + mid[ROWS:] + last[:ROWS]
        lower[...] += first[:ROWS]
        upper[...] += last[ROWS:]

    tiles(half // TILE, tile)
    total = level[...] + below(lower[...]) + above(upper[...])
    out[...] = (start[...] + total[:OWN]).astype(out.dtype)


def backward(ids, slope, start, weight, mine, dtype):
    half = weight.shape[1]
    return pl.pallas_call(
        functools.partial(backward_kernel, mine),
        in_specs=[SM] + [VM] * 3,
        out_specs=VM,
        out_shape=shape((OWN, half), dtype),
        scratch_shapes=[pltpu.VMEM((ROWS, half), F32)] * 3,
        compiler_params=params(10),
        cost_estimate=cost(2 * 2 * ROWS * weight.size // 2, weight.size),
        name="backward",
    )(ids, slope, start, weight)


def place(at):
    return at // 16, at // 4 % 4, at // 2 % 2, at % 2


def moves(dx=0, dz=0, dy=0, dc=0):
    pairs = []
    for at in range(64):
        x, z, y, c = place(at)
        pairs.append((at, (x + dx) % 4 * 16 + (z + dz) % 4 * 4 + (y ^ dy) * 2 + (c ^ dc)))
    return pairs


def swap(value):
    return lax.ppermute(value, "head", [(0, 1), (1, 0)])


def send(value, **step):
    return lax.ppermute(value, "seq", moves(**step))


def regroup(value):
    groups = [[x * 16 + rest for x in range(4)] for rest in range(16)]
    return lax.all_to_all(value, "seq", 0, 0, axis_index_groups=groups, tiled=True)


def per_device(
    dna_bases,
    stem_weight,
    encoder_weight,
    norm_gain,
    attention_weight,
    logit_scale,
    out_weight,
    decoder_weight,
    grad_out,
):
    at = lax.axis_index("seq")
    x = at // 16
    ids = jnp.stack([lax.axis_index("head"), x, at]).astype(jnp.int32)
    feats = grad_out.shape[1]

    codes, last, first, encoder_weight = prepare(
        dna_bases.reshape(OWN, 128), grad_out, encoder_weight
    )
    before = lax.ppermute(last, "seq", [(i, i + 1) for i in range(63)])
    after = lax.ppermute(first, "seq", [(i + 1, i) for i in range(63)])
    encoded, attention_weight = encode(
        ids, codes, before, after, stem_weight, encoder_weight, attention_weight
    )
    gain = norm_gain.reshape(1, feats)
    queries, keyvals = project(ids, encoded, swap(encoded), gain, attention_weight)

    keyvals = regroup(keyvals).reshape(4 * OWN, 384)
    queries = regroup(queries).reshape(4 * ROWS, 256)
    near = [send(keyvals, dz=1), send(keyvals, dz=3)]
    far = send(keyvals, dz=2)
    near[0], near[1], queries = lax.optimization_barrier((near[0], near[1], queries))
    queries = [queries, send(queries, dy=1)]
    pieces = [keyvals, send(keyvals, dc=1)]
    pieces += near + [send(piece, dc=1) for piece in near]
    scale = lax.dynamic_slice_in_dim(logit_scale, x, 1)
    state = attend(scale, queries, pieces, (), False)
    far, *state = lax.optimization_barrier((far, *state))
    own, other = attend(scale, queries, [far, send(far, dc=1)], state, True)
    heads = regroup(merge([own, send(other, dy=1)]))

    sent = swap(output(ids, heads, out_weight, False, BF16))
    kept = output(ids, heads, out_weight, True, F32)
    inputs, sent = decode_send(ids, kept, sent, encoded, decoder_weight)
    sent = swap(sent)
    kept = decode_own(ids, inputs, decoder_weight)
    decoded, slope, paired = slopes(ids, kept, sent, inputs, grad_out, before, after)
    sent = swap(slope)
    partial = backward(ids, slope, paired, decoder_weight, True, F32)
    bins_grad = backward(ids, sent, partial, decoder_weight, False, BF16)
    return decoded, bins_grad


def solution(mesh):
    in_specs = (
        P("seq"),
        P(),
        P(None, None, "head"),
        P(),
        P(None, None, "head"),
        P("head"),
        P("head", None),
        P(None, "head", None),
        P("seq", None),
    )
    out_specs = (P("seq", "head"), P("seq", "head"))
    return jax.shard_map(
        per_device, mesh=mesh, in_specs=in_specs, out_specs=out_specs, check_vma=False
    )
```

time: 447 us -> 148 us (0.33); the launches traced: 440 us -> 148 us
  waiting for transfers between devices: 269 us -> 48.7 us
  matrix products: 54.6 us -> 0 us
  local copies, waits for them, and re-layouts: 49.1 us -> 8.47 us
  Pallas kernels: 0 us -> 40.2 us
  other arithmetic: 26.8 us -> 0.08 us
  starting transfers between devices: 12.2 us -> 25.6 us
  between operations: 14.1 us -> 0.84 us
  blocking collectives: 13.9 us -> 23.9 us
    all_gather x2 -> x0, waiting for transfers between devices: 194 us -> none  [the longest x1 114 us: per_device(): lax.all_gather(keys, 'seq', axis=0, tiled=True)]
    psum x2 -> x0, waiting for transfers between devices: 74.6 us -> none  [the longest x1 44.1 us: per_device(): lax.psum(partials.astype(jnp.bfloat16), 'head').astype(jnp.float32)]
    dot_general x16 -> x0, matrix products: 54.6 us -> none  [the longest x1 11.4 us: per_device(): jnp.einsum('hqk,khd->hqd', exps.astype(jnp.bfloat16), value_heads, prefer...]
    ppermute x6 -> x15, waiting for transfers between devices: 0.02 us -> 42 us  [the longest x4 22.7 us: swap(): return lax.ppermute(value, 'head', [(0, 1), (1, 0)])]
    pallas_call x0 -> x13, Pallas kernels: none -> 40.2 us  [the longest x2 14.9 us: attend(): pl.pallas_call(functools.partial(attend_kernel, len(pieces), bool(state),...]
    all_gather x2 -> x0, local copies, waits for them, and re-layouts: 31.4 us -> none  [the longest x1 15.7 us: per_device(): lax.all_gather(keys, 'seq', axis=0, tiled=True)]
    all_to_all x0 -> x2, blocking collectives: none -> 23.9 us  [regroup(): lax.all_to_all(value, 'seq', 0, 0, axis_index_groups=groups, tiled=True)]
    reduce_sum x6 -> x0, other arithmetic: 16.7 us -> none  [the longest x1 7.4 us: head_scores(): jnp.mean(jnp.square(key_heads.astype(jnp.float32)), axis=2) + 1e-06]
  transfers between devices with their start and end apart: 10 -> 16, of which waited for: 4 -> 9; matrix products, arithmetic and copies ran while one was open for 13% -> 0% of each run, Pallas kernels for 0% -> 10%
where the time goes in v3:
time: 148 us
  waiting for transfers between devices  48.7 us (33%)
  Pallas kernels  40.2 us (27%)
  starting transfers between devices  25.6 us (17%)
  blocking collectives  23.9 us (16%)
  local copies, waits for them, and re-layouts  8.47 us (6%)
    all_to_all x2, blocking collectives, regroup(): lax.all_to_all(value, 'seq', 0, 0, axis_index_groups=groups, tiled=True)  23.9 us
    ppermute x4, waiting for transfers between devices, swap(): return lax.ppermute(value, 'head', [(0, 1), (1, 0)])  22.7 us
    ppermute x9, waiting for transfers between devices, send(): return lax.ppermute(value, 'seq', moves(**step))  15.8 us
    pallas_call x2, Pallas kernels, attend(): pl.pallas_call(functools.partial(attend_kernel, len(pieces), bool(state),...  14.9 us
    ppermute x4, starting transfers between devices, swap(): return lax.ppermute(value, 'head', [(0, 1), (1, 0)])  11.2 us
    ppermute x9, starting transfers between devices, send(): return lax.ppermute(value, 'seq', moves(**step))  8.45 us
    unnamed x22, local copies, waits for them, and re-layouts  7.88 us
    all_to_all x1, waiting for transfers between devices, regroup(): lax.all_to_all(value, 'seq', 0, 0, axis_index_groups=groups, tiled=True)  6.64 us
  transfers between devices with their start and end apart: 16, of which 9 were waited for; matrix products, arithmetic and copies ran while one was open for 0% of the time, Pallas kernels for 10%

profile of v3, /device:TPU:0, one launch (start us, length us, event | category | flops | bytes accessed | tf_op | source)
XLA Modules:
  0.0 147.7 jit_solution(3812461161226999118)
XLA Ops:
  0.6 0.0 copy-start.3
  0.6 1.1 copy-done.3
  1.8 0.8 copy-done.6
  2.6 3.1 %prepare.1 = (bf16[128,128]{1,0:T(8,128)(2,1)S(1)}, bf16[8,1664]{1,0:T(8,128)(2,1)S(1)}, bf16[8,1664]{1,0:T(8,128)(2,1)S(1)}, bf16[3,1536,768]{2,1,0:T(8,128)(2,1)S(1)}) custom-call(s32[128,128]{1,0:T(8,128)S(1)} %bitcast.16, bf16[256,1536]{1,0:T(8,128)(2,1)S(1)} %copy-done.3, bf16[3,1536,768]{2,1,0:T(8,128)(2,1)} %weight.7), custom_call_target="tpu_custom_call" | custom-call | flops 1000000 | bytes 7077888 | tf_op jit(solution)/shard_map/prepare/pallas_call | solution.py:87
  5.7 0.0 copy-start.1
  5.7 2.9 %copy-done.1 = bf16[3,1536,768]{2,1,0:T(8,128)(2,1)} copy-done((bf16[3,1536,768]{2,1,0:T(8,128)(2,1)}, bf16[3,1536,768]{2,1,0:T(8,128)(2,1)S(1)}, u32[]{:S(2)}) %copy-start.1) | copy-done | bytes 7077912
  8.6 1.3 collective-permute-start
  9.9 1.3 collective-permute-start.1
  11.2 0.1 pad_add_fusion.ids
  11.3 0.0 collective-permute-done.before
  11.3 3.6 %collective-permute-done.1.after = bf16[8,1664]{1,0:T(8,128)(2,1)S(1)} collective-permute-done((bf16[8,1664]{1,0:T(8,128)(2,1)S(1)}, bf16[8,1664]{1,0:T(8,128)(2,1)S(1)}, u32[]{:S(2)}, u32[]{:S(2)}) %collective-permute-start.1) | collective-permute-done | bytes 26656 | tf_op jit(solution)/shard_map/ppermute | solution.py:532
  14.9 0.0 copy-done.5
  14.9 3.0 %copy-done.2 = bf16[3,1536,768]{2,1,0:T(8,128)(2,1)S(1)} copy-done((bf16[3,1536,768]{2,1,0:T(8,128)(2,1)S(1)}, bf16[3,1536,768]{2,1,0:T(8,128)(2,1)}, u32[]{:S(2)}) %copy-start.2) | copy-done | bytes 7077912
  17.9 4.6 %encode.1 = (bf16[272,768]{1,0:T(8,128)(2,1)S(1)}, bf16[3,1536,768]{2,1,0:T(8,128)(2,1)S(1)}) custom-call(s32[3]{0:T(128)S(1)} %pad_add_fusion.ids, bf16[128,128]{1,0:T(8,128)(2,1)S(1)} %get-tuple-element.25.codes, bf16[8,1664]{1,0:T(8,128)(2,1)S(1)} %collective-permute-done.before, bf16[8,1664]{1,0:T(8,128)(2,1)S(1)} %collective-permute-done.1.after, ...), custom_call_target="tpu_custom_call" | custom-call | flops 1925185536 | bytes 14155776 | tf_op jit(solution)/shard_map/encode/pallas_call | solution.py:142
  22.5 0.0 copy-start.8
  22.5 3.0 %collective-permute-start.2 = (bf16[272,768]{1,0:T(8,128)(2,1)S(1)}, bf16[272,768]{1,0:T(8,128)(2,1)S(1)}, u32[]{:S(2)}, u32[]{:S(2)}) collective-permute-start(bf16[272,768]{1,0:T(8,128)(2,1)S(1)} %get-tuple-element.29.mine.encoded), channel_id=1, source_target_pairs={{0,1},{1,0},{2,3},{3,2},{4,5},{5,4},{6,7},{7,6},{8,9},{9,8},{10,11... | collective-permute-start | bytes 1253384 | tf_op jit(solution)/shard_map/ppermute | solution.py:500
  25.5 0.0 copy-done.7
  25.5 9.4 %collective-permute-done.2.theirs = bf16[272,768]{1,0:T(8,128)(2,1)S(1)} collective-permute-done((bf16[272,768]{1,0:T(8,128)(2,1)S(1)}, bf16[272,768]{1,0:T(8,128)(2,1)S(1)}, u32[]{:S(2)}, u32[]{:S(2)}) %collective-permute-start.2) | collective-permute-done | bytes 417824 | tf_op jit(solution)/shard_map/ppermute | solution.py:500
  35.0 2.7 %project.1 = (bf16[4,136,256]{2,1,0:T(8,128)(2,1)}, bf16[4,128,384]{2,1,0:T(8,128)(2,1)S(1)}) custom-call(s32[3]{0:T(128)S(1)} %pad_add_fusion.ids, bf16[272,768]{1,0:T(8,128)(2,1)S(1)} %get-tuple-element.29.mine.encoded, bf16[272,768]{1,0:T(8,128)(2,1)S(1)} %collective-permute-done.2.theirs, f32[1,1536]{1,0:T(1,128)S(1)} %reshape.17.gain, ...), custom_call_target="tpu_custom_call" | custom-call | flops 962592768 | bytes 7077888 | tf_op jit(solution)/shard_map/project/pallas_call | solution.py:191
  37.6 14.7 %all_to_all.15 = bf16[4,128,384]{2,1,0:T(8,128)(2,1)S(1)} all-to-all(bf16[4,128,384]{2,1,0:T(8,128)(2,1)S(1)} %get-tuple-element.31), channel_id=1, replica_groups={{0,32,64,96},{2,34,66,98},{4,36,68,100},{6,38,70,102},{8,40,72,104},{10..., dimensions={0} | all-to-all | bytes 786432 | tf_op jit(solution)/shard_map/all_to_all | solution.py:509
  52.4 2.7 %collective-permute-start.3 = (bf16[512,384]{1,0:T(8,128)(2,1)S(1)}, bf16[512,384]{1,0:T(8,128)(2,1)S(1)}, u32[]{:S(2)}, u32[]{:S(2)}) collective-permute-start(bf16[512,384]{1,0:T(8,128)(2,1)S(1)} %bitcast.8), channel_id=1, source_target_pairs={{0,8},{2,10},{4,12},{6,14},{8,16},{10,18},{12,20},{14,22},{16,24},... | collective-permute-start | bytes 1179656 | tf_op jit(solution)/shard_map/ppermute | solution.py:504
  55.1 2.1 %collective-permute-start.4 = (bf16[512,384]{1,0:T(8,128)(2,1)S(1)}, bf16[512,384]{1,0:T(8,128)(2,1)S(1)}, u32[]{:S(2)}, u32[]{:S(2)}) collective-permute-start(bf16[512,384]{1,0:T(8,128)(2,1)S(1)} %bitcast.9), channel_id=1, source_target_pairs={{0,24},{2,26},{4,28},{6,30},{8,0},{10,2},{12,4},{14,6},{16,8},{18,... | collective-permute-start | bytes 1179656 | tf_op jit(solution)/shard_map/ppermute | solution.py:504
  57.2 3.5 %all-to-all-start.1 = ((bf16[4,136,256]{2,1,0:T(8,128)(2,1)}), bf16[4,136,256]{2,1,0:T(8,128)(2,1)S(1)}, u32[]{:S(2)}, u32[]{:S(2)}) async-start(bf16[4,136,256]{2,1,0:T(8,128)(2,1)} %get-tuple-element.32), calls=%async_computation.1 | async-start | bytes 557056 | tf_op jit(solution)/shard_map/all_to_all | solution.py:509
  60.6 0.1 collective-permute-start.7
  60.7 6.6 %all-to-all-done.1 = bf16[4,136,256]{2,1,0:T(8,128)(2,1)S(1)} async-done(((bf16[4,136,256]{2,1,0:T(8,128)(2,1)}), bf16[4,136,256]{2,1,0:T(8,128)(2,1)S(1)}, u32[]{:S(2)}, u32[]{:S(2)}) %all-to-all-start.1) | async-done | bytes 278560 | tf_op jit(solution)/shard_map/all_to_all | solution.py:509
  67.4 0.0 collective-permute-done.3.refs_4_
  67.4 0.0 collective-permute-done.4.refs_5_
  67.4 0.0 collective-permute-start.8
  67.4 0.5 collective-permute-start.9
  67.9 0.3 collective-permute-start.5
  68.2 2.1 %collective-permute-start.6 = (bf16[512,384]{1,0:T(8,128)(2,1)S(1)}, bf16[512,384]{1,0:T(8,128)(2,1)S(1)}, u32[]{:S(2)}, u32[]{:S(2)}) collective-permute-start(bf16[512,384]{1,0:T(8,128)(2,1)S(1)} %bitcast.11), channel_id=1, source_target_pairs={{0,16},{2,18},{4,20},{6,22},{8,24},{10,26},{12,28},{14,30},{16,0},... | collective-permute-start | bytes 1179656 | tf_op jit(solution)/shard_map/ppermute | solution.py:504
  70.3 0.0 copy-done.8
  70.3 0.6 dynamic_slice.3.scale
  70.9 0.0 collective-permute-done.7.refs_3_
  70.9 5.7 %collective-permute-done.5.refs_1_ = bf16[544,256]{1,0:T(8,128)(2,1)S(1)} collective-permute-done((bf16[544,256]{1,0:T(8,128)(2,1)S(1)}, bf16[544,256]{1,0:T(8,128)(2,1)S(1)}, u32[]{:S(2)}, u32[]{:S(2)}) %collective-permute-start.5) | collective-permute-done | bytes 278560 | tf_op jit(solution)/shard_map/ppermute | solution.py:504
  76.5 0.0 collective-permute-done.8.refs_6_
  76.5 0.0 collective-permute-done.9.refs_7_
  76.5 9.7 %attend.2 = (f32[1088,256]{1,0:T(8,128)S(1)}, f32[1088,128]{1,0:T(8,128)S(1)}) custom-call(f32[1]{0:T(128)} %dynamic_slice.3.scale, bf16[544,256]{1,0:T(8,128)(2,1)S(1)} %bitcast.14, bf16[544,256]{1,0:T(8,128)(2,1)S(1)} %collective-permute-done.5.refs_1_, bf16[512,384]{1,0:T(8,128)(2,1)S(1)} %bitcast.12, ...), custom_call_target="tpu_custom_call" | custom-call | flops 3422552064 | bytes 4456448 | tf_op jit(solution)/shard_map/attend/pallas_call | solution.py:282
  86.2 0.0 collective-permute-done.6.refs_2_
  86.2 0.1 collective-permute-start.10
  86.3 1.7 %collective-permute-done.10.refs_3_ = bf16[512,384]{1,0:T(8,128)(2,1)S(1)} collective-permute-done((bf16[512,384]{1,0:T(8,128)(2,1)S(1)}, bf16[512,384]{1,0:T(8,128)(2,1)S(1)}, u32[]{:S(2)}, u32[]{:S(2)}) %collective-permute-start.10) | collective-permute-done | bytes 393248 | tf_op jit(solution)/shard_map/ppermute | solution.py:504
  88.0 5.2 %attend.3 = (bf16[544,256]{1,0:T(8,128)(2,1)S(1)}, bf16[544,256]{1,0:T(8,128)(2,1)S(1)}) custom-call(f32[1]{0:T(128)} %dynamic_slice.3.scale, bf16[544,256]{1,0:T(8,128)(2,1)S(1)} %bitcast.15, bf16[544,256]{1,0:T(8,128)(2,1)S(1)} %collective-permute-done.5.refs_1_, bf16[512,384]{1,0:T(8,128)(2,1)S(1)} %collective-permute-done.6.refs_2_, ...), custom_call_target="tpu_custom_call" | custom-call | flops 1140850688 | bytes 4456448 | tf_op jit(solution)/shard_map/attend/pallas_call | solution.py:282
  93.2 0.6 collective-permute-start.11
  93.8 8.4 %collective-permute-done.11.a1 = bf16[544,256]{1,0:T(8,128)(2,1)S(1)} collective-permute-done((bf16[544,256]{1,0:T(8,128)(2,1)S(1)}, bf16[544,256]{1,0:T(8,128)(2,1)S(1)}, u32[]{:S(2)}, u32[]{:S(2)}) %collective-permute-start.11) | collective-permute-done | bytes 278560 | tf_op jit(solution)/shard_map/ppermute | solution.py:504
  102.2 0.6 merge.1
  102.7 9.1 %all_to_all.16.heads = bf16[4,136,256]{2,1,0:T(8,128)(2,1)S(1)} all-to-all(bf16[4,136,256]{2,1,0:T(8,128)(2,1)S(1)} %merge.1), channel_id=1, replica_groups={{0,32,64,96},{2,34,66,98},{4,36,68,100},{6,38,70,102},{8,40,72,104},{10..., dimensions={0} | all-to-all | bytes 557056 | tf_op jit(solution)/shard_map/all_to_all | solution.py:509
  111.9 0.0 copy-done
  111.9 1.2 output.3
  113.1 2.8 %collective-permute-start.12 = (bf16[136,768]{1,0:T(8,128)(2,1)S(1)}, bf16[136,768]{1,0:T(8,128)(2,1)S(1)}, u32[]{:S(2)}, u32[]{:S(2)}) collective-permute-start(bf16[136,768]{1,0:T(8,128)(2,1)S(1)} %output.3), channel_id=1, source_target_pairs={{0,1},{1,0},{2,3},{3,2},{4,5},{5,4},{6,7},{7,6},{8,9},{9,8},{10,11... | collective-permute-start | bytes 626696 | tf_op jit(solution)/shard_map/ppermute | solution.py:500
  115.9 1.2 output.2.own
  117.1 0.0 copy-start.4
  117.2 3.4 %collective-permute-done.12.other = bf16[136,768]{1,0:T(8,128)(2,1)S(1)} collective-permute-done((bf16[136,768]{1,0:T(8,128)(2,1)S(1)}, bf16[136,768]{1,0:T(8,128)(2,1)S(1)}, u32[]{:S(2)}, u32[]{:S(2)}) %collective-permute-start.12) | collective-permute-done | bytes 208928 | tf_op jit(solution)/shard_map/ppermute | solution.py:500
  120.5 0.0 slice-done
  120.5 0.0 slice-done.1
  120.5 2.3 %decode_send.1 = (bf16[272,768]{1,0:T(8,128)(2,1)S(1)}, bf16[272,768]{1,0:T(8,128)(2,1)S(1)}) custom-call(s32[3]{0:T(128)S(1)} %pad_add_fusion.ids, f32[136,768]{1,0:T(8,128)S(1)} %output.2.own, bf16[136,768]{1,0:T(8,128)(2,1)S(1)} %collective-permute-done.12.other, bf16[272,768]{1,0:T(8,128)(2,1)S(1)} %get-tuple-element.29.mine.encoded, ...), custom_call_target="tpu_custom_call" | custom-call | flops 962592768 | bytes 3538944 | tf_op jit(solution)/shard_map/decode_send/pallas_call | solution.py:373
  122.8 2.8 %collective-permute-start.13 = (bf16[272,768]{1,0:T(8,128)(2,1)S(1)}, bf16[272,768]{1,0:T(8,128)(2,1)S(1)}, u32[]{:S(2)}, u32[]{:S(2)}) collective-permute-start(bf16[272,768]{1,0:T(8,128)(2,1)S(1)} %get-tuple-element.44), channel_id=1, source_target_pairs={{0,1},{1,0},{2,3},{3,2},{4,5},{5,4},{6,7},{7,6},{8,9},{9,8},{10,11... | collective-permute-start | bytes 1253384 | tf_op jit(solution)/shard_map/ppermute | solution.py:500
  125.5 2.1 %decode_own.1.own = f32[272,768]{1,0:T(8,128)S(1)} custom-call(s32[3]{0:T(128)S(1)} %pad_add_fusion.ids, bf16[272,768]{1,0:T(8,128)(2,1)S(1)} %get-tuple-element.43.inputs, bf16[3,768,1536]{2,1,0:T(8,128)(2,1)S(1)} %bitcast.7), custom_call_target="tpu_custom_call" | custom-call | flops 962592768 | bytes 3538944 | tf_op jit(solution)/shard_map/decode_own/pallas_call | solution.py:396
  127.6 5.3 %collective-permute-done.13.other = bf16[272,768]{1,0:T(8,128)(2,1)S(1)} collective-permute-done((bf16[272,768]{1,0:T(8,128)(2,1)S(1)}, bf16[272,768]{1,0:T(8,128)(2,1)S(1)}, u32[]{:S(2)}, u32[]{:S(2)}) %collective-permute-start.13) | collective-permute-done | bytes 417824 | tf_op jit(solution)/shard_map/ppermute | solution.py:500
  132.9 0.0 copy-done.4
  132.9 2.2 %slopes.1 = (bf16[256,768]{1,0:T(8,128)(2,1)}, bf16[272,768]{1,0:T(8,128)(2,1)S(1)}, f32[128,768]{1,0:T(8,128)S(1)}) custom-call(s32[3]{0:T(128)S(1)} %pad_add_fusion.ids, f32[272,768]{1,0:T(8,128)S(1)} %decode_own.1.own, bf16[272,768]{1,0:T(8,128)(2,1)S(1)} %collective-permute-done.13.other, bf16[272,768]{1,0:T(8,128)(2,1)S(1)} %get-tuple-element.43.inputs, ...), custom_call_target="tpu_custom_call" | custom-call | flops 6266880 | bytes 2924544 | tf_op jit(solution)/shard_map/slopes/pallas_call | solution.py:437
  135.1 2.7 %collective-permute-start.14 = (bf16[272,768]{1,0:T(8,128)(2,1)S(1)}, bf16[272,768]{1,0:T(8,128)(2,1)S(1)}, u32[]{:S(2)}, u32[]{:S(2)}) collective-permute-start(bf16[272,768]{1,0:T(8,128)(2,1)S(1)} %get-tuple-element.46.slope), channel_id=1, source_target_pairs={{0,1},{1,0},{2,3},{3,2},{4,5},{5,4},{6,7},{7,6},{8,9},{9,8},{10,11... | collective-permute-start | bytes 1253384 | tf_op jit(solution)/shard_map/ppermute | solution.py:500
  137.8 2.3 %backward.2.start = f32[128,768]{1,0:T(8,128)S(1)} custom-call(s32[3]{0:T(128)S(1)} %pad_add_fusion.ids, bf16[272,768]{1,0:T(8,128)(2,1)S(1)} %get-tuple-element.46.slope, f32[128,768]{1,0:T(8,128)S(1)} %get-tuple-element.47.start, bf16[3,768,1536]{2,1,0:T(8,128)(2,1)S(1)} %bitcast.7), custom_call_target="tpu_custom_call" | custom-call | flops 962592768 | bytes 3538944 | tf_op jit(solution)/shard_map/backward/pallas_call | solution.py:475
  140.1 4.5 %collective-permute-done.14.slope = bf16[272,768]{1,0:T(8,128)(2,1)S(1)} collective-permute-done((bf16[272,768]{1,0:T(8,128)(2,1)S(1)}, bf16[272,768]{1,0:T(8,128)(2,1)S(1)}, u32[]{:S(2)}, u32[]{:S(2)}) %collective-permute-start.14) | collective-permute-done | bytes 417824 | tf_op jit(solution)/shard_map/ppermute | solution.py:500
  144.7 3.0 %backward.3 = bf16[128,768]{1,0:T(8,128)(2,1)} custom-call(s32[3]{0:T(128)S(1)} %pad_add_fusion.ids, bf16[272,768]{1,0:T(8,128)(2,1)S(1)} %collective-permute-done.14.slope, f32[128,768]{1,0:T(8,128)S(1)} %backward.2.start, bf16[3,768,1536]{2,1,0:T(8,128)(2,1)S(1)} %bitcast.7), custom_call_target="tpu_custom_call" | custom-call | flops 962592768 | bytes 3538944 | tf_op jit(solution)/shard_map/backward/pallas_call | solution.py:475
  (9 shorter events, 0.0 us)
Async XLA Ops:
  0.6 1.1 copy-start.3
  1.8 0.8 copy-start.6
  2.6 12.3 %copy-start.5 = (bf16[256,1536]{1,0:T(8,128)(2,1)S(1)}, bf16[256,1536]{1,0:T(8,128)(2,1)}, u32[]{:S(2)}) copy-start(bf16[256,1536]{1,0:T(8,128)(2,1)} %stem.1) | copy-start | bytes 2359300
  5.7 2.9 %copy-start.1 = (bf16[3,1536,768]{2,1,0:T(8,128)(2,1)}, bf16[3,1536,768]{2,1,0:T(8,128)(2,1)S(1)}, u32[]{:S(2)}) copy-start(bf16[3,1536,768]{2,1,0:T(8,128)(2,1)S(1)} %get-tuple-element.28.weight) | copy-start | bytes 21233668
  8.6 2.7 %collective-permute-start = (bf16[8,1664]{1,0:T(8,128)(2,1)S(1)}, bf16[8,1664]{1,0:T(8,128)(2,1)S(1)}, u32[]{:S(2)}, u32[]{:S(2)}) collective-permute-start(bf16[8,1664]{1,0:T(8,128)(2,1)S(1)} %get-tuple-element.26), channel_id=1, source_target_pairs={{0,2},{2,4},{4,6},{6,8},{8,10},{10,12},{12,14},{14,16},{16,18},{18... | collective-permute-start | bytes 79880 | tf_op jit(solution)/shard_map/ppermute | solution.py:531
  9.9 5.0 %collective-permute-start.1 = (bf16[8,1664]{1,0:T(8,128)(2,1)S(1)}, bf16[8,1664]{1,0:T(8,128)(2,1)S(1)}, u32[]{:S(2)}, u32[]{:S(2)}) collective-permute-start(bf16[8,1664]{1,0:T(8,128)(2,1)S(1)} %get-tuple-element.27), channel_id=1, source_target_pairs={{2,0},{4,2},{6,4},{8,6},{10,8},{12,10},{14,12},{16,14},{18,16},{20... | collective-permute-start | bytes 79880 | tf_op jit(solution)/shard_map/ppermute | solution.py:532
  14.9 3.0 %copy-start.2 = (bf16[3,1536,768]{2,1,0:T(8,128)(2,1)S(1)}, bf16[3,1536,768]{2,1,0:T(8,128)(2,1)}, u32[]{:S(2)}) copy-start(bf16[3,1536,768]{2,1,0:T(8,128)(2,1)} %copy-done.1) | copy-start | bytes 21233668
  17.9 7.6 %copy-start.7 = (f32[1536]{0:T(1024)S(1)}, f32[1536]{0:T(1024)}, u32[]{:S(2)}) copy-start(f32[1536]{0:T(1024)} %param.12) | copy-start | bytes 18436
  22.5 47.7 %copy-start.8 = (f32[4]{0:T(128)S(1)}, f32[4]{0:T(128)}, u32[]{:S(2)}) copy-start(f32[4]{0:T(128)} %param.14) | copy-start | bytes 52
  22.5 12.4 %collective-permute-start.2 = (bf16[272,768]{1,0:T(8,128)(2,1)S(1)}, bf16[272,768]{1,0:T(8,128)(2,1)S(1)}, u32[]{:S(2)}, u32[]{:S(2)}) collective-permute-start(bf16[272,768]{1,0:T(8,128)(2,1)S(1)} %get-tuple-element.29.mine.encoded), channel_id=1, source_target_pairs={{0,1},{1,0},{2,3},{3,2},{4,5},{5,4},{6,7},{7,6},{8,9},{9,8},{10,11... | collective-permute-start | bytes 1253384 | tf_op jit(solution)/shard_map/ppermute | solution.py:500
  52.4 15.0 %collective-permute-start.3 = (bf16[512,384]{1,0:T(8,128)(2,1)S(1)}, bf16[512,384]{1,0:T(8,128)(2,1)S(1)}, u32[]{:S(2)}, u32[]{:S(2)}) collective-permute-start(bf16[512,384]{1,0:T(8,128)(2,1)S(1)} %bitcast.8), channel_id=1, source_target_pairs={{0,8},{2,10},{4,12},{6,14},{8,16},{10,18},{12,20},{14,22},{16,24},... | collective-permute-start | bytes 1179656 | tf_op jit(solution)/shard_map/ppermute | solution.py:504
  55.1 12.3 %collective-permute-start.4 = (bf16[512,384]{1,0:T(8,128)(2,1)S(1)}, bf16[512,384]{1,0:T(8,128)(2,1)S(1)}, u32[]{:S(2)}, u32[]{:S(2)}) collective-permute-start(bf16[512,384]{1,0:T(8,128)(2,1)S(1)} %bitcast.9), channel_id=1, source_target_pairs={{0,24},{2,26},{4,28},{6,30},{8,0},{10,2},{12,4},{14,6},{16,8},{18,... | collective-permute-start | bytes 1179656 | tf_op jit(solution)/shard_map/ppermute | solution.py:504
  57.2 10.2 %all-to-all-start.1 = ((bf16[4,136,256]{2,1,0:T(8,128)(2,1)}), bf16[4,136,256]{2,1,0:T(8,128)(2,1)S(1)}, u32[]{:S(2)}, u32[]{:S(2)}) async-start(bf16[4,136,256]{2,1,0:T(8,128)(2,1)} %get-tuple-element.32), calls=%async_computation.1 | async-start | bytes 557056 | tf_op jit(solution)/shard_map/all_to_all | solution.py:509
  60.6 10.2 %collective-permute-start.7 = (bf16[512,384]{1,0:T(8,128)(2,1)S(1)}, bf16[512,384]{1,0:T(8,128)(2,1)S(1)}, u32[]{:S(2)}, u32[]{:S(2)}) collective-permute-start(bf16[512,384]{1,0:T(8,128)(2,1)S(1)} %bitcast.10), channel_id=1, source_target_pairs={{0,2},{2,0},{4,6},{6,4},{8,10},{10,8},{12,14},{14,12},{16,18},{18,... | collective-permute-start | bytes 1179656 | tf_op jit(solution)/shard_map/ppermute | solution.py:504
  67.4 9.2 %collective-permute-start.8 = (bf16[512,384]{1,0:T(8,128)(2,1)S(1)}, bf16[512,384]{1,0:T(8,128)(2,1)S(1)}, u32[]{:S(2)}, u32[]{:S(2)}) collective-permute-start(bf16[512,384]{1,0:T(8,128)(2,1)S(1)} %collective-permute-done.3.refs_4_), channel_id=1, source_target_pairs={{0,2},{2,0},{4,6},{6,4},{8,10},{10,8},{12,14},{14,12},{16,18},{18,... | collective-permute-start | bytes 1179656 | tf_op jit(solution)/shard_map/ppermute | solution.py:504
  67.4 9.2 %collective-permute-start.9 = (bf16[512,384]{1,0:T(8,128)(2,1)S(1)}, bf16[512,384]{1,0:T(8,128)(2,1)}, u32[]{:S(2)}, u32[]{:S(2)}) collective-permute-start(bf16[512,384]{1,0:T(8,128)(2,1)S(1)} %collective-permute-done.4.refs_5_), channel_id=1, source_target_pairs={{0,2},{2,0},{4,6},{6,4},{8,10},{10,8},{12,14},{14,12},{16,18},{18,... | collective-permute-start | bytes 1179656 | tf_op jit(solution)/shard_map/ppermute | solution.py:504
  67.9 8.6 %collective-permute-start.5 = (bf16[544,256]{1,0:T(8,128)(2,1)S(1)}, bf16[544,256]{1,0:T(8,128)(2,1)S(1)}, u32[]{:S(2)}, u32[]{:S(2)}) collective-permute-start(bf16[544,256]{1,0:T(8,128)(2,1)S(1)} %bitcast.13), channel_id=1, source_target_pairs={{0,4},{2,6},{4,0},{6,2},{8,12},{10,14},{12,8},{14,10},{16,20},{18,... | collective-permute-start | bytes 835592 | tf_op jit(solution)/shard_map/ppermute | solution.py:504
  68.2 18.0 %collective-permute-start.6 = (bf16[512,384]{1,0:T(8,128)(2,1)S(1)}, bf16[512,384]{1,0:T(8,128)(2,1)S(1)}, u32[]{:S(2)}, u32[]{:S(2)}) collective-permute-start(bf16[512,384]{1,0:T(8,128)(2,1)S(1)} %bitcast.11), channel_id=1, source_target_pairs={{0,16},{2,18},{4,20},{6,22},{8,24},{10,26},{12,28},{14,30},{16,0},... | collective-permute-start | bytes 1179656 | tf_op jit(solution)/shard_map/ppermute | solution.py:504
  70.3 50.3 %slice-start = ((s8[7077888]{0:T(1024)(128)(4,1)}), s8[4194304]{0:T(1024)(128)(4,1)S(1)}, s32[]{:S(2)}) async-start(s8[7077888]{0:T(1024)(128)(4,1)} %bitcast.6), calls=%async_computation.3 | async-start | bytes 8388608
  70.9 41.0 %copy-start = (bf16[768,1536]{1,0:T(8,128)(2,1)S(1)}, bf16[768,1536]{1,0:T(8,128)(2,1)}, u32[]{:S(2)}) copy-start(bf16[768,1536]{1,0:T(8,128)(2,1)} %weight.9) | copy-start | bytes 7077892
  70.9 49.7 %slice-start.1 = ((s8[7077888]{0:T(1024)(128)(4,1)}), s8[2883584]{0:T(1024)(128)(4,1)S(1)}, s32[]{:S(2)}) async-start(s8[7077888]{0:T(1024)(128)(4,1)} %bitcast.6), calls=%async_computation.4 | async-start | bytes 5767168
  86.2 1.8 %collective-permute-start.10 = (bf16[512,384]{1,0:T(8,128)(2,1)S(1)}, bf16[512,384]{1,0:T(8,128)(2,1)S(1)}, u32[]{:S(2)}, u32[]{:S(2)}) collective-permute-start(bf16[512,384]{1,0:T(8,128)(2,1)S(1)} %collective-permute-done.6.refs_2_), channel_id=1, source_target_pairs={{0,2},{2,0},{4,6},{6,4},{8,10},{10,8},{12,14},{14,12},{16,18},{18,... | collective-permute-start | bytes 1179656 | tf_op jit(solution)/shard_map/ppermute | solution.py:504
  93.2 9.0 %collective-permute-start.11 = (bf16[544,256]{1,0:T(8,128)(2,1)S(1)}, bf16[544,256]{1,0:T(8,128)(2,1)S(1)}, u32[]{:S(2)}, u32[]{:S(2)}) collective-permute-start(bf16[544,256]{1,0:T(8,128)(2,1)S(1)} %get-tuple-element.42), channel_id=1, source_target_pairs={{0,4},{2,6},{4,0},{6,2},{8,12},{10,14},{12,8},{14,10},{16,20},{18,... | collective-permute-start | bytes 835592 | tf_op jit(solution)/shard_map/ppermute | solution.py:504
  113.1 7.4 %collective-permute-start.12 = (bf16[136,768]{1,0:T(8,128)(2,1)S(1)}, bf16[136,768]{1,0:T(8,128)(2,1)S(1)}, u32[]{:S(2)}, u32[]{:S(2)}) collective-permute-start(bf16[136,768]{1,0:T(8,128)(2,1)S(1)} %output.3), channel_id=1, source_target_pairs={{0,1},{1,0},{2,3},{3,2},{4,5},{5,4},{6,7},{7,6},{8,9},{9,8},{10,11... | collective-permute-start | bytes 626696 | tf_op jit(solution)/shard_map/ppermute | solution.py:500
  117.1 15.8 %copy-start.4 = (bf16[256,1536]{1,0:T(8,128)(2,1)S(1)}, bf16[256,1536]{1,0:T(8,128)(2,1)}, u32[]{:S(2)}) copy-start(bf16[256,1536]{1,0:T(8,128)(2,1)} %grad.3) | copy-start | bytes 2359300
  122.8 10.1 %collective-permute-start.13 = (bf16[272,768]{1,0:T(8,128)(2,1)S(1)}, bf16[272,768]{1,0:T(8,128)(2,1)S(1)}, u32[]{:S(2)}, u32[]{:S(2)}) collective-permute-start(bf16[272,768]{1,0:T(8,128)(2,1)S(1)} %get-tuple-element.44), channel_id=1, source_target_pairs={{0,1},{1,0},{2,3},{3,2},{4,5},{5,4},{6,7},{7,6},{8,9},{9,8},{10,11... | collective-permute-start | bytes 1253384 | tf_op jit(solution)/shard_map/ppermute | solution.py:500
  135.1 9.5 %collective-permute-start.14 = (bf16[272,768]{1,0:T(8,128)(2,1)S(1)}, bf16[272,768]{1,0:T(8,128)(2,1)S(1)}, u32[]{:S(2)}, u32[]{:S(2)}) collective-permute-start(bf16[272,768]{1,0:T(8,128)(2,1)S(1)} %get-tuple-element.46.slope), channel_id=1, source_target_pairs={{0,1},{1,0},{2,3},{3,2},{4,5},{5,4},{6,7},{7,6},{8,9},{9,8},{10,11... | collective-permute-start | bytes 1253384 | tf_op jit(solution)/shard_map/ppermute | solution.py:500

commit v4 on v3

--- a/solution.py
+++ b/solution.py
@@ -69,44 +69,72 @@
     return jnp.concatenate([even, odd], axis=0)
 
 
-def prepare_kernel(bases, grad, weight, codes, last, first, loaded, sem):
-    copy = pltpu.make_async_copy(weight, loaded, sem)
-    copy.start()
-    code = (bases[...] + 1).astype(F32)
-    codes[...] = code.astype(BF16)
+def prepare_kernel(bases, grad, codes, last, first, code, head, tail, sems):
+    rows = grad.shape[0]
+    copies = [
+        pltpu.make_async_copy(bases, code, sems.at[0]),
+        pltpu.make_async_copy(grad.at[pl.ds(0, 16)], head, sems.at[1]),
+        pltpu.make_async_copy(grad.at[pl.ds(rows - 16, 16)], tail, sems.at[2]),
+    ]
+    for copy in copies:
+        copy.start()
+    for copy in copies:
+        copy.wait()
     feats = grad.shape[1]
-    last[:, :feats] = grad[2 * OWN - 16 :, :].astype(F32)[8:].astype(BF16)
-    last[:, feats:] = code[OWN - 8 :].astype(BF16)
-    first[:, :feats] = grad[:16, :].astype(F32)[:8].astype(BF16)
-    first[:, feats:] = code[:8].astype(BF16)
-    copy.wait()
-
-
-def prepare(bases, grad, weight):
-    width = grad.shape[1] + 128
+    letters = (code[...] + 1).astype(F32)
+    codes[...] = letters.astype(BF16)
+    last[:, :feats] = tail[...].astype(F32)[8:].astype(BF16)
+    last[:, feats:] = letters[OWN - 8 :].astype(BF16)
+    first[:, :feats] = head[...].astype(F32)[:8].astype(BF16)
+    first[:, feats:] = letters[:8].astype(BF16)
+
+
+def far_memory(value):
+    return pltpu.with_memory_space_constraint(value, pltpu.HBM)
+
+
+def prepare(bases, grad):
+    feats = grad.shape[1]
     return pl.pallas_call(
         prepare_kernel,
-        in_specs=[VM, VM, HBM],
-        out_specs=[VM] * 4,
+        in_specs=[HBM, HBM],
+        out_specs=[VM] * 3,
         out_shape=[
             shape((OWN, 128), BF16),
-            shape((8, width), BF16),
-            shape((8, width), BF16),
-            pltpu.VMEM(weight.shape, BF16),
+            shape((8, feats + 128), BF16),
+            shape((8, feats + 128), BF16),
         ],
-        scratch_shapes=[pltpu.SemaphoreType.DMA(())],
-        compiler_params=params(8),
-        cost_estimate=cost(10**6, weight.size * 2),
+        scratch_shapes=[
+            pltpu.VMEM(bases.shape, jnp.int32),
+            pltpu.VMEM((16, feats), BF16),
+            pltpu.VMEM((16, feats), BF16),
+            pltpu.SemaphoreType.DMA((3,)),
+        ],
+        compiler_params=params(4),
+        cost_estimate=cost(10**5, 10**5),
         name="prepare",
-    )(bases, grad, pltpu.with_memory_space_constraint(weight, pltpu.HBM))
-
-
-def encode_kernel(ids, codes, before, after, stem, weight, ahead, encoded, loaded, embedded, sem):
-    copy = pltpu.make_async_copy(ahead, loaded, sem)
-    copy.start()
+    )(far_memory(bases), far_memory(grad))
+
+
+def encode_kernel(
+    ids, codes, before, after, stems, weights, ahead, encoded, loaded, stem, weight, embedded, sems
+):
     patch = stem.shape[0] // 4
     feats = stem.shape[1]
     half = weight.shape[2]
+    count = half // TILE
+    first = pltpu.make_async_copy(stems, stem, sems.at[count])
+    copies = [
+        pltpu.make_async_copy(
+            weights.at[:, :, pl.ds(i * TILE, TILE)],
+            weight.at[:, :, pl.ds(i * TILE, TILE)],
+            sems.at[i],
+        )
+        for i in range(count)
+    ]
+    later = pltpu.make_async_copy(ahead, loaded, sems.at[count + 1])
+    for copy in [first] + copies + [later]:
+        copy.start()
     row = lax.broadcasted_iota(jnp.int32, (2 * patch, 4 * patch), 0)
     col = lax.broadcasted_iota(jnp.int32, (2 * patch, 4 * patch), 1)
     place = lax.broadcasted_iota(jnp.int32, (ROWS - OWN, 128), 0)
@@ -120,20 +148,22 @@
     base = lax.broadcasted_iota(jnp.int32, spread.shape, 1) % 4 + 1
     onehot = (spread == base.astype(F32)).astype(F32).astype(BF16)
 
+    first.wait()
+
     def embed(i):
         at = lanes(i * TILE, TILE)
         embedded[:, at] = dot(onehot, stem[:, at]).astype(BF16)
 
     tiles(feats // TILE, embed)
 
-    def convolve(i):
-        at = lanes(i * TILE, TILE)
+    for i in range(count):
+        copies[i].wait()
+        at = slice(i * TILE, (i + 1) * TILE)
         pre = conv_taps(embedded[...], lambda t: weight[t, :, at])
         mine = embedded[:, lanes(ids[0] * half + i * TILE, TILE)].astype(F32)
         encoded[:, at] = (mine + 0.5 * pre * (1.0 + gelu_tanh(pre))).astype(BF16)
 
-    tiles(half // TILE, convolve)
-    copy.wait()
+    later.wait()
 
 
 def encode(ids, codes, before, after, stem, weight, ahead):
@@ -141,17 +171,23 @@
     feats = stem.shape[1]
     return pl.pallas_call(
         encode_kernel,
-        in_specs=[SM, VM, VM, VM, VM, VM, HBM],
+        in_specs=[SM, VM, VM, VM, HBM, HBM, HBM],
         out_specs=[VM, VM],
         out_shape=[shape((2 * ROWS, half), BF16), pltpu.VMEM(ahead.shape, BF16)],
-        scratch_shapes=[pltpu.VMEM((2 * ROWS, feats), BF16), pltpu.SemaphoreType.DMA(())],
-        compiler_params=params(12),
+        scratch_shapes=[
+            pltpu.VMEM(stem.shape, BF16),
+            pltpu.VMEM(weight.shape, BF16),
+            pltpu.VMEM((2 * ROWS, feats), BF16),
+            pltpu.SemaphoreType.DMA((half // TILE + 2,)),
+        ],
+        compiler_params=params(20),
         cost_estimate=cost(2 * 2 * ROWS * 3 * feats * half, weight.size * 4),
         name="encode",
-    )(ids, codes, before, after, stem, weight, pltpu.with_memory_space_constraint(ahead, pltpu.HBM))
-
-
-def project_kernel(ids, mine, theirs, gain, weight, queries, keyvals):
+    )(ids, codes, before, after, far_memory(stem), far_memory(weight), far_memory(ahead))
+
+
+def project_kernel(ids, mine, theirs, gain, weight, *refs):
+    queries, keyvals, packed = refs[:4], refs[4:8], refs[8]
     half = mine.shape[1]
     near = lanes(ids[0] * half, half)
     far = lanes((1 - ids[0]) * half, half)
@@ -179,20 +215,25 @@
                 (r[0][:, :128], r[0][:, 128:256]) if side == 0 else (r[1][:, 128:256], r[1][:, 256:384])
                 for r in rows
             )
-            queries[head, :, :128] = query[0].astype(BF16)
-            queries[head, :, 128:] = jnp.where(low, query[1], 0.0).astype(BF16)
-            keyvals[head, :, :128] = key[0][:OWN].astype(BF16)
-            keyvals[head, :, 128:256] = value[0][:OWN].astype(BF16)
+            packed[head, :, :128] = key[0].astype(BF16)
+            packed[head, :, 128:256] = value[0].astype(BF16)
             tail = jnp.where(low, key[1], pltpu.roll(value[1], 64, 1))
-            keyvals[head, :, 256:] = tail[:OWN].astype(BF16)
+            packed[head, :, 256:384] = tail.astype(BF16)
+            packed[head, :, 384:512] = query[0].astype(BF16)
+            packed[head, :, 512:] = jnp.where(low, query[1], 0.0).astype(BF16)
+    for distance in range(4):
+        head = lax.rem(ids[1] + distance, 4)
+        keyvals[distance][...] = packed[head, :OWN, :384]
+        queries[distance][...] = packed[head, :, 384:]
 
 
 def project(ids, mine, theirs, gain, weight):
     return pl.pallas_call(
         project_kernel,
         in_specs=[SM, VM, VM, VM, VM],
-        out_specs=[VM, VM],
-        out_shape=[shape((4, ROWS, 256), BF16), shape((4, OWN, 384), BF16)],
+        out_specs=[VM] * 8,
+        out_shape=[shape((ROWS, 256), BF16)] * 4 + [shape((OWN, 384), BF16)] * 4,
+        scratch_shapes=[pltpu.VMEM((4, ROWS, 640), BF16)],
         compiler_params=params(12),
         cost_estimate=cost(2 * ROWS * weight.size, weight.size * 2),
         name="project",
@@ -200,131 +241,117 @@
 
 
 BLOCK = 2 * ROWS
-
-
-def attend_kernel(count, resumed, final, scale, *refs):
-    queries, refs = refs[:2], refs[2:]
+LOG2E = 1.4426950408889634
+
+
+def attend_kernel(count, again, scale, queries, *refs):
     pieces, refs = refs[:count], refs[count:]
-    if resumed:
-        (old_mixed, old_stats), refs = refs[:2], refs[2:]
-    outs, inverse = refs[:2], refs[2]
+    if again:
+        inverse, out = refs
+    else:
+        out, inverse = refs
     chunk = pieces[0].shape[0]
-    lane = lax.broadcasted_iota(jnp.int32, (8, 256), 1)
-    ones = (lane < HEAD).astype(F32).astype(BF16)
 
     def keys(ref):
         return jnp.concatenate([ref[:, :128], ref[:, 256:]], axis=1)
 
-    for at, ref in enumerate(pieces):
-        key = keys(ref).astype(F32)
-        square = key * key
-        high = square.astype(BF16)
-        rest = (square - high.astype(F32)).astype(BF16)
-        total = dot_t(ones, high) + dot_t(ones, rest)
-        inverse[:, at * chunk : (at + 1) * chunk] = lax.rsqrt(total * (1.0 / HEAD) + EPS)
+    if not again:
+        lane = lax.broadcasted_iota(jnp.int32, (8, 256), 1)
+        ones = (lane < HEAD).astype(F32).astype(BF16)
+        for at, ref in enumerate(pieces):
+            key = keys(ref).astype(F32)
+            square = key * key
+            high = square.astype(BF16)
+            rest = (square - high.astype(F32)).astype(BF16)
+            total = dot_t(ones, high) + dot_t(ones, rest)
+            inverse[:, at * chunk : (at + 1) * chunk] = lax.rsqrt(total * (1.0 / HEAD) + EPS)
 
     def block(i):
-        for side, query_ref in enumerate(queries):
-            span = query_ref.shape[0]
-            rows = lanes(i * BLOCK, BLOCK)
-            state = lanes(side * span + i * BLOCK, BLOCK)
-            query = query_ref[rows, :]
-            wide = query.astype(F32)
-            own = lax.rsqrt(jnp.sum(wide * wide, axis=1, keepdims=True) * (1.0 / HEAD) + EPS)
-            factor = own * (scale[0] * (1.0 / HEAD))
-            scores = []
-            peak = old_stats[state, 0:1] if resumed else None
-            before = peak
-            for at, ref in enumerate(pieces):
-                part = dot_t(query, keys(ref)) * factor
-                part = part * inverse[0:1, at * chunk : (at + 1) * chunk]
-                top = jnp.max(part, axis=1, keepdims=True)
-                peak = top if peak is None else jnp.maximum(peak, top)
-                scores.append(part)
-            total, mixed = None, None
-            if resumed:
-                shrink = jnp.exp(before - peak)
-                total = old_stats[state, 64:65] * shrink
-                mixed = old_mixed[state, :] * shrink
-            for part, ref in zip(scores, pieces):
-                exps = jnp.exp(part - peak)
-                sums = jnp.sum(exps, axis=1, keepdims=True)
-                values = jnp.concatenate([ref[:, 128:256], ref[:, 256:]], axis=1)
-                term = dot(exps.astype(BF16), values)
-                total = sums if total is None else total + sums
-                mixed = term if mixed is None else mixed + term
-            if not final:
-                outs[0][state, :] = mixed
-                half = lax.broadcasted_iota(jnp.int32, (BLOCK, 128), 1) < 64
-                outs[1][state, :] = jnp.where(half, peak, total)
-                continue
-            mixed = mixed / total
-            weight = peak + jnp.log(total)
-            high = weight.astype(BF16).astype(F32)
-            rest = weight - high
-            mid = rest.astype(BF16).astype(F32)
-            place = lax.broadcasted_iota(jnp.int32, mixed.shape, 1)
-            mixed = jnp.where(place == 128, high, mixed)
-            mixed = jnp.where(place == 129, mid, mixed)
-            mixed = jnp.where(place == 130, rest - mid, mixed)
-            outs[side][rows, :] = mixed.astype(BF16)
-
-    tiles(queries[0].shape[0] // BLOCK, block)
-
-
-def attend(scale, queries, pieces, state, final):
-    rows = queries[0].shape[0]
+        rows = lanes(i * BLOCK, BLOCK)
+        query = queries[rows, :]
+        wide = query.astype(F32)
+        own = lax.rsqrt(jnp.sum(wide * wide, axis=1, keepdims=True) * (1.0 / HEAD) + EPS)
+        factor = own * (scale[0] * (LOG2E / HEAD))
+        scores = []
+        peak = None
+        for at, ref in enumerate(pieces):
+            part = dot_t(query, keys(ref)) * inverse[0:1, at * chunk : (at + 1) * chunk]
+            top = jnp.max(part, axis=1, keepdims=True)
+            peak = top if peak is None else jnp.maximum(peak, top)
+            scores.append(part)
+        total, mixed = None, None
+        for part, ref in zip(scores, pieces):
+            exps = jnp.exp2((part - peak) * factor)
+            sums = jnp.sum(exps, axis=1, keepdims=True)
+            values = jnp.concatenate([ref[:, 128:256], ref[:, 256:]], axis=1)
+            term = dot(exps.astype(BF16), values)
+            total = sums if total is None else total + sums
+            mixed = term if mixed is None else mixed + term
+        mixed = mixed / total
+        weight = peak * factor + jnp.log(total) * LOG2E
+        high = weight.astype(BF16).astype(F32)
+        rest = weight - high
+        mid = rest.astype(BF16).astype(F32)
+        place = lax.broadcasted_iota(jnp.int32, mixed.shape, 1)
+        mixed = jnp.where(place == 128, high, mixed)
+        mixed = jnp.where(place == 129, mid, mixed)
+        mixed = jnp.where(place == 130, rest - mid, mixed)
+        out[rows, :] = mixed.astype(BF16)
+
+    tiles(queries.shape[0] // BLOCK, block)
+
+
+def attend(scale, queries, pieces, inverse=None):
+    again = inverse is not None
+    rows = queries.shape[0]
     keys = len(pieces) * pieces[0].shape[0]
-    if final:
-        outs = [shape((rows, 256), BF16)] * 2
-    else:
-        outs = [shape((2 * rows, 256), F32), shape((2 * rows, 128), F32)]
-    return pl.pallas_call(
-        functools.partial(attend_kernel, len(pieces), bool(state), final),
-        in_specs=[SM] + [VM] * (2 + len(pieces) + len(state)),
-        out_specs=[VM] * 2,
+    outs = [shape((rows, 256), BF16)] + ([] if again else [shape((8, keys), F32)])
+    return pl.pallas_call(
+        functools.partial(attend_kernel, len(pieces), again),
+        in_specs=[SM] + [VM] * (1 + len(pieces) + again),
+        out_specs=[VM] * len(outs),
         out_shape=outs,
-        scratch_shapes=[pltpu.VMEM((8, keys), F32)],
-        compiler_params=params(20),
-        cost_estimate=cost(4 * 2 * rows * keys * 256, 8 * rows * 1024),
+        compiler_params=params(24),
+        cost_estimate=cost(4 * rows * keys * 256, 8 * rows * 1024),
         name="attend",
-    )(scale, *queries, *pieces, *state)
-
-
-def merge_kernel(a0, a1, out):
+    )(scale, queries, *pieces, *([inverse] if again else []))
+
+
+def merge_kernel(a0, a1, *outs):
     parts = [ref[...].astype(F32) for ref in (a0, a1)]
     logs = [p[:, 128:129] + p[:, 129:130] + p[:, 130:131] for p in parts]
     peak = functools.reduce(jnp.maximum, logs)
-    shares = [jnp.exp(log - peak) for log in logs]
+    shares = [jnp.exp2(log - peak) for log in logs]
     total = sum(shares)
     mixed = sum(p * (share / total) for p, share in zip(parts, shares))
     mixed = jnp.concatenate([mixed[:, :128], pltpu.roll(mixed[:, 128:], 64, 1)], axis=1)
     for block in range(4):
-        out[block] = mixed[block * ROWS : (block + 1) * ROWS].astype(BF16)
+        outs[block][...] = mixed[block * ROWS : (block + 1) * ROWS].astype(BF16)
 
 
 def merge(parts):
     return pl.pallas_call(
         merge_kernel,
         in_specs=[VM] * 2,
-        out_specs=VM,
-        out_shape=shape((4, ROWS, 256), BF16),
+        out_specs=[VM] * 4,
+        out_shape=[shape((ROWS, 256), BF16)] * 4,
         compiler_params=params(8),
         cost_estimate=cost(20 * parts[0].size, 10 * parts[0].size),
         name="merge",
     )(*parts)
 
 
-def output_kernel(mine, ids, heads, weight, out):
+def output_kernel(mine, ids, a0, a1, a2, a3, weight, out):
     half = out.shape[1]
     side = ids[0] if mine else 1 - ids[0]
 
     def tile(i):
         at = lanes(side * half + i * TILE, TILE)
         total = None
-        for head in range(4):
-            rows = weight[head * HEAD : (head + 1) * HEAD, at]
-            term = dot(heads[head, :, :HEAD], rows)
+        for distance, ref in enumerate((a0, a1, a2, a3)):
+            head = lax.rem(ids[1] + distance, 4)
+            rows = weight[pl.ds(pl.multiple_of(head * HEAD, HEAD), HEAD), at]
+            term = dot(ref[:, :HEAD], rows)
             total = term if total is None else total + term
         out[:, lanes(i * TILE, TILE)] = total.astype(out.dtype)
 
@@ -335,13 +362,13 @@
     half = weight.shape[1] // 2
     return pl.pallas_call(
         functools.partial(output_kernel, mine),
-        in_specs=[SM, VM, VM],
+        in_specs=[SM] + [VM] * 5,
         out_specs=VM,
         out_shape=shape((ROWS, half), dtype),
         compiler_params=params(6),
         cost_estimate=cost(2 * ROWS * weight.size // 2, weight.size),
         name="output",
-    )(ids, heads, weight)
+    )(ids, *heads, weight)
 
 
 def decode_send_kernel(ids, own, other, encoded, weight, inputs, out):
@@ -504,11 +531,6 @@
     return lax.ppermute(value, "seq", moves(**step))
 
 
-def regroup(value):
-    groups = [[x * 16 + rest for x in range(4)] for rest in range(16)]
-    return lax.all_to_all(value, "seq", 0, 0, axis_index_groups=groups, tiled=True)
-
-
 def per_device(
     dna_bases,
     stem_weight,
@@ -525,30 +547,34 @@
     ids = jnp.stack([lax.axis_index("head"), x, at]).astype(jnp.int32)
     feats = grad_out.shape[1]
 
-    codes, last, first, encoder_weight = prepare(
-        dna_bases.reshape(OWN, 128), grad_out, encoder_weight
-    )
+    codes, last, first = prepare(dna_bases.reshape(OWN, 128), grad_out)
     before = lax.ppermute(last, "seq", [(i, i + 1) for i in range(63)])
     after = lax.ppermute(first, "seq", [(i + 1, i) for i in range(63)])
     encoded, attention_weight = encode(
         ids, codes, before, after, stem_weight, encoder_weight, attention_weight
     )
     gain = norm_gain.reshape(1, feats)
-    queries, keyvals = project(ids, encoded, swap(encoded), gain, attention_weight)
-
-    keyvals = regroup(keyvals).reshape(4 * OWN, 384)
-    queries = regroup(queries).reshape(4 * ROWS, 256)
-    near = [send(keyvals, dz=1), send(keyvals, dz=3)]
-    far = send(keyvals, dz=2)
-    near[0], near[1], queries = lax.optimization_barrier((near[0], near[1], queries))
-    queries = [queries, send(queries, dy=1)]
-    pieces = [keyvals, send(keyvals, dc=1)]
-    pieces += near + [send(piece, dc=1) for piece in near]
+    made = project(ids, encoded, swap(encoded), gain, attention_weight)
+    queries, keyvals = made[:4], made[4:]
+
+    def regroup(blocks):
+        got = [blocks[0]] + [send(blocks[d], dx=d) for d in (1, 3, 2)]
+        return jnp.concatenate(lax.optimization_barrier(got), axis=0)
+
+    keyvals = regroup(keyvals)
+    keyvals, *queries = lax.optimization_barrier((keyvals, *queries))
+    pieces = [send(keyvals, dz=d) for d in (1, 3, 2)]
+    queries = regroup(queries)
+    others = send(queries, dy=1)
+    pieces[0], pieces[1], others = lax.optimization_barrier((pieces[0], pieces[1], others))
+    pieces = [keyvals] + pieces
+    pieces += [send(piece, dc=1) for piece in pieces]
     scale = lax.dynamic_slice_in_dim(logit_scale, x, 1)
-    state = attend(scale, queries, pieces, (), False)
-    far, *state = lax.optimization_barrier((far, *state))
-    own, other = attend(scale, queries, [far, send(far, dc=1)], state, True)
-    heads = regroup(merge([own, send(other, dy=1)]))
+    other, inverse = attend(scale, others, pieces)
+    other = send(other, dy=1)
+    own = attend(scale, queries, pieces, inverse)[0]
+    mixed = merge([own, other])
+    heads = [mixed[0], send(mixed[1], dx=-1), send(mixed[3], dx=-2), send(mixed[2], dx=-3)]
 
     sent = swap(output(ids, heads, out_weight, False, BF16))
     kept = output(ids, heads, out_weight, True, F32)

time: 148 us -> 137 us (0.926)
  blocking collectives: 23.9 us -> 0 us
  starting transfers between devices: 25.6 us -> 39.2 us
  local copies, waits for them, and re-layouts: 8.47 us -> 2.31 us
  waiting for transfers between devices: 48.7 us -> 51.3 us
  Pallas kernels: 40.2 us -> 42.5 us
    all_to_all x2 -> x0, blocking collectives: 23.9 us -> none  [regroup(): lax.all_to_all(value, 'seq', 0, 0, axis_index_groups=groups, tiled=True)]
    ppermute x9 -> x18, starting transfers between devices: 8.45 us -> 25.2 us  [send(): return lax.ppermute(value, 'seq', moves(**step))]
    ppermute x9 -> x18, waiting for transfers between devices: 15.8 us -> 22.8 us  [send(): return lax.ppermute(value, 'seq', moves(**step))]
    all_to_all x1 -> x0, waiting for transfers between devices: 6.64 us -> none  [regroup(): lax.all_to_all(value, 'seq', 0, 0, axis_index_groups=groups, tiled=True)]
    unnamed x22 -> x19, local copies, waits for them, and re-layouts: 7.88 us -> 1.71 us
    all_to_all x1 -> x0, starting transfers between devices: 3.45 us -> none  [regroup(): lax.all_to_all(value, 'seq', 0, 0, axis_index_groups=groups, tiled=True)]
    pallas_call x7, Pallas kernels: 25.6 us -> 28.1 us  [the longest x2 18.1 us: attend(): pl.pallas_call(functools.partial(attend_kernel, len(pieces), again), in_s...]
    ppermute x4, waiting for transfers between devices: 22.7 us -> 24.9 us  [swap(): return lax.ppermute(value, 'head', [(0, 1), (1, 0)])]
  transfers between devices with their start and end apart: 16 -> 24, of which waited for: 9 -> 14; matrix products, arithmetic and copies ran while one was open for 0% -> 1% of each run, Pallas kernels for 10% -> 11%
where the time goes in v4:
time: 137 us; the launch traced here: 136 us
  waiting for transfers between devices  51.3 us (37%)
  Pallas kernels  42.5 us (31%)
  starting transfers between devices  39.2 us (29%)
  local copies, waits for them, and re-layouts  2.31 us (2%)
    ppermute x18, starting transfers between devices, send(): return lax.ppermute(value, 'seq', moves(**step))  25.2 us
    ppermute x4, waiting for transfers between devices, swap(): return lax.ppermute(value, 'head', [(0, 1), (1, 0)])  24.9 us
    ppermute x18, waiting for transfers between devices, send(): return lax.ppermute(value, 'seq', moves(**step))  22.8 us
    pallas_call x2, Pallas kernels, attend(): pl.pallas_call(functools.partial(attend_kernel, len(pieces), again), in_s...  18.1 us
    ppermute x4, starting transfers between devices, swap(): return lax.ppermute(value, 'head', [(0, 1), (1, 0)])  11.3 us
    pallas_call x1, Pallas kernels, encode(): pl.pallas_call(encode_kernel, in_specs=[SM, VM, VM, VM, HBM, HBM, HBM], o...  6 us
    pallas_call x2, Pallas kernels, backward(): pl.pallas_call(functools.partial(backward_kernel, mine), in_specs=[SM] +...  5.35 us
    ppermute x1, waiting for transfers between devices, per_device(): after = lax.ppermute(first, 'seq', [(i + 1, i) for i in range(63)])  3.59 us
  transfers between devices with their start and end apart: 24, of which 14 were waited for; matrix products, arithmetic and copies ran while one was open for 1% of the time, Pallas kernels for 11%

profile of v4, /device:TPU:0, one launch (start us, length us, event | category | flops | bytes accessed | tf_op | source)
XLA Modules:
  0.0 136.3 jit_solution(8978037242097397779)
XLA Ops:
  0.6 0.9 prepare.1
  1.5 1.3 collective-permute-start
  2.8 1.3 collective-permute-start.1
  4.1 0.1 pad_add_fusion.ids
  4.2 0.0 collective-permute-done.before
  4.2 3.6 %collective-permute-done.1.after = bf16[8,1664]{1,0:T(8,128)(2,1)S(1)} collective-permute-done((bf16[8,1664]{1,0:T(8,128)(2,1)S(1)}, bf16[8,1664]{1,0:T(8,128)(2,1)S(1)}, u32[]{:S(2)}, u32[]{:S(2)}) %collective-permute-start.1) | collective-permute-done | bytes 26656 | tf_op jit(solution)/shard_map/ppermute | solution.py:552
  7.8 6.0 %encode.1 = (bf16[272,768]{1,0:T(8,128)(2,1)S(1)}, bf16[3,1536,768]{2,1,0:T(8,128)(2,1)S(1)}) custom-call(s32[3]{0:T(128)S(1)} %pad_add_fusion.ids, bf16[128,128]{1,0:T(8,128)(2,1)S(1)} %get-tuple-element.42.codes, bf16[8,1664]{1,0:T(8,128)(2,1)S(1)} %collective-permute-done.before, bf16[8,1664]{1,0:T(8,128)(2,1)S(1)} %collective-permute-done.1.after, ...), custom_call_target="tpu_custom_call" | custom-call | flops 1925185536 | bytes 14155776 | tf_op jit(solution)/shard_map/encode/pallas_call | solution.py:172
  13.8 0.0 copy-start.5
  13.8 3.0 %collective-permute-start.2 = (bf16[272,768]{1,0:T(8,128)(2,1)S(1)}, bf16[272,768]{1,0:T(8,128)(2,1)S(1)}, u32[]{:S(2)}, u32[]{:S(2)}) collective-permute-start(bf16[272,768]{1,0:T(8,128)(2,1)S(1)} %get-tuple-element.45.mine.encoded), channel_id=1, source_target_pairs={{0,1},{1,0},{2,3},{3,2},{4,5},{5,4},{6,7},{7,6},{8,9},{9,8},{10,11... | collective-permute-start | bytes 1253384 | tf_op jit(solution)/shard_map/ppermute | solution.py:527
  16.8 9.4 %collective-permute-done.2.theirs = bf16[272,768]{1,0:T(8,128)(2,1)S(1)} collective-permute-done((bf16[272,768]{1,0:T(8,128)(2,1)S(1)}, bf16[272,768]{1,0:T(8,128)(2,1)S(1)}, u32[]{:S(2)}, u32[]{:S(2)}) %collective-permute-start.2) | collective-permute-done | bytes 417824 | tf_op jit(solution)/shard_map/ppermute | solution.py:527
  26.3 2.6 %project.1 = (bf16[136,256]{1,0:T(8,128)(2,1)S(1)}, bf16[136,256]{1,0:T(8,128)(2,1)S(1)}, bf16[136,256]{1,0:T(8,128)(2,1)S(1)}, bf16[136,256]{1,0:T(8,128)(2,1)S...) custom-call(s32[3]{0:T(128)S(1)} %pad_add_fusion.ids, ...), custom_call_target="tpu_custom_call" | custom-call | flops 962592768 | bytes 7077888 | tf_op jit(solution)/shard_map/project/pallas_call | solution.py:231
  28.8 4.8 %collective-permute-start.3 = (bf16[128,384]{1,0:T(8,128)(2,1)S(1)}, bf16[128,384]{1,0:T(8,128)(2,1)S(1)}, u32[]{:S(2)}, u32[]{:S(2)}) collective-permute-start(bf16[128,384]{1,0:T(8,128)(2,1)S(1)} %get-tuple-element.48), channel_id=1, source_target_pairs={{0,32},{2,34},{4,36},{6,38},{8,40},{10,42},{12,44},{14,46},{16,48}... | collective-permute-start | bytes 294920 | tf_op jit(solution)/shard_map/ppermute | solution.py:531
  33.7 1.4 %collective-permute-start.4 = (bf16[128,384]{1,0:T(8,128)(2,1)S(1)}, bf16[128,384]{1,0:T(8,128)(2,1)S(1)}, u32[]{:S(2)}, u32[]{:S(2)}) collective-permute-start(bf16[128,384]{1,0:T(8,128)(2,1)S(1)} %get-tuple-element.49), channel_id=1, source_target_pairs={{0,96},{2,98},{4,100},{6,102},{8,104},{10,106},{12,108},{14,110},{... | collective-permute-start | bytes 294920 | tf_op jit(solution)/shard_map/ppermute | solution.py:531
  35.1 2.2 %collective-permute-start.5 = (bf16[128,384]{1,0:T(8,128)(2,1)S(1)}, bf16[128,384]{1,0:T(8,128)(2,1)S(1)}, u32[]{:S(2)}, u32[]{:S(2)}) collective-permute-start(bf16[128,384]{1,0:T(8,128)(2,1)S(1)} %get-tuple-element.50), channel_id=1, source_target_pairs={{0,64},{2,66},{4,68},{6,70},{8,72},{10,74},{12,76},{14,78},{16,80}... | collective-permute-start | bytes 294920 | tf_op jit(solution)/shard_map/ppermute | solution.py:531
  37.2 1.4 %collective-permute-done.3 = bf16[128,384]{1,0:T(8,128)(2,1)S(1)} collective-permute-done((bf16[128,384]{1,0:T(8,128)(2,1)S(1)}, bf16[128,384]{1,0:T(8,128)(2,1)S(1)}, u32[]{:S(2)}, u32[]{:S(2)}) %collective-permute-start.3) | collective-permute-done | bytes 98336 | tf_op jit(solution)/shard_map/ppermute | solution.py:531
  38.6 0.0 collective-permute-done.4
  38.6 2.6 %collective-permute-done.5 = bf16[128,384]{1,0:T(8,128)(2,1)S(1)} collective-permute-done((bf16[128,384]{1,0:T(8,128)(2,1)S(1)}, bf16[128,384]{1,0:T(8,128)(2,1)S(1)}, u32[]{:S(2)}, u32[]{:S(2)}) %collective-permute-start.5) | collective-permute-done | bytes 98336 | tf_op jit(solution)/shard_map/ppermute | solution.py:531
  41.2 0.7 collective-permute-start.6
  41.9 2.6 %collective-permute-start.7 = (bf16[136,256]{1,0:T(8,128)(2,1)S(1)}, bf16[136,256]{1,0:T(8,128)(2,1)S(1)}, u32[]{:S(2)}, u32[]{:S(2)}) collective-permute-start(bf16[136,256]{1,0:T(8,128)(2,1)S(1)} %get-tuple-element.61), channel_id=1, source_target_pairs={{0,96},{2,98},{4,100},{6,102},{8,104},{10,106},{12,108},{14,110},{... | collective-permute-start | bytes 208904 | tf_op jit(solution)/shard_map/ppermute | solution.py:531
  44.5 1.6 %collective-permute-start.8 = (bf16[136,256]{1,0:T(8,128)(2,1)S(1)}, bf16[136,256]{1,0:T(8,128)(2,1)S(1)}, u32[]{:S(2)}, u32[]{:S(2)}) collective-permute-start(bf16[136,256]{1,0:T(8,128)(2,1)S(1)} %get-tuple-element.62), channel_id=1, source_target_pairs={{0,64},{2,66},{4,68},{6,70},{8,72},{10,74},{12,76},{14,78},{16,80}... | collective-permute-start | bytes 208904 | tf_op jit(solution)/shard_map/ppermute | solution.py:531
  46.1 3.3 %collective-permute-start.12 = (bf16[512,384]{1,0:T(8,128)(2,1)S(1)}, bf16[512,384]{1,0:T(8,128)(2,1)S(1)}, u32[]{:S(2)}, u32[]{:S(2)}) collective-permute-start(bf16[512,384]{1,0:T(8,128)(2,1)S(1)} %pad_maximum_fusion.refs_0_), channel_id=1, source_target_pairs={{0,16},{2,18},{4,20},{6,22},{8,24},{10,26},{12,28},{14,30},{16,0},... | collective-permute-start | bytes 1179656 | tf_op jit(solution)/shard_map/ppermute | solution.py:531
  49.4 0.7 collective-permute-start.10
  50.1 0.0 collective-permute-done.6
  50.1 1.3 collective-permute-start.9
  51.4 0.0 collective-permute-done.7
  51.4 0.0 collective-permute-done.8
  51.5 0.3 collective-permute-start.11
  51.8 0.0 collective-permute-start.13
  51.8 6.3 %collective-permute-done.11.queries = bf16[544,256]{1,0:T(8,128)(2,1)S(1)} collective-permute-done((bf16[544,256]{1,0:T(8,128)(2,1)S(1)}, bf16[544,256]{1,0:T(8,128)(2,1)S(1)}, u32[]{:S(2)}, u32[]{:S(2)}) %collective-permute-start.11) | collective-permute-done | bytes 278560 | tf_op jit(solution)/shard_map/ppermute | solution.py:531
  58.1 0.7 copy-done.2
  58.8 6.5 %collective-permute-done.10.refs_2_ = bf16[512,384]{1,0:T(8,128)(2,1)S(1)} collective-permute-done((bf16[512,384]{1,0:T(8,128)(2,1)S(1)}, bf16[512,384]{1,0:T(8,128)(2,1)S(1)}, u32[]{:S(2)}, u32[]{:S(2)}) %collective-permute-start.10) | collective-permute-done | bytes 393248 | tf_op jit(solution)/shard_map/ppermute | solution.py:531
  65.3 0.0 collective-permute-done.9.refs_1_
  65.3 0.5 collective-permute-start.16
  65.8 0.1 collective-permute-start.15
  65.9 0.6 dynamic_slice.3.scale
  66.5 1.7 %collective-permute-done.16.refs_7_ = bf16[512,384]{1,0:T(8,128)(2,1)S(1)} collective-permute-done((bf16[512,384]{1,0:T(8,128)(2,1)S(1)}, bf16[512,384]{1,0:T(8,128)(2,1)S(1)}, u32[]{:S(2)}, u32[]{:S(2)}) %collective-permute-start.16) | collective-permute-done | bytes 393248 | tf_op jit(solution)/shard_map/ppermute | solution.py:531
  68.1 0.0 collective-permute-done.14.refs_5_
  68.1 0.1 collective-permute-done.15.refs_6_
  68.3 1.0 copy-done.3
  69.2 9.4 %attend.2 = (bf16[544,256]{1,0:T(8,128)(2,1)S(1)}, f32[8,4096]{1,0:T(8,128)S(1)}) custom-call(f32[1]{0:T(128)} %dynamic_slice.3.scale, bf16[544,256]{1,0:T(8,128)(2,1)S(1)} %copy-done.3, bf16[512,384]{1,0:T(8,128)(2,1)S(1)} %pad_maximum_fusion.refs_0_, bf16[512,384]{1,0:T(8,128)(2,1)S(1)} %collective-permute-done.9.refs_1_, ...), custom_call_target="tpu_custom_call" | custom-call | flops 2281701376 | bytes 4456448 | tf_op jit(solution)/shard_map/attend/pallas_call | solution.py:309
  78.6 1.7 %collective-permute-start.17 = (bf16[544,256]{1,0:T(8,128)(2,1)S(1)}, bf16[544,256]{1,0:T(8,128)(2,1)S(1)}, u32[]{:S(2)}, u32[]{:S(2)}) collective-permute-start(bf16[544,256]{1,0:T(8,128)(2,1)S(1)} %get-tuple-element.72), channel_id=1, source_target_pairs={{0,4},{2,6},{4,0},{6,2},{8,12},{10,14},{12,8},{14,10},{16,20},{18,... | collective-permute-start | bytes 835592 | tf_op jit(solution)/shard_map/ppermute | solution.py:531
  80.3 8.7 %attend.3.a0 = bf16[544,256]{1,0:T(8,128)(2,1)S(1)} custom-call(f32[1]{0:T(128)} %dynamic_slice.3.scale, bf16[544,256]{1,0:T(8,128)(2,1)S(1)} %constant_dynamic-update-slice_fusion.queries, bf16[512,384]{1,0:T(8,128)(2,1)S(1)} %pad_maximum_fusion.refs_0_, bf16[512,384]{1,0:T(8,128)(2,1)S(1)} %collective-permute-done.9.refs_1_, ...), custom_call_target="tpu_custom_call" | custom-call | flops 2281701376 | bytes 4456448 | tf_op jit(solution)/shard_map/attend/pallas_call | solution.py:309
  89.0 0.0 collective-permute-done.17.a1
  89.0 0.5 merge.1
  89.6 1.5 %collective-permute-start.18 = (bf16[136,256]{1,0:T(8,128)(2,1)S(1)}, bf16[136,256]{1,0:T(8,128)(2,1)S(1)}, u32[]{:S(2)}, u32[]{:S(2)}) collective-permute-start(bf16[136,256]{1,0:T(8,128)(2,1)S(1)} %get-tuple-element.74), channel_id=1, source_target_pairs={{0,96},{2,98},{4,100},{6,102},{8,104},{10,106},{12,108},{14,110},{... | collective-permute-start | bytes 208904 | tf_op jit(solution)/shard_map/ppermute | solution.py:531
  91.1 1.2 collective-permute-start.19
  92.3 1.3 collective-permute-start.20
  93.6 0.5 collective-permute-done.18.a1
  94.2 3.0 %collective-permute-done.19.a2 = bf16[136,256]{1,0:T(8,128)(2,1)S(1)} collective-permute-done((bf16[136,256]{1,0:T(8,128)(2,1)S(1)}, bf16[136,256]{1,0:T(8,128)(2,1)S(1)}, u32[]{:S(2)}, u32[]{:S(2)}) %collective-permute-start.19) | collective-permute-done | bytes 69664 | tf_op jit(solution)/shard_map/ppermute | solution.py:531
  97.2 0.7 collective-permute-done.20.a3
  97.9 1.3 output.3
  99.2 2.7 %collective-permute-start.21 = (bf16[136,768]{1,0:T(8,128)(2,1)S(1)}, bf16[136,768]{1,0:T(8,128)(2,1)S(1)}, u32[]{:S(2)}, u32[]{:S(2)}) collective-permute-start(bf16[136,768]{1,0:T(8,128)(2,1)S(1)} %output.3), channel_id=1, source_target_pairs={{0,1},{1,0},{2,3},{3,2},{4,5},{5,4},{6,7},{7,6},{8,9},{9,8},{10,11... | collective-permute-start | bytes 626696 | tf_op jit(solution)/shard_map/ppermute | solution.py:527
  101.9 1.3 output.2.own
  103.2 0.0 copy-start.1
  103.2 3.8 %collective-permute-done.21.other = bf16[136,768]{1,0:T(8,128)(2,1)S(1)} collective-permute-done((bf16[136,768]{1,0:T(8,128)(2,1)S(1)}, bf16[136,768]{1,0:T(8,128)(2,1)S(1)}, u32[]{:S(2)}, u32[]{:S(2)}) %collective-permute-start.21) | collective-permute-done | bytes 208928 | tf_op jit(solution)/shard_map/ppermute | solution.py:527
  107.0 2.3 %decode_send.1 = (bf16[272,768]{1,0:T(8,128)(2,1)S(1)}, bf16[272,768]{1,0:T(8,128)(2,1)S(1)}) custom-call(s32[3]{0:T(128)S(1)} %pad_add_fusion.ids, f32[136,768]{1,0:T(8,128)S(1)} %output.2.own, bf16[136,768]{1,0:T(8,128)(2,1)S(1)} %collective-permute-done.21.other, bf16[272,768]{1,0:T(8,128)(2,1)S(1)} %get-tuple-element.45.mine.encoded, ...), custom_call_target="tpu_custom_call" | custom-call | flops 962592768 | bytes 3538944 | tf_op jit(solution)/shard_map/decode_send/pallas_call | solution.py:400
  109.3 2.8 %collective-permute-start.22 = (bf16[272,768]{1,0:T(8,128)(2,1)S(1)}, bf16[272,768]{1,0:T(8,128)(2,1)S(1)}, u32[]{:S(2)}, u32[]{:S(2)}) collective-permute-start(bf16[272,768]{1,0:T(8,128)(2,1)S(1)} %get-tuple-element.78), channel_id=1, source_target_pairs={{0,1},{1,0},{2,3},{3,2},{4,5},{5,4},{6,7},{7,6},{8,9},{9,8},{10,11... | collective-permute-start | bytes 1253384 | tf_op jit(solution)/shard_map/ppermute | solution.py:527
  112.1 2.1 %decode_own.1.own = f32[272,768]{1,0:T(8,128)S(1)} custom-call(s32[3]{0:T(128)S(1)} %pad_add_fusion.ids, bf16[272,768]{1,0:T(8,128)(2,1)S(1)} %get-tuple-element.77.inputs, bf16[3,768,1536]{2,1,0:T(8,128)(2,1)S(1)} %bitcast.5), custom_call_target="tpu_custom_call" | custom-call | flops 962592768 | bytes 3538944 | tf_op jit(solution)/shard_map/decode_own/pallas_call | solution.py:423
  114.2 6.5 %collective-permute-done.22.other = bf16[272,768]{1,0:T(8,128)(2,1)S(1)} collective-permute-done((bf16[272,768]{1,0:T(8,128)(2,1)S(1)}, bf16[272,768]{1,0:T(8,128)(2,1)S(1)}, u32[]{:S(2)}, u32[]{:S(2)}) %collective-permute-start.22) | collective-permute-done | bytes 417824 | tf_op jit(solution)/shard_map/ppermute | solution.py:527
  120.7 2.2 %slopes.1 = (bf16[256,768]{1,0:T(8,128)(2,1)}, bf16[272,768]{1,0:T(8,128)(2,1)S(1)}, f32[128,768]{1,0:T(8,128)S(1)}) custom-call(s32[3]{0:T(128)S(1)} %pad_add_fusion.ids, f32[272,768]{1,0:T(8,128)S(1)} %decode_own.1.own, bf16[272,768]{1,0:T(8,128)(2,1)S(1)} %collective-permute-done.22.other, bf16[272,768]{1,0:T(8,128)(2,1)S(1)} %get-tuple-element.77.inputs, ...), custom_call_target="tpu_custom_call" | custom-call | flops 6266880 | bytes 2924544 | tf_op jit(solution)/shard_map/slopes/pallas_call | solution.py:464
  122.9 2.9 %collective-permute-start.23 = (bf16[272,768]{1,0:T(8,128)(2,1)S(1)}, bf16[272,768]{1,0:T(8,128)(2,1)S(1)}, u32[]{:S(2)}, u32[]{:S(2)}) collective-permute-start(bf16[272,768]{1,0:T(8,128)(2,1)S(1)} %get-tuple-element.80.slope), channel_id=1, source_target_pairs={{0,1},{1,0},{2,3},{3,2},{4,5},{5,4},{6,7},{7,6},{8,9},{9,8},{10,11... | collective-permute-start | bytes 1253384 | tf_op jit(solution)/shard_map/ppermute | solution.py:527
  125.7 2.3 %backward.2.start = f32[128,768]{1,0:T(8,128)S(1)} custom-call(s32[3]{0:T(128)S(1)} %pad_add_fusion.ids, bf16[272,768]{1,0:T(8,128)(2,1)S(1)} %get-tuple-element.80.slope, f32[128,768]{1,0:T(8,128)S(1)} %get-tuple-element.81.start, bf16[3,768,1536]{2,1,0:T(8,128)(2,1)S(1)} %bitcast.5), custom_call_target="tpu_custom_call" | custom-call | flops 962592768 | bytes 3538944 | tf_op jit(solution)/shard_map/backward/pallas_call | solution.py:502
  128.1 5.2 %collective-permute-done.23.slope = bf16[272,768]{1,0:T(8,128)(2,1)S(1)} collective-permute-done((bf16[272,768]{1,0:T(8,128)(2,1)S(1)}, bf16[272,768]{1,0:T(8,128)(2,1)S(1)}, u32[]{:S(2)}, u32[]{:S(2)}) %collective-permute-start.23) | collective-permute-done | bytes 417824 | tf_op jit(solution)/shard_map/ppermute | solution.py:527
  133.2 3.0 %backward.3 = bf16[128,768]{1,0:T(8,128)(2,1)} custom-call(s32[3]{0:T(128)S(1)} %pad_add_fusion.ids, bf16[272,768]{1,0:T(8,128)(2,1)S(1)} %collective-permute-done.23.slope, f32[128,768]{1,0:T(8,128)S(1)} %backward.2.start, bf16[3,768,1536]{2,1,0:T(8,128)(2,1)S(1)} %bitcast.5), custom_call_target="tpu_custom_call" | custom-call | flops 962592768 | bytes 3538944 | tf_op jit(solution)/shard_map/backward/pallas_call | solution.py:502
  (22 shorter events, 0.1 us)
Async XLA Ops:
  1.5 2.7 %collective-permute-start = (bf16[8,1664]{1,0:T(8,128)(2,1)S(1)}, bf16[8,1664]{1,0:T(8,128)(2,1)S(1)}, u32[]{:S(2)}, u32[]{:S(2)}) collective-permute-start(bf16[8,1664]{1,0:T(8,128)(2,1)S(1)} %get-tuple-element.43), channel_id=1, source_target_pairs={{0,2},{2,4},{4,6},{6,8},{8,10},{10,12},{12,14},{14,16},{16,18},{18... | collective-permute-start | bytes 79880 | tf_op jit(solution)/shard_map/ppermute | solution.py:551
  2.8 5.0 %collective-permute-start.1 = (bf16[8,1664]{1,0:T(8,128)(2,1)S(1)}, bf16[8,1664]{1,0:T(8,128)(2,1)S(1)}, u32[]{:S(2)}, u32[]{:S(2)}) collective-permute-start(bf16[8,1664]{1,0:T(8,128)(2,1)S(1)} %get-tuple-element.44), channel_id=1, source_target_pairs={{2,0},{4,2},{6,4},{8,6},{10,8},{12,10},{14,12},{16,14},{18,16},{20... | collective-permute-start | bytes 79880 | tf_op jit(solution)/shard_map/ppermute | solution.py:552
  7.8 9.0 %copy-start.4 = (f32[1536]{0:T(1024)S(1)}, f32[1536]{0:T(1024)}, u32[]{:S(2)}) copy-start(f32[1536]{0:T(1024)} %param.12) | copy-start | bytes 18436
  13.8 52.1 %copy-start.5 = (f32[4]{0:T(128)S(1)}, f32[4]{0:T(128)}, u32[]{:S(2)}) copy-start(f32[4]{0:T(128)} %param.14) | copy-start | bytes 52
  13.8 12.4 %collective-permute-start.2 = (bf16[272,768]{1,0:T(8,128)(2,1)S(1)}, bf16[272,768]{1,0:T(8,128)(2,1)S(1)}, u32[]{:S(2)}, u32[]{:S(2)}) collective-permute-start(bf16[272,768]{1,0:T(8,128)(2,1)S(1)} %get-tuple-element.45.mine.encoded), channel_id=1, source_target_pairs={{0,1},{1,0},{2,3},{3,2},{4,5},{5,4},{6,7},{7,6},{8,9},{9,8},{10,11... | collective-permute-start | bytes 1253384 | tf_op jit(solution)/shard_map/ppermute | solution.py:527
  28.8 9.8 %collective-permute-start.3 = (bf16[128,384]{1,0:T(8,128)(2,1)S(1)}, bf16[128,384]{1,0:T(8,128)(2,1)S(1)}, u32[]{:S(2)}, u32[]{:S(2)}) collective-permute-start(bf16[128,384]{1,0:T(8,128)(2,1)S(1)} %get-tuple-element.48), channel_id=1, source_target_pairs={{0,32},{2,34},{4,36},{6,38},{8,40},{10,42},{12,44},{14,46},{16,48}... | collective-permute-start | bytes 294920 | tf_op jit(solution)/shard_map/ppermute | solution.py:531
  33.7 4.9 %collective-permute-start.4 = (bf16[128,384]{1,0:T(8,128)(2,1)S(1)}, bf16[128,384]{1,0:T(8,128)(2,1)S(1)}, u32[]{:S(2)}, u32[]{:S(2)}) collective-permute-start(bf16[128,384]{1,0:T(8,128)(2,1)S(1)} %get-tuple-element.49), channel_id=1, source_target_pairs={{0,96},{2,98},{4,100},{6,102},{8,104},{10,106},{12,108},{14,110},{... | collective-permute-start | bytes 294920 | tf_op jit(solution)/shard_map/ppermute | solution.py:531
  35.1 6.1 %collective-permute-start.5 = (bf16[128,384]{1,0:T(8,128)(2,1)S(1)}, bf16[128,384]{1,0:T(8,128)(2,1)S(1)}, u32[]{:S(2)}, u32[]{:S(2)}) collective-permute-start(bf16[128,384]{1,0:T(8,128)(2,1)S(1)} %get-tuple-element.50), channel_id=1, source_target_pairs={{0,64},{2,66},{4,68},{6,70},{8,72},{10,74},{12,76},{14,78},{16,80}... | collective-permute-start | bytes 294920 | tf_op jit(solution)/shard_map/ppermute | solution.py:531
  41.2 8.9 %collective-permute-start.6 = (bf16[136,256]{1,0:T(8,128)(2,1)S(1)}, bf16[136,256]{1,0:T(8,128)(2,1)S(1)}, u32[]{:S(2)}, u32[]{:S(2)}) collective-permute-start(bf16[136,256]{1,0:T(8,128)(2,1)S(1)} %get-tuple-element.60), channel_id=1, source_target_pairs={{0,32},{2,34},{4,36},{6,38},{8,40},{10,42},{12,44},{14,46},{16,48}... | collective-permute-start | bytes 208904 | tf_op jit(solution)/shard_map/ppermute | solution.py:531
  41.9 9.5 %collective-permute-start.7 = (bf16[136,256]{1,0:T(8,128)(2,1)S(1)}, bf16[136,256]{1,0:T(8,128)(2,1)S(1)}, u32[]{:S(2)}, u32[]{:S(2)}) collective-permute-start(bf16[136,256]{1,0:T(8,128)(2,1)S(1)} %get-tuple-element.61), channel_id=1, source_target_pairs={{0,96},{2,98},{4,100},{6,102},{8,104},{10,106},{12,108},{14,110},{... | collective-permute-start | bytes 208904 | tf_op jit(solution)/shard_map/ppermute | solution.py:531
  44.5 6.9 %collective-permute-start.8 = (bf16[136,256]{1,0:T(8,128)(2,1)S(1)}, bf16[136,256]{1,0:T(8,128)(2,1)S(1)}, u32[]{:S(2)}, u32[]{:S(2)}) collective-permute-start(bf16[136,256]{1,0:T(8,128)(2,1)S(1)} %get-tuple-element.62), channel_id=1, source_target_pairs={{0,64},{2,66},{4,68},{6,70},{8,72},{10,74},{12,76},{14,78},{16,80}... | collective-permute-start | bytes 208904 | tf_op jit(solution)/shard_map/ppermute | solution.py:531
  46.1 19.2 %collective-permute-start.12 = (bf16[512,384]{1,0:T(8,128)(2,1)S(1)}, bf16[512,384]{1,0:T(8,128)(2,1)S(1)}, u32[]{:S(2)}, u32[]{:S(2)}) collective-permute-start(bf16[512,384]{1,0:T(8,128)(2,1)S(1)} %pad_maximum_fusion.refs_0_), channel_id=1, source_target_pairs={{0,16},{2,18},{4,20},{6,22},{8,24},{10,26},{12,28},{14,30},{16,0},... | collective-permute-start | bytes 1179656 | tf_op jit(solution)/shard_map/ppermute | solution.py:531
  49.4 15.9 %collective-permute-start.10 = (bf16[512,384]{1,0:T(8,128)(2,1)S(1)}, bf16[512,384]{1,0:T(8,128)(2,1)S(1)}, u32[]{:S(2)}, u32[]{:S(2)}) collective-permute-start(bf16[512,384]{1,0:T(8,128)(2,1)S(1)} %pad_maximum_fusion.refs_0_), channel_id=1, source_target_pairs={{0,24},{2,26},{4,28},{6,30},{8,0},{10,2},{12,4},{14,6},{16,8},{18,... | collective-permute-start | bytes 1179656 | tf_op jit(solution)/shard_map/ppermute | solution.py:531
  50.1 15.2 %collective-permute-start.9 = (bf16[512,384]{1,0:T(8,128)(2,1)S(1)}, bf16[512,384]{1,0:T(8,128)(2,1)S(1)}, u32[]{:S(2)}, u32[]{:S(2)}) collective-permute-start(bf16[512,384]{1,0:T(8,128)(2,1)S(1)} %pad_maximum_fusion.refs_0_), channel_id=1, source_target_pairs={{0,8},{2,10},{4,12},{6,14},{8,16},{10,18},{12,20},{14,22},{16,24},... | collective-permute-start | bytes 1179656 | tf_op jit(solution)/shard_map/ppermute | solution.py:531
  51.5 6.6 %collective-permute-start.11 = (bf16[544,256]{1,0:T(8,128)(2,1)S(1)}, bf16[544,256]{1,0:T(8,128)(2,1)S(1)}, u32[]{:S(2)}, u32[]{:S(2)}) collective-permute-start(bf16[544,256]{1,0:T(8,128)(2,1)S(1)} %constant_dynamic-update-slice_fusion.queries), channel_id=1, source_target_pairs={{0,4},{2,6},{4,0},{6,2},{8,12},{10,14},{12,8},{14,10},{16,20},{18,... | collective-permute-start | bytes 835592 | tf_op jit(solution)/shard_map/ppermute | solution.py:531
  51.8 14.7 %collective-permute-start.13 = (bf16[512,384]{1,0:T(8,128)(2,1)S(1)}, bf16[512,384]{1,0:T(8,128)(2,1)S(1)}, u32[]{:S(2)}, u32[]{:S(2)}) collective-permute-start(bf16[512,384]{1,0:T(8,128)(2,1)S(1)} %pad_maximum_fusion.refs_0_), channel_id=1, source_target_pairs={{0,2},{2,0},{4,6},{6,4},{8,10},{10,8},{12,14},{14,12},{16,18},{18,... | collective-permute-start | bytes 1179656 | tf_op jit(solution)/shard_map/ppermute | solution.py:531
  58.1 0.7 copy-start.2
  65.3 2.9 %collective-permute-start.14 = (bf16[512,384]{1,0:T(8,128)(2,1)S(1)}, bf16[512,384]{1,0:T(8,128)(2,1)S(1)}, u32[]{:S(2)}, u32[]{:S(2)}) collective-permute-start(bf16[512,384]{1,0:T(8,128)(2,1)S(1)} %collective-permute-done.9.refs_1_), channel_id=1, source_target_pairs={{0,2},{2,0},{4,6},{6,4},{8,10},{10,8},{12,14},{14,12},{16,18},{18,... | collective-permute-start | bytes 1179656 | tf_op jit(solution)/shard_map/ppermute | solution.py:531
  65.3 2.8 %collective-permute-start.16 = (bf16[512,384]{1,0:T(8,128)(2,1)S(1)}, bf16[512,384]{1,0:T(8,128)(2,1)S(1)}, u32[]{:S(2)}, u32[]{:S(2)}) collective-permute-start(bf16[512,384]{1,0:T(8,128)(2,1)S(1)} %collective-permute-done.12.refs_3_), channel_id=1, source_target_pairs={{0,2},{2,0},{4,6},{6,4},{8,10},{10,8},{12,14},{14,12},{16,18},{18,... | collective-permute-start | bytes 1179656 | tf_op jit(solution)/shard_map/ppermute | solution.py:531
  65.8 2.5 %collective-permute-start.15 = (bf16[512,384]{1,0:T(8,128)(2,1)S(1)}, bf16[512,384]{1,0:T(8,128)(2,1)}, u32[]{:S(2)}, u32[]{:S(2)}) collective-permute-start(bf16[512,384]{1,0:T(8,128)(2,1)S(1)} %collective-permute-done.10.refs_2_), channel_id=1, source_target_pairs={{0,2},{2,0},{4,6},{6,4},{8,10},{10,8},{12,14},{14,12},{16,18},{18,... | collective-permute-start | bytes 1179656 | tf_op jit(solution)/shard_map/ppermute | solution.py:531
  66.5 31.5 %copy-start = (bf16[768,1536]{1,0:T(8,128)(2,1)S(1)}, bf16[768,1536]{1,0:T(8,128)(2,1)}, u32[]{:S(2)}) copy-start(bf16[768,1536]{1,0:T(8,128)(2,1)} %weight.7) | copy-start | bytes 7077892
  68.3 1.0 copy-start.3
  78.6 10.4 %collective-permute-start.17 = (bf16[544,256]{1,0:T(8,128)(2,1)S(1)}, bf16[544,256]{1,0:T(8,128)(2,1)S(1)}, u32[]{:S(2)}, u32[]{:S(2)}) collective-permute-start(bf16[544,256]{1,0:T(8,128)(2,1)S(1)} %get-tuple-element.72), channel_id=1, source_target_pairs={{0,4},{2,6},{4,0},{6,2},{8,12},{10,14},{12,8},{14,10},{16,20},{18,... | collective-permute-start | bytes 835592 | tf_op jit(solution)/shard_map/ppermute | solution.py:531
  80.3 26.7 %slice-start = ((s8[7077888]{0:T(1024)(128)(4,1)}), s8[4194304]{0:T(1024)(128)(4,1)S(1)}, s32[]{:S(2)}) async-start(s8[7077888]{0:T(1024)(128)(4,1)} %bitcast.4), calls=%async_computation | async-start | bytes 8388608
  80.3 26.7 %slice-start.1 = ((s8[7077888]{0:T(1024)(128)(4,1)}), s8[2883584]{0:T(1024)(128)(4,1)S(1)}, s32[]{:S(2)}) async-start(s8[7077888]{0:T(1024)(128)(4,1)} %bitcast.4), calls=%async_computation.1 | async-start | bytes 5767168
  89.6 4.6 %collective-permute-start.18 = (bf16[136,256]{1,0:T(8,128)(2,1)S(1)}, bf16[136,256]{1,0:T(8,128)(2,1)S(1)}, u32[]{:S(2)}, u32[]{:S(2)}) collective-permute-start(bf16[136,256]{1,0:T(8,128)(2,1)S(1)} %get-tuple-element.74), channel_id=1, source_target_pairs={{0,96},{2,98},{4,100},{6,102},{8,104},{10,106},{12,108},{14,110},{... | collective-permute-start | bytes 208904 | tf_op jit(solution)/shard_map/ppermute | solution.py:531
  91.1 6.1 %collective-permute-start.19 = (bf16[136,256]{1,0:T(8,128)(2,1)S(1)}, bf16[136,256]{1,0:T(8,128)(2,1)S(1)}, u32[]{:S(2)}, u32[]{:S(2)}) collective-permute-start(bf16[136,256]{1,0:T(8,128)(2,1)S(1)} %get-tuple-element.75), channel_id=1, source_target_pairs={{0,64},{2,66},{4,68},{6,70},{8,72},{10,74},{12,76},{14,78},{16,80}... | collective-permute-start | bytes 208904 | tf_op jit(solution)/shard_map/ppermute | solution.py:531
  92.3 5.6 %collective-permute-start.20 = (bf16[136,256]{1,0:T(8,128)(2,1)S(1)}, bf16[136,256]{1,0:T(8,128)(2,1)S(1)}, u32[]{:S(2)}, u32[]{:S(2)}) collective-permute-start(bf16[136,256]{1,0:T(8,128)(2,1)S(1)} %get-tuple-element.76), channel_id=1, source_target_pairs={{0,32},{2,34},{4,36},{6,38},{8,40},{10,42},{12,44},{14,46},{16,48}... | collective-permute-start | bytes 208904 | tf_op jit(solution)/shard_map/ppermute | solution.py:531
  99.2 7.8 %collective-permute-start.21 = (bf16[136,768]{1,0:T(8,128)(2,1)S(1)}, bf16[136,768]{1,0:T(8,128)(2,1)S(1)}, u32[]{:S(2)}, u32[]{:S(2)}) collective-permute-start(bf16[136,768]{1,0:T(8,128)(2,1)S(1)} %output.3), channel_id=1, source_target_pairs={{0,1},{1,0},{2,3},{3,2},{4,5},{5,4},{6,7},{7,6},{8,9},{9,8},{10,11... | collective-permute-start | bytes 626696 | tf_op jit(solution)/shard_map/ppermute | solution.py:527
  103.2 17.5 %copy-start.1 = (bf16[256,1536]{1,0:T(8,128)(2,1)S(1)}, bf16[256,1536]{1,0:T(8,128)(2,1)}, u32[]{:S(2)}) copy-start(bf16[256,1536]{1,0:T(8,128)(2,1)} %grad.3) | copy-start | bytes 2359300
  109.3 11.4 %collective-permute-start.22 = (bf16[272,768]{1,0:T(8,128)(2,1)S(1)}, bf16[272,768]{1,0:T(8,128)(2,1)S(1)}, u32[]{:S(2)}, u32[]{:S(2)}) collective-permute-start(bf16[272,768]{1,0:T(8,128)(2,1)S(1)} %get-tuple-element.78), channel_id=1, source_target_pairs={{0,1},{1,0},{2,3},{3,2},{4,5},{5,4},{6,7},{7,6},{8,9},{9,8},{10,11... | collective-permute-start | bytes 1253384 | tf_op jit(solution)/shard_map/ppermute | solution.py:527
  122.9 10.4 %collective-permute-start.23 = (bf16[272,768]{1,0:T(8,128)(2,1)S(1)}, bf16[272,768]{1,0:T(8,128)(2,1)S(1)}, u32[]{:S(2)}, u32[]{:S(2)}) collective-permute-start(bf16[272,768]{1,0:T(8,128)(2,1)S(1)} %get-tuple-element.80.slope), channel_id=1, source_target_pairs={{0,1},{1,0},{2,3},{3,2},{4,5},{5,4},{6,7},{7,6},{8,9},{9,8},{10,11... | collective-permute-start | bytes 1253384 | tf_op jit(solution)/shard_map/ppermute | solution.py:527

commit v5 on v4

--- a/solution.py
+++ b/solution.py
@@ -87,6 +87,10 @@
     last[:, feats:] = letters[OWN - 8 :].astype(BF16)
     first[:, :feats] = head[...].astype(F32)[:8].astype(BF16)
     first[:, feats:] = letters[:8].astype(BF16)
+
+
+def near_memory(value):
+    return pltpu.with_memory_space_constraint(value, pltpu.VMEM)
 
 
 def far_memory(value):
@@ -244,49 +248,84 @@
 LOG2E = 1.4426950408889634
 
 
-def attend_kernel(count, again, scale, queries, *refs):
+def attend_kernel(count, known, resumed, final, ids, scale, queries, *refs):
     pieces, refs = refs[:count], refs[count:]
-    if again:
-        inverse, out = refs
-    else:
-        out, inverse = refs
-    chunk = pieces[0].shape[0]
+    inverses, refs = refs[:known], refs[known:]
+    if resumed:
+        (old_mixed, old_stats), refs = refs[:2], refs[2:]
+    sizes = [ref.shape[0] for ref in pieces]
+    starts = [sum(sizes[:i]) for i in range(count)]
 
     def keys(ref):
         return jnp.concatenate([ref[:, :128], ref[:, 256:]], axis=1)
 
-    if not again:
+    if not known:
+        outs, inverse = refs[:-1], refs[-1]
         lane = lax.broadcasted_iota(jnp.int32, (8, 256), 1)
         ones = (lane < HEAD).astype(F32).astype(BF16)
-        for at, ref in enumerate(pieces):
+        for at, size, ref in zip(starts, sizes, pieces):
             key = keys(ref).astype(F32)
             square = key * key
             high = square.astype(BF16)
             rest = (square - high.astype(F32)).astype(BF16)
             total = dot_t(ones, high) + dot_t(ones, rest)
-            inverse[:, at * chunk : (at + 1) * chunk] = lax.rsqrt(total * (1.0 / HEAD) + EPS)
-
-    def block(i):
-        rows = lanes(i * BLOCK, BLOCK)
-        query = queries[rows, :]
-        wide = query.astype(F32)
-        own = lax.rsqrt(jnp.sum(wide * wide, axis=1, keepdims=True) * (1.0 / HEAD) + EPS)
-        factor = own * (scale[0] * (LOG2E / HEAD))
-        scores = []
-        peak = None
-        for at, ref in enumerate(pieces):
-            part = dot_t(query, keys(ref)) * inverse[0:1, at * chunk : (at + 1) * chunk]
+            inverse[:, at : at + size] = lax.rsqrt(total * (1.0 / HEAD) + EPS)
+        inverses = (inverse,)
+    else:
+        outs = refs
+
+    def inverse_of(at, size):
+        for ref in inverses:
+            if at < ref.shape[1]:
+                return ref[0:1, at : at + size]
+            at -= ref.shape[1]
+
+    groups, room = [], 0
+    for triple in zip(starts, sizes, pieces):
+        if room < triple[1]:
+            groups.append([])
+            room = 2048
+        groups[-1].append(triple)
+        room -= triple[1]
+
+    def unit(query, factor, group):
+        scores, peak = [], None
+        for at, size, ref in group:
+            part = dot_t(query, keys(ref)) * inverse_of(at, size)
             top = jnp.max(part, axis=1, keepdims=True)
             peak = top if peak is None else jnp.maximum(peak, top)
             scores.append(part)
         total, mixed = None, None
-        for part, ref in zip(scores, pieces):
+        for part, (_, _, ref) in zip(scores, group):
             exps = jnp.exp2((part - peak) * factor)
             sums = jnp.sum(exps, axis=1, keepdims=True)
             values = jnp.concatenate([ref[:, 128:256], ref[:, 256:]], axis=1)
             term = dot(exps.astype(BF16), values)
             total = sums if total is None else total + sums
             mixed = term if mixed is None else mixed + term
+        return peak, total, mixed
+
+    for begin in range(0, queries.shape[0], BLOCK):
+        rows = slice(begin, begin + BLOCK)
+        query = queries[rows, :]
+        wide = query.astype(F32)
+        own = lax.rsqrt(jnp.sum(wide * wide, axis=1, keepdims=True) * (1.0 / HEAD) + EPS)
+        factor = own * (scale[ids[1]] * (LOG2E / HEAD))
+        states = [unit(query, factor, group) for group in groups]
+        if resumed:
+            states.append((old_stats[rows, 0:1], old_stats[rows, 64:65], old_mixed[rows, :]))
+        peak = functools.reduce(jnp.maximum, [state[0] for state in states])
+        if len(states) > 1:
+            shrink = [jnp.exp2((state[0] - peak) * factor) for state in states]
+            total = sum(state[1] * part for state, part in zip(states, shrink))
+            mixed = sum(state[2] * part for state, part in zip(states, shrink))
+        else:
+            _, total, mixed = states[0]
+        if not final:
+            outs[0][rows, :] = mixed
+            half = lax.broadcasted_iota(jnp.int32, (BLOCK, 128), 1) < 64
+            outs[1][rows, :] = jnp.where(half, peak, total)
+            continue
         mixed = mixed / total
         weight = peak * factor + jnp.log(total) * LOG2E
         high = weight.astype(BF16).astype(F32)
@@ -296,25 +335,27 @@
         mixed = jnp.where(place == 128, high, mixed)
         mixed = jnp.where(place == 129, mid, mixed)
         mixed = jnp.where(place == 130, rest - mid, mixed)
-        out[rows, :] = mixed.astype(BF16)
-
-    tiles(queries.shape[0] // BLOCK, block)
-
-
-def attend(scale, queries, pieces, inverse=None):
-    again = inverse is not None
+        outs[0][rows, :] = mixed.astype(BF16)
+
+
+def attend(ids, scale, queries, pieces, inverses=(), state=(), final=True):
     rows = queries.shape[0]
-    keys = len(pieces) * pieces[0].shape[0]
-    outs = [shape((rows, 256), BF16)] + ([] if again else [shape((8, keys), F32)])
-    return pl.pallas_call(
-        functools.partial(attend_kernel, len(pieces), again),
-        in_specs=[SM] + [VM] * (1 + len(pieces) + again),
+    keys = sum(piece.shape[0] for piece in pieces)
+    if final:
+        outs = [shape((rows, 256), BF16)]
+    else:
+        outs = [shape((rows, 256), F32), shape((rows, 128), F32)]
+    if not inverses:
+        outs.append(shape((8, keys), F32))
+    return pl.pallas_call(
+        functools.partial(attend_kernel, len(pieces), len(inverses), bool(state), final),
+        in_specs=[SM, SM] + [VM] * (1 + len(pieces) + len(inverses) + len(state)),
         out_specs=[VM] * len(outs),
         out_shape=outs,
-        compiler_params=params(24),
+        compiler_params=params(28),
         cost_estimate=cost(4 * rows * keys * 256, 8 * rows * 1024),
         name="attend",
-    )(scale, queries, *pieces, *([inverse] if again else []))
+    )(ids, scale, near_memory(queries), *pieces, *inverses, *state)
 
 
 def merge_kernel(a0, a1, *outs):
@@ -563,16 +604,21 @@
 
     keyvals = regroup(keyvals)
     keyvals, *queries = lax.optimization_barrier((keyvals, *queries))
-    pieces = [send(keyvals, dz=d) for d in (1, 3, 2)]
+    near = [send(keyvals, dz=1), send(keyvals, dz=3)]
     queries = regroup(queries)
     others = send(queries, dy=1)
-    pieces[0], pieces[1], others = lax.optimization_barrier((pieces[0], pieces[1], others))
-    pieces = [keyvals] + pieces
+    near[0], near[1], others = lax.optimization_barrier((near[0], near[1], others))
+    half = keyvals.shape[0] // 2
+    far = [send(near[0][:half], dz=1), send(near[1][half:], dz=3)]
+    pieces = [keyvals] + near
     pieces += [send(piece, dc=1) for piece in pieces]
-    scale = lax.dynamic_slice_in_dim(logit_scale, x, 1)
-    other, inverse = attend(scale, others, pieces)
+    *state, inverse = attend(ids, logit_scale, others, pieces, final=False)
+    *far, state[0], state[1] = lax.optimization_barrier((*far, *state))
+    far = jnp.concatenate(far, axis=0)
+    late = [far, send(far, dc=1)]
+    other, later = attend(ids, logit_scale, others, late, state=state)
     other = send(other, dy=1)
-    own = attend(scale, queries, pieces, inverse)[0]
+    own = attend(ids, logit_scale, queries, pieces + late, inverses=[inverse, later])[0]
     mixed = merge([own, other])
     heads = [mixed[0], send(mixed[1], dx=-1), send(mixed[3], dx=-2), send(mixed[2], dx=-3)]
 

time: 137 us -> 128 us (0.934)
  Pallas kernels: 42.5 us -> 36.3 us
  local copies, waits for them, and re-layouts: 2.31 us -> 0.16 us
  starting transfers between devices: 39.2 us -> 37.1 us
  waiting for transfers between devices: 51.3 us -> 53.2 us
    pallas_call x2 -> x3, Pallas kernels: 18.1 us -> 11.8 us  [attend(): pl.pallas_call(functools.partial(attend_kernel, len(pieces), len(inverses...]
    ppermute x18 -> x19, waiting for transfers between devices: 22.8 us -> 27.9 us  [send(): return lax.ppermute(value, 'seq', moves(**step))]
    ppermute x4, waiting for transfers between devices: 24.9 us -> 21.7 us  [swap(): return lax.ppermute(value, 'head', [(0, 1), (1, 0)])]
    ppermute x18 -> x19, starting transfers between devices: 25.2 us -> 22.7 us  [send(): return lax.ppermute(value, 'seq', moves(**step))]
    unnamed x19 -> x16, local copies, waits for them, and re-layouts: 1.71 us -> 0.07 us
  transfers between devices with their start and end apart: 24 -> 25, of which waited for: 14 -> 17; matrix products, arithmetic and copies ran while one was open for 1% -> 0% of each run, Pallas kernels for 11% -> 11%
where the time goes in v5:
time: 128 us
  waiting for transfers between devices  53.2 us (42%)
  starting transfers between devices  37.1 us (29%)
  Pallas kernels  36.3 us (28%)
    ppermute x19, waiting for transfers between devices, send(): return lax.ppermute(value, 'seq', moves(**step))  27.9 us
    ppermute x19, starting transfers between devices, send(): return lax.ppermute(value, 'seq', moves(**step))  22.7 us
    ppermute x4, waiting for transfers between devices, swap(): return lax.ppermute(value, 'head', [(0, 1), (1, 0)])  21.7 us
    pallas_call x3, Pallas kernels, attend(): pl.pallas_call(functools.partial(attend_kernel, len(pieces), len(inverses...  11.8 us
    ppermute x4, starting transfers between devices, swap(): return lax.ppermute(value, 'head', [(0, 1), (1, 0)])  11.8 us
    pallas_call x1, Pallas kernels, encode(): pl.pallas_call(encode_kernel, in_specs=[SM, VM, VM, VM, HBM, HBM, HBM], o...  6 us
    pallas_call x2, Pallas kernels, backward(): pl.pallas_call(functools.partial(backward_kernel, mine), in_specs=[SM] +...  5.35 us
    ppermute x1, waiting for transfers between devices, per_device(): after = lax.ppermute(first, 'seq', [(i + 1, i) for i in range(63)])  3.59 us
  transfers between devices with their start and end apart: 25, of which 17 were waited for; matrix products, arithmetic and copies ran while one was open for 0% of the time, Pallas kernels for 11%

profile of v5, /device:TPU:0, one launch (start us, length us, event | category | flops | bytes accessed | tf_op | source)
XLA Modules:
  0.0 127.8 jit_solution(17084757447380876049)
XLA Ops:
  0.6 0.9 prepare.1
  1.5 1.3 %collective-permute-start = (bf16[8,1664]{1,0:T(8,128)(2,1)S(1)}, bf16[8,1664]{1,0:T(8,128)(2,1)S(1)}, u32[]{:S(2)}, u32[]{:S(2)}) collective-permute-start(bf16[8,1664]{1,0:T(8,128)(2,1)S(1)} %get-tuple-element.50), channel_id=1, source_target_pairs={{0,2},{2,4},{4,6},{6,8},{8,10},{10,12},{12,14},{14,16},{16,18},{18... | collective-permute-start | bytes 79880 | tf_op jit(solution)/shard_map/ppermute | solution.py:592
  2.8 1.3 %collective-permute-start.1 = (bf16[8,1664]{1,0:T(8,128)(2,1)S(1)}, bf16[8,1664]{1,0:T(8,128)(2,1)S(1)}, u32[]{:S(2)}, u32[]{:S(2)}) collective-permute-start(bf16[8,1664]{1,0:T(8,128)(2,1)S(1)} %get-tuple-element.51), channel_id=1, source_target_pairs={{2,0},{4,2},{6,4},{8,6},{10,8},{12,10},{14,12},{16,14},{18,16},{20... | collective-permute-start | bytes 79880 | tf_op jit(solution)/shard_map/ppermute | solution.py:593
  4.1 0.1 pad_add_fusion.ids
  4.2 3.6 %collective-permute-done.1.after = bf16[8,1664]{1,0:T(8,128)(2,1)S(1)} collective-permute-done((bf16[8,1664]{1,0:T(8,128)(2,1)S(1)}, bf16[8,1664]{1,0:T(8,128)(2,1)S(1)}, u32[]{:S(2)}, u32[]{:S(2)}) %collective-permute-start.1) | collective-permute-done | bytes 26656 | tf_op jit(solution)/shard_map/ppermute | solution.py:593
  7.8 6.0 %encode.1 = (bf16[272,768]{1,0:T(8,128)(2,1)S(1)}, bf16[3,1536,768]{2,1,0:T(8,128)(2,1)S(1)}) custom-call(s32[3]{0:T(128)S(1)} %pad_add_fusion.ids, bf16[128,128]{1,0:T(8,128)(2,1)S(1)} %get-tuple-element.49.codes, bf16[8,1664]{1,0:T(8,128)(2,1)S(1)} %collective-permute-done.before, bf16[8,1664]{1,0:T(8,128)(2,1)S(1)} %collective-permute-done.1.after, ...), custom_call_target="tpu_custom_call" | custom-call | flops 1925185536 | bytes 14155776 | tf_op jit(solution)/shard_map/encode/pallas_call | solution.py:176
  13.8 0.0 copy-start.2
  13.8 3.0 %collective-permute-start.2 = (bf16[272,768]{1,0:T(8,128)(2,1)S(1)}, bf16[272,768]{1,0:T(8,128)(2,1)S(1)}, u32[]{:S(2)}, u32[]{:S(2)}) collective-permute-start(bf16[272,768]{1,0:T(8,128)(2,1)S(1)} %get-tuple-element.52.mine.encoded), channel_id=1, source_target_pairs={{0,1},{1,0},{2,3},{3,2},{4,5},{5,4},{6,7},{7,6},{8,9},{9,8},{10,11... | collective-permute-start | bytes 1253384 | tf_op jit(solution)/shard_map/ppermute | solution.py:568
  16.8 9.4 %collective-permute-done.2.theirs = bf16[272,768]{1,0:T(8,128)(2,1)S(1)} collective-permute-done((bf16[272,768]{1,0:T(8,128)(2,1)S(1)}, bf16[272,768]{1,0:T(8,128)(2,1)S(1)}, u32[]{:S(2)}, u32[]{:S(2)}) %collective-permute-start.2) | collective-permute-done | bytes 417824 | tf_op jit(solution)/shard_map/ppermute | solution.py:568
  26.3 2.6 %project.1 = (bf16[136,256]{1,0:T(8,128)(2,1)S(1)}, bf16[136,256]{1,0:T(8,128)(2,1)S(1)}, bf16[136,256]{1,0:T(8,128)(2,1)S(1)}, bf16[136,256]{1,0:T(8,128)(2,1)S...) custom-call(s32[3]{0:T(128)S(1)} %pad_add_fusion.ids, ...), custom_call_target="tpu_custom_call" | custom-call | flops 962592768 | bytes 7077888 | tf_op jit(solution)/shard_map/project/pallas_call | solution.py:235
  28.9 4.8 %collective-permute-start.3 = (bf16[128,384]{1,0:T(8,128)(2,1)S(1)}, bf16[128,384]{1,0:T(8,128)(2,1)S(1)}, u32[]{:S(2)}, u32[]{:S(2)}) collective-permute-start(bf16[128,384]{1,0:T(8,128)(2,1)S(1)} %get-tuple-element.55), channel_id=1, source_target_pairs={{0,32},{2,34},{4,36},{6,38},{8,40},{10,42},{12,44},{14,46},{16,48}... | collective-permute-start | bytes 294920 | tf_op jit(solution)/shard_map/ppermute | solution.py:572
  33.7 1.4 %collective-permute-start.4 = (bf16[128,384]{1,0:T(8,128)(2,1)S(1)}, bf16[128,384]{1,0:T(8,128)(2,1)S(1)}, u32[]{:S(2)}, u32[]{:S(2)}) collective-permute-start(bf16[128,384]{1,0:T(8,128)(2,1)S(1)} %get-tuple-element.56), channel_id=1, source_target_pairs={{0,96},{2,98},{4,100},{6,102},{8,104},{10,106},{12,108},{14,110},{... | collective-permute-start | bytes 294920 | tf_op jit(solution)/shard_map/ppermute | solution.py:572
  35.1 2.2 %collective-permute-start.5 = (bf16[128,384]{1,0:T(8,128)(2,1)S(1)}, bf16[128,384]{1,0:T(8,128)(2,1)S(1)}, u32[]{:S(2)}, u32[]{:S(2)}) collective-permute-start(bf16[128,384]{1,0:T(8,128)(2,1)S(1)} %get-tuple-element.57), channel_id=1, source_target_pairs={{0,64},{2,66},{4,68},{6,70},{8,72},{10,74},{12,76},{14,78},{16,80}... | collective-permute-start | bytes 294920 | tf_op jit(solution)/shard_map/ppermute | solution.py:572
  37.3 1.4 %collective-permute-done.3 = bf16[128,384]{1,0:T(8,128)(2,1)S(1)} collective-permute-done((bf16[128,384]{1,0:T(8,128)(2,1)S(1)}, bf16[128,384]{1,0:T(8,128)(2,1)S(1)}, u32[]{:S(2)}, u32[]{:S(2)}) %collective-permute-start.3) | collective-permute-done | bytes 98336 | tf_op jit(solution)/shard_map/ppermute | solution.py:572
  38.6 0.0 collective-permute-done.4
  38.6 2.6 %collective-permute-done.5 = bf16[128,384]{1,0:T(8,128)(2,1)S(1)} collective-permute-done((bf16[128,384]{1,0:T(8,128)(2,1)S(1)}, bf16[128,384]{1,0:T(8,128)(2,1)S(1)}, u32[]{:S(2)}, u32[]{:S(2)}) %collective-permute-start.5) | collective-permute-done | bytes 98336 | tf_op jit(solution)/shard_map/ppermute | solution.py:572
  41.2 0.7 collective-permute-start.6
  41.9 2.6 %collective-permute-start.7 = (bf16[136,256]{1,0:T(8,128)(2,1)S(1)}, bf16[136,256]{1,0:T(8,128)(2,1)S(1)}, u32[]{:S(2)}, u32[]{:S(2)}) collective-permute-start(bf16[136,256]{1,0:T(8,128)(2,1)S(1)} %get-tuple-element.68), channel_id=1, source_target_pairs={{0,96},{2,98},{4,100},{6,102},{8,104},{10,106},{12,108},{14,110},{... | collective-permute-start | bytes 208904 | tf_op jit(solution)/shard_map/ppermute | solution.py:572
  44.5 1.6 %collective-permute-start.8 = (bf16[136,256]{1,0:T(8,128)(2,1)S(1)}, bf16[136,256]{1,0:T(8,128)(2,1)S(1)}, u32[]{:S(2)}, u32[]{:S(2)}) collective-permute-start(bf16[136,256]{1,0:T(8,128)(2,1)S(1)} %get-tuple-element.69), channel_id=1, source_target_pairs={{0,64},{2,66},{4,68},{6,70},{8,72},{10,74},{12,76},{14,78},{16,80}... | collective-permute-start | bytes 208904 | tf_op jit(solution)/shard_map/ppermute | solution.py:572
  46.1 3.4 %collective-permute-start.10 = (bf16[512,384]{1,0:T(8,128)(2,1)S(1)}, bf16[512,384]{1,0:T(8,128)(2,1)S(1)}, u32[]{:S(2)}, u32[]{:S(2)}) collective-permute-start(bf16[512,384]{1,0:T(8,128)(2,1)S(1)} %pad_maximum_fusion.refs_0_), channel_id=1, source_target_pairs={{0,24},{2,26},{4,28},{6,30},{8,0},{10,2},{12,4},{14,6},{16,8},{18,... | collective-permute-start | bytes 1179656 | tf_op jit(solution)/shard_map/ppermute | solution.py:572
  49.6 0.0 collective-permute-done.7
  49.6 0.8 collective-permute-done.8
  50.4 0.3 collective-permute-start.11
  50.7 6.4 %collective-permute-done.11.queries = bf16[544,256]{1,0:T(8,128)(2,1)S(1)} collective-permute-done((bf16[544,256]{1,0:T(8,128)(2,1)S(1)}, bf16[544,256]{1,0:T(8,128)(2,1)S(1)}, u32[]{:S(2)}, u32[]{:S(2)}) %collective-permute-start.11) | collective-permute-done | bytes 278560 | tf_op jit(solution)/shard_map/ppermute | solution.py:572
  57.0 0.0 collective-permute-done.10.refs_2_
  57.0 1.9 %collective-permute-done.9.refs_1_ = bf16[512,384]{1,0:T(8,128)(2,1)S(1)} collective-permute-done((bf16[512,384]{1,0:T(8,128)(2,1)S(1)}, bf16[512,384]{1,0:T(8,128)(2,1)S(1)}, u32[]{:S(2)}, u32[]{:S(2)}) %collective-permute-start.9) | collective-permute-done | bytes 393248 | tf_op jit(solution)/shard_map/ppermute | solution.py:572
  58.9 0.5 collective-permute-start.14
  59.5 2.6 %collective-permute-start.16 = (bf16[256,384]{1,0:T(8,128)(2,1)S(1)}, bf16[256,384]{1,0:T(8,128)(2,1)S(1)}, u32[]{:S(2)}, u32[]{:S(2)}) collective-permute-start(bf16[256,384]{1,0:T(8,128)(2,1)S(1)} %slice.7), channel_id=1, source_target_pairs={{0,24},{2,26},{4,28},{6,30},{8,0},{10,2},{12,4},{14,6},{16,8},{18,... | collective-permute-start | bytes 589832 | tf_op jit(solution)/shard_map/ppermute | solution.py:572
  62.1 0.0 collective-permute-start.15
  62.1 0.0 collective-permute-done.12.refs_3_
  62.1 0.0 collective-permute-done.13.refs_4_
  62.1 4.0 %attend.3 = (f32[544,256]{1,0:T(8,128)S(1)}, f32[544,128]{1,0:T(8,128)S(1)}, f32[8,3072]{1,0:T(8,128)S(1)}) custom-call(s32[3]{0:T(128)S(1)} %pad_add_fusion.ids, f32[4]{0:T(128)S(1)} %copy-done.2, bf16[544,256]{1,0:T(8,128)(2,1)S(1)} %collective-permute-done.11.queries, bf16[512,384]{1,0:T(8,128)(2,1)S(1)} %pad_maximum_fusion.refs_0_, ...), custom_call_target="tpu_custom_call" | custom-call | flops 1711276032 | bytes 4456448 | tf_op jit(solution)/shard_map/attend/pallas_call | solution.py:350
  66.1 0.0 copy-start
  66.1 0.4 collective-permute-done.16
  66.5 3.4 %collective-permute-done.15 = bf16[256,384]{1,0:T(8,128)(2,1)S(1)} collective-permute-done((bf16[256,384]{1,0:T(8,128)(2,1)S(1)}, bf16[256,384]{1,0:T(8,128)(2,1)S(1)}, u32[]{:S(2)}, u32[]{:S(2)}) %collective-permute-start.15) | collective-permute-done | bytes 196640 | tf_op jit(solution)/shard_map/ppermute | solution.py:572
  70.0 0.1 collective-permute-start.17
  70.1 1.7 %collective-permute-done.17.refs_1_.refs_7_ = bf16[512,384]{1,0:T(8,128)(2,1)S(1)} collective-permute-done((bf16[512,384]{1,0:T(8,128)(2,1)S(1)}, bf16[512,384]{1,0:T(8,128)(2,1)S(1)}, u32[]{:S(2)}, u32[]{:S(2)}) %collective-permute-start.17) | collective-permute-done | bytes 393248 | tf_op jit(solution)/shard_map/ppermute | solution.py:572
  71.8 3.5 %attend.4 = (bf16[544,256]{1,0:T(8,128)(2,1)S(1)}, f32[8,1024]{1,0:T(8,128)S(1)}) custom-call(s32[3]{0:T(128)S(1)} %pad_add_fusion.ids, f32[4]{0:T(128)S(1)} %copy-done.2, bf16[544,256]{1,0:T(8,128)(2,1)S(1)} %collective-permute-done.11.queries, bf16[512,384]{1,0:T(8,128)(2,1)S(1)} %constant_dynamic-update-slice_fusion.4.refs_0_.refs_6_, ...), custom_call_target="tpu_custom_call" | custom-call | flops 570425344 | bytes 4456448 | tf_op jit(solution)/shard_map/attend/pallas_call | solution.py:350
  75.3 0.1 collective-permute-start.18
  75.4 0.0 slice-start
  75.4 0.0 slice-start.1
  75.4 4.4 %attend.5.a0 = bf16[544,256]{1,0:T(8,128)(2,1)S(1)} custom-call(s32[3]{0:T(128)S(1)} %pad_add_fusion.ids, f32[4]{0:T(128)S(1)} %copy-done.2, bf16[544,256]{1,0:T(8,128)(2,1)S(1)} %constant_dynamic-update-slice_fusion.queries, bf16[512,384]{1,0:T(8,128)(2,1)S(1)} %pad_maximum_fusion.refs_0_, bf16[512,384]{1,0:T(8,128)(2,1)S(1)} %collective-permute-done.9.refs_1_, ...), custom_call_target="tpu_custom_call" | custom-call | flops 2281701376 | bytes 4456448 | tf_op jit(solution)/shard_map/attend/pallas_call | solution.py:350
  79.8 4.3 %collective-permute-done.18.a1 = bf16[544,256]{1,0:T(8,128)(2,1)S(1)} collective-permute-done((bf16[544,256]{1,0:T(8,128)(2,1)S(1)}, bf16[544,256]{1,0:T(8,128)(2,1)S(1)}, u32[]{:S(2)}, u32[]{:S(2)}) %collective-permute-start.18) | collective-permute-done | bytes 278560 | tf_op jit(solution)/shard_map/ppermute | solution.py:572
  84.1 0.5 merge.1
  84.6 0.7 collective-permute-start.19
  85.3 1.0 collective-permute-start.20
  86.3 0.8 collective-permute-start.21
  87.1 1.9 %collective-permute-done.19.a1 = bf16[136,256]{1,0:T(8,128)(2,1)S(1)} collective-permute-done((bf16[136,256]{1,0:T(8,128)(2,1)S(1)}, bf16[136,256]{1,0:T(8,128)(2,1)S(1)}, u32[]{:S(2)}, u32[]{:S(2)}) %collective-permute-start.19) | collective-permute-done | bytes 69664 | tf_op jit(solution)/shard_map/ppermute | solution.py:572
  89.0 2.8 %collective-permute-done.20.a2 = bf16[136,256]{1,0:T(8,128)(2,1)S(1)} collective-permute-done((bf16[136,256]{1,0:T(8,128)(2,1)S(1)}, bf16[136,256]{1,0:T(8,128)(2,1)S(1)}, u32[]{:S(2)}, u32[]{:S(2)}) %collective-permute-start.20) | collective-permute-done | bytes 69664 | tf_op jit(solution)/shard_map/ppermute | solution.py:572
  91.8 0.5 collective-permute-done.21.a3
  92.2 1.3 %output.3 = bf16[136,768]{1,0:T(8,128)(2,1)S(1)} custom-call(s32[3]{0:T(128)S(1)} %pad_add_fusion.ids, bf16[136,256]{1,0:T(8,128)(2,1)S(1)} %get-tuple-element.87.a0, bf16[136,256]{1,0:T(8,128)(2,1)S(1)} %collective-permute-done.19.a1, bf16[136,256]{1,0:T(8,128)(2,1)S(1)} %collective-permute-done.20.a2, bf16[136,256]{1,0:T(8,128)(2,1)S(1)} %collective-permute-done.21.a3, ...), custom_call_target="tpu_custom_call" | custom-call | flops 160432128 | bytes 1179648 | tf_op jit(solution)/shard_map/output/pallas_call | solution.py:404
  93.5 3.1 %collective-permute-start.22 = (bf16[136,768]{1,0:T(8,128)(2,1)S(1)}, bf16[136,768]{1,0:T(8,128)(2,1)S(1)}, u32[]{:S(2)}, u32[]{:S(2)}) collective-permute-start(bf16[136,768]{1,0:T(8,128)(2,1)S(1)} %output.3), channel_id=1, source_target_pairs={{0,1},{1,0},{2,3},{3,2},{4,5},{5,4},{6,7},{7,6},{8,9},{9,8},{10,11... | collective-permute-start | bytes 626696 | tf_op jit(solution)/shard_map/ppermute | solution.py:568
  96.6 1.3 output.2.own
  97.9 0.0 copy-start.1
  97.9 3.2 %collective-permute-done.22.other = bf16[136,768]{1,0:T(8,128)(2,1)S(1)} collective-permute-done((bf16[136,768]{1,0:T(8,128)(2,1)S(1)}, bf16[136,768]{1,0:T(8,128)(2,1)S(1)}, u32[]{:S(2)}, u32[]{:S(2)}) %collective-permute-start.22) | collective-permute-done | bytes 208928 | tf_op jit(solution)/shard_map/ppermute | solution.py:568
  101.1 2.3 %decode_send.1 = (bf16[272,768]{1,0:T(8,128)(2,1)S(1)}, bf16[272,768]{1,0:T(8,128)(2,1)S(1)}) custom-call(s32[3]{0:T(128)S(1)} %pad_add_fusion.ids, f32[136,768]{1,0:T(8,128)S(1)} %output.2.own, bf16[136,768]{1,0:T(8,128)(2,1)S(1)} %collective-permute-done.22.other, bf16[272,768]{1,0:T(8,128)(2,1)S(1)} %get-tuple-element.52.mine.encoded, ...), custom_call_target="tpu_custom_call" | custom-call | flops 962592768 | bytes 3538944 | tf_op jit(solution)/shard_map/decode_send/pallas_call | solution.py:441
  103.4 2.9 %collective-permute-start.23 = (bf16[272,768]{1,0:T(8,128)(2,1)S(1)}, bf16[272,768]{1,0:T(8,128)(2,1)S(1)}, u32[]{:S(2)}, u32[]{:S(2)}) collective-permute-start(bf16[272,768]{1,0:T(8,128)(2,1)S(1)} %get-tuple-element.92), channel_id=1, source_target_pairs={{0,1},{1,0},{2,3},{3,2},{4,5},{5,4},{6,7},{7,6},{8,9},{9,8},{10,11... | collective-permute-start | bytes 1253384 | tf_op jit(solution)/shard_map/ppermute | solution.py:568
  106.3 2.1 %decode_own.1.own = f32[272,768]{1,0:T(8,128)S(1)} custom-call(s32[3]{0:T(128)S(1)} %pad_add_fusion.ids, bf16[272,768]{1,0:T(8,128)(2,1)S(1)} %get-tuple-element.91.inputs, bf16[3,768,1536]{2,1,0:T(8,128)(2,1)S(1)} %bitcast.5), custom_call_target="tpu_custom_call" | custom-call | flops 962592768 | bytes 3538944 | tf_op jit(solution)/shard_map/decode_own/pallas_call | solution.py:464
  108.4 4.7 %collective-permute-done.23.other = bf16[272,768]{1,0:T(8,128)(2,1)S(1)} collective-permute-done((bf16[272,768]{1,0:T(8,128)(2,1)S(1)}, bf16[272,768]{1,0:T(8,128)(2,1)S(1)}, u32[]{:S(2)}, u32[]{:S(2)}) %collective-permute-start.23) | collective-permute-done | bytes 417824 | tf_op jit(solution)/shard_map/ppermute | solution.py:568
  113.0 2.2 %slopes.1 = (bf16[256,768]{1,0:T(8,128)(2,1)}, bf16[272,768]{1,0:T(8,128)(2,1)S(1)}, f32[128,768]{1,0:T(8,128)S(1)}) custom-call(s32[3]{0:T(128)S(1)} %pad_add_fusion.ids, f32[272,768]{1,0:T(8,128)S(1)} %decode_own.1.own, bf16[272,768]{1,0:T(8,128)(2,1)S(1)} %collective-permute-done.23.other, bf16[272,768]{1,0:T(8,128)(2,1)S(1)} %get-tuple-element.91.inputs, ...), custom_call_target="tpu_custom_call" | custom-call | flops 6266880 | bytes 2924544 | tf_op jit(solution)/shard_map/slopes/pallas_call | solution.py:505
  115.2 2.8 %collective-permute-start.24 = (bf16[272,768]{1,0:T(8,128)(2,1)S(1)}, bf16[272,768]{1,0:T(8,128)(2,1)S(1)}, u32[]{:S(2)}, u32[]{:S(2)}) collective-permute-start(bf16[272,768]{1,0:T(8,128)(2,1)S(1)} %get-tuple-element.94.slope), channel_id=1, source_target_pairs={{0,1},{1,0},{2,3},{3,2},{4,5},{5,4},{6,7},{7,6},{8,9},{9,8},{10,11... | collective-permute-start | bytes 1253384 | tf_op jit(solution)/shard_map/ppermute | solution.py:568
  118.0 2.3 %backward.2.start = f32[128,768]{1,0:T(8,128)S(1)} custom-call(s32[3]{0:T(128)S(1)} %pad_add_fusion.ids, bf16[272,768]{1,0:T(8,128)(2,1)S(1)} %get-tuple-element.94.slope, f32[128,768]{1,0:T(8,128)S(1)} %get-tuple-element.95.start, bf16[3,768,1536]{2,1,0:T(8,128)(2,1)S(1)} %bitcast.5), custom_call_target="tpu_custom_call" | custom-call | flops 962592768 | bytes 3538944 | tf_op jit(solution)/shard_map/backward/pallas_call | solution.py:543
  120.4 4.4 %collective-permute-done.24.slope = bf16[272,768]{1,0:T(8,128)(2,1)S(1)} collective-permute-done((bf16[272,768]{1,0:T(8,128)(2,1)S(1)}, bf16[272,768]{1,0:T(8,128)(2,1)S(1)}, u32[]{:S(2)}, u32[]{:S(2)}) %collective-permute-start.24) | collective-permute-done | bytes 417824 | tf_op jit(solution)/shard_map/ppermute | solution.py:568
  124.8 3.0 %backward.3 = bf16[128,768]{1,0:T(8,128)(2,1)} custom-call(s32[3]{0:T(128)S(1)} %pad_add_fusion.ids, bf16[272,768]{1,0:T(8,128)(2,1)S(1)} %collective-permute-done.24.slope, f32[128,768]{1,0:T(8,128)S(1)} %backward.2.start, bf16[3,768,1536]{2,1,0:T(8,128)(2,1)S(1)} %bitcast.5), custom_call_target="tpu_custom_call" | custom-call | flops 962592768 | bytes 3538944 | tf_op jit(solution)/shard_map/backward/pallas_call | solution.py:543
  (24 shorter events, 0.2 us)
Async XLA Ops:
  1.5 2.7 %collective-permute-start = (bf16[8,1664]{1,0:T(8,128)(2,1)S(1)}, bf16[8,1664]{1,0:T(8,128)(2,1)S(1)}, u32[]{:S(2)}, u32[]{:S(2)}) collective-permute-start(bf16[8,1664]{1,0:T(8,128)(2,1)S(1)} %get-tuple-element.50), channel_id=1, source_target_pairs={{0,2},{2,4},{4,6},{6,8},{8,10},{10,12},{12,14},{14,16},{16,18},{18... | collective-permute-start | bytes 79880 | tf_op jit(solution)/shard_map/ppermute | solution.py:592
  2.8 5.0 %collective-permute-start.1 = (bf16[8,1664]{1,0:T(8,128)(2,1)S(1)}, bf16[8,1664]{1,0:T(8,128)(2,1)S(1)}, u32[]{:S(2)}, u32[]{:S(2)}) collective-permute-start(bf16[8,1664]{1,0:T(8,128)(2,1)S(1)} %get-tuple-element.51), channel_id=1, source_target_pairs={{2,0},{4,2},{6,4},{8,6},{10,8},{12,10},{14,12},{16,14},{18,16},{20... | collective-permute-start | bytes 79880 | tf_op jit(solution)/shard_map/ppermute | solution.py:593
  7.8 9.0 %copy-start.3 = (f32[1536]{0:T(1024)S(1)}, f32[1536]{0:T(1024)}, u32[]{:S(2)}) copy-start(f32[1536]{0:T(1024)} %param.12) | copy-start | bytes 18436
  13.8 48.3 %copy-start.2 = (f32[4]{0:T(128)S(1)}, f32[4]{0:T(128)}, u32[]{:S(2)}) copy-start(f32[4]{0:T(128)} %scale.5) | copy-start | bytes 52
  13.8 12.4 %collective-permute-start.2 = (bf16[272,768]{1,0:T(8,128)(2,1)S(1)}, bf16[272,768]{1,0:T(8,128)(2,1)S(1)}, u32[]{:S(2)}, u32[]{:S(2)}) collective-permute-start(bf16[272,768]{1,0:T(8,128)(2,1)S(1)} %get-tuple-element.52.mine.encoded), channel_id=1, source_target_pairs={{0,1},{1,0},{2,3},{3,2},{4,5},{5,4},{6,7},{7,6},{8,9},{9,8},{10,11... | collective-permute-start | bytes 1253384 | tf_op jit(solution)/shard_map/ppermute | solution.py:568
  28.9 9.8 %collective-permute-start.3 = (bf16[128,384]{1,0:T(8,128)(2,1)S(1)}, bf16[128,384]{1,0:T(8,128)(2,1)S(1)}, u32[]{:S(2)}, u32[]{:S(2)}) collective-permute-start(bf16[128,384]{1,0:T(8,128)(2,1)S(1)} %get-tuple-element.55), channel_id=1, source_target_pairs={{0,32},{2,34},{4,36},{6,38},{8,40},{10,42},{12,44},{14,46},{16,48}... | collective-permute-start | bytes 294920 | tf_op jit(solution)/shard_map/ppermute | solution.py:572
  33.7 4.9 %collective-permute-start.4 = (bf16[128,384]{1,0:T(8,128)(2,1)S(1)}, bf16[128,384]{1,0:T(8,128)(2,1)S(1)}, u32[]{:S(2)}, u32[]{:S(2)}) collective-permute-start(bf16[128,384]{1,0:T(8,128)(2,1)S(1)} %get-tuple-element.56), channel_id=1, source_target_pairs={{0,96},{2,98},{4,100},{6,102},{8,104},{10,106},{12,108},{14,110},{... | collective-permute-start | bytes 294920 | tf_op jit(solution)/shard_map/ppermute | solution.py:572
  35.1 6.1 %collective-permute-start.5 = (bf16[128,384]{1,0:T(8,128)(2,1)S(1)}, bf16[128,384]{1,0:T(8,128)(2,1)S(1)}, u32[]{:S(2)}, u32[]{:S(2)}) collective-permute-start(bf16[128,384]{1,0:T(8,128)(2,1)S(1)} %get-tuple-element.57), channel_id=1, source_target_pairs={{0,64},{2,66},{4,68},{6,70},{8,72},{10,74},{12,76},{14,78},{16,80}... | collective-permute-start | bytes 294920 | tf_op jit(solution)/shard_map/ppermute | solution.py:572
  41.2 8.3 %collective-permute-start.6 = (bf16[136,256]{1,0:T(8,128)(2,1)S(1)}, bf16[136,256]{1,0:T(8,128)(2,1)S(1)}, u32[]{:S(2)}, u32[]{:S(2)}) collective-permute-start(bf16[136,256]{1,0:T(8,128)(2,1)S(1)} %get-tuple-element.67), channel_id=1, source_target_pairs={{0,32},{2,34},{4,36},{6,38},{8,40},{10,42},{12,44},{14,46},{16,48}... | collective-permute-start | bytes 208904 | tf_op jit(solution)/shard_map/ppermute | solution.py:572
  41.9 7.6 %collective-permute-start.7 = (bf16[136,256]{1,0:T(8,128)(2,1)S(1)}, bf16[136,256]{1,0:T(8,128)(2,1)S(1)}, u32[]{:S(2)}, u32[]{:S(2)}) collective-permute-start(bf16[136,256]{1,0:T(8,128)(2,1)S(1)} %get-tuple-element.68), channel_id=1, source_target_pairs={{0,96},{2,98},{4,100},{6,102},{8,104},{10,106},{12,108},{14,110},{... | collective-permute-start | bytes 208904 | tf_op jit(solution)/shard_map/ppermute | solution.py:572
  44.5 5.8 %collective-permute-start.8 = (bf16[136,256]{1,0:T(8,128)(2,1)S(1)}, bf16[136,256]{1,0:T(8,128)(2,1)S(1)}, u32[]{:S(2)}, u32[]{:S(2)}) collective-permute-start(bf16[136,256]{1,0:T(8,128)(2,1)S(1)} %get-tuple-element.69), channel_id=1, source_target_pairs={{0,64},{2,66},{4,68},{6,70},{8,72},{10,74},{12,76},{14,78},{16,80}... | collective-permute-start | bytes 208904 | tf_op jit(solution)/shard_map/ppermute | solution.py:572
  46.1 10.9 %collective-permute-start.10 = (bf16[512,384]{1,0:T(8,128)(2,1)S(1)}, bf16[512,384]{1,0:T(8,128)(2,1)S(1)}, u32[]{:S(2)}, u32[]{:S(2)}) collective-permute-start(bf16[512,384]{1,0:T(8,128)(2,1)S(1)} %pad_maximum_fusion.refs_0_), channel_id=1, source_target_pairs={{0,24},{2,26},{4,28},{6,30},{8,0},{10,2},{12,4},{14,6},{16,8},{18,... | collective-permute-start | bytes 1179656 | tf_op jit(solution)/shard_map/ppermute | solution.py:572
  49.6 9.4 %collective-permute-start.9 = (bf16[512,384]{1,0:T(8,128)(2,1)S(1)}, bf16[512,384]{1,0:T(8,128)(2,1)S(1)}, u32[]{:S(2)}, u32[]{:S(2)}) collective-permute-start(bf16[512,384]{1,0:T(8,128)(2,1)S(1)} %pad_maximum_fusion.refs_0_), channel_id=1, source_target_pairs={{0,8},{2,10},{4,12},{6,14},{8,16},{10,18},{12,20},{14,22},{16,24},... | collective-permute-start | bytes 1179656 | tf_op jit(solution)/shard_map/ppermute | solution.py:572
  50.4 6.6 %collective-permute-start.11 = (bf16[544,256]{1,0:T(8,128)(2,1)S(1)}, bf16[544,256]{1,0:T(8,128)(2,1)S(1)}, u32[]{:S(2)}, u32[]{:S(2)}) collective-permute-start(bf16[544,256]{1,0:T(8,128)(2,1)S(1)} %constant_dynamic-update-slice_fusion.queries), channel_id=1, source_target_pairs={{0,4},{2,6},{4,0},{6,2},{8,12},{10,14},{12,8},{14,10},{16,20},{18,... | collective-permute-start | bytes 835592 | tf_op jit(solution)/shard_map/ppermute | solution.py:572
  50.7 11.4 %collective-permute-start.12 = (bf16[512,384]{1,0:T(8,128)(2,1)S(1)}, bf16[512,384]{1,0:T(8,128)(2,1)S(1)}, u32[]{:S(2)}, u32[]{:S(2)}) collective-permute-start(bf16[512,384]{1,0:T(8,128)(2,1)S(1)} %pad_maximum_fusion.refs_0_), channel_id=1, source_target_pairs={{0,2},{2,0},{4,6},{6,4},{8,10},{10,8},{12,14},{14,12},{16,18},{18,... | collective-permute-start | bytes 1179656 | tf_op jit(solution)/shard_map/ppermute | solution.py:572
  58.9 3.2 %collective-permute-start.13 = (bf16[512,384]{1,0:T(8,128)(2,1)S(1)}, bf16[512,384]{1,0:T(8,128)(2,1)S(1)}, u32[]{:S(2)}, u32[]{:S(2)}) collective-permute-start(bf16[512,384]{1,0:T(8,128)(2,1)S(1)} %collective-permute-done.9.refs_1_), channel_id=1, source_target_pairs={{0,2},{2,0},{4,6},{6,4},{8,10},{10,8},{12,14},{14,12},{16,18},{18,... | collective-permute-start | bytes 1179656 | tf_op jit(solution)/shard_map/ppermute | solution.py:572
  58.9 3.2 %collective-permute-start.14 = (bf16[512,384]{1,0:T(8,128)(2,1)S(1)}, bf16[512,384]{1,0:T(8,128)(2,1)S(1)}, u32[]{:S(2)}, u32[]{:S(2)}) collective-permute-start(bf16[512,384]{1,0:T(8,128)(2,1)S(1)} %collective-permute-done.10.refs_2_), channel_id=1, source_target_pairs={{0,2},{2,0},{4,6},{6,4},{8,10},{10,8},{12,14},{14,12},{16,18},{18,... | collective-permute-start | bytes 1179656 | tf_op jit(solution)/shard_map/ppermute | solution.py:572
  59.5 7.0 %collective-permute-start.16 = (bf16[256,384]{1,0:T(8,128)(2,1)S(1)}, bf16[256,384]{1,0:T(8,128)(2,1)S(1)}, u32[]{:S(2)}, u32[]{:S(2)}) collective-permute-start(bf16[256,384]{1,0:T(8,128)(2,1)S(1)} %slice.7), channel_id=1, source_target_pairs={{0,24},{2,26},{4,28},{6,30},{8,0},{10,2},{12,4},{14,6},{16,8},{18,... | collective-permute-start | bytes 589832 | tf_op jit(solution)/shard_map/ppermute | solution.py:572
  62.1 7.8 %collective-permute-start.15 = (bf16[256,384]{1,0:T(8,128)(2,1)S(1)}, bf16[256,384]{1,0:T(8,128)(2,1)S(1)}, u32[]{:S(2)}, u32[]{:S(2)}) collective-permute-start(bf16[256,384]{1,0:T(8,128)(2,1)S(1)} %slice.6), channel_id=1, source_target_pairs={{0,8},{2,10},{4,12},{6,14},{8,16},{10,18},{12,20},{14,22},{16,24},... | collective-permute-start | bytes 589832 | tf_op jit(solution)/shard_map/ppermute | solution.py:572
  66.1 26.2 %copy-start = (bf16[768,1536]{1,0:T(8,128)(2,1)S(1)}, bf16[768,1536]{1,0:T(8,128)(2,1)}, u32[]{:S(2)}) copy-start(bf16[768,1536]{1,0:T(8,128)(2,1)} %weight.7) | copy-start | bytes 7077892
  70.0 1.8 %collective-permute-start.17 = (bf16[512,384]{1,0:T(8,128)(2,1)S(1)}, bf16[512,384]{1,0:T(8,128)(2,1)S(1)}, u32[]{:S(2)}, u32[]{:S(2)}) collective-permute-start(bf16[512,384]{1,0:T(8,128)(2,1)S(1)} %constant_dynamic-update-slice_fusion.4.refs_0_.refs_6_), channel_id=1, source_target_pairs={{0,2},{2,0},{4,6},{6,4},{8,10},{10,8},{12,14},{14,12},{16,18},{18,... | collective-permute-start | bytes 1179656 | tf_op jit(solution)/shard_map/ppermute | solution.py:572
  75.3 8.8 %collective-permute-start.18 = (bf16[544,256]{1,0:T(8,128)(2,1)S(1)}, bf16[544,256]{1,0:T(8,128)(2,1)S(1)}, u32[]{:S(2)}, u32[]{:S(2)}) collective-permute-start(bf16[544,256]{1,0:T(8,128)(2,1)S(1)} %get-tuple-element.86), channel_id=1, source_target_pairs={{0,4},{2,6},{4,0},{6,2},{8,12},{10,14},{12,8},{14,10},{16,20},{18,... | collective-permute-start | bytes 835592 | tf_op jit(solution)/shard_map/ppermute | solution.py:572
  75.4 25.7 %slice-start = ((s8[7077888]{0:T(1024)(128)(4,1)}), s8[4194304]{0:T(1024)(128)(4,1)S(1)}, s32[]{:S(2)}) async-start(s8[7077888]{0:T(1024)(128)(4,1)} %bitcast.4), calls=%async_computation | async-start | bytes 8388608
  75.4 25.7 %slice-start.1 = ((s8[7077888]{0:T(1024)(128)(4,1)}), s8[2883584]{0:T(1024)(128)(4,1)S(1)}, s32[]{:S(2)}) async-start(s8[7077888]{0:T(1024)(128)(4,1)} %bitcast.4), calls=%async_computation.1 | async-start | bytes 5767168
  84.6 4.4 %collective-permute-start.19 = (bf16[136,256]{1,0:T(8,128)(2,1)S(1)}, bf16[136,256]{1,0:T(8,128)(2,1)S(1)}, u32[]{:S(2)}, u32[]{:S(2)}) collective-permute-start(bf16[136,256]{1,0:T(8,128)(2,1)S(1)} %get-tuple-element.88), channel_id=1, source_target_pairs={{0,96},{2,98},{4,100},{6,102},{8,104},{10,106},{12,108},{14,110},{... | collective-permute-start | bytes 208904 | tf_op jit(solution)/shard_map/ppermute | solution.py:572
  85.3 6.5 %collective-permute-start.20 = (bf16[136,256]{1,0:T(8,128)(2,1)S(1)}, bf16[136,256]{1,0:T(8,128)(2,1)S(1)}, u32[]{:S(2)}, u32[]{:S(2)}) collective-permute-start(bf16[136,256]{1,0:T(8,128)(2,1)S(1)} %get-tuple-element.89), channel_id=1, source_target_pairs={{0,64},{2,66},{4,68},{6,70},{8,72},{10,74},{12,76},{14,78},{16,80}... | collective-permute-start | bytes 208904 | tf_op jit(solution)/shard_map/ppermute | solution.py:572
  86.3 5.9 %collective-permute-start.21 = (bf16[136,256]{1,0:T(8,128)(2,1)S(1)}, bf16[136,256]{1,0:T(8,128)(2,1)S(1)}, u32[]{:S(2)}, u32[]{:S(2)}) collective-permute-start(bf16[136,256]{1,0:T(8,128)(2,1)S(1)} %get-tuple-element.90), channel_id=1, source_target_pairs={{0,32},{2,34},{4,36},{6,38},{8,40},{10,42},{12,44},{14,46},{16,48}... | collective-permute-start | bytes 208904 | tf_op jit(solution)/shard_map/ppermute | solution.py:572
  93.5 7.6 %collective-permute-start.22 = (bf16[136,768]{1,0:T(8,128)(2,1)S(1)}, bf16[136,768]{1,0:T(8,128)(2,1)S(1)}, u32[]{:S(2)}, u32[]{:S(2)}) collective-permute-start(bf16[136,768]{1,0:T(8,128)(2,1)S(1)} %output.3), channel_id=1, source_target_pairs={{0,1},{1,0},{2,3},{3,2},{4,5},{5,4},{6,7},{7,6},{8,9},{9,8},{10,11... | collective-permute-start | bytes 626696 | tf_op jit(solution)/shard_map/ppermute | solution.py:568
  97.9 15.1 %copy-start.1 = (bf16[256,1536]{1,0:T(8,128)(2,1)S(1)}, bf16[256,1536]{1,0:T(8,128)(2,1)}, u32[]{:S(2)}) copy-start(bf16[256,1536]{1,0:T(8,128)(2,1)} %grad.3) | copy-start | bytes 2359300
  103.4 9.6 %collective-permute-start.23 = (bf16[272,768]{1,0:T(8,128)(2,1)S(1)}, bf16[272,768]{1,0:T(8,128)(2,1)S(1)}, u32[]{:S(2)}, u32[]{:S(2)}) collective-permute-start(bf16[272,768]{1,0:T(8,128)(2,1)S(1)} %get-tuple-element.92), channel_id=1, source_target_pairs={{0,1},{1,0},{2,3},{3,2},{4,5},{5,4},{6,7},{7,6},{8,9},{9,8},{10,11... | collective-permute-start | bytes 1253384 | tf_op jit(solution)/shard_map/ppermute | solution.py:568
  115.2 9.5 %collective-permute-start.24 = (bf16[272,768]{1,0:T(8,128)(2,1)S(1)}, bf16[272,768]{1,0:T(8,128)(2,1)S(1)}, u32[]{:S(2)}, u32[]{:S(2)}) collective-permute-start(bf16[272,768]{1,0:T(8,128)(2,1)S(1)} %get-tuple-element.94.slope), channel_id=1, source_target_pairs={{0,1},{1,0},{2,3},{3,2},{4,5},{5,4},{6,7},{7,6},{8,9},{9,8},{10,11... | collective-permute-start | bytes 1253384 | tf_op jit(solution)/shard_map/ppermute | solution.py:568

commit v6 on v5

--- a/solution.py
+++ b/solution.py
@@ -42,12 +42,14 @@
 HBM = pl.BlockSpec(memory_space=pltpu.HBM)
 
 
-def above(rows):
-    return pltpu.roll(rows, 1, 0)
-
-
-def below(rows):
-    return pltpu.roll(rows, ROWS - 1, 0)
+def above(rows, span):
+    parts = [pltpu.roll(rows[i : i + span], 1, 0) for i in range(0, rows.shape[0], span)]
+    return jnp.concatenate(parts, axis=0)
+
+
+def below(rows, span):
+    parts = [pltpu.roll(rows[i : i + span], span - 1, 0) for i in range(0, rows.shape[0], span)]
+    return jnp.concatenate(parts, axis=0)
 
 
 def lanes(at, size):
@@ -62,10 +64,11 @@
     return jnp.tanh(0.7978845608028654 * (x + 0.044715 * (x * x * x)))
 
 
-def conv_taps(rows, weight):
+def conv_taps(rows, weight, span):
+    half = rows.shape[0] // 2
     first, mid, last = (dot(rows, weight(t)) for t in range(3))
-    even = above(first[ROWS:]) + mid[:ROWS] + last[ROWS:]
-    odd = first[:ROWS] + mid[ROWS:] + below(last[:ROWS])
+    even = above(first[half:], span) + mid[:half] + last[half:]
+    odd = first[:half] + mid[half:] + below(last[:half], span)
     return jnp.concatenate([even, odd], axis=0)
 
 
@@ -120,9 +123,7 @@
     )(far_memory(bases), far_memory(grad))
 
 
-def encode_kernel(
-    ids, codes, before, after, stems, weights, ahead, encoded, loaded, stem, weight, embedded, sems
-):
+def encode_body(side, code, stems, weights, encoded, stem, weight, embedded, sems, span):
     patch = stem.shape[0] // 4
     feats = stem.shape[1]
     half = weight.shape[2]
@@ -136,22 +137,16 @@
         )
         for i in range(count)
     ]
-    later = pltpu.make_async_copy(ahead, loaded, sems.at[count + 1])
-    for copy in [first] + copies + [later]:
+    for copy in [first] + copies:
         copy.start()
     row = lax.broadcasted_iota(jnp.int32, (2 * patch, 4 * patch), 0)
     col = lax.broadcasted_iota(jnp.int32, (2 * patch, 4 * patch), 1)
-    place = lax.broadcasted_iota(jnp.int32, (ROWS - OWN, 128), 0)
-    halo = jnp.where(place >= 6, before[:, feats:].astype(F32), 0.0)
-    halo = jnp.where(place < 2, after[:, feats:].astype(F32), halo)
-    code = jnp.concatenate([codes[...].astype(F32), halo], axis=0).astype(BF16)
     spread = [
         dot(code, (row == col // 4 + offset).astype(F32).astype(BF16)) for offset in (0, patch)
     ]
     spread = jnp.concatenate(spread, axis=0)
     base = lax.broadcasted_iota(jnp.int32, spread.shape, 1) % 4 + 1
     onehot = (spread == base.astype(F32)).astype(F32).astype(BF16)
-
     first.wait()
 
     def embed(i):
@@ -159,89 +154,171 @@
         embedded[:, at] = dot(onehot, stem[:, at]).astype(BF16)
 
     tiles(feats // TILE, embed)
-
     for i in range(count):
         copies[i].wait()
         at = slice(i * TILE, (i + 1) * TILE)
-        pre = conv_taps(embedded[...], lambda t: weight[t, :, at])
-        mine = embedded[:, lanes(ids[0] * half + i * TILE, TILE)].astype(F32)
+        pre = conv_taps(embedded[...], lambda t: weight[t, :, at], span)
+        mine = embedded[:, lanes(side * half + i * TILE, TILE)].astype(F32)
         encoded[:, at] = (mine + 0.5 * pre * (1.0 + gelu_tanh(pre))).astype(BF16)
 
+
+def encode_kernel(ids, codes, stems, weights, encoded, *scratch):
+    encode_body(ids[0], codes[...], stems, weights, encoded, *scratch, OWN)
+
+
+def encode_edges_kernel(
+    ids, codes, before, after, stems, weights, ahead, encoded, loaded, stem, weight, embedded, sems
+):
+    later = pltpu.make_async_copy(ahead, loaded, sems.at[sems.shape[0] - 1])
+    later.start()
+    feats = stem.shape[1]
+    place = lax.broadcasted_iota(jnp.int32, (8, 128), 0)
+    code = codes[...].astype(F32)
+    low = jnp.where(place >= 6, before[:, feats:].astype(F32), 0.0)
+    low = jnp.where(place == 0, code[:8], low)
+    high = jnp.where(place < 2, after[:, feats:].astype(F32), 0.0)
+    high = jnp.where(place == 7, code[OWN - 8 :], high)
+    code = jnp.concatenate([low, high], axis=0).astype(BF16)
+    encode_body(ids[0], code, stems, weights, encoded, stem, weight, embedded, sems, 8)
     later.wait()
 
 
-def encode(ids, codes, before, after, stem, weight, ahead):
+def encode_scratch(rows, stem, weight):
+    return [
+        pltpu.VMEM(stem.shape, BF16),
+        pltpu.VMEM(weight.shape, BF16),
+        pltpu.VMEM((rows, stem.shape[1]), BF16),
+        pltpu.SemaphoreType.DMA((weight.shape[2] // TILE + 2,)),
+    ]
+
+
+def encode(ids, codes, stem, weight):
     half = weight.shape[2]
-    feats = stem.shape[1]
     return pl.pallas_call(
         encode_kernel,
+        in_specs=[SM, VM, HBM, HBM],
+        out_specs=VM,
+        out_shape=shape((2 * OWN, half), BF16),
+        scratch_shapes=encode_scratch(2 * OWN, stem, weight),
+        compiler_params=params(20),
+        cost_estimate=cost(4 * OWN * weight.size, weight.size * 4),
+        name="encode",
+    )(ids, codes, far_memory(stem), far_memory(weight))
+
+
+def encode_edges(ids, codes, before, after, stem, weight, ahead):
+    half = weight.shape[2]
+    return pl.pallas_call(
+        encode_edges_kernel,
         in_specs=[SM, VM, VM, VM, HBM, HBM, HBM],
         out_specs=[VM, VM],
-        out_shape=[shape((2 * ROWS, half), BF16), pltpu.VMEM(ahead.shape, BF16)],
-        scratch_shapes=[
-            pltpu.VMEM(stem.shape, BF16),
-            pltpu.VMEM(weight.shape, BF16),
-            pltpu.VMEM((2 * ROWS, feats), BF16),
-            pltpu.SemaphoreType.DMA((half // TILE + 2,)),
+        out_shape=[shape((32, half), BF16), pltpu.VMEM(ahead.shape, BF16)],
+        scratch_shapes=encode_scratch(32, stem, weight),
+        compiler_params=params(14),
+        cost_estimate=cost(4 * OWN * weight.size, weight.size * 4),
+        name="encode_edges",
+    )(ids, codes, before, after, far_memory(stem), far_memory(weight), far_memory(ahead))
+
+
+def joined(main, edges):
+    main, edges = main[...].astype(F32), edges[...].astype(F32)
+    even, odd = main[:OWN], main[OWN:]
+    even_low, even_high, odd_low, odd_high = (edges[i : i + 8] for i in range(0, 32, 8))
+    place = lax.broadcasted_iota(jnp.int32, even_low.shape, 0)
+    return jnp.concatenate(
+        [
+            jnp.where(place == 0, even_low, even[:8]),
+            even[8:],
+            jnp.where(place < 4, even_high, even_low),
+            odd[: OWN - 8],
+            jnp.where(place == 7, odd_high, odd[OWN - 8 :]),
+            jnp.where(place < 4, odd_high, odd_low),
         ],
-        compiler_params=params(20),
-        cost_estimate=cost(2 * 2 * ROWS * 3 * feats * half, weight.size * 4),
-        name="encode",
-    )(ids, codes, before, after, far_memory(stem), far_memory(weight), far_memory(ahead))
-
-
-def project_kernel(ids, mine, theirs, gain, weight, *refs):
-    queries, keyvals, packed = refs[:4], refs[4:8], refs[8]
+        axis=0,
+    )
+
+
+def unpacked(both):
+    both = both.astype(BF16).astype(F32)
+    turned = pltpu.roll(both, 2 * HEAD - 64, 1)
+    return (both[:, :128], both[:, 128:256]), (turned[:, 128:256], turned[:, 256:384])
+
+
+def project_keys_kernel(
+    ids, mine, mine_edges, theirs, their_edges, gain, weight, encoded, normed, k0, k1, k2, k3, packed
+):
     half = mine.shape[1]
     near = lanes(ids[0] * half, half)
     far = lanes((1 - ids[0]) * half, half)
-
-    def pairs(ref):
-        enc = ref[...].astype(F32)
-        return (enc[:ROWS] + enc[ROWS:]) * 0.5
-
-    binned = pairs(mine), pairs(theirs)
+    ring = joined(mine, mine_edges)
+    encoded[...] = ring.astype(BF16)
+    other = joined(theirs, their_edges)
+    binned = [(part[:ROWS] + part[ROWS:]) * 0.5 for part in (ring, other)]
     total = sum(jnp.sum(part * part, axis=1, keepdims=True) for part in binned)
     inverse = lax.rsqrt(total * (1.0 / (2 * half)) + EPS)
     here = (binned[0] * inverse * gain[:, near]).astype(BF16)
     there = (binned[1] * inverse * gain[:, far]).astype(BF16)
+    normed[0] = here
+    normed[1] = there
     low = lax.broadcasted_iota(jnp.int32, (ROWS, 128), 1) < 64
     for pair in range(2):
         at = slice(pair * 2 * HEAD, (pair + 1) * 2 * HEAD)
-        rows = []
-        for kind in range(3):
-            both = dot(here, weight[kind, near, at]) + dot(there, weight[kind, far, at])
-            both = both.astype(BF16).astype(F32)
-            rows.append((both, pltpu.roll(both, 2 * HEAD - 64, 1)))
+        keys, values = (
+            unpacked(dot(here, weight[kind, near, at]) + dot(there, weight[kind, far, at]))
+            for kind in (1, 2)
+        )
         for side in range(2):
             head = 2 * pair + side
-            query, key, value = (
-                (r[0][:, :128], r[0][:, 128:256]) if side == 0 else (r[1][:, 128:256], r[1][:, 256:384])
-                for r in rows
-            )
+            key, value = keys[side], values[side]
             packed[head, :, :128] = key[0].astype(BF16)
             packed[head, :, 128:256] = value[0].astype(BF16)
             tail = jnp.where(low, key[1], pltpu.roll(value[1], 64, 1))
-            packed[head, :, 256:384] = tail.astype(BF16)
-            packed[head, :, 384:512] = query[0].astype(BF16)
-            packed[head, :, 512:] = jnp.where(low, query[1], 0.0).astype(BF16)
-    for distance in range(4):
-        head = lax.rem(ids[1] + distance, 4)
-        keyvals[distance][...] = packed[head, :OWN, :384]
-        queries[distance][...] = packed[head, :, 384:]
-
-
-def project(ids, mine, theirs, gain, weight):
-    return pl.pallas_call(
-        project_kernel,
-        in_specs=[SM, VM, VM, VM, VM],
-        out_specs=[VM] * 8,
-        out_shape=[shape((ROWS, 256), BF16)] * 4 + [shape((OWN, 384), BF16)] * 4,
-        scratch_shapes=[pltpu.VMEM((4, ROWS, 640), BF16)],
+            packed[head, :, 256:] = tail.astype(BF16)
+    for distance, out in enumerate((k0, k1, k2, k3)):
+        out[...] = packed[lax.rem(ids[1] + distance, 4), :OWN, :]
+
+
+def project_keys(ids, mine, mine_edges, theirs, their_edges, gain, weight):
+    half = mine.shape[1]
+    return pl.pallas_call(
+        project_keys_kernel,
+        in_specs=[SM] + [VM] * 6,
+        out_specs=[VM] * 6,
+        out_shape=[shape((2 * ROWS, half), BF16), shape((2, ROWS, half), BF16)]
+        + [shape((OWN, 384), BF16)] * 4,
+        scratch_shapes=[pltpu.VMEM((4, ROWS, 384), BF16)],
         compiler_params=params(12),
-        cost_estimate=cost(2 * ROWS * weight.size, weight.size * 2),
-        name="project",
-    )(ids, mine, theirs, gain, weight)
+        cost_estimate=cost(2 * ROWS * weight.size * 2 // 3, weight.size * 2),
+        name="project_keys",
+    )(ids, mine, mine_edges, theirs, their_edges, gain, weight)
+
+
+def project_queries_kernel(ids, normed, weight, q0, q1, q2, q3, packed):
+    half = normed.shape[2]
+    near = lanes(ids[0] * half, half)
+    far = lanes((1 - ids[0]) * half, half)
+    low = lax.broadcasted_iota(jnp.int32, (ROWS, 128), 1) < 64
+    for pair in range(2):
+        at = slice(pair * 2 * HEAD, (pair + 1) * 2 * HEAD)
+        both = dot(normed[0], weight[0, near, at]) + dot(normed[1], weight[0, far, at])
+        for side, query in enumerate(unpacked(both)):
+            packed[2 * pair + side, :, :128] = query[0].astype(BF16)
+            packed[2 * pair + side, :, 128:] = jnp.where(low, query[1], 0.0).astype(BF16)
+    for distance, out in enumerate((q0, q1, q2, q3)):
+        out[...] = packed[lax.rem(ids[1] + distance, 4)]
+
+
+def project_queries(ids, normed, weight):
+    return pl.pallas_call(
+        project_queries_kernel,
+        in_specs=[SM, VM, VM],
+        out_specs=[VM] * 4,
+        out_shape=[shape((ROWS, 256), BF16)] * 4,
+        scratch_shapes=[pltpu.VMEM((4, ROWS, 256), BF16)],
+        compiler_params=params(10),
+        cost_estimate=cost(2 * ROWS * weight.size // 3, weight.size),
+        name="project_queries",
+    )(ids, normed, near_memory(weight))
 
 
 BLOCK = 2 * ROWS
@@ -412,8 +489,8 @@
     )(ids, *heads, weight)
 
 
-def decode_send_kernel(ids, own, other, encoded, weight, inputs, out):
-    half = out.shape[1]
+def decode_first_kernel(ids, own, other, encoded, weight, inputs, out):
+    half = weight.shape[1]
 
     def mix(i):
         at = lanes(i * TILE, TILE)
@@ -428,62 +505,68 @@
         inputs[:, at] = jnp.concatenate([even, odd], axis=0).astype(BF16)
 
     tiles(half // TILE, mix)
-
+    decode_tiles(inputs, weight, out, (1 - ids[0]) * half)
+
+
+def decode_tiles(inputs, weight, out, begin):
     def tile(i):
-        at = lanes((1 - ids[0]) * half + i * TILE, TILE)
-        out[:, lanes(i * TILE, TILE)] = conv_taps(inputs[...], lambda t: weight[t, :, at]).astype(BF16)
-
-    tiles(half // TILE, tile)
-
-
-def decode_send(ids, own, other, encoded, weight):
+        at = lanes(begin + i * TILE, TILE)
+        result = conv_taps(inputs[...], lambda t: weight[t, :, at], ROWS)
+        out[:, lanes(i * TILE, TILE)] = result.astype(out.dtype)
+
+    tiles(out.shape[1] // TILE, tile)
+
+
+def decode_first(ids, own, other, encoded, weight, width):
     half = weight.shape[1]
     return pl.pallas_call(
-        decode_send_kernel,
+        decode_first_kernel,
         in_specs=[SM] + [VM] * 4,
         out_specs=[VM] * 2,
-        out_shape=[shape((2 * ROWS, half), BF16)] * 2,
+        out_shape=[shape((2 * ROWS, half), BF16), shape((2 * ROWS, width), BF16)],
         compiler_params=params(8),
-        cost_estimate=cost(2 * 2 * ROWS * weight.size // 2, weight.size),
-        name="decode_send",
+        cost_estimate=cost(2 * 2 * ROWS * 3 * half * width, weight.size),
+        name="decode_first",
     )(ids, own, other, encoded, weight)
 
 
-def decode_own_kernel(ids, inputs, weight, out):
-    half = out.shape[1]
-
-    def tile(i):
-        at = lanes(ids[0] * half + i * TILE, TILE)
-        out[:, lanes(i * TILE, TILE)] = conv_taps(inputs[...], lambda t: weight[t, :, at])
-
-    tiles(half // TILE, tile)
-
-
-def decode_own(ids, inputs, weight):
+def decode_kernel(mine, first, ids, inputs, weight, out):
+    side = ids[0] if mine else 1 - ids[0]
+    decode_tiles(inputs, weight, out, side * weight.shape[1] + first)
+
+
+def decode(ids, inputs, weight, mine, first, width, dtype):
     half = weight.shape[1]
     return pl.pallas_call(
-        decode_own_kernel,
+        functools.partial(decode_kernel, mine, first),
         in_specs=[SM, VM, VM],
         out_specs=VM,
-        out_shape=shape((2 * ROWS, half), F32),
+        out_shape=shape((2 * ROWS, width), dtype),
         compiler_params=params(8),
-        cost_estimate=cost(2 * 2 * ROWS * weight.size // 2, weight.size),
-        name="decode_own",
+        cost_estimate=cost(2 * 2 * ROWS * 3 * half * width, weight.size),
+        name="decode",
     )(ids, inputs, weight)
 
 
-def slope_kernel(ids, own, other, inputs, grad, before, after, decoded, slope, paired, wide):
+def slope_kernel(first, ids, own, other, inputs, grad, before, after, *refs):
+    done, (decoded, slope, paired, wide) = refs[:-4], refs[-4:]
     half = own.shape[1]
+    begin = 0
+    if done:
+        begin = first
+        decoded[:, :first] = done[0][...]
 
     def tile(i):
         at = lanes(i * 128, 128)
-        column = lanes(ids[0] * half + i * 128, 128)
-        pre = own[:, at] + other[:, at].astype(F32)
+        target = lanes(begin + i * 128, 128)
+        source = lanes(first + i * 128, 128)
+        column = lanes(ids[0] * half + first + i * 128, 128)
+        pre = own[:, source] + other[:, at].astype(F32)
         tanh = gelu_tanh(pre)
-        result = inputs[:, at].astype(F32) + 0.5 * pre * (1.0 + tanh)
+        result = inputs[:, source].astype(F32) + 0.5 * pre * (1.0 + tanh)
         wide[0, pl.ds(0, OWN, 2), :] = result[:OWN]
         wide[0, pl.ds(1, OWN, 2), :] = result[ROWS : ROWS + OWN]
-        decoded[:, at] = wide[0].astype(BF16)
+        decoded[:, target] = wide[0].astype(BF16)
         slant = 0.5 * (1.0 + tanh) + (0.5 * 0.7978845608028654) * pre * (1.0 - tanh * tanh) * (
             1.0 + (3 * 0.044715) * (pre * pre)
         )
@@ -497,59 +580,68 @@
         cotangent = jnp.concatenate([even, even_edge, odd, odd_edge], axis=0)
         slope[:, at] = (cotangent * slant).astype(BF16)
 
-    tiles(half // 128, tile)
-
-
-def slopes(ids, own, other, inputs, grad, before, after):
-    half = own.shape[1]
-    return pl.pallas_call(
-        slope_kernel,
-        in_specs=[SM] + [VM] * 6,
+    tiles(other.shape[1] // 128, tile)
+
+
+def slopes(ids, own, other, inputs, grad, before, after, first, done=()):
+    width = other.shape[1]
+    return pl.pallas_call(
+        functools.partial(slope_kernel, first),
+        in_specs=[SM] + [VM] * (6 + len(done)),
         out_specs=[VM] * 3,
         out_shape=[
-            shape((2 * OWN, half), BF16),
-            shape((2 * ROWS, half), BF16),
-            shape((OWN, half), F32),
+            shape((2 * OWN, width + (first if done else 0)), BF16),
+            shape((2 * ROWS, width), BF16),
+            shape((OWN, width), F32),
         ],
         scratch_shapes=[pltpu.VMEM((2, 2 * OWN, 128), F32)],
         compiler_params=params(6),
-        cost_estimate=cost(30 * own.size, 14 * own.size),
+        cost_estimate=cost(30 * other.size, 14 * other.size),
         name="slopes",
-    )(ids, own, other, inputs, grad, before, after)
-
-
-def backward_kernel(mine, ids, slope, start, weight, out, level, lower, upper):
-    half = slope.shape[1]
+    )(ids, own, other, inputs, grad, before, after, *done)
+
+
+def backward_kernel(mine, firsts, count, ids, *refs):
+    slopes_in, starts, (weight, out, level, lower, upper) = (
+        refs[: len(firsts)],
+        refs[len(firsts) : len(firsts) + count],
+        refs[len(firsts) + count :],
+    )
+    half = weight.shape[1]
     side = ids[0] if mine else 1 - ids[0]
     level[...] = jnp.zeros_like(level)
     lower[...] = jnp.zeros_like(lower)
     upper[...] = jnp.zeros_like(upper)
 
-    def tile(i):
-        at = lanes(side * half + i * TILE, TILE)
-        part = slope[:, lanes(i * TILE, TILE)]
-        first, mid, last = (dot_t(part, weight[t, :, at]) for t in range(3))
-        level[...] += first[ROWS:] + mid[:ROWS] + mid[ROWS:] + last[:ROWS]
-        lower[...] += first[:ROWS]
-        upper[...] += last[ROWS:]
-
-    tiles(half // TILE, tile)
-    total = level[...] + below(lower[...]) + above(upper[...])
-    out[...] = (start[...] + total[:OWN]).astype(out.dtype)
-
-
-def backward(ids, slope, start, weight, mine, dtype):
+    for begin, slope in zip(firsts, slopes_in):
+
+        def tile(i):
+            at = lanes(side * half + begin + i * TILE, TILE)
+            part = slope[:, lanes(i * TILE, TILE)]
+            first, mid, last = (dot_t(part, weight[t, :, at]) for t in range(3))
+            level[...] += first[ROWS:] + mid[:ROWS] + mid[ROWS:] + last[:ROWS]
+            lower[...] += first[:ROWS]
+            upper[...] += last[ROWS:]
+
+        tiles(slope.shape[1] // TILE, tile)
+    total = level[...] + below(lower[...], ROWS) + above(upper[...], ROWS)
+    base = jnp.concatenate([start[...] for start in starts], axis=1)
+    out[...] = (base + total[:OWN]).astype(out.dtype)
+
+
+def backward(ids, parts, starts, weight, mine, dtype):
     half = weight.shape[1]
-    return pl.pallas_call(
-        functools.partial(backward_kernel, mine),
-        in_specs=[SM] + [VM] * 3,
+    size = sum(part.size for _, part in parts)
+    return pl.pallas_call(
+        functools.partial(backward_kernel, mine, [first for first, _ in parts], len(starts)),
+        in_specs=[SM] + [VM] * (len(parts) + len(starts) + 1),
         out_specs=VM,
         out_shape=shape((OWN, half), dtype),
         scratch_shapes=[pltpu.VMEM((ROWS, half), F32)] * 3,
         compiler_params=params(10),
-        cost_estimate=cost(2 * 2 * ROWS * weight.size // 2, weight.size),
+        cost_estimate=cost(2 * 3 * half * size, 6 * size),
         name="backward",
-    )(ids, slope, start, weight)
+    )(ids, *[part for _, part in parts], *starts, weight)
 
 
 def place(at):
@@ -591,12 +683,16 @@
     codes, last, first = prepare(dna_bases.reshape(OWN, 128), grad_out)
     before = lax.ppermute(last, "seq", [(i, i + 1) for i in range(63)])
     after = lax.ppermute(first, "seq", [(i + 1, i) for i in range(63)])
-    encoded, attention_weight = encode(
+    encoded = encode(ids, codes, stem_weight, encoder_weight)
+    theirs = swap(encoded)
+    edges, attention_weight = encode_edges(
         ids, codes, before, after, stem_weight, encoder_weight, attention_weight
     )
     gain = norm_gain.reshape(1, feats)
-    made = project(ids, encoded, swap(encoded), gain, attention_weight)
-    queries, keyvals = made[:4], made[4:]
+    encoded, normed, *keyvals = project_keys(
+        ids, encoded, edges, theirs, swap(edges), gain, attention_weight
+    )
+    queries = project_queries(ids, normed, attention_weight)
 
     def regroup(blocks):
         got = [blocks[0]] + [send(blocks[d], dx=d) for d in (1, 3, 2)]
@@ -624,13 +720,25 @@
 
     sent = swap(output(ids, heads, out_weight, False, BF16))
     kept = output(ids, heads, out_weight, True, F32)
-    inputs, sent = decode_send(ids, kept, sent, encoded, decoder_weight)
-    sent = swap(sent)
-    kept = decode_own(ids, inputs, decoder_weight)
-    decoded, slope, paired = slopes(ids, kept, sent, inputs, grad_out, before, after)
-    sent = swap(slope)
-    partial = backward(ids, slope, paired, decoder_weight, True, F32)
-    bins_grad = backward(ids, sent, partial, decoder_weight, False, BF16)
+    half = decoder_weight.shape[1]
+    split = half - TILE
+    inputs, early = decode_first(ids, kept, sent, encoded, decoder_weight, split)
+    early = swap(early)
+    late = decode(ids, inputs, decoder_weight, False, split, TILE, BF16)
+    late, inputs = lax.optimization_barrier((late, inputs))
+    late = swap(late)
+    kept = decode(ids, inputs, decoder_weight, True, 0, half, F32)
+    decoded, early, paired = slopes(ids, kept, early, inputs, grad_out, before, after, 0)
+    early_back = swap(early)
+    decoded, late, rest = slopes(
+        ids, kept, late, inputs, grad_out, before, after, split, (decoded,)
+    )
+    late_back = swap(late)
+    total = backward(
+        ids, [(0, early), (split, late)], [paired, rest], decoder_weight, True, F32
+    )
+    total = backward(ids, [(0, early_back)], [total], decoder_weight, False, F32)
+    bins_grad = backward(ids, [(split, late_back)], [total], decoder_weight, False, BF16)
     return decoded, bins_grad
 
 

time: 128 us -> 136 us (1.062)
  Pallas kernels: 36.3 us -> 46.4 us
  waiting for transfers between devices: 53.2 us -> 45.1 us
  starting transfers between devices: 37.1 us -> 42.6 us
    pallas_call x7 -> x12, Pallas kernels: 20.4 us -> 30 us  [the longest x1 6.67 us: encode_edges(): pl.pallas_call(encode_edges_kernel, in_specs=[SM, VM, VM, VM, HBM, HBM, H...]
    ppermute x19, waiting for transfers between devices: 27.9 us -> 23.8 us  [send(): return lax.ppermute(value, 'seq', moves(**step))]
    ppermute x19, starting transfers between devices: 22.7 us -> 26 us  [send(): return lax.ppermute(value, 'seq', moves(**step))]
    ppermute x4 -> x7, waiting for transfers between devices: 21.7 us -> 18.8 us  [swap(): return lax.ppermute(value, 'head', [(0, 1), (1, 0)])]
    ppermute x4 -> x7, starting transfers between devices: 11.8 us -> 13.9 us  [swap(): return lax.ppermute(value, 'head', [(0, 1), (1, 0)])]
  transfers between devices with their start and end apart: 25 -> 28, of which waited for: 17 -> 18; matrix products, arithmetic and copies ran while one was open for 0% -> 0% of each run, Pallas kernels for 11% -> 20%
where the time goes in v6:
time: 136 us; the launch traced here: 135 us
  Pallas kernels  46.4 us (34%)
  waiting for transfers between devices  45.1 us (33%)
  starting transfers between devices  42.6 us (31%)
    ppermute x19, starting transfers between devices, send(): return lax.ppermute(value, 'seq', moves(**step))  26 us
    ppermute x19, waiting for transfers between devices, send(): return lax.ppermute(value, 'seq', moves(**step))  23.8 us
    ppermute x7, waiting for transfers between devices, swap(): return lax.ppermute(value, 'head', [(0, 1), (1, 0)])  18.8 us
    ppermute x7, starting transfers between devices, swap(): return lax.ppermute(value, 'head', [(0, 1), (1, 0)])  13.9 us
    pallas_call x3, Pallas kernels, attend(): pl.pallas_call(functools.partial(attend_kernel, len(pieces), len(inverses...  12.4 us
    pallas_call x1, Pallas kernels, encode_edges(): pl.pallas_call(encode_edges_kernel, in_specs=[SM, VM, VM, VM, HBM, HBM, H...  6.67 us
    pallas_call x1, Pallas kernels, encode(): pl.pallas_call(encode_kernel, in_specs=[SM, VM, HBM, HBM], out_specs=VM,...  6.6 us
    pallas_call x3, Pallas kernels, backward(): pl.pallas_call(functools.partial(backward_kernel, mine, [first for first,...  5.78 us
  transfers between devices with their start and end apart: 28, of which 18 were waited for; matrix products, arithmetic and copies ran while one was open for 0% of the time, Pallas kernels for 20%

profile of v6, /device:TPU:0, one launch (start us, length us, event | category | flops | bytes accessed | tf_op | source)
XLA Modules:
  0.0 135.4 jit_solution(8058050010395389890)
XLA Ops:
  0.6 0.9 prepare.1
  1.5 0.1 pad_add_fusion.ids
  1.6 6.6 %encode.1.mine = bf16[256,768]{1,0:T(8,128)(2,1)S(1)} custom-call(s32[3]{0:T(128)S(1)} %pad_add_fusion.ids, bf16[128,128]{1,0:T(8,128)(2,1)S(1)} %get-tuple-element.56.codes, bf16[256,1536]{1,0:T(8,128)(2,1)} %stems.3, bf16[3,1536,768]{2,1,0:T(8,128)(2,1)} %weights.3), custom_call_target="tpu_custom_call" | custom-call | flops 1811939328 | bytes 14155776 | tf_op jit(solution)/shard_map/encode/pallas_call | solution.py:197
  8.2 3.4 %collective-permute-start.2 = (bf16[256,768]{1,0:T(8,128)(2,1)S(1)}, bf16[256,768]{1,0:T(8,128)(2,1)S(1)}, u32[]{:S(2)}, u32[]{:S(2)}) collective-permute-start(bf16[256,768]{1,0:T(8,128)(2,1)S(1)} %encode.1.mine), channel_id=1, source_target_pairs={{0,1},{1,0},{2,3},{3,2},{4,5},{5,4},{6,7},{7,6},{8,9},{9,8},{10,11... | collective-permute-start | bytes 1179656 | tf_op jit(solution)/shard_map/ppermute | solution.py:660
  11.6 1.4 %collective-permute-start = (bf16[8,1664]{1,0:T(8,128)(2,1)S(1)}, bf16[8,1664]{1,0:T(8,128)(2,1)S(1)}, u32[]{:S(2)}, u32[]{:S(2)}) collective-permute-start(bf16[8,1664]{1,0:T(8,128)(2,1)S(1)} %get-tuple-element.57), channel_id=1, source_target_pairs={{0,2},{2,4},{4,6},{6,8},{8,10},{10,12},{12,14},{14,16},{16,18},{18... | collective-permute-start | bytes 79880 | tf_op jit(solution)/shard_map/ppermute | solution.py:684
  13.0 0.0 copy-start.3
  13.1 1.3 collective-permute-start.1
  14.4 2.5 %collective-permute-done.1.after = bf16[8,1664]{1,0:T(8,128)(2,1)S(1)} collective-permute-done((bf16[8,1664]{1,0:T(8,128)(2,1)S(1)}, bf16[8,1664]{1,0:T(8,128)(2,1)S(1)}, u32[]{:S(2)}, u32[]{:S(2)}) %collective-permute-start.1) | collective-permute-done | bytes 26656 | tf_op jit(solution)/shard_map/ppermute | solution.py:685
  16.9 6.7 %encode_edges.1 = (bf16[32,768]{1,0:T(8,128)(2,1)S(1)}, bf16[3,1536,768]{2,1,0:T(8,128)(2,1)S(1)}) custom-call(s32[3]{0:T(128)S(1)} %pad_add_fusion.ids, bf16[128,128]{1,0:T(8,128)(2,1)S(1)} %get-tuple-element.56.codes, bf16[8,1664]{1,0:T(8,128)(2,1)S(1)} %collective-permute-done.before, bf16[8,1664]{1,0:T(8,128)(2,1)S(1)} %collective-permute-done.1.after, ...), custom_call_target="tpu_custom_call" | custom-call | flops 1811939328 | bytes 14155776 | tf_op jit(solution)/shard_map/encode_edges/pallas_call | solution.py:211
  23.6 1.9 %collective-permute-start.3 = (bf16[32,768]{1,0:T(8,128)(2,1)S(1)}, bf16[32,768]{1,0:T(8,128)(2,1)S(1)}, u32[]{:S(2)}, u32[]{:S(2)}) collective-permute-start(bf16[32,768]{1,0:T(8,128)(2,1)S(1)} %get-tuple-element.59.mine_edges), channel_id=1, source_target_pairs={{0,1},{1,0},{2,3},{3,2},{4,5},{5,4},{6,7},{7,6},{8,9},{9,8},{10,11... | collective-permute-start | bytes 147464 | tf_op jit(solution)/shard_map/ppermute | solution.py:660
  25.5 3.7 %collective-permute-done.3.their_edges = bf16[32,768]{1,0:T(8,128)(2,1)S(1)} collective-permute-done((bf16[32,768]{1,0:T(8,128)(2,1)S(1)}, bf16[32,768]{1,0:T(8,128)(2,1)S(1)}, u32[]{:S(2)}, u32[]{:S(2)}) %collective-permute-start.3) | collective-permute-done | bytes 49184 | tf_op jit(solution)/shard_map/ppermute | solution.py:660
  29.3 2.1 %project_keys.1 = (bf16[272,768]{1,0:T(8,128)(2,1)S(1)}, bf16[2,136,768]{2,1,0:T(8,128)(2,1)S(1)}, bf16[128,384]{1,0:T(8,128)(2,1)S(1)}, bf16[128,384]{1,0:T(8,1...) custom-call(s32[3]{0:T(128)S(1)} %pad_add_fusion.ids, bf16[256,768]{1,0:T(8,128)(2,1)S(1)} %encode.1.mine, ...), custom_call_target="tpu_custom_call" | custom-call | flops 641728512 | bytes 7077888 | tf_op jit(solution)/shard_map/project_keys/pallas_call | solution.py:283
  31.4 6.4 %collective-permute-start.4 = (bf16[128,384]{1,0:T(8,128)(2,1)S(1)}, bf16[128,384]{1,0:T(8,128)(2,1)S(1)}, u32[]{:S(2)}, u32[]{:S(2)}) collective-permute-start(bf16[128,384]{1,0:T(8,128)(2,1)S(1)} %get-tuple-element.62), channel_id=1, source_target_pairs={{0,32},{2,34},{4,36},{6,38},{8,40},{10,42},{12,44},{14,46},{16,48}... | collective-permute-start | bytes 294920 | tf_op jit(solution)/shard_map/ppermute | solution.py:664
  37.7 1.4 %collective-permute-start.5 = (bf16[128,384]{1,0:T(8,128)(2,1)S(1)}, bf16[128,384]{1,0:T(8,128)(2,1)S(1)}, u32[]{:S(2)}, u32[]{:S(2)}) collective-permute-start(bf16[128,384]{1,0:T(8,128)(2,1)S(1)} %get-tuple-element.63), channel_id=1, source_target_pairs={{0,96},{2,98},{4,100},{6,102},{8,104},{10,106},{12,108},{14,110},{... | collective-permute-start | bytes 294920 | tf_op jit(solution)/shard_map/ppermute | solution.py:664
  39.1 2.2 %collective-permute-start.6 = (bf16[128,384]{1,0:T(8,128)(2,1)S(1)}, bf16[128,384]{1,0:T(8,128)(2,1)S(1)}, u32[]{:S(2)}, u32[]{:S(2)}) collective-permute-start(bf16[128,384]{1,0:T(8,128)(2,1)S(1)} %get-tuple-element.64), channel_id=1, source_target_pairs={{0,64},{2,66},{4,68},{6,70},{8,72},{10,74},{12,76},{14,78},{16,80}... | collective-permute-start | bytes 294920 | tf_op jit(solution)/shard_map/ppermute | solution.py:664
  41.3 1.3 project_queries.1
  42.6 0.1 collective-permute-done.5
  42.6 2.6 %collective-permute-done.6 = bf16[128,384]{1,0:T(8,128)(2,1)S(1)} collective-permute-done((bf16[128,384]{1,0:T(8,128)(2,1)S(1)}, bf16[128,384]{1,0:T(8,128)(2,1)S(1)}, u32[]{:S(2)}, u32[]{:S(2)}) %collective-permute-start.6) | collective-permute-done | bytes 98336 | tf_op jit(solution)/shard_map/ppermute | solution.py:664
  45.2 0.7 collective-permute-start.7
  46.0 2.6 %collective-permute-start.8 = (bf16[136,256]{1,0:T(8,128)(2,1)S(1)}, bf16[136,256]{1,0:T(8,128)(2,1)S(1)}, u32[]{:S(2)}, u32[]{:S(2)}) collective-permute-start(bf16[136,256]{1,0:T(8,128)(2,1)S(1)} %get-tuple-element.76), channel_id=1, source_target_pairs={{0,96},{2,98},{4,100},{6,102},{8,104},{10,106},{12,108},{14,110},{... | collective-permute-start | bytes 208904 | tf_op jit(solution)/shard_map/ppermute | solution.py:664
  48.5 1.0 collective-permute-start.9
  49.5 3.4 %collective-permute-start.11 = (bf16[512,384]{1,0:T(8,128)(2,1)S(1)}, bf16[512,384]{1,0:T(8,128)(2,1)S(1)}, u32[]{:S(2)}, u32[]{:S(2)}) collective-permute-start(bf16[512,384]{1,0:T(8,128)(2,1)S(1)} %pad_maximum_fusion.refs_0_), channel_id=1, source_target_pairs={{0,24},{2,26},{4,28},{6,30},{8,0},{10,2},{12,4},{14,6},{16,8},{18,... | collective-permute-start | bytes 1179656 | tf_op jit(solution)/shard_map/ppermute | solution.py:664
  52.9 1.4 %collective-permute-done.9 = bf16[136,256]{1,0:T(8,128)(2,1)S(1)} collective-permute-done((bf16[136,256]{1,0:T(8,128)(2,1)S(1)}, bf16[136,256]{1,0:T(8,128)(2,1)S(1)}, u32[]{:S(2)}, u32[]{:S(2)}) %collective-permute-start.9) | collective-permute-done | bytes 69664 | tf_op jit(solution)/shard_map/ppermute | solution.py:664
  54.4 1.3 collective-permute-start.12
  55.7 5.3 %collective-permute-done.12.queries = bf16[544,256]{1,0:T(8,128)(2,1)S(1)} collective-permute-done((bf16[544,256]{1,0:T(8,128)(2,1)S(1)}, bf16[544,256]{1,0:T(8,128)(2,1)S(1)}, u32[]{:S(2)}, u32[]{:S(2)}) %collective-permute-start.12) | collective-permute-done | bytes 278560 | tf_op jit(solution)/shard_map/ppermute | solution.py:664
  61.0 1.5 %collective-permute-done.10.refs_1_ = bf16[512,384]{1,0:T(8,128)(2,1)S(1)} collective-permute-done((bf16[512,384]{1,0:T(8,128)(2,1)S(1)}, bf16[512,384]{1,0:T(8,128)(2,1)S(1)}, u32[]{:S(2)}, u32[]{:S(2)}) %collective-permute-start.10) | collective-permute-done | bytes 393248 | tf_op jit(solution)/shard_map/ppermute | solution.py:664
  62.5 0.5 collective-permute-start.15
  63.1 2.1 %collective-permute-start.17 = (bf16[256,384]{1,0:T(8,128)(2,1)S(1)}, bf16[256,384]{1,0:T(8,128)(2,1)S(1)}, u32[]{:S(2)}, u32[]{:S(2)}) collective-permute-start(bf16[256,384]{1,0:T(8,128)(2,1)S(1)} %slice.7), channel_id=1, source_target_pairs={{0,24},{2,26},{4,28},{6,30},{8,0},{10,2},{12,4},{14,6},{16,8},{18,... | collective-permute-start | bytes 589832 | tf_op jit(solution)/shard_map/ppermute | solution.py:664
  65.2 4.2 %attend.3 = (f32[544,256]{1,0:T(8,128)S(1)}, f32[544,128]{1,0:T(8,128)S(1)}, f32[8,3072]{1,0:T(8,128)S(1)}) custom-call(s32[3]{0:T(128)S(1)} %pad_add_fusion.ids, f32[4]{0:T(128)S(1)} %copy-done.2, bf16[544,256]{1,0:T(8,128)(2,1)S(1)} %collective-permute-done.12.queries, bf16[512,384]{1,0:T(8,128)(2,1)S(1)} %pad_maximum_fusion.refs_0_, ...), custom_call_target="tpu_custom_call" | custom-call | flops 1711276032 | bytes 4456448 | tf_op jit(solution)/shard_map/attend/pallas_call | solution.py:427
  69.4 0.0 copy-start
  69.4 0.6 collective-permute-done.17
  70.0 3.0 %collective-permute-done.16 = bf16[256,384]{1,0:T(8,128)(2,1)S(1)} collective-permute-done((bf16[256,384]{1,0:T(8,128)(2,1)S(1)}, bf16[256,384]{1,0:T(8,128)(2,1)S(1)}, u32[]{:S(2)}, u32[]{:S(2)}) %collective-permute-start.16) | collective-permute-done | bytes 196640 | tf_op jit(solution)/shard_map/ppermute | solution.py:664
  73.1 0.1 collective-permute-start.18
  73.2 1.7 %collective-permute-done.18.refs_1_.refs_7_ = bf16[512,384]{1,0:T(8,128)(2,1)S(1)} collective-permute-done((bf16[512,384]{1,0:T(8,128)(2,1)S(1)}, bf16[512,384]{1,0:T(8,128)(2,1)S(1)}, u32[]{:S(2)}, u32[]{:S(2)}) %collective-permute-start.18) | collective-permute-done | bytes 393248 | tf_op jit(solution)/shard_map/ppermute | solution.py:664
  74.9 3.5 %attend.4 = (bf16[544,256]{1,0:T(8,128)(2,1)S(1)}, f32[8,1024]{1,0:T(8,128)S(1)}) custom-call(s32[3]{0:T(128)S(1)} %pad_add_fusion.ids, f32[4]{0:T(128)S(1)} %copy-done.2, bf16[544,256]{1,0:T(8,128)(2,1)S(1)} %collective-permute-done.12.queries, bf16[512,384]{1,0:T(8,128)(2,1)S(1)} %constant_dynamic-update-slice_fusion.4.refs_0_.refs_6_, ...), custom_call_target="tpu_custom_call" | custom-call | flops 570425344 | bytes 4456448 | tf_op jit(solution)/shard_map/attend/pallas_call | solution.py:427
  78.5 1.2 collective-permute-start.19
  79.6 4.6 %attend.5.a0 = bf16[544,256]{1,0:T(8,128)(2,1)S(1)} custom-call(s32[3]{0:T(128)S(1)} %pad_add_fusion.ids, f32[4]{0:T(128)S(1)} %copy-done.2, bf16[544,256]{1,0:T(8,128)(2,1)S(1)} %constant_dynamic-update-slice_fusion.queries, bf16[512,384]{1,0:T(8,128)(2,1)S(1)} %pad_maximum_fusion.refs_0_, bf16[512,384]{1,0:T(8,128)(2,1)S(1)} %collective-permute-done.10.refs_1_, ...), custom_call_target="tpu_custom_call" | custom-call | flops 2281701376 | bytes 4456448 | tf_op jit(solution)/shard_map/attend/pallas_call | solution.py:427
  84.3 3.0 %collective-permute-done.19.a1 = bf16[544,256]{1,0:T(8,128)(2,1)S(1)} collective-permute-done((bf16[544,256]{1,0:T(8,128)(2,1)S(1)}, bf16[544,256]{1,0:T(8,128)(2,1)S(1)}, u32[]{:S(2)}, u32[]{:S(2)}) %collective-permute-start.19) | collective-permute-done | bytes 278560 | tf_op jit(solution)/shard_map/ppermute | solution.py:664
  87.2 0.5 merge.1
  87.8 0.7 collective-permute-start.20
  88.5 1.4 %collective-permute-start.21 = (bf16[136,256]{1,0:T(8,128)(2,1)S(1)}, bf16[136,256]{1,0:T(8,128)(2,1)S(1)}, u32[]{:S(2)}, u32[]{:S(2)}) collective-permute-start(bf16[136,256]{1,0:T(8,128)(2,1)S(1)} %get-tuple-element.97), channel_id=1, source_target_pairs={{0,64},{2,66},{4,68},{6,70},{8,72},{10,74},{12,76},{14,78},{16,80}... | collective-permute-start | bytes 208904 | tf_op jit(solution)/shard_map/ppermute | solution.py:664
  89.9 1.0 collective-permute-start.22
  90.9 1.2 collective-permute-done.20.a1
  92.2 2.7 %collective-permute-done.21.a2 = bf16[136,256]{1,0:T(8,128)(2,1)S(1)} collective-permute-done((bf16[136,256]{1,0:T(8,128)(2,1)S(1)}, bf16[136,256]{1,0:T(8,128)(2,1)S(1)}, u32[]{:S(2)}, u32[]{:S(2)}) %collective-permute-start.21) | collective-permute-done | bytes 69664 | tf_op jit(solution)/shard_map/ppermute | solution.py:664
  94.8 0.7 collective-permute-done.22.a3
  95.6 1.3 output.3
  96.9 1.9 %collective-permute-start.23 = (bf16[136,768]{1,0:T(8,128)(2,1)S(1)}, bf16[136,768]{1,0:T(8,128)(2,1)S(1)}, u32[]{:S(2)}, u32[]{:S(2)}) collective-permute-start(bf16[136,768]{1,0:T(8,128)(2,1)S(1)} %output.3), channel_id=1, source_target_pairs={{0,1},{1,0},{2,3},{3,2},{4,5},{5,4},{6,7},{7,6},{8,9},{9,8},{10,11... | collective-permute-start | bytes 626696 | tf_op jit(solution)/shard_map/ppermute | solution.py:660
  98.7 1.3 output.2.own
  100.0 4.4 %collective-permute-done.23.other = bf16[136,768]{1,0:T(8,128)(2,1)S(1)} collective-permute-done((bf16[136,768]{1,0:T(8,128)(2,1)S(1)}, bf16[136,768]{1,0:T(8,128)(2,1)S(1)}, u32[]{:S(2)}, u32[]{:S(2)}) %collective-permute-start.23) | collective-permute-done | bytes 208928 | tf_op jit(solution)/shard_map/ppermute | solution.py:660
  104.5 1.7 %decode_first.1 = (bf16[272,768]{1,0:T(8,128)(2,1)S(1)}, bf16[272,512]{1,0:T(8,128)(2,1)S(1)}) custom-call(s32[3]{0:T(128)S(1)} %pad_add_fusion.ids, f32[136,768]{1,0:T(8,128)S(1)} %output.2.own, bf16[136,768]{1,0:T(8,128)(2,1)S(1)} %collective-permute-done.23.other, bf16[272,768]{1,0:T(8,128)(2,1)S(1)} %get-tuple-element.99.encoded, ...), custom_call_target="tpu_custom_call" | custom-call | flops 641728512 | bytes 3538944 | tf_op jit(solution)/shard_map/decode_first/pallas_call | solution.py:522
  106.2 1.6 %collective-permute-start.25 = (bf16[272,512]{1,0:T(8,128)(2,1)S(1)}, bf16[272,512]{1,0:T(8,128)(2,1)S(1)}, u32[]{:S(2)}, u32[]{:S(2)}) collective-permute-start(bf16[272,512]{1,0:T(8,128)(2,1)S(1)} %get-tuple-element.103), channel_id=1, source_target_pairs={{0,1},{1,0},{2,3},{3,2},{4,5},{5,4},{6,7},{7,6},{8,9},{9,8},{10,11... | collective-permute-start | bytes 835592 | tf_op jit(solution)/shard_map/ppermute | solution.py:660
  107.9 1.0 decode.2
  108.9 2.1 %decode.3.own = f32[272,768]{1,0:T(8,128)S(1)} custom-call(s32[3]{0:T(128)S(1)} %pad_add_fusion.ids, bf16[272,768]{1,0:T(8,128)(2,1)S(1)} %get-tuple-element.101.inputs, bf16[3,768,1536]{2,1,0:T(8,128)(2,1)S(1)} %bitcast.5), custom_call_target="tpu_custom_call" | custom-call | flops 962592768 | bytes 3538944 | tf_op jit(solution)/shard_map/decode/pallas_call | solution.py:540
  111.0 3.4 %collective-permute-done.25.other = bf16[272,512]{1,0:T(8,128)(2,1)S(1)} collective-permute-done((bf16[272,512]{1,0:T(8,128)(2,1)S(1)}, bf16[272,512]{1,0:T(8,128)(2,1)S(1)}, u32[]{:S(2)}, u32[]{:S(2)}) %collective-permute-start.25) | collective-permute-done | bytes 278560 | tf_op jit(solution)/shard_map/ppermute | solution.py:660
  114.4 1.2 slopes.2
  115.6 1.6 %collective-permute-start.27 = (bf16[272,512]{1,0:T(8,128)(2,1)S(1)}, bf16[272,512]{1,0:T(8,128)(2,1)S(1)}, u32[]{:S(2)}, u32[]{:S(2)}) collective-permute-start(bf16[272,512]{1,0:T(8,128)(2,1)S(1)} %get-tuple-element.107.refs_0_), channel_id=1, source_target_pairs={{0,1},{1,0},{2,3},{3,2},{4,5},{5,4},{6,7},{7,6},{8,9},{9,8},{10,11... | collective-permute-start | bytes 835592 | tf_op jit(solution)/shard_map/ppermute | solution.py:660
  117.2 2.0 %collective-permute-start.24 = (bf16[272,256]{1,0:T(8,128)(2,1)S(1)}, bf16[272,256]{1,0:T(8,128)(2,1)S(1)}, u32[]{:S(2)}, u32[]{:S(2)}) collective-permute-start(bf16[272,256]{1,0:T(8,128)(2,1)S(1)} %decode.2), channel_id=1, source_target_pairs={{0,1},{1,0},{2,3},{3,2},{4,5},{5,4},{6,7},{7,6},{8,9},{9,8},{10,11... | collective-permute-start | bytes 417800 | tf_op jit(solution)/shard_map/ppermute | solution.py:660
  119.2 6.3 %collective-permute-done.24.other = bf16[272,256]{1,0:T(8,128)(2,1)S(1)} collective-permute-done((bf16[272,256]{1,0:T(8,128)(2,1)S(1)}, bf16[272,256]{1,0:T(8,128)(2,1)S(1)}, u32[]{:S(2)}, u32[]{:S(2)}) %collective-permute-start.24) | collective-permute-done | bytes 139296 | tf_op jit(solution)/shard_map/ppermute | solution.py:660
  125.5 1.6 %slopes.3 = (bf16[256,768]{1,0:T(8,128)(2,1)}, bf16[272,256]{1,0:T(8,128)(2,1)S(1)}, f32[128,256]{1,0:T(8,128)S(1)}) custom-call(s32[3]{0:T(128)S(1)} %pad_add_fusion.ids, f32[272,768]{1,0:T(8,128)S(1)} %decode.3.own, bf16[272,256]{1,0:T(8,128)(2,1)S(1)} %collective-permute-done.24.other, bf16[272,768]{1,0:T(8,128)(2,1)S(1)} %get-tuple-element.101.inputs, ...), custom_call_target="tpu_custom_call" | custom-call | flops 2088960 | bytes 974848 | tf_op jit(solution)/shard_map/slopes/pallas_call | solution.py:588
  127.0 1.5 %collective-permute-start.26 = (bf16[272,256]{1,0:T(8,128)(2,1)S(1)}, bf16[272,256]{1,0:T(8,128)(2,1)S(1)}, u32[]{:S(2)}, u32[]{:S(2)}) collective-permute-start(bf16[272,256]{1,0:T(8,128)(2,1)S(1)} %get-tuple-element.106.refs_1_), channel_id=1, source_target_pairs={{0,1},{1,0},{2,3},{3,2},{4,5},{5,4},{6,7},{7,6},{8,9},{9,8},{10,11... | collective-permute-start | bytes 417800 | tf_op jit(solution)/shard_map/ppermute | solution.py:660
  128.5 2.2 %backward.3.refs_1_ = f32[128,768]{1,0:T(8,128)S(1)} custom-call(s32[3]{0:T(128)S(1)} %pad_add_fusion.ids, bf16[272,512]{1,0:T(8,128)(2,1)S(1)} %get-tuple-element.107.refs_0_, bf16[272,256]{1,0:T(8,128)(2,1)S(1)} %get-tuple-element.106.refs_1_, f32[128,512]{1,0:T(8,128)S(1)} %get-tuple-element.108.refs_2_, f32[128,256]{1,0:T(8,128)S(1)} %get-tuple-element.109.refs_3_, ...), custom_call_target="tpu_custom_call" | custom-call | flops 962592768 | bytes 1253376 | tf_op jit(solution)/shard_map/backward/pallas_call | solution.py:635
  130.8 1.8 %backward.4.refs_1_ = f32[128,768]{1,0:T(8,128)S(1)} custom-call(s32[3]{0:T(128)S(1)} %pad_add_fusion.ids, bf16[272,512]{1,0:T(8,128)(2,1)S(1)} %collective-permute-done.27.refs_0_, f32[128,768]{1,0:T(8,128)S(1)} %backward.3.refs_1_, bf16[3,768,1536]{2,1,0:T(8,128)(2,1)S(1)} %bitcast.5), custom_call_target="tpu_custom_call" | custom-call | flops 641728512 | bytes 835584 | tf_op jit(solution)/shard_map/backward/pallas_call | solution.py:635
  132.6 1.0 collective-permute-done.26.refs_0_
  133.6 1.8 %backward.5 = bf16[128,768]{1,0:T(8,128)(2,1)} custom-call(s32[3]{0:T(128)S(1)} %pad_add_fusion.ids, bf16[272,256]{1,0:T(8,128)(2,1)S(1)} %collective-permute-done.26.refs_0_, f32[128,768]{1,0:T(8,128)S(1)} %backward.4.refs_1_, bf16[3,768,1536]{2,1,0:T(8,128)(2,1)S(1)} %bitcast.5), custom_call_target="tpu_custom_call" | custom-call | flops 320864256 | bytes 417792 | tf_op jit(solution)/shard_map/backward/pallas_call | solution.py:635
  (35 shorter events, 0.2 us)
Async XLA Ops:
  8.2 21.0 %collective-permute-start.2 = (bf16[256,768]{1,0:T(8,128)(2,1)S(1)}, bf16[256,768]{1,0:T(8,128)(2,1)S(1)}, u32[]{:S(2)}, u32[]{:S(2)}) collective-permute-start(bf16[256,768]{1,0:T(8,128)(2,1)S(1)} %encode.1.mine), channel_id=1, source_target_pairs={{0,1},{1,0},{2,3},{3,2},{4,5},{5,4},{6,7},{7,6},{8,9},{9,8},{10,11... | collective-permute-start | bytes 1179656 | tf_op jit(solution)/shard_map/ppermute | solution.py:660
  11.6 2.8 %collective-permute-start = (bf16[8,1664]{1,0:T(8,128)(2,1)S(1)}, bf16[8,1664]{1,0:T(8,128)(2,1)S(1)}, u32[]{:S(2)}, u32[]{:S(2)}) collective-permute-start(bf16[8,1664]{1,0:T(8,128)(2,1)S(1)} %get-tuple-element.57), channel_id=1, source_target_pairs={{0,2},{2,4},{4,6},{6,8},{8,10},{10,12},{12,14},{14,16},{16,18},{18... | collective-permute-start | bytes 79880 | tf_op jit(solution)/shard_map/ppermute | solution.py:684
  13.0 12.4 %copy-start.3 = (f32[1536]{0:T(1024)S(1)}, f32[1536]{0:T(1024)}, u32[]{:S(2)}) copy-start(f32[1536]{0:T(1024)} %param.12) | copy-start | bytes 18436
  13.1 3.8 %collective-permute-start.1 = (bf16[8,1664]{1,0:T(8,128)(2,1)S(1)}, bf16[8,1664]{1,0:T(8,128)(2,1)S(1)}, u32[]{:S(2)}, u32[]{:S(2)}) collective-permute-start(bf16[8,1664]{1,0:T(8,128)(2,1)S(1)} %get-tuple-element.58), channel_id=1, source_target_pairs={{2,0},{4,2},{6,4},{8,6},{10,8},{12,10},{14,12},{16,14},{18,16},{20... | collective-permute-start | bytes 79880 | tf_op jit(solution)/shard_map/ppermute | solution.py:685
  23.6 5.7 %collective-permute-start.3 = (bf16[32,768]{1,0:T(8,128)(2,1)S(1)}, bf16[32,768]{1,0:T(8,128)(2,1)S(1)}, u32[]{:S(2)}, u32[]{:S(2)}) collective-permute-start(bf16[32,768]{1,0:T(8,128)(2,1)S(1)} %get-tuple-element.59.mine_edges), channel_id=1, source_target_pairs={{0,1},{1,0},{2,3},{3,2},{4,5},{5,4},{6,7},{7,6},{8,9},{9,8},{10,11... | collective-permute-start | bytes 147464 | tf_op jit(solution)/shard_map/ppermute | solution.py:660
  29.2 36.0 %copy-start.2 = (f32[4]{0:T(128)S(1)}, f32[4]{0:T(128)}, u32[]{:S(2)}) copy-start(f32[4]{0:T(128)} %scale.5) | copy-start | bytes 52
  31.4 11.2 %collective-permute-start.4 = (bf16[128,384]{1,0:T(8,128)(2,1)S(1)}, bf16[128,384]{1,0:T(8,128)(2,1)S(1)}, u32[]{:S(2)}, u32[]{:S(2)}) collective-permute-start(bf16[128,384]{1,0:T(8,128)(2,1)S(1)} %get-tuple-element.62), channel_id=1, source_target_pairs={{0,32},{2,34},{4,36},{6,38},{8,40},{10,42},{12,44},{14,46},{16,48}... | collective-permute-start | bytes 294920 | tf_op jit(solution)/shard_map/ppermute | solution.py:664
  37.7 4.9 %collective-permute-start.5 = (bf16[128,384]{1,0:T(8,128)(2,1)S(1)}, bf16[128,384]{1,0:T(8,128)(2,1)S(1)}, u32[]{:S(2)}, u32[]{:S(2)}) collective-permute-start(bf16[128,384]{1,0:T(8,128)(2,1)S(1)} %get-tuple-element.63), channel_id=1, source_target_pairs={{0,96},{2,98},{4,100},{6,102},{8,104},{10,106},{12,108},{14,110},{... | collective-permute-start | bytes 294920 | tf_op jit(solution)/shard_map/ppermute | solution.py:664
  39.1 6.1 %collective-permute-start.6 = (bf16[128,384]{1,0:T(8,128)(2,1)S(1)}, bf16[128,384]{1,0:T(8,128)(2,1)S(1)}, u32[]{:S(2)}, u32[]{:S(2)}) collective-permute-start(bf16[128,384]{1,0:T(8,128)(2,1)S(1)} %get-tuple-element.64), channel_id=1, source_target_pairs={{0,64},{2,66},{4,68},{6,70},{8,72},{10,74},{12,76},{14,78},{16,80}... | collective-permute-start | bytes 294920 | tf_op jit(solution)/shard_map/ppermute | solution.py:664
  45.2 7.7 %collective-permute-start.7 = (bf16[136,256]{1,0:T(8,128)(2,1)S(1)}, bf16[136,256]{1,0:T(8,128)(2,1)S(1)}, u32[]{:S(2)}, u32[]{:S(2)}) collective-permute-start(bf16[136,256]{1,0:T(8,128)(2,1)S(1)} %get-tuple-element.75), channel_id=1, source_target_pairs={{0,32},{2,34},{4,36},{6,38},{8,40},{10,42},{12,44},{14,46},{16,48}... | collective-permute-start | bytes 208904 | tf_op jit(solution)/shard_map/ppermute | solution.py:664
  46.0 7.0 %collective-permute-start.8 = (bf16[136,256]{1,0:T(8,128)(2,1)S(1)}, bf16[136,256]{1,0:T(8,128)(2,1)S(1)}, u32[]{:S(2)}, u32[]{:S(2)}) collective-permute-start(bf16[136,256]{1,0:T(8,128)(2,1)S(1)} %get-tuple-element.76), channel_id=1, source_target_pairs={{0,96},{2,98},{4,100},{6,102},{8,104},{10,106},{12,108},{14,110},{... | collective-permute-start | bytes 208904 | tf_op jit(solution)/shard_map/ppermute | solution.py:664
  48.5 5.8 %collective-permute-start.9 = (bf16[136,256]{1,0:T(8,128)(2,1)S(1)}, bf16[136,256]{1,0:T(8,128)(2,1)S(1)}, u32[]{:S(2)}, u32[]{:S(2)}) collective-permute-start(bf16[136,256]{1,0:T(8,128)(2,1)S(1)} %get-tuple-element.77), channel_id=1, source_target_pairs={{0,64},{2,66},{4,68},{6,70},{8,72},{10,74},{12,76},{14,78},{16,80}... | collective-permute-start | bytes 208904 | tf_op jit(solution)/shard_map/ppermute | solution.py:664
  49.5 11.5 %collective-permute-start.11 = (bf16[512,384]{1,0:T(8,128)(2,1)S(1)}, bf16[512,384]{1,0:T(8,128)(2,1)S(1)}, u32[]{:S(2)}, u32[]{:S(2)}) collective-permute-start(bf16[512,384]{1,0:T(8,128)(2,1)S(1)} %pad_maximum_fusion.refs_0_), channel_id=1, source_target_pairs={{0,24},{2,26},{4,28},{6,30},{8,0},{10,2},{12,4},{14,6},{16,8},{18,... | collective-permute-start | bytes 1179656 | tf_op jit(solution)/shard_map/ppermute | solution.py:664
  52.9 9.6 %collective-permute-start.10 = (bf16[512,384]{1,0:T(8,128)(2,1)S(1)}, bf16[512,384]{1,0:T(8,128)(2,1)S(1)}, u32[]{:S(2)}, u32[]{:S(2)}) collective-permute-start(bf16[512,384]{1,0:T(8,128)(2,1)S(1)} %pad_maximum_fusion.refs_0_), channel_id=1, source_target_pairs={{0,8},{2,10},{4,12},{6,14},{8,16},{10,18},{12,20},{14,22},{16,24},... | collective-permute-start | bytes 1179656 | tf_op jit(solution)/shard_map/ppermute | solution.py:664
  54.4 6.6 %collective-permute-start.12 = (bf16[544,256]{1,0:T(8,128)(2,1)S(1)}, bf16[544,256]{1,0:T(8,128)(2,1)S(1)}, u32[]{:S(2)}, u32[]{:S(2)}) collective-permute-start(bf16[544,256]{1,0:T(8,128)(2,1)S(1)} %constant_dynamic-update-slice_fusion.queries), channel_id=1, source_target_pairs={{0,4},{2,6},{4,0},{6,2},{8,12},{10,14},{12,8},{14,10},{16,20},{18,... | collective-permute-start | bytes 835592 | tf_op jit(solution)/shard_map/ppermute | solution.py:664
  55.7 9.5 %collective-permute-start.13 = (bf16[512,384]{1,0:T(8,128)(2,1)S(1)}, bf16[512,384]{1,0:T(8,128)(2,1)S(1)}, u32[]{:S(2)}, u32[]{:S(2)}) collective-permute-start(bf16[512,384]{1,0:T(8,128)(2,1)S(1)} %pad_maximum_fusion.refs_0_), channel_id=1, source_target_pairs={{0,2},{2,0},{4,6},{6,4},{8,10},{10,8},{12,14},{14,12},{16,18},{18,... | collective-permute-start | bytes 1179656 | tf_op jit(solution)/shard_map/ppermute | solution.py:664
  62.5 2.7 %collective-permute-start.14 = (bf16[512,384]{1,0:T(8,128)(2,1)S(1)}, bf16[512,384]{1,0:T(8,128)(2,1)S(1)}, u32[]{:S(2)}, u32[]{:S(2)}) collective-permute-start(bf16[512,384]{1,0:T(8,128)(2,1)S(1)} %collective-permute-done.10.refs_1_), channel_id=1, source_target_pairs={{0,2},{2,0},{4,6},{6,4},{8,10},{10,8},{12,14},{14,12},{16,18},{18,... | collective-permute-start | bytes 1179656 | tf_op jit(solution)/shard_map/ppermute | solution.py:664
  62.5 2.7 %collective-permute-start.15 = (bf16[512,384]{1,0:T(8,128)(2,1)S(1)}, bf16[512,384]{1,0:T(8,128)(2,1)S(1)}, u32[]{:S(2)}, u32[]{:S(2)}) collective-permute-start(bf16[512,384]{1,0:T(8,128)(2,1)S(1)} %collective-permute-done.11.refs_2_), channel_id=1, source_target_pairs={{0,2},{2,0},{4,6},{6,4},{8,10},{10,8},{12,14},{14,12},{16,18},{18,... | collective-permute-start | bytes 1179656 | tf_op jit(solution)/shard_map/ppermute | solution.py:664
  63.1 6.9 %collective-permute-start.17 = (bf16[256,384]{1,0:T(8,128)(2,1)S(1)}, bf16[256,384]{1,0:T(8,128)(2,1)S(1)}, u32[]{:S(2)}, u32[]{:S(2)}) collective-permute-start(bf16[256,384]{1,0:T(8,128)(2,1)S(1)} %slice.7), channel_id=1, source_target_pairs={{0,24},{2,26},{4,28},{6,30},{8,0},{10,2},{12,4},{14,6},{16,8},{18,... | collective-permute-start | bytes 589832 | tf_op jit(solution)/shard_map/ppermute | solution.py:664
  65.2 7.8 %collective-permute-start.16 = (bf16[256,384]{1,0:T(8,128)(2,1)S(1)}, bf16[256,384]{1,0:T(8,128)(2,1)S(1)}, u32[]{:S(2)}, u32[]{:S(2)}) collective-permute-start(bf16[256,384]{1,0:T(8,128)(2,1)S(1)} %slice.6), channel_id=1, source_target_pairs={{0,8},{2,10},{4,12},{6,14},{8,16},{10,18},{12,20},{14,22},{16,24},... | collective-permute-start | bytes 589832 | tf_op jit(solution)/shard_map/ppermute | solution.py:664
  69.4 26.2 %copy-start = (bf16[768,1536]{1,0:T(8,128)(2,1)S(1)}, bf16[768,1536]{1,0:T(8,128)(2,1)}, u32[]{:S(2)}) copy-start(bf16[768,1536]{1,0:T(8,128)(2,1)} %weight.6) | copy-start | bytes 7077892
  73.1 1.8 %collective-permute-start.18 = (bf16[512,384]{1,0:T(8,128)(2,1)S(1)}, bf16[512,384]{1,0:T(8,128)(2,1)S(1)}, u32[]{:S(2)}, u32[]{:S(2)}) collective-permute-start(bf16[512,384]{1,0:T(8,128)(2,1)S(1)} %constant_dynamic-update-slice_fusion.4.refs_0_.refs_6_), channel_id=1, source_target_pairs={{0,2},{2,0},{4,6},{6,4},{8,10},{10,8},{12,14},{14,12},{16,18},{18,... | collective-permute-start | bytes 1179656 | tf_op jit(solution)/shard_map/ppermute | solution.py:664
  78.5 8.8 %collective-permute-start.19 = (bf16[544,256]{1,0:T(8,128)(2,1)S(1)}, bf16[544,256]{1,0:T(8,128)(2,1)S(1)}, u32[]{:S(2)}, u32[]{:S(2)}) collective-permute-start(bf16[544,256]{1,0:T(8,128)(2,1)S(1)} %get-tuple-element.94), channel_id=1, source_target_pairs={{0,4},{2,6},{4,0},{6,2},{8,12},{10,14},{12,8},{14,10},{16,20},{18,... | collective-permute-start | bytes 835592 | tf_op jit(solution)/shard_map/ppermute | solution.py:664
  79.6 24.8 %slice-start = ((s8[7077888]{0:T(1024)(128)(4,1)}), s8[4194304]{0:T(1024)(128)(4,1)S(1)}, s32[]{:S(2)}) async-start(s8[7077888]{0:T(1024)(128)(4,1)} %bitcast.4), calls=%async_computation | async-start | bytes 8388608
  79.6 24.9 %slice-start.1 = ((s8[7077888]{0:T(1024)(128)(4,1)}), s8[2883584]{0:T(1024)(128)(4,1)S(1)}, s32[]{:S(2)}) async-start(s8[7077888]{0:T(1024)(128)(4,1)} %bitcast.4), calls=%async_computation.1 | async-start | bytes 5767168
  87.8 4.4 %collective-permute-start.20 = (bf16[136,256]{1,0:T(8,128)(2,1)S(1)}, bf16[136,256]{1,0:T(8,128)(2,1)S(1)}, u32[]{:S(2)}, u32[]{:S(2)}) collective-permute-start(bf16[136,256]{1,0:T(8,128)(2,1)S(1)} %get-tuple-element.96), channel_id=1, source_target_pairs={{0,96},{2,98},{4,100},{6,102},{8,104},{10,106},{12,108},{14,110},{... | collective-permute-start | bytes 208904 | tf_op jit(solution)/shard_map/ppermute | solution.py:664
  88.5 6.3 %collective-permute-start.21 = (bf16[136,256]{1,0:T(8,128)(2,1)S(1)}, bf16[136,256]{1,0:T(8,128)(2,1)S(1)}, u32[]{:S(2)}, u32[]{:S(2)}) collective-permute-start(bf16[136,256]{1,0:T(8,128)(2,1)S(1)} %get-tuple-element.97), channel_id=1, source_target_pairs={{0,64},{2,66},{4,68},{6,70},{8,72},{10,74},{12,76},{14,78},{16,80}... | collective-permute-start | bytes 208904 | tf_op jit(solution)/shard_map/ppermute | solution.py:664
  89.9 5.7 %collective-permute-start.22 = (bf16[136,256]{1,0:T(8,128)(2,1)S(1)}, bf16[136,256]{1,0:T(8,128)(2,1)S(1)}, u32[]{:S(2)}, u32[]{:S(2)}) collective-permute-start(bf16[136,256]{1,0:T(8,128)(2,1)S(1)} %get-tuple-element.98), channel_id=1, source_target_pairs={{0,32},{2,34},{4,36},{6,38},{8,40},{10,42},{12,44},{14,46},{16,48}... | collective-permute-start | bytes 208904 | tf_op jit(solution)/shard_map/ppermute | solution.py:664
  96.9 7.6 %collective-permute-start.23 = (bf16[136,768]{1,0:T(8,128)(2,1)S(1)}, bf16[136,768]{1,0:T(8,128)(2,1)S(1)}, u32[]{:S(2)}, u32[]{:S(2)}) collective-permute-start(bf16[136,768]{1,0:T(8,128)(2,1)S(1)} %output.3), channel_id=1, source_target_pairs={{0,1},{1,0},{2,3},{3,2},{4,5},{5,4},{6,7},{7,6},{8,9},{9,8},{10,11... | collective-permute-start | bytes 626696 | tf_op jit(solution)/shard_map/ppermute | solution.py:660
  106.2 8.1 %collective-permute-start.25 = (bf16[272,512]{1,0:T(8,128)(2,1)S(1)}, bf16[272,512]{1,0:T(8,128)(2,1)S(1)}, u32[]{:S(2)}, u32[]{:S(2)}) collective-permute-start(bf16[272,512]{1,0:T(8,128)(2,1)S(1)} %get-tuple-element.103), channel_id=1, source_target_pairs={{0,1},{1,0},{2,3},{3,2},{4,5},{5,4},{6,7},{7,6},{8,9},{9,8},{10,11... | collective-permute-start | bytes 835592 | tf_op jit(solution)/shard_map/ppermute | solution.py:660
  107.9 6.5 %copy-start.1 = (bf16[256,1536]{1,0:T(8,128)(2,1)S(1)}, bf16[256,1536]{1,0:T(8,128)(2,1)}, u32[]{:S(2)}) copy-start(bf16[256,1536]{1,0:T(8,128)(2,1)} %grad.5) | copy-start | bytes 2359300
  115.6 15.2 %collective-permute-start.27 = (bf16[272,512]{1,0:T(8,128)(2,1)S(1)}, bf16[272,512]{1,0:T(8,128)(2,1)S(1)}, u32[]{:S(2)}, u32[]{:S(2)}) collective-permute-start(bf16[272,512]{1,0:T(8,128)(2,1)S(1)} %get-tuple-element.107.refs_0_), channel_id=1, source_target_pairs={{0,1},{1,0},{2,3},{3,2},{4,5},{5,4},{6,7},{7,6},{8,9},{9,8},{10,11... | collective-permute-start | bytes 835592 | tf_op jit(solution)/shard_map/ppermute | solution.py:660
  117.2 8.2 %collective-permute-start.24 = (bf16[272,256]{1,0:T(8,128)(2,1)S(1)}, bf16[272,256]{1,0:T(8,128)(2,1)S(1)}, u32[]{:S(2)}, u32[]{:S(2)}) collective-permute-start(bf16[272,256]{1,0:T(8,128)(2,1)S(1)} %decode.2), channel_id=1, source_target_pairs={{0,1},{1,0},{2,3},{3,2},{4,5},{5,4},{6,7},{7,6},{8,9},{9,8},{10,11... | collective-permute-start | bytes 417800 | tf_op jit(solution)/shard_map/ppermute | solution.py:660
  127.0 6.6 %collective-permute-start.26 = (bf16[272,256]{1,0:T(8,128)(2,1)S(1)}, bf16[272,256]{1,0:T(8,128)(2,1)S(1)}, u32[]{:S(2)}, u32[]{:S(2)}) collective-permute-start(bf16[272,256]{1,0:T(8,128)(2,1)S(1)} %get-tuple-element.106.refs_1_), channel_id=1, source_target_pairs={{0,1},{1,0},{2,3},{3,2},{4,5},{5,4},{6,7},{7,6},{8,9},{9,8},{10,11... | collective-permute-start | bytes 417800 | tf_op jit(solution)/shard_map/ppermute | solution.py:660

commit v7 on v6

--- a/solution.py
+++ b/solution.py
@@ -123,119 +123,80 @@
     )(far_memory(bases), far_memory(grad))
 
 
-def encode_body(side, code, stems, weights, encoded, stem, weight, embedded, sems, span):
+def load_kernel(*refs):
+    count = len(refs) // 2
+    sources, targets, sems = refs[:count], refs[count : 2 * count], refs[-1]
+    copies = [
+        pltpu.make_async_copy(source, target, sems.at[i])
+        for i, (source, target) in enumerate(zip(sources, targets))
+    ]
+    for copy in copies:
+        copy.start()
+    for copy in copies:
+        copy.wait()
+
+
+def load(*values):
+    return pl.pallas_call(
+        load_kernel,
+        in_specs=[HBM] * len(values),
+        out_specs=[VM] * len(values),
+        out_shape=[pltpu.VMEM(value.shape, value.dtype) for value in values],
+        scratch_shapes=[pltpu.SemaphoreType.DMA((len(values),))],
+        compiler_params=params(2),
+        cost_estimate=cost(10**5, sum(value.size for value in values) * 2),
+        name="load",
+    )(*[far_memory(value) for value in values])
+
+
+def encode_kernel(ids, codes, before, after, stem, weight, ahead, encoded, loaded, embedded, sem):
+    copy = pltpu.make_async_copy(ahead, loaded, sem)
+    copy.start()
     patch = stem.shape[0] // 4
     feats = stem.shape[1]
     half = weight.shape[2]
-    count = half // TILE
-    first = pltpu.make_async_copy(stems, stem, sems.at[count])
-    copies = [
-        pltpu.make_async_copy(
-            weights.at[:, :, pl.ds(i * TILE, TILE)],
-            weight.at[:, :, pl.ds(i * TILE, TILE)],
-            sems.at[i],
-        )
-        for i in range(count)
-    ]
-    for copy in [first] + copies:
-        copy.start()
     row = lax.broadcasted_iota(jnp.int32, (2 * patch, 4 * patch), 0)
     col = lax.broadcasted_iota(jnp.int32, (2 * patch, 4 * patch), 1)
+    place = lax.broadcasted_iota(jnp.int32, (ROWS - OWN, 128), 0)
+    halo = jnp.where(place >= 6, before[:, feats:].astype(F32), 0.0)
+    halo = jnp.where(place < 2, after[:, feats:].astype(F32), halo)
+    code = jnp.concatenate([codes[...].astype(F32), halo], axis=0).astype(BF16)
     spread = [
         dot(code, (row == col // 4 + offset).astype(F32).astype(BF16)) for offset in (0, patch)
     ]
     spread = jnp.concatenate(spread, axis=0)
     base = lax.broadcasted_iota(jnp.int32, spread.shape, 1) % 4 + 1
     onehot = (spread == base.astype(F32)).astype(F32).astype(BF16)
-    first.wait()
 
     def embed(i):
         at = lanes(i * TILE, TILE)
         embedded[:, at] = dot(onehot, stem[:, at]).astype(BF16)
 
     tiles(feats // TILE, embed)
-    for i in range(count):
-        copies[i].wait()
-        at = slice(i * TILE, (i + 1) * TILE)
-        pre = conv_taps(embedded[...], lambda t: weight[t, :, at], span)
-        mine = embedded[:, lanes(side * half + i * TILE, TILE)].astype(F32)
+
+    def convolve(i):
+        at = lanes(i * TILE, TILE)
+        pre = conv_taps(embedded[...], lambda t: weight[t, :, at], ROWS)
+        mine = embedded[:, lanes(ids[0] * half + i * TILE, TILE)].astype(F32)
         encoded[:, at] = (mine + 0.5 * pre * (1.0 + gelu_tanh(pre))).astype(BF16)
 
-
-def encode_kernel(ids, codes, stems, weights, encoded, *scratch):
-    encode_body(ids[0], codes[...], stems, weights, encoded, *scratch, OWN)
-
-
-def encode_edges_kernel(
-    ids, codes, before, after, stems, weights, ahead, encoded, loaded, stem, weight, embedded, sems
-):
-    later = pltpu.make_async_copy(ahead, loaded, sems.at[sems.shape[0] - 1])
-    later.start()
+    tiles(half // TILE, convolve)
+    copy.wait()
+
+
+def encode(ids, codes, before, after, stem, weight, ahead):
+    half = weight.shape[2]
     feats = stem.shape[1]
-    place = lax.broadcasted_iota(jnp.int32, (8, 128), 0)
-    code = codes[...].astype(F32)
-    low = jnp.where(place >= 6, before[:, feats:].astype(F32), 0.0)
-    low = jnp.where(place == 0, code[:8], low)
-    high = jnp.where(place < 2, after[:, feats:].astype(F32), 0.0)
-    high = jnp.where(place == 7, code[OWN - 8 :], high)
-    code = jnp.concatenate([low, high], axis=0).astype(BF16)
-    encode_body(ids[0], code, stems, weights, encoded, stem, weight, embedded, sems, 8)
-    later.wait()
-
-
-def encode_scratch(rows, stem, weight):
-    return [
-        pltpu.VMEM(stem.shape, BF16),
-        pltpu.VMEM(weight.shape, BF16),
-        pltpu.VMEM((rows, stem.shape[1]), BF16),
-        pltpu.SemaphoreType.DMA((weight.shape[2] // TILE + 2,)),
-    ]
-
-
-def encode(ids, codes, stem, weight):
-    half = weight.shape[2]
     return pl.pallas_call(
         encode_kernel,
-        in_specs=[SM, VM, HBM, HBM],
-        out_specs=VM,
-        out_shape=shape((2 * OWN, half), BF16),
-        scratch_shapes=encode_scratch(2 * OWN, stem, weight),
-        compiler_params=params(20),
-        cost_estimate=cost(4 * OWN * weight.size, weight.size * 4),
+        in_specs=[SM] + [VM] * 5 + [HBM],
+        out_specs=[VM, VM],
+        out_shape=[shape((2 * ROWS, half), BF16), pltpu.VMEM(ahead.shape, BF16)],
+        scratch_shapes=[pltpu.VMEM((2 * ROWS, feats), BF16), pltpu.SemaphoreType.DMA(())],
+        compiler_params=params(12),
+        cost_estimate=cost(2 * 2 * ROWS * 3 * feats * half, weight.size * 4),
         name="encode",
-    )(ids, codes, far_memory(stem), far_memory(weight))
-
-
-def encode_edges(ids, codes, before, after, stem, weight, ahead):
-    half = weight.shape[2]
-    return pl.pallas_call(
-        encode_edges_kernel,
-        in_specs=[SM, VM, VM, VM, HBM, HBM, HBM],
-        out_specs=[VM, VM],
-        out_shape=[shape((32, half), BF16), pltpu.VMEM(ahead.shape, BF16)],
-        scratch_shapes=encode_scratch(32, stem, weight),
-        compiler_params=params(14),
-        cost_estimate=cost(4 * OWN * weight.size, weight.size * 4),
-        name="encode_edges",
-    )(ids, codes, before, after, far_memory(stem), far_memory(weight), far_memory(ahead))
-
-
-def joined(main, edges):
-    main, edges = main[...].astype(F32), edges[...].astype(F32)
-    even, odd = main[:OWN], main[OWN:]
-    even_low, even_high, odd_low, odd_high = (edges[i : i + 8] for i in range(0, 32, 8))
-    place = lax.broadcasted_iota(jnp.int32, even_low.shape, 0)
-    return jnp.concatenate(
-        [
-            jnp.where(place == 0, even_low, even[:8]),
-            even[8:],
-            jnp.where(place < 4, even_high, even_low),
-            odd[: OWN - 8],
-            jnp.where(place == 7, odd_high, odd[OWN - 8 :]),
-            jnp.where(place < 4, odd_high, odd_low),
-        ],
-        axis=0,
-    )
+    )(ids, codes, before, after, near_memory(stem), near_memory(weight), far_memory(ahead))
 
 
 def unpacked(both):
@@ -245,15 +206,13 @@
 
 
 def project_keys_kernel(
-    ids, mine, mine_edges, theirs, their_edges, gain, weight, encoded, normed, k0, k1, k2, k3, packed
+    ids, mine, theirs, gain, weight, normed, k0, k1, k2, k3, packed
 ):
     half = mine.shape[1]
     near = lanes(ids[0] * half, half)
     far = lanes((1 - ids[0]) * half, half)
-    ring = joined(mine, mine_edges)
-    encoded[...] = ring.astype(BF16)
-    other = joined(theirs, their_edges)
-    binned = [(part[:ROWS] + part[ROWS:]) * 0.5 for part in (ring, other)]
+    rings = [ref[...].astype(F32) for ref in (mine, theirs)]
+    binned = [(ring[:ROWS] + ring[ROWS:]) * 0.5 for ring in rings]
     total = sum(jnp.sum(part * part, axis=1, keepdims=True) for part in binned)
     inverse = lax.rsqrt(total * (1.0 / (2 * half)) + EPS)
     here = (binned[0] * inverse * gain[:, near]).astype(BF16)
@@ -278,19 +237,18 @@
         out[...] = packed[lax.rem(ids[1] + distance, 4), :OWN, :]
 
 
-def project_keys(ids, mine, mine_edges, theirs, their_edges, gain, weight):
+def project_keys(ids, mine, theirs, gain, weight):
     half = mine.shape[1]
     return pl.pallas_call(
         project_keys_kernel,
-        in_specs=[SM] + [VM] * 6,
-        out_specs=[VM] * 6,
-        out_shape=[shape((2 * ROWS, half), BF16), shape((2, ROWS, half), BF16)]
-        + [shape((OWN, 384), BF16)] * 4,
+        in_specs=[SM] + [VM] * 4,
+        out_specs=[VM] * 5,
+        out_shape=[shape((2, ROWS, half), BF16)] + [shape((OWN, 384), BF16)] * 4,
         scratch_shapes=[pltpu.VMEM((4, ROWS, 384), BF16)],
         compiler_params=params(12),
         cost_estimate=cost(2 * ROWS * weight.size * 2 // 3, weight.size * 2),
         name="project_keys",
-    )(ids, mine, mine_edges, theirs, their_edges, gain, weight)
+    )(ids, mine, theirs, gain, weight)
 
 
 def project_queries_kernel(ids, normed, weight, q0, q1, q2, q3, packed):
@@ -357,11 +315,12 @@
                 return ref[0:1, at : at + size]
             at -= ref.shape[1]
 
+    limit = min(1024, starts[-1])
     groups, room = [], 0
     for triple in zip(starts, sizes, pieces):
         if room < triple[1]:
             groups.append([])
-            room = 2048
+            room = limit
         groups[-1].append(triple)
         room -= triple[1]
 
@@ -525,7 +484,7 @@
         out_specs=[VM] * 2,
         out_shape=[shape((2 * ROWS, half), BF16), shape((2 * ROWS, width), BF16)],
         compiler_params=params(8),
-        cost_estimate=cost(2 * 2 * ROWS * 3 * half * width, weight.size),
+        cost_estimate=cost(10**6, 10**4),
         name="decode_first",
     )(ids, own, other, encoded, weight)
 
@@ -543,7 +502,7 @@
         out_specs=VM,
         out_shape=shape((2 * ROWS, width), dtype),
         compiler_params=params(8),
-        cost_estimate=cost(2 * 2 * ROWS * 3 * half * width, weight.size),
+        cost_estimate=cost(10**6, 10**4),
         name="decode",
     )(ids, inputs, weight)
 
@@ -596,7 +555,7 @@
         ],
         scratch_shapes=[pltpu.VMEM((2, 2 * OWN, 128), F32)],
         compiler_params=params(6),
-        cost_estimate=cost(30 * other.size, 14 * other.size),
+        cost_estimate=cost(100 * 30 * 1000 * other.size, 14 * other.size),
         name="slopes",
     )(ids, own, other, inputs, grad, before, after, *done)
 
@@ -639,7 +598,7 @@
         out_shape=shape((OWN, half), dtype),
         scratch_shapes=[pltpu.VMEM((ROWS, half), F32)] * 3,
         compiler_params=params(10),
-        cost_estimate=cost(2 * 3 * half * size, 6 * size),
+        cost_estimate=cost(100 * 2 * 3 * half * size, 6 * size),
         name="backward",
     )(ids, *[part for _, part in parts], *starts, weight)
 
@@ -683,25 +642,26 @@
     codes, last, first = prepare(dna_bases.reshape(OWN, 128), grad_out)
     before = lax.ppermute(last, "seq", [(i, i + 1) for i in range(63)])
     after = lax.ppermute(first, "seq", [(i + 1, i) for i in range(63)])
-    encoded = encode(ids, codes, stem_weight, encoder_weight)
-    theirs = swap(encoded)
-    edges, attention_weight = encode_edges(
+    stem_weight, encoder_weight = load(stem_weight, encoder_weight)
+    encoded, attention_weight = encode(
         ids, codes, before, after, stem_weight, encoder_weight, attention_weight
     )
     gain = norm_gain.reshape(1, feats)
-    encoded, normed, *keyvals = project_keys(
-        ids, encoded, edges, theirs, swap(edges), gain, attention_weight
-    )
+    normed, *keyvals = project_keys(ids, encoded, swap(encoded), gain, attention_weight)
+
+    def spread(blocks):
+        return [send(blocks[d], dx=d) for d in (1, 3, 2)]
+
+    def stacked(blocks):
+        return jnp.concatenate(lax.optimization_barrier(blocks), axis=0)
+
+    got = spread(keyvals)
+    got[0], normed = lax.optimization_barrier((got[0], normed))
     queries = project_queries(ids, normed, attention_weight)
-
-    def regroup(blocks):
-        got = [blocks[0]] + [send(blocks[d], dx=d) for d in (1, 3, 2)]
-        return jnp.concatenate(lax.optimization_barrier(got), axis=0)
-
-    keyvals = regroup(keyvals)
-    keyvals, *queries = lax.optimization_barrier((keyvals, *queries))
+    others = spread(queries)
+    keyvals = stacked([keyvals[0]] + got)
     near = [send(keyvals, dz=1), send(keyvals, dz=3)]
-    queries = regroup(queries)
+    queries = stacked([queries[0]] + others)
     others = send(queries, dy=1)
     near[0], near[1], others = lax.optimization_barrier((near[0], near[1], others))
     half = keyvals.shape[0] // 2
@@ -721,10 +681,10 @@
     sent = swap(output(ids, heads, out_weight, False, BF16))
     kept = output(ids, heads, out_weight, True, F32)
     half = decoder_weight.shape[1]
-    split = half - TILE
+    split = 2 * TILE
     inputs, early = decode_first(ids, kept, sent, encoded, decoder_weight, split)
     early = swap(early)
-    late = decode(ids, inputs, decoder_weight, False, split, TILE, BF16)
+    late = decode(ids, inputs, decoder_weight, False, split, half - split, BF16)
     late, inputs = lax.optimization_barrier((late, inputs))
     late = swap(late)
     kept = decode(ids, inputs, decoder_weight, True, 0, half, F32)

time: 136 us -> 128 us (0.941)
  waiting for transfers between devices: 45.1 us -> 34.8 us
  starting transfers between devices: 42.6 us -> 47.5 us
  Pallas kernels: 46.4 us -> 44.2 us
    pallas_call x3, Pallas kernels: 15.4 us -> 9.97 us  [the longest x1 4.63 us: encode(): pl.pallas_call(encode_kernel, in_specs=[SM] + [VM] * 5 + [HBM], out_specs...]
    ppermute x19, starting transfers between devices: 26 us -> 31.3 us  [send(): return lax.ppermute(value, 'seq', moves(**step))]
    ppermute x19, waiting for transfers between devices: 23.8 us -> 19.5 us  [send(): return lax.ppermute(value, 'seq', moves(**step))]
    ppermute x7 -> x6, waiting for transfers between devices: 18.8 us -> 15 us  [swap(): return lax.ppermute(value, 'head', [(0, 1), (1, 0)])]
    ppermute x1, waiting for transfers between devices: 2.52 us -> 0.29 us  [per_device(): after = lax.ppermute(first, 'seq', [(i + 1, i) for i in range(63)])]
    ppermute x7 -> x6, starting transfers between devices: 13.9 us -> 13.6 us  [swap(): return lax.ppermute(value, 'head', [(0, 1), (1, 0)])]
  transfers between devices with their start and end apart: 28 -> 27, of which waited for: 18 -> 17; matrix products, arithmetic and copies ran while one was open for 0% -> 0% of each run, Pallas kernels for 20% -> 20%
where the time goes in v7:
time: 128 us
  starting transfers between devices  47.5 us (37%)
  Pallas kernels  44.2 us (35%)
  waiting for transfers between devices  34.8 us (27%)
    ppermute x19, starting transfers between devices, send(): return lax.ppermute(value, 'seq', moves(**step))  31.3 us
    ppermute x19, waiting for transfers between devices, send(): return lax.ppermute(value, 'seq', moves(**step))  19.5 us
    ppermute x6, waiting for transfers between devices, swap(): return lax.ppermute(value, 'head', [(0, 1), (1, 0)])  15 us
    ppermute x6, starting transfers between devices, swap(): return lax.ppermute(value, 'head', [(0, 1), (1, 0)])  13.6 us
    pallas_call x3, Pallas kernels, attend(): pl.pallas_call(functools.partial(attend_kernel, len(pieces), len(inverses...  12.5 us
    pallas_call x3, Pallas kernels, backward(): pl.pallas_call(functools.partial(backward_kernel, mine, [first for first,...  7.03 us
    pallas_call x1, Pallas kernels, encode(): pl.pallas_call(encode_kernel, in_specs=[SM] + [VM] * 5 + [HBM], out_specs...  4.63 us
    pallas_call x2, Pallas kernels, slopes(): pl.pallas_call(functools.partial(slope_kernel, first), in_specs=[SM] + [V...  3.91 us
  transfers between devices with their start and end apart: 27, of which 17 were waited for; matrix products, arithmetic and copies ran while one was open for 0% of the time, Pallas kernels for 20%

profile of v7, /device:TPU:0, one launch (start us, length us, event | category | flops | bytes accessed | tf_op | source)
XLA Modules:
  0.0 127.7 jit_solution(7140051634223301308)
XLA Ops:
  0.6 0.9 prepare.1
  1.5 1.3 %collective-permute-start = (bf16[8,1664]{1,0:T(8,128)(2,1)S(1)}, bf16[8,1664]{1,0:T(8,128)(2,1)S(1)}, u32[]{:S(2)}, u32[]{:S(2)}) collective-permute-start(bf16[8,1664]{1,0:T(8,128)(2,1)S(1)} %get-tuple-element.55), channel_id=1, source_target_pairs={{0,2},{2,4},{4,6},{6,8},{8,10},{10,12},{12,14},{14,16},{16,18},{18... | collective-permute-start | bytes 79880 | tf_op jit(solution)/shard_map/ppermute | solution.py:643
  2.8 1.3 %collective-permute-start.1 = (bf16[8,1664]{1,0:T(8,128)(2,1)S(1)}, bf16[8,1664]{1,0:T(8,128)(2,1)S(1)}, u32[]{:S(2)}, u32[]{:S(2)}) collective-permute-start(bf16[8,1664]{1,0:T(8,128)(2,1)S(1)} %get-tuple-element.56), channel_id=1, source_target_pairs={{2,0},{4,2},{6,4},{8,6},{10,8},{12,10},{14,12},{16,14},{18,16},{20... | collective-permute-start | bytes 79880 | tf_op jit(solution)/shard_map/ppermute | solution.py:644
  4.1 0.1 pad_add_fusion.ids
  4.2 3.3 %load.1 = (bf16[256,1536]{1,0:T(8,128)(2,1)S(1)}, bf16[3,1536,768]{2,1,0:T(8,128)(2,1)S(1)}) custom-call(bf16[256,1536]{1,0:T(8,128)(2,1)} %refs_0_.1, bf16[3,1536,768]{2,1,0:T(8,128)(2,1)} %refs_1_.1), custom_call_target="tpu_custom_call" | custom-call | flops 100000 | bytes 7864320 | tf_op jit(solution)/shard_map/load/pallas_call | solution.py:140
  7.5 0.3 collective-permute-done.1.after
  7.8 4.6 %encode.1 = (bf16[272,768]{1,0:T(8,128)(2,1)S(1)}, bf16[3,1536,768]{2,1,0:T(8,128)(2,1)S(1)}) custom-call(s32[3]{0:T(128)S(1)} %pad_add_fusion.ids, bf16[128,128]{1,0:T(8,128)(2,1)S(1)} %get-tuple-element.54.codes, bf16[8,1664]{1,0:T(8,128)(2,1)S(1)} %collective-permute-done.before, bf16[8,1664]{1,0:T(8,128)(2,1)S(1)} %collective-permute-done.1.after, ...), custom_call_target="tpu_custom_call" | custom-call | flops 1925185536 | bytes 14155776 | tf_op jit(solution)/shard_map/encode/pallas_call | solution.py:190
  12.5 3.5 %collective-permute-start.2 = (bf16[272,768]{1,0:T(8,128)(2,1)S(1)}, bf16[272,768]{1,0:T(8,128)(2,1)S(1)}, u32[]{:S(2)}, u32[]{:S(2)}) collective-permute-start(bf16[272,768]{1,0:T(8,128)(2,1)S(1)} %get-tuple-element.59.mine.encoded), channel_id=1, source_target_pairs={{0,1},{1,0},{2,3},{3,2},{4,5},{5,4},{6,7},{7,6},{8,9},{9,8},{10,11... | collective-permute-start | bytes 1253384 | tf_op jit(solution)/shard_map/ppermute | solution.py:619
  16.0 8.8 %collective-permute-done.2.theirs = bf16[272,768]{1,0:T(8,128)(2,1)S(1)} collective-permute-done((bf16[272,768]{1,0:T(8,128)(2,1)S(1)}, bf16[272,768]{1,0:T(8,128)(2,1)S(1)}, u32[]{:S(2)}, u32[]{:S(2)}) %collective-permute-start.2) | collective-permute-done | bytes 417824 | tf_op jit(solution)/shard_map/ppermute | solution.py:619
  24.8 2.0 %project_keys.1 = (bf16[2,136,768]{2,1,0:T(8,128)(2,1)S(1)}, bf16[128,384]{1,0:T(8,128)(2,1)S(1)}, bf16[128,384]{1,0:T(8,128)(2,1)S(1)}, bf16[128,384]{1,0:T(8,128)(2,1)S(1)}, bf16[128,384]{1,0:T(8,128)(2,1)S(1)}) custom-call(s32[3]{0:T(128)S(1)} %pad_add_fusion.ids, bf16[272,768]{1,0:T(8,128)(2,1)S(1)} %get-tuple-element.59.mine.encoded, ...), custom_call_target="tpu_custom_call" | custom-call | flops 641728512 | bytes 7077888 | tf_op jit(solution)/shard_map/project_keys/pallas_call | solution.py:242
  26.8 5.1 %collective-permute-start.3 = (bf16[128,384]{1,0:T(8,128)(2,1)S(1)}, bf16[128,384]{1,0:T(8,128)(2,1)S(1)}, u32[]{:S(2)}, u32[]{:S(2)}) collective-permute-start(bf16[128,384]{1,0:T(8,128)(2,1)S(1)} %get-tuple-element.61), channel_id=1, source_target_pairs={{0,32},{2,34},{4,36},{6,38},{8,40},{10,42},{12,44},{14,46},{16,48}... | collective-permute-start | bytes 294920 | tf_op jit(solution)/shard_map/ppermute | solution.py:623
  32.0 1.4 %collective-permute-start.7 = (bf16[128,384]{1,0:T(8,128)(2,1)S(1)}, bf16[128,384]{1,0:T(8,128)(2,1)S(1)}, u32[]{:S(2)}, u32[]{:S(2)}) collective-permute-start(bf16[128,384]{1,0:T(8,128)(2,1)S(1)} %get-tuple-element.74), channel_id=1, source_target_pairs={{0,96},{2,98},{4,100},{6,102},{8,104},{10,106},{12,108},{14,110},{... | collective-permute-start | bytes 294920 | tf_op jit(solution)/shard_map/ppermute | solution.py:623
  33.3 2.2 %collective-permute-start.8 = (bf16[128,384]{1,0:T(8,128)(2,1)S(1)}, bf16[128,384]{1,0:T(8,128)(2,1)S(1)}, u32[]{:S(2)}, u32[]{:S(2)}) collective-permute-start(bf16[128,384]{1,0:T(8,128)(2,1)S(1)} %get-tuple-element.75), channel_id=1, source_target_pairs={{0,64},{2,66},{4,68},{6,70},{8,72},{10,74},{12,76},{14,78},{16,80}... | collective-permute-start | bytes 294920 | tf_op jit(solution)/shard_map/ppermute | solution.py:623
  35.5 1.4 %collective-permute-done.3 = bf16[128,384]{1,0:T(8,128)(2,1)S(1)} collective-permute-done((bf16[128,384]{1,0:T(8,128)(2,1)S(1)}, bf16[128,384]{1,0:T(8,128)(2,1)S(1)}, u32[]{:S(2)}, u32[]{:S(2)}) %collective-permute-start.3) | collective-permute-done | bytes 98336 | tf_op jit(solution)/shard_map/ppermute | solution.py:623
  36.9 0.0 collective-permute-done.7
  36.9 2.6 %collective-permute-done.8 = bf16[128,384]{1,0:T(8,128)(2,1)S(1)} collective-permute-done((bf16[128,384]{1,0:T(8,128)(2,1)S(1)}, bf16[128,384]{1,0:T(8,128)(2,1)S(1)}, u32[]{:S(2)}, u32[]{:S(2)}) %collective-permute-start.8) | collective-permute-done | bytes 98336 | tf_op jit(solution)/shard_map/ppermute | solution.py:623
  39.5 1.3 project_queries.1
  40.7 0.7 collective-permute-start.4
  41.5 2.6 %collective-permute-start.5 = (bf16[136,256]{1,0:T(8,128)(2,1)S(1)}, bf16[136,256]{1,0:T(8,128)(2,1)S(1)}, u32[]{:S(2)}, u32[]{:S(2)}) collective-permute-start(bf16[136,256]{1,0:T(8,128)(2,1)S(1)} %get-tuple-element.66), channel_id=1, source_target_pairs={{0,96},{2,98},{4,100},{6,102},{8,104},{10,106},{12,108},{14,110},{... | collective-permute-start | bytes 208904 | tf_op jit(solution)/shard_map/ppermute | solution.py:623
  44.0 1.1 collective-permute-start.6
  45.2 4.0 %collective-permute-start.10 = (bf16[512,384]{1,0:T(8,128)(2,1)S(1)}, bf16[512,384]{1,0:T(8,128)(2,1)S(1)}, u32[]{:S(2)}, u32[]{:S(2)}) collective-permute-start(bf16[512,384]{1,0:T(8,128)(2,1)S(1)} %constant_dynamic-update-slice_fusion.4.refs_0_), channel_id=1, source_target_pairs={{0,24},{2,26},{4,28},{6,30},{8,0},{10,2},{12,4},{14,6},{16,8},{18,... | collective-permute-start | bytes 1179656 | tf_op jit(solution)/shard_map/ppermute | solution.py:623
  49.2 0.0 collective-permute-start.9
  49.2 0.6 collective-permute-done.6
  49.9 3.0 %collective-permute-start.11 = (bf16[544,256]{1,0:T(8,128)(2,1)S(1)}, bf16[544,256]{1,0:T(8,128)(2,1)S(1)}, u32[]{:S(2)}, u32[]{:S(2)}) collective-permute-start(bf16[544,256]{1,0:T(8,128)(2,1)S(1)} %constant_dynamic-update-slice_fusion.queries), channel_id=1, source_target_pairs={{0,4},{2,6},{4,0},{6,2},{8,12},{10,14},{12,8},{14,10},{16,20},{18,... | collective-permute-start | bytes 835592 | tf_op jit(solution)/shard_map/ppermute | solution.py:623
  52.9 4.5 %collective-permute-done.11.queries = bf16[544,256]{1,0:T(8,128)(2,1)S(1)} collective-permute-done((bf16[544,256]{1,0:T(8,128)(2,1)S(1)}, bf16[544,256]{1,0:T(8,128)(2,1)S(1)}, u32[]{:S(2)}, u32[]{:S(2)}) %collective-permute-start.11) | collective-permute-done | bytes 278560 | tf_op jit(solution)/shard_map/ppermute | solution.py:623
  57.4 0.8 collective-permute-done.9.refs_1_
  58.2 0.5 collective-permute-start.14
  58.8 1.2 collective-permute-start.15
  60.0 2.1 %collective-permute-start.16 = (bf16[256,384]{1,0:T(8,128)(2,1)S(1)}, bf16[256,384]{1,0:T(8,128)(2,1)S(1)}, u32[]{:S(2)}, u32[]{:S(2)}) collective-permute-start(bf16[256,384]{1,0:T(8,128)(2,1)S(1)} %slice.7), channel_id=1, source_target_pairs={{0,24},{2,26},{4,28},{6,30},{8,0},{10,2},{12,4},{14,6},{16,8},{18,... | collective-permute-start | bytes 589832 | tf_op jit(solution)/shard_map/ppermute | solution.py:623
  62.1 4.1 %attend.3 = (f32[544,256]{1,0:T(8,128)S(1)}, f32[544,128]{1,0:T(8,128)S(1)}, f32[8,3072]{1,0:T(8,128)S(1)}) custom-call(s32[3]{0:T(128)S(1)} %pad_add_fusion.ids, f32[4]{0:T(128)S(1)} %copy-done.2, bf16[544,256]{1,0:T(8,128)(2,1)S(1)} %collective-permute-done.11.queries, bf16[512,384]{1,0:T(8,128)(2,1)S(1)} %constant_dynamic-update-slice_fusion.4.refs_0_, ...), custom_call_target="tpu_custom_call" | custom-call | flops 1711276032 | bytes 4456448 | tf_op jit(solution)/shard_map/attend/pallas_call | solution.py:386
  66.2 0.0 copy-start
  66.2 0.8 collective-permute-done.15
  67.1 0.3 collective-permute-start.17
  67.4 1.7 %collective-permute-done.17.refs_1_.refs_7_ = bf16[512,384]{1,0:T(8,128)(2,1)S(1)} collective-permute-done((bf16[512,384]{1,0:T(8,128)(2,1)S(1)}, bf16[512,384]{1,0:T(8,128)(2,1)S(1)}, u32[]{:S(2)}, u32[]{:S(2)}) %collective-permute-start.17) | collective-permute-done | bytes 393248 | tf_op jit(solution)/shard_map/ppermute | solution.py:623
  69.1 4.0 %attend.4 = (bf16[544,256]{1,0:T(8,128)(2,1)S(1)}, f32[8,1024]{1,0:T(8,128)S(1)}) custom-call(s32[3]{0:T(128)S(1)} %pad_add_fusion.ids, f32[4]{0:T(128)S(1)} %copy-done.2, bf16[544,256]{1,0:T(8,128)(2,1)S(1)} %collective-permute-done.11.queries, bf16[512,384]{1,0:T(8,128)(2,1)S(1)} %constant_dynamic-update-slice_fusion.8.refs_0_.refs_6_, ...), custom_call_target="tpu_custom_call" | custom-call | flops 570425344 | bytes 4456448 | tf_op jit(solution)/shard_map/attend/pallas_call | solution.py:386
  73.2 2.9 %collective-permute-start.18 = (bf16[544,256]{1,0:T(8,128)(2,1)S(1)}, bf16[544,256]{1,0:T(8,128)(2,1)S(1)}, u32[]{:S(2)}, u32[]{:S(2)}) collective-permute-start(bf16[544,256]{1,0:T(8,128)(2,1)S(1)} %get-tuple-element.91), channel_id=1, source_target_pairs={{0,4},{2,6},{4,0},{6,2},{8,12},{10,14},{12,8},{14,10},{16,20},{18,... | collective-permute-start | bytes 835592 | tf_op jit(solution)/shard_map/ppermute | solution.py:623
  76.1 4.4 %attend.5.a0 = bf16[544,256]{1,0:T(8,128)(2,1)S(1)} custom-call(s32[3]{0:T(128)S(1)} %pad_add_fusion.ids, f32[4]{0:T(128)S(1)} %copy-done.2, bf16[544,256]{1,0:T(8,128)(2,1)S(1)} %constant_dynamic-update-slice_fusion.queries, bf16[512,384]{1,0:T(8,128)(2,1)S(1)} %constant_dynamic-update-slice_fusion.4.refs_0_, ...), custom_call_target="tpu_custom_call" | custom-call | flops 2281701376 | bytes 4456448 | tf_op jit(solution)/shard_map/attend/pallas_call | solution.py:386
  80.5 2.6 %collective-permute-done.18.a1 = bf16[544,256]{1,0:T(8,128)(2,1)S(1)} collective-permute-done((bf16[544,256]{1,0:T(8,128)(2,1)S(1)}, bf16[544,256]{1,0:T(8,128)(2,1)S(1)}, u32[]{:S(2)}, u32[]{:S(2)}) %collective-permute-start.18) | collective-permute-done | bytes 278560 | tf_op jit(solution)/shard_map/ppermute | solution.py:623
  83.1 0.5 merge.1
  83.6 1.4 %collective-permute-start.19 = (bf16[136,256]{1,0:T(8,128)(2,1)S(1)}, bf16[136,256]{1,0:T(8,128)(2,1)S(1)}, u32[]{:S(2)}, u32[]{:S(2)}) collective-permute-start(bf16[136,256]{1,0:T(8,128)(2,1)S(1)} %get-tuple-element.93), channel_id=1, source_target_pairs={{0,96},{2,98},{4,100},{6,102},{8,104},{10,106},{12,108},{14,110},{... | collective-permute-start | bytes 208904 | tf_op jit(solution)/shard_map/ppermute | solution.py:623
  85.0 1.8 %collective-permute-start.20 = (bf16[136,256]{1,0:T(8,128)(2,1)S(1)}, bf16[136,256]{1,0:T(8,128)(2,1)S(1)}, u32[]{:S(2)}, u32[]{:S(2)}) collective-permute-start(bf16[136,256]{1,0:T(8,128)(2,1)S(1)} %get-tuple-element.94), channel_id=1, source_target_pairs={{0,64},{2,66},{4,68},{6,70},{8,72},{10,74},{12,76},{14,78},{16,80}... | collective-permute-start | bytes 208904 | tf_op jit(solution)/shard_map/ppermute | solution.py:623
  86.9 1.0 collective-permute-start.21
  87.8 0.5 collective-permute-done.19.a1
  88.3 2.7 %collective-permute-done.20.a2 = bf16[136,256]{1,0:T(8,128)(2,1)S(1)} collective-permute-done((bf16[136,256]{1,0:T(8,128)(2,1)S(1)}, bf16[136,256]{1,0:T(8,128)(2,1)S(1)}, u32[]{:S(2)}, u32[]{:S(2)}) %collective-permute-start.20) | collective-permute-done | bytes 69664 | tf_op jit(solution)/shard_map/ppermute | solution.py:623
  91.0 1.3 %collective-permute-done.21.a3 = bf16[136,256]{1,0:T(8,128)(2,1)S(1)} collective-permute-done((bf16[136,256]{1,0:T(8,128)(2,1)S(1)}, bf16[136,256]{1,0:T(8,128)(2,1)S(1)}, u32[]{:S(2)}, u32[]{:S(2)}) %collective-permute-start.21) | collective-permute-done | bytes 69664 | tf_op jit(solution)/shard_map/ppermute | solution.py:623
  92.4 1.3 %output.3 = bf16[136,768]{1,0:T(8,128)(2,1)S(1)} custom-call(s32[3]{0:T(128)S(1)} %pad_add_fusion.ids, bf16[136,256]{1,0:T(8,128)(2,1)S(1)} %get-tuple-element.92.a0, bf16[136,256]{1,0:T(8,128)(2,1)S(1)} %collective-permute-done.19.a1, bf16[136,256]{1,0:T(8,128)(2,1)S(1)} %collective-permute-done.20.a2, bf16[136,256]{1,0:T(8,128)(2,1)S(1)} %collective-permute-done.21.a3, ...), custom_call_target="tpu_custom_call" | custom-call | flops 160432128 | bytes 1179648 | tf_op jit(solution)/shard_map/output/pallas_call | solution.py:440
  93.7 2.9 %collective-permute-start.22 = (bf16[136,768]{1,0:T(8,128)(2,1)S(1)}, bf16[136,768]{1,0:T(8,128)(2,1)S(1)}, u32[]{:S(2)}, u32[]{:S(2)}) collective-permute-start(bf16[136,768]{1,0:T(8,128)(2,1)S(1)} %output.3), channel_id=1, source_target_pairs={{0,1},{1,0},{2,3},{3,2},{4,5},{5,4},{6,7},{7,6},{8,9},{9,8},{10,11... | collective-permute-start | bytes 626696 | tf_op jit(solution)/shard_map/ppermute | solution.py:619
  96.6 1.3 output.2.own
  97.8 3.2 %collective-permute-done.22.other = bf16[136,768]{1,0:T(8,128)(2,1)S(1)} collective-permute-done((bf16[136,768]{1,0:T(8,128)(2,1)S(1)}, bf16[136,768]{1,0:T(8,128)(2,1)S(1)}, u32[]{:S(2)}, u32[]{:S(2)}) %collective-permute-start.22) | collective-permute-done | bytes 208928 | tf_op jit(solution)/shard_map/ppermute | solution.py:619
  101.1 1.7 %decode_first.1 = (bf16[272,768]{1,0:T(8,128)(2,1)S(1)}, bf16[272,512]{1,0:T(8,128)(2,1)S(1)}) custom-call(s32[3]{0:T(128)S(1)} %pad_add_fusion.ids, f32[136,768]{1,0:T(8,128)S(1)} %output.2.own, bf16[136,768]{1,0:T(8,128)(2,1)S(1)} %collective-permute-done.22.other, bf16[272,768]{1,0:T(8,128)(2,1)S(1)} %get-tuple-element.59.mine.encoded, ...), custom_call_target="tpu_custom_call" | custom-call | flops 1000000 | bytes 10000 | tf_op jit(solution)/shard_map/decode_first/pallas_call | solution.py:481
  102.8 2.9 %collective-permute-start.24 = (bf16[272,512]{1,0:T(8,128)(2,1)S(1)}, bf16[272,512]{1,0:T(8,128)(2,1)S(1)}, u32[]{:S(2)}, u32[]{:S(2)}) collective-permute-start(bf16[272,512]{1,0:T(8,128)(2,1)S(1)} %get-tuple-element.99), channel_id=1, source_target_pairs={{0,1},{1,0},{2,3},{3,2},{4,5},{5,4},{6,7},{7,6},{8,9},{9,8},{10,11... | collective-permute-start | bytes 835592 | tf_op jit(solution)/shard_map/ppermute | solution.py:619
  105.7 1.7 %decode.2 = bf16[272,256]{1,0:T(8,128)(2,1)} custom-call(s32[3]{0:T(128)S(1)} %pad_add_fusion.ids, bf16[272,768]{1,0:T(8,128)(2,1)S(1)} %get-tuple-element.97.inputs, bf16[3,768,1536]{2,1,0:T(8,128)(2,1)S(1)} %bitcast.5), custom_call_target="tpu_custom_call" | custom-call | flops 1000000 | bytes 10000 | tf_op jit(solution)/shard_map/decode/pallas_call | solution.py:499
  107.4 0.7 collective-permute-start.23
  108.1 2.1 %decode.3.own = f32[272,768]{1,0:T(8,128)S(1)} custom-call(s32[3]{0:T(128)S(1)} %pad_add_fusion.ids, bf16[272,768]{1,0:T(8,128)(2,1)S(1)} %get-tuple-element.97.inputs, bf16[3,768,1536]{2,1,0:T(8,128)(2,1)S(1)} %bitcast.5), custom_call_target="tpu_custom_call" | custom-call | flops 1000000 | bytes 10000 | tf_op jit(solution)/shard_map/decode/pallas_call | solution.py:499
  110.2 2.2 %collective-permute-done.24.other = bf16[272,512]{1,0:T(8,128)(2,1)S(1)} collective-permute-done((bf16[272,512]{1,0:T(8,128)(2,1)S(1)}, bf16[272,512]{1,0:T(8,128)(2,1)S(1)}, u32[]{:S(2)}, u32[]{:S(2)}) %collective-permute-start.24) | collective-permute-done | bytes 278560 | tf_op jit(solution)/shard_map/ppermute | solution.py:619
  112.4 1.9 %slopes.2 = (bf16[256,512]{1,0:T(8,128)(2,1)S(1)}, bf16[272,512]{1,0:T(8,128)(2,1)}, f32[128,512]{1,0:T(8,128)S(1)}) custom-call(s32[3]{0:T(128)S(1)} %pad_add_fusion.ids, f32[272,768]{1,0:T(8,128)S(1)} %decode.3.own, bf16[272,512]{1,0:T(8,128)(2,1)S(1)} %collective-permute-done.24.other, bf16[272,768]{1,0:T(8,128)(2,1)S(1)} %get-tuple-element.97.inputs, ...), custom_call_target="tpu_custom_call" | custom-call | flops 417792000000 | bytes 1949696 | tf_op jit(solution)/shard_map/slopes/pallas_call | solution.py:547
  114.4 2.3 %collective-permute-start.26 = (bf16[272,512]{1,0:T(8,128)(2,1)}, bf16[272,512]{1,0:T(8,128)(2,1)}, u32[]{:S(2)}, u32[]{:S(2)}) collective-permute-start(bf16[272,512]{1,0:T(8,128)(2,1)} %get-tuple-element.103.refs_0_), channel_id=1, source_target_pairs={{0,1},{1,0},{2,3},{3,2},{4,5},{5,4},{6,7},{7,6},{8,9},{9,8},{10,11... | collective-permute-start | bytes 835592 | tf_op jit(solution)/shard_map/ppermute | solution.py:619
  116.7 2.0 %slopes.3 = (bf16[256,768]{1,0:T(8,128)(2,1)}, bf16[272,256]{1,0:T(8,128)(2,1)}, f32[128,256]{1,0:T(8,128)S(1)}) custom-call(s32[3]{0:T(128)S(1)} %pad_add_fusion.ids, f32[272,768]{1,0:T(8,128)S(1)} %decode.3.own, bf16[272,256]{1,0:T(8,128)(2,1)} %collective-permute-done.23.other, bf16[272,768]{1,0:T(8,128)(2,1)S(1)} %get-tuple-element.97.inputs, ...), custom_call_target="tpu_custom_call" | custom-call | flops 208896000000 | bytes 974848 | tf_op jit(solution)/shard_map/slopes/pallas_call | solution.py:547
  118.7 1.2 collective-permute-start.25
  119.9 2.7 %backward.3.refs_1_ = f32[128,768]{1,0:T(8,128)S(1)} custom-call(s32[3]{0:T(128)S(1)} %pad_add_fusion.ids, bf16[272,512]{1,0:T(8,128)(2,1)} %get-tuple-element.103.refs_0_, bf16[272,256]{1,0:T(8,128)(2,1)} %get-tuple-element.102.refs_1_, f32[128,512]{1,0:T(8,128)S(1)} %get-tuple-element.104.refs_2_, f32[128,256]{1,0:T(8,128)S(1)} %get-tuple-element.105.refs_3_, ...), custom_call_target="tpu_custom_call" | custom-call | flops 96259276800 | bytes 1253376 | tf_op jit(solution)/shard_map/backward/pallas_call | solution.py:594
  122.6 0.3 collective-permute-done.26.refs_0_
  122.9 2.2 %backward.4.refs_1_ = f32[128,768]{1,0:T(8,128)S(1)} custom-call(s32[3]{0:T(128)S(1)} %pad_add_fusion.ids, bf16[272,512]{1,0:T(8,128)(2,1)} %collective-permute-done.26.refs_0_, f32[128,768]{1,0:T(8,128)S(1)} %backward.3.refs_1_, bf16[3,768,1536]{2,1,0:T(8,128)(2,1)S(1)} %bitcast.5), custom_call_target="tpu_custom_call" | custom-call | flops 64172851200 | bytes 835584 | tf_op jit(solution)/shard_map/backward/pallas_call | solution.py:594
  125.1 0.4 collective-permute-done.25.refs_0_
  125.6 2.1 %backward.5 = bf16[128,768]{1,0:T(8,128)(2,1)} custom-call(s32[3]{0:T(128)S(1)} %pad_add_fusion.ids, bf16[272,256]{1,0:T(8,128)(2,1)} %collective-permute-done.25.refs_0_, f32[128,768]{1,0:T(8,128)S(1)} %backward.4.refs_1_, bf16[3,768,1536]{2,1,0:T(8,128)(2,1)S(1)} %bitcast.5), custom_call_target="tpu_custom_call" | custom-call | flops 32086425600 | bytes 417792 | tf_op jit(solution)/shard_map/backward/pallas_call | solution.py:594
  (36 shorter events, 0.2 us)
Async XLA Ops:
  1.5 6.0 %collective-permute-start = (bf16[8,1664]{1,0:T(8,128)(2,1)S(1)}, bf16[8,1664]{1,0:T(8,128)(2,1)S(1)}, u32[]{:S(2)}, u32[]{:S(2)}) collective-permute-start(bf16[8,1664]{1,0:T(8,128)(2,1)S(1)} %get-tuple-element.55), channel_id=1, source_target_pairs={{0,2},{2,4},{4,6},{6,8},{8,10},{10,12},{12,14},{14,16},{16,18},{18... | collective-permute-start | bytes 79880 | tf_op jit(solution)/shard_map/ppermute | solution.py:643
  2.8 5.0 %collective-permute-start.1 = (bf16[8,1664]{1,0:T(8,128)(2,1)S(1)}, bf16[8,1664]{1,0:T(8,128)(2,1)S(1)}, u32[]{:S(2)}, u32[]{:S(2)}) collective-permute-start(bf16[8,1664]{1,0:T(8,128)(2,1)S(1)} %get-tuple-element.56), channel_id=1, source_target_pairs={{2,0},{4,2},{6,4},{8,6},{10,8},{12,10},{14,12},{16,14},{18,16},{20... | collective-permute-start | bytes 79880 | tf_op jit(solution)/shard_map/ppermute | solution.py:644
  7.8 8.2 %copy-start.3 = (f32[1536]{0:T(1024)S(1)}, f32[1536]{0:T(1024)}, u32[]{:S(2)}) copy-start(f32[1536]{0:T(1024)} %param.12) | copy-start | bytes 18436
  12.5 12.3 %collective-permute-start.2 = (bf16[272,768]{1,0:T(8,128)(2,1)S(1)}, bf16[272,768]{1,0:T(8,128)(2,1)S(1)}, u32[]{:S(2)}, u32[]{:S(2)}) collective-permute-start(bf16[272,768]{1,0:T(8,128)(2,1)S(1)} %get-tuple-element.59.mine.encoded), channel_id=1, source_target_pairs={{0,1},{1,0},{2,3},{3,2},{4,5},{5,4},{6,7},{7,6},{8,9},{9,8},{10,11... | collective-permute-start | bytes 1253384 | tf_op jit(solution)/shard_map/ppermute | solution.py:619
  24.8 37.3 %copy-start.2 = (f32[4]{0:T(128)S(1)}, f32[4]{0:T(128)}, u32[]{:S(2)}) copy-start(f32[4]{0:T(128)} %scale.5) | copy-start | bytes 52
  26.8 10.1 %collective-permute-start.3 = (bf16[128,384]{1,0:T(8,128)(2,1)S(1)}, bf16[128,384]{1,0:T(8,128)(2,1)S(1)}, u32[]{:S(2)}, u32[]{:S(2)}) collective-permute-start(bf16[128,384]{1,0:T(8,128)(2,1)S(1)} %get-tuple-element.61), channel_id=1, source_target_pairs={{0,32},{2,34},{4,36},{6,38},{8,40},{10,42},{12,44},{14,46},{16,48}... | collective-permute-start | bytes 294920 | tf_op jit(solution)/shard_map/ppermute | solution.py:623
  32.0 4.9 %collective-permute-start.7 = (bf16[128,384]{1,0:T(8,128)(2,1)S(1)}, bf16[128,384]{1,0:T(8,128)(2,1)S(1)}, u32[]{:S(2)}, u32[]{:S(2)}) collective-permute-start(bf16[128,384]{1,0:T(8,128)(2,1)S(1)} %get-tuple-element.74), channel_id=1, source_target_pairs={{0,96},{2,98},{4,100},{6,102},{8,104},{10,106},{12,108},{14,110},{... | collective-permute-start | bytes 294920 | tf_op jit(solution)/shard_map/ppermute | solution.py:623
  33.3 6.1 %collective-permute-start.8 = (bf16[128,384]{1,0:T(8,128)(2,1)S(1)}, bf16[128,384]{1,0:T(8,128)(2,1)S(1)}, u32[]{:S(2)}, u32[]{:S(2)}) collective-permute-start(bf16[128,384]{1,0:T(8,128)(2,1)S(1)} %get-tuple-element.75), channel_id=1, source_target_pairs={{0,64},{2,66},{4,68},{6,70},{8,72},{10,74},{12,76},{14,78},{16,80}... | collective-permute-start | bytes 294920 | tf_op jit(solution)/shard_map/ppermute | solution.py:623
  40.7 8.5 %collective-permute-start.4 = (bf16[136,256]{1,0:T(8,128)(2,1)S(1)}, bf16[136,256]{1,0:T(8,128)(2,1)S(1)}, u32[]{:S(2)}, u32[]{:S(2)}) collective-permute-start(bf16[136,256]{1,0:T(8,128)(2,1)S(1)} %get-tuple-element.65), channel_id=1, source_target_pairs={{0,32},{2,34},{4,36},{6,38},{8,40},{10,42},{12,44},{14,46},{16,48}... | collective-permute-start | bytes 208904 | tf_op jit(solution)/shard_map/ppermute | solution.py:623
  41.5 7.8 %collective-permute-start.5 = (bf16[136,256]{1,0:T(8,128)(2,1)S(1)}, bf16[136,256]{1,0:T(8,128)(2,1)S(1)}, u32[]{:S(2)}, u32[]{:S(2)}) collective-permute-start(bf16[136,256]{1,0:T(8,128)(2,1)S(1)} %get-tuple-element.66), channel_id=1, source_target_pairs={{0,96},{2,98},{4,100},{6,102},{8,104},{10,106},{12,108},{14,110},{... | collective-permute-start | bytes 208904 | tf_op jit(solution)/shard_map/ppermute | solution.py:623
  44.0 5.8 %collective-permute-start.6 = (bf16[136,256]{1,0:T(8,128)(2,1)S(1)}, bf16[136,256]{1,0:T(8,128)(2,1)S(1)}, u32[]{:S(2)}, u32[]{:S(2)}) collective-permute-start(bf16[136,256]{1,0:T(8,128)(2,1)S(1)} %get-tuple-element.67), channel_id=1, source_target_pairs={{0,64},{2,66},{4,68},{6,70},{8,72},{10,74},{12,76},{14,78},{16,80}... | collective-permute-start | bytes 208904 | tf_op jit(solution)/shard_map/ppermute | solution.py:623
  45.2 12.2 %collective-permute-start.10 = (bf16[512,384]{1,0:T(8,128)(2,1)S(1)}, bf16[512,384]{1,0:T(8,128)(2,1)S(1)}, u32[]{:S(2)}, u32[]{:S(2)}) collective-permute-start(bf16[512,384]{1,0:T(8,128)(2,1)S(1)} %constant_dynamic-update-slice_fusion.4.refs_0_), channel_id=1, source_target_pairs={{0,24},{2,26},{4,28},{6,30},{8,0},{10,2},{12,4},{14,6},{16,8},{18,... | collective-permute-start | bytes 1179656 | tf_op jit(solution)/shard_map/ppermute | solution.py:623
  49.2 9.0 %collective-permute-start.9 = (bf16[512,384]{1,0:T(8,128)(2,1)S(1)}, bf16[512,384]{1,0:T(8,128)(2,1)S(1)}, u32[]{:S(2)}, u32[]{:S(2)}) collective-permute-start(bf16[512,384]{1,0:T(8,128)(2,1)S(1)} %constant_dynamic-update-slice_fusion.4.refs_0_), channel_id=1, source_target_pairs={{0,8},{2,10},{4,12},{6,14},{8,16},{10,18},{12,20},{14,22},{16,24},... | collective-permute-start | bytes 1179656 | tf_op jit(solution)/shard_map/ppermute | solution.py:623
  49.9 7.5 %collective-permute-start.11 = (bf16[544,256]{1,0:T(8,128)(2,1)S(1)}, bf16[544,256]{1,0:T(8,128)(2,1)S(1)}, u32[]{:S(2)}, u32[]{:S(2)}) collective-permute-start(bf16[544,256]{1,0:T(8,128)(2,1)S(1)} %constant_dynamic-update-slice_fusion.queries), channel_id=1, source_target_pairs={{0,4},{2,6},{4,0},{6,2},{8,12},{10,14},{12,8},{14,10},{16,20},{18,... | collective-permute-start | bytes 835592 | tf_op jit(solution)/shard_map/ppermute | solution.py:623
  52.9 9.2 %collective-permute-start.12 = (bf16[512,384]{1,0:T(8,128)(2,1)S(1)}, bf16[512,384]{1,0:T(8,128)(2,1)S(1)}, u32[]{:S(2)}, u32[]{:S(2)}) collective-permute-start(bf16[512,384]{1,0:T(8,128)(2,1)S(1)} %constant_dynamic-update-slice_fusion.4.refs_0_), channel_id=1, source_target_pairs={{0,2},{2,0},{4,6},{6,4},{8,10},{10,8},{12,14},{14,12},{16,18},{18,... | collective-permute-start | bytes 1179656 | tf_op jit(solution)/shard_map/ppermute | solution.py:623
  58.2 3.9 %collective-permute-start.13 = (bf16[512,384]{1,0:T(8,128)(2,1)S(1)}, bf16[512,384]{1,0:T(8,128)(2,1)S(1)}, u32[]{:S(2)}, u32[]{:S(2)}) collective-permute-start(bf16[512,384]{1,0:T(8,128)(2,1)S(1)} %collective-permute-done.9.refs_1_), channel_id=1, source_target_pairs={{0,2},{2,0},{4,6},{6,4},{8,10},{10,8},{12,14},{14,12},{16,18},{18,... | collective-permute-start | bytes 1179656 | tf_op jit(solution)/shard_map/ppermute | solution.py:623
  58.2 3.9 %collective-permute-start.14 = (bf16[512,384]{1,0:T(8,128)(2,1)S(1)}, bf16[512,384]{1,0:T(8,128)(2,1)S(1)}, u32[]{:S(2)}, u32[]{:S(2)}) collective-permute-start(bf16[512,384]{1,0:T(8,128)(2,1)S(1)} %collective-permute-done.10.refs_2_), channel_id=1, source_target_pairs={{0,2},{2,0},{4,6},{6,4},{8,10},{10,8},{12,14},{14,12},{16,18},{18,... | collective-permute-start | bytes 1179656 | tf_op jit(solution)/shard_map/ppermute | solution.py:623
  58.8 8.3 %collective-permute-start.15 = (bf16[256,384]{1,0:T(8,128)(2,1)S(1)}, bf16[256,384]{1,0:T(8,128)(2,1)S(1)}, u32[]{:S(2)}, u32[]{:S(2)}) collective-permute-start(bf16[256,384]{1,0:T(8,128)(2,1)S(1)} %slice.6), channel_id=1, source_target_pairs={{0,8},{2,10},{4,12},{6,14},{8,16},{10,18},{12,20},{14,22},{16,24},... | collective-permute-start | bytes 589832 | tf_op jit(solution)/shard_map/ppermute | solution.py:623
  60.0 7.1 %collective-permute-start.16 = (bf16[256,384]{1,0:T(8,128)(2,1)S(1)}, bf16[256,384]{1,0:T(8,128)(2,1)S(1)}, u32[]{:S(2)}, u32[]{:S(2)}) collective-permute-start(bf16[256,384]{1,0:T(8,128)(2,1)S(1)} %slice.7), channel_id=1, source_target_pairs={{0,24},{2,26},{4,28},{6,30},{8,0},{10,2},{12,4},{14,6},{16,8},{18,... | collective-permute-start | bytes 589832 | tf_op jit(solution)/shard_map/ppermute | solution.py:623
  66.2 26.1 %copy-start = (bf16[768,1536]{1,0:T(8,128)(2,1)S(1)}, bf16[768,1536]{1,0:T(8,128)(2,1)}, u32[]{:S(2)}) copy-start(bf16[768,1536]{1,0:T(8,128)(2,1)} %weight.6) | copy-start | bytes 7077892
  67.1 2.0 %collective-permute-start.17 = (bf16[512,384]{1,0:T(8,128)(2,1)S(1)}, bf16[512,384]{1,0:T(8,128)(2,1)S(1)}, u32[]{:S(2)}, u32[]{:S(2)}) collective-permute-start(bf16[512,384]{1,0:T(8,128)(2,1)S(1)} %constant_dynamic-update-slice_fusion.8.refs_0_.refs_6_), channel_id=1, source_target_pairs={{0,2},{2,0},{4,6},{6,4},{8,10},{10,8},{12,14},{14,12},{16,18},{18,... | collective-permute-start | bytes 1179656 | tf_op jit(solution)/shard_map/ppermute | solution.py:623
  73.2 9.9 %collective-permute-start.18 = (bf16[544,256]{1,0:T(8,128)(2,1)S(1)}, bf16[544,256]{1,0:T(8,128)(2,1)S(1)}, u32[]{:S(2)}, u32[]{:S(2)}) collective-permute-start(bf16[544,256]{1,0:T(8,128)(2,1)S(1)} %get-tuple-element.91), channel_id=1, source_target_pairs={{0,4},{2,6},{4,0},{6,2},{8,12},{10,14},{12,8},{14,10},{16,20},{18,... | collective-permute-start | bytes 835592 | tf_op jit(solution)/shard_map/ppermute | solution.py:623
  76.1 25.0 %slice-start = ((s8[7077888]{0:T(1024)(128)(4,1)}), s8[4194304]{0:T(1024)(128)(4,1)S(1)}, s32[]{:S(2)}) async-start(s8[7077888]{0:T(1024)(128)(4,1)} %bitcast.4), calls=%async_computation | async-start | bytes 8388608
  76.1 25.0 %slice-start.1 = ((s8[7077888]{0:T(1024)(128)(4,1)}), s8[2883584]{0:T(1024)(128)(4,1)S(1)}, s32[]{:S(2)}) async-start(s8[7077888]{0:T(1024)(128)(4,1)} %bitcast.4), calls=%async_computation.1 | async-start | bytes 5767168
  83.6 4.7 %collective-permute-start.19 = (bf16[136,256]{1,0:T(8,128)(2,1)S(1)}, bf16[136,256]{1,0:T(8,128)(2,1)S(1)}, u32[]{:S(2)}, u32[]{:S(2)}) collective-permute-start(bf16[136,256]{1,0:T(8,128)(2,1)S(1)} %get-tuple-element.93), channel_id=1, source_target_pairs={{0,96},{2,98},{4,100},{6,102},{8,104},{10,106},{12,108},{14,110},{... | collective-permute-start | bytes 208904 | tf_op jit(solution)/shard_map/ppermute | solution.py:623
  85.0 6.0 %collective-permute-start.20 = (bf16[136,256]{1,0:T(8,128)(2,1)S(1)}, bf16[136,256]{1,0:T(8,128)(2,1)S(1)}, u32[]{:S(2)}, u32[]{:S(2)}) collective-permute-start(bf16[136,256]{1,0:T(8,128)(2,1)S(1)} %get-tuple-element.94), channel_id=1, source_target_pairs={{0,64},{2,66},{4,68},{6,70},{8,72},{10,74},{12,76},{14,78},{16,80}... | collective-permute-start | bytes 208904 | tf_op jit(solution)/shard_map/ppermute | solution.py:623
  86.9 5.5 %collective-permute-start.21 = (bf16[136,256]{1,0:T(8,128)(2,1)S(1)}, bf16[136,256]{1,0:T(8,128)(2,1)S(1)}, u32[]{:S(2)}, u32[]{:S(2)}) collective-permute-start(bf16[136,256]{1,0:T(8,128)(2,1)S(1)} %get-tuple-element.95), channel_id=1, source_target_pairs={{0,32},{2,34},{4,36},{6,38},{8,40},{10,42},{12,44},{14,46},{16,48}... | collective-permute-start | bytes 208904 | tf_op jit(solution)/shard_map/ppermute | solution.py:623
  93.7 7.4 %collective-permute-start.22 = (bf16[136,768]{1,0:T(8,128)(2,1)S(1)}, bf16[136,768]{1,0:T(8,128)(2,1)S(1)}, u32[]{:S(2)}, u32[]{:S(2)}) collective-permute-start(bf16[136,768]{1,0:T(8,128)(2,1)S(1)} %output.3), channel_id=1, source_target_pairs={{0,1},{1,0},{2,3},{3,2},{4,5},{5,4},{6,7},{7,6},{8,9},{9,8},{10,11... | collective-permute-start | bytes 626696 | tf_op jit(solution)/shard_map/ppermute | solution.py:619
  102.8 9.6 %collective-permute-start.24 = (bf16[272,512]{1,0:T(8,128)(2,1)S(1)}, bf16[272,512]{1,0:T(8,128)(2,1)S(1)}, u32[]{:S(2)}, u32[]{:S(2)}) collective-permute-start(bf16[272,512]{1,0:T(8,128)(2,1)S(1)} %get-tuple-element.99), channel_id=1, source_target_pairs={{0,1},{1,0},{2,3},{3,2},{4,5},{5,4},{6,7},{7,6},{8,9},{9,8},{10,11... | collective-permute-start | bytes 835592 | tf_op jit(solution)/shard_map/ppermute | solution.py:619
  105.7 6.7 %copy-start.1 = (bf16[256,1536]{1,0:T(8,128)(2,1)S(1)}, bf16[256,1536]{1,0:T(8,128)(2,1)}, u32[]{:S(2)}) copy-start(bf16[256,1536]{1,0:T(8,128)(2,1)} %grad.5) | copy-start | bytes 2359300
  107.4 9.3 %collective-permute-start.23 = (bf16[272,256]{1,0:T(8,128)(2,1)}, bf16[272,256]{1,0:T(8,128)(2,1)}, u32[]{:S(2)}, u32[]{:S(2)}) collective-permute-start(bf16[272,256]{1,0:T(8,128)(2,1)} %decode.2), channel_id=1, source_target_pairs={{0,1},{1,0},{2,3},{3,2},{4,5},{5,4},{6,7},{7,6},{8,9},{9,8},{10,11... | collective-permute-start | bytes 417800 | tf_op jit(solution)/shard_map/ppermute | solution.py:619
  114.4 8.6 %collective-permute-start.26 = (bf16[272,512]{1,0:T(8,128)(2,1)}, bf16[272,512]{1,0:T(8,128)(2,1)}, u32[]{:S(2)}, u32[]{:S(2)}) collective-permute-start(bf16[272,512]{1,0:T(8,128)(2,1)} %get-tuple-element.103.refs_0_), channel_id=1, source_target_pairs={{0,1},{1,0},{2,3},{3,2},{4,5},{5,4},{6,7},{7,6},{8,9},{9,8},{10,11... | collective-permute-start | bytes 835592 | tf_op jit(solution)/shard_map/ppermute | solution.py:619
  118.7 6.9 %collective-permute-start.25 = (bf16[272,256]{1,0:T(8,128)(2,1)}, bf16[272,256]{1,0:T(8,128)(2,1)}, u32[]{:S(2)}, u32[]{:S(2)}) collective-permute-start(bf16[272,256]{1,0:T(8,128)(2,1)} %get-tuple-element.102.refs_1_), channel_id=1, source_target_pairs={{0,1},{1,0},{2,3},{3,2},{4,5},{5,4},{6,7},{7,6},{8,9},{9,8},{10,11... | collective-permute-start | bytes 417800 | tf_op jit(solution)/shard_map/ppermute | solution.py:619

commit v8 on v7

--- a/solution.py
+++ b/solution.py
@@ -72,7 +72,7 @@
     return jnp.concatenate([even, odd], axis=0)
 
 
-def prepare_kernel(bases, grad, codes, last, first, code, head, tail, sems):
+def prepare_kernel(ids, bases, grad, codes, near, far, code, head, tail, sems):
     rows = grad.shape[0]
     copies = [
         pltpu.make_async_copy(bases, code, sems.at[0]),
@@ -86,10 +86,11 @@
     feats = grad.shape[1]
     letters = (code[...] + 1).astype(F32)
     codes[...] = letters.astype(BF16)
-    last[:, :feats] = tail[...].astype(F32)[8:].astype(BF16)
-    last[:, feats:] = letters[OWN - 8 :].astype(BF16)
-    first[:, :feats] = head[...].astype(F32)[:8].astype(BF16)
-    first[:, feats:] = letters[:8].astype(BF16)
+    odd = lax.rem(ids[2], 2) == 1
+    last = jnp.concatenate([tail[...].astype(F32)[8:], letters[OWN - 8 :]], axis=1)
+    first = jnp.concatenate([head[...].astype(F32)[:8], letters[:8]], axis=1)
+    near[...] = jnp.where(odd, first, last).astype(BF16)
+    far[...] = jnp.where(odd, last, first).astype(BF16)
 
 
 def near_memory(value):
@@ -100,11 +101,11 @@
     return pltpu.with_memory_space_constraint(value, pltpu.HBM)
 
 
-def prepare(bases, grad):
+def prepare(ids, bases, grad):
     feats = grad.shape[1]
     return pl.pallas_call(
         prepare_kernel,
-        in_specs=[HBM, HBM],
+        in_specs=[SM, HBM, HBM],
         out_specs=[VM] * 3,
         out_shape=[
             shape((OWN, 128), BF16),
@@ -120,7 +121,7 @@
         compiler_params=params(4),
         cost_estimate=cost(10**5, 10**5),
         name="prepare",
-    )(far_memory(bases), far_memory(grad))
+    )(ids, far_memory(bases), far_memory(grad))
 
 
 def load_kernel(*refs):
@@ -294,18 +295,22 @@
     def keys(ref):
         return jnp.concatenate([ref[:, :128], ref[:, 256:]], axis=1)
 
-    if not known:
+    total_known = sum(ref.shape[1] for ref in inverses)
+    if total_known < sum(sizes):
         outs, inverse = refs[:-1], refs[-1]
         lane = lax.broadcasted_iota(jnp.int32, (8, 256), 1)
         ones = (lane < HEAD).astype(F32).astype(BF16)
         for at, size, ref in zip(starts, sizes, pieces):
+            if at < total_known:
+                continue
             key = keys(ref).astype(F32)
             square = key * key
             high = square.astype(BF16)
             rest = (square - high.astype(F32)).astype(BF16)
             total = dot_t(ones, high) + dot_t(ones, rest)
+            at -= total_known
             inverse[:, at : at + size] = lax.rsqrt(total * (1.0 / HEAD) + EPS)
-        inverses = (inverse,)
+        inverses = (*inverses, inverse)
     else:
         outs = refs
 
@@ -315,7 +320,7 @@
                 return ref[0:1, at : at + size]
             at -= ref.shape[1]
 
-    limit = min(1024, starts[-1])
+    limit = 1024
     groups, room = [], 0
     for triple in zip(starts, sizes, pieces):
         if room < triple[1]:
@@ -381,8 +386,9 @@
         outs = [shape((rows, 256), BF16)]
     else:
         outs = [shape((rows, 256), F32), shape((rows, 128), F32)]
-    if not inverses:
-        outs.append(shape((8, keys), F32))
+    known = sum(inverse.shape[1] for inverse in inverses)
+    if known < keys:
+        outs.append(shape((8, keys - known), F32))
     return pl.pallas_call(
         functools.partial(attend_kernel, len(pieces), len(inverses), bool(state), final),
         in_specs=[SM, SM] + [VM] * (1 + len(pieces) + len(inverses) + len(state)),
@@ -639,9 +645,13 @@
     ids = jnp.stack([lax.axis_index("head"), x, at]).astype(jnp.int32)
     feats = grad_out.shape[1]
 
-    codes, last, first = prepare(dna_bases.reshape(OWN, 128), grad_out)
-    before = lax.ppermute(last, "seq", [(i, i + 1) for i in range(63)])
-    after = lax.ppermute(first, "seq", [(i + 1, i) for i in range(63)])
+    codes, near, far = prepare(ids, dna_bases.reshape(OWN, 128), grad_out)
+    near = send(near, dc=1)
+    pairs = [(i, i + 1) for i in range(1, 63, 2)]
+    far = lax.ppermute(far, "seq", pairs + [(b, a) for a, b in pairs])
+    odd = at % 2 == 1
+    before = jnp.where(odd, near, far)
+    after = jnp.where(odd, far, near)
     stem_weight, encoder_weight = load(stem_weight, encoder_weight)
     encoded, attention_weight = encode(
         ids, codes, before, after, stem_weight, encoder_weight, attention_weight
@@ -655,26 +665,22 @@
     def stacked(blocks):
         return jnp.concatenate(lax.optimization_barrier(blocks), axis=0)
 
-    got = spread(keyvals)
-    got[0], normed = lax.optimization_barrier((got[0], normed))
+    keyvals = stacked([keyvals[0]] + spread(keyvals))
+    near = [send(keyvals, dz=1), send(keyvals, dz=3)]
+    beside, normed = lax.optimization_barrier((send(keyvals, dc=1), normed))
     queries = project_queries(ids, normed, attention_weight)
-    others = spread(queries)
-    keyvals = stacked([keyvals[0]] + got)
-    near = [send(keyvals, dz=1), send(keyvals, dz=3)]
-    queries = stacked([queries[0]] + others)
+    *near, got1, got3, got2 = lax.optimization_barrier((*near, *spread(queries)))
+    queries = jnp.concatenate([queries[0], got1, got3, got2], axis=0)
     others = send(queries, dy=1)
-    near[0], near[1], others = lax.optimization_barrier((near[0], near[1], others))
     half = keyvals.shape[0] // 2
     far = [send(near[0][:half], dz=1), send(near[1][half:], dz=3)]
-    pieces = [keyvals] + near
-    pieces += [send(piece, dc=1) for piece in pieces]
-    *state, inverse = attend(ids, logit_scale, others, pieces, final=False)
-    *far, state[0], state[1] = lax.optimization_barrier((*far, *state))
+    across = [send(piece, dc=1) for piece in near]
+    *far, across[0], across[1], others = lax.optimization_barrier((*far, *across, others))
     far = jnp.concatenate(far, axis=0)
-    late = [far, send(far, dc=1)]
-    other, later = attend(ids, logit_scale, others, late, state=state)
+    pieces = [keyvals, beside] + near + across + [far, send(far, dc=1)]
+    other, inverse = attend(ids, logit_scale, others, pieces)
     other = send(other, dy=1)
-    own = attend(ids, logit_scale, queries, pieces + late, inverses=[inverse, later])[0]
+    own = attend(ids, logit_scale, queries, pieces, inverses=[inverse])[0]
     mixed = merge([own, other])
     heads = [mixed[0], send(mixed[1], dx=-1), send(mixed[3], dx=-2), send(mixed[2], dx=-3)]
 

time: 128 us -> 129 us (level)
  starting transfers between devices: 47.5 us -> 41.1 us
  local copies, waits for them, and re-layouts: 0.22 us -> 6.06 us
  waiting for transfers between devices: 34.8 us -> 38 us
  Pallas kernels: 44.2 us -> 42.8 us
    unnamed x19 -> x23, local copies, waits for them, and re-layouts: 0.11 us -> 5.95 us
    ppermute x19 -> x20, starting transfers between devices: 31.3 us -> 26.4 us  [send(): return lax.ppermute(value, 'seq', moves(**step))]
    ppermute x19 -> x20, waiting for transfers between devices: 19.5 us -> 24.1 us  [send(): return lax.ppermute(value, 'seq', moves(**step))]
    ppermute x2 -> x1, starting transfers between devices: 2.58 us -> 0.66 us  [per_device(): far = lax.ppermute(far, 'seq', pairs + [(b, a) for a, b in pairs])]
    pallas_call x3 -> x2, Pallas kernels: 12.5 us -> 10.6 us  [attend(): pl.pallas_call(functools.partial(attend_kernel, len(pieces), len(inverses...]
  transfers between devices with their start and end apart: 27 -> 27, of which waited for: 17 -> 15; matrix products, arithmetic and copies ran while one was open for 0% -> 0% of each run, Pallas kernels for 20% -> 18%
where the time goes in v8:
time: 129 us
  Pallas kernels  42.8 us (33%)
  starting transfers between devices  41.1 us (32%)
  waiting for transfers between devices  38 us (29%)
  local copies, waits for them, and re-layouts  6.06 us (5%)
    ppermute x20, starting transfers between devices, send(): return lax.ppermute(value, 'seq', moves(**step))  26.4 us
    ppermute x20, waiting for transfers between devices, send(): return lax.ppermute(value, 'seq', moves(**step))  24.1 us
    ppermute x6, starting transfers between devices, swap(): return lax.ppermute(value, 'head', [(0, 1), (1, 0)])  14 us
    ppermute x6, waiting for transfers between devices, swap(): return lax.ppermute(value, 'head', [(0, 1), (1, 0)])  13.9 us
    pallas_call x2, Pallas kernels, attend(): pl.pallas_call(functools.partial(attend_kernel, len(pieces), len(inverses...  10.6 us
    pallas_call x3, Pallas kernels, backward(): pl.pallas_call(functools.partial(backward_kernel, mine, [first for first,...  7.02 us
    unnamed x23, local copies, waits for them, and re-layouts  5.95 us
    pallas_call x1, Pallas kernels, encode(): pl.pallas_call(encode_kernel, in_specs=[SM] + [VM] * 5 + [HBM], out_specs...  4.64 us
  transfers between devices with their start and end apart: 27, of which 15 were waited for; matrix products, arithmetic and copies ran while one was open for 0% of the time, Pallas kernels for 18%

profile of v8, /device:TPU:0, one launch (start us, length us, event | category | flops | bytes accessed | tf_op | source)
XLA Modules:
  0.0 129.0 jit_solution(1191963621797725454)
XLA Ops:
  0.6 0.1 pad_add_fusion.ids
  0.7 1.4 %prepare.1 = (bf16[128,128]{1,0:T(8,128)(2,1)S(1)}, bf16[8,1664]{1,0:T(8,128)(2,1)S(1)}, bf16[8,1664]{1,0:T(8,128)(2,1)S(1)}) custom-call(s32[3]{0:T(128)S(1)} %pad_add_fusion.ids, s32[128,128]{1,0:T(8,128)} %bitcast.6, bf16[256,1536]{1,0:T(8,128)(2,1)} %grad.5), custom_call_target="tpu_custom_call" | custom-call | flops 100000 | bytes 100000 | tf_op jit(solution)/shard_map/prepare/pallas_call | solution.py:106
  2.2 0.1 collective-permute-start
  2.3 0.7 collective-permute-start.1
  2.9 3.3 %load.1 = (bf16[256,1536]{1,0:T(8,128)(2,1)S(1)}, bf16[3,1536,768]{2,1,0:T(8,128)(2,1)S(1)}) custom-call(bf16[256,1536]{1,0:T(8,128)(2,1)} %refs_0_.1, bf16[3,1536,768]{2,1,0:T(8,128)(2,1)} %refs_1_.1), custom_call_target="tpu_custom_call" | custom-call | flops 100000 | bytes 7864320 | tf_op jit(solution)/shard_map/load/pallas_call | solution.py:141
  6.2 2.8 %copy-done.1 = bf16[3,1536,768]{2,1,0:T(8,128)(2,1)} copy-done((bf16[3,1536,768]{2,1,0:T(8,128)(2,1)}, bf16[3,1536,768]{2,1,0:T(8,128)(2,1)S(1)}, u32[]{:S(2)}) %copy-start.1) | copy-done | bytes 7077912
  9.1 3.0 %copy-done.2 = bf16[3,1536,768]{2,1,0:T(8,128)(2,1)S(1)} copy-done((bf16[3,1536,768]{2,1,0:T(8,128)(2,1)S(1)}, bf16[3,1536,768]{2,1,0:T(8,128)(2,1)}, u32[]{:S(2)}) %copy-start.2) | copy-done | bytes 7077912
  12.1 4.6 %encode.1 = (bf16[272,768]{1,0:T(8,128)(2,1)S(1)}, bf16[3,1536,768]{2,1,0:T(8,128)(2,1)S(1)}) custom-call(s32[3]{0:T(128)S(1)} %pad_add_fusion.ids, bf16[128,128]{1,0:T(8,128)(2,1)S(1)} %get-tuple-element.50.codes, bf16[8,1664]{1,0:T(8,128)(2,1)S(1)} %get-tuple-element.99.before, bf16[8,1664]{1,0:T(8,128)(2,1)S(1)} %get-tuple-element.98.after, ...), custom_call_target="tpu_custom_call" | custom-call | flops 1925185536 | bytes 14155776 | tf_op jit(solution)/shard_map/encode/pallas_call | solution.py:191
  16.8 3.4 %collective-permute-start.2 = (bf16[272,768]{1,0:T(8,128)(2,1)S(1)}, bf16[272,768]{1,0:T(8,128)(2,1)S(1)}, u32[]{:S(2)}, u32[]{:S(2)}) collective-permute-start(bf16[272,768]{1,0:T(8,128)(2,1)S(1)} %get-tuple-element.55.mine.encoded), channel_id=1, source_target_pairs={{0,1},{1,0},{2,3},{3,2},{4,5},{5,4},{6,7},{7,6},{8,9},{9,8},{10,11... | collective-permute-start | bytes 1253384 | tf_op jit(solution)/shard_map/ppermute | solution.py:625
  20.1 8.6 %collective-permute-done.2.theirs = bf16[272,768]{1,0:T(8,128)(2,1)S(1)} collective-permute-done((bf16[272,768]{1,0:T(8,128)(2,1)S(1)}, bf16[272,768]{1,0:T(8,128)(2,1)S(1)}, u32[]{:S(2)}, u32[]{:S(2)}) %collective-permute-start.2) | collective-permute-done | bytes 417824 | tf_op jit(solution)/shard_map/ppermute | solution.py:625
  28.7 2.0 %project_keys.1 = (bf16[2,136,768]{2,1,0:T(8,128)(2,1)S(1)}, bf16[128,384]{1,0:T(8,128)(2,1)S(1)}, bf16[128,384]{1,0:T(8,128)(2,1)S(1)}, bf16[128,384]{1,0:T(8,128)(2,1)S(1)}, bf16[128,384]{1,0:T(8,128)(2,1)S(1)}) custom-call(s32[3]{0:T(128)S(1)} %pad_add_fusion.ids, bf16[272,768]{1,0:T(8,128)(2,1)S(1)} %get-tuple-element.55.mine.encoded, ...), custom_call_target="tpu_custom_call" | custom-call | flops 641728512 | bytes 7077888 | tf_op jit(solution)/shard_map/project_keys/pallas_call | solution.py:243
  30.8 0.0 copy-start.4
  30.8 5.7 %collective-permute-start.3 = (bf16[128,384]{1,0:T(8,128)(2,1)S(1)}, bf16[128,384]{1,0:T(8,128)(2,1)S(1)}, u32[]{:S(2)}, u32[]{:S(2)}) collective-permute-start(bf16[128,384]{1,0:T(8,128)(2,1)S(1)} %get-tuple-element.58), channel_id=1, source_target_pairs={{0,32},{2,34},{4,36},{6,38},{8,40},{10,42},{12,44},{14,46},{16,48}... | collective-permute-start | bytes 294920 | tf_op jit(solution)/shard_map/ppermute | solution.py:629
  36.5 1.6 %collective-permute-start.4 = (bf16[128,384]{1,0:T(8,128)(2,1)S(1)}, bf16[128,384]{1,0:T(8,128)(2,1)S(1)}, u32[]{:S(2)}, u32[]{:S(2)}) collective-permute-start(bf16[128,384]{1,0:T(8,128)(2,1)S(1)} %get-tuple-element.59), channel_id=1, source_target_pairs={{0,96},{2,98},{4,100},{6,102},{8,104},{10,106},{12,108},{14,110},{... | collective-permute-start | bytes 294920 | tf_op jit(solution)/shard_map/ppermute | solution.py:629
  38.1 2.0 %collective-permute-start.5 = (bf16[128,384]{1,0:T(8,128)(2,1)S(1)}, bf16[128,384]{1,0:T(8,128)(2,1)S(1)}, u32[]{:S(2)}, u32[]{:S(2)}) collective-permute-start(bf16[128,384]{1,0:T(8,128)(2,1)S(1)} %get-tuple-element.60), channel_id=1, source_target_pairs={{0,64},{2,66},{4,68},{6,70},{8,72},{10,74},{12,76},{14,78},{16,80}... | collective-permute-start | bytes 294920 | tf_op jit(solution)/shard_map/ppermute | solution.py:629
  40.1 1.6 %collective-permute-done.3 = bf16[128,384]{1,0:T(8,128)(2,1)S(1)} collective-permute-done((bf16[128,384]{1,0:T(8,128)(2,1)S(1)}, bf16[128,384]{1,0:T(8,128)(2,1)S(1)}, u32[]{:S(2)}, u32[]{:S(2)}) %collective-permute-start.3) | collective-permute-done | bytes 98336 | tf_op jit(solution)/shard_map/ppermute | solution.py:629
  41.7 2.6 %collective-permute-done.5 = bf16[128,384]{1,0:T(8,128)(2,1)S(1)} collective-permute-done((bf16[128,384]{1,0:T(8,128)(2,1)S(1)}, bf16[128,384]{1,0:T(8,128)(2,1)S(1)}, u32[]{:S(2)}, u32[]{:S(2)}) %collective-permute-start.5) | collective-permute-done | bytes 98336 | tf_op jit(solution)/shard_map/ppermute | solution.py:629
  44.3 0.1 collective-permute-start.6
  44.4 2.2 %collective-permute-start.7 = (bf16[512,384]{1,0:T(8,128)(2,1)S(1)}, bf16[512,384]{1,0:T(8,128)(2,1)S(1)}, u32[]{:S(2)}, u32[]{:S(2)}) collective-permute-start(bf16[512,384]{1,0:T(8,128)(2,1)S(1)} %constant_dynamic-update-slice_fusion.refs_0_), channel_id=1, source_target_pairs={{0,8},{2,10},{4,12},{6,14},{8,16},{10,18},{12,20},{14,22},{16,24},... | collective-permute-start | bytes 1179656 | tf_op jit(solution)/shard_map/ppermute | solution.py:629
  46.6 2.2 %collective-permute-start.8 = (bf16[512,384]{1,0:T(8,128)(2,1)S(1)}, bf16[512,384]{1,0:T(8,128)(2,1)S(1)}, u32[]{:S(2)}, u32[]{:S(2)}) collective-permute-start(bf16[512,384]{1,0:T(8,128)(2,1)S(1)} %constant_dynamic-update-slice_fusion.refs_0_), channel_id=1, source_target_pairs={{0,24},{2,26},{4,28},{6,30},{8,0},{10,2},{12,4},{14,6},{16,8},{18,... | collective-permute-start | bytes 1179656 | tf_op jit(solution)/shard_map/ppermute | solution.py:629
  48.8 1.3 project_queries.1
  50.0 1.7 %collective-permute-start.10 = (bf16[136,256]{1,0:T(8,128)(2,1)S(1)}, bf16[136,256]{1,0:T(8,128)(2,1)S(1)}, u32[]{:S(2)}, u32[]{:S(2)}) collective-permute-start(bf16[136,256]{1,0:T(8,128)(2,1)S(1)} %get-tuple-element.69), channel_id=1, source_target_pairs={{0,96},{2,98},{4,100},{6,102},{8,104},{10,106},{12,108},{14,110},{... | collective-permute-start | bytes 208904 | tf_op jit(solution)/shard_map/ppermute | solution.py:629
  51.8 0.7 collective-permute-start.11
  52.5 0.9 collective-permute-start.9
  53.4 5.0 %collective-permute-done.7.refs_2_ = bf16[512,384]{1,0:T(8,128)(2,1)S(1)} collective-permute-done((bf16[512,384]{1,0:T(8,128)(2,1)S(1)}, bf16[512,384]{1,0:T(8,128)(2,1)S(1)}, u32[]{:S(2)}, u32[]{:S(2)}) %collective-permute-start.7) | collective-permute-done | bytes 393248 | tf_op jit(solution)/shard_map/ppermute | solution.py:629
  58.4 0.2 collective-permute-done.9
  58.6 0.5 collective-permute-start.15
  59.2 0.7 collective-permute-start.16
  60.0 1.8 %collective-permute-start.12 = (bf16[256,384]{1,0:T(8,128)(2,1)S(1)}, bf16[256,384]{1,0:T(8,128)(2,1)S(1)}, u32[]{:S(2)}, u32[]{:S(2)}) collective-permute-start(bf16[256,384]{1,0:T(8,128)(2,1)S(1)} %slice.6), channel_id=1, source_target_pairs={{0,8},{2,10},{4,12},{6,14},{8,16},{10,18},{12,20},{14,22},{16,24},... | collective-permute-start | bytes 589832 | tf_op jit(solution)/shard_map/ppermute | solution.py:629
  61.8 1.5 %collective-permute-start.13 = (bf16[256,384]{1,0:T(8,128)(2,1)S(1)}, bf16[256,384]{1,0:T(8,128)(2,1)S(1)}, u32[]{:S(2)}, u32[]{:S(2)}) collective-permute-start(bf16[256,384]{1,0:T(8,128)(2,1)S(1)} %slice.7), channel_id=1, source_target_pairs={{0,24},{2,26},{4,28},{6,30},{8,0},{10,2},{12,4},{14,6},{16,8},{18,... | collective-permute-start | bytes 589832 | tf_op jit(solution)/shard_map/ppermute | solution.py:629
  63.3 4.6 %collective-permute-done.12 = bf16[256,384]{1,0:T(8,128)(2,1)S(1)} collective-permute-done((bf16[256,384]{1,0:T(8,128)(2,1)S(1)}, bf16[256,384]{1,0:T(8,128)(2,1)S(1)}, u32[]{:S(2)}, u32[]{:S(2)}) %collective-permute-start.12) | collective-permute-done | bytes 196640 | tf_op jit(solution)/shard_map/ppermute | solution.py:629
  67.9 0.3 collective-permute-done.13
  68.2 0.3 collective-permute-start.17
  68.5 1.7 %collective-permute-done.17.refs_7_ = bf16[512,384]{1,0:T(8,128)(2,1)S(1)} collective-permute-done((bf16[512,384]{1,0:T(8,128)(2,1)S(1)}, bf16[512,384]{1,0:T(8,128)(2,1)S(1)}, u32[]{:S(2)}, u32[]{:S(2)}) %collective-permute-start.17) | collective-permute-done | bytes 393248 | tf_op jit(solution)/shard_map/ppermute | solution.py:629
  70.2 5.9 %attend.2 = (bf16[544,256]{1,0:T(8,128)(2,1)S(1)}, f32[8,4096]{1,0:T(8,128)S(1)}) custom-call(s32[3]{0:T(128)S(1)} %pad_add_fusion.ids, f32[4]{0:T(128)S(1)} %copy-done.4, bf16[544,256]{1,0:T(8,128)(2,1)S(1)} %collective-permute-done.16.queries, bf16[512,384]{1,0:T(8,128)(2,1)S(1)} %constant_dynamic-update-slice_fusion.refs_0_, ...), custom_call_target="tpu_custom_call" | custom-call | flops 2281701376 | bytes 4456448 | tf_op jit(solution)/shard_map/attend/pallas_call | solution.py:392
  76.1 1.1 collective-permute-start.18
  77.2 4.8 %attend.3.a0 = bf16[544,256]{1,0:T(8,128)(2,1)S(1)} custom-call(s32[3]{0:T(128)S(1)} %pad_add_fusion.ids, f32[4]{0:T(128)S(1)} %copy-done.4, bf16[544,256]{1,0:T(8,128)(2,1)S(1)} %constant_dynamic-update-slice_fusion.4.queries, bf16[512,384]{1,0:T(8,128)(2,1)S(1)} %constant_dynamic-update-slice_fusion.refs_0_, ...), custom_call_target="tpu_custom_call" | custom-call | flops 2281701376 | bytes 4456448 | tf_op jit(solution)/shard_map/attend/pallas_call | solution.py:392
  82.0 2.9 %collective-permute-done.18.a1 = bf16[544,256]{1,0:T(8,128)(2,1)S(1)} collective-permute-done((bf16[544,256]{1,0:T(8,128)(2,1)S(1)}, bf16[544,256]{1,0:T(8,128)(2,1)S(1)}, u32[]{:S(2)}, u32[]{:S(2)}) %collective-permute-start.18) | collective-permute-done | bytes 278560 | tf_op jit(solution)/shard_map/ppermute | solution.py:629
  84.8 0.5 merge.1
  85.4 1.9 %collective-permute-start.19 = (bf16[136,256]{1,0:T(8,128)(2,1)S(1)}, bf16[136,256]{1,0:T(8,128)(2,1)S(1)}, u32[]{:S(2)}, u32[]{:S(2)}) collective-permute-start(bf16[136,256]{1,0:T(8,128)(2,1)S(1)} %get-tuple-element.85), channel_id=1, source_target_pairs={{0,96},{2,98},{4,100},{6,102},{8,104},{10,106},{12,108},{14,110},{... | collective-permute-start | bytes 208904 | tf_op jit(solution)/shard_map/ppermute | solution.py:629
  87.3 1.2 collective-permute-start.20
  88.5 0.2 collective-permute-start.21
  88.7 1.1 collective-permute-done.19.a1
  89.8 3.3 %collective-permute-done.20.a2 = bf16[136,256]{1,0:T(8,128)(2,1)S(1)} collective-permute-done((bf16[136,256]{1,0:T(8,128)(2,1)S(1)}, bf16[136,256]{1,0:T(8,128)(2,1)S(1)}, u32[]{:S(2)}, u32[]{:S(2)}) %collective-permute-start.20) | collective-permute-done | bytes 69664 | tf_op jit(solution)/shard_map/ppermute | solution.py:629
  93.1 0.9 collective-permute-done.21.a3
  94.0 1.3 output.3
  95.3 3.3 %collective-permute-start.22 = (bf16[136,768]{1,0:T(8,128)(2,1)S(1)}, bf16[136,768]{1,0:T(8,128)(2,1)S(1)}, u32[]{:S(2)}, u32[]{:S(2)}) collective-permute-start(bf16[136,768]{1,0:T(8,128)(2,1)S(1)} %output.3), channel_id=1, source_target_pairs={{0,1},{1,0},{2,3},{3,2},{4,5},{5,4},{6,7},{7,6},{8,9},{9,8},{10,11... | collective-permute-start | bytes 626696 | tf_op jit(solution)/shard_map/ppermute | solution.py:625
  98.6 1.3 output.2.own
  99.9 2.8 %collective-permute-done.22.other = bf16[136,768]{1,0:T(8,128)(2,1)S(1)} collective-permute-done((bf16[136,768]{1,0:T(8,128)(2,1)S(1)}, bf16[136,768]{1,0:T(8,128)(2,1)S(1)}, u32[]{:S(2)}, u32[]{:S(2)}) %collective-permute-start.22) | collective-permute-done | bytes 208928 | tf_op jit(solution)/shard_map/ppermute | solution.py:625
  102.7 1.7 %decode_first.1 = (bf16[272,768]{1,0:T(8,128)(2,1)S(1)}, bf16[272,512]{1,0:T(8,128)(2,1)S(1)}) custom-call(s32[3]{0:T(128)S(1)} %pad_add_fusion.ids, f32[136,768]{1,0:T(8,128)S(1)} %output.2.own, bf16[136,768]{1,0:T(8,128)(2,1)S(1)} %collective-permute-done.22.other, bf16[272,768]{1,0:T(8,128)(2,1)S(1)} %get-tuple-element.55.mine.encoded, ...), custom_call_target="tpu_custom_call" | custom-call | flops 1000000 | bytes 10000 | tf_op jit(solution)/shard_map/decode_first/pallas_call | solution.py:487
  104.5 3.5 %collective-permute-start.24 = (bf16[272,512]{1,0:T(8,128)(2,1)S(1)}, bf16[272,512]{1,0:T(8,128)(2,1)S(1)}, u32[]{:S(2)}, u32[]{:S(2)}) collective-permute-start(bf16[272,512]{1,0:T(8,128)(2,1)S(1)} %get-tuple-element.91), channel_id=1, source_target_pairs={{0,1},{1,0},{2,3},{3,2},{4,5},{5,4},{6,7},{7,6},{8,9},{9,8},{10,11... | collective-permute-start | bytes 835592 | tf_op jit(solution)/shard_map/ppermute | solution.py:625
  107.9 1.7 %decode.2 = bf16[272,256]{1,0:T(8,128)(2,1)} custom-call(s32[3]{0:T(128)S(1)} %pad_add_fusion.ids, bf16[272,768]{1,0:T(8,128)(2,1)S(1)} %get-tuple-element.89.inputs, bf16[3,768,1536]{2,1,0:T(8,128)(2,1)S(1)} %bitcast.5), custom_call_target="tpu_custom_call" | custom-call | flops 1000000 | bytes 10000 | tf_op jit(solution)/shard_map/decode/pallas_call | solution.py:505
  109.7 0.3 collective-permute-start.23
  110.0 2.1 %decode.3.own = f32[272,768]{1,0:T(8,128)S(1)} custom-call(s32[3]{0:T(128)S(1)} %pad_add_fusion.ids, bf16[272,768]{1,0:T(8,128)(2,1)S(1)} %get-tuple-element.89.inputs, bf16[3,768,1536]{2,1,0:T(8,128)(2,1)S(1)} %bitcast.5), custom_call_target="tpu_custom_call" | custom-call | flops 1000000 | bytes 10000 | tf_op jit(solution)/shard_map/decode/pallas_call | solution.py:505
  112.1 2.2 %collective-permute-done.24.other = bf16[272,512]{1,0:T(8,128)(2,1)S(1)} collective-permute-done((bf16[272,512]{1,0:T(8,128)(2,1)S(1)}, bf16[272,512]{1,0:T(8,128)(2,1)S(1)}, u32[]{:S(2)}, u32[]{:S(2)}) %collective-permute-start.24) | collective-permute-done | bytes 278560 | tf_op jit(solution)/shard_map/ppermute | solution.py:625
  114.3 1.9 %slopes.2 = (bf16[256,512]{1,0:T(8,128)(2,1)S(1)}, bf16[272,512]{1,0:T(8,128)(2,1)}, f32[128,512]{1,0:T(8,128)S(1)}) custom-call(s32[3]{0:T(128)S(1)} %pad_add_fusion.ids, f32[272,768]{1,0:T(8,128)S(1)} %decode.3.own, bf16[272,512]{1,0:T(8,128)(2,1)S(1)} %collective-permute-done.24.other, bf16[272,768]{1,0:T(8,128)(2,1)S(1)} %get-tuple-element.89.inputs, ...), custom_call_target="tpu_custom_call" | custom-call | flops 417792000000 | bytes 1949696 | tf_op jit(solution)/shard_map/slopes/pallas_call | solution.py:553
  116.2 1.8 %collective-permute-start.26 = (bf16[272,512]{1,0:T(8,128)(2,1)}, bf16[272,512]{1,0:T(8,128)(2,1)}, u32[]{:S(2)}, u32[]{:S(2)}) collective-permute-start(bf16[272,512]{1,0:T(8,128)(2,1)} %get-tuple-element.95.refs_0_), channel_id=1, source_target_pairs={{0,1},{1,0},{2,3},{3,2},{4,5},{5,4},{6,7},{7,6},{8,9},{9,8},{10,11... | collective-permute-start | bytes 835592 | tf_op jit(solution)/shard_map/ppermute | solution.py:625
  118.0 2.0 %slopes.3 = (bf16[256,768]{1,0:T(8,128)(2,1)}, bf16[272,256]{1,0:T(8,128)(2,1)}, f32[128,256]{1,0:T(8,128)S(1)}) custom-call(s32[3]{0:T(128)S(1)} %pad_add_fusion.ids, f32[272,768]{1,0:T(8,128)S(1)} %decode.3.own, bf16[272,256]{1,0:T(8,128)(2,1)} %collective-permute-done.23.other, bf16[272,768]{1,0:T(8,128)(2,1)S(1)} %get-tuple-element.89.inputs, ...), custom_call_target="tpu_custom_call" | custom-call | flops 208896000000 | bytes 974848 | tf_op jit(solution)/shard_map/slopes/pallas_call | solution.py:553
  120.0 1.8 %collective-permute-start.25 = (bf16[272,256]{1,0:T(8,128)(2,1)}, bf16[272,256]{1,0:T(8,128)(2,1)}, u32[]{:S(2)}, u32[]{:S(2)}) collective-permute-start(bf16[272,256]{1,0:T(8,128)(2,1)} %get-tuple-element.94.refs_1_), channel_id=1, source_target_pairs={{0,1},{1,0},{2,3},{3,2},{4,5},{5,4},{6,7},{7,6},{8,9},{9,8},{10,11... | collective-permute-start | bytes 417800 | tf_op jit(solution)/shard_map/ppermute | solution.py:625
  121.7 2.7 %backward.3.refs_1_ = f32[128,768]{1,0:T(8,128)S(1)} custom-call(s32[3]{0:T(128)S(1)} %pad_add_fusion.ids, bf16[272,512]{1,0:T(8,128)(2,1)} %get-tuple-element.95.refs_0_, bf16[272,256]{1,0:T(8,128)(2,1)} %get-tuple-element.94.refs_1_, f32[128,512]{1,0:T(8,128)S(1)} %get-tuple-element.96.refs_2_, f32[128,256]{1,0:T(8,128)S(1)} %get-tuple-element.97.refs_3_, ...), custom_call_target="tpu_custom_call" | custom-call | flops 96259276800 | bytes 1253376 | tf_op jit(solution)/shard_map/backward/pallas_call | solution.py:600
  124.4 0.2 collective-permute-done.26.refs_0_
  124.6 2.2 %backward.4.refs_1_ = f32[128,768]{1,0:T(8,128)S(1)} custom-call(s32[3]{0:T(128)S(1)} %pad_add_fusion.ids, bf16[272,512]{1,0:T(8,128)(2,1)} %collective-permute-done.26.refs_0_, f32[128,768]{1,0:T(8,128)S(1)} %backward.3.refs_1_, bf16[3,768,1536]{2,1,0:T(8,128)(2,1)S(1)} %bitcast.5), custom_call_target="tpu_custom_call" | custom-call | flops 64172851200 | bytes 835584 | tf_op jit(solution)/shard_map/backward/pallas_call | solution.py:600
  126.8 0.0 collective-permute-done.25.refs_0_
  126.8 2.1 %backward.5 = bf16[128,768]{1,0:T(8,128)(2,1)} custom-call(s32[3]{0:T(128)S(1)} %pad_add_fusion.ids, bf16[272,256]{1,0:T(8,128)(2,1)} %collective-permute-done.25.refs_0_, f32[128,768]{1,0:T(8,128)S(1)} %backward.4.refs_1_, bf16[3,768,1536]{2,1,0:T(8,128)(2,1)S(1)} %bitcast.5), custom_call_target="tpu_custom_call" | custom-call | flops 32086425600 | bytes 417792 | tf_op jit(solution)/shard_map/backward/pallas_call | solution.py:600
  (40 shorter events, 0.3 us)
Async XLA Ops:
  2.2 6.9 %collective-permute-start = (bf16[8,1664]{1,0:T(8,128)(2,1)S(1)}, bf16[8,1664]{1,0:T(8,128)(2,1)S(1)}, u32[]{:S(2)}, u32[]{:S(2)}) collective-permute-start(bf16[8,1664]{1,0:T(8,128)(2,1)S(1)} %get-tuple-element.51), channel_id=1, source_target_pairs={{0,2},{2,0},{4,6},{6,4},{8,10},{10,8},{12,14},{14,12},{16,18},{18,... | collective-permute-start | bytes 79880 | tf_op jit(solution)/shard_map/ppermute | solution.py:629
  2.3 6.8 %collective-permute-start.1 = (bf16[8,1664]{1,0:T(8,128)(2,1)S(1)}, bf16[8,1664]{1,0:T(8,128)(2,1)S(1)}, u32[]{:S(2)}, u32[]{:S(2)}) collective-permute-start(bf16[8,1664]{1,0:T(8,128)(2,1)S(1)} %get-tuple-element.52), channel_id=1, source_target_pairs={{2,4},{6,8},{10,12},{14,16},{18,20},{22,24},{26,28},{30,32},{34,36... | collective-permute-start | bytes 79880 | tf_op jit(solution)/shard_map/ppermute | solution.py:651
  6.2 2.8 %copy-start.1 = (bf16[3,1536,768]{2,1,0:T(8,128)(2,1)}, bf16[3,1536,768]{2,1,0:T(8,128)(2,1)S(1)}, u32[]{:S(2)}) copy-start(bf16[3,1536,768]{2,1,0:T(8,128)(2,1)S(1)} %get-tuple-element.54.weight) | copy-start | bytes 21233668
  9.1 3.0 %copy-start.2 = (bf16[3,1536,768]{2,1,0:T(8,128)(2,1)S(1)}, bf16[3,1536,768]{2,1,0:T(8,128)(2,1)}, u32[]{:S(2)}) copy-start(bf16[3,1536,768]{2,1,0:T(8,128)(2,1)} %copy-done.1) | copy-start | bytes 21233668
  12.1 8.0 %copy-start.5 = (f32[1536]{0:T(1024)S(1)}, f32[1536]{0:T(1024)}, u32[]{:S(2)}) copy-start(f32[1536]{0:T(1024)} %param.12) | copy-start | bytes 18436
  16.8 12.0 %collective-permute-start.2 = (bf16[272,768]{1,0:T(8,128)(2,1)S(1)}, bf16[272,768]{1,0:T(8,128)(2,1)S(1)}, u32[]{:S(2)}, u32[]{:S(2)}) collective-permute-start(bf16[272,768]{1,0:T(8,128)(2,1)S(1)} %get-tuple-element.55.mine.encoded), channel_id=1, source_target_pairs={{0,1},{1,0},{2,3},{3,2},{4,5},{5,4},{6,7},{7,6},{8,9},{9,8},{10,11... | collective-permute-start | bytes 1253384 | tf_op jit(solution)/shard_map/ppermute | solution.py:625
  30.8 39.4 %copy-start.4 = (f32[4]{0:T(128)S(1)}, f32[4]{0:T(128)}, u32[]{:S(2)}) copy-start(f32[4]{0:T(128)} %scale.3) | copy-start | bytes 52
  30.8 10.9 %collective-permute-start.3 = (bf16[128,384]{1,0:T(8,128)(2,1)S(1)}, bf16[128,384]{1,0:T(8,128)(2,1)S(1)}, u32[]{:S(2)}, u32[]{:S(2)}) collective-permute-start(bf16[128,384]{1,0:T(8,128)(2,1)S(1)} %get-tuple-element.58), channel_id=1, source_target_pairs={{0,32},{2,34},{4,36},{6,38},{8,40},{10,42},{12,44},{14,46},{16,48}... | collective-permute-start | bytes 294920 | tf_op jit(solution)/shard_map/ppermute | solution.py:629
  36.5 5.1 %collective-permute-start.4 = (bf16[128,384]{1,0:T(8,128)(2,1)S(1)}, bf16[128,384]{1,0:T(8,128)(2,1)S(1)}, u32[]{:S(2)}, u32[]{:S(2)}) collective-permute-start(bf16[128,384]{1,0:T(8,128)(2,1)S(1)} %get-tuple-element.59), channel_id=1, source_target_pairs={{0,96},{2,98},{4,100},{6,102},{8,104},{10,106},{12,108},{14,110},{... | collective-permute-start | bytes 294920 | tf_op jit(solution)/shard_map/ppermute | solution.py:629
  38.1 6.1 %collective-permute-start.5 = (bf16[128,384]{1,0:T(8,128)(2,1)S(1)}, bf16[128,384]{1,0:T(8,128)(2,1)S(1)}, u32[]{:S(2)}, u32[]{:S(2)}) collective-permute-start(bf16[128,384]{1,0:T(8,128)(2,1)S(1)} %get-tuple-element.60), channel_id=1, source_target_pairs={{0,64},{2,66},{4,68},{6,70},{8,72},{10,74},{12,76},{14,78},{16,80}... | collective-permute-start | bytes 294920 | tf_op jit(solution)/shard_map/ppermute | solution.py:629
  44.3 4.5 %collective-permute-start.6 = (bf16[512,384]{1,0:T(8,128)(2,1)S(1)}, bf16[512,384]{1,0:T(8,128)(2,1)S(1)}, u32[]{:S(2)}, u32[]{:S(2)}) collective-permute-start(bf16[512,384]{1,0:T(8,128)(2,1)S(1)} %constant_dynamic-update-slice_fusion.refs_0_), channel_id=1, source_target_pairs={{0,2},{2,0},{4,6},{6,4},{8,10},{10,8},{12,14},{14,12},{16,18},{18,... | collective-permute-start | bytes 1179656 | tf_op jit(solution)/shard_map/ppermute | solution.py:629
  44.4 14.0 %collective-permute-start.7 = (bf16[512,384]{1,0:T(8,128)(2,1)S(1)}, bf16[512,384]{1,0:T(8,128)(2,1)S(1)}, u32[]{:S(2)}, u32[]{:S(2)}) collective-permute-start(bf16[512,384]{1,0:T(8,128)(2,1)S(1)} %constant_dynamic-update-slice_fusion.refs_0_), channel_id=1, source_target_pairs={{0,8},{2,10},{4,12},{6,14},{8,16},{10,18},{12,20},{14,22},{16,24},... | collective-permute-start | bytes 1179656 | tf_op jit(solution)/shard_map/ppermute | solution.py:629
  46.6 11.8 %collective-permute-start.8 = (bf16[512,384]{1,0:T(8,128)(2,1)S(1)}, bf16[512,384]{1,0:T(8,128)(2,1)S(1)}, u32[]{:S(2)}, u32[]{:S(2)}) collective-permute-start(bf16[512,384]{1,0:T(8,128)(2,1)S(1)} %constant_dynamic-update-slice_fusion.refs_0_), channel_id=1, source_target_pairs={{0,24},{2,26},{4,28},{6,30},{8,0},{10,2},{12,4},{14,6},{16,8},{18,... | collective-permute-start | bytes 1179656 | tf_op jit(solution)/shard_map/ppermute | solution.py:629
  50.0 8.4 %collective-permute-start.10 = (bf16[136,256]{1,0:T(8,128)(2,1)S(1)}, bf16[136,256]{1,0:T(8,128)(2,1)S(1)}, u32[]{:S(2)}, u32[]{:S(2)}) collective-permute-start(bf16[136,256]{1,0:T(8,128)(2,1)S(1)} %get-tuple-element.69), channel_id=1, source_target_pairs={{0,96},{2,98},{4,100},{6,102},{8,104},{10,106},{12,108},{14,110},{... | collective-permute-start | bytes 208904 | tf_op jit(solution)/shard_map/ppermute | solution.py:629
  51.8 6.6 %collective-permute-start.11 = (bf16[136,256]{1,0:T(8,128)(2,1)S(1)}, bf16[136,256]{1,0:T(8,128)(2,1)S(1)}, u32[]{:S(2)}, u32[]{:S(2)}) collective-permute-start(bf16[136,256]{1,0:T(8,128)(2,1)S(1)} %get-tuple-element.70), channel_id=1, source_target_pairs={{0,64},{2,66},{4,68},{6,70},{8,72},{10,74},{12,76},{14,78},{16,80}... | collective-permute-start | bytes 208904 | tf_op jit(solution)/shard_map/ppermute | solution.py:629
  52.5 6.2 %collective-permute-start.9 = (bf16[136,256]{1,0:T(8,128)(2,1)S(1)}, bf16[136,256]{1,0:T(8,128)(2,1)S(1)}, u32[]{:S(2)}, u32[]{:S(2)}) collective-permute-start(bf16[136,256]{1,0:T(8,128)(2,1)S(1)} %get-tuple-element.68), channel_id=1, source_target_pairs={{0,32},{2,34},{4,36},{6,38},{8,40},{10,42},{12,44},{14,46},{16,48}... | collective-permute-start | bytes 208904 | tf_op jit(solution)/shard_map/ppermute | solution.py:629
  58.6 9.5 %collective-permute-start.14 = (bf16[512,384]{1,0:T(8,128)(2,1)S(1)}, bf16[512,384]{1,0:T(8,128)(2,1)S(1)}, u32[]{:S(2)}, u32[]{:S(2)}) collective-permute-start(bf16[512,384]{1,0:T(8,128)(2,1)S(1)} %collective-permute-done.7.refs_2_), channel_id=1, source_target_pairs={{0,2},{2,0},{4,6},{6,4},{8,10},{10,8},{12,14},{14,12},{16,18},{18,... | collective-permute-start | bytes 1179656 | tf_op jit(solution)/shard_map/ppermute | solution.py:629
  58.6 9.5 %collective-permute-start.15 = (bf16[512,384]{1,0:T(8,128)(2,1)S(1)}, bf16[512,384]{1,0:T(8,128)(2,1)S(1)}, u32[]{:S(2)}, u32[]{:S(2)}) collective-permute-start(bf16[512,384]{1,0:T(8,128)(2,1)S(1)} %collective-permute-done.8.refs_3_), channel_id=1, source_target_pairs={{0,2},{2,0},{4,6},{6,4},{8,10},{10,8},{12,14},{14,12},{16,18},{18,... | collective-permute-start | bytes 1179656 | tf_op jit(solution)/shard_map/ppermute | solution.py:629
  59.2 8.9 %collective-permute-start.16 = (bf16[544,256]{1,0:T(8,128)(2,1)S(1)}, bf16[544,256]{1,0:T(8,128)(2,1)S(1)}, u32[]{:S(2)}, u32[]{:S(2)}) collective-permute-start(bf16[544,256]{1,0:T(8,128)(2,1)S(1)} %constant_dynamic-update-slice_fusion.4.queries), channel_id=1, source_target_pairs={{0,4},{2,6},{4,0},{6,2},{8,12},{10,14},{12,8},{14,10},{16,20},{18,... | collective-permute-start | bytes 835592 | tf_op jit(solution)/shard_map/ppermute | solution.py:629
  60.0 7.9 %collective-permute-start.12 = (bf16[256,384]{1,0:T(8,128)(2,1)S(1)}, bf16[256,384]{1,0:T(8,128)(2,1)S(1)}, u32[]{:S(2)}, u32[]{:S(2)}) collective-permute-start(bf16[256,384]{1,0:T(8,128)(2,1)S(1)} %slice.6), channel_id=1, source_target_pairs={{0,8},{2,10},{4,12},{6,14},{8,16},{10,18},{12,20},{14,22},{16,24},... | collective-permute-start | bytes 589832 | tf_op jit(solution)/shard_map/ppermute | solution.py:629
  61.8 6.3 %collective-permute-start.13 = (bf16[256,384]{1,0:T(8,128)(2,1)S(1)}, bf16[256,384]{1,0:T(8,128)(2,1)S(1)}, u32[]{:S(2)}, u32[]{:S(2)}) collective-permute-start(bf16[256,384]{1,0:T(8,128)(2,1)S(1)} %slice.7), channel_id=1, source_target_pairs={{0,24},{2,26},{4,28},{6,30},{8,0},{10,2},{12,4},{14,6},{16,8},{18,... | collective-permute-start | bytes 589832 | tf_op jit(solution)/shard_map/ppermute | solution.py:629
  68.2 25.8 %copy-start = (bf16[768,1536]{1,0:T(8,128)(2,1)S(1)}, bf16[768,1536]{1,0:T(8,128)(2,1)}, u32[]{:S(2)}) copy-start(bf16[768,1536]{1,0:T(8,128)(2,1)} %weight.6) | copy-start | bytes 7077892
  68.2 2.0 %collective-permute-start.17 = (bf16[512,384]{1,0:T(8,128)(2,1)S(1)}, bf16[512,384]{1,0:T(8,128)(2,1)S(1)}, u32[]{:S(2)}, u32[]{:S(2)}) collective-permute-start(bf16[512,384]{1,0:T(8,128)(2,1)S(1)} %constant_dynamic-update-slice_fusion.8.refs_6_), channel_id=1, source_target_pairs={{0,2},{2,0},{4,6},{6,4},{8,10},{10,8},{12,14},{14,12},{16,18},{18,... | collective-permute-start | bytes 1179656 | tf_op jit(solution)/shard_map/ppermute | solution.py:629
  76.1 8.8 %collective-permute-start.18 = (bf16[544,256]{1,0:T(8,128)(2,1)S(1)}, bf16[544,256]{1,0:T(8,128)(2,1)S(1)}, u32[]{:S(2)}, u32[]{:S(2)}) collective-permute-start(bf16[544,256]{1,0:T(8,128)(2,1)S(1)} %get-tuple-element.83), channel_id=1, source_target_pairs={{0,4},{2,6},{4,0},{6,2},{8,12},{10,14},{12,8},{14,10},{16,20},{18,... | collective-permute-start | bytes 835592 | tf_op jit(solution)/shard_map/ppermute | solution.py:629
  77.2 25.5 %slice-start = ((s8[7077888]{0:T(1024)(128)(4,1)}), s8[4194304]{0:T(1024)(128)(4,1)S(1)}, s32[]{:S(2)}) async-start(s8[7077888]{0:T(1024)(128)(4,1)} %bitcast.4), calls=%async_computation | async-start | bytes 8388608
  77.2 25.5 %slice-start.1 = ((s8[7077888]{0:T(1024)(128)(4,1)}), s8[2883584]{0:T(1024)(128)(4,1)S(1)}, s32[]{:S(2)}) async-start(s8[7077888]{0:T(1024)(128)(4,1)} %bitcast.4), calls=%async_computation.1 | async-start | bytes 5767168
  85.4 4.4 %collective-permute-start.19 = (bf16[136,256]{1,0:T(8,128)(2,1)S(1)}, bf16[136,256]{1,0:T(8,128)(2,1)S(1)}, u32[]{:S(2)}, u32[]{:S(2)}) collective-permute-start(bf16[136,256]{1,0:T(8,128)(2,1)S(1)} %get-tuple-element.85), channel_id=1, source_target_pairs={{0,96},{2,98},{4,100},{6,102},{8,104},{10,106},{12,108},{14,110},{... | collective-permute-start | bytes 208904 | tf_op jit(solution)/shard_map/ppermute | solution.py:629
  87.3 5.8 %collective-permute-start.20 = (bf16[136,256]{1,0:T(8,128)(2,1)S(1)}, bf16[136,256]{1,0:T(8,128)(2,1)S(1)}, u32[]{:S(2)}, u32[]{:S(2)}) collective-permute-start(bf16[136,256]{1,0:T(8,128)(2,1)S(1)} %get-tuple-element.86), channel_id=1, source_target_pairs={{0,64},{2,66},{4,68},{6,70},{8,72},{10,74},{12,76},{14,78},{16,80}... | collective-permute-start | bytes 208904 | tf_op jit(solution)/shard_map/ppermute | solution.py:629
  88.5 5.5 %collective-permute-start.21 = (bf16[136,256]{1,0:T(8,128)(2,1)S(1)}, bf16[136,256]{1,0:T(8,128)(2,1)S(1)}, u32[]{:S(2)}, u32[]{:S(2)}) collective-permute-start(bf16[136,256]{1,0:T(8,128)(2,1)S(1)} %get-tuple-element.87), channel_id=1, source_target_pairs={{0,32},{2,34},{4,36},{6,38},{8,40},{10,42},{12,44},{14,46},{16,48}... | collective-permute-start | bytes 208904 | tf_op jit(solution)/shard_map/ppermute | solution.py:629
  95.3 7.4 %collective-permute-start.22 = (bf16[136,768]{1,0:T(8,128)(2,1)S(1)}, bf16[136,768]{1,0:T(8,128)(2,1)S(1)}, u32[]{:S(2)}, u32[]{:S(2)}) collective-permute-start(bf16[136,768]{1,0:T(8,128)(2,1)S(1)} %output.3), channel_id=1, source_target_pairs={{0,1},{1,0},{2,3},{3,2},{4,5},{5,4},{6,7},{7,6},{8,9},{9,8},{10,11... | collective-permute-start | bytes 626696 | tf_op jit(solution)/shard_map/ppermute | solution.py:625
  104.5 9.8 %collective-permute-start.24 = (bf16[272,512]{1,0:T(8,128)(2,1)S(1)}, bf16[272,512]{1,0:T(8,128)(2,1)S(1)}, u32[]{:S(2)}, u32[]{:S(2)}) collective-permute-start(bf16[272,512]{1,0:T(8,128)(2,1)S(1)} %get-tuple-element.91), channel_id=1, source_target_pairs={{0,1},{1,0},{2,3},{3,2},{4,5},{5,4},{6,7},{7,6},{8,9},{9,8},{10,11... | collective-permute-start | bytes 835592 | tf_op jit(solution)/shard_map/ppermute | solution.py:625
  107.9 6.4 %copy-start.3 = (bf16[256,1536]{1,0:T(8,128)(2,1)S(1)}, bf16[256,1536]{1,0:T(8,128)(2,1)}, u32[]{:S(2)}) copy-start(bf16[256,1536]{1,0:T(8,128)(2,1)} %grad.5) | copy-start | bytes 2359300
  109.7 8.3 %collective-permute-start.23 = (bf16[272,256]{1,0:T(8,128)(2,1)}, bf16[272,256]{1,0:T(8,128)(2,1)}, u32[]{:S(2)}, u32[]{:S(2)}) collective-permute-start(bf16[272,256]{1,0:T(8,128)(2,1)} %decode.2), channel_id=1, source_target_pairs={{0,1},{1,0},{2,3},{3,2},{4,5},{5,4},{6,7},{7,6},{8,9},{9,8},{10,11... | collective-permute-start | bytes 417800 | tf_op jit(solution)/shard_map/ppermute | solution.py:625
  116.2 8.4 %collective-permute-start.26 = (bf16[272,512]{1,0:T(8,128)(2,1)}, bf16[272,512]{1,0:T(8,128)(2,1)}, u32[]{:S(2)}, u32[]{:S(2)}) collective-permute-start(bf16[272,512]{1,0:T(8,128)(2,1)} %get-tuple-element.95.refs_0_), channel_id=1, source_target_pairs={{0,1},{1,0},{2,3},{3,2},{4,5},{5,4},{6,7},{7,6},{8,9},{9,8},{10,11... | collective-permute-start | bytes 835592 | tf_op jit(solution)/shard_map/ppermute | solution.py:625
  120.0 6.9 %collective-permute-start.25 = (bf16[272,256]{1,0:T(8,128)(2,1)}, bf16[272,256]{1,0:T(8,128)(2,1)}, u32[]{:S(2)}, u32[]{:S(2)}) collective-permute-start(bf16[272,256]{1,0:T(8,128)(2,1)} %get-tuple-element.94.refs_1_), channel_id=1, source_target_pairs={{0,1},{1,0},{2,3},{3,2},{4,5},{5,4},{6,7},{7,6},{8,9},{9,8},{10,11... | collective-permute-start | bytes 417800 | tf_op jit(solution)/shard_map/ppermute | solution.py:625

commit v9 on v8

--- a/solution.py
+++ b/solution.py
@@ -70,6 +70,11 @@
     even = above(first[half:], span) + mid[:half] + last[half:]
     odd = first[:half] + mid[half:] + below(last[:half], span)
     return jnp.concatenate([even, odd], axis=0)
+
+
+def sides(ids, near, far):
+    odd = lax.rem(ids[2], 2) == 1
+    return jnp.where(odd, near, far), jnp.where(odd, far, near)
 
 
 def prepare_kernel(ids, bases, grad, codes, near, far, code, head, tail, sems):
@@ -124,44 +129,10 @@
     )(ids, far_memory(bases), far_memory(grad))
 
 
-def load_kernel(*refs):
-    count = len(refs) // 2
-    sources, targets, sems = refs[:count], refs[count : 2 * count], refs[-1]
-    copies = [
-        pltpu.make_async_copy(source, target, sems.at[i])
-        for i, (source, target) in enumerate(zip(sources, targets))
-    ]
-    for copy in copies:
-        copy.start()
-    for copy in copies:
-        copy.wait()
-
-
-def load(*values):
-    return pl.pallas_call(
-        load_kernel,
-        in_specs=[HBM] * len(values),
-        out_specs=[VM] * len(values),
-        out_shape=[pltpu.VMEM(value.shape, value.dtype) for value in values],
-        scratch_shapes=[pltpu.SemaphoreType.DMA((len(values),))],
-        compiler_params=params(2),
-        cost_estimate=cost(10**5, sum(value.size for value in values) * 2),
-        name="load",
-    )(*[far_memory(value) for value in values])
-
-
-def encode_kernel(ids, codes, before, after, stem, weight, ahead, encoded, loaded, embedded, sem):
-    copy = pltpu.make_async_copy(ahead, loaded, sem)
-    copy.start()
+def embed_letters(code, stem, embedded):
     patch = stem.shape[0] // 4
-    feats = stem.shape[1]
-    half = weight.shape[2]
     row = lax.broadcasted_iota(jnp.int32, (2 * patch, 4 * patch), 0)
     col = lax.broadcasted_iota(jnp.int32, (2 * patch, 4 * patch), 1)
-    place = lax.broadcasted_iota(jnp.int32, (ROWS - OWN, 128), 0)
-    halo = jnp.where(place >= 6, before[:, feats:].astype(F32), 0.0)
-    halo = jnp.where(place < 2, after[:, feats:].astype(F32), halo)
-    code = jnp.concatenate([codes[...].astype(F32), halo], axis=0).astype(BF16)
     spread = [
         dot(code, (row == col // 4 + offset).astype(F32).astype(BF16)) for offset in (0, patch)
     ]
@@ -173,31 +144,130 @@
         at = lanes(i * TILE, TILE)
         embedded[:, at] = dot(onehot, stem[:, at]).astype(BF16)
 
-    tiles(feats // TILE, embed)
-
-    def convolve(i):
+    tiles(stem.shape[1] // TILE, embed)
+
+
+def activate(side, pre, embedded, encoded):
+    half = encoded.shape[1]
+
+    def tile(i):
         at = lanes(i * TILE, TILE)
-        pre = conv_taps(embedded[...], lambda t: weight[t, :, at], ROWS)
-        mine = embedded[:, lanes(ids[0] * half + i * TILE, TILE)].astype(F32)
-        encoded[:, at] = (mine + 0.5 * pre * (1.0 + gelu_tanh(pre))).astype(BF16)
-
-    tiles(half // TILE, convolve)
-    copy.wait()
-
-
-def encode(ids, codes, before, after, stem, weight, ahead):
+        mine = embedded[:, lanes(side * half + i * TILE, TILE)].astype(F32)
+        value = pre[:, at]
+        encoded[:, at] = (mine + 0.5 * value * (1.0 + gelu_tanh(value))).astype(BF16)
+
+    tiles(half // TILE, tile)
+
+
+def convolve_tap(tap, weight, embedded, pre, span):
+    rows = embedded.shape[0] // 2
+
+    def tile(i):
+        at = lanes(i * TILE, TILE)
+        part = dot(embedded[...], weight[tap, :, at])
+        if tap == 1:
+            pre[:, at] = part
+        elif tap == 0:
+            pre[:, at] += jnp.concatenate([above(part[rows:], span), part[:rows]], axis=0)
+        else:
+            pre[:, at] += jnp.concatenate([part[rows:], below(part[:rows], span)], axis=0)
+
+    tiles(pre.shape[1] // TILE, tile)
+
+
+def encode_kernel(ids, codes, stems, weights, encoded, stem, weight, embedded, pre, sems):
+    copies = [pltpu.make_async_copy(stems, stem, sems.at[3])]
+    copies += [
+        pltpu.make_async_copy(weights.at[tap], weight.at[tap], sems.at[tap]) for tap in (1, 0, 2)
+    ]
+    for copy in copies:
+        copy.start()
+    copies[0].wait()
+    embed_letters(codes[...], stem, embedded)
+    for tap, copy in zip((1, 0, 2), copies[1:]):
+        copy.wait()
+        convolve_tap(tap, weight, embedded, pre, OWN)
+    activate(ids[0], pre, embedded, encoded)
+
+
+def encode(ids, codes, stem, weight):
     half = weight.shape[2]
     feats = stem.shape[1]
     return pl.pallas_call(
         encode_kernel,
+        in_specs=[SM, VM, HBM, HBM],
+        out_specs=[VM] * 3,
+        out_shape=[
+            shape((2 * OWN, half), BF16),
+            pltpu.VMEM(stem.shape, BF16),
+            pltpu.VMEM(weight.shape, BF16),
+        ],
+        scratch_shapes=[
+            pltpu.VMEM((2 * OWN, feats), BF16),
+            pltpu.VMEM((2 * OWN, half), F32),
+            pltpu.SemaphoreType.DMA((4,)),
+        ],
+        compiler_params=params(10),
+        cost_estimate=cost(4 * OWN * weight.size, weight.size * 4),
+        name="encode",
+    )(ids, codes, far_memory(stem), far_memory(weight))
+
+
+def encode_edges_kernel(
+    ids, codes, near, far, stem, weight, ahead, encoded, loaded, embedded, pre, sem
+):
+    copy = pltpu.make_async_copy(ahead, loaded, sem)
+    copy.start()
+    feats = stem.shape[1]
+    place = lax.broadcasted_iota(jnp.int32, (8, 128), 0)
+    code = codes[...].astype(F32)
+    before, after = sides(ids, near[:, feats:].astype(F32), far[:, feats:].astype(F32))
+    low = jnp.where(place >= 6, before, 0.0)
+    low = jnp.where(place == 0, code[:8], low)
+    high = jnp.where(place < 2, after, 0.0)
+    high = jnp.where(place == 7, code[OWN - 8 :], high)
+    embed_letters(jnp.concatenate([low, high], axis=0).astype(BF16), stem, embedded)
+    for tap in (1, 0, 2):
+        convolve_tap(tap, weight, embedded, pre, 8)
+    activate(ids[0], pre, embedded, encoded)
+    copy.wait()
+
+
+def encode_edges(ids, codes, near, far, stem, weight, ahead):
+    half = weight.shape[2]
+    feats = stem.shape[1]
+    return pl.pallas_call(
+        encode_edges_kernel,
         in_specs=[SM] + [VM] * 5 + [HBM],
         out_specs=[VM, VM],
-        out_shape=[shape((2 * ROWS, half), BF16), pltpu.VMEM(ahead.shape, BF16)],
-        scratch_shapes=[pltpu.VMEM((2 * ROWS, feats), BF16), pltpu.SemaphoreType.DMA(())],
-        compiler_params=params(12),
-        cost_estimate=cost(2 * 2 * ROWS * 3 * feats * half, weight.size * 4),
-        name="encode",
-    )(ids, codes, before, after, near_memory(stem), near_memory(weight), far_memory(ahead))
+        out_shape=[shape((32, half), BF16), pltpu.VMEM(ahead.shape, BF16)],
+        scratch_shapes=[
+            pltpu.VMEM((32, feats), BF16),
+            pltpu.VMEM((32, half), F32),
+            pltpu.SemaphoreType.DMA(()),
+        ],
+        compiler_params=params(6),
+        cost_estimate=cost(4 * OWN * weight.size, weight.size * 4),
+        name="encode_edges",
+    )(ids, codes, near, far, near_memory(stem), near_memory(weight), far_memory(ahead))
+
+
+def joined(main, edges):
+    main, edges = main[...].astype(F32), edges[...].astype(F32)
+    even, odd = main[:OWN], main[OWN:]
+    even_low, even_high, odd_low, odd_high = (edges[i : i + 8] for i in range(0, 32, 8))
+    place = lax.broadcasted_iota(jnp.int32, even_low.shape, 0)
+    return jnp.concatenate(
+        [
+            jnp.where(place == 0, even_low, even[:8]),
+            even[8:],
+            jnp.where(place < 4, even_high, even_low),
+            odd[: OWN - 8],
+            jnp.where(place == 7, odd_high, odd[OWN - 8 :]),
+            jnp.where(place < 4, odd_high, odd_low),
+        ],
+        axis=0,
+    )
 
 
 def unpacked(both):
@@ -207,12 +277,13 @@
 
 
 def project_keys_kernel(
-    ids, mine, theirs, gain, weight, normed, k0, k1, k2, k3, packed
+    ids, mine, mine_edges, theirs, their_edges, gain, weight, encoded, normed, k0, k1, k2, k3, packed
 ):
     half = mine.shape[1]
     near = lanes(ids[0] * half, half)
     far = lanes((1 - ids[0]) * half, half)
-    rings = [ref[...].astype(F32) for ref in (mine, theirs)]
+    rings = joined(mine, mine_edges), joined(theirs, their_edges)
+    encoded[...] = rings[0].astype(BF16)
     binned = [(ring[:ROWS] + ring[ROWS:]) * 0.5 for ring in rings]
     total = sum(jnp.sum(part * part, axis=1, keepdims=True) for part in binned)
     inverse = lax.rsqrt(total * (1.0 / (2 * half)) + EPS)
@@ -238,18 +309,19 @@
         out[...] = packed[lax.rem(ids[1] + distance, 4), :OWN, :]
 
 
-def project_keys(ids, mine, theirs, gain, weight):
+def project_keys(ids, mine, mine_edges, theirs, their_edges, gain, weight):
     half = mine.shape[1]
     return pl.pallas_call(
         project_keys_kernel,
-        in_specs=[SM] + [VM] * 4,
-        out_specs=[VM] * 5,
-        out_shape=[shape((2, ROWS, half), BF16)] + [shape((OWN, 384), BF16)] * 4,
+        in_specs=[SM] + [VM] * 6,
+        out_specs=[VM] * 6,
+        out_shape=[shape((2 * ROWS, half), BF16), shape((2, ROWS, half), BF16)]
+        + [shape((OWN, 384), BF16)] * 4,
         scratch_shapes=[pltpu.VMEM((4, ROWS, 384), BF16)],
         compiler_params=params(12),
         cost_estimate=cost(2 * ROWS * weight.size * 2 // 3, weight.size * 2),
         name="project_keys",
-    )(ids, mine, theirs, gain, weight)
+    )(ids, mine, mine_edges, theirs, their_edges, gain, weight)
 
 
 def project_queries_kernel(ids, normed, weight, q0, q1, q2, q3, packed):
@@ -513,7 +585,7 @@
     )(ids, inputs, weight)
 
 
-def slope_kernel(first, ids, own, other, inputs, grad, before, after, *refs):
+def slope_kernel(first, ids, own, other, inputs, grad, near, far, *refs):
     done, (decoded, slope, paired, wide) = refs[:-4], refs[-4:]
     half = own.shape[1]
     begin = 0
@@ -540,15 +612,16 @@
         odd = wide[1, pl.ds(1, OWN, 2), :]
         paired[:, at] = even + odd
         row = lax.broadcasted_iota(jnp.int32, (ROWS - OWN, 128), 0)
-        even_edge = jnp.where(row == 0, after[:, column].astype(F32), 0.0)
-        odd_edge = jnp.where(row == ROWS - OWN - 1, before[:, column].astype(F32), 0.0)
+        before, after = sides(ids, near[:, column].astype(F32), far[:, column].astype(F32))
+        even_edge = jnp.where(row == 0, after, 0.0)
+        odd_edge = jnp.where(row == ROWS - OWN - 1, before, 0.0)
         cotangent = jnp.concatenate([even, even_edge, odd, odd_edge], axis=0)
         slope[:, at] = (cotangent * slant).astype(BF16)
 
     tiles(other.shape[1] // 128, tile)
 
 
-def slopes(ids, own, other, inputs, grad, before, after, first, done=()):
+def slopes(ids, own, other, inputs, grad, near, far, first, done=()):
     width = other.shape[1]
     return pl.pallas_call(
         functools.partial(slope_kernel, first),
@@ -563,7 +636,7 @@
         compiler_params=params(6),
         cost_estimate=cost(100 * 30 * 1000 * other.size, 14 * other.size),
         name="slopes",
-    )(ids, own, other, inputs, grad, before, after, *done)
+    )(ids, own, other, inputs, grad, near, far, *done)
 
 
 def backward_kernel(mine, firsts, count, ids, *refs):
@@ -649,15 +722,16 @@
     near = send(near, dc=1)
     pairs = [(i, i + 1) for i in range(1, 63, 2)]
     far = lax.ppermute(far, "seq", pairs + [(b, a) for a, b in pairs])
-    odd = at % 2 == 1
-    before = jnp.where(odd, near, far)
-    after = jnp.where(odd, far, near)
-    stem_weight, encoder_weight = load(stem_weight, encoder_weight)
-    encoded, attention_weight = encode(
-        ids, codes, before, after, stem_weight, encoder_weight, attention_weight
+    halo = near, far
+    encoded, stem_weight, encoder_weight = encode(ids, codes, stem_weight, encoder_weight)
+    theirs = swap(encoded)
+    edges, attention_weight = encode_edges(
+        ids, codes, *halo, stem_weight, encoder_weight, attention_weight
     )
     gain = norm_gain.reshape(1, feats)
-    normed, *keyvals = project_keys(ids, encoded, swap(encoded), gain, attention_weight)
+    encoded, normed, *keyvals = project_keys(
+        ids, encoded, edges, theirs, swap(edges), gain, attention_weight
+    )
 
     def spread(blocks):
         return [send(blocks[d], dx=d) for d in (1, 3, 2)]
@@ -666,18 +740,14 @@
         return jnp.concatenate(lax.optimization_barrier(blocks), axis=0)
 
     keyvals = stacked([keyvals[0]] + spread(keyvals))
-    near = [send(keyvals, dz=1), send(keyvals, dz=3)]
+    ring = [send(keyvals, dz=d) for d in (1, 3, 2)]
     beside, normed = lax.optimization_barrier((send(keyvals, dc=1), normed))
     queries = project_queries(ids, normed, attention_weight)
-    *near, got1, got3, got2 = lax.optimization_barrier((*near, *spread(queries)))
-    queries = jnp.concatenate([queries[0], got1, got3, got2], axis=0)
+    ring[0], ring[1], *got = lax.optimization_barrier((ring[0], ring[1], *spread(queries)))
+    queries = jnp.concatenate([queries[0]] + got, axis=0)
     others = send(queries, dy=1)
-    half = keyvals.shape[0] // 2
-    far = [send(near[0][:half], dz=1), send(near[1][half:], dz=3)]
-    across = [send(piece, dc=1) for piece in near]
-    *far, across[0], across[1], others = lax.optimization_barrier((*far, *across, others))
-    far = jnp.concatenate(far, axis=0)
-    pieces = [keyvals, beside] + near + across + [far, send(far, dc=1)]
+    ring[2], others = lax.optimization_barrier((ring[2], others))
+    pieces = [keyvals, beside] + ring + [send(piece, dc=1) for piece in ring]
     other, inverse = attend(ids, logit_scale, others, pieces)
     other = send(other, dy=1)
     own = attend(ids, logit_scale, queries, pieces, inverses=[inverse])[0]
@@ -687,17 +757,17 @@
     sent = swap(output(ids, heads, out_weight, False, BF16))
     kept = output(ids, heads, out_weight, True, F32)
     half = decoder_weight.shape[1]
-    split = 2 * TILE
+    split = TILE
     inputs, early = decode_first(ids, kept, sent, encoded, decoder_weight, split)
     early = swap(early)
     late = decode(ids, inputs, decoder_weight, False, split, half - split, BF16)
     late, inputs = lax.optimization_barrier((late, inputs))
     late = swap(late)
     kept = decode(ids, inputs, decoder_weight, True, 0, half, F32)
-    decoded, early, paired = slopes(ids, kept, early, inputs, grad_out, before, after, 0)
+    decoded, early, paired = slopes(ids, kept, early, inputs, grad_out, *halo, 0)
     early_back = swap(early)
     decoded, late, rest = slopes(
-        ids, kept, late, inputs, grad_out, before, after, split, (decoded,)
+        ids, kept, late, inputs, grad_out, *halo, split, (decoded,)
     )
     late_back = swap(late)
     total = backward(

time: 129 us -> 132 us (1.023)
  local copies, waits for them, and re-layouts: 6.06 us -> 0.13 us
  waiting for transfers between devices: 38 us -> 42.1 us
  Pallas kernels: 42.8 us -> 45.2 us
  starting transfers between devices: 41.1 us -> 43.4 us
    unnamed x23 -> x18, local copies, waits for them, and re-layouts: 5.95 us -> 0.09 us
    ppermute x20 -> x19, starting transfers between devices: 26.4 us -> 29.6 us  [send(): return lax.ppermute(value, 'seq', moves(**step))]
    ppermute x20 -> x19, waiting for transfers between devices: 24.1 us -> 27.3 us  [send(): return lax.ppermute(value, 'seq', moves(**step))]
    pallas_call x3, Pallas kernels: 9.98 us -> 12.7 us  [the longest x1 6.74 us: encode(): pl.pallas_call(encode_kernel, in_specs=[SM, VM, HBM, HBM], out_specs=[VM]...]
    ppermute x6 -> x7, waiting for transfers between devices: 13.9 us -> 14.8 us  [swap(): return lax.ppermute(value, 'head', [(0, 1), (1, 0)])]
    ppermute x6 -> x7, starting transfers between devices: 14 us -> 13.2 us  [swap(): return lax.ppermute(value, 'head', [(0, 1), (1, 0)])]
  transfers between devices with their start and end apart: 27 -> 27, of which waited for: 15 -> 16; matrix products, arithmetic and copies ran while one was open for 0% -> 0% of each run, Pallas kernels for 18% -> 18%
where the time goes in v9:
time: 132 us
  Pallas kernels  45.2 us (34%)
  starting transfers between devices  43.4 us (33%)
  waiting for transfers between devices  42.1 us (32%)
    ppermute x19, starting transfers between devices, send(): return lax.ppermute(value, 'seq', moves(**step))  29.6 us
    ppermute x19, waiting for transfers between devices, send(): return lax.ppermute(value, 'seq', moves(**step))  27.3 us
    ppermute x7, waiting for transfers between devices, swap(): return lax.ppermute(value, 'head', [(0, 1), (1, 0)])  14.8 us
    ppermute x7, starting transfers between devices, swap(): return lax.ppermute(value, 'head', [(0, 1), (1, 0)])  13.2 us
    pallas_call x2, Pallas kernels, attend(): pl.pallas_call(functools.partial(attend_kernel, len(pieces), len(inverses...  10.6 us
    pallas_call x1, Pallas kernels, encode(): pl.pallas_call(encode_kernel, in_specs=[SM, VM, HBM, HBM], out_specs=[VM]...  6.74 us
    pallas_call x3, Pallas kernels, backward(): pl.pallas_call(functools.partial(backward_kernel, mine, [first for first,...  6.56 us
    pallas_call x2, Pallas kernels, decode(): pl.pallas_call(functools.partial(decode_kernel, mine, first), in_specs=[S...  4.32 us
  transfers between devices with their start and end apart: 27, of which 16 were waited for; matrix products, arithmetic and copies ran while one was open for 0% of the time, Pallas kernels for 18%

profile of v9, /device:TPU:0, one launch (start us, length us, event | category | flops | bytes accessed | tf_op | source)
XLA Modules:
  0.0 131.8 jit_solution(18077703555096573787)
XLA Ops:
  0.6 0.1 pad_add_fusion.ids
  0.7 1.4 %prepare.1 = (bf16[128,128]{1,0:T(8,128)(2,1)S(1)}, bf16[8,1664]{1,0:T(8,128)(2,1)S(1)}, bf16[8,1664]{1,0:T(8,128)(2,1)S(1)}) custom-call(s32[3]{0:T(128)S(1)} %pad_add_fusion.ids, s32[128,128]{1,0:T(8,128)} %bitcast.6, bf16[256,1536]{1,0:T(8,128)(2,1)} %grad.5), custom_call_target="tpu_custom_call" | custom-call | flops 100000 | bytes 100000 | tf_op jit(solution)/shard_map/prepare/pallas_call | solution.py:111
  2.2 6.7 %encode.1 = (bf16[256,768]{1,0:T(8,128)(2,1)S(1)}, bf16[256,1536]{1,0:T(8,128)(2,1)S(1)}, bf16[3,1536,768]{2,1,0:T(8,128)(2,1)S(1)}) custom-call(s32[3]{0:T(128)S(1)} %pad_add_fusion.ids, bf16[128,128]{1,0:T(8,128)(2,1)S(1)} %get-tuple-element.49.codes, bf16[256,1536]{1,0:T(8,128)(2,1)} %stems.1, bf16[3,1536,768]{2,1,0:T(8,128)(2,1)} %weights.1), custom_call_target="tpu_custom_call" | custom-call | flops 1811939328 | bytes 14155776 | tf_op jit(solution)/shard_map/encode/pallas_call | solution.py:196
  8.9 3.4 %collective-permute-start.2 = (bf16[256,768]{1,0:T(8,128)(2,1)S(1)}, bf16[256,768]{1,0:T(8,128)(2,1)S(1)}, u32[]{:S(2)}, u32[]{:S(2)}) collective-permute-start(bf16[256,768]{1,0:T(8,128)(2,1)S(1)} %get-tuple-element.50.mine), channel_id=1, source_target_pairs={{0,1},{1,0},{2,3},{3,2},{4,5},{5,4},{6,7},{7,6},{8,9},{9,8},{10,11... | collective-permute-start | bytes 1179656 | tf_op jit(solution)/shard_map/ppermute | solution.py:698
  12.3 0.7 collective-permute-start.1
  12.9 0.5 collective-permute-done.near
  13.5 0.0 collective-permute-done.1.far
  13.5 3.9 %encode_edges.1 = (bf16[32,768]{1,0:T(8,128)(2,1)S(1)}, bf16[3,1536,768]{2,1,0:T(8,128)(2,1)S(1)}) custom-call(s32[3]{0:T(128)S(1)} %pad_add_fusion.ids, bf16[128,128]{1,0:T(8,128)(2,1)S(1)} %get-tuple-element.49.codes, bf16[8,1664]{1,0:T(8,128)(2,1)S(1)} %collective-permute-done.near, bf16[8,1664]{1,0:T(8,128)(2,1)S(1)} %collective-permute-done.1.far, ...), custom_call_target="tpu_custom_call" | custom-call | flops 1811939328 | bytes 14155776 | tf_op jit(solution)/shard_map/encode_edges/pallas_call | solution.py:239
  17.4 0.3 collective-permute-start.3
  17.7 5.6 %collective-permute-done.3.their_edges = bf16[32,768]{1,0:T(8,128)(2,1)S(1)} collective-permute-done((bf16[32,768]{1,0:T(8,128)(2,1)S(1)}, bf16[32,768]{1,0:T(8,128)(2,1)S(1)}, u32[]{:S(2)}, u32[]{:S(2)}) %collective-permute-start.3) | collective-permute-done | bytes 49184 | tf_op jit(solution)/shard_map/ppermute | solution.py:698
  23.3 2.1 %project_keys.1 = (bf16[272,768]{1,0:T(8,128)(2,1)S(1)}, bf16[2,136,768]{2,1,0:T(8,128)(2,1)S(1)}, bf16[128,384]{1,0:T(8,128)(2,1)S(1)}, bf16[128,384]{1,0:T(8,1...) custom-call(s32[3]{0:T(128)S(1)} %pad_add_fusion.ids, ...), custom_call_target="tpu_custom_call" | custom-call | flops 641728512 | bytes 7077888 | tf_op jit(solution)/shard_map/project_keys/pallas_call | solution.py:314
  25.4 8.3 %collective-permute-start.4 = (bf16[128,384]{1,0:T(8,128)(2,1)S(1)}, bf16[128,384]{1,0:T(8,128)(2,1)S(1)}, u32[]{:S(2)}, u32[]{:S(2)}) collective-permute-start(bf16[128,384]{1,0:T(8,128)(2,1)S(1)} %get-tuple-element.58), channel_id=1, source_target_pairs={{0,32},{2,34},{4,36},{6,38},{8,40},{10,42},{12,44},{14,46},{16,48}... | collective-permute-start | bytes 294920 | tf_op jit(solution)/shard_map/ppermute | solution.py:702
  33.8 1.3 %collective-permute-start.5 = (bf16[128,384]{1,0:T(8,128)(2,1)S(1)}, bf16[128,384]{1,0:T(8,128)(2,1)S(1)}, u32[]{:S(2)}, u32[]{:S(2)}) collective-permute-start(bf16[128,384]{1,0:T(8,128)(2,1)S(1)} %get-tuple-element.59), channel_id=1, source_target_pairs={{0,96},{2,98},{4,100},{6,102},{8,104},{10,106},{12,108},{14,110},{... | collective-permute-start | bytes 294920 | tf_op jit(solution)/shard_map/ppermute | solution.py:702
  35.1 2.2 %collective-permute-start.6 = (bf16[128,384]{1,0:T(8,128)(2,1)S(1)}, bf16[128,384]{1,0:T(8,128)(2,1)S(1)}, u32[]{:S(2)}, u32[]{:S(2)}) collective-permute-start(bf16[128,384]{1,0:T(8,128)(2,1)S(1)} %get-tuple-element.60), channel_id=1, source_target_pairs={{0,64},{2,66},{4,68},{6,70},{8,72},{10,74},{12,76},{14,78},{16,80}... | collective-permute-start | bytes 294920 | tf_op jit(solution)/shard_map/ppermute | solution.py:702
  37.3 1.1 collective-permute-done.4
  38.4 2.0 %collective-permute-done.5 = bf16[128,384]{1,0:T(8,128)(2,1)S(1)} collective-permute-done((bf16[128,384]{1,0:T(8,128)(2,1)S(1)}, bf16[128,384]{1,0:T(8,128)(2,1)S(1)}, u32[]{:S(2)}, u32[]{:S(2)}) %collective-permute-start.5) | collective-permute-done | bytes 98336 | tf_op jit(solution)/shard_map/ppermute | solution.py:702
  40.4 1.6 %collective-permute-done.6 = bf16[128,384]{1,0:T(8,128)(2,1)S(1)} collective-permute-done((bf16[128,384]{1,0:T(8,128)(2,1)S(1)}, bf16[128,384]{1,0:T(8,128)(2,1)S(1)}, u32[]{:S(2)}, u32[]{:S(2)}) %collective-permute-start.6) | collective-permute-done | bytes 98336 | tf_op jit(solution)/shard_map/ppermute | solution.py:702
  42.0 0.1 collective-permute-start.7
  42.1 2.9 %collective-permute-start.8 = (bf16[512,384]{1,0:T(8,128)(2,1)S(1)}, bf16[512,384]{1,0:T(8,128)(2,1)S(1)}, u32[]{:S(2)}, u32[]{:S(2)}) collective-permute-start(bf16[512,384]{1,0:T(8,128)(2,1)S(1)} %constant_dynamic-update-slice_fusion.refs_0_), channel_id=1, source_target_pairs={{0,8},{2,10},{4,12},{6,14},{8,16},{10,18},{12,20},{14,22},{16,24},... | collective-permute-start | bytes 1179656 | tf_op jit(solution)/shard_map/ppermute | solution.py:702
  45.0 1.9 %collective-permute-start.9 = (bf16[512,384]{1,0:T(8,128)(2,1)S(1)}, bf16[512,384]{1,0:T(8,128)(2,1)S(1)}, u32[]{:S(2)}, u32[]{:S(2)}) collective-permute-start(bf16[512,384]{1,0:T(8,128)(2,1)S(1)} %constant_dynamic-update-slice_fusion.refs_0_), channel_id=1, source_target_pairs={{0,24},{2,26},{4,28},{6,30},{8,0},{10,2},{12,4},{14,6},{16,8},{18,... | collective-permute-start | bytes 1179656 | tf_op jit(solution)/shard_map/ppermute | solution.py:702
  46.9 0.0 collective-permute-done.7.refs_1_
  46.9 1.3 project_queries.1
  48.2 1.0 collective-permute-start.10
  49.2 2.3 %collective-permute-start.11 = (bf16[136,256]{1,0:T(8,128)(2,1)S(1)}, bf16[136,256]{1,0:T(8,128)(2,1)S(1)}, u32[]{:S(2)}, u32[]{:S(2)}) collective-permute-start(bf16[136,256]{1,0:T(8,128)(2,1)S(1)} %get-tuple-element.69), channel_id=1, source_target_pairs={{0,96},{2,98},{4,100},{6,102},{8,104},{10,106},{12,108},{14,110},{... | collective-permute-start | bytes 208904 | tf_op jit(solution)/shard_map/ppermute | solution.py:702
  51.5 0.9 collective-permute-start.12
  52.4 4.1 %collective-permute-done.8.refs_2_ = bf16[512,384]{1,0:T(8,128)(2,1)S(1)} collective-permute-done((bf16[512,384]{1,0:T(8,128)(2,1)S(1)}, bf16[512,384]{1,0:T(8,128)(2,1)S(1)}, u32[]{:S(2)}, u32[]{:S(2)}) %collective-permute-start.8) | collective-permute-done | bytes 393248 | tf_op jit(solution)/shard_map/ppermute | solution.py:702
  56.5 1.9 %collective-permute-start.13 = (bf16[512,384]{1,0:T(8,128)(2,1)S(1)}, bf16[512,384]{1,0:T(8,128)(2,1)S(1)}, u32[]{:S(2)}, u32[]{:S(2)}) collective-permute-start(bf16[512,384]{1,0:T(8,128)(2,1)S(1)} %constant_dynamic-update-slice_fusion.refs_0_), channel_id=1, source_target_pairs={{0,16},{2,18},{4,20},{6,22},{8,24},{10,26},{12,28},{14,30},{16,0},... | collective-permute-start | bytes 1179656 | tf_op jit(solution)/shard_map/ppermute | solution.py:702
  58.4 0.0 collective-permute-done.11
  58.5 0.0 copy-start
  58.5 1.4 %collective-permute-start.14 = (bf16[544,256]{1,0:T(8,128)(2,1)S(1)}, bf16[544,256]{1,0:T(8,128)(2,1)S(1)}, u32[]{:S(2)}, u32[]{:S(2)}) collective-permute-start(bf16[544,256]{1,0:T(8,128)(2,1)S(1)} %constant_dynamic-update-slice_fusion.4.queries), channel_id=1, source_target_pairs={{0,4},{2,6},{4,0},{6,2},{8,12},{10,14},{12,8},{14,10},{16,20},{18,... | collective-permute-start | bytes 835592 | tf_op jit(solution)/shard_map/ppermute | solution.py:702
  59.9 0.5 collective-permute-start.16
  60.4 8.5 %collective-permute-done.13.refs_4_ = bf16[512,384]{1,0:T(8,128)(2,1)S(1)} collective-permute-done((bf16[512,384]{1,0:T(8,128)(2,1)S(1)}, bf16[512,384]{1,0:T(8,128)(2,1)S(1)}, u32[]{:S(2)}, u32[]{:S(2)}) %collective-permute-start.13) | collective-permute-done | bytes 393248 | tf_op jit(solution)/shard_map/ppermute | solution.py:702
  68.9 0.0 collective-permute-start.17
  68.9 1.7 %collective-permute-done.17.refs_7_ = bf16[512,384]{1,0:T(8,128)(2,1)S(1)} collective-permute-done((bf16[512,384]{1,0:T(8,128)(2,1)S(1)}, bf16[512,384]{1,0:T(8,128)(2,1)S(1)}, u32[]{:S(2)}, u32[]{:S(2)}) %collective-permute-start.17) | collective-permute-done | bytes 393248 | tf_op jit(solution)/shard_map/ppermute | solution.py:702
  70.6 5.9 %attend.2 = (bf16[544,256]{1,0:T(8,128)(2,1)S(1)}, f32[8,4096]{1,0:T(8,128)S(1)}) custom-call(s32[3]{0:T(128)S(1)} %pad_add_fusion.ids, f32[4]{0:T(128)S(1)} %copy-done.2, bf16[544,256]{1,0:T(8,128)(2,1)S(1)} %collective-permute-done.14.queries, bf16[512,384]{1,0:T(8,128)(2,1)S(1)} %constant_dynamic-update-slice_fusion.refs_0_, ...), custom_call_target="tpu_custom_call" | custom-call | flops 2281701376 | bytes 4456448 | tf_op jit(solution)/shard_map/attend/pallas_call | solution.py:464
  76.5 1.2 collective-permute-start.18
  77.7 4.8 %attend.3.a0 = bf16[544,256]{1,0:T(8,128)(2,1)S(1)} custom-call(s32[3]{0:T(128)S(1)} %pad_add_fusion.ids, f32[4]{0:T(128)S(1)} %copy-done.2, bf16[544,256]{1,0:T(8,128)(2,1)S(1)} %constant_dynamic-update-slice_fusion.4.queries, bf16[512,384]{1,0:T(8,128)(2,1)S(1)} %constant_dynamic-update-slice_fusion.refs_0_, ...), custom_call_target="tpu_custom_call" | custom-call | flops 2281701376 | bytes 4456448 | tf_op jit(solution)/shard_map/attend/pallas_call | solution.py:464
  82.5 2.8 %collective-permute-done.18.a1 = bf16[544,256]{1,0:T(8,128)(2,1)S(1)} collective-permute-done((bf16[544,256]{1,0:T(8,128)(2,1)S(1)}, bf16[544,256]{1,0:T(8,128)(2,1)S(1)}, u32[]{:S(2)}, u32[]{:S(2)}) %collective-permute-start.18) | collective-permute-done | bytes 278560 | tf_op jit(solution)/shard_map/ppermute | solution.py:702
  85.3 0.5 merge.1
  85.9 1.9 %collective-permute-start.19 = (bf16[136,256]{1,0:T(8,128)(2,1)S(1)}, bf16[136,256]{1,0:T(8,128)(2,1)S(1)}, u32[]{:S(2)}, u32[]{:S(2)}) collective-permute-start(bf16[136,256]{1,0:T(8,128)(2,1)S(1)} %get-tuple-element.82), channel_id=1, source_target_pairs={{0,96},{2,98},{4,100},{6,102},{8,104},{10,106},{12,108},{14,110},{... | collective-permute-start | bytes 208904 | tf_op jit(solution)/shard_map/ppermute | solution.py:702
  87.7 1.2 collective-permute-start.20
  88.9 0.5 collective-permute-start.21
  89.5 1.1 collective-permute-done.19.a1
  90.5 3.0 %collective-permute-done.20.a2 = bf16[136,256]{1,0:T(8,128)(2,1)S(1)} collective-permute-done((bf16[136,256]{1,0:T(8,128)(2,1)S(1)}, bf16[136,256]{1,0:T(8,128)(2,1)S(1)}, u32[]{:S(2)}, u32[]{:S(2)}) %collective-permute-start.20) | collective-permute-done | bytes 69664 | tf_op jit(solution)/shard_map/ppermute | solution.py:702
  93.6 0.9 collective-permute-done.21.a3
  94.4 1.3 output.3
  95.7 2.2 %collective-permute-start.22 = (bf16[136,768]{1,0:T(8,128)(2,1)S(1)}, bf16[136,768]{1,0:T(8,128)(2,1)S(1)}, u32[]{:S(2)}, u32[]{:S(2)}) collective-permute-start(bf16[136,768]{1,0:T(8,128)(2,1)S(1)} %output.3), channel_id=1, source_target_pairs={{0,1},{1,0},{2,3},{3,2},{4,5},{5,4},{6,7},{7,6},{8,9},{9,8},{10,11... | collective-permute-start | bytes 626696 | tf_op jit(solution)/shard_map/ppermute | solution.py:698
  97.9 1.3 output.2.own
  99.2 3.9 %collective-permute-done.22.other = bf16[136,768]{1,0:T(8,128)(2,1)S(1)} collective-permute-done((bf16[136,768]{1,0:T(8,128)(2,1)S(1)}, bf16[136,768]{1,0:T(8,128)(2,1)S(1)}, u32[]{:S(2)}, u32[]{:S(2)}) %collective-permute-start.22) | collective-permute-done | bytes 208928 | tf_op jit(solution)/shard_map/ppermute | solution.py:698
  103.1 1.2 decode_first.1
  104.4 2.4 %collective-permute-start.24 = (bf16[272,256]{1,0:T(8,128)(2,1)S(1)}, bf16[272,256]{1,0:T(8,128)(2,1)S(1)}, u32[]{:S(2)}, u32[]{:S(2)}) collective-permute-start(bf16[272,256]{1,0:T(8,128)(2,1)S(1)} %get-tuple-element.89), channel_id=1, source_target_pairs={{0,1},{1,0},{2,3},{3,2},{4,5},{5,4},{6,7},{7,6},{8,9},{9,8},{10,11... | collective-permute-start | bytes 417800 | tf_op jit(solution)/shard_map/ppermute | solution.py:698
  106.8 2.3 %decode.2 = bf16[272,512]{1,0:T(8,128)(2,1)} custom-call(s32[3]{0:T(128)S(1)} %pad_add_fusion.ids, bf16[272,768]{1,0:T(8,128)(2,1)S(1)} %get-tuple-element.87.inputs, bf16[3,768,1536]{2,1,0:T(8,128)(2,1)S(1)} %bitcast.5), custom_call_target="tpu_custom_call" | custom-call | flops 1000000 | bytes 10000 | tf_op jit(solution)/shard_map/decode/pallas_call | solution.py:577
  109.1 1.4 %collective-permute-start.23 = (bf16[272,512]{1,0:T(8,128)(2,1)}, bf16[272,512]{1,0:T(8,128)(2,1)}, u32[]{:S(2)}, u32[]{:S(2)}) collective-permute-start(bf16[272,512]{1,0:T(8,128)(2,1)} %decode.2), channel_id=1, source_target_pairs={{0,1},{1,0},{2,3},{3,2},{4,5},{5,4},{6,7},{7,6},{8,9},{9,8},{10,11... | collective-permute-start | bytes 835592 | tf_op jit(solution)/shard_map/ppermute | solution.py:698
  110.5 2.1 %decode.3.own = f32[272,768]{1,0:T(8,128)S(1)} custom-call(s32[3]{0:T(128)S(1)} %pad_add_fusion.ids, bf16[272,768]{1,0:T(8,128)(2,1)S(1)} %get-tuple-element.87.inputs, bf16[3,768,1536]{2,1,0:T(8,128)(2,1)S(1)} %bitcast.5), custom_call_target="tpu_custom_call" | custom-call | flops 1000000 | bytes 10000 | tf_op jit(solution)/shard_map/decode/pallas_call | solution.py:577
  112.5 0.2 collective-permute-done.24.other
  112.7 1.5 %slopes.2 = (bf16[256,256]{1,0:T(8,128)(2,1)S(1)}, bf16[272,256]{1,0:T(8,128)(2,1)}, f32[128,256]{1,0:T(8,128)S(1)}) custom-call(s32[3]{0:T(128)S(1)} %pad_add_fusion.ids, f32[272,768]{1,0:T(8,128)S(1)} %decode.3.own, bf16[272,256]{1,0:T(8,128)(2,1)S(1)} %collective-permute-done.24.other, bf16[272,768]{1,0:T(8,128)(2,1)S(1)} %get-tuple-element.87.inputs, ...), custom_call_target="tpu_custom_call" | custom-call | flops 208896000000 | bytes 974848 | tf_op jit(solution)/shard_map/slopes/pallas_call | solution.py:626
  114.2 2.1 %collective-permute-start.26 = (bf16[272,256]{1,0:T(8,128)(2,1)}, bf16[272,256]{1,0:T(8,128)(2,1)}, u32[]{:S(2)}, u32[]{:S(2)}) collective-permute-start(bf16[272,256]{1,0:T(8,128)(2,1)} %get-tuple-element.93.refs_0_), channel_id=1, source_target_pairs={{0,1},{1,0},{2,3},{3,2},{4,5},{5,4},{6,7},{7,6},{8,9},{9,8},{10,11... | collective-permute-start | bytes 417800 | tf_op jit(solution)/shard_map/ppermute | solution.py:698
  116.3 2.6 %collective-permute-done.23.other = bf16[272,512]{1,0:T(8,128)(2,1)} collective-permute-done((bf16[272,512]{1,0:T(8,128)(2,1)}, bf16[272,512]{1,0:T(8,128)(2,1)}, u32[]{:S(2)}, u32[]{:S(2)}) %collective-permute-start.23) | collective-permute-done | bytes 278560 | tf_op jit(solution)/shard_map/ppermute | solution.py:698
  118.9 2.4 %slopes.3 = (bf16[256,768]{1,0:T(8,128)(2,1)}, bf16[272,512]{1,0:T(8,128)(2,1)S(1)}, f32[128,512]{1,0:T(8,128)S(1)}) custom-call(s32[3]{0:T(128)S(1)} %pad_add_fusion.ids, f32[272,768]{1,0:T(8,128)S(1)} %decode.3.own, bf16[272,512]{1,0:T(8,128)(2,1)} %collective-permute-done.23.other, bf16[272,768]{1,0:T(8,128)(2,1)S(1)} %get-tuple-element.87.inputs, ...), custom_call_target="tpu_custom_call" | custom-call | flops 417792000000 | bytes 1949696 | tf_op jit(solution)/shard_map/slopes/pallas_call | solution.py:626
  121.3 1.4 %collective-permute-start.25 = (bf16[272,512]{1,0:T(8,128)(2,1)S(1)}, bf16[272,512]{1,0:T(8,128)(2,1)S(1)}, u32[]{:S(2)}, u32[]{:S(2)}) collective-permute-start(bf16[272,512]{1,0:T(8,128)(2,1)S(1)} %get-tuple-element.92.refs_1_), channel_id=1, source_target_pairs={{0,1},{1,0},{2,3},{3,2},{4,5},{5,4},{6,7},{7,6},{8,9},{9,8},{10,11... | collective-permute-start | bytes 835592 | tf_op jit(solution)/shard_map/ppermute | solution.py:698
  122.7 2.6 %backward.3.refs_1_ = f32[128,768]{1,0:T(8,128)S(1)} custom-call(s32[3]{0:T(128)S(1)} %pad_add_fusion.ids, bf16[272,256]{1,0:T(8,128)(2,1)} %get-tuple-element.93.refs_0_, bf16[272,512]{1,0:T(8,128)(2,1)S(1)} %get-tuple-element.92.refs_1_, f32[128,256]{1,0:T(8,128)S(1)} %get-tuple-element.94.refs_2_, f32[128,512]{1,0:T(8,128)S(1)} %get-tuple-element.95.refs_3_, ...), custom_call_target="tpu_custom_call" | custom-call | flops 96259276800 | bytes 1253376 | tf_op jit(solution)/shard_map/backward/pallas_call | solution.py:673
  125.3 1.5 %backward.4.refs_1_ = f32[128,768]{1,0:T(8,128)S(1)} custom-call(s32[3]{0:T(128)S(1)} %pad_add_fusion.ids, bf16[272,256]{1,0:T(8,128)(2,1)} %collective-permute-done.26.refs_0_, f32[128,768]{1,0:T(8,128)S(1)} %backward.3.refs_1_, bf16[3,768,1536]{2,1,0:T(8,128)(2,1)S(1)} %bitcast.5), custom_call_target="tpu_custom_call" | custom-call | flops 32086425600 | bytes 417792 | tf_op jit(solution)/shard_map/backward/pallas_call | solution.py:673
  126.8 2.5 %collective-permute-done.25.refs_0_ = bf16[272,512]{1,0:T(8,128)(2,1)S(1)} collective-permute-done((bf16[272,512]{1,0:T(8,128)(2,1)S(1)}, bf16[272,512]{1,0:T(8,128)(2,1)S(1)}, u32[]{:S(2)}, u32[]{:S(2)}) %collective-permute-start.25) | collective-permute-done | bytes 278560 | tf_op jit(solution)/shard_map/ppermute | solution.py:698
  129.3 2.5 %backward.5 = bf16[128,768]{1,0:T(8,128)(2,1)} custom-call(s32[3]{0:T(128)S(1)} %pad_add_fusion.ids, bf16[272,512]{1,0:T(8,128)(2,1)S(1)} %collective-permute-done.25.refs_0_, f32[128,768]{1,0:T(8,128)S(1)} %backward.4.refs_1_, bf16[3,768,1536]{2,1,0:T(8,128)(2,1)S(1)} %bitcast.5), custom_call_target="tpu_custom_call" | custom-call | flops 64172851200 | bytes 835584 | tf_op jit(solution)/shard_map/backward/pallas_call | solution.py:673
  (31 shorter events, 0.1 us)
Async XLA Ops:
  8.9 14.4 %collective-permute-start.2 = (bf16[256,768]{1,0:T(8,128)(2,1)S(1)}, bf16[256,768]{1,0:T(8,128)(2,1)S(1)}, u32[]{:S(2)}, u32[]{:S(2)}) collective-permute-start(bf16[256,768]{1,0:T(8,128)(2,1)S(1)} %get-tuple-element.50.mine), channel_id=1, source_target_pairs={{0,1},{1,0},{2,3},{3,2},{4,5},{5,4},{6,7},{7,6},{8,9},{9,8},{10,11... | collective-permute-start | bytes 1179656 | tf_op jit(solution)/shard_map/ppermute | solution.py:698
  12.3 1.2 collective-permute-start
  12.3 1.2 collective-permute-start.1
  13.5 4.2 %copy-start.3 = (f32[1536]{0:T(1024)S(1)}, f32[1536]{0:T(1024)}, u32[]{:S(2)}) copy-start(f32[1536]{0:T(1024)} %param.12) | copy-start | bytes 18436
  17.4 6.0 %collective-permute-start.3 = (bf16[32,768]{1,0:T(8,128)(2,1)S(1)}, bf16[32,768]{1,0:T(8,128)(2,1)S(1)}, u32[]{:S(2)}, u32[]{:S(2)}) collective-permute-start(bf16[32,768]{1,0:T(8,128)(2,1)S(1)} %get-tuple-element.55.mine_edges), channel_id=1, source_target_pairs={{0,1},{1,0},{2,3},{3,2},{4,5},{5,4},{6,7},{7,6},{8,9},{9,8},{10,11... | collective-permute-start | bytes 147464 | tf_op jit(solution)/shard_map/ppermute | solution.py:698
  23.3 47.3 %copy-start.2 = (f32[4]{0:T(128)S(1)}, f32[4]{0:T(128)}, u32[]{:S(2)}) copy-start(f32[4]{0:T(128)} %scale.3) | copy-start | bytes 52
  25.4 13.0 %collective-permute-start.4 = (bf16[128,384]{1,0:T(8,128)(2,1)S(1)}, bf16[128,384]{1,0:T(8,128)(2,1)S(1)}, u32[]{:S(2)}, u32[]{:S(2)}) collective-permute-start(bf16[128,384]{1,0:T(8,128)(2,1)S(1)} %get-tuple-element.58), channel_id=1, source_target_pairs={{0,32},{2,34},{4,36},{6,38},{8,40},{10,42},{12,44},{14,46},{16,48}... | collective-permute-start | bytes 294920 | tf_op jit(solution)/shard_map/ppermute | solution.py:702
  33.8 6.6 %collective-permute-start.5 = (bf16[128,384]{1,0:T(8,128)(2,1)S(1)}, bf16[128,384]{1,0:T(8,128)(2,1)S(1)}, u32[]{:S(2)}, u32[]{:S(2)}) collective-permute-start(bf16[128,384]{1,0:T(8,128)(2,1)S(1)} %get-tuple-element.59), channel_id=1, source_target_pairs={{0,96},{2,98},{4,100},{6,102},{8,104},{10,106},{12,108},{14,110},{... | collective-permute-start | bytes 294920 | tf_op jit(solution)/shard_map/ppermute | solution.py:702
  35.1 6.8 %collective-permute-start.6 = (bf16[128,384]{1,0:T(8,128)(2,1)S(1)}, bf16[128,384]{1,0:T(8,128)(2,1)S(1)}, u32[]{:S(2)}, u32[]{:S(2)}) collective-permute-start(bf16[128,384]{1,0:T(8,128)(2,1)S(1)} %get-tuple-element.60), channel_id=1, source_target_pairs={{0,64},{2,66},{4,68},{6,70},{8,72},{10,74},{12,76},{14,78},{16,80}... | collective-permute-start | bytes 294920 | tf_op jit(solution)/shard_map/ppermute | solution.py:702
  42.0 4.9 %collective-permute-start.7 = (bf16[512,384]{1,0:T(8,128)(2,1)S(1)}, bf16[512,384]{1,0:T(8,128)(2,1)S(1)}, u32[]{:S(2)}, u32[]{:S(2)}) collective-permute-start(bf16[512,384]{1,0:T(8,128)(2,1)S(1)} %constant_dynamic-update-slice_fusion.refs_0_), channel_id=1, source_target_pairs={{0,2},{2,0},{4,6},{6,4},{8,10},{10,8},{12,14},{14,12},{16,18},{18,... | collective-permute-start | bytes 1179656 | tf_op jit(solution)/shard_map/ppermute | solution.py:702
  42.1 14.4 %collective-permute-start.8 = (bf16[512,384]{1,0:T(8,128)(2,1)S(1)}, bf16[512,384]{1,0:T(8,128)(2,1)S(1)}, u32[]{:S(2)}, u32[]{:S(2)}) collective-permute-start(bf16[512,384]{1,0:T(8,128)(2,1)S(1)} %constant_dynamic-update-slice_fusion.refs_0_), channel_id=1, source_target_pairs={{0,8},{2,10},{4,12},{6,14},{8,16},{10,18},{12,20},{14,22},{16,24},... | collective-permute-start | bytes 1179656 | tf_op jit(solution)/shard_map/ppermute | solution.py:702
  45.0 13.4 %collective-permute-start.9 = (bf16[512,384]{1,0:T(8,128)(2,1)S(1)}, bf16[512,384]{1,0:T(8,128)(2,1)S(1)}, u32[]{:S(2)}, u32[]{:S(2)}) collective-permute-start(bf16[512,384]{1,0:T(8,128)(2,1)S(1)} %constant_dynamic-update-slice_fusion.refs_0_), channel_id=1, source_target_pairs={{0,24},{2,26},{4,28},{6,30},{8,0},{10,2},{12,4},{14,6},{16,8},{18,... | collective-permute-start | bytes 1179656 | tf_op jit(solution)/shard_map/ppermute | solution.py:702
  48.2 10.2 %collective-permute-start.10 = (bf16[136,256]{1,0:T(8,128)(2,1)S(1)}, bf16[136,256]{1,0:T(8,128)(2,1)S(1)}, u32[]{:S(2)}, u32[]{:S(2)}) collective-permute-start(bf16[136,256]{1,0:T(8,128)(2,1)S(1)} %get-tuple-element.68), channel_id=1, source_target_pairs={{0,32},{2,34},{4,36},{6,38},{8,40},{10,42},{12,44},{14,46},{16,48}... | collective-permute-start | bytes 208904 | tf_op jit(solution)/shard_map/ppermute | solution.py:702
  49.2 9.3 %collective-permute-start.11 = (bf16[136,256]{1,0:T(8,128)(2,1)S(1)}, bf16[136,256]{1,0:T(8,128)(2,1)S(1)}, u32[]{:S(2)}, u32[]{:S(2)}) collective-permute-start(bf16[136,256]{1,0:T(8,128)(2,1)S(1)} %get-tuple-element.69), channel_id=1, source_target_pairs={{0,96},{2,98},{4,100},{6,102},{8,104},{10,106},{12,108},{14,110},{... | collective-permute-start | bytes 208904 | tf_op jit(solution)/shard_map/ppermute | solution.py:702
  51.5 6.9 %collective-permute-start.12 = (bf16[136,256]{1,0:T(8,128)(2,1)S(1)}, bf16[136,256]{1,0:T(8,128)(2,1)S(1)}, u32[]{:S(2)}, u32[]{:S(2)}) collective-permute-start(bf16[136,256]{1,0:T(8,128)(2,1)S(1)} %get-tuple-element.70), channel_id=1, source_target_pairs={{0,64},{2,66},{4,68},{6,70},{8,72},{10,74},{12,76},{14,78},{16,80}... | collective-permute-start | bytes 208904 | tf_op jit(solution)/shard_map/ppermute | solution.py:702
  56.5 12.4 %collective-permute-start.13 = (bf16[512,384]{1,0:T(8,128)(2,1)S(1)}, bf16[512,384]{1,0:T(8,128)(2,1)S(1)}, u32[]{:S(2)}, u32[]{:S(2)}) collective-permute-start(bf16[512,384]{1,0:T(8,128)(2,1)S(1)} %constant_dynamic-update-slice_fusion.refs_0_), channel_id=1, source_target_pairs={{0,16},{2,18},{4,20},{6,22},{8,24},{10,26},{12,28},{14,30},{16,0},... | collective-permute-start | bytes 1179656 | tf_op jit(solution)/shard_map/ppermute | solution.py:702
  58.5 35.9 %copy-start = (bf16[768,1536]{1,0:T(8,128)(2,1)S(1)}, bf16[768,1536]{1,0:T(8,128)(2,1)}, u32[]{:S(2)}) copy-start(bf16[768,1536]{1,0:T(8,128)(2,1)} %weight.6) | copy-start | bytes 7077892
  58.5 10.4 %collective-permute-start.14 = (bf16[544,256]{1,0:T(8,128)(2,1)S(1)}, bf16[544,256]{1,0:T(8,128)(2,1)S(1)}, u32[]{:S(2)}, u32[]{:S(2)}) collective-permute-start(bf16[544,256]{1,0:T(8,128)(2,1)S(1)} %constant_dynamic-update-slice_fusion.4.queries), channel_id=1, source_target_pairs={{0,4},{2,6},{4,0},{6,2},{8,12},{10,14},{12,8},{14,10},{16,20},{18,... | collective-permute-start | bytes 835592 | tf_op jit(solution)/shard_map/ppermute | solution.py:702
  59.9 9.0 %collective-permute-start.15 = (bf16[512,384]{1,0:T(8,128)(2,1)S(1)}, bf16[512,384]{1,0:T(8,128)(2,1)S(1)}, u32[]{:S(2)}, u32[]{:S(2)}) collective-permute-start(bf16[512,384]{1,0:T(8,128)(2,1)S(1)} %collective-permute-done.8.refs_2_), channel_id=1, source_target_pairs={{0,2},{2,0},{4,6},{6,4},{8,10},{10,8},{12,14},{14,12},{16,18},{18,... | collective-permute-start | bytes 1179656 | tf_op jit(solution)/shard_map/ppermute | solution.py:702
  59.9 9.0 %collective-permute-start.16 = (bf16[512,384]{1,0:T(8,128)(2,1)S(1)}, bf16[512,384]{1,0:T(8,128)(2,1)S(1)}, u32[]{:S(2)}, u32[]{:S(2)}) collective-permute-start(bf16[512,384]{1,0:T(8,128)(2,1)S(1)} %collective-permute-done.9.refs_3_), channel_id=1, source_target_pairs={{0,2},{2,0},{4,6},{6,4},{8,10},{10,8},{12,14},{14,12},{16,18},{18,... | collective-permute-start | bytes 1179656 | tf_op jit(solution)/shard_map/ppermute | solution.py:702
  68.9 1.7 %collective-permute-start.17 = (bf16[512,384]{1,0:T(8,128)(2,1)S(1)}, bf16[512,384]{1,0:T(8,128)(2,1)S(1)}, u32[]{:S(2)}, u32[]{:S(2)}) collective-permute-start(bf16[512,384]{1,0:T(8,128)(2,1)S(1)} %collective-permute-done.13.refs_4_), channel_id=1, source_target_pairs={{0,2},{2,0},{4,6},{6,4},{8,10},{10,8},{12,14},{14,12},{16,18},{18,... | collective-permute-start | bytes 1179656 | tf_op jit(solution)/shard_map/ppermute | solution.py:702
  76.5 8.8 %collective-permute-start.18 = (bf16[544,256]{1,0:T(8,128)(2,1)S(1)}, bf16[544,256]{1,0:T(8,128)(2,1)S(1)}, u32[]{:S(2)}, u32[]{:S(2)}) collective-permute-start(bf16[544,256]{1,0:T(8,128)(2,1)S(1)} %get-tuple-element.80), channel_id=1, source_target_pairs={{0,4},{2,6},{4,0},{6,2},{8,12},{10,14},{12,8},{14,10},{16,20},{18,... | collective-permute-start | bytes 835592 | tf_op jit(solution)/shard_map/ppermute | solution.py:702
  77.7 25.4 %slice-start = ((s8[7077888]{0:T(1024)(128)(4,1)}), s8[4194304]{0:T(1024)(128)(4,1)S(1)}, s32[]{:S(2)}) async-start(s8[7077888]{0:T(1024)(128)(4,1)} %bitcast.4), calls=%async_computation | async-start | bytes 8388608
  77.7 25.4 %slice-start.1 = ((s8[7077888]{0:T(1024)(128)(4,1)}), s8[2883584]{0:T(1024)(128)(4,1)S(1)}, s32[]{:S(2)}) async-start(s8[7077888]{0:T(1024)(128)(4,1)} %bitcast.4), calls=%async_computation.1 | async-start | bytes 5767168
  85.9 4.7 %collective-permute-start.19 = (bf16[136,256]{1,0:T(8,128)(2,1)S(1)}, bf16[136,256]{1,0:T(8,128)(2,1)S(1)}, u32[]{:S(2)}, u32[]{:S(2)}) collective-permute-start(bf16[136,256]{1,0:T(8,128)(2,1)S(1)} %get-tuple-element.82), channel_id=1, source_target_pairs={{0,96},{2,98},{4,100},{6,102},{8,104},{10,106},{12,108},{14,110},{... | collective-permute-start | bytes 208904 | tf_op jit(solution)/shard_map/ppermute | solution.py:702
  87.7 5.8 %collective-permute-start.20 = (bf16[136,256]{1,0:T(8,128)(2,1)S(1)}, bf16[136,256]{1,0:T(8,128)(2,1)S(1)}, u32[]{:S(2)}, u32[]{:S(2)}) collective-permute-start(bf16[136,256]{1,0:T(8,128)(2,1)S(1)} %get-tuple-element.83), channel_id=1, source_target_pairs={{0,64},{2,66},{4,68},{6,70},{8,72},{10,74},{12,76},{14,78},{16,80}... | collective-permute-start | bytes 208904 | tf_op jit(solution)/shard_map/ppermute | solution.py:702
  88.9 5.5 %collective-permute-start.21 = (bf16[136,256]{1,0:T(8,128)(2,1)S(1)}, bf16[136,256]{1,0:T(8,128)(2,1)S(1)}, u32[]{:S(2)}, u32[]{:S(2)}) collective-permute-start(bf16[136,256]{1,0:T(8,128)(2,1)S(1)} %get-tuple-element.84), channel_id=1, source_target_pairs={{0,32},{2,34},{4,36},{6,38},{8,40},{10,42},{12,44},{14,46},{16,48}... | collective-permute-start | bytes 208904 | tf_op jit(solution)/shard_map/ppermute | solution.py:702
  95.7 7.4 %collective-permute-start.22 = (bf16[136,768]{1,0:T(8,128)(2,1)S(1)}, bf16[136,768]{1,0:T(8,128)(2,1)S(1)}, u32[]{:S(2)}, u32[]{:S(2)}) collective-permute-start(bf16[136,768]{1,0:T(8,128)(2,1)S(1)} %output.3), channel_id=1, source_target_pairs={{0,1},{1,0},{2,3},{3,2},{4,5},{5,4},{6,7},{7,6},{8,9},{9,8},{10,11... | collective-permute-start | bytes 626696 | tf_op jit(solution)/shard_map/ppermute | solution.py:698
  104.4 8.3 %collective-permute-start.24 = (bf16[272,256]{1,0:T(8,128)(2,1)S(1)}, bf16[272,256]{1,0:T(8,128)(2,1)S(1)}, u32[]{:S(2)}, u32[]{:S(2)}) collective-permute-start(bf16[272,256]{1,0:T(8,128)(2,1)S(1)} %get-tuple-element.89), channel_id=1, source_target_pairs={{0,1},{1,0},{2,3},{3,2},{4,5},{5,4},{6,7},{7,6},{8,9},{9,8},{10,11... | collective-permute-start | bytes 417800 | tf_op jit(solution)/shard_map/ppermute | solution.py:698
  106.8 5.9 %copy-start.1 = (bf16[256,1536]{1,0:T(8,128)(2,1)S(1)}, bf16[256,1536]{1,0:T(8,128)(2,1)}, u32[]{:S(2)}) copy-start(bf16[256,1536]{1,0:T(8,128)(2,1)} %grad.5) | copy-start | bytes 2359300
  109.1 9.9 %collective-permute-start.23 = (bf16[272,512]{1,0:T(8,128)(2,1)}, bf16[272,512]{1,0:T(8,128)(2,1)}, u32[]{:S(2)}, u32[]{:S(2)}) collective-permute-start(bf16[272,512]{1,0:T(8,128)(2,1)} %decode.2), channel_id=1, source_target_pairs={{0,1},{1,0},{2,3},{3,2},{4,5},{5,4},{6,7},{7,6},{8,9},{9,8},{10,11... | collective-permute-start | bytes 835592 | tf_op jit(solution)/shard_map/ppermute | solution.py:698
  114.2 11.1 %collective-permute-start.26 = (bf16[272,256]{1,0:T(8,128)(2,1)}, bf16[272,256]{1,0:T(8,128)(2,1)}, u32[]{:S(2)}, u32[]{:S(2)}) collective-permute-start(bf16[272,256]{1,0:T(8,128)(2,1)} %get-tuple-element.93.refs_0_), channel_id=1, source_target_pairs={{0,1},{1,0},{2,3},{3,2},{4,5},{5,4},{6,7},{7,6},{8,9},{9,8},{10,11... | collective-permute-start | bytes 417800 | tf_op jit(solution)/shard_map/ppermute | solution.py:698
  121.3 8.1 %collective-permute-start.25 = (bf16[272,512]{1,0:T(8,128)(2,1)S(1)}, bf16[272,512]{1,0:T(8,128)(2,1)S(1)}, u32[]{:S(2)}, u32[]{:S(2)}) collective-permute-start(bf16[272,512]{1,0:T(8,128)(2,1)S(1)} %get-tuple-element.92.refs_1_), channel_id=1, source_target_pairs={{0,1},{1,0},{2,3},{3,2},{4,5},{5,4},{6,7},{7,6},{8,9},{9,8},{10,11... | collective-permute-start | bytes 835592 | tf_op jit(solution)/shard_map/ppermute | solution.py:698

commit v10 on v8

--- a/solution.py
+++ b/solution.py
@@ -70,6 +70,11 @@
     even = above(first[half:], span) + mid[:half] + last[half:]
     odd = first[:half] + mid[half:] + below(last[:half], span)
     return jnp.concatenate([even, odd], axis=0)
+
+
+def sides(ids, near, far):
+    odd = lax.rem(ids[2], 2) == 1
+    return jnp.where(odd, near, far), jnp.where(odd, far, near)
 
 
 def prepare_kernel(ids, bases, grad, codes, near, far, code, head, tail, sems):
@@ -124,44 +129,10 @@
     )(ids, far_memory(bases), far_memory(grad))
 
 
-def load_kernel(*refs):
-    count = len(refs) // 2
-    sources, targets, sems = refs[:count], refs[count : 2 * count], refs[-1]
-    copies = [
-        pltpu.make_async_copy(source, target, sems.at[i])
-        for i, (source, target) in enumerate(zip(sources, targets))
-    ]
-    for copy in copies:
-        copy.start()
-    for copy in copies:
-        copy.wait()
-
-
-def load(*values):
-    return pl.pallas_call(
-        load_kernel,
-        in_specs=[HBM] * len(values),
-        out_specs=[VM] * len(values),
-        out_shape=[pltpu.VMEM(value.shape, value.dtype) for value in values],
-        scratch_shapes=[pltpu.SemaphoreType.DMA((len(values),))],
-        compiler_params=params(2),
-        cost_estimate=cost(10**5, sum(value.size for value in values) * 2),
-        name="load",
-    )(*[far_memory(value) for value in values])
-
-
-def encode_kernel(ids, codes, before, after, stem, weight, ahead, encoded, loaded, embedded, sem):
-    copy = pltpu.make_async_copy(ahead, loaded, sem)
-    copy.start()
+def embed_letters(code, stem, embedded):
     patch = stem.shape[0] // 4
-    feats = stem.shape[1]
-    half = weight.shape[2]
     row = lax.broadcasted_iota(jnp.int32, (2 * patch, 4 * patch), 0)
     col = lax.broadcasted_iota(jnp.int32, (2 * patch, 4 * patch), 1)
-    place = lax.broadcasted_iota(jnp.int32, (ROWS - OWN, 128), 0)
-    halo = jnp.where(place >= 6, before[:, feats:].astype(F32), 0.0)
-    halo = jnp.where(place < 2, after[:, feats:].astype(F32), halo)
-    code = jnp.concatenate([codes[...].astype(F32), halo], axis=0).astype(BF16)
     spread = [
         dot(code, (row == col // 4 + offset).astype(F32).astype(BF16)) for offset in (0, patch)
     ]
@@ -173,19 +144,75 @@
         at = lanes(i * TILE, TILE)
         embedded[:, at] = dot(onehot, stem[:, at]).astype(BF16)
 
-    tiles(feats // TILE, embed)
+    tiles(stem.shape[1] // TILE, embed)
+
+
+def load_kernel(codes, stems, weights, embedded, stem, weight, sems):
+    copies = [
+        pltpu.make_async_copy(stems, stem, sems.at[0]),
+        pltpu.make_async_copy(weights, weight, sems.at[1]),
+    ]
+    for copy in copies:
+        copy.start()
+    copies[0].wait()
+    embed_letters(codes[...], stem, embedded)
+    copies[1].wait()
+
+
+def load(codes, stem, weight):
+    return pl.pallas_call(
+        load_kernel,
+        in_specs=[VM, HBM, HBM],
+        out_specs=[VM] * 3,
+        out_shape=[
+            pltpu.VMEM((2 * OWN, stem.shape[1]), BF16),
+            pltpu.VMEM(stem.shape, BF16),
+            pltpu.VMEM(weight.shape, BF16),
+        ],
+        scratch_shapes=[pltpu.SemaphoreType.DMA((2,))],
+        compiler_params=params(4),
+        cost_estimate=cost(10**5, weight.size * 2),
+        name="load",
+    )(codes, far_memory(stem), far_memory(weight))
+
+
+def ring_order(rows):
+    half = ROWS - OWN
+    return (
+        jnp.concatenate([rows[:OWN], rows[2 * OWN : 2 * OWN + half]], axis=0),
+        jnp.concatenate([rows[OWN : 2 * OWN], rows[2 * OWN + half :]], axis=0),
+    )
+
+
+def encode_kernel(ids, near, far, rows, stem, weight, ahead, encoded, loaded, embedded, halo, sem):
+    copy = pltpu.make_async_copy(ahead, loaded, sem)
+    copy.start()
+    feats = stem.shape[1]
+    half = weight.shape[2]
+    place = lax.broadcasted_iota(jnp.int32, (ROWS - OWN, 128), 0)
+    before, after = sides(ids, near[:, feats:].astype(F32), far[:, feats:].astype(F32))
+    code = jnp.where(place >= 6, before, 0.0)
+    code = jnp.where(place < 2, after, code)
+    embed_letters(code.astype(BF16), stem, halo)
+    embedded[: 2 * OWN, :] = rows[...]
+    embedded[2 * OWN :, :] = halo[...]
 
     def convolve(i):
         at = lanes(i * TILE, TILE)
-        pre = conv_taps(embedded[...], lambda t: weight[t, :, at], ROWS)
+        parts = [dot(embedded[...], weight[tap, :, at]) for tap in range(3)]
+        (first_even, first_odd), (even, odd), (last_even, last_odd) = map(ring_order, parts)
+        even = above(first_odd, ROWS) + even + last_odd
+        odd = first_even + odd + below(last_even, ROWS)
+        pre = jnp.concatenate([even, odd], axis=0)
         mine = embedded[:, lanes(ids[0] * half + i * TILE, TILE)].astype(F32)
+        mine = jnp.concatenate(ring_order(mine), axis=0)
         encoded[:, at] = (mine + 0.5 * pre * (1.0 + gelu_tanh(pre))).astype(BF16)
 
     tiles(half // TILE, convolve)
     copy.wait()
 
 
-def encode(ids, codes, before, after, stem, weight, ahead):
+def encode(ids, near, far, rows, stem, weight, ahead):
     half = weight.shape[2]
     feats = stem.shape[1]
     return pl.pallas_call(
@@ -193,11 +220,23 @@
         in_specs=[SM] + [VM] * 5 + [HBM],
         out_specs=[VM, VM],
         out_shape=[shape((2 * ROWS, half), BF16), pltpu.VMEM(ahead.shape, BF16)],
-        scratch_shapes=[pltpu.VMEM((2 * ROWS, feats), BF16), pltpu.SemaphoreType.DMA(())],
+        scratch_shapes=[
+            pltpu.VMEM((2 * ROWS, feats), BF16),
+            pltpu.VMEM((2 * (ROWS - OWN), feats), BF16),
+            pltpu.SemaphoreType.DMA(()),
+        ],
         compiler_params=params(12),
-        cost_estimate=cost(2 * 2 * ROWS * 3 * feats * half, weight.size * 4),
+        cost_estimate=cost(4 * OWN * weight.size, weight.size * 4),
         name="encode",
-    )(ids, codes, before, after, near_memory(stem), near_memory(weight), far_memory(ahead))
+    )(
+        ids,
+        near,
+        far,
+        near_memory(rows),
+        near_memory(stem),
+        near_memory(weight),
+        far_memory(ahead),
+    )
 
 
 def unpacked(both):
@@ -513,7 +552,7 @@
     )(ids, inputs, weight)
 
 
-def slope_kernel(first, ids, own, other, inputs, grad, before, after, *refs):
+def slope_kernel(first, ids, own, other, inputs, grad, near, far, *refs):
     done, (decoded, slope, paired, wide) = refs[:-4], refs[-4:]
     half = own.shape[1]
     begin = 0
@@ -540,15 +579,16 @@
         odd = wide[1, pl.ds(1, OWN, 2), :]
         paired[:, at] = even + odd
         row = lax.broadcasted_iota(jnp.int32, (ROWS - OWN, 128), 0)
-        even_edge = jnp.where(row == 0, after[:, column].astype(F32), 0.0)
-        odd_edge = jnp.where(row == ROWS - OWN - 1, before[:, column].astype(F32), 0.0)
+        before, after = sides(ids, near[:, column].astype(F32), far[:, column].astype(F32))
+        even_edge = jnp.where(row == 0, after, 0.0)
+        odd_edge = jnp.where(row == ROWS - OWN - 1, before, 0.0)
         cotangent = jnp.concatenate([even, even_edge, odd, odd_edge], axis=0)
         slope[:, at] = (cotangent * slant).astype(BF16)
 
     tiles(other.shape[1] // 128, tile)
 
 
-def slopes(ids, own, other, inputs, grad, before, after, first, done=()):
+def slopes(ids, own, other, inputs, grad, near, far, first, done=()):
     width = other.shape[1]
     return pl.pallas_call(
         functools.partial(slope_kernel, first),
@@ -563,7 +603,7 @@
         compiler_params=params(6),
         cost_estimate=cost(100 * 30 * 1000 * other.size, 14 * other.size),
         name="slopes",
-    )(ids, own, other, inputs, grad, before, after, *done)
+    )(ids, own, other, inputs, grad, near, far, *done)
 
 
 def backward_kernel(mine, firsts, count, ids, *refs):
@@ -649,12 +689,10 @@
     near = send(near, dc=1)
     pairs = [(i, i + 1) for i in range(1, 63, 2)]
     far = lax.ppermute(far, "seq", pairs + [(b, a) for a, b in pairs])
-    odd = at % 2 == 1
-    before = jnp.where(odd, near, far)
-    after = jnp.where(odd, far, near)
-    stem_weight, encoder_weight = load(stem_weight, encoder_weight)
+    halo = near, far
+    rows, stem_weight, encoder_weight = load(codes, stem_weight, encoder_weight)
     encoded, attention_weight = encode(
-        ids, codes, before, after, stem_weight, encoder_weight, attention_weight
+        ids, *halo, rows, stem_weight, encoder_weight, attention_weight
     )
     gain = norm_gain.reshape(1, feats)
     normed, *keyvals = project_keys(ids, encoded, swap(encoded), gain, attention_weight)
@@ -665,19 +703,19 @@
     def stacked(blocks):
         return jnp.concatenate(lax.optimization_barrier(blocks), axis=0)
 
-    keyvals = stacked([keyvals[0]] + spread(keyvals))
+    got = spread(keyvals)
+    keyvals = stacked([keyvals[0]] + got)
     near = [send(keyvals, dz=1), send(keyvals, dz=3)]
-    beside, normed = lax.optimization_barrier((send(keyvals, dc=1), normed))
     queries = project_queries(ids, normed, attention_weight)
-    *near, got1, got3, got2 = lax.optimization_barrier((*near, *spread(queries)))
-    queries = jnp.concatenate([queries[0], got1, got3, got2], axis=0)
+    *near, got = lax.optimization_barrier((*near, spread(queries)))
+    queries = jnp.concatenate([queries[0]] + got, axis=0)
     others = send(queries, dy=1)
     half = keyvals.shape[0] // 2
     far = [send(near[0][:half], dz=1), send(near[1][half:], dz=3)]
-    across = [send(piece, dc=1) for piece in near]
-    *far, across[0], across[1], others = lax.optimization_barrier((*far, *across, others))
+    across = [send(piece, dc=1) for piece in (keyvals, *near)]
+    *far, across, others = lax.optimization_barrier((*far, across, others))
     far = jnp.concatenate(far, axis=0)
-    pieces = [keyvals, beside] + near + across + [far, send(far, dc=1)]
+    pieces = [keyvals] + near + across + [far, send(far, dc=1)]
     other, inverse = attend(ids, logit_scale, others, pieces)
     other = send(other, dy=1)
     own = attend(ids, logit_scale, queries, pieces, inverses=[inverse])[0]
@@ -687,17 +725,17 @@
     sent = swap(output(ids, heads, out_weight, False, BF16))
     kept = output(ids, heads, out_weight, True, F32)
     half = decoder_weight.shape[1]
-    split = 2 * TILE
+    split = TILE
     inputs, early = decode_first(ids, kept, sent, encoded, decoder_weight, split)
     early = swap(early)
     late = decode(ids, inputs, decoder_weight, False, split, half - split, BF16)
     late, inputs = lax.optimization_barrier((late, inputs))
     late = swap(late)
     kept = decode(ids, inputs, decoder_weight, True, 0, half, F32)
-    decoded, early, paired = slopes(ids, kept, early, inputs, grad_out, before, after, 0)
+    decoded, early, paired = slopes(ids, kept, early, inputs, grad_out, *halo, 0)
     early_back = swap(early)
     decoded, late, rest = slopes(
-        ids, kept, late, inputs, grad_out, before, after, split, (decoded,)
+        ids, kept, late, inputs, grad_out, *halo, split, (decoded,)
     )
     late_back = swap(late)
     total = backward(

time: 129 us -> 125 us (0.969)
  local copies, waits for them, and re-layouts: 6.06 us -> 0.22 us
  starting transfers between devices: 41.1 us -> 44.3 us
    unnamed x23 -> x19, local copies, waits for them, and re-layouts: 5.95 us -> 0.12 us
    ppermute x20, waiting for transfers between devices: 24.1 us -> 20.8 us  [send(): return lax.ppermute(value, 'seq', moves(**step))]
    ppermute x20, starting transfers between devices: 26.4 us -> 29.4 us  [send(): return lax.ppermute(value, 'seq', moves(**step))]
    ppermute x6, waiting for transfers between devices: 13.9 us -> 16.6 us  [swap(): return lax.ppermute(value, 'head', [(0, 1), (1, 0)])]
  transfers between devices with their start and end apart: 27 -> 27, of which waited for: 15 -> 14; matrix products, arithmetic and copies ran while one was open for 0% -> 0% of each run, Pallas kernels for 18% -> 18%
where the time goes in v10:
time: 125 us
  starting transfers between devices  44.3 us (35%)
  Pallas kernels  41.8 us (33%)
  waiting for transfers between devices  37.4 us (30%)
    ppermute x20, starting transfers between devices, send(): return lax.ppermute(value, 'seq', moves(**step))  29.4 us
    ppermute x20, waiting for transfers between devices, send(): return lax.ppermute(value, 'seq', moves(**step))  20.8 us
    ppermute x6, waiting for transfers between devices, swap(): return lax.ppermute(value, 'head', [(0, 1), (1, 0)])  16.6 us
    ppermute x6, starting transfers between devices, swap(): return lax.ppermute(value, 'head', [(0, 1), (1, 0)])  14.3 us
    pallas_call x2, Pallas kernels, attend(): pl.pallas_call(functools.partial(attend_kernel, len(pieces), len(inverses...  10.3 us
    pallas_call x3, Pallas kernels, backward(): pl.pallas_call(functools.partial(backward_kernel, mine, [first for first,...  6.56 us
    pallas_call x1, Pallas kernels, encode(): pl.pallas_call(encode_kernel, in_specs=[SM] + [VM] * 5 + [HBM], out_specs...  4.35 us
    pallas_call x2, Pallas kernels, decode(): pl.pallas_call(functools.partial(decode_kernel, mine, first), in_specs=[S...  4.31 us
  transfers between devices with their start and end apart: 27, of which 14 were waited for; matrix products, arithmetic and copies ran while one was open for 0% of the time, Pallas kernels for 18%

profile of v10, /device:TPU:0, one launch (start us, length us, event | category | flops | bytes accessed | tf_op | source)
XLA Modules:
  0.0 124.8 jit_solution(13646180439082549504)
XLA Ops:
  0.6 0.1 pad_add_fusion.ids
  0.7 1.4 %prepare.1 = (bf16[128,128]{1,0:T(8,128)(2,1)S(1)}, bf16[8,1664]{1,0:T(8,128)(2,1)S(1)}, bf16[8,1664]{1,0:T(8,128)(2,1)S(1)}) custom-call(s32[3]{0:T(128)S(1)} %pad_add_fusion.ids, s32[128,128]{1,0:T(8,128)} %bitcast.6, bf16[256,1536]{1,0:T(8,128)(2,1)} %grad.5), custom_call_target="tpu_custom_call" | custom-call | flops 100000 | bytes 100000 | tf_op jit(solution)/shard_map/prepare/pallas_call | solution.py:111
  2.2 0.1 collective-permute-start
  2.3 0.7 collective-permute-start.1
  2.9 3.3 %load.1 = (bf16[256,1536]{1,0:T(8,128)(2,1)S(1)}, bf16[256,1536]{1,0:T(8,128)(2,1)S(1)}, bf16[3,1536,768]{2,1,0:T(8,128)(2,1)S(1)}) custom-call(bf16[128,128]{1,0:T(8,128)(2,1)S(1)} %get-tuple-element.52.codes, bf16[256,1536]{1,0:T(8,128)(2,1)} %stems.1, bf16[3,1536,768]{2,1,0:T(8,128)(2,1)} %weights.1), custom_call_target="tpu_custom_call" | custom-call | flops 100000 | bytes 7077888 | tf_op jit(solution)/shard_map/load/pallas_call | solution.py:163
  6.2 0.0 collective-permute-done.1.far
  6.2 0.0 copy-start.3
  6.3 4.3 %encode.1 = (bf16[272,768]{1,0:T(8,128)(2,1)S(1)}, bf16[3,1536,768]{2,1,0:T(8,128)(2,1)S(1)}) custom-call(s32[3]{0:T(128)S(1)} %pad_add_fusion.ids, bf16[8,1664]{1,0:T(8,128)(2,1)S(1)} %collective-permute-done.near, bf16[8,1664]{1,0:T(8,128)(2,1)S(1)} %collective-permute-done.1.far, bf16[256,1536]{1,0:T(8,128)(2,1)S(1)} %get-tuple-element.53.rows, ...), custom_call_target="tpu_custom_call" | custom-call | flops 1811939328 | bytes 14155776 | tf_op jit(solution)/shard_map/encode/pallas_call | solution.py:218
  10.6 3.4 %collective-permute-start.2 = (bf16[272,768]{1,0:T(8,128)(2,1)S(1)}, bf16[272,768]{1,0:T(8,128)(2,1)S(1)}, u32[]{:S(2)}, u32[]{:S(2)}) collective-permute-start(bf16[272,768]{1,0:T(8,128)(2,1)S(1)} %get-tuple-element.56.mine.encoded), channel_id=1, source_target_pairs={{0,1},{1,0},{2,3},{3,2},{4,5},{5,4},{6,7},{7,6},{8,9},{9,8},{10,11... | collective-permute-start | bytes 1253384 | tf_op jit(solution)/shard_map/ppermute | solution.py:665
  14.0 8.6 %collective-permute-done.2.theirs = bf16[272,768]{1,0:T(8,128)(2,1)S(1)} collective-permute-done((bf16[272,768]{1,0:T(8,128)(2,1)S(1)}, bf16[272,768]{1,0:T(8,128)(2,1)S(1)}, u32[]{:S(2)}, u32[]{:S(2)}) %collective-permute-start.2) | collective-permute-done | bytes 417824 | tf_op jit(solution)/shard_map/ppermute | solution.py:665
  22.6 2.0 %project_keys.1 = (bf16[2,136,768]{2,1,0:T(8,128)(2,1)S(1)}, bf16[128,384]{1,0:T(8,128)(2,1)S(1)}, bf16[128,384]{1,0:T(8,128)(2,1)S(1)}, bf16[128,384]{1,0:T(8,128)(2,1)S(1)}, bf16[128,384]{1,0:T(8,128)(2,1)S(1)}) custom-call(s32[3]{0:T(128)S(1)} %pad_add_fusion.ids, bf16[272,768]{1,0:T(8,128)(2,1)S(1)} %get-tuple-element.56.mine.encoded, ...), custom_call_target="tpu_custom_call" | custom-call | flops 641728512 | bytes 7077888 | tf_op jit(solution)/shard_map/project_keys/pallas_call | solution.py:282
  24.7 0.0 copy-start.2
  24.7 5.7 %collective-permute-start.3 = (bf16[128,384]{1,0:T(8,128)(2,1)S(1)}, bf16[128,384]{1,0:T(8,128)(2,1)S(1)}, u32[]{:S(2)}, u32[]{:S(2)}) collective-permute-start(bf16[128,384]{1,0:T(8,128)(2,1)S(1)} %get-tuple-element.61), channel_id=1, source_target_pairs={{0,32},{2,34},{4,36},{6,38},{8,40},{10,42},{12,44},{14,46},{16,48}... | collective-permute-start | bytes 294920 | tf_op jit(solution)/shard_map/ppermute | solution.py:669
  30.4 1.6 %collective-permute-start.4 = (bf16[128,384]{1,0:T(8,128)(2,1)S(1)}, bf16[128,384]{1,0:T(8,128)(2,1)S(1)}, u32[]{:S(2)}, u32[]{:S(2)}) collective-permute-start(bf16[128,384]{1,0:T(8,128)(2,1)S(1)} %get-tuple-element.62), channel_id=1, source_target_pairs={{0,96},{2,98},{4,100},{6,102},{8,104},{10,106},{12,108},{14,110},{... | collective-permute-start | bytes 294920 | tf_op jit(solution)/shard_map/ppermute | solution.py:669
  32.0 2.0 %collective-permute-start.5 = (bf16[128,384]{1,0:T(8,128)(2,1)S(1)}, bf16[128,384]{1,0:T(8,128)(2,1)S(1)}, u32[]{:S(2)}, u32[]{:S(2)}) collective-permute-start(bf16[128,384]{1,0:T(8,128)(2,1)S(1)} %get-tuple-element.63), channel_id=1, source_target_pairs={{0,64},{2,66},{4,68},{6,70},{8,72},{10,74},{12,76},{14,78},{16,80}... | collective-permute-start | bytes 294920 | tf_op jit(solution)/shard_map/ppermute | solution.py:669
  34.0 1.6 %collective-permute-done.3 = bf16[128,384]{1,0:T(8,128)(2,1)S(1)} collective-permute-done((bf16[128,384]{1,0:T(8,128)(2,1)S(1)}, bf16[128,384]{1,0:T(8,128)(2,1)S(1)}, u32[]{:S(2)}, u32[]{:S(2)}) %collective-permute-start.3) | collective-permute-done | bytes 98336 | tf_op jit(solution)/shard_map/ppermute | solution.py:669
  35.5 2.6 %collective-permute-done.5 = bf16[128,384]{1,0:T(8,128)(2,1)S(1)} collective-permute-done((bf16[128,384]{1,0:T(8,128)(2,1)S(1)}, bf16[128,384]{1,0:T(8,128)(2,1)S(1)}, u32[]{:S(2)}, u32[]{:S(2)}) %collective-permute-start.5) | collective-permute-done | bytes 98336 | tf_op jit(solution)/shard_map/ppermute | solution.py:669
  38.2 2.2 %collective-permute-start.6 = (bf16[512,384]{1,0:T(8,128)(2,1)S(1)}, bf16[512,384]{1,0:T(8,128)(2,1)S(1)}, u32[]{:S(2)}, u32[]{:S(2)}) collective-permute-start(bf16[512,384]{1,0:T(8,128)(2,1)S(1)} %constant_dynamic-update-slice_fusion.refs_0_), channel_id=1, source_target_pairs={{0,8},{2,10},{4,12},{6,14},{8,16},{10,18},{12,20},{14,22},{16,24},... | collective-permute-start | bytes 1179656 | tf_op jit(solution)/shard_map/ppermute | solution.py:669
  40.3 2.2 %collective-permute-start.7 = (bf16[512,384]{1,0:T(8,128)(2,1)S(1)}, bf16[512,384]{1,0:T(8,128)(2,1)S(1)}, u32[]{:S(2)}, u32[]{:S(2)}) collective-permute-start(bf16[512,384]{1,0:T(8,128)(2,1)S(1)} %constant_dynamic-update-slice_fusion.refs_0_), channel_id=1, source_target_pairs={{0,24},{2,26},{4,28},{6,30},{8,0},{10,2},{12,4},{14,6},{16,8},{18,... | collective-permute-start | bytes 1179656 | tf_op jit(solution)/shard_map/ppermute | solution.py:669
  42.5 1.3 %project_queries.1 = (bf16[136,256]{1,0:T(8,128)(2,1)S(1)}, bf16[136,256]{1,0:T(8,128)(2,1)S(1)}, bf16[136,256]{1,0:T(8,128)(2,1)S(1)}, bf16[136,256]{1,0:T(8,128)(2,1)S(1)}) custom-call(s32[3]{0:T(128)S(1)} %pad_add_fusion.ids, bf16[2,136,768]{2,1,0:T(8,128)(2,1)S(1)} %get-tuple-element.58.normed, bf16[3,1536,768]{2,1,0:T(8,128)(2,1)S(1)} %get-tuple-element.57.weight), custom_call_target="tpu_custom_call" | custom-call | flops 320864256 | bytes 3538944 | tf_op jit(solution)/shard_map/project_queries/pallas_call | solution.py:310
  43.8 1.9 %collective-permute-start.10 = (bf16[136,256]{1,0:T(8,128)(2,1)S(1)}, bf16[136,256]{1,0:T(8,128)(2,1)S(1)}, u32[]{:S(2)}, u32[]{:S(2)}) collective-permute-start(bf16[136,256]{1,0:T(8,128)(2,1)S(1)} %get-tuple-element.70), channel_id=1, source_target_pairs={{0,64},{2,66},{4,68},{6,70},{8,72},{10,74},{12,76},{14,78},{16,80}... | collective-permute-start | bytes 208904 | tf_op jit(solution)/shard_map/ppermute | solution.py:669
  45.7 0.7 collective-permute-start.8
  46.4 2.6 %collective-permute-start.9 = (bf16[136,256]{1,0:T(8,128)(2,1)S(1)}, bf16[136,256]{1,0:T(8,128)(2,1)S(1)}, u32[]{:S(2)}, u32[]{:S(2)}) collective-permute-start(bf16[136,256]{1,0:T(8,128)(2,1)S(1)} %get-tuple-element.69), channel_id=1, source_target_pairs={{0,96},{2,98},{4,100},{6,102},{8,104},{10,106},{12,108},{14,110},{... | collective-permute-start | bytes 208904 | tf_op jit(solution)/shard_map/ppermute | solution.py:669
  49.0 0.7 collective-permute-done.10
  49.7 0.0 collective-permute-start.13
  49.7 1.5 %collective-permute-done.8 = bf16[136,256]{1,0:T(8,128)(2,1)S(1)} collective-permute-done((bf16[136,256]{1,0:T(8,128)(2,1)S(1)}, bf16[136,256]{1,0:T(8,128)(2,1)S(1)}, u32[]{:S(2)}, u32[]{:S(2)}) %collective-permute-start.8) | collective-permute-done | bytes 69664 | tf_op jit(solution)/shard_map/ppermute | solution.py:669
  51.2 0.0 collective-permute-done.6.refs_1_
  51.3 0.1 collective-permute-start.14
  51.3 0.5 collective-permute-start.15
  51.9 0.8 collective-permute-start.16
  52.7 1.2 collective-permute-start.11
  53.9 2.1 %collective-permute-start.12 = (bf16[256,384]{1,0:T(8,128)(2,1)S(1)}, bf16[256,384]{1,0:T(8,128)(2,1)S(1)}, u32[]{:S(2)}, u32[]{:S(2)}) collective-permute-start(bf16[256,384]{1,0:T(8,128)(2,1)S(1)} %slice.7), channel_id=1, source_target_pairs={{0,24},{2,26},{4,28},{6,30},{8,0},{10,2},{12,4},{14,6},{16,8},{18,... | collective-permute-start | bytes 589832 | tf_op jit(solution)/shard_map/ppermute | solution.py:669
  56.0 4.6 %collective-permute-done.11 = bf16[256,384]{1,0:T(8,128)(2,1)S(1)} collective-permute-done((bf16[256,384]{1,0:T(8,128)(2,1)S(1)}, bf16[256,384]{1,0:T(8,128)(2,1)S(1)}, u32[]{:S(2)}, u32[]{:S(2)}) %collective-permute-start.11) | collective-permute-done | bytes 196640 | tf_op jit(solution)/shard_map/ppermute | solution.py:669
  60.7 0.0 copy-start
  60.7 0.3 collective-permute-start.17
  61.0 1.7 %collective-permute-done.17.refs_7_ = bf16[512,384]{1,0:T(8,128)(2,1)S(1)} collective-permute-done((bf16[512,384]{1,0:T(8,128)(2,1)S(1)}, bf16[512,384]{1,0:T(8,128)(2,1)S(1)}, u32[]{:S(2)}, u32[]{:S(2)}) %collective-permute-start.17) | collective-permute-done | bytes 393248 | tf_op jit(solution)/shard_map/ppermute | solution.py:669
  62.7 5.7 %attend.2 = (bf16[544,256]{1,0:T(8,128)(2,1)S(1)}, f32[8,4096]{1,0:T(8,128)S(1)}) custom-call(s32[3]{0:T(128)S(1)} %pad_add_fusion.ids, f32[4]{0:T(128)S(1)} %copy-done.2, bf16[544,256]{1,0:T(8,128)(2,1)S(1)} %collective-permute-done.16.queries, bf16[512,384]{1,0:T(8,128)(2,1)S(1)} %constant_dynamic-update-slice_fusion.refs_0_, ...), custom_call_target="tpu_custom_call" | custom-call | flops 2281701376 | bytes 4456448 | tf_op jit(solution)/shard_map/attend/pallas_call | solution.py:431
  68.4 1.4 %collective-permute-start.18 = (bf16[544,256]{1,0:T(8,128)(2,1)S(1)}, bf16[544,256]{1,0:T(8,128)(2,1)S(1)}, u32[]{:S(2)}, u32[]{:S(2)}) collective-permute-start(bf16[544,256]{1,0:T(8,128)(2,1)S(1)} %get-tuple-element.83), channel_id=1, source_target_pairs={{0,4},{2,6},{4,0},{6,2},{8,12},{10,14},{12,8},{14,10},{16,20},{18,... | collective-permute-start | bytes 835592 | tf_op jit(solution)/shard_map/ppermute | solution.py:669
  69.8 4.6 %attend.3.a0 = bf16[544,256]{1,0:T(8,128)(2,1)S(1)} custom-call(s32[3]{0:T(128)S(1)} %pad_add_fusion.ids, f32[4]{0:T(128)S(1)} %copy-done.2, bf16[544,256]{1,0:T(8,128)(2,1)S(1)} %constant_dynamic-update-slice_fusion.4.queries, bf16[512,384]{1,0:T(8,128)(2,1)S(1)} %constant_dynamic-update-slice_fusion.refs_0_, ...), custom_call_target="tpu_custom_call" | custom-call | flops 2281701376 | bytes 4456448 | tf_op jit(solution)/shard_map/attend/pallas_call | solution.py:431
  74.4 2.8 %collective-permute-done.18.a1 = bf16[544,256]{1,0:T(8,128)(2,1)S(1)} collective-permute-done((bf16[544,256]{1,0:T(8,128)(2,1)S(1)}, bf16[544,256]{1,0:T(8,128)(2,1)S(1)}, u32[]{:S(2)}, u32[]{:S(2)}) %collective-permute-start.18) | collective-permute-done | bytes 278560 | tf_op jit(solution)/shard_map/ppermute | solution.py:669
  77.2 0.5 merge.1
  77.7 3.2 %collective-permute-start.19 = (bf16[136,256]{1,0:T(8,128)(2,1)S(1)}, bf16[136,256]{1,0:T(8,128)(2,1)S(1)}, u32[]{:S(2)}, u32[]{:S(2)}) collective-permute-start(bf16[136,256]{1,0:T(8,128)(2,1)S(1)} %get-tuple-element.85), channel_id=1, source_target_pairs={{0,96},{2,98},{4,100},{6,102},{8,104},{10,106},{12,108},{14,110},{... | collective-permute-start | bytes 208904 | tf_op jit(solution)/shard_map/ppermute | solution.py:669
  80.9 0.9 collective-permute-start.21
  81.9 1.7 %collective-permute-done.19.a1 = bf16[136,256]{1,0:T(8,128)(2,1)S(1)} collective-permute-done((bf16[136,256]{1,0:T(8,128)(2,1)S(1)}, bf16[136,256]{1,0:T(8,128)(2,1)S(1)}, u32[]{:S(2)}, u32[]{:S(2)}) %collective-permute-start.19) | collective-permute-done | bytes 69664 | tf_op jit(solution)/shard_map/ppermute | solution.py:669
  83.5 3.3 %collective-permute-done.20.a2 = bf16[136,256]{1,0:T(8,128)(2,1)S(1)} collective-permute-done((bf16[136,256]{1,0:T(8,128)(2,1)S(1)}, bf16[136,256]{1,0:T(8,128)(2,1)S(1)}, u32[]{:S(2)}, u32[]{:S(2)}) %collective-permute-start.20) | collective-permute-done | bytes 69664 | tf_op jit(solution)/shard_map/ppermute | solution.py:669
  86.8 0.4 collective-permute-done.21.a3
  87.2 1.3 %output.3 = bf16[136,768]{1,0:T(8,128)(2,1)S(1)} custom-call(s32[3]{0:T(128)S(1)} %pad_add_fusion.ids, bf16[136,256]{1,0:T(8,128)(2,1)S(1)} %get-tuple-element.84.a0, bf16[136,256]{1,0:T(8,128)(2,1)S(1)} %collective-permute-done.19.a1, bf16[136,256]{1,0:T(8,128)(2,1)S(1)} %collective-permute-done.20.a2, bf16[136,256]{1,0:T(8,128)(2,1)S(1)} %collective-permute-done.21.a3, ...), custom_call_target="tpu_custom_call" | custom-call | flops 160432128 | bytes 1179648 | tf_op jit(solution)/shard_map/output/pallas_call | solution.py:485
  88.5 3.3 %collective-permute-start.22 = (bf16[136,768]{1,0:T(8,128)(2,1)S(1)}, bf16[136,768]{1,0:T(8,128)(2,1)S(1)}, u32[]{:S(2)}, u32[]{:S(2)}) collective-permute-start(bf16[136,768]{1,0:T(8,128)(2,1)S(1)} %output.3), channel_id=1, source_target_pairs={{0,1},{1,0},{2,3},{3,2},{4,5},{5,4},{6,7},{7,6},{8,9},{9,8},{10,11... | collective-permute-start | bytes 626696 | tf_op jit(solution)/shard_map/ppermute | solution.py:665
  91.8 1.3 %output.2.own = f32[136,768]{1,0:T(8,128)S(1)} custom-call(s32[3]{0:T(128)S(1)} %pad_add_fusion.ids, bf16[136,256]{1,0:T(8,128)(2,1)S(1)} %get-tuple-element.84.a0, bf16[136,256]{1,0:T(8,128)(2,1)S(1)} %collective-permute-done.19.a1, bf16[136,256]{1,0:T(8,128)(2,1)S(1)} %collective-permute-done.20.a2, bf16[136,256]{1,0:T(8,128)(2,1)S(1)} %collective-permute-done.21.a3, ...), custom_call_target="tpu_custom_call" | custom-call | flops 160432128 | bytes 1179648 | tf_op jit(solution)/shard_map/output/pallas_call | solution.py:485
  93.1 2.8 %collective-permute-done.22.other = bf16[136,768]{1,0:T(8,128)(2,1)S(1)} collective-permute-done((bf16[136,768]{1,0:T(8,128)(2,1)S(1)}, bf16[136,768]{1,0:T(8,128)(2,1)S(1)}, u32[]{:S(2)}, u32[]{:S(2)}) %collective-permute-start.22) | collective-permute-done | bytes 208928 | tf_op jit(solution)/shard_map/ppermute | solution.py:665
  95.9 1.2 decode_first.1
  97.1 3.5 %collective-permute-start.24 = (bf16[272,256]{1,0:T(8,128)(2,1)S(1)}, bf16[272,256]{1,0:T(8,128)(2,1)S(1)}, u32[]{:S(2)}, u32[]{:S(2)}) collective-permute-start(bf16[272,256]{1,0:T(8,128)(2,1)S(1)} %get-tuple-element.91), channel_id=1, source_target_pairs={{0,1},{1,0},{2,3},{3,2},{4,5},{5,4},{6,7},{7,6},{8,9},{9,8},{10,11... | collective-permute-start | bytes 417800 | tf_op jit(solution)/shard_map/ppermute | solution.py:665
  100.7 2.3 %decode.2 = bf16[272,512]{1,0:T(8,128)(2,1)} custom-call(s32[3]{0:T(128)S(1)} %pad_add_fusion.ids, bf16[272,768]{1,0:T(8,128)(2,1)S(1)} %get-tuple-element.89.inputs, bf16[3,768,1536]{2,1,0:T(8,128)(2,1)S(1)} %bitcast.5), custom_call_target="tpu_custom_call" | custom-call | flops 1000000 | bytes 10000 | tf_op jit(solution)/shard_map/decode/pallas_call | solution.py:544
  102.9 0.3 collective-permute-start.23
  103.2 2.0 %decode.3.own = f32[272,768]{1,0:T(8,128)S(1)} custom-call(s32[3]{0:T(128)S(1)} %pad_add_fusion.ids, bf16[272,768]{1,0:T(8,128)(2,1)S(1)} %get-tuple-element.89.inputs, bf16[3,768,1536]{2,1,0:T(8,128)(2,1)S(1)} %bitcast.5), custom_call_target="tpu_custom_call" | custom-call | flops 1000000 | bytes 10000 | tf_op jit(solution)/shard_map/decode/pallas_call | solution.py:544
  105.3 1.5 %slopes.2 = (bf16[256,256]{1,0:T(8,128)(2,1)S(1)}, bf16[272,256]{1,0:T(8,128)(2,1)}, f32[128,256]{1,0:T(8,128)S(1)}) custom-call(s32[3]{0:T(128)S(1)} %pad_add_fusion.ids, f32[272,768]{1,0:T(8,128)S(1)} %decode.3.own, bf16[272,256]{1,0:T(8,128)(2,1)S(1)} %collective-permute-done.24.other, bf16[272,768]{1,0:T(8,128)(2,1)S(1)} %get-tuple-element.89.inputs, ...), custom_call_target="tpu_custom_call" | custom-call | flops 208896000000 | bytes 974848 | tf_op jit(solution)/shard_map/slopes/pallas_call | solution.py:593
  106.8 3.3 %collective-permute-start.26 = (bf16[272,256]{1,0:T(8,128)(2,1)}, bf16[272,256]{1,0:T(8,128)(2,1)}, u32[]{:S(2)}, u32[]{:S(2)}) collective-permute-start(bf16[272,256]{1,0:T(8,128)(2,1)} %get-tuple-element.95.refs_0_), channel_id=1, source_target_pairs={{0,1},{1,0},{2,3},{3,2},{4,5},{5,4},{6,7},{7,6},{8,9},{9,8},{10,11... | collective-permute-start | bytes 417800 | tf_op jit(solution)/shard_map/ppermute | solution.py:665
  110.1 1.8 %collective-permute-done.23.other = bf16[272,512]{1,0:T(8,128)(2,1)} collective-permute-done((bf16[272,512]{1,0:T(8,128)(2,1)}, bf16[272,512]{1,0:T(8,128)(2,1)}, u32[]{:S(2)}, u32[]{:S(2)}) %collective-permute-start.23) | collective-permute-done | bytes 278560 | tf_op jit(solution)/shard_map/ppermute | solution.py:665
  111.9 2.4 %slopes.3 = (bf16[256,768]{1,0:T(8,128)(2,1)}, bf16[272,512]{1,0:T(8,128)(2,1)S(1)}, f32[128,512]{1,0:T(8,128)S(1)}) custom-call(s32[3]{0:T(128)S(1)} %pad_add_fusion.ids, f32[272,768]{1,0:T(8,128)S(1)} %decode.3.own, bf16[272,512]{1,0:T(8,128)(2,1)} %collective-permute-done.23.other, bf16[272,768]{1,0:T(8,128)(2,1)S(1)} %get-tuple-element.89.inputs, ...), custom_call_target="tpu_custom_call" | custom-call | flops 417792000000 | bytes 1949696 | tf_op jit(solution)/shard_map/slopes/pallas_call | solution.py:593
  114.3 0.5 collective-permute-start.25
  114.8 2.6 %backward.3.refs_1_ = f32[128,768]{1,0:T(8,128)S(1)} custom-call(s32[3]{0:T(128)S(1)} %pad_add_fusion.ids, bf16[272,256]{1,0:T(8,128)(2,1)} %get-tuple-element.95.refs_0_, bf16[272,512]{1,0:T(8,128)(2,1)S(1)} %get-tuple-element.94.refs_1_, f32[128,256]{1,0:T(8,128)S(1)} %get-tuple-element.96.refs_2_, f32[128,512]{1,0:T(8,128)S(1)} %get-tuple-element.97.refs_3_, ...), custom_call_target="tpu_custom_call" | custom-call | flops 96259276800 | bytes 1253376 | tf_op jit(solution)/shard_map/backward/pallas_call | solution.py:640
  117.5 1.5 %backward.4.refs_1_ = f32[128,768]{1,0:T(8,128)S(1)} custom-call(s32[3]{0:T(128)S(1)} %pad_add_fusion.ids, bf16[272,256]{1,0:T(8,128)(2,1)} %collective-permute-done.26.refs_0_, f32[128,768]{1,0:T(8,128)S(1)} %backward.3.refs_1_, bf16[3,768,1536]{2,1,0:T(8,128)(2,1)S(1)} %bitcast.5), custom_call_target="tpu_custom_call" | custom-call | flops 32086425600 | bytes 417792 | tf_op jit(solution)/shard_map/backward/pallas_call | solution.py:640
  118.9 3.4 %collective-permute-done.25.refs_0_ = bf16[272,512]{1,0:T(8,128)(2,1)S(1)} collective-permute-done((bf16[272,512]{1,0:T(8,128)(2,1)S(1)}, bf16[272,512]{1,0:T(8,128)(2,1)S(1)}, u32[]{:S(2)}, u32[]{:S(2)}) %collective-permute-start.25) | collective-permute-done | bytes 278560 | tf_op jit(solution)/shard_map/ppermute | solution.py:665
  122.3 2.5 %backward.5 = bf16[128,768]{1,0:T(8,128)(2,1)} custom-call(s32[3]{0:T(128)S(1)} %pad_add_fusion.ids, bf16[272,512]{1,0:T(8,128)(2,1)S(1)} %collective-permute-done.25.refs_0_, f32[128,768]{1,0:T(8,128)S(1)} %backward.4.refs_1_, bf16[3,768,1536]{2,1,0:T(8,128)(2,1)S(1)} %bitcast.5), custom_call_target="tpu_custom_call" | custom-call | flops 64172851200 | bytes 835584 | tf_op jit(solution)/shard_map/backward/pallas_call | solution.py:640
  (35 shorter events, 0.2 us)
Async XLA Ops:
  2.2 4.1 %collective-permute-start = (bf16[8,1664]{1,0:T(8,128)(2,1)S(1)}, bf16[8,1664]{1,0:T(8,128)(2,1)S(1)}, u32[]{:S(2)}, u32[]{:S(2)}) collective-permute-start(bf16[8,1664]{1,0:T(8,128)(2,1)S(1)} %get-tuple-element.50), channel_id=1, source_target_pairs={{0,2},{2,0},{4,6},{6,4},{8,10},{10,8},{12,14},{14,12},{16,18},{18,... | collective-permute-start | bytes 79880 | tf_op jit(solution)/shard_map/ppermute | solution.py:669
  2.3 4.0 %collective-permute-start.1 = (bf16[8,1664]{1,0:T(8,128)(2,1)S(1)}, bf16[8,1664]{1,0:T(8,128)(2,1)S(1)}, u32[]{:S(2)}, u32[]{:S(2)}) collective-permute-start(bf16[8,1664]{1,0:T(8,128)(2,1)S(1)} %get-tuple-element.51), channel_id=1, source_target_pairs={{2,4},{6,8},{10,12},{14,16},{18,20},{22,24},{26,28},{30,32},{34,36... | collective-permute-start | bytes 79880 | tf_op jit(solution)/shard_map/ppermute | solution.py:691
  6.2 7.7 %copy-start.3 = (f32[1536]{0:T(1024)S(1)}, f32[1536]{0:T(1024)}, u32[]{:S(2)}) copy-start(f32[1536]{0:T(1024)} %param.12) | copy-start | bytes 18436
  10.6 12.0 %collective-permute-start.2 = (bf16[272,768]{1,0:T(8,128)(2,1)S(1)}, bf16[272,768]{1,0:T(8,128)(2,1)S(1)}, u32[]{:S(2)}, u32[]{:S(2)}) collective-permute-start(bf16[272,768]{1,0:T(8,128)(2,1)S(1)} %get-tuple-element.56.mine.encoded), channel_id=1, source_target_pairs={{0,1},{1,0},{2,3},{3,2},{4,5},{5,4},{6,7},{7,6},{8,9},{9,8},{10,11... | collective-permute-start | bytes 1253384 | tf_op jit(solution)/shard_map/ppermute | solution.py:665
  24.7 38.1 %copy-start.2 = (f32[4]{0:T(128)S(1)}, f32[4]{0:T(128)}, u32[]{:S(2)}) copy-start(f32[4]{0:T(128)} %scale.3) | copy-start | bytes 52
  24.7 10.9 %collective-permute-start.3 = (bf16[128,384]{1,0:T(8,128)(2,1)S(1)}, bf16[128,384]{1,0:T(8,128)(2,1)S(1)}, u32[]{:S(2)}, u32[]{:S(2)}) collective-permute-start(bf16[128,384]{1,0:T(8,128)(2,1)S(1)} %get-tuple-element.61), channel_id=1, source_target_pairs={{0,32},{2,34},{4,36},{6,38},{8,40},{10,42},{12,44},{14,46},{16,48}... | collective-permute-start | bytes 294920 | tf_op jit(solution)/shard_map/ppermute | solution.py:669
  30.4 5.1 %collective-permute-start.4 = (bf16[128,384]{1,0:T(8,128)(2,1)S(1)}, bf16[128,384]{1,0:T(8,128)(2,1)S(1)}, u32[]{:S(2)}, u32[]{:S(2)}) collective-permute-start(bf16[128,384]{1,0:T(8,128)(2,1)S(1)} %get-tuple-element.62), channel_id=1, source_target_pairs={{0,96},{2,98},{4,100},{6,102},{8,104},{10,106},{12,108},{14,110},{... | collective-permute-start | bytes 294920 | tf_op jit(solution)/shard_map/ppermute | solution.py:669
  32.0 6.1 %collective-permute-start.5 = (bf16[128,384]{1,0:T(8,128)(2,1)S(1)}, bf16[128,384]{1,0:T(8,128)(2,1)S(1)}, u32[]{:S(2)}, u32[]{:S(2)}) collective-permute-start(bf16[128,384]{1,0:T(8,128)(2,1)S(1)} %get-tuple-element.63), channel_id=1, source_target_pairs={{0,64},{2,66},{4,68},{6,70},{8,72},{10,74},{12,76},{14,78},{16,80}... | collective-permute-start | bytes 294920 | tf_op jit(solution)/shard_map/ppermute | solution.py:669
  38.2 13.1 %collective-permute-start.6 = (bf16[512,384]{1,0:T(8,128)(2,1)S(1)}, bf16[512,384]{1,0:T(8,128)(2,1)S(1)}, u32[]{:S(2)}, u32[]{:S(2)}) collective-permute-start(bf16[512,384]{1,0:T(8,128)(2,1)S(1)} %constant_dynamic-update-slice_fusion.refs_0_), channel_id=1, source_target_pairs={{0,8},{2,10},{4,12},{6,14},{8,16},{10,18},{12,20},{14,22},{16,24},... | collective-permute-start | bytes 1179656 | tf_op jit(solution)/shard_map/ppermute | solution.py:669
  40.3 10.9 %collective-permute-start.7 = (bf16[512,384]{1,0:T(8,128)(2,1)S(1)}, bf16[512,384]{1,0:T(8,128)(2,1)S(1)}, u32[]{:S(2)}, u32[]{:S(2)}) collective-permute-start(bf16[512,384]{1,0:T(8,128)(2,1)S(1)} %constant_dynamic-update-slice_fusion.refs_0_), channel_id=1, source_target_pairs={{0,24},{2,26},{4,28},{6,30},{8,0},{10,2},{12,4},{14,6},{16,8},{18,... | collective-permute-start | bytes 1179656 | tf_op jit(solution)/shard_map/ppermute | solution.py:669
  43.8 5.9 %collective-permute-start.10 = (bf16[136,256]{1,0:T(8,128)(2,1)S(1)}, bf16[136,256]{1,0:T(8,128)(2,1)S(1)}, u32[]{:S(2)}, u32[]{:S(2)}) collective-permute-start(bf16[136,256]{1,0:T(8,128)(2,1)S(1)} %get-tuple-element.70), channel_id=1, source_target_pairs={{0,64},{2,66},{4,68},{6,70},{8,72},{10,74},{12,76},{14,78},{16,80}... | collective-permute-start | bytes 208904 | tf_op jit(solution)/shard_map/ppermute | solution.py:669
  45.7 5.5 %collective-permute-start.8 = (bf16[136,256]{1,0:T(8,128)(2,1)S(1)}, bf16[136,256]{1,0:T(8,128)(2,1)S(1)}, u32[]{:S(2)}, u32[]{:S(2)}) collective-permute-start(bf16[136,256]{1,0:T(8,128)(2,1)S(1)} %get-tuple-element.68), channel_id=1, source_target_pairs={{0,32},{2,34},{4,36},{6,38},{8,40},{10,42},{12,44},{14,46},{16,48}... | collective-permute-start | bytes 208904 | tf_op jit(solution)/shard_map/ppermute | solution.py:669
  46.4 4.8 %collective-permute-start.9 = (bf16[136,256]{1,0:T(8,128)(2,1)S(1)}, bf16[136,256]{1,0:T(8,128)(2,1)S(1)}, u32[]{:S(2)}, u32[]{:S(2)}) collective-permute-start(bf16[136,256]{1,0:T(8,128)(2,1)S(1)} %get-tuple-element.69), channel_id=1, source_target_pairs={{0,96},{2,98},{4,100},{6,102},{8,104},{10,106},{12,108},{14,110},{... | collective-permute-start | bytes 208904 | tf_op jit(solution)/shard_map/ppermute | solution.py:669
  49.7 4.2 %collective-permute-start.13 = (bf16[512,384]{1,0:T(8,128)(2,1)S(1)}, bf16[512,384]{1,0:T(8,128)(2,1)S(1)}, u32[]{:S(2)}, u32[]{:S(2)}) collective-permute-start(bf16[512,384]{1,0:T(8,128)(2,1)S(1)} %constant_dynamic-update-slice_fusion.refs_0_), channel_id=1, source_target_pairs={{0,2},{2,0},{4,6},{6,4},{8,10},{10,8},{12,14},{14,12},{16,18},{18,... | collective-permute-start | bytes 1179656 | tf_op jit(solution)/shard_map/ppermute | solution.py:669
  51.3 9.4 %collective-permute-start.14 = (bf16[512,384]{1,0:T(8,128)(2,1)S(1)}, bf16[512,384]{1,0:T(8,128)(2,1)S(1)}, u32[]{:S(2)}, u32[]{:S(2)}) collective-permute-start(bf16[512,384]{1,0:T(8,128)(2,1)S(1)} %collective-permute-done.6.refs_1_), channel_id=1, source_target_pairs={{0,2},{2,0},{4,6},{6,4},{8,10},{10,8},{12,14},{14,12},{16,18},{18,... | collective-permute-start | bytes 1179656 | tf_op jit(solution)/shard_map/ppermute | solution.py:669
  51.3 9.3 %collective-permute-start.15 = (bf16[512,384]{1,0:T(8,128)(2,1)S(1)}, bf16[512,384]{1,0:T(8,128)(2,1)S(1)}, u32[]{:S(2)}, u32[]{:S(2)}) collective-permute-start(bf16[512,384]{1,0:T(8,128)(2,1)S(1)} %collective-permute-done.7.refs_2_), channel_id=1, source_target_pairs={{0,2},{2,0},{4,6},{6,4},{8,10},{10,8},{12,14},{14,12},{16,18},{18,... | collective-permute-start | bytes 1179656 | tf_op jit(solution)/shard_map/ppermute | solution.py:669
  51.9 8.8 %collective-permute-start.16 = (bf16[544,256]{1,0:T(8,128)(2,1)S(1)}, bf16[544,256]{1,0:T(8,128)(2,1)S(1)}, u32[]{:S(2)}, u32[]{:S(2)}) collective-permute-start(bf16[544,256]{1,0:T(8,128)(2,1)S(1)} %constant_dynamic-update-slice_fusion.4.queries), channel_id=1, source_target_pairs={{0,4},{2,6},{4,0},{6,2},{8,12},{10,14},{12,8},{14,10},{16,20},{18,... | collective-permute-start | bytes 835592 | tf_op jit(solution)/shard_map/ppermute | solution.py:669
  52.7 7.9 %collective-permute-start.11 = (bf16[256,384]{1,0:T(8,128)(2,1)S(1)}, bf16[256,384]{1,0:T(8,128)(2,1)S(1)}, u32[]{:S(2)}, u32[]{:S(2)}) collective-permute-start(bf16[256,384]{1,0:T(8,128)(2,1)S(1)} %slice.6), channel_id=1, source_target_pairs={{0,8},{2,10},{4,12},{6,14},{8,16},{10,18},{12,20},{14,22},{16,24},... | collective-permute-start | bytes 589832 | tf_op jit(solution)/shard_map/ppermute | solution.py:669
  53.9 6.7 %collective-permute-start.12 = (bf16[256,384]{1,0:T(8,128)(2,1)S(1)}, bf16[256,384]{1,0:T(8,128)(2,1)S(1)}, u32[]{:S(2)}, u32[]{:S(2)}) collective-permute-start(bf16[256,384]{1,0:T(8,128)(2,1)S(1)} %slice.7), channel_id=1, source_target_pairs={{0,24},{2,26},{4,28},{6,30},{8,0},{10,2},{12,4},{14,6},{16,8},{18,... | collective-permute-start | bytes 589832 | tf_op jit(solution)/shard_map/ppermute | solution.py:669
  60.7 26.5 %copy-start = (bf16[768,1536]{1,0:T(8,128)(2,1)S(1)}, bf16[768,1536]{1,0:T(8,128)(2,1)}, u32[]{:S(2)}) copy-start(bf16[768,1536]{1,0:T(8,128)(2,1)} %weight.6) | copy-start | bytes 7077892
  60.7 2.0 %collective-permute-start.17 = (bf16[512,384]{1,0:T(8,128)(2,1)S(1)}, bf16[512,384]{1,0:T(8,128)(2,1)S(1)}, u32[]{:S(2)}, u32[]{:S(2)}) collective-permute-start(bf16[512,384]{1,0:T(8,128)(2,1)S(1)} %constant_dynamic-update-slice_fusion.8.refs_6_), channel_id=1, source_target_pairs={{0,2},{2,0},{4,6},{6,4},{8,10},{10,8},{12,14},{14,12},{16,18},{18,... | collective-permute-start | bytes 1179656 | tf_op jit(solution)/shard_map/ppermute | solution.py:669
  68.4 8.8 %collective-permute-start.18 = (bf16[544,256]{1,0:T(8,128)(2,1)S(1)}, bf16[544,256]{1,0:T(8,128)(2,1)S(1)}, u32[]{:S(2)}, u32[]{:S(2)}) collective-permute-start(bf16[544,256]{1,0:T(8,128)(2,1)S(1)} %get-tuple-element.83), channel_id=1, source_target_pairs={{0,4},{2,6},{4,0},{6,2},{8,12},{10,14},{12,8},{14,10},{16,20},{18,... | collective-permute-start | bytes 835592 | tf_op jit(solution)/shard_map/ppermute | solution.py:669
  69.8 26.1 %slice-start = ((s8[7077888]{0:T(1024)(128)(4,1)}), s8[4194304]{0:T(1024)(128)(4,1)S(1)}, s32[]{:S(2)}) async-start(s8[7077888]{0:T(1024)(128)(4,1)} %bitcast.4), calls=%async_computation | async-start | bytes 8388608
  69.8 26.1 %slice-start.1 = ((s8[7077888]{0:T(1024)(128)(4,1)}), s8[2883584]{0:T(1024)(128)(4,1)S(1)}, s32[]{:S(2)}) async-start(s8[7077888]{0:T(1024)(128)(4,1)} %bitcast.4), calls=%async_computation.1 | async-start | bytes 5767168
  77.7 5.8 %collective-permute-start.19 = (bf16[136,256]{1,0:T(8,128)(2,1)S(1)}, bf16[136,256]{1,0:T(8,128)(2,1)S(1)}, u32[]{:S(2)}, u32[]{:S(2)}) collective-permute-start(bf16[136,256]{1,0:T(8,128)(2,1)S(1)} %get-tuple-element.85), channel_id=1, source_target_pairs={{0,96},{2,98},{4,100},{6,102},{8,104},{10,106},{12,108},{14,110},{... | collective-permute-start | bytes 208904 | tf_op jit(solution)/shard_map/ppermute | solution.py:669
  80.9 5.9 %collective-permute-start.20 = (bf16[136,256]{1,0:T(8,128)(2,1)S(1)}, bf16[136,256]{1,0:T(8,128)(2,1)S(1)}, u32[]{:S(2)}, u32[]{:S(2)}) collective-permute-start(bf16[136,256]{1,0:T(8,128)(2,1)S(1)} %get-tuple-element.86), channel_id=1, source_target_pairs={{0,64},{2,66},{4,68},{6,70},{8,72},{10,74},{12,76},{14,78},{16,80}... | collective-permute-start | bytes 208904 | tf_op jit(solution)/shard_map/ppermute | solution.py:669
  80.9 6.3 %collective-permute-start.21 = (bf16[136,256]{1,0:T(8,128)(2,1)S(1)}, bf16[136,256]{1,0:T(8,128)(2,1)S(1)}, u32[]{:S(2)}, u32[]{:S(2)}) collective-permute-start(bf16[136,256]{1,0:T(8,128)(2,1)S(1)} %get-tuple-element.87), channel_id=1, source_target_pairs={{0,32},{2,34},{4,36},{6,38},{8,40},{10,42},{12,44},{14,46},{16,48}... | collective-permute-start | bytes 208904 | tf_op jit(solution)/shard_map/ppermute | solution.py:669
  88.5 7.4 %collective-permute-start.22 = (bf16[136,768]{1,0:T(8,128)(2,1)S(1)}, bf16[136,768]{1,0:T(8,128)(2,1)S(1)}, u32[]{:S(2)}, u32[]{:S(2)}) collective-permute-start(bf16[136,768]{1,0:T(8,128)(2,1)S(1)} %output.3), channel_id=1, source_target_pairs={{0,1},{1,0},{2,3},{3,2},{4,5},{5,4},{6,7},{7,6},{8,9},{9,8},{10,11... | collective-permute-start | bytes 626696 | tf_op jit(solution)/shard_map/ppermute | solution.py:665
  97.1 8.2 %collective-permute-start.24 = (bf16[272,256]{1,0:T(8,128)(2,1)S(1)}, bf16[272,256]{1,0:T(8,128)(2,1)S(1)}, u32[]{:S(2)}, u32[]{:S(2)}) collective-permute-start(bf16[272,256]{1,0:T(8,128)(2,1)S(1)} %get-tuple-element.91), channel_id=1, source_target_pairs={{0,1},{1,0},{2,3},{3,2},{4,5},{5,4},{6,7},{7,6},{8,9},{9,8},{10,11... | collective-permute-start | bytes 417800 | tf_op jit(solution)/shard_map/ppermute | solution.py:665
  100.7 4.6 %copy-start.1 = (bf16[256,1536]{1,0:T(8,128)(2,1)S(1)}, bf16[256,1536]{1,0:T(8,128)(2,1)}, u32[]{:S(2)}) copy-start(bf16[256,1536]{1,0:T(8,128)(2,1)} %grad.5) | copy-start | bytes 2359300
  102.9 9.0 %collective-permute-start.23 = (bf16[272,512]{1,0:T(8,128)(2,1)}, bf16[272,512]{1,0:T(8,128)(2,1)}, u32[]{:S(2)}, u32[]{:S(2)}) collective-permute-start(bf16[272,512]{1,0:T(8,128)(2,1)} %decode.2), channel_id=1, source_target_pairs={{0,1},{1,0},{2,3},{3,2},{4,5},{5,4},{6,7},{7,6},{8,9},{9,8},{10,11... | collective-permute-start | bytes 835592 | tf_op jit(solution)/shard_map/ppermute | solution.py:665
  106.8 10.6 %collective-permute-start.26 = (bf16[272,256]{1,0:T(8,128)(2,1)}, bf16[272,256]{1,0:T(8,128)(2,1)}, u32[]{:S(2)}, u32[]{:S(2)}) collective-permute-start(bf16[272,256]{1,0:T(8,128)(2,1)} %get-tuple-element.95.refs_0_), channel_id=1, source_target_pairs={{0,1},{1,0},{2,3},{3,2},{4,5},{5,4},{6,7},{7,6},{8,9},{9,8},{10,11... | collective-permute-start | bytes 417800 | tf_op jit(solution)/shard_map/ppermute | solution.py:665
  114.3 8.1 %collective-permute-start.25 = (bf16[272,512]{1,0:T(8,128)(2,1)S(1)}, bf16[272,512]{1,0:T(8,128)(2,1)S(1)}, u32[]{:S(2)}, u32[]{:S(2)}) collective-permute-start(bf16[272,512]{1,0:T(8,128)(2,1)S(1)} %get-tuple-element.94.refs_1_), channel_id=1, source_target_pairs={{0,1},{1,0},{2,3},{3,2},{4,5},{5,4},{6,7},{7,6},{8,9},{9,8},{10,11... | collective-permute-start | bytes 835592 | tf_op jit(solution)/shard_map/ppermute | solution.py:665

commit v11 on v10

--- a/solution.py
+++ b/solution.py
@@ -319,7 +319,7 @@
     )(ids, normed, near_memory(weight))
 
 
-BLOCK = 2 * ROWS
+BLOCK = 4 * ROWS
 LOG2E = 1.4426950408889634
 
 
@@ -607,31 +607,42 @@
 
 
 def backward_kernel(mine, firsts, count, ids, *refs):
-    slopes_in, starts, (weight, out, level, lower, upper) = (
+    slopes_in, starts, (weight, out) = (
         refs[: len(firsts)],
         refs[len(firsts) : len(firsts) + count],
         refs[len(firsts) + count :],
     )
     half = weight.shape[1]
     side = ids[0] if mine else 1 - ids[0]
-    level[...] = jnp.zeros_like(level)
-    lower[...] = jnp.zeros_like(lower)
-    upper[...] = jnp.zeros_like(upper)
-
-    for begin, slope in zip(firsts, slopes_in):
-
-        def tile(i):
-            at = lanes(side * half + begin + i * TILE, TILE)
-            part = slope[:, lanes(i * TILE, TILE)]
-            first, mid, last = (dot_t(part, weight[t, :, at]) for t in range(3))
-            level[...] += first[ROWS:] + mid[:ROWS] + mid[ROWS:] + last[:ROWS]
-            lower[...] += first[:ROWS]
-            upper[...] += last[ROWS:]
-
-        tiles(slope.shape[1] // TILE, tile)
-    total = level[...] + below(lower[...], ROWS) + above(upper[...], ROWS)
-    base = jnp.concatenate([start[...] for start in starts], axis=1)
-    out[...] = (base + total[:OWN]).astype(out.dtype)
+    whole = [start for start in starts if start.shape[1] == half]
+    chunks = [start for start in starts if start.shape[1] < half]
+
+    def tile(i, chunk, begin):
+        inner = lanes(i * TILE, TILE)
+        first = mid = last = None
+        for offset, slope in zip(firsts, slopes_in):
+            at = pl.ds(pl.multiple_of(side * half + offset, TILE), slope.shape[1])
+            terms = [dot_t(slope[...], weight[t, inner, at]) for t in range(3)]
+            if first is None:
+                first, mid, last = terms
+            else:
+                first, mid, last = first + terms[0], mid + terms[1], last + terms[2]
+        total = first[ROWS:] + mid[:ROWS] + mid[ROWS:] + last[:ROWS]
+        total = total + below(first[:ROWS], ROWS) + above(last[ROWS:], ROWS)
+        total = total[:OWN]
+        for start in whole:
+            total = total + start[:, inner]
+        if chunk is not None:
+            total = total + chunk[:, lanes(i * TILE - begin, TILE)]
+        out[:, inner] = total.astype(out.dtype)
+
+    if not chunks:
+        tiles(half // TILE, lambda i: tile(i, None, 0))
+    begin = 0
+    for chunk in chunks:
+        width = chunk.shape[1]
+        tiles(width // TILE, lambda i: tile(i + begin // TILE, chunk, begin))
+        begin += width
 
 
 def backward(ids, parts, starts, weight, mine, dtype):
@@ -642,7 +653,6 @@
         in_specs=[SM] + [VM] * (len(parts) + len(starts) + 1),
         out_specs=VM,
         out_shape=shape((OWN, half), dtype),
-        scratch_shapes=[pltpu.VMEM((ROWS, half), F32)] * 3,
         compiler_params=params(10),
         cost_estimate=cost(100 * 2 * 3 * half * size, 6 * size),
         name="backward",
@@ -725,7 +735,7 @@
     sent = swap(output(ids, heads, out_weight, False, BF16))
     kept = output(ids, heads, out_weight, True, F32)
     half = decoder_weight.shape[1]
-    split = TILE
+    split = 2 * TILE
     inputs, early = decode_first(ids, kept, sent, encoded, decoder_weight, split)
     early = swap(early)
     late = decode(ids, inputs, decoder_weight, False, split, half - split, BF16)

time: 125 us -> 123 us (0.984)
  waiting for transfers between devices: 37.4 us -> 34.9 us
    ppermute x6, waiting for transfers between devices: 16.6 us -> 14.1 us  [swap(): return lax.ppermute(value, 'head', [(0, 1), (1, 0)])]
  transfers between devices with their start and end apart: 27 -> 27, of which waited for: 14 -> 15; matrix products, arithmetic and copies ran while one was open for 0% -> 0% of each run, Pallas kernels for 18% -> 19%
where the time goes in v11:
time: 123 us
  starting transfers between devices  44.1 us (36%)
  Pallas kernels  42.7 us (35%)
  waiting for transfers between devices  34.9 us (28%)
    ppermute x20, starting transfers between devices, send(): return lax.ppermute(value, 'seq', moves(**step))  29.4 us
    ppermute x20, waiting for transfers between devices, send(): return lax.ppermute(value, 'seq', moves(**step))  20.8 us
    ppermute x6, waiting for transfers between devices, swap(): return lax.ppermute(value, 'head', [(0, 1), (1, 0)])  14.1 us
    ppermute x6, starting transfers between devices, swap(): return lax.ppermute(value, 'head', [(0, 1), (1, 0)])  14.1 us
    pallas_call x2, Pallas kernels, attend(): pl.pallas_call(functools.partial(attend_kernel, len(pieces), len(inverses...  10.4 us
    pallas_call x3, Pallas kernels, backward(): pl.pallas_call(functools.partial(backward_kernel, mine, [first for first,...  7.37 us
    pallas_call x1, Pallas kernels, encode(): pl.pallas_call(encode_kernel, in_specs=[SM] + [VM] * 5 + [HBM], out_specs...  4.35 us
    pallas_call x2, Pallas kernels, slopes(): pl.pallas_call(functools.partial(slope_kernel, first), in_specs=[SM] + [V...  3.97 us
  transfers between devices with their start and end apart: 27, of which 15 were waited for; matrix products, arithmetic and copies ran while one was open for 0% of the time, Pallas kernels for 19%

profile of v11, /device:TPU:0, one launch (start us, length us, event | category | flops | bytes accessed | tf_op | source)
XLA Modules:
  0.0 122.9 jit_solution(5551886072241409347)
XLA Ops:
  0.6 0.1 pad_add_fusion.ids
  0.7 1.4 %prepare.1 = (bf16[128,128]{1,0:T(8,128)(2,1)S(1)}, bf16[8,1664]{1,0:T(8,128)(2,1)S(1)}, bf16[8,1664]{1,0:T(8,128)(2,1)S(1)}) custom-call(s32[3]{0:T(128)S(1)} %pad_add_fusion.ids, s32[128,128]{1,0:T(8,128)} %bitcast.6, bf16[256,1536]{1,0:T(8,128)(2,1)} %grad.5), custom_call_target="tpu_custom_call" | custom-call | flops 100000 | bytes 100000 | tf_op jit(solution)/shard_map/prepare/pallas_call | solution.py:111
  2.2 0.1 collective-permute-start
  2.3 0.7 collective-permute-start.1
  2.9 3.3 %load.1 = (bf16[256,1536]{1,0:T(8,128)(2,1)S(1)}, bf16[256,1536]{1,0:T(8,128)(2,1)S(1)}, bf16[3,1536,768]{2,1,0:T(8,128)(2,1)S(1)}) custom-call(bf16[128,128]{1,0:T(8,128)(2,1)S(1)} %get-tuple-element.52.codes, bf16[256,1536]{1,0:T(8,128)(2,1)} %stems.1, bf16[3,1536,768]{2,1,0:T(8,128)(2,1)} %weights.1), custom_call_target="tpu_custom_call" | custom-call | flops 100000 | bytes 7077888 | tf_op jit(solution)/shard_map/load/pallas_call | solution.py:163
  6.2 0.0 collective-permute-done.1.far
  6.2 0.0 copy-start.3
  6.3 4.3 %encode.1 = (bf16[272,768]{1,0:T(8,128)(2,1)S(1)}, bf16[3,1536,768]{2,1,0:T(8,128)(2,1)S(1)}) custom-call(s32[3]{0:T(128)S(1)} %pad_add_fusion.ids, bf16[8,1664]{1,0:T(8,128)(2,1)S(1)} %collective-permute-done.near, bf16[8,1664]{1,0:T(8,128)(2,1)S(1)} %collective-permute-done.1.far, bf16[256,1536]{1,0:T(8,128)(2,1)S(1)} %get-tuple-element.53.rows, ...), custom_call_target="tpu_custom_call" | custom-call | flops 1811939328 | bytes 14155776 | tf_op jit(solution)/shard_map/encode/pallas_call | solution.py:218
  10.6 3.4 %collective-permute-start.2 = (bf16[272,768]{1,0:T(8,128)(2,1)S(1)}, bf16[272,768]{1,0:T(8,128)(2,1)S(1)}, u32[]{:S(2)}, u32[]{:S(2)}) collective-permute-start(bf16[272,768]{1,0:T(8,128)(2,1)S(1)} %get-tuple-element.56.mine.encoded), channel_id=1, source_target_pairs={{0,1},{1,0},{2,3},{3,2},{4,5},{5,4},{6,7},{7,6},{8,9},{9,8},{10,11... | collective-permute-start | bytes 1253384 | tf_op jit(solution)/shard_map/ppermute | solution.py:675
  14.0 8.6 %collective-permute-done.2.theirs = bf16[272,768]{1,0:T(8,128)(2,1)S(1)} collective-permute-done((bf16[272,768]{1,0:T(8,128)(2,1)S(1)}, bf16[272,768]{1,0:T(8,128)(2,1)S(1)}, u32[]{:S(2)}, u32[]{:S(2)}) %collective-permute-start.2) | collective-permute-done | bytes 417824 | tf_op jit(solution)/shard_map/ppermute | solution.py:675
  22.6 2.0 %project_keys.1 = (bf16[2,136,768]{2,1,0:T(8,128)(2,1)S(1)}, bf16[128,384]{1,0:T(8,128)(2,1)S(1)}, bf16[128,384]{1,0:T(8,128)(2,1)S(1)}, bf16[128,384]{1,0:T(8,128)(2,1)S(1)}, bf16[128,384]{1,0:T(8,128)(2,1)S(1)}) custom-call(s32[3]{0:T(128)S(1)} %pad_add_fusion.ids, bf16[272,768]{1,0:T(8,128)(2,1)S(1)} %get-tuple-element.56.mine.encoded, ...), custom_call_target="tpu_custom_call" | custom-call | flops 641728512 | bytes 7077888 | tf_op jit(solution)/shard_map/project_keys/pallas_call | solution.py:282
  24.7 0.0 copy-start.2
  24.7 5.7 %collective-permute-start.3 = (bf16[128,384]{1,0:T(8,128)(2,1)S(1)}, bf16[128,384]{1,0:T(8,128)(2,1)S(1)}, u32[]{:S(2)}, u32[]{:S(2)}) collective-permute-start(bf16[128,384]{1,0:T(8,128)(2,1)S(1)} %get-tuple-element.61), channel_id=1, source_target_pairs={{0,32},{2,34},{4,36},{6,38},{8,40},{10,42},{12,44},{14,46},{16,48}... | collective-permute-start | bytes 294920 | tf_op jit(solution)/shard_map/ppermute | solution.py:679
  30.4 1.6 %collective-permute-start.4 = (bf16[128,384]{1,0:T(8,128)(2,1)S(1)}, bf16[128,384]{1,0:T(8,128)(2,1)S(1)}, u32[]{:S(2)}, u32[]{:S(2)}) collective-permute-start(bf16[128,384]{1,0:T(8,128)(2,1)S(1)} %get-tuple-element.62), channel_id=1, source_target_pairs={{0,96},{2,98},{4,100},{6,102},{8,104},{10,106},{12,108},{14,110},{... | collective-permute-start | bytes 294920 | tf_op jit(solution)/shard_map/ppermute | solution.py:679
  32.0 2.0 %collective-permute-start.5 = (bf16[128,384]{1,0:T(8,128)(2,1)S(1)}, bf16[128,384]{1,0:T(8,128)(2,1)S(1)}, u32[]{:S(2)}, u32[]{:S(2)}) collective-permute-start(bf16[128,384]{1,0:T(8,128)(2,1)S(1)} %get-tuple-element.63), channel_id=1, source_target_pairs={{0,64},{2,66},{4,68},{6,70},{8,72},{10,74},{12,76},{14,78},{16,80}... | collective-permute-start | bytes 294920 | tf_op jit(solution)/shard_map/ppermute | solution.py:679
  34.0 1.6 %collective-permute-done.3 = bf16[128,384]{1,0:T(8,128)(2,1)S(1)} collective-permute-done((bf16[128,384]{1,0:T(8,128)(2,1)S(1)}, bf16[128,384]{1,0:T(8,128)(2,1)S(1)}, u32[]{:S(2)}, u32[]{:S(2)}) %collective-permute-start.3) | collective-permute-done | bytes 98336 | tf_op jit(solution)/shard_map/ppermute | solution.py:679
  35.5 2.6 %collective-permute-done.5 = bf16[128,384]{1,0:T(8,128)(2,1)S(1)} collective-permute-done((bf16[128,384]{1,0:T(8,128)(2,1)S(1)}, bf16[128,384]{1,0:T(8,128)(2,1)S(1)}, u32[]{:S(2)}, u32[]{:S(2)}) %collective-permute-start.5) | collective-permute-done | bytes 98336 | tf_op jit(solution)/shard_map/ppermute | solution.py:679
  38.2 2.2 %collective-permute-start.6 = (bf16[512,384]{1,0:T(8,128)(2,1)S(1)}, bf16[512,384]{1,0:T(8,128)(2,1)S(1)}, u32[]{:S(2)}, u32[]{:S(2)}) collective-permute-start(bf16[512,384]{1,0:T(8,128)(2,1)S(1)} %constant_dynamic-update-slice_fusion.refs_0_), channel_id=1, source_target_pairs={{0,8},{2,10},{4,12},{6,14},{8,16},{10,18},{12,20},{14,22},{16,24},... | collective-permute-start | bytes 1179656 | tf_op jit(solution)/shard_map/ppermute | solution.py:679
  40.3 2.2 %collective-permute-start.7 = (bf16[512,384]{1,0:T(8,128)(2,1)S(1)}, bf16[512,384]{1,0:T(8,128)(2,1)S(1)}, u32[]{:S(2)}, u32[]{:S(2)}) collective-permute-start(bf16[512,384]{1,0:T(8,128)(2,1)S(1)} %constant_dynamic-update-slice_fusion.refs_0_), channel_id=1, source_target_pairs={{0,24},{2,26},{4,28},{6,30},{8,0},{10,2},{12,4},{14,6},{16,8},{18,... | collective-permute-start | bytes 1179656 | tf_op jit(solution)/shard_map/ppermute | solution.py:679
  42.5 1.3 %project_queries.1 = (bf16[136,256]{1,0:T(8,128)(2,1)S(1)}, bf16[136,256]{1,0:T(8,128)(2,1)S(1)}, bf16[136,256]{1,0:T(8,128)(2,1)S(1)}, bf16[136,256]{1,0:T(8,128)(2,1)S(1)}) custom-call(s32[3]{0:T(128)S(1)} %pad_add_fusion.ids, bf16[2,136,768]{2,1,0:T(8,128)(2,1)S(1)} %get-tuple-element.58.normed, bf16[3,1536,768]{2,1,0:T(8,128)(2,1)S(1)} %get-tuple-element.57.weight), custom_call_target="tpu_custom_call" | custom-call | flops 320864256 | bytes 3538944 | tf_op jit(solution)/shard_map/project_queries/pallas_call | solution.py:310
  43.8 1.9 %collective-permute-start.10 = (bf16[136,256]{1,0:T(8,128)(2,1)S(1)}, bf16[136,256]{1,0:T(8,128)(2,1)S(1)}, u32[]{:S(2)}, u32[]{:S(2)}) collective-permute-start(bf16[136,256]{1,0:T(8,128)(2,1)S(1)} %get-tuple-element.70), channel_id=1, source_target_pairs={{0,64},{2,66},{4,68},{6,70},{8,72},{10,74},{12,76},{14,78},{16,80}... | collective-permute-start | bytes 208904 | tf_op jit(solution)/shard_map/ppermute | solution.py:679
  45.7 0.7 collective-permute-start.8
  46.4 2.6 %collective-permute-start.9 = (bf16[136,256]{1,0:T(8,128)(2,1)S(1)}, bf16[136,256]{1,0:T(8,128)(2,1)S(1)}, u32[]{:S(2)}, u32[]{:S(2)}) collective-permute-start(bf16[136,256]{1,0:T(8,128)(2,1)S(1)} %get-tuple-element.69), channel_id=1, source_target_pairs={{0,96},{2,98},{4,100},{6,102},{8,104},{10,106},{12,108},{14,110},{... | collective-permute-start | bytes 208904 | tf_op jit(solution)/shard_map/ppermute | solution.py:679
  49.0 0.7 collective-permute-done.10
  49.7 0.0 collective-permute-start.13
  49.7 1.5 %collective-permute-done.8 = bf16[136,256]{1,0:T(8,128)(2,1)S(1)} collective-permute-done((bf16[136,256]{1,0:T(8,128)(2,1)S(1)}, bf16[136,256]{1,0:T(8,128)(2,1)S(1)}, u32[]{:S(2)}, u32[]{:S(2)}) %collective-permute-start.8) | collective-permute-done | bytes 69664 | tf_op jit(solution)/shard_map/ppermute | solution.py:679
  51.3 0.1 collective-permute-start.14
  51.3 0.5 collective-permute-start.15
  51.9 0.8 collective-permute-start.16
  52.7 1.2 collective-permute-start.11
  53.9 2.1 %collective-permute-start.12 = (bf16[256,384]{1,0:T(8,128)(2,1)S(1)}, bf16[256,384]{1,0:T(8,128)(2,1)S(1)}, u32[]{:S(2)}, u32[]{:S(2)}) collective-permute-start(bf16[256,384]{1,0:T(8,128)(2,1)S(1)} %slice.7), channel_id=1, source_target_pairs={{0,24},{2,26},{4,28},{6,30},{8,0},{10,2},{12,4},{14,6},{16,8},{18,... | collective-permute-start | bytes 589832 | tf_op jit(solution)/shard_map/ppermute | solution.py:679
  56.0 4.6 %collective-permute-done.11 = bf16[256,384]{1,0:T(8,128)(2,1)S(1)} collective-permute-done((bf16[256,384]{1,0:T(8,128)(2,1)S(1)}, bf16[256,384]{1,0:T(8,128)(2,1)S(1)}, u32[]{:S(2)}, u32[]{:S(2)}) %collective-permute-start.11) | collective-permute-done | bytes 196640 | tf_op jit(solution)/shard_map/ppermute | solution.py:679
  60.7 0.0 copy-start
  60.7 0.3 collective-permute-start.17
  61.0 1.7 %collective-permute-done.17.refs_7_ = bf16[512,384]{1,0:T(8,128)(2,1)S(1)} collective-permute-done((bf16[512,384]{1,0:T(8,128)(2,1)S(1)}, bf16[512,384]{1,0:T(8,128)(2,1)S(1)}, u32[]{:S(2)}, u32[]{:S(2)}) %collective-permute-start.17) | collective-permute-done | bytes 393248 | tf_op jit(solution)/shard_map/ppermute | solution.py:679
  62.7 5.8 %attend.2 = (bf16[544,256]{1,0:T(8,128)(2,1)S(1)}, f32[8,4096]{1,0:T(8,128)S(1)}) custom-call(s32[3]{0:T(128)S(1)} %pad_add_fusion.ids, f32[4]{0:T(128)S(1)} %copy-done.2, bf16[544,256]{1,0:T(8,128)(2,1)S(1)} %collective-permute-done.16.queries, bf16[512,384]{1,0:T(8,128)(2,1)S(1)} %constant_dynamic-update-slice_fusion.refs_0_, ...), custom_call_target="tpu_custom_call" | custom-call | flops 2281701376 | bytes 4456448 | tf_op jit(solution)/shard_map/attend/pallas_call | solution.py:431
  68.5 1.4 %collective-permute-start.18 = (bf16[544,256]{1,0:T(8,128)(2,1)S(1)}, bf16[544,256]{1,0:T(8,128)(2,1)S(1)}, u32[]{:S(2)}, u32[]{:S(2)}) collective-permute-start(bf16[544,256]{1,0:T(8,128)(2,1)S(1)} %get-tuple-element.83), channel_id=1, source_target_pairs={{0,4},{2,6},{4,0},{6,2},{8,12},{10,14},{12,8},{14,10},{16,20},{18,... | collective-permute-start | bytes 835592 | tf_op jit(solution)/shard_map/ppermute | solution.py:679
  69.9 4.6 %attend.3.a0 = bf16[544,256]{1,0:T(8,128)(2,1)S(1)} custom-call(s32[3]{0:T(128)S(1)} %pad_add_fusion.ids, f32[4]{0:T(128)S(1)} %copy-done.2, bf16[544,256]{1,0:T(8,128)(2,1)S(1)} %constant_dynamic-update-slice_fusion.4.queries, bf16[512,384]{1,0:T(8,128)(2,1)S(1)} %constant_dynamic-update-slice_fusion.refs_0_, ...), custom_call_target="tpu_custom_call" | custom-call | flops 2281701376 | bytes 4456448 | tf_op jit(solution)/shard_map/attend/pallas_call | solution.py:431
  74.5 2.7 %collective-permute-done.18.a1 = bf16[544,256]{1,0:T(8,128)(2,1)S(1)} collective-permute-done((bf16[544,256]{1,0:T(8,128)(2,1)S(1)}, bf16[544,256]{1,0:T(8,128)(2,1)S(1)}, u32[]{:S(2)}, u32[]{:S(2)}) %collective-permute-start.18) | collective-permute-done | bytes 278560 | tf_op jit(solution)/shard_map/ppermute | solution.py:679
  77.3 0.5 merge.1
  77.8 3.2 %collective-permute-start.19 = (bf16[136,256]{1,0:T(8,128)(2,1)S(1)}, bf16[136,256]{1,0:T(8,128)(2,1)S(1)}, u32[]{:S(2)}, u32[]{:S(2)}) collective-permute-start(bf16[136,256]{1,0:T(8,128)(2,1)S(1)} %get-tuple-element.85), channel_id=1, source_target_pairs={{0,96},{2,98},{4,100},{6,102},{8,104},{10,106},{12,108},{14,110},{... | collective-permute-start | bytes 208904 | tf_op jit(solution)/shard_map/ppermute | solution.py:679
  81.0 0.9 collective-permute-start.21
  81.9 1.7 %collective-permute-done.19.a1 = bf16[136,256]{1,0:T(8,128)(2,1)S(1)} collective-permute-done((bf16[136,256]{1,0:T(8,128)(2,1)S(1)}, bf16[136,256]{1,0:T(8,128)(2,1)S(1)}, u32[]{:S(2)}, u32[]{:S(2)}) %collective-permute-start.19) | collective-permute-done | bytes 69664 | tf_op jit(solution)/shard_map/ppermute | solution.py:679
  83.6 3.3 %collective-permute-done.20.a2 = bf16[136,256]{1,0:T(8,128)(2,1)S(1)} collective-permute-done((bf16[136,256]{1,0:T(8,128)(2,1)S(1)}, bf16[136,256]{1,0:T(8,128)(2,1)S(1)}, u32[]{:S(2)}, u32[]{:S(2)}) %collective-permute-start.20) | collective-permute-done | bytes 69664 | tf_op jit(solution)/shard_map/ppermute | solution.py:679
  86.9 0.4 collective-permute-done.21.a3
  87.3 1.3 %output.3 = bf16[136,768]{1,0:T(8,128)(2,1)S(1)} custom-call(s32[3]{0:T(128)S(1)} %pad_add_fusion.ids, bf16[136,256]{1,0:T(8,128)(2,1)S(1)} %get-tuple-element.84.a0, bf16[136,256]{1,0:T(8,128)(2,1)S(1)} %collective-permute-done.19.a1, bf16[136,256]{1,0:T(8,128)(2,1)S(1)} %collective-permute-done.20.a2, bf16[136,256]{1,0:T(8,128)(2,1)S(1)} %collective-permute-done.21.a3, ...), custom_call_target="tpu_custom_call" | custom-call | flops 160432128 | bytes 1179648 | tf_op jit(solution)/shard_map/output/pallas_call | solution.py:485
  88.5 3.3 %collective-permute-start.22 = (bf16[136,768]{1,0:T(8,128)(2,1)S(1)}, bf16[136,768]{1,0:T(8,128)(2,1)S(1)}, u32[]{:S(2)}, u32[]{:S(2)}) collective-permute-start(bf16[136,768]{1,0:T(8,128)(2,1)S(1)} %output.3), channel_id=1, source_target_pairs={{0,1},{1,0},{2,3},{3,2},{4,5},{5,4},{6,7},{7,6},{8,9},{9,8},{10,11... | collective-permute-start | bytes 626696 | tf_op jit(solution)/shard_map/ppermute | solution.py:675
  91.9 1.3 %output.2.own = f32[136,768]{1,0:T(8,128)S(1)} custom-call(s32[3]{0:T(128)S(1)} %pad_add_fusion.ids, bf16[136,256]{1,0:T(8,128)(2,1)S(1)} %get-tuple-element.84.a0, bf16[136,256]{1,0:T(8,128)(2,1)S(1)} %collective-permute-done.19.a1, bf16[136,256]{1,0:T(8,128)(2,1)S(1)} %collective-permute-done.20.a2, bf16[136,256]{1,0:T(8,128)(2,1)S(1)} %collective-permute-done.21.a3, ...), custom_call_target="tpu_custom_call" | custom-call | flops 160432128 | bytes 1179648 | tf_op jit(solution)/shard_map/output/pallas_call | solution.py:485
  93.2 2.8 %collective-permute-done.22.other = bf16[136,768]{1,0:T(8,128)(2,1)S(1)} collective-permute-done((bf16[136,768]{1,0:T(8,128)(2,1)S(1)}, bf16[136,768]{1,0:T(8,128)(2,1)S(1)}, u32[]{:S(2)}, u32[]{:S(2)}) %collective-permute-start.22) | collective-permute-done | bytes 208928 | tf_op jit(solution)/shard_map/ppermute | solution.py:675
  95.9 1.7 %decode_first.1 = (bf16[272,768]{1,0:T(8,128)(2,1)S(1)}, bf16[272,512]{1,0:T(8,128)(2,1)S(1)}) custom-call(s32[3]{0:T(128)S(1)} %pad_add_fusion.ids, f32[136,768]{1,0:T(8,128)S(1)} %output.2.own, bf16[136,768]{1,0:T(8,128)(2,1)S(1)} %collective-permute-done.22.other, bf16[272,768]{1,0:T(8,128)(2,1)S(1)} %get-tuple-element.56.mine.encoded, ...), custom_call_target="tpu_custom_call" | custom-call | flops 1000000 | bytes 10000 | tf_op jit(solution)/shard_map/decode_first/pallas_call | solution.py:526
  97.7 3.6 %collective-permute-start.24 = (bf16[272,512]{1,0:T(8,128)(2,1)S(1)}, bf16[272,512]{1,0:T(8,128)(2,1)S(1)}, u32[]{:S(2)}, u32[]{:S(2)}) collective-permute-start(bf16[272,512]{1,0:T(8,128)(2,1)S(1)} %get-tuple-element.91), channel_id=1, source_target_pairs={{0,1},{1,0},{2,3},{3,2},{4,5},{5,4},{6,7},{7,6},{8,9},{9,8},{10,11... | collective-permute-start | bytes 835592 | tf_op jit(solution)/shard_map/ppermute | solution.py:675
  101.2 1.7 %decode.2 = bf16[272,256]{1,0:T(8,128)(2,1)} custom-call(s32[3]{0:T(128)S(1)} %pad_add_fusion.ids, bf16[272,768]{1,0:T(8,128)(2,1)S(1)} %get-tuple-element.89.inputs, bf16[3,768,1536]{2,1,0:T(8,128)(2,1)S(1)} %bitcast.5), custom_call_target="tpu_custom_call" | custom-call | flops 1000000 | bytes 10000 | tf_op jit(solution)/shard_map/decode/pallas_call | solution.py:544
  102.9 0.3 collective-permute-start.23
  103.2 2.1 %decode.3.own = f32[272,768]{1,0:T(8,128)S(1)} custom-call(s32[3]{0:T(128)S(1)} %pad_add_fusion.ids, bf16[272,768]{1,0:T(8,128)(2,1)S(1)} %get-tuple-element.89.inputs, bf16[3,768,1536]{2,1,0:T(8,128)(2,1)S(1)} %bitcast.5), custom_call_target="tpu_custom_call" | custom-call | flops 1000000 | bytes 10000 | tf_op jit(solution)/shard_map/decode/pallas_call | solution.py:544
  105.3 2.2 %collective-permute-done.24.other = bf16[272,512]{1,0:T(8,128)(2,1)S(1)} collective-permute-done((bf16[272,512]{1,0:T(8,128)(2,1)S(1)}, bf16[272,512]{1,0:T(8,128)(2,1)S(1)}, u32[]{:S(2)}, u32[]{:S(2)}) %collective-permute-start.24) | collective-permute-done | bytes 278560 | tf_op jit(solution)/shard_map/ppermute | solution.py:675
  107.5 1.9 %slopes.2 = (bf16[256,512]{1,0:T(8,128)(2,1)S(1)}, bf16[272,512]{1,0:T(8,128)(2,1)}, f32[128,512]{1,0:T(8,128)S(1)}) custom-call(s32[3]{0:T(128)S(1)} %pad_add_fusion.ids, f32[272,768]{1,0:T(8,128)S(1)} %decode.3.own, bf16[272,512]{1,0:T(8,128)(2,1)S(1)} %collective-permute-done.24.other, bf16[272,768]{1,0:T(8,128)(2,1)S(1)} %get-tuple-element.89.inputs, ...), custom_call_target="tpu_custom_call" | custom-call | flops 417792000000 | bytes 1949696 | tf_op jit(solution)/shard_map/slopes/pallas_call | solution.py:593
  109.5 2.0 %collective-permute-start.26 = (bf16[272,512]{1,0:T(8,128)(2,1)}, bf16[272,512]{1,0:T(8,128)(2,1)}, u32[]{:S(2)}, u32[]{:S(2)}) collective-permute-start(bf16[272,512]{1,0:T(8,128)(2,1)} %get-tuple-element.95.refs_0_), channel_id=1, source_target_pairs={{0,1},{1,0},{2,3},{3,2},{4,5},{5,4},{6,7},{7,6},{8,9},{9,8},{10,11... | collective-permute-start | bytes 835592 | tf_op jit(solution)/shard_map/ppermute | solution.py:675
  111.5 2.0 %slopes.3 = (bf16[256,768]{1,0:T(8,128)(2,1)}, bf16[272,256]{1,0:T(8,128)(2,1)}, f32[128,256]{1,0:T(8,128)S(1)}) custom-call(s32[3]{0:T(128)S(1)} %pad_add_fusion.ids, f32[272,768]{1,0:T(8,128)S(1)} %decode.3.own, bf16[272,256]{1,0:T(8,128)(2,1)} %collective-permute-done.23.other, bf16[272,768]{1,0:T(8,128)(2,1)S(1)} %get-tuple-element.89.inputs, ...), custom_call_target="tpu_custom_call" | custom-call | flops 208896000000 | bytes 974848 | tf_op jit(solution)/shard_map/slopes/pallas_call | solution.py:593
  113.5 1.5 %collective-permute-start.25 = (bf16[272,256]{1,0:T(8,128)(2,1)}, bf16[272,256]{1,0:T(8,128)(2,1)}, u32[]{:S(2)}, u32[]{:S(2)}) collective-permute-start(bf16[272,256]{1,0:T(8,128)(2,1)} %get-tuple-element.94.refs_1_), channel_id=1, source_target_pairs={{0,1},{1,0},{2,3},{3,2},{4,5},{5,4},{6,7},{7,6},{8,9},{9,8},{10,11... | collective-permute-start | bytes 417800 | tf_op jit(solution)/shard_map/ppermute | solution.py:675
  115.0 2.6 %backward.3.refs_1_ = f32[128,768]{1,0:T(8,128)S(1)} custom-call(s32[3]{0:T(128)S(1)} %pad_add_fusion.ids, bf16[272,512]{1,0:T(8,128)(2,1)} %get-tuple-element.95.refs_0_, bf16[272,256]{1,0:T(8,128)(2,1)} %get-tuple-element.94.refs_1_, f32[128,512]{1,0:T(8,128)S(1)} %get-tuple-element.96.refs_2_, f32[128,256]{1,0:T(8,128)S(1)} %get-tuple-element.97.refs_3_, ...), custom_call_target="tpu_custom_call" | custom-call | flops 96259276800 | bytes 1253376 | tf_op jit(solution)/shard_map/backward/pallas_call | solution.py:651
  117.6 0.2 collective-permute-done.26.refs_0_
  117.8 2.2 %backward.4.refs_1_ = f32[128,768]{1,0:T(8,128)S(1)} custom-call(s32[3]{0:T(128)S(1)} %pad_add_fusion.ids, bf16[272,512]{1,0:T(8,128)(2,1)} %collective-permute-done.26.refs_0_, f32[128,768]{1,0:T(8,128)S(1)} %backward.3.refs_1_, bf16[3,768,1536]{2,1,0:T(8,128)(2,1)S(1)} %bitcast.5), custom_call_target="tpu_custom_call" | custom-call | flops 64172851200 | bytes 835584 | tf_op jit(solution)/shard_map/backward/pallas_call | solution.py:651
  120.1 0.3 collective-permute-done.25.refs_0_
  120.4 2.5 %backward.5 = bf16[128,768]{1,0:T(8,128)(2,1)} custom-call(s32[3]{0:T(128)S(1)} %pad_add_fusion.ids, bf16[272,256]{1,0:T(8,128)(2,1)} %collective-permute-done.25.refs_0_, f32[128,768]{1,0:T(8,128)S(1)} %backward.4.refs_1_, bf16[3,768,1536]{2,1,0:T(8,128)(2,1)S(1)} %bitcast.5), custom_call_target="tpu_custom_call" | custom-call | flops 32086425600 | bytes 417792 | tf_op jit(solution)/shard_map/backward/pallas_call | solution.py:651
  (35 shorter events, 0.2 us)
Async XLA Ops:
  2.2 4.1 %collective-permute-start = (bf16[8,1664]{1,0:T(8,128)(2,1)S(1)}, bf16[8,1664]{1,0:T(8,128)(2,1)S(1)}, u32[]{:S(2)}, u32[]{:S(2)}) collective-permute-start(bf16[8,1664]{1,0:T(8,128)(2,1)S(1)} %get-tuple-element.50), channel_id=1, source_target_pairs={{0,2},{2,0},{4,6},{6,4},{8,10},{10,8},{12,14},{14,12},{16,18},{18,... | collective-permute-start | bytes 79880 | tf_op jit(solution)/shard_map/ppermute | solution.py:679
  2.3 4.0 %collective-permute-start.1 = (bf16[8,1664]{1,0:T(8,128)(2,1)S(1)}, bf16[8,1664]{1,0:T(8,128)(2,1)S(1)}, u32[]{:S(2)}, u32[]{:S(2)}) collective-permute-start(bf16[8,1664]{1,0:T(8,128)(2,1)S(1)} %get-tuple-element.51), channel_id=1, source_target_pairs={{2,4},{6,8},{10,12},{14,16},{18,20},{22,24},{26,28},{30,32},{34,36... | collective-permute-start | bytes 79880 | tf_op jit(solution)/shard_map/ppermute | solution.py:701
  6.2 7.7 %copy-start.3 = (f32[1536]{0:T(1024)S(1)}, f32[1536]{0:T(1024)}, u32[]{:S(2)}) copy-start(f32[1536]{0:T(1024)} %param.12) | copy-start | bytes 18436
  10.6 12.0 %collective-permute-start.2 = (bf16[272,768]{1,0:T(8,128)(2,1)S(1)}, bf16[272,768]{1,0:T(8,128)(2,1)S(1)}, u32[]{:S(2)}, u32[]{:S(2)}) collective-permute-start(bf16[272,768]{1,0:T(8,128)(2,1)S(1)} %get-tuple-element.56.mine.encoded), channel_id=1, source_target_pairs={{0,1},{1,0},{2,3},{3,2},{4,5},{5,4},{6,7},{7,6},{8,9},{9,8},{10,11... | collective-permute-start | bytes 1253384 | tf_op jit(solution)/shard_map/ppermute | solution.py:675
  24.7 38.1 %copy-start.2 = (f32[4]{0:T(128)S(1)}, f32[4]{0:T(128)}, u32[]{:S(2)}) copy-start(f32[4]{0:T(128)} %scale.3) | copy-start | bytes 52
  24.7 10.9 %collective-permute-start.3 = (bf16[128,384]{1,0:T(8,128)(2,1)S(1)}, bf16[128,384]{1,0:T(8,128)(2,1)S(1)}, u32[]{:S(2)}, u32[]{:S(2)}) collective-permute-start(bf16[128,384]{1,0:T(8,128)(2,1)S(1)} %get-tuple-element.61), channel_id=1, source_target_pairs={{0,32},{2,34},{4,36},{6,38},{8,40},{10,42},{12,44},{14,46},{16,48}... | collective-permute-start | bytes 294920 | tf_op jit(solution)/shard_map/ppermute | solution.py:679
  30.4 5.1 %collective-permute-start.4 = (bf16[128,384]{1,0:T(8,128)(2,1)S(1)}, bf16[128,384]{1,0:T(8,128)(2,1)S(1)}, u32[]{:S(2)}, u32[]{:S(2)}) collective-permute-start(bf16[128,384]{1,0:T(8,128)(2,1)S(1)} %get-tuple-element.62), channel_id=1, source_target_pairs={{0,96},{2,98},{4,100},{6,102},{8,104},{10,106},{12,108},{14,110},{... | collective-permute-start | bytes 294920 | tf_op jit(solution)/shard_map/ppermute | solution.py:679
  32.0 6.1 %collective-permute-start.5 = (bf16[128,384]{1,0:T(8,128)(2,1)S(1)}, bf16[128,384]{1,0:T(8,128)(2,1)S(1)}, u32[]{:S(2)}, u32[]{:S(2)}) collective-permute-start(bf16[128,384]{1,0:T(8,128)(2,1)S(1)} %get-tuple-element.63), channel_id=1, source_target_pairs={{0,64},{2,66},{4,68},{6,70},{8,72},{10,74},{12,76},{14,78},{16,80}... | collective-permute-start | bytes 294920 | tf_op jit(solution)/shard_map/ppermute | solution.py:679
  38.2 13.1 %collective-permute-start.6 = (bf16[512,384]{1,0:T(8,128)(2,1)S(1)}, bf16[512,384]{1,0:T(8,128)(2,1)S(1)}, u32[]{:S(2)}, u32[]{:S(2)}) collective-permute-start(bf16[512,384]{1,0:T(8,128)(2,1)S(1)} %constant_dynamic-update-slice_fusion.refs_0_), channel_id=1, source_target_pairs={{0,8},{2,10},{4,12},{6,14},{8,16},{10,18},{12,20},{14,22},{16,24},... | collective-permute-start | bytes 1179656 | tf_op jit(solution)/shard_map/ppermute | solution.py:679
  40.3 10.9 %collective-permute-start.7 = (bf16[512,384]{1,0:T(8,128)(2,1)S(1)}, bf16[512,384]{1,0:T(8,128)(2,1)S(1)}, u32[]{:S(2)}, u32[]{:S(2)}) collective-permute-start(bf16[512,384]{1,0:T(8,128)(2,1)S(1)} %constant_dynamic-update-slice_fusion.refs_0_), channel_id=1, source_target_pairs={{0,24},{2,26},{4,28},{6,30},{8,0},{10,2},{12,4},{14,6},{16,8},{18,... | collective-permute-start | bytes 1179656 | tf_op jit(solution)/shard_map/ppermute | solution.py:679
  43.8 5.9 %collective-permute-start.10 = (bf16[136,256]{1,0:T(8,128)(2,1)S(1)}, bf16[136,256]{1,0:T(8,128)(2,1)S(1)}, u32[]{:S(2)}, u32[]{:S(2)}) collective-permute-start(bf16[136,256]{1,0:T(8,128)(2,1)S(1)} %get-tuple-element.70), channel_id=1, source_target_pairs={{0,64},{2,66},{4,68},{6,70},{8,72},{10,74},{12,76},{14,78},{16,80}... | collective-permute-start | bytes 208904 | tf_op jit(solution)/shard_map/ppermute | solution.py:679
  45.7 5.5 %collective-permute-start.8 = (bf16[136,256]{1,0:T(8,128)(2,1)S(1)}, bf16[136,256]{1,0:T(8,128)(2,1)S(1)}, u32[]{:S(2)}, u32[]{:S(2)}) collective-permute-start(bf16[136,256]{1,0:T(8,128)(2,1)S(1)} %get-tuple-element.68), channel_id=1, source_target_pairs={{0,32},{2,34},{4,36},{6,38},{8,40},{10,42},{12,44},{14,46},{16,48}... | collective-permute-start | bytes 208904 | tf_op jit(solution)/shard_map/ppermute | solution.py:679
  46.4 4.8 %collective-permute-start.9 = (bf16[136,256]{1,0:T(8,128)(2,1)S(1)}, bf16[136,256]{1,0:T(8,128)(2,1)S(1)}, u32[]{:S(2)}, u32[]{:S(2)}) collective-permute-start(bf16[136,256]{1,0:T(8,128)(2,1)S(1)} %get-tuple-element.69), channel_id=1, source_target_pairs={{0,96},{2,98},{4,100},{6,102},{8,104},{10,106},{12,108},{14,110},{... | collective-permute-start | bytes 208904 | tf_op jit(solution)/shard_map/ppermute | solution.py:679
  49.7 4.2 %collective-permute-start.13 = (bf16[512,384]{1,0:T(8,128)(2,1)S(1)}, bf16[512,384]{1,0:T(8,128)(2,1)S(1)}, u32[]{:S(2)}, u32[]{:S(2)}) collective-permute-start(bf16[512,384]{1,0:T(8,128)(2,1)S(1)} %constant_dynamic-update-slice_fusion.refs_0_), channel_id=1, source_target_pairs={{0,2},{2,0},{4,6},{6,4},{8,10},{10,8},{12,14},{14,12},{16,18},{18,... | collective-permute-start | bytes 1179656 | tf_op jit(solution)/shard_map/ppermute | solution.py:679
  51.3 9.4 %collective-permute-start.14 = (bf16[512,384]{1,0:T(8,128)(2,1)S(1)}, bf16[512,384]{1,0:T(8,128)(2,1)S(1)}, u32[]{:S(2)}, u32[]{:S(2)}) collective-permute-start(bf16[512,384]{1,0:T(8,128)(2,1)S(1)} %collective-permute-done.6.refs_1_), channel_id=1, source_target_pairs={{0,2},{2,0},{4,6},{6,4},{8,10},{10,8},{12,14},{14,12},{16,18},{18,... | collective-permute-start | bytes 1179656 | tf_op jit(solution)/shard_map/ppermute | solution.py:679
  51.3 9.3 %collective-permute-start.15 = (bf16[512,384]{1,0:T(8,128)(2,1)S(1)}, bf16[512,384]{1,0:T(8,128)(2,1)S(1)}, u32[]{:S(2)}, u32[]{:S(2)}) collective-permute-start(bf16[512,384]{1,0:T(8,128)(2,1)S(1)} %collective-permute-done.7.refs_2_), channel_id=1, source_target_pairs={{0,2},{2,0},{4,6},{6,4},{8,10},{10,8},{12,14},{14,12},{16,18},{18,... | collective-permute-start | bytes 1179656 | tf_op jit(solution)/shard_map/ppermute | solution.py:679
  51.9 8.8 %collective-permute-start.16 = (bf16[544,256]{1,0:T(8,128)(2,1)S(1)}, bf16[544,256]{1,0:T(8,128)(2,1)S(1)}, u32[]{:S(2)}, u32[]{:S(2)}) collective-permute-start(bf16[544,256]{1,0:T(8,128)(2,1)S(1)} %constant_dynamic-update-slice_fusion.4.queries), channel_id=1, source_target_pairs={{0,4},{2,6},{4,0},{6,2},{8,12},{10,14},{12,8},{14,10},{16,20},{18,... | collective-permute-start | bytes 835592 | tf_op jit(solution)/shard_map/ppermute | solution.py:679
  52.7 7.9 %collective-permute-start.11 = (bf16[256,384]{1,0:T(8,128)(2,1)S(1)}, bf16[256,384]{1,0:T(8,128)(2,1)S(1)}, u32[]{:S(2)}, u32[]{:S(2)}) collective-permute-start(bf16[256,384]{1,0:T(8,128)(2,1)S(1)} %slice.6), channel_id=1, source_target_pairs={{0,8},{2,10},{4,12},{6,14},{8,16},{10,18},{12,20},{14,22},{16,24},... | collective-permute-start | bytes 589832 | tf_op jit(solution)/shard_map/ppermute | solution.py:679
  53.9 6.7 %collective-permute-start.12 = (bf16[256,384]{1,0:T(8,128)(2,1)S(1)}, bf16[256,384]{1,0:T(8,128)(2,1)S(1)}, u32[]{:S(2)}, u32[]{:S(2)}) collective-permute-start(bf16[256,384]{1,0:T(8,128)(2,1)S(1)} %slice.7), channel_id=1, source_target_pairs={{0,24},{2,26},{4,28},{6,30},{8,0},{10,2},{12,4},{14,6},{16,8},{18,... | collective-permute-start | bytes 589832 | tf_op jit(solution)/shard_map/ppermute | solution.py:679
  60.7 26.5 %copy-start = (bf16[768,1536]{1,0:T(8,128)(2,1)S(1)}, bf16[768,1536]{1,0:T(8,128)(2,1)}, u32[]{:S(2)}) copy-start(bf16[768,1536]{1,0:T(8,128)(2,1)} %weight.6) | copy-start | bytes 7077892
  60.7 2.0 %collective-permute-start.17 = (bf16[512,384]{1,0:T(8,128)(2,1)S(1)}, bf16[512,384]{1,0:T(8,128)(2,1)S(1)}, u32[]{:S(2)}, u32[]{:S(2)}) collective-permute-start(bf16[512,384]{1,0:T(8,128)(2,1)S(1)} %constant_dynamic-update-slice_fusion.8.refs_6_), channel_id=1, source_target_pairs={{0,2},{2,0},{4,6},{6,4},{8,10},{10,8},{12,14},{14,12},{16,18},{18,... | collective-permute-start | bytes 1179656 | tf_op jit(solution)/shard_map/ppermute | solution.py:679
  68.5 8.8 %collective-permute-start.18 = (bf16[544,256]{1,0:T(8,128)(2,1)S(1)}, bf16[544,256]{1,0:T(8,128)(2,1)S(1)}, u32[]{:S(2)}, u32[]{:S(2)}) collective-permute-start(bf16[544,256]{1,0:T(8,128)(2,1)S(1)} %get-tuple-element.83), channel_id=1, source_target_pairs={{0,4},{2,6},{4,0},{6,2},{8,12},{10,14},{12,8},{14,10},{16,20},{18,... | collective-permute-start | bytes 835592 | tf_op jit(solution)/shard_map/ppermute | solution.py:679
  69.9 26.1 %slice-start = ((s8[7077888]{0:T(1024)(128)(4,1)}), s8[4194304]{0:T(1024)(128)(4,1)S(1)}, s32[]{:S(2)}) async-start(s8[7077888]{0:T(1024)(128)(4,1)} %bitcast.4), calls=%async_computation | async-start | bytes 8388608
  69.9 26.1 %slice-start.1 = ((s8[7077888]{0:T(1024)(128)(4,1)}), s8[2883584]{0:T(1024)(128)(4,1)S(1)}, s32[]{:S(2)}) async-start(s8[7077888]{0:T(1024)(128)(4,1)} %bitcast.4), calls=%async_computation.1 | async-start | bytes 5767168
  77.8 5.8 %collective-permute-start.19 = (bf16[136,256]{1,0:T(8,128)(2,1)S(1)}, bf16[136,256]{1,0:T(8,128)(2,1)S(1)}, u32[]{:S(2)}, u32[]{:S(2)}) collective-permute-start(bf16[136,256]{1,0:T(8,128)(2,1)S(1)} %get-tuple-element.85), channel_id=1, source_target_pairs={{0,96},{2,98},{4,100},{6,102},{8,104},{10,106},{12,108},{14,110},{... | collective-permute-start | bytes 208904 | tf_op jit(solution)/shard_map/ppermute | solution.py:679
  81.0 5.9 %collective-permute-start.20 = (bf16[136,256]{1,0:T(8,128)(2,1)S(1)}, bf16[136,256]{1,0:T(8,128)(2,1)S(1)}, u32[]{:S(2)}, u32[]{:S(2)}) collective-permute-start(bf16[136,256]{1,0:T(8,128)(2,1)S(1)} %get-tuple-element.86), channel_id=1, source_target_pairs={{0,64},{2,66},{4,68},{6,70},{8,72},{10,74},{12,76},{14,78},{16,80}... | collective-permute-start | bytes 208904 | tf_op jit(solution)/shard_map/ppermute | solution.py:679
  81.0 6.3 %collective-permute-start.21 = (bf16[136,256]{1,0:T(8,128)(2,1)S(1)}, bf16[136,256]{1,0:T(8,128)(2,1)S(1)}, u32[]{:S(2)}, u32[]{:S(2)}) collective-permute-start(bf16[136,256]{1,0:T(8,128)(2,1)S(1)} %get-tuple-element.87), channel_id=1, source_target_pairs={{0,32},{2,34},{4,36},{6,38},{8,40},{10,42},{12,44},{14,46},{16,48}... | collective-permute-start | bytes 208904 | tf_op jit(solution)/shard_map/ppermute | solution.py:679
  88.5 7.4 %collective-permute-start.22 = (bf16[136,768]{1,0:T(8,128)(2,1)S(1)}, bf16[136,768]{1,0:T(8,128)(2,1)S(1)}, u32[]{:S(2)}, u32[]{:S(2)}) collective-permute-start(bf16[136,768]{1,0:T(8,128)(2,1)S(1)} %output.3), channel_id=1, source_target_pairs={{0,1},{1,0},{2,3},{3,2},{4,5},{5,4},{6,7},{7,6},{8,9},{9,8},{10,11... | collective-permute-start | bytes 626696 | tf_op jit(solution)/shard_map/ppermute | solution.py:675
  97.7 9.8 %collective-permute-start.24 = (bf16[272,512]{1,0:T(8,128)(2,1)S(1)}, bf16[272,512]{1,0:T(8,128)(2,1)S(1)}, u32[]{:S(2)}, u32[]{:S(2)}) collective-permute-start(bf16[272,512]{1,0:T(8,128)(2,1)S(1)} %get-tuple-element.91), channel_id=1, source_target_pairs={{0,1},{1,0},{2,3},{3,2},{4,5},{5,4},{6,7},{7,6},{8,9},{9,8},{10,11... | collective-permute-start | bytes 835592 | tf_op jit(solution)/shard_map/ppermute | solution.py:675
  101.2 6.3 %copy-start.1 = (bf16[256,1536]{1,0:T(8,128)(2,1)S(1)}, bf16[256,1536]{1,0:T(8,128)(2,1)}, u32[]{:S(2)}) copy-start(bf16[256,1536]{1,0:T(8,128)(2,1)} %grad.5) | copy-start | bytes 2359300
  102.9 8.5 %collective-permute-start.23 = (bf16[272,256]{1,0:T(8,128)(2,1)}, bf16[272,256]{1,0:T(8,128)(2,1)}, u32[]{:S(2)}, u32[]{:S(2)}) collective-permute-start(bf16[272,256]{1,0:T(8,128)(2,1)} %decode.2), channel_id=1, source_target_pairs={{0,1},{1,0},{2,3},{3,2},{4,5},{5,4},{6,7},{7,6},{8,9},{9,8},{10,11... | collective-permute-start | bytes 417800 | tf_op jit(solution)/shard_map/ppermute | solution.py:675
  109.5 8.4 %collective-permute-start.26 = (bf16[272,512]{1,0:T(8,128)(2,1)}, bf16[272,512]{1,0:T(8,128)(2,1)}, u32[]{:S(2)}, u32[]{:S(2)}) collective-permute-start(bf16[272,512]{1,0:T(8,128)(2,1)} %get-tuple-element.95.refs_0_), channel_id=1, source_target_pairs={{0,1},{1,0},{2,3},{3,2},{4,5},{5,4},{6,7},{7,6},{8,9},{9,8},{10,11... | collective-permute-start | bytes 835592 | tf_op jit(solution)/shard_map/ppermute | solution.py:675
  113.5 6.9 %collective-permute-start.25 = (bf16[272,256]{1,0:T(8,128)(2,1)}, bf16[272,256]{1,0:T(8,128)(2,1)}, u32[]{:S(2)}, u32[]{:S(2)}) collective-permute-start(bf16[272,256]{1,0:T(8,128)(2,1)} %get-tuple-element.94.refs_1_), channel_id=1, source_target_pairs={{0,1},{1,0},{2,3},{3,2},{4,5},{5,4},{6,7},{7,6},{8,9},{9,8},{10,11... | collective-permute-start | bytes 417800 | tf_op jit(solution)/shard_map/ppermute | solution.py:675

commit v12 on v11

--- a/solution.py
+++ b/solution.py
@@ -53,11 +53,12 @@
 
 
 def lanes(at, size):
-    return pl.ds(pl.multiple_of(at, size), size)
+    return pl.ds(at if isinstance(at, int) else pl.multiple_of(at, size), size)
 
 
 def tiles(count, body):
-    lax.fori_loop(0, count, lambda i, carry: (body(i), carry)[1], 0)
+    for i in range(count):
+        body(i)
 
 
 def gelu_tanh(x):
@@ -323,6 +324,42 @@
 LOG2E = 1.4426950408889634
 
 
+def key_columns(ref):
+    return jnp.concatenate([ref[:, :128], ref[:, 256:]], axis=1)
+
+
+def inverse_norms(ref):
+    lane = lax.broadcasted_iota(jnp.int32, (8, 256), 1)
+    ones = (lane < HEAD).astype(F32).astype(BF16)
+    key = key_columns(ref).astype(F32)
+    square = key * key
+    high = square.astype(BF16)
+    rest = (square - high.astype(F32)).astype(BF16)
+    total = dot_t(ones, high) + dot_t(ones, rest)
+    return lax.rsqrt(total * (1.0 / HEAD) + EPS)
+
+
+def norms_kernel(*refs):
+    pieces, out = refs[:-1], refs[-1]
+    at = 0
+    for ref in pieces:
+        out[:, at : at + ref.shape[0]] = inverse_norms(ref)
+        at += ref.shape[0]
+
+
+def norms(pieces):
+    keys = sum(piece.shape[0] for piece in pieces)
+    return pl.pallas_call(
+        norms_kernel,
+        in_specs=[VM] * len(pieces),
+        out_specs=VM,
+        out_shape=shape((8, keys), F32),
+        compiler_params=params(6),
+        cost_estimate=cost(10**6, 10**5),
+        name="norms",
+    )(*pieces)
+
+
 def attend_kernel(count, known, resumed, final, ids, scale, queries, *refs):
     pieces, refs = refs[:count], refs[count:]
     inverses, refs = refs[:known], refs[known:]
@@ -331,24 +368,12 @@
     sizes = [ref.shape[0] for ref in pieces]
     starts = [sum(sizes[:i]) for i in range(count)]
 
-    def keys(ref):
-        return jnp.concatenate([ref[:, :128], ref[:, 256:]], axis=1)
-
     total_known = sum(ref.shape[1] for ref in inverses)
     if total_known < sum(sizes):
         outs, inverse = refs[:-1], refs[-1]
-        lane = lax.broadcasted_iota(jnp.int32, (8, 256), 1)
-        ones = (lane < HEAD).astype(F32).astype(BF16)
         for at, size, ref in zip(starts, sizes, pieces):
-            if at < total_known:
-                continue
-            key = keys(ref).astype(F32)
-            square = key * key
-            high = square.astype(BF16)
-            rest = (square - high.astype(F32)).astype(BF16)
-            total = dot_t(ones, high) + dot_t(ones, rest)
-            at -= total_known
-            inverse[:, at : at + size] = lax.rsqrt(total * (1.0 / HEAD) + EPS)
+            if at >= total_known:
+                inverse[:, at - total_known : at - total_known + size] = inverse_norms(ref)
         inverses = (*inverses, inverse)
     else:
         outs = refs
@@ -371,7 +396,7 @@
     def unit(query, factor, group):
         scores, peak = [], None
         for at, size, ref in group:
-            part = dot_t(query, keys(ref)) * inverse_of(at, size)
+            part = dot_t(query, key_columns(ref)) * inverse_of(at, size)
             top = jnp.max(part, axis=1, keepdims=True)
             peak = top if peak is None else jnp.maximum(peak, top)
             scores.append(part)
@@ -568,15 +593,15 @@
         pre = own[:, source] + other[:, at].astype(F32)
         tanh = gelu_tanh(pre)
         result = inputs[:, source].astype(F32) + 0.5 * pre * (1.0 + tanh)
-        wide[0, pl.ds(0, OWN, 2), :] = result[:OWN]
-        wide[0, pl.ds(1, OWN, 2), :] = result[ROWS : ROWS + OWN]
-        decoded[:, target] = wide[0].astype(BF16)
+        wide[2 * i, pl.ds(0, OWN, 2), :] = result[:OWN]
+        wide[2 * i, pl.ds(1, OWN, 2), :] = result[ROWS : ROWS + OWN]
+        decoded[:, target] = wide[2 * i].astype(BF16)
         slant = 0.5 * (1.0 + tanh) + (0.5 * 0.7978845608028654) * pre * (1.0 - tanh * tanh) * (
             1.0 + (3 * 0.044715) * (pre * pre)
         )
-        wide[1] = grad[:, column].astype(F32)
-        even = wide[1, pl.ds(0, OWN, 2), :]
-        odd = wide[1, pl.ds(1, OWN, 2), :]
+        wide[2 * i + 1] = grad[:, column].astype(F32)
+        even = wide[2 * i + 1, pl.ds(0, OWN, 2), :]
+        odd = wide[2 * i + 1, pl.ds(1, OWN, 2), :]
         paired[:, at] = even + odd
         row = lax.broadcasted_iota(jnp.int32, (ROWS - OWN, 128), 0)
         before, after = sides(ids, near[:, column].astype(F32), far[:, column].astype(F32))
@@ -599,8 +624,8 @@
             shape((2 * ROWS, width), BF16),
             shape((OWN, width), F32),
         ],
-        scratch_shapes=[pltpu.VMEM((2, 2 * OWN, 128), F32)],
-        compiler_params=params(6),
+        scratch_shapes=[pltpu.VMEM((width // 64, 2 * OWN, 128), F32)],
+        compiler_params=params(8),
         cost_estimate=cost(100 * 30 * 1000 * other.size, 14 * other.size),
         name="slopes",
     )(ids, own, other, inputs, grad, near, far, *done)
@@ -723,12 +748,14 @@
     half = keyvals.shape[0] // 2
     far = [send(near[0][:half], dz=1), send(near[1][half:], dz=3)]
     across = [send(piece, dc=1) for piece in (keyvals, *near)]
-    *far, across, others = lax.optimization_barrier((*far, across, others))
+    pieces = [keyvals] + near + across
+    inverse = norms(pieces)
+    *far, inverse, others = lax.optimization_barrier((*far, inverse, others))
     far = jnp.concatenate(far, axis=0)
-    pieces = [keyvals] + near + across + [far, send(far, dc=1)]
-    other, inverse = attend(ids, logit_scale, others, pieces)
+    pieces += [far, send(far, dc=1)]
+    other, later = attend(ids, logit_scale, others, pieces, inverses=[inverse])
     other = send(other, dy=1)
-    own = attend(ids, logit_scale, queries, pieces, inverses=[inverse])[0]
+    own = attend(ids, logit_scale, queries, pieces, inverses=[inverse, later])[0]
     mixed = merge([own, other])
     heads = [mixed[0], send(mixed[1], dx=-1), send(mixed[3], dx=-2), send(mixed[2], dx=-3)]
 

time: 123 us -> 120 us (0.976)
  Pallas kernels: 42.7 us -> 39.5 us
    ppermute x6, waiting for transfers between devices: 14.1 us -> 15.6 us  [swap(): return lax.ppermute(value, 'head', [(0, 1), (1, 0)])]
where the time goes in v12:
time: 120 us
  starting transfers between devices  44 us (37%)
  Pallas kernels  39.5 us (33%)
  waiting for transfers between devices  35.5 us (30%)
    ppermute x20, starting transfers between devices, send(): return lax.ppermute(value, 'seq', moves(**step))  29.3 us
    ppermute x20, waiting for transfers between devices, send(): return lax.ppermute(value, 'seq', moves(**step))  19.8 us
    ppermute x6, waiting for transfers between devices, swap(): return lax.ppermute(value, 'head', [(0, 1), (1, 0)])  15.6 us
    ppermute x6, starting transfers between devices, swap(): return lax.ppermute(value, 'head', [(0, 1), (1, 0)])  14 us
    pallas_call x2, Pallas kernels, attend(): pl.pallas_call(functools.partial(attend_kernel, len(pieces), len(inverses...  9.55 us
    pallas_call x3, Pallas kernels, backward(): pl.pallas_call(functools.partial(backward_kernel, mine, [first for first,...  6.19 us
    pallas_call x2, Pallas kernels, slopes(): pl.pallas_call(functools.partial(slope_kernel, first), in_specs=[SM] + [V...  3.87 us
    pallas_call x1, Pallas kernels, encode(): pl.pallas_call(encode_kernel, in_specs=[SM] + [VM] * 5 + [HBM], out_specs...  3.57 us
  transfers between devices with their start and end apart: 27, of which 15 were waited for; matrix products, arithmetic and copies ran while one was open for 0% of the time, Pallas kernels for 19%

profile of v12, /device:TPU:0, one launch (start us, length us, event | category | flops | bytes accessed | tf_op | source)
XLA Modules:
  0.0 120.2 jit_solution(1563959876714514815)
XLA Ops:
  0.6 0.1 pad_add_fusion.ids
  0.7 1.4 %prepare.1 = (bf16[128,128]{1,0:T(8,128)(2,1)S(1)}, bf16[8,1664]{1,0:T(8,128)(2,1)S(1)}, bf16[8,1664]{1,0:T(8,128)(2,1)S(1)}) custom-call(s32[3]{0:T(128)S(1)} %pad_add_fusion.ids, s32[128,128]{1,0:T(8,128)} %bitcast.6, bf16[256,1536]{1,0:T(8,128)(2,1)} %grad.5), custom_call_target="tpu_custom_call" | custom-call | flops 100000 | bytes 100000 | tf_op jit(solution)/shard_map/prepare/pallas_call | solution.py:112
  2.2 0.1 collective-permute-start
  2.3 0.7 collective-permute-start.1
  2.9 3.3 %load.1 = (bf16[256,1536]{1,0:T(8,128)(2,1)S(1)}, bf16[256,1536]{1,0:T(8,128)(2,1)S(1)}, bf16[3,1536,768]{2,1,0:T(8,128)(2,1)S(1)}) custom-call(bf16[128,128]{1,0:T(8,128)(2,1)S(1)} %get-tuple-element.50.codes, bf16[256,1536]{1,0:T(8,128)(2,1)} %stems.1, bf16[3,1536,768]{2,1,0:T(8,128)(2,1)} %weights.1), custom_call_target="tpu_custom_call" | custom-call | flops 100000 | bytes 7077888 | tf_op jit(solution)/shard_map/load/pallas_call | solution.py:164
  6.2 0.0 collective-permute-done.1.far
  6.2 0.0 copy-start.3
  6.3 3.6 %encode.1 = (bf16[272,768]{1,0:T(8,128)(2,1)S(1)}, bf16[3,1536,768]{2,1,0:T(8,128)(2,1)S(1)}) custom-call(s32[3]{0:T(128)S(1)} %pad_add_fusion.ids, bf16[8,1664]{1,0:T(8,128)(2,1)S(1)} %collective-permute-done.near, bf16[8,1664]{1,0:T(8,128)(2,1)S(1)} %collective-permute-done.1.far, bf16[256,1536]{1,0:T(8,128)(2,1)S(1)} %get-tuple-element.51.rows, ...), custom_call_target="tpu_custom_call" | custom-call | flops 1811939328 | bytes 14155776 | tf_op jit(solution)/shard_map/encode/pallas_call | solution.py:219
  9.8 3.4 %collective-permute-start.2 = (bf16[272,768]{1,0:T(8,128)(2,1)S(1)}, bf16[272,768]{1,0:T(8,128)(2,1)S(1)}, u32[]{:S(2)}, u32[]{:S(2)}) collective-permute-start(bf16[272,768]{1,0:T(8,128)(2,1)S(1)} %get-tuple-element.54.mine.encoded), channel_id=1, source_target_pairs={{0,1},{1,0},{2,3},{3,2},{4,5},{5,4},{6,7},{7,6},{8,9},{9,8},{10,11... | collective-permute-start | bytes 1253384 | tf_op jit(solution)/shard_map/ppermute | solution.py:700
  13.2 8.6 %collective-permute-done.2.theirs = bf16[272,768]{1,0:T(8,128)(2,1)S(1)} collective-permute-done((bf16[272,768]{1,0:T(8,128)(2,1)S(1)}, bf16[272,768]{1,0:T(8,128)(2,1)S(1)}, u32[]{:S(2)}, u32[]{:S(2)}) %collective-permute-start.2) | collective-permute-done | bytes 417824 | tf_op jit(solution)/shard_map/ppermute | solution.py:700
  21.8 2.0 %project_keys.1 = (bf16[2,136,768]{2,1,0:T(8,128)(2,1)S(1)}, bf16[128,384]{1,0:T(8,128)(2,1)S(1)}, bf16[128,384]{1,0:T(8,128)(2,1)S(1)}, bf16[128,384]{1,0:T(8,128)(2,1)S(1)}, bf16[128,384]{1,0:T(8,128)(2,1)S(1)}) custom-call(s32[3]{0:T(128)S(1)} %pad_add_fusion.ids, bf16[272,768]{1,0:T(8,128)(2,1)S(1)} %get-tuple-element.54.mine.encoded, ...), custom_call_target="tpu_custom_call" | custom-call | flops 641728512 | bytes 7077888 | tf_op jit(solution)/shard_map/project_keys/pallas_call | solution.py:283
  23.9 0.0 copy-start.2
  23.9 5.7 %collective-permute-start.3 = (bf16[128,384]{1,0:T(8,128)(2,1)S(1)}, bf16[128,384]{1,0:T(8,128)(2,1)S(1)}, u32[]{:S(2)}, u32[]{:S(2)}) collective-permute-start(bf16[128,384]{1,0:T(8,128)(2,1)S(1)} %get-tuple-element.59), channel_id=1, source_target_pairs={{0,32},{2,34},{4,36},{6,38},{8,40},{10,42},{12,44},{14,46},{16,48}... | collective-permute-start | bytes 294920 | tf_op jit(solution)/shard_map/ppermute | solution.py:704
  29.6 1.6 %collective-permute-start.4 = (bf16[128,384]{1,0:T(8,128)(2,1)S(1)}, bf16[128,384]{1,0:T(8,128)(2,1)S(1)}, u32[]{:S(2)}, u32[]{:S(2)}) collective-permute-start(bf16[128,384]{1,0:T(8,128)(2,1)S(1)} %get-tuple-element.60), channel_id=1, source_target_pairs={{0,96},{2,98},{4,100},{6,102},{8,104},{10,106},{12,108},{14,110},{... | collective-permute-start | bytes 294920 | tf_op jit(solution)/shard_map/ppermute | solution.py:704
  31.2 2.0 %collective-permute-start.5 = (bf16[128,384]{1,0:T(8,128)(2,1)S(1)}, bf16[128,384]{1,0:T(8,128)(2,1)S(1)}, u32[]{:S(2)}, u32[]{:S(2)}) collective-permute-start(bf16[128,384]{1,0:T(8,128)(2,1)S(1)} %get-tuple-element.61), channel_id=1, source_target_pairs={{0,64},{2,66},{4,68},{6,70},{8,72},{10,74},{12,76},{14,78},{16,80}... | collective-permute-start | bytes 294920 | tf_op jit(solution)/shard_map/ppermute | solution.py:704
  33.2 1.6 %collective-permute-done.3 = bf16[128,384]{1,0:T(8,128)(2,1)S(1)} collective-permute-done((bf16[128,384]{1,0:T(8,128)(2,1)S(1)}, bf16[128,384]{1,0:T(8,128)(2,1)S(1)}, u32[]{:S(2)}, u32[]{:S(2)}) %collective-permute-start.3) | collective-permute-done | bytes 98336 | tf_op jit(solution)/shard_map/ppermute | solution.py:704
  34.7 2.6 %collective-permute-done.5 = bf16[128,384]{1,0:T(8,128)(2,1)S(1)} collective-permute-done((bf16[128,384]{1,0:T(8,128)(2,1)S(1)}, bf16[128,384]{1,0:T(8,128)(2,1)S(1)}, u32[]{:S(2)}, u32[]{:S(2)}) %collective-permute-start.5) | collective-permute-done | bytes 98336 | tf_op jit(solution)/shard_map/ppermute | solution.py:704
  37.4 2.2 %collective-permute-start.6 = (bf16[512,384]{1,0:T(8,128)(2,1)S(1)}, bf16[512,384]{1,0:T(8,128)(2,1)S(1)}, u32[]{:S(2)}, u32[]{:S(2)}) collective-permute-start(bf16[512,384]{1,0:T(8,128)(2,1)S(1)} %constant_dynamic-update-slice_fusion.refs_0_), channel_id=1, source_target_pairs={{0,8},{2,10},{4,12},{6,14},{8,16},{10,18},{12,20},{14,22},{16,24},... | collective-permute-start | bytes 1179656 | tf_op jit(solution)/shard_map/ppermute | solution.py:704
  39.6 2.2 %collective-permute-start.7 = (bf16[512,384]{1,0:T(8,128)(2,1)S(1)}, bf16[512,384]{1,0:T(8,128)(2,1)S(1)}, u32[]{:S(2)}, u32[]{:S(2)}) collective-permute-start(bf16[512,384]{1,0:T(8,128)(2,1)S(1)} %constant_dynamic-update-slice_fusion.refs_0_), channel_id=1, source_target_pairs={{0,24},{2,26},{4,28},{6,30},{8,0},{10,2},{12,4},{14,6},{16,8},{18,... | collective-permute-start | bytes 1179656 | tf_op jit(solution)/shard_map/ppermute | solution.py:704
  41.8 1.3 %project_queries.1 = (bf16[136,256]{1,0:T(8,128)(2,1)S(1)}, bf16[136,256]{1,0:T(8,128)(2,1)S(1)}, bf16[136,256]{1,0:T(8,128)(2,1)S(1)}, bf16[136,256]{1,0:T(8,128)(2,1)S(1)}) custom-call(s32[3]{0:T(128)S(1)} %pad_add_fusion.ids, bf16[2,136,768]{2,1,0:T(8,128)(2,1)S(1)} %get-tuple-element.56.normed, bf16[3,1536,768]{2,1,0:T(8,128)(2,1)S(1)} %get-tuple-element.55.weight), custom_call_target="tpu_custom_call" | custom-call | flops 320864256 | bytes 3538944 | tf_op jit(solution)/shard_map/project_queries/pallas_call | solution.py:311
  43.0 1.9 %collective-permute-start.10 = (bf16[136,256]{1,0:T(8,128)(2,1)S(1)}, bf16[136,256]{1,0:T(8,128)(2,1)S(1)}, u32[]{:S(2)}, u32[]{:S(2)}) collective-permute-start(bf16[136,256]{1,0:T(8,128)(2,1)S(1)} %get-tuple-element.68), channel_id=1, source_target_pairs={{0,64},{2,66},{4,68},{6,70},{8,72},{10,74},{12,76},{14,78},{16,80}... | collective-permute-start | bytes 208904 | tf_op jit(solution)/shard_map/ppermute | solution.py:704
  44.9 0.7 collective-permute-start.8
  45.6 2.6 %collective-permute-start.9 = (bf16[136,256]{1,0:T(8,128)(2,1)S(1)}, bf16[136,256]{1,0:T(8,128)(2,1)S(1)}, u32[]{:S(2)}, u32[]{:S(2)}) collective-permute-start(bf16[136,256]{1,0:T(8,128)(2,1)S(1)} %get-tuple-element.67), channel_id=1, source_target_pairs={{0,96},{2,98},{4,100},{6,102},{8,104},{10,106},{12,108},{14,110},{... | collective-permute-start | bytes 208904 | tf_op jit(solution)/shard_map/ppermute | solution.py:704
  48.2 0.7 collective-permute-done.10
  48.9 1.5 %collective-permute-done.8 = bf16[136,256]{1,0:T(8,128)(2,1)S(1)} collective-permute-done((bf16[136,256]{1,0:T(8,128)(2,1)S(1)}, bf16[136,256]{1,0:T(8,128)(2,1)S(1)}, u32[]{:S(2)}, u32[]{:S(2)}) %collective-permute-start.8) | collective-permute-done | bytes 69664 | tf_op jit(solution)/shard_map/ppermute | solution.py:704
  50.5 0.1 collective-permute-start.12
  50.6 0.5 collective-permute-start.13
  51.1 0.8 collective-permute-start.16
  52.0 1.2 %collective-permute-start.14 = (bf16[256,384]{1,0:T(8,128)(2,1)S(1)}, bf16[256,384]{1,0:T(8,128)(2,1)S(1)}, u32[]{:S(2)}, u32[]{:S(2)}) collective-permute-start(bf16[256,384]{1,0:T(8,128)(2,1)S(1)} %slice.6), channel_id=1, source_target_pairs={{0,8},{2,10},{4,12},{6,14},{8,16},{10,18},{12,20},{14,22},{16,24},... | collective-permute-start | bytes 589832 | tf_op jit(solution)/shard_map/ppermute | solution.py:704
  53.2 2.1 %collective-permute-start.15 = (bf16[256,384]{1,0:T(8,128)(2,1)S(1)}, bf16[256,384]{1,0:T(8,128)(2,1)S(1)}, u32[]{:S(2)}, u32[]{:S(2)}) collective-permute-start(bf16[256,384]{1,0:T(8,128)(2,1)S(1)} %slice.7), channel_id=1, source_target_pairs={{0,24},{2,26},{4,28},{6,30},{8,0},{10,2},{12,4},{14,6},{16,8},{18,... | collective-permute-start | bytes 589832 | tf_op jit(solution)/shard_map/ppermute | solution.py:704
  55.3 0.9 norms.1.refs_8_
  56.2 3.6 %collective-permute-done.14 = bf16[256,384]{1,0:T(8,128)(2,1)S(1)} collective-permute-done((bf16[256,384]{1,0:T(8,128)(2,1)S(1)}, bf16[256,384]{1,0:T(8,128)(2,1)S(1)}, u32[]{:S(2)}, u32[]{:S(2)}) %collective-permute-start.14) | collective-permute-done | bytes 196640 | tf_op jit(solution)/shard_map/ppermute | solution.py:704
  59.9 0.0 copy-start
  59.9 0.3 collective-permute-start.17
  60.2 1.7 %collective-permute-done.17.refs_7_ = bf16[512,384]{1,0:T(8,128)(2,1)S(1)} collective-permute-done((bf16[512,384]{1,0:T(8,128)(2,1)S(1)}, bf16[512,384]{1,0:T(8,128)(2,1)S(1)}, u32[]{:S(2)}, u32[]{:S(2)}) %collective-permute-start.17) | collective-permute-done | bytes 393248 | tf_op jit(solution)/shard_map/ppermute | solution.py:704
  61.9 4.9 %attend.2 = (bf16[544,256]{1,0:T(8,128)(2,1)S(1)}, f32[8,1024]{1,0:T(8,128)S(1)}) custom-call(s32[3]{0:T(128)S(1)} %pad_add_fusion.ids, f32[4]{0:T(128)S(1)} %copy-done.2, bf16[544,256]{1,0:T(8,128)(2,1)S(1)} %collective-permute-done.16.queries, bf16[512,384]{1,0:T(8,128)(2,1)S(1)} %constant_dynamic-update-slice_fusion.refs_0_, ...), custom_call_target="tpu_custom_call" | custom-call | flops 2281701376 | bytes 4456448 | tf_op jit(solution)/shard_map/attend/pallas_call | solution.py:456
  66.9 1.4 %collective-permute-start.18 = (bf16[544,256]{1,0:T(8,128)(2,1)S(1)}, bf16[544,256]{1,0:T(8,128)(2,1)S(1)}, u32[]{:S(2)}, u32[]{:S(2)}) collective-permute-start(bf16[544,256]{1,0:T(8,128)(2,1)S(1)} %get-tuple-element.79), channel_id=1, source_target_pairs={{0,4},{2,6},{4,0},{6,2},{8,12},{10,14},{12,8},{14,10},{16,20},{18,... | collective-permute-start | bytes 835592 | tf_op jit(solution)/shard_map/ppermute | solution.py:704
  68.2 4.6 %attend.3.a0 = bf16[544,256]{1,0:T(8,128)(2,1)S(1)} custom-call(s32[3]{0:T(128)S(1)} %pad_add_fusion.ids, f32[4]{0:T(128)S(1)} %copy-done.2, bf16[544,256]{1,0:T(8,128)(2,1)S(1)} %constant_dynamic-update-slice_fusion.4.queries, bf16[512,384]{1,0:T(8,128)(2,1)S(1)} %constant_dynamic-update-slice_fusion.refs_0_, ...), custom_call_target="tpu_custom_call" | custom-call | flops 2281701376 | bytes 4456448 | tf_op jit(solution)/shard_map/attend/pallas_call | solution.py:456
  72.9 2.8 %collective-permute-done.18.a1 = bf16[544,256]{1,0:T(8,128)(2,1)S(1)} collective-permute-done((bf16[544,256]{1,0:T(8,128)(2,1)S(1)}, bf16[544,256]{1,0:T(8,128)(2,1)S(1)}, u32[]{:S(2)}, u32[]{:S(2)}) %collective-permute-start.18) | collective-permute-done | bytes 278560 | tf_op jit(solution)/shard_map/ppermute | solution.py:704
  75.6 0.5 merge.1
  76.2 3.2 %collective-permute-start.19 = (bf16[136,256]{1,0:T(8,128)(2,1)S(1)}, bf16[136,256]{1,0:T(8,128)(2,1)S(1)}, u32[]{:S(2)}, u32[]{:S(2)}) collective-permute-start(bf16[136,256]{1,0:T(8,128)(2,1)S(1)} %get-tuple-element.81), channel_id=1, source_target_pairs={{0,96},{2,98},{4,100},{6,102},{8,104},{10,106},{12,108},{14,110},{... | collective-permute-start | bytes 208904 | tf_op jit(solution)/shard_map/ppermute | solution.py:704
  79.4 0.9 collective-permute-start.21
  80.3 1.7 %collective-permute-done.19.a1 = bf16[136,256]{1,0:T(8,128)(2,1)S(1)} collective-permute-done((bf16[136,256]{1,0:T(8,128)(2,1)S(1)}, bf16[136,256]{1,0:T(8,128)(2,1)S(1)}, u32[]{:S(2)}, u32[]{:S(2)}) %collective-permute-start.19) | collective-permute-done | bytes 69664 | tf_op jit(solution)/shard_map/ppermute | solution.py:704
  82.0 3.3 %collective-permute-done.20.a2 = bf16[136,256]{1,0:T(8,128)(2,1)S(1)} collective-permute-done((bf16[136,256]{1,0:T(8,128)(2,1)S(1)}, bf16[136,256]{1,0:T(8,128)(2,1)S(1)}, u32[]{:S(2)}, u32[]{:S(2)}) %collective-permute-start.20) | collective-permute-done | bytes 69664 | tf_op jit(solution)/shard_map/ppermute | solution.py:704
  85.3 0.4 collective-permute-done.21.a3
  85.6 0.9 output.3
  86.6 3.3 %collective-permute-start.22 = (bf16[136,768]{1,0:T(8,128)(2,1)S(1)}, bf16[136,768]{1,0:T(8,128)(2,1)S(1)}, u32[]{:S(2)}, u32[]{:S(2)}) collective-permute-start(bf16[136,768]{1,0:T(8,128)(2,1)S(1)} %output.3), channel_id=1, source_target_pairs={{0,1},{1,0},{2,3},{3,2},{4,5},{5,4},{6,7},{7,6},{8,9},{9,8},{10,11... | collective-permute-start | bytes 626696 | tf_op jit(solution)/shard_map/ppermute | solution.py:700
  89.9 0.9 output.2.own
  90.9 3.1 %collective-permute-done.22.other = bf16[136,768]{1,0:T(8,128)(2,1)S(1)} collective-permute-done((bf16[136,768]{1,0:T(8,128)(2,1)S(1)}, bf16[136,768]{1,0:T(8,128)(2,1)S(1)}, u32[]{:S(2)}, u32[]{:S(2)}) %collective-permute-start.22) | collective-permute-done | bytes 208928 | tf_op jit(solution)/shard_map/ppermute | solution.py:700
  94.0 1.4 %decode_first.1 = (bf16[272,768]{1,0:T(8,128)(2,1)S(1)}, bf16[272,512]{1,0:T(8,128)(2,1)S(1)}) custom-call(s32[3]{0:T(128)S(1)} %pad_add_fusion.ids, f32[136,768]{1,0:T(8,128)S(1)} %output.2.own, bf16[136,768]{1,0:T(8,128)(2,1)S(1)} %collective-permute-done.22.other, bf16[272,768]{1,0:T(8,128)(2,1)S(1)} %get-tuple-element.54.mine.encoded, ...), custom_call_target="tpu_custom_call" | custom-call | flops 1000000 | bytes 10000 | tf_op jit(solution)/shard_map/decode_first/pallas_call | solution.py:551
  95.4 3.5 %collective-permute-start.24 = (bf16[272,512]{1,0:T(8,128)(2,1)S(1)}, bf16[272,512]{1,0:T(8,128)(2,1)S(1)}, u32[]{:S(2)}, u32[]{:S(2)}) collective-permute-start(bf16[272,512]{1,0:T(8,128)(2,1)S(1)} %get-tuple-element.87), channel_id=1, source_target_pairs={{0,1},{1,0},{2,3},{3,2},{4,5},{5,4},{6,7},{7,6},{8,9},{9,8},{10,11... | collective-permute-start | bytes 835592 | tf_op jit(solution)/shard_map/ppermute | solution.py:700
  99.0 1.7 %decode.2 = bf16[272,256]{1,0:T(8,128)(2,1)} custom-call(s32[3]{0:T(128)S(1)} %pad_add_fusion.ids, bf16[272,768]{1,0:T(8,128)(2,1)S(1)} %get-tuple-element.85.inputs, bf16[3,768,1536]{2,1,0:T(8,128)(2,1)S(1)} %bitcast.5), custom_call_target="tpu_custom_call" | custom-call | flops 1000000 | bytes 10000 | tf_op jit(solution)/shard_map/decode/pallas_call | solution.py:569
  100.7 0.3 collective-permute-start.23
  101.0 1.7 %decode.3.own = f32[272,768]{1,0:T(8,128)S(1)} custom-call(s32[3]{0:T(128)S(1)} %pad_add_fusion.ids, bf16[272,768]{1,0:T(8,128)(2,1)S(1)} %get-tuple-element.85.inputs, bf16[3,768,1536]{2,1,0:T(8,128)(2,1)S(1)} %bitcast.5), custom_call_target="tpu_custom_call" | custom-call | flops 1000000 | bytes 10000 | tf_op jit(solution)/shard_map/decode/pallas_call | solution.py:569
  102.7 2.6 %collective-permute-done.24.other = bf16[272,512]{1,0:T(8,128)(2,1)S(1)} collective-permute-done((bf16[272,512]{1,0:T(8,128)(2,1)S(1)}, bf16[272,512]{1,0:T(8,128)(2,1)S(1)}, u32[]{:S(2)}, u32[]{:S(2)}) %collective-permute-start.24) | collective-permute-done | bytes 278560 | tf_op jit(solution)/shard_map/ppermute | solution.py:700
  105.3 1.9 %slopes.2 = (bf16[256,512]{1,0:T(8,128)(2,1)S(1)}, bf16[272,512]{1,0:T(8,128)(2,1)}, f32[128,512]{1,0:T(8,128)S(1)}) custom-call(s32[3]{0:T(128)S(1)} %pad_add_fusion.ids, f32[272,768]{1,0:T(8,128)S(1)} %decode.3.own, bf16[272,512]{1,0:T(8,128)(2,1)S(1)} %collective-permute-done.24.other, bf16[272,768]{1,0:T(8,128)(2,1)S(1)} %get-tuple-element.85.inputs, ...), custom_call_target="tpu_custom_call" | custom-call | flops 417792000000 | bytes 1949696 | tf_op jit(solution)/shard_map/slopes/pallas_call | solution.py:618
  107.2 2.0 %collective-permute-start.26 = (bf16[272,512]{1,0:T(8,128)(2,1)}, bf16[272,512]{1,0:T(8,128)(2,1)}, u32[]{:S(2)}, u32[]{:S(2)}) collective-permute-start(bf16[272,512]{1,0:T(8,128)(2,1)} %get-tuple-element.91.refs_0_), channel_id=1, source_target_pairs={{0,1},{1,0},{2,3},{3,2},{4,5},{5,4},{6,7},{7,6},{8,9},{9,8},{10,11... | collective-permute-start | bytes 835592 | tf_op jit(solution)/shard_map/ppermute | solution.py:700
  109.2 2.0 %slopes.3 = (bf16[256,768]{1,0:T(8,128)(2,1)}, bf16[272,256]{1,0:T(8,128)(2,1)}, f32[128,256]{1,0:T(8,128)S(1)}) custom-call(s32[3]{0:T(128)S(1)} %pad_add_fusion.ids, f32[272,768]{1,0:T(8,128)S(1)} %decode.3.own, bf16[272,256]{1,0:T(8,128)(2,1)} %collective-permute-done.23.other, bf16[272,768]{1,0:T(8,128)(2,1)S(1)} %get-tuple-element.85.inputs, ...), custom_call_target="tpu_custom_call" | custom-call | flops 208896000000 | bytes 974848 | tf_op jit(solution)/shard_map/slopes/pallas_call | solution.py:618
  111.1 1.5 %collective-permute-start.25 = (bf16[272,256]{1,0:T(8,128)(2,1)}, bf16[272,256]{1,0:T(8,128)(2,1)}, u32[]{:S(2)}, u32[]{:S(2)}) collective-permute-start(bf16[272,256]{1,0:T(8,128)(2,1)} %get-tuple-element.90.refs_1_), channel_id=1, source_target_pairs={{0,1},{1,0},{2,3},{3,2},{4,5},{5,4},{6,7},{7,6},{8,9},{9,8},{10,11... | collective-permute-start | bytes 417800 | tf_op jit(solution)/shard_map/ppermute | solution.py:700
  112.7 2.2 %backward.3.refs_1_ = f32[128,768]{1,0:T(8,128)S(1)} custom-call(s32[3]{0:T(128)S(1)} %pad_add_fusion.ids, bf16[272,512]{1,0:T(8,128)(2,1)} %get-tuple-element.91.refs_0_, bf16[272,256]{1,0:T(8,128)(2,1)} %get-tuple-element.90.refs_1_, f32[128,512]{1,0:T(8,128)S(1)} %get-tuple-element.92.refs_2_, f32[128,256]{1,0:T(8,128)S(1)} %get-tuple-element.93.refs_3_, ...), custom_call_target="tpu_custom_call" | custom-call | flops 96259276800 | bytes 1253376 | tf_op jit(solution)/shard_map/backward/pallas_call | solution.py:676
  114.9 0.7 collective-permute-done.26.refs_0_
  115.5 1.9 %backward.4.refs_1_ = f32[128,768]{1,0:T(8,128)S(1)} custom-call(s32[3]{0:T(128)S(1)} %pad_add_fusion.ids, bf16[272,512]{1,0:T(8,128)(2,1)} %collective-permute-done.26.refs_0_, f32[128,768]{1,0:T(8,128)S(1)} %backward.3.refs_1_, bf16[3,768,1536]{2,1,0:T(8,128)(2,1)S(1)} %bitcast.5), custom_call_target="tpu_custom_call" | custom-call | flops 64172851200 | bytes 835584 | tf_op jit(solution)/shard_map/backward/pallas_call | solution.py:676
  117.4 0.6 collective-permute-done.25.refs_0_
  118.0 2.1 %backward.5 = bf16[128,768]{1,0:T(8,128)(2,1)} custom-call(s32[3]{0:T(128)S(1)} %pad_add_fusion.ids, bf16[272,256]{1,0:T(8,128)(2,1)} %collective-permute-done.25.refs_0_, f32[128,768]{1,0:T(8,128)S(1)} %backward.4.refs_1_, bf16[3,768,1536]{2,1,0:T(8,128)(2,1)S(1)} %bitcast.5), custom_call_target="tpu_custom_call" | custom-call | flops 32086425600 | bytes 417792 | tf_op jit(solution)/shard_map/backward/pallas_call | solution.py:676
  (36 shorter events, 0.2 us)
Async XLA Ops:
  2.2 4.1 %collective-permute-start = (bf16[8,1664]{1,0:T(8,128)(2,1)S(1)}, bf16[8,1664]{1,0:T(8,128)(2,1)S(1)}, u32[]{:S(2)}, u32[]{:S(2)}) collective-permute-start(bf16[8,1664]{1,0:T(8,128)(2,1)S(1)} %get-tuple-element.48), channel_id=1, source_target_pairs={{0,2},{2,0},{4,6},{6,4},{8,10},{10,8},{12,14},{14,12},{16,18},{18,... | collective-permute-start | bytes 79880 | tf_op jit(solution)/shard_map/ppermute | solution.py:704
  2.3 4.0 %collective-permute-start.1 = (bf16[8,1664]{1,0:T(8,128)(2,1)S(1)}, bf16[8,1664]{1,0:T(8,128)(2,1)S(1)}, u32[]{:S(2)}, u32[]{:S(2)}) collective-permute-start(bf16[8,1664]{1,0:T(8,128)(2,1)S(1)} %get-tuple-element.49), channel_id=1, source_target_pairs={{2,4},{6,8},{10,12},{14,16},{18,20},{22,24},{26,28},{30,32},{34,36... | collective-permute-start | bytes 79880 | tf_op jit(solution)/shard_map/ppermute | solution.py:726
  6.2 6.9 %copy-start.3 = (f32[1536]{0:T(1024)S(1)}, f32[1536]{0:T(1024)}, u32[]{:S(2)}) copy-start(f32[1536]{0:T(1024)} %param.12) | copy-start | bytes 18436
  9.8 12.0 %collective-permute-start.2 = (bf16[272,768]{1,0:T(8,128)(2,1)S(1)}, bf16[272,768]{1,0:T(8,128)(2,1)S(1)}, u32[]{:S(2)}, u32[]{:S(2)}) collective-permute-start(bf16[272,768]{1,0:T(8,128)(2,1)S(1)} %get-tuple-element.54.mine.encoded), channel_id=1, source_target_pairs={{0,1},{1,0},{2,3},{3,2},{4,5},{5,4},{6,7},{7,6},{8,9},{9,8},{10,11... | collective-permute-start | bytes 1253384 | tf_op jit(solution)/shard_map/ppermute | solution.py:700
  23.9 38.0 %copy-start.2 = (f32[4]{0:T(128)S(1)}, f32[4]{0:T(128)}, u32[]{:S(2)}) copy-start(f32[4]{0:T(128)} %scale.3) | copy-start | bytes 52
  23.9 10.8 %collective-permute-start.3 = (bf16[128,384]{1,0:T(8,128)(2,1)S(1)}, bf16[128,384]{1,0:T(8,128)(2,1)S(1)}, u32[]{:S(2)}, u32[]{:S(2)}) collective-permute-start(bf16[128,384]{1,0:T(8,128)(2,1)S(1)} %get-tuple-element.59), channel_id=1, source_target_pairs={{0,32},{2,34},{4,36},{6,38},{8,40},{10,42},{12,44},{14,46},{16,48}... | collective-permute-start | bytes 294920 | tf_op jit(solution)/shard_map/ppermute | solution.py:704
  29.6 5.1 %collective-permute-start.4 = (bf16[128,384]{1,0:T(8,128)(2,1)S(1)}, bf16[128,384]{1,0:T(8,128)(2,1)S(1)}, u32[]{:S(2)}, u32[]{:S(2)}) collective-permute-start(bf16[128,384]{1,0:T(8,128)(2,1)S(1)} %get-tuple-element.60), channel_id=1, source_target_pairs={{0,96},{2,98},{4,100},{6,102},{8,104},{10,106},{12,108},{14,110},{... | collective-permute-start | bytes 294920 | tf_op jit(solution)/shard_map/ppermute | solution.py:704
  31.2 6.1 %collective-permute-start.5 = (bf16[128,384]{1,0:T(8,128)(2,1)S(1)}, bf16[128,384]{1,0:T(8,128)(2,1)S(1)}, u32[]{:S(2)}, u32[]{:S(2)}) collective-permute-start(bf16[128,384]{1,0:T(8,128)(2,1)S(1)} %get-tuple-element.61), channel_id=1, source_target_pairs={{0,64},{2,66},{4,68},{6,70},{8,72},{10,74},{12,76},{14,78},{16,80}... | collective-permute-start | bytes 294920 | tf_op jit(solution)/shard_map/ppermute | solution.py:704
  37.4 13.1 %collective-permute-start.6 = (bf16[512,384]{1,0:T(8,128)(2,1)S(1)}, bf16[512,384]{1,0:T(8,128)(2,1)S(1)}, u32[]{:S(2)}, u32[]{:S(2)}) collective-permute-start(bf16[512,384]{1,0:T(8,128)(2,1)S(1)} %constant_dynamic-update-slice_fusion.refs_0_), channel_id=1, source_target_pairs={{0,8},{2,10},{4,12},{6,14},{8,16},{10,18},{12,20},{14,22},{16,24},... | collective-permute-start | bytes 1179656 | tf_op jit(solution)/shard_map/ppermute | solution.py:704
  39.6 10.9 %collective-permute-start.7 = (bf16[512,384]{1,0:T(8,128)(2,1)S(1)}, bf16[512,384]{1,0:T(8,128)(2,1)S(1)}, u32[]{:S(2)}, u32[]{:S(2)}) collective-permute-start(bf16[512,384]{1,0:T(8,128)(2,1)S(1)} %constant_dynamic-update-slice_fusion.refs_0_), channel_id=1, source_target_pairs={{0,24},{2,26},{4,28},{6,30},{8,0},{10,2},{12,4},{14,6},{16,8},{18,... | collective-permute-start | bytes 1179656 | tf_op jit(solution)/shard_map/ppermute | solution.py:704
  43.0 5.9 %collective-permute-start.10 = (bf16[136,256]{1,0:T(8,128)(2,1)S(1)}, bf16[136,256]{1,0:T(8,128)(2,1)S(1)}, u32[]{:S(2)}, u32[]{:S(2)}) collective-permute-start(bf16[136,256]{1,0:T(8,128)(2,1)S(1)} %get-tuple-element.68), channel_id=1, source_target_pairs={{0,64},{2,66},{4,68},{6,70},{8,72},{10,74},{12,76},{14,78},{16,80}... | collective-permute-start | bytes 208904 | tf_op jit(solution)/shard_map/ppermute | solution.py:704
  44.9 5.5 %collective-permute-start.8 = (bf16[136,256]{1,0:T(8,128)(2,1)S(1)}, bf16[136,256]{1,0:T(8,128)(2,1)S(1)}, u32[]{:S(2)}, u32[]{:S(2)}) collective-permute-start(bf16[136,256]{1,0:T(8,128)(2,1)S(1)} %get-tuple-element.66), channel_id=1, source_target_pairs={{0,32},{2,34},{4,36},{6,38},{8,40},{10,42},{12,44},{14,46},{16,48}... | collective-permute-start | bytes 208904 | tf_op jit(solution)/shard_map/ppermute | solution.py:704
  45.6 4.8 %collective-permute-start.9 = (bf16[136,256]{1,0:T(8,128)(2,1)S(1)}, bf16[136,256]{1,0:T(8,128)(2,1)S(1)}, u32[]{:S(2)}, u32[]{:S(2)}) collective-permute-start(bf16[136,256]{1,0:T(8,128)(2,1)S(1)} %get-tuple-element.67), channel_id=1, source_target_pairs={{0,96},{2,98},{4,100},{6,102},{8,104},{10,106},{12,108},{14,110},{... | collective-permute-start | bytes 208904 | tf_op jit(solution)/shard_map/ppermute | solution.py:704
  48.9 4.2 %collective-permute-start.11 = (bf16[512,384]{1,0:T(8,128)(2,1)S(1)}, bf16[512,384]{1,0:T(8,128)(2,1)S(1)}, u32[]{:S(2)}, u32[]{:S(2)}) collective-permute-start(bf16[512,384]{1,0:T(8,128)(2,1)S(1)} %constant_dynamic-update-slice_fusion.refs_0_), channel_id=1, source_target_pairs={{0,2},{2,0},{4,6},{6,4},{8,10},{10,8},{12,14},{14,12},{16,18},{18,... | collective-permute-start | bytes 1179656 | tf_op jit(solution)/shard_map/ppermute | solution.py:704
  50.5 4.8 %collective-permute-start.12 = (bf16[512,384]{1,0:T(8,128)(2,1)S(1)}, bf16[512,384]{1,0:T(8,128)(2,1)S(1)}, u32[]{:S(2)}, u32[]{:S(2)}) collective-permute-start(bf16[512,384]{1,0:T(8,128)(2,1)S(1)} %collective-permute-done.6.refs_1_), channel_id=1, source_target_pairs={{0,2},{2,0},{4,6},{6,4},{8,10},{10,8},{12,14},{14,12},{16,18},{18,... | collective-permute-start | bytes 1179656 | tf_op jit(solution)/shard_map/ppermute | solution.py:704
  50.6 4.7 %collective-permute-start.13 = (bf16[512,384]{1,0:T(8,128)(2,1)S(1)}, bf16[512,384]{1,0:T(8,128)(2,1)S(1)}, u32[]{:S(2)}, u32[]{:S(2)}) collective-permute-start(bf16[512,384]{1,0:T(8,128)(2,1)S(1)} %collective-permute-done.7.refs_2_), channel_id=1, source_target_pairs={{0,2},{2,0},{4,6},{6,4},{8,10},{10,8},{12,14},{14,12},{16,18},{18,... | collective-permute-start | bytes 1179656 | tf_op jit(solution)/shard_map/ppermute | solution.py:704
  51.1 8.8 %collective-permute-start.16 = (bf16[544,256]{1,0:T(8,128)(2,1)S(1)}, bf16[544,256]{1,0:T(8,128)(2,1)S(1)}, u32[]{:S(2)}, u32[]{:S(2)}) collective-permute-start(bf16[544,256]{1,0:T(8,128)(2,1)S(1)} %constant_dynamic-update-slice_fusion.4.queries), channel_id=1, source_target_pairs={{0,4},{2,6},{4,0},{6,2},{8,12},{10,14},{12,8},{14,10},{16,20},{18,... | collective-permute-start | bytes 835592 | tf_op jit(solution)/shard_map/ppermute | solution.py:704
  52.0 7.9 %collective-permute-start.14 = (bf16[256,384]{1,0:T(8,128)(2,1)S(1)}, bf16[256,384]{1,0:T(8,128)(2,1)S(1)}, u32[]{:S(2)}, u32[]{:S(2)}) collective-permute-start(bf16[256,384]{1,0:T(8,128)(2,1)S(1)} %slice.6), channel_id=1, source_target_pairs={{0,8},{2,10},{4,12},{6,14},{8,16},{10,18},{12,20},{14,22},{16,24},... | collective-permute-start | bytes 589832 | tf_op jit(solution)/shard_map/ppermute | solution.py:704
  53.2 6.7 %collective-permute-start.15 = (bf16[256,384]{1,0:T(8,128)(2,1)S(1)}, bf16[256,384]{1,0:T(8,128)(2,1)S(1)}, u32[]{:S(2)}, u32[]{:S(2)}) collective-permute-start(bf16[256,384]{1,0:T(8,128)(2,1)S(1)} %slice.7), channel_id=1, source_target_pairs={{0,24},{2,26},{4,28},{6,30},{8,0},{10,2},{12,4},{14,6},{16,8},{18,... | collective-permute-start | bytes 589832 | tf_op jit(solution)/shard_map/ppermute | solution.py:704
  59.9 25.7 %copy-start = (bf16[768,1536]{1,0:T(8,128)(2,1)S(1)}, bf16[768,1536]{1,0:T(8,128)(2,1)}, u32[]{:S(2)}) copy-start(bf16[768,1536]{1,0:T(8,128)(2,1)} %weight.6) | copy-start | bytes 7077892
  59.9 2.0 %collective-permute-start.17 = (bf16[512,384]{1,0:T(8,128)(2,1)S(1)}, bf16[512,384]{1,0:T(8,128)(2,1)S(1)}, u32[]{:S(2)}, u32[]{:S(2)}) collective-permute-start(bf16[512,384]{1,0:T(8,128)(2,1)S(1)} %constant_dynamic-update-slice_fusion.8.refs_6_), channel_id=1, source_target_pairs={{0,2},{2,0},{4,6},{6,4},{8,10},{10,8},{12,14},{14,12},{16,18},{18,... | collective-permute-start | bytes 1179656 | tf_op jit(solution)/shard_map/ppermute | solution.py:704
  66.9 8.8 %collective-permute-start.18 = (bf16[544,256]{1,0:T(8,128)(2,1)S(1)}, bf16[544,256]{1,0:T(8,128)(2,1)S(1)}, u32[]{:S(2)}, u32[]{:S(2)}) collective-permute-start(bf16[544,256]{1,0:T(8,128)(2,1)S(1)} %get-tuple-element.79), channel_id=1, source_target_pairs={{0,4},{2,6},{4,0},{6,2},{8,12},{10,14},{12,8},{14,10},{16,20},{18,... | collective-permute-start | bytes 835592 | tf_op jit(solution)/shard_map/ppermute | solution.py:704
  68.2 25.7 %slice-start = ((s8[7077888]{0:T(1024)(128)(4,1)}), s8[4194304]{0:T(1024)(128)(4,1)S(1)}, s32[]{:S(2)}) async-start(s8[7077888]{0:T(1024)(128)(4,1)} %bitcast.4), calls=%async_computation | async-start | bytes 8388608
  68.2 25.7 %slice-start.1 = ((s8[7077888]{0:T(1024)(128)(4,1)}), s8[2883584]{0:T(1024)(128)(4,1)S(1)}, s32[]{:S(2)}) async-start(s8[7077888]{0:T(1024)(128)(4,1)} %bitcast.4), calls=%async_computation.1 | async-start | bytes 5767168
  76.2 5.8 %collective-permute-start.19 = (bf16[136,256]{1,0:T(8,128)(2,1)S(1)}, bf16[136,256]{1,0:T(8,128)(2,1)S(1)}, u32[]{:S(2)}, u32[]{:S(2)}) collective-permute-start(bf16[136,256]{1,0:T(8,128)(2,1)S(1)} %get-tuple-element.81), channel_id=1, source_target_pairs={{0,96},{2,98},{4,100},{6,102},{8,104},{10,106},{12,108},{14,110},{... | collective-permute-start | bytes 208904 | tf_op jit(solution)/shard_map/ppermute | solution.py:704
  79.4 5.9 %collective-permute-start.20 = (bf16[136,256]{1,0:T(8,128)(2,1)S(1)}, bf16[136,256]{1,0:T(8,128)(2,1)S(1)}, u32[]{:S(2)}, u32[]{:S(2)}) collective-permute-start(bf16[136,256]{1,0:T(8,128)(2,1)S(1)} %get-tuple-element.82), channel_id=1, source_target_pairs={{0,64},{2,66},{4,68},{6,70},{8,72},{10,74},{12,76},{14,78},{16,80}... | collective-permute-start | bytes 208904 | tf_op jit(solution)/shard_map/ppermute | solution.py:704
  79.4 6.3 %collective-permute-start.21 = (bf16[136,256]{1,0:T(8,128)(2,1)S(1)}, bf16[136,256]{1,0:T(8,128)(2,1)S(1)}, u32[]{:S(2)}, u32[]{:S(2)}) collective-permute-start(bf16[136,256]{1,0:T(8,128)(2,1)S(1)} %get-tuple-element.83), channel_id=1, source_target_pairs={{0,32},{2,34},{4,36},{6,38},{8,40},{10,42},{12,44},{14,46},{16,48}... | collective-permute-start | bytes 208904 | tf_op jit(solution)/shard_map/ppermute | solution.py:704
  86.6 7.4 %collective-permute-start.22 = (bf16[136,768]{1,0:T(8,128)(2,1)S(1)}, bf16[136,768]{1,0:T(8,128)(2,1)S(1)}, u32[]{:S(2)}, u32[]{:S(2)}) collective-permute-start(bf16[136,768]{1,0:T(8,128)(2,1)S(1)} %output.3), channel_id=1, source_target_pairs={{0,1},{1,0},{2,3},{3,2},{4,5},{5,4},{6,7},{7,6},{8,9},{9,8},{10,11... | collective-permute-start | bytes 626696 | tf_op jit(solution)/shard_map/ppermute | solution.py:700
  95.4 9.8 %collective-permute-start.24 = (bf16[272,512]{1,0:T(8,128)(2,1)S(1)}, bf16[272,512]{1,0:T(8,128)(2,1)S(1)}, u32[]{:S(2)}, u32[]{:S(2)}) collective-permute-start(bf16[272,512]{1,0:T(8,128)(2,1)S(1)} %get-tuple-element.87), channel_id=1, source_target_pairs={{0,1},{1,0},{2,3},{3,2},{4,5},{5,4},{6,7},{7,6},{8,9},{9,8},{10,11... | collective-permute-start | bytes 835592 | tf_op jit(solution)/shard_map/ppermute | solution.py:700
  99.0 6.3 %copy-start.1 = (bf16[256,1536]{1,0:T(8,128)(2,1)S(1)}, bf16[256,1536]{1,0:T(8,128)(2,1)}, u32[]{:S(2)}) copy-start(bf16[256,1536]{1,0:T(8,128)(2,1)} %grad.5) | copy-start | bytes 2359300
  100.7 8.5 %collective-permute-start.23 = (bf16[272,256]{1,0:T(8,128)(2,1)}, bf16[272,256]{1,0:T(8,128)(2,1)}, u32[]{:S(2)}, u32[]{:S(2)}) collective-permute-start(bf16[272,256]{1,0:T(8,128)(2,1)} %decode.2), channel_id=1, source_target_pairs={{0,1},{1,0},{2,3},{3,2},{4,5},{5,4},{6,7},{7,6},{8,9},{9,8},{10,11... | collective-permute-start | bytes 417800 | tf_op jit(solution)/shard_map/ppermute | solution.py:700
  107.2 8.4 %collective-permute-start.26 = (bf16[272,512]{1,0:T(8,128)(2,1)}, bf16[272,512]{1,0:T(8,128)(2,1)}, u32[]{:S(2)}, u32[]{:S(2)}) collective-permute-start(bf16[272,512]{1,0:T(8,128)(2,1)} %get-tuple-element.91.refs_0_), channel_id=1, source_target_pairs={{0,1},{1,0},{2,3},{3,2},{4,5},{5,4},{6,7},{7,6},{8,9},{9,8},{10,11... | collective-permute-start | bytes 835592 | tf_op jit(solution)/shard_map/ppermute | solution.py:700
  111.1 6.9 %collective-permute-start.25 = (bf16[272,256]{1,0:T(8,128)(2,1)}, bf16[272,256]{1,0:T(8,128)(2,1)}, u32[]{:S(2)}, u32[]{:S(2)}) collective-permute-start(bf16[272,256]{1,0:T(8,128)(2,1)} %get-tuple-element.90.refs_1_), channel_id=1, source_target_pairs={{0,1},{1,0},{2,3},{3,2},{4,5},{5,4},{6,7},{7,6},{8,9},{9,8},{10,11... | collective-permute-start | bytes 417800 | tf_op jit(solution)/shard_map/ppermute | solution.py:700

commit v13 on v12

--- a/solution.py
+++ b/solution.py
@@ -38,7 +38,6 @@
 
 
 VM = pl.BlockSpec(memory_space=pltpu.VMEM)
-SM = pl.BlockSpec(memory_space=pltpu.SMEM)
 HBM = pl.BlockSpec(memory_space=pltpu.HBM)
 
 
@@ -73,12 +72,17 @@
     return jnp.concatenate([even, odd], axis=0)
 
 
-def sides(ids, near, far):
-    odd = lax.rem(ids[2], 2) == 1
+def position():
+    at = lax.axis_index("seq")
+    return lax.axis_index("head"), at // 16, at
+
+
+def sides(odd, near, far):
     return jnp.where(odd, near, far), jnp.where(odd, far, near)
 
 
-def prepare_kernel(ids, bases, grad, codes, near, far, code, head, tail, sems):
+def prepare_kernel(bases, grad, codes, near, far, code, head, tail, sems):
+    ids = position()
     rows = grad.shape[0]
     copies = [
         pltpu.make_async_copy(bases, code, sems.at[0]),
@@ -107,11 +111,11 @@
     return pltpu.with_memory_space_constraint(value, pltpu.HBM)
 
 
-def prepare(ids, bases, grad):
+def prepare(bases, grad):
     feats = grad.shape[1]
     return pl.pallas_call(
         prepare_kernel,
-        in_specs=[SM, HBM, HBM],
+        in_specs=[HBM, HBM],
         out_specs=[VM] * 3,
         out_shape=[
             shape((OWN, 128), BF16),
@@ -127,7 +131,7 @@
         compiler_params=params(4),
         cost_estimate=cost(10**5, 10**5),
         name="prepare",
-    )(ids, far_memory(bases), far_memory(grad))
+    )(far_memory(bases), far_memory(grad))
 
 
 def embed_letters(code, stem, embedded):
@@ -185,13 +189,14 @@
     )
 
 
-def encode_kernel(ids, near, far, rows, stem, weight, ahead, encoded, loaded, embedded, halo, sem):
+def encode_kernel(near, far, rows, stem, weight, ahead, encoded, loaded, embedded, halo, sem):
+    ids = position()
     copy = pltpu.make_async_copy(ahead, loaded, sem)
     copy.start()
     feats = stem.shape[1]
     half = weight.shape[2]
     place = lax.broadcasted_iota(jnp.int32, (ROWS - OWN, 128), 0)
-    before, after = sides(ids, near[:, feats:].astype(F32), far[:, feats:].astype(F32))
+    before, after = sides(lax.rem(ids[2], 2) == 1, near[:, feats:].astype(F32), far[:, feats:].astype(F32))
     code = jnp.where(place >= 6, before, 0.0)
     code = jnp.where(place < 2, after, code)
     embed_letters(code.astype(BF16), stem, halo)
@@ -213,12 +218,12 @@
     copy.wait()
 
 
-def encode(ids, near, far, rows, stem, weight, ahead):
+def encode(near, far, rows, stem, weight, ahead):
     half = weight.shape[2]
     feats = stem.shape[1]
     return pl.pallas_call(
         encode_kernel,
-        in_specs=[SM] + [VM] * 5 + [HBM],
+        in_specs=[VM] * 5 + [HBM],
         out_specs=[VM, VM],
         out_shape=[shape((2 * ROWS, half), BF16), pltpu.VMEM(ahead.shape, BF16)],
         scratch_shapes=[
@@ -230,7 +235,6 @@
         cost_estimate=cost(4 * OWN * weight.size, weight.size * 4),
         name="encode",
     )(
-        ids,
         near,
         far,
         near_memory(rows),
@@ -247,8 +251,9 @@
 
 
 def project_keys_kernel(
-    ids, mine, theirs, gain, weight, normed, k0, k1, k2, k3, packed
+    mine, theirs, gain, weight, normed, k0, k1, k2, k3, packed
 ):
+    ids = position()
     half = mine.shape[1]
     near = lanes(ids[0] * half, half)
     far = lanes((1 - ids[0]) * half, half)
@@ -278,21 +283,22 @@
         out[...] = packed[lax.rem(ids[1] + distance, 4), :OWN, :]
 
 
-def project_keys(ids, mine, theirs, gain, weight):
+def project_keys(mine, theirs, gain, weight):
     half = mine.shape[1]
     return pl.pallas_call(
         project_keys_kernel,
-        in_specs=[SM] + [VM] * 4,
+        in_specs=[VM] * 4,
         out_specs=[VM] * 5,
         out_shape=[shape((2, ROWS, half), BF16)] + [shape((OWN, 384), BF16)] * 4,
         scratch_shapes=[pltpu.VMEM((4, ROWS, 384), BF16)],
         compiler_params=params(12),
         cost_estimate=cost(2 * ROWS * weight.size * 2 // 3, weight.size * 2),
         name="project_keys",
-    )(ids, mine, theirs, gain, weight)
-
-
-def project_queries_kernel(ids, normed, weight, q0, q1, q2, q3, packed):
+    )(mine, theirs, gain, weight)
+
+
+def project_queries_kernel(normed, weight, q0, q1, q2, q3, packed):
+    ids = position()
     half = normed.shape[2]
     near = lanes(ids[0] * half, half)
     far = lanes((1 - ids[0]) * half, half)
@@ -307,17 +313,17 @@
         out[...] = packed[lax.rem(ids[1] + distance, 4)]
 
 
-def project_queries(ids, normed, weight):
+def project_queries(normed, weight):
     return pl.pallas_call(
         project_queries_kernel,
-        in_specs=[SM, VM, VM],
+        in_specs=[VM, VM],
         out_specs=[VM] * 4,
         out_shape=[shape((ROWS, 256), BF16)] * 4,
         scratch_shapes=[pltpu.VMEM((4, ROWS, 256), BF16)],
         compiler_params=params(10),
         cost_estimate=cost(2 * ROWS * weight.size // 3, weight.size),
         name="project_queries",
-    )(ids, normed, near_memory(weight))
+    )(normed, near_memory(weight))
 
 
 BLOCK = 4 * ROWS
@@ -360,7 +366,10 @@
     )(*pieces)
 
 
-def attend_kernel(count, known, resumed, final, ids, scale, queries, *refs):
+def attend_kernel(count, known, resumed, final, scale, queries, *refs):
+    heads = lax.broadcasted_iota(jnp.int32, scale.shape, 1)
+    gain = jnp.sum(jnp.where(heads == position()[1], scale[...], 0.0), axis=1, keepdims=True)
+    gain = gain * (LOG2E / HEAD)
     pieces, refs = refs[:count], refs[count:]
     inverses, refs = refs[:known], refs[known:]
     if resumed:
@@ -415,7 +424,7 @@
         query = queries[rows, :]
         wide = query.astype(F32)
         own = lax.rsqrt(jnp.sum(wide * wide, axis=1, keepdims=True) * (1.0 / HEAD) + EPS)
-        factor = own * (scale[ids[1]] * (LOG2E / HEAD))
+        factor = own * gain
         states = [unit(query, factor, group) for group in groups]
         if resumed:
             states.append((old_stats[rows, 0:1], old_stats[rows, 64:65], old_mixed[rows, :]))
@@ -443,7 +452,7 @@
         outs[0][rows, :] = mixed.astype(BF16)
 
 
-def attend(ids, scale, queries, pieces, inverses=(), state=(), final=True):
+def attend(scale, queries, pieces, inverses=(), state=(), final=True):
     rows = queries.shape[0]
     keys = sum(piece.shape[0] for piece in pieces)
     if final:
@@ -455,13 +464,13 @@
         outs.append(shape((8, keys - known), F32))
     return pl.pallas_call(
         functools.partial(attend_kernel, len(pieces), len(inverses), bool(state), final),
-        in_specs=[SM, SM] + [VM] * (1 + len(pieces) + len(inverses) + len(state)),
+        in_specs=[VM] + [VM] * (1 + len(pieces) + len(inverses) + len(state)),
         out_specs=[VM] * len(outs),
         out_shape=outs,
         compiler_params=params(28),
         cost_estimate=cost(4 * rows * keys * 256, 8 * rows * 1024),
         name="attend",
-    )(ids, scale, near_memory(queries), *pieces, *inverses, *state)
+    )(scale, near_memory(queries), *pieces, *inverses, *state)
 
 
 def merge_kernel(a0, a1, *outs):
@@ -488,7 +497,8 @@
     )(*parts)
 
 
-def output_kernel(mine, ids, a0, a1, a2, a3, weight, out):
+def output_kernel(mine, a0, a1, a2, a3, weight, out):
+    ids = position()
     half = out.shape[1]
     side = ids[0] if mine else 1 - ids[0]
 
@@ -505,20 +515,21 @@
     tiles(half // TILE, tile)
 
 
-def output(ids, heads, weight, mine, dtype):
+def output(heads, weight, mine, dtype):
     half = weight.shape[1] // 2
     return pl.pallas_call(
         functools.partial(output_kernel, mine),
-        in_specs=[SM] + [VM] * 5,
+        in_specs=[VM] * 5,
         out_specs=VM,
         out_shape=shape((ROWS, half), dtype),
         compiler_params=params(6),
         cost_estimate=cost(2 * ROWS * weight.size // 2, weight.size),
         name="output",
-    )(ids, *heads, weight)
-
-
-def decode_first_kernel(ids, own, other, encoded, weight, inputs, out):
+    )(*heads, weight)
+
+
+def decode_first_kernel(own, other, encoded, weight, inputs, out):
+    ids = position()
     half = weight.shape[1]
 
     def mix(i):
@@ -546,38 +557,40 @@
     tiles(out.shape[1] // TILE, tile)
 
 
-def decode_first(ids, own, other, encoded, weight, width):
+def decode_first(own, other, encoded, weight, width):
     half = weight.shape[1]
     return pl.pallas_call(
         decode_first_kernel,
-        in_specs=[SM] + [VM] * 4,
+        in_specs=[VM] * 4,
         out_specs=[VM] * 2,
         out_shape=[shape((2 * ROWS, half), BF16), shape((2 * ROWS, width), BF16)],
         compiler_params=params(8),
         cost_estimate=cost(10**6, 10**4),
         name="decode_first",
-    )(ids, own, other, encoded, weight)
-
-
-def decode_kernel(mine, first, ids, inputs, weight, out):
+    )(own, other, encoded, weight)
+
+
+def decode_kernel(mine, first, inputs, weight, out):
+    ids = position()
     side = ids[0] if mine else 1 - ids[0]
     decode_tiles(inputs, weight, out, side * weight.shape[1] + first)
 
 
-def decode(ids, inputs, weight, mine, first, width, dtype):
+def decode(inputs, weight, mine, first, width, dtype):
     half = weight.shape[1]
     return pl.pallas_call(
         functools.partial(decode_kernel, mine, first),
-        in_specs=[SM, VM, VM],
+        in_specs=[VM, VM],
         out_specs=VM,
         out_shape=shape((2 * ROWS, width), dtype),
         compiler_params=params(8),
         cost_estimate=cost(10**6, 10**4),
         name="decode",
-    )(ids, inputs, weight)
-
-
-def slope_kernel(first, ids, own, other, inputs, grad, near, far, *refs):
+    )(inputs, weight)
+
+
+def slope_kernel(first, own, other, inputs, grad, near, far, *refs):
+    ids = position()
     done, (decoded, slope, paired, wide) = refs[:-4], refs[-4:]
     half = own.shape[1]
     begin = 0
@@ -604,7 +617,7 @@
         odd = wide[2 * i + 1, pl.ds(1, OWN, 2), :]
         paired[:, at] = even + odd
         row = lax.broadcasted_iota(jnp.int32, (ROWS - OWN, 128), 0)
-        before, after = sides(ids, near[:, column].astype(F32), far[:, column].astype(F32))
+        before, after = sides(lax.rem(ids[2], 2) == 1, near[:, column].astype(F32), far[:, column].astype(F32))
         even_edge = jnp.where(row == 0, after, 0.0)
         odd_edge = jnp.where(row == ROWS - OWN - 1, before, 0.0)
         cotangent = jnp.concatenate([even, even_edge, odd, odd_edge], axis=0)
@@ -613,11 +626,11 @@
     tiles(other.shape[1] // 128, tile)
 
 
-def slopes(ids, own, other, inputs, grad, near, far, first, done=()):
+def slopes(own, other, inputs, grad, near, far, first, done=()):
     width = other.shape[1]
     return pl.pallas_call(
         functools.partial(slope_kernel, first),
-        in_specs=[SM] + [VM] * (6 + len(done)),
+        in_specs=[VM] * (6 + len(done)),
         out_specs=[VM] * 3,
         out_shape=[
             shape((2 * OWN, width + (first if done else 0)), BF16),
@@ -628,10 +641,11 @@
         compiler_params=params(8),
         cost_estimate=cost(100 * 30 * 1000 * other.size, 14 * other.size),
         name="slopes",
-    )(ids, own, other, inputs, grad, near, far, *done)
-
-
-def backward_kernel(mine, firsts, count, ids, *refs):
+    )(own, other, inputs, grad, near, far, *done)
+
+
+def backward_kernel(mine, firsts, count, *refs):
+    ids = position()
     slopes_in, starts, (weight, out) = (
         refs[: len(firsts)],
         refs[len(firsts) : len(firsts) + count],
@@ -670,18 +684,18 @@
         begin += width
 
 
-def backward(ids, parts, starts, weight, mine, dtype):
+def backward(parts, starts, weight, mine, dtype):
     half = weight.shape[1]
     size = sum(part.size for _, part in parts)
     return pl.pallas_call(
         functools.partial(backward_kernel, mine, [first for first, _ in parts], len(starts)),
-        in_specs=[SM] + [VM] * (len(parts) + len(starts) + 1),
+        in_specs=[VM] * (len(parts) + len(starts) + 1),
         out_specs=VM,
         out_shape=shape((OWN, half), dtype),
         compiler_params=params(10),
         cost_estimate=cost(100 * 2 * 3 * half * size, 6 * size),
         name="backward",
-    )(ids, *[part for _, part in parts], *starts, weight)
+    )(*[part for _, part in parts], *starts, weight)
 
 
 def place(at):
@@ -717,20 +731,19 @@
 ):
     at = lax.axis_index("seq")
     x = at // 16
-    ids = jnp.stack([lax.axis_index("head"), x, at]).astype(jnp.int32)
     feats = grad_out.shape[1]
 
-    codes, near, far = prepare(ids, dna_bases.reshape(OWN, 128), grad_out)
+    codes, near, far = prepare(dna_bases.reshape(OWN, 128), grad_out)
     near = send(near, dc=1)
     pairs = [(i, i + 1) for i in range(1, 63, 2)]
     far = lax.ppermute(far, "seq", pairs + [(b, a) for a, b in pairs])
     halo = near, far
     rows, stem_weight, encoder_weight = load(codes, stem_weight, encoder_weight)
     encoded, attention_weight = encode(
-        ids, *halo, rows, stem_weight, encoder_weight, attention_weight
+        *halo, rows, stem_weight, encoder_weight, attention_weight
     )
     gain = norm_gain.reshape(1, feats)
-    normed, *keyvals = project_keys(ids, encoded, swap(encoded), gain, attention_weight)
+    normed, *keyvals = project_keys(encoded, swap(encoded), gain, attention_weight)
 
     def spread(blocks):
         return [send(blocks[d], dx=d) for d in (1, 3, 2)]
@@ -741,7 +754,7 @@
     got = spread(keyvals)
     keyvals = stacked([keyvals[0]] + got)
     near = [send(keyvals, dz=1), send(keyvals, dz=3)]
-    queries = project_queries(ids, normed, attention_weight)
+    queries = project_queries(normed, attention_weight)
     *near, got = lax.optimization_barrier((*near, spread(queries)))
     queries = jnp.concatenate([queries[0]] + got, axis=0)
     others = send(queries, dy=1)
@@ -753,33 +766,34 @@
     *far, inverse, others = lax.optimization_barrier((*far, inverse, others))
     far = jnp.concatenate(far, axis=0)
     pieces += [far, send(far, dc=1)]
-    other, later = attend(ids, logit_scale, others, pieces, inverses=[inverse])
+    scale = logit_scale.reshape(1, 4)
+    other, later = attend(scale, others, pieces, inverses=[inverse])
     other = send(other, dy=1)
-    own = attend(ids, logit_scale, queries, pieces, inverses=[inverse, later])[0]
+    own = attend(scale, queries, pieces, inverses=[inverse, later])[0]
     mixed = merge([own, other])
     heads = [mixed[0], send(mixed[1], dx=-1), send(mixed[3], dx=-2), send(mixed[2], dx=-3)]
 
-    sent = swap(output(ids, heads, out_weight, False, BF16))
-    kept = output(ids, heads, out_weight, True, F32)
+    sent = swap(output(heads, out_weight, False, BF16))
+    kept = output(heads, out_weight, True, F32)
     half = decoder_weight.shape[1]
     split = 2 * TILE
-    inputs, early = decode_first(ids, kept, sent, encoded, decoder_weight, split)
+    inputs, early = decode_first(kept, sent, encoded, decoder_weight, split)
     early = swap(early)
-    late = decode(ids, inputs, decoder_weight, False, split, half - split, BF16)
+    late = decode(inputs, decoder_weight, False, split, half - split, BF16)
     late, inputs = lax.optimization_barrier((late, inputs))
     late = swap(late)
-    kept = decode(ids, inputs, decoder_weight, True, 0, half, F32)
-    decoded, early, paired = slopes(ids, kept, early, inputs, grad_out, *halo, 0)
+    kept = decode(inputs, decoder_weight, True, 0, half, F32)
+    decoded, early, paired = slopes(kept, early, inputs, grad_out, *halo, 0)
     early_back = swap(early)
     decoded, late, rest = slopes(
-        ids, kept, late, inputs, grad_out, *halo, split, (decoded,)
+        kept, late, inputs, grad_out, *halo, split, (decoded,)
     )
     late_back = swap(late)
     total = backward(
-        ids, [(0, early), (split, late)], [paired, rest], decoder_weight, True, F32
+        [(0, early), (split, late)], [paired, rest], decoder_weight, True, F32
     )
-    total = backward(ids, [(0, early_back)], [total], decoder_weight, False, F32)
-    bins_grad = backward(ids, [(split, late_back)], [total], decoder_weight, False, BF16)
+    total = backward([(0, early_back)], [total], decoder_weight, False, F32)
+    bins_grad = backward([(split, late_back)], [total], decoder_weight, False, BF16)
     return decoded, bins_grad
 
 

time: 120 us -> 118 us (0.983)
  Pallas kernels: 39.5 us -> 34.8 us
  waiting for transfers between devices: 35.5 us -> 38.6 us
    pallas_call x11, Pallas kernels: 18.9 us -> 15.6 us  [the longest x1 5.16 us: encode(): pl.pallas_call(encode_kernel, in_specs=[VM] * 5 + [HBM], out_specs=[VM, V...]
    ppermute x6, waiting for transfers between devices: 15.6 us -> 17.3 us  [swap(): return lax.ppermute(value, 'head', [(0, 1), (1, 0)])]
    ppermute x20, waiting for transfers between devices: 19.8 us -> 21.3 us  [send(): return lax.ppermute(value, 'seq', moves(**step))]
  transfers between devices with their start and end apart: 27 -> 27, of which waited for: 15 -> 16; matrix products, arithmetic and copies ran while one was open for 0% -> 0% of each run, Pallas kernels for 19% -> 16%
where the time goes in v13:
time: 118 us
  starting transfers between devices  43.4 us (37%)
  waiting for transfers between devices  38.6 us (33%)
  Pallas kernels  34.8 us (29%)
    ppermute x20, starting transfers between devices, send(): return lax.ppermute(value, 'seq', moves(**step))  28.8 us
    ppermute x20, waiting for transfers between devices, send(): return lax.ppermute(value, 'seq', moves(**step))  21.3 us
    ppermute x6, waiting for transfers between devices, swap(): return lax.ppermute(value, 'head', [(0, 1), (1, 0)])  17.3 us
    ppermute x6, starting transfers between devices, swap(): return lax.ppermute(value, 'head', [(0, 1), (1, 0)])  13.9 us
    pallas_call x2, Pallas kernels, attend(): pl.pallas_call(functools.partial(attend_kernel, len(pieces), len(inverses...  8.36 us
    pallas_call x3, Pallas kernels, backward(): pl.pallas_call(functools.partial(backward_kernel, mine, [first for first,...  6.12 us
    pallas_call x1, Pallas kernels, encode(): pl.pallas_call(encode_kernel, in_specs=[VM] * 5 + [HBM], out_specs=[VM, V...  5.16 us
    pallas_call x2, Pallas kernels, slopes(): pl.pallas_call(functools.partial(slope_kernel, first), in_specs=[VM] * (6...  3.32 us
  transfers between devices with their start and end apart: 27, of which 16 were waited for; matrix products, arithmetic and copies ran while one was open for 0% of the time, Pallas kernels for 16%

profile of v13, /device:TPU:0, one launch (start us, length us, event | category | flops | bytes accessed | tf_op | source)
XLA Modules:
  0.0 117.9 jit_solution(8739368119057231400)
XLA Ops:
  0.6 0.9 prepare.1
  1.5 0.1 collective-permute-start
  1.6 0.7 collective-permute-start.1
  2.3 3.3 %load.1 = (bf16[256,1536]{1,0:T(8,128)(2,1)S(1)}, bf16[256,1536]{1,0:T(8,128)(2,1)S(1)}, bf16[3,1536,768]{2,1,0:T(8,128)(2,1)S(1)}) custom-call(bf16[128,128]{1,0:T(8,128)(2,1)S(1)} %get-tuple-element.50.codes, bf16[256,1536]{1,0:T(8,128)(2,1)} %stems.1, bf16[3,1536,768]{2,1,0:T(8,128)(2,1)} %weights.1), custom_call_target="tpu_custom_call" | custom-call | flops 100000 | bytes 7077888 | tf_op jit(solution)/shard_map/load/pallas_call | solution.py:168
  5.6 0.0 collective-permute-done.near
  5.6 0.0 copy-start.3
  5.6 5.2 %encode.1 = (bf16[272,768]{1,0:T(8,128)(2,1)S(1)}, bf16[3,1536,768]{2,1,0:T(8,128)(2,1)S(1)}) custom-call(bf16[8,1664]{1,0:T(8,128)(2,1)S(1)} %collective-permute-done.near, bf16[8,1664]{1,0:T(8,128)(2,1)S(1)} %collective-permute-done.1.far, bf16[256,1536]{1,0:T(8,128)(2,1)S(1)} %get-tuple-element.51.rows, bf16[256,1536]{1,0:T(8,128)(2,1)S(1)} %get-tuple-element.52.stem, ...), custom_call_target="tpu_custom_call" | custom-call | flops 1811939328 | bytes 14155776 | tf_op jit(solution)/shard_map/encode/pallas_call | solution.py:224
  10.8 3.4 %collective-permute-start.2 = (bf16[272,768]{1,0:T(8,128)(2,1)S(1)}, bf16[272,768]{1,0:T(8,128)(2,1)S(1)}, u32[]{:S(2)}, u32[]{:S(2)}) collective-permute-start(bf16[272,768]{1,0:T(8,128)(2,1)S(1)} %get-tuple-element.54.mine.encoded), channel_id=1, source_target_pairs={{0,1},{1,0},{2,3},{3,2},{4,5},{5,4},{6,7},{7,6},{8,9},{9,8},{10,11... | collective-permute-start | bytes 1253384 | tf_op jit(solution)/shard_map/ppermute | solution.py:714
  14.2 8.6 %collective-permute-done.2.theirs = bf16[272,768]{1,0:T(8,128)(2,1)S(1)} collective-permute-done((bf16[272,768]{1,0:T(8,128)(2,1)S(1)}, bf16[272,768]{1,0:T(8,128)(2,1)S(1)}, u32[]{:S(2)}, u32[]{:S(2)}) %collective-permute-start.2) | collective-permute-done | bytes 417824 | tf_op jit(solution)/shard_map/ppermute | solution.py:714
  22.8 1.5 %project_keys.1 = (bf16[2,136,768]{2,1,0:T(8,128)(2,1)S(1)}, bf16[128,384]{1,0:T(8,128)(2,1)S(1)}, bf16[128,384]{1,0:T(8,128)(2,1)S(1)}, bf16[128,384]{1,0:T(8,128)(2,1)S(1)}, bf16[128,384]{1,0:T(8,128)(2,1)S(1)}) custom-call(bf16[272,768]{1,0:T(8,128)(2,1)S(1)} %get-tuple-element.54.mine.encoded, bf16[272,768]{1,0:T(8,128)(2,1)S(1)} %collective-permute-done.2.theirs, ...), custom_call_target="tpu_custom_call" | custom-call | flops 641728512 | bytes 7077888 | tf_op jit(solution)/shard_map/project_keys/pallas_call | solution.py:288
  24.3 0.0 copy-start.2
  24.3 5.7 %collective-permute-start.3 = (bf16[128,384]{1,0:T(8,128)(2,1)S(1)}, bf16[128,384]{1,0:T(8,128)(2,1)S(1)}, u32[]{:S(2)}, u32[]{:S(2)}) collective-permute-start(bf16[128,384]{1,0:T(8,128)(2,1)S(1)} %get-tuple-element.59), channel_id=1, source_target_pairs={{0,32},{2,34},{4,36},{6,38},{8,40},{10,42},{12,44},{14,46},{16,48}... | collective-permute-start | bytes 294920 | tf_op jit(solution)/shard_map/ppermute | solution.py:718
  30.0 1.6 %collective-permute-start.4 = (bf16[128,384]{1,0:T(8,128)(2,1)S(1)}, bf16[128,384]{1,0:T(8,128)(2,1)S(1)}, u32[]{:S(2)}, u32[]{:S(2)}) collective-permute-start(bf16[128,384]{1,0:T(8,128)(2,1)S(1)} %get-tuple-element.60), channel_id=1, source_target_pairs={{0,96},{2,98},{4,100},{6,102},{8,104},{10,106},{12,108},{14,110},{... | collective-permute-start | bytes 294920 | tf_op jit(solution)/shard_map/ppermute | solution.py:718
  31.6 2.0 %collective-permute-start.5 = (bf16[128,384]{1,0:T(8,128)(2,1)S(1)}, bf16[128,384]{1,0:T(8,128)(2,1)S(1)}, u32[]{:S(2)}, u32[]{:S(2)}) collective-permute-start(bf16[128,384]{1,0:T(8,128)(2,1)S(1)} %get-tuple-element.61), channel_id=1, source_target_pairs={{0,64},{2,66},{4,68},{6,70},{8,72},{10,74},{12,76},{14,78},{16,80}... | collective-permute-start | bytes 294920 | tf_op jit(solution)/shard_map/ppermute | solution.py:718
  33.6 1.6 %collective-permute-done.3 = bf16[128,384]{1,0:T(8,128)(2,1)S(1)} collective-permute-done((bf16[128,384]{1,0:T(8,128)(2,1)S(1)}, bf16[128,384]{1,0:T(8,128)(2,1)S(1)}, u32[]{:S(2)}, u32[]{:S(2)}) %collective-permute-start.3) | collective-permute-done | bytes 98336 | tf_op jit(solution)/shard_map/ppermute | solution.py:718
  35.1 2.6 %collective-permute-done.5 = bf16[128,384]{1,0:T(8,128)(2,1)S(1)} collective-permute-done((bf16[128,384]{1,0:T(8,128)(2,1)S(1)}, bf16[128,384]{1,0:T(8,128)(2,1)S(1)}, u32[]{:S(2)}, u32[]{:S(2)}) %collective-permute-start.5) | collective-permute-done | bytes 98336 | tf_op jit(solution)/shard_map/ppermute | solution.py:718
  37.8 2.2 %collective-permute-start.6 = (bf16[512,384]{1,0:T(8,128)(2,1)S(1)}, bf16[512,384]{1,0:T(8,128)(2,1)S(1)}, u32[]{:S(2)}, u32[]{:S(2)}) collective-permute-start(bf16[512,384]{1,0:T(8,128)(2,1)S(1)} %constant_dynamic-update-slice_fusion.refs_0_), channel_id=1, source_target_pairs={{0,8},{2,10},{4,12},{6,14},{8,16},{10,18},{12,20},{14,22},{16,24},... | collective-permute-start | bytes 1179656 | tf_op jit(solution)/shard_map/ppermute | solution.py:718
  39.9 2.2 %collective-permute-start.7 = (bf16[512,384]{1,0:T(8,128)(2,1)S(1)}, bf16[512,384]{1,0:T(8,128)(2,1)S(1)}, u32[]{:S(2)}, u32[]{:S(2)}) collective-permute-start(bf16[512,384]{1,0:T(8,128)(2,1)S(1)} %constant_dynamic-update-slice_fusion.refs_0_), channel_id=1, source_target_pairs={{0,24},{2,26},{4,28},{6,30},{8,0},{10,2},{12,4},{14,6},{16,8},{18,... | collective-permute-start | bytes 1179656 | tf_op jit(solution)/shard_map/ppermute | solution.py:718
  42.1 0.7 project_queries.1
  42.9 1.9 %collective-permute-start.10 = (bf16[136,256]{1,0:T(8,128)(2,1)S(1)}, bf16[136,256]{1,0:T(8,128)(2,1)S(1)}, u32[]{:S(2)}, u32[]{:S(2)}) collective-permute-start(bf16[136,256]{1,0:T(8,128)(2,1)S(1)} %get-tuple-element.68), channel_id=1, source_target_pairs={{0,64},{2,66},{4,68},{6,70},{8,72},{10,74},{12,76},{14,78},{16,80}... | collective-permute-start | bytes 208904 | tf_op jit(solution)/shard_map/ppermute | solution.py:718
  44.8 0.7 collective-permute-start.8
  45.4 2.6 %collective-permute-start.9 = (bf16[136,256]{1,0:T(8,128)(2,1)S(1)}, bf16[136,256]{1,0:T(8,128)(2,1)S(1)}, u32[]{:S(2)}, u32[]{:S(2)}) collective-permute-start(bf16[136,256]{1,0:T(8,128)(2,1)S(1)} %get-tuple-element.67), channel_id=1, source_target_pairs={{0,96},{2,98},{4,100},{6,102},{8,104},{10,106},{12,108},{14,110},{... | collective-permute-start | bytes 208904 | tf_op jit(solution)/shard_map/ppermute | solution.py:718
  48.0 0.7 collective-permute-done.10
  48.8 1.5 %collective-permute-done.8 = bf16[136,256]{1,0:T(8,128)(2,1)S(1)} collective-permute-done((bf16[136,256]{1,0:T(8,128)(2,1)S(1)}, bf16[136,256]{1,0:T(8,128)(2,1)S(1)}, u32[]{:S(2)}, u32[]{:S(2)}) %collective-permute-start.8) | collective-permute-done | bytes 69664 | tf_op jit(solution)/shard_map/ppermute | solution.py:718
  50.3 0.1 collective-permute-start.12
  50.4 0.5 collective-permute-start.13
  50.9 1.4 %collective-permute-start.16 = (bf16[544,256]{1,0:T(8,128)(2,1)S(1)}, bf16[544,256]{1,0:T(8,128)(2,1)S(1)}, u32[]{:S(2)}, u32[]{:S(2)}) collective-permute-start(bf16[544,256]{1,0:T(8,128)(2,1)S(1)} %constant_dynamic-update-slice_fusion.4.queries), channel_id=1, source_target_pairs={{0,4},{2,6},{4,0},{6,2},{8,12},{10,14},{12,8},{14,10},{16,20},{18,... | collective-permute-start | bytes 835592 | tf_op jit(solution)/shard_map/ppermute | solution.py:718
  52.4 1.2 %collective-permute-start.14 = (bf16[256,384]{1,0:T(8,128)(2,1)S(1)}, bf16[256,384]{1,0:T(8,128)(2,1)S(1)}, u32[]{:S(2)}, u32[]{:S(2)}) collective-permute-start(bf16[256,384]{1,0:T(8,128)(2,1)S(1)} %slice.6), channel_id=1, source_target_pairs={{0,8},{2,10},{4,12},{6,14},{8,16},{10,18},{12,20},{14,22},{16,24},... | collective-permute-start | bytes 589832 | tf_op jit(solution)/shard_map/ppermute | solution.py:718
  53.6 2.1 %collective-permute-start.15 = (bf16[256,384]{1,0:T(8,128)(2,1)S(1)}, bf16[256,384]{1,0:T(8,128)(2,1)S(1)}, u32[]{:S(2)}, u32[]{:S(2)}) collective-permute-start(bf16[256,384]{1,0:T(8,128)(2,1)S(1)} %slice.7), channel_id=1, source_target_pairs={{0,24},{2,26},{4,28},{6,30},{8,0},{10,2},{12,4},{14,6},{16,8},{18,... | collective-permute-start | bytes 589832 | tf_op jit(solution)/shard_map/ppermute | solution.py:718
  55.7 0.9 norms.1.refs_8_
  56.6 3.6 %collective-permute-done.14 = bf16[256,384]{1,0:T(8,128)(2,1)S(1)} collective-permute-done((bf16[256,384]{1,0:T(8,128)(2,1)S(1)}, bf16[256,384]{1,0:T(8,128)(2,1)S(1)}, u32[]{:S(2)}, u32[]{:S(2)}) %collective-permute-start.14) | collective-permute-done | bytes 196640 | tf_op jit(solution)/shard_map/ppermute | solution.py:718
  60.3 0.3 collective-permute-start.17
  60.6 1.7 %collective-permute-done.17.refs_7_ = bf16[512,384]{1,0:T(8,128)(2,1)S(1)} collective-permute-done((bf16[512,384]{1,0:T(8,128)(2,1)S(1)}, bf16[512,384]{1,0:T(8,128)(2,1)S(1)}, u32[]{:S(2)}, u32[]{:S(2)}) %collective-permute-start.17) | collective-permute-done | bytes 393248 | tf_op jit(solution)/shard_map/ppermute | solution.py:718
  62.3 4.3 %attend.2 = (bf16[544,256]{1,0:T(8,128)(2,1)S(1)}, f32[8,1024]{1,0:T(8,128)S(1)}) custom-call(f32[1,4]{1,0:T(1,128)S(1)} %bitcast.4, bf16[544,256]{1,0:T(8,128)(2,1)S(1)} %collective-permute-done.16.queries, bf16[512,384]{1,0:T(8,128)(2,1)S(1)} %constant_dynamic-update-slice_fusion.refs_0_, bf16[512,384]{1,0:T(8,128)(2,1)S(1)} %collective-permute-done.6.refs_1_, ...), custom_call_target="tpu_custom_call" | custom-call | flops 2281701376 | bytes 4456448 | tf_op jit(solution)/shard_map/attend/pallas_call | solution.py:465
  66.6 0.8 collective-permute-start.18
  67.5 4.0 %attend.3.a0 = bf16[544,256]{1,0:T(8,128)(2,1)S(1)} custom-call(f32[1,4]{1,0:T(1,128)S(1)} %bitcast.5, bf16[544,256]{1,0:T(8,128)(2,1)S(1)} %constant_dynamic-update-slice_fusion.4.queries, bf16[512,384]{1,0:T(8,128)(2,1)S(1)} %constant_dynamic-update-slice_fusion.refs_0_, bf16[512,384]{1,0:T(8,128)(2,1)S(1)} %collective-permute-done.6.refs_1_, ...), custom_call_target="tpu_custom_call" | custom-call | flops 2281701376 | bytes 4456448 | tf_op jit(solution)/shard_map/attend/pallas_call | solution.py:465
  71.5 3.9 %collective-permute-done.18.a1 = bf16[544,256]{1,0:T(8,128)(2,1)S(1)} collective-permute-done((bf16[544,256]{1,0:T(8,128)(2,1)S(1)}, bf16[544,256]{1,0:T(8,128)(2,1)S(1)}, u32[]{:S(2)}, u32[]{:S(2)}) %collective-permute-start.18) | collective-permute-done | bytes 278560 | tf_op jit(solution)/shard_map/ppermute | solution.py:718
  75.4 0.5 merge.1
  76.0 2.6 %collective-permute-start.19 = (bf16[136,256]{1,0:T(8,128)(2,1)S(1)}, bf16[136,256]{1,0:T(8,128)(2,1)S(1)}, u32[]{:S(2)}, u32[]{:S(2)}) collective-permute-start(bf16[136,256]{1,0:T(8,128)(2,1)S(1)} %get-tuple-element.81), channel_id=1, source_target_pairs={{0,96},{2,98},{4,100},{6,102},{8,104},{10,106},{12,108},{14,110},{... | collective-permute-start | bytes 208904 | tf_op jit(solution)/shard_map/ppermute | solution.py:718
  78.6 0.5 collective-permute-start.20
  79.0 0.5 collective-permute-start.21
  79.5 1.7 %collective-permute-done.19.a1 = bf16[136,256]{1,0:T(8,128)(2,1)S(1)} collective-permute-done((bf16[136,256]{1,0:T(8,128)(2,1)S(1)}, bf16[136,256]{1,0:T(8,128)(2,1)S(1)}, u32[]{:S(2)}, u32[]{:S(2)}) %collective-permute-start.19) | collective-permute-done | bytes 69664 | tf_op jit(solution)/shard_map/ppermute | solution.py:718
  81.2 3.3 %collective-permute-done.20.a2 = bf16[136,256]{1,0:T(8,128)(2,1)S(1)} collective-permute-done((bf16[136,256]{1,0:T(8,128)(2,1)S(1)}, bf16[136,256]{1,0:T(8,128)(2,1)S(1)}, u32[]{:S(2)}, u32[]{:S(2)}) %collective-permute-start.20) | collective-permute-done | bytes 69664 | tf_op jit(solution)/shard_map/ppermute | solution.py:718
  84.5 0.7 collective-permute-done.21.a3
  85.2 0.4 output.3
  85.6 3.3 %collective-permute-start.22 = (bf16[136,768]{1,0:T(8,128)(2,1)S(1)}, bf16[136,768]{1,0:T(8,128)(2,1)S(1)}, u32[]{:S(2)}, u32[]{:S(2)}) collective-permute-start(bf16[136,768]{1,0:T(8,128)(2,1)S(1)} %output.3), channel_id=1, source_target_pairs={{0,1},{1,0},{2,3},{3,2},{4,5},{5,4},{6,7},{7,6},{8,9},{9,8},{10,11... | collective-permute-start | bytes 626696 | tf_op jit(solution)/shard_map/ppermute | solution.py:714
  88.8 0.4 output.2.own
  89.2 3.7 %collective-permute-done.22.other = bf16[136,768]{1,0:T(8,128)(2,1)S(1)} collective-permute-done((bf16[136,768]{1,0:T(8,128)(2,1)S(1)}, bf16[136,768]{1,0:T(8,128)(2,1)S(1)}, u32[]{:S(2)}, u32[]{:S(2)}) %collective-permute-start.22) | collective-permute-done | bytes 208928 | tf_op jit(solution)/shard_map/ppermute | solution.py:714
  92.9 0.9 decode_first.1
  93.9 3.5 %collective-permute-start.24 = (bf16[272,512]{1,0:T(8,128)(2,1)S(1)}, bf16[272,512]{1,0:T(8,128)(2,1)S(1)}, u32[]{:S(2)}, u32[]{:S(2)}) collective-permute-start(bf16[272,512]{1,0:T(8,128)(2,1)S(1)} %get-tuple-element.87), channel_id=1, source_target_pairs={{0,1},{1,0},{2,3},{3,2},{4,5},{5,4},{6,7},{7,6},{8,9},{9,8},{10,11... | collective-permute-start | bytes 835592 | tf_op jit(solution)/shard_map/ppermute | solution.py:714
  97.4 1.2 decode.2
  98.5 0.3 collective-permute-start.23
  98.8 1.2 decode.3.own
  100.0 3.6 %collective-permute-done.24.other = bf16[272,512]{1,0:T(8,128)(2,1)S(1)} collective-permute-done((bf16[272,512]{1,0:T(8,128)(2,1)S(1)}, bf16[272,512]{1,0:T(8,128)(2,1)S(1)}, u32[]{:S(2)}, u32[]{:S(2)}) %collective-permute-start.24) | collective-permute-done | bytes 278560 | tf_op jit(solution)/shard_map/ppermute | solution.py:714
  103.6 1.4 %slopes.2 = (bf16[256,512]{1,0:T(8,128)(2,1)S(1)}, bf16[272,512]{1,0:T(8,128)(2,1)}, f32[128,512]{1,0:T(8,128)S(1)}) custom-call(f32[272,768]{1,0:T(8,128)S(1)} %decode.3.own, bf16[272,512]{1,0:T(8,128)(2,1)S(1)} %collective-permute-done.24.other, bf16[272,768]{1,0:T(8,128)(2,1)S(1)} %get-tuple-element.85.inputs, bf16[256,1536]{1,0:T(8,128)(2,1)S(1)} %copy-done.1, ...), custom_call_target="tpu_custom_call" | custom-call | flops 417792000000 | bytes 1949696 | tf_op jit(solution)/shard_map/slopes/pallas_call | solution.py:631
  105.0 1.8 %collective-permute-start.26 = (bf16[272,512]{1,0:T(8,128)(2,1)}, bf16[272,512]{1,0:T(8,128)(2,1)}, u32[]{:S(2)}, u32[]{:S(2)}) collective-permute-start(bf16[272,512]{1,0:T(8,128)(2,1)} %get-tuple-element.91.refs_0_), channel_id=1, source_target_pairs={{0,1},{1,0},{2,3},{3,2},{4,5},{5,4},{6,7},{7,6},{8,9},{9,8},{10,11... | collective-permute-start | bytes 835592 | tf_op jit(solution)/shard_map/ppermute | solution.py:714
  106.8 0.1 collective-permute-done.23.other
  106.9 2.0 %slopes.3 = (bf16[256,768]{1,0:T(8,128)(2,1)}, bf16[272,256]{1,0:T(8,128)(2,1)}, f32[128,256]{1,0:T(8,128)S(1)}) custom-call(f32[272,768]{1,0:T(8,128)S(1)} %decode.3.own, bf16[272,256]{1,0:T(8,128)(2,1)} %collective-permute-done.23.other, bf16[272,768]{1,0:T(8,128)(2,1)S(1)} %get-tuple-element.85.inputs, bf16[256,1536]{1,0:T(8,128)(2,1)S(1)} %copy-done.1, ...), custom_call_target="tpu_custom_call" | custom-call | flops 208896000000 | bytes 974848 | tf_op jit(solution)/shard_map/slopes/pallas_call | solution.py:631
  108.9 1.6 %collective-permute-start.25 = (bf16[272,256]{1,0:T(8,128)(2,1)}, bf16[272,256]{1,0:T(8,128)(2,1)}, u32[]{:S(2)}, u32[]{:S(2)}) collective-permute-start(bf16[272,256]{1,0:T(8,128)(2,1)} %get-tuple-element.90.refs_1_), channel_id=1, source_target_pairs={{0,1},{1,0},{2,3},{3,2},{4,5},{5,4},{6,7},{7,6},{8,9},{9,8},{10,11... | collective-permute-start | bytes 417800 | tf_op jit(solution)/shard_map/ppermute | solution.py:714
  110.5 2.2 %backward.3.refs_1_ = f32[128,768]{1,0:T(8,128)S(1)} custom-call(bf16[272,512]{1,0:T(8,128)(2,1)} %get-tuple-element.91.refs_0_, bf16[272,256]{1,0:T(8,128)(2,1)} %get-tuple-element.90.refs_1_, f32[128,512]{1,0:T(8,128)S(1)} %get-tuple-element.92.refs_2_, f32[128,256]{1,0:T(8,128)S(1)} %get-tuple-element.93.refs_3_, bf16[3,768,1536]{2,1,0:T(8,128)(2,1)S(1)} %bitcast.3), custom_call_target="tpu_custom_call" | custom-call | flops 96259276800 | bytes 1253376 | tf_op jit(solution)/shard_map/backward/pallas_call | solution.py:690
  112.7 0.7 collective-permute-done.26.refs_0_
  113.3 1.8 %backward.4.refs_1_ = f32[128,768]{1,0:T(8,128)S(1)} custom-call(bf16[272,512]{1,0:T(8,128)(2,1)} %collective-permute-done.26.refs_0_, f32[128,768]{1,0:T(8,128)S(1)} %backward.3.refs_1_, bf16[3,768,1536]{2,1,0:T(8,128)(2,1)S(1)} %bitcast.3), custom_call_target="tpu_custom_call" | custom-call | flops 64172851200 | bytes 835584 | tf_op jit(solution)/shard_map/backward/pallas_call | solution.py:690
  115.1 0.6 collective-permute-done.25.refs_0_
  115.7 2.1 %backward.5 = bf16[128,768]{1,0:T(8,128)(2,1)} custom-call(bf16[272,256]{1,0:T(8,128)(2,1)} %collective-permute-done.25.refs_0_, f32[128,768]{1,0:T(8,128)S(1)} %backward.4.refs_1_, bf16[3,768,1536]{2,1,0:T(8,128)(2,1)S(1)} %bitcast.3), custom_call_target="tpu_custom_call" | custom-call | flops 32086425600 | bytes 417792 | tf_op jit(solution)/shard_map/backward/pallas_call | solution.py:690
  (35 shorter events, 0.2 us)
Async XLA Ops:
  1.5 4.1 %collective-permute-start = (bf16[8,1664]{1,0:T(8,128)(2,1)S(1)}, bf16[8,1664]{1,0:T(8,128)(2,1)S(1)}, u32[]{:S(2)}, u32[]{:S(2)}) collective-permute-start(bf16[8,1664]{1,0:T(8,128)(2,1)S(1)} %get-tuple-element.48), channel_id=1, source_target_pairs={{0,2},{2,0},{4,6},{6,4},{8,10},{10,8},{12,14},{14,12},{16,18},{18,... | collective-permute-start | bytes 79880 | tf_op jit(solution)/shard_map/ppermute | solution.py:718
  1.6 4.0 %collective-permute-start.1 = (bf16[8,1664]{1,0:T(8,128)(2,1)S(1)}, bf16[8,1664]{1,0:T(8,128)(2,1)S(1)}, u32[]{:S(2)}, u32[]{:S(2)}) collective-permute-start(bf16[8,1664]{1,0:T(8,128)(2,1)S(1)} %get-tuple-element.49), channel_id=1, source_target_pairs={{2,4},{6,8},{10,12},{14,16},{18,20},{22,24},{26,28},{30,32},{34,36... | collective-permute-start | bytes 79880 | tf_op jit(solution)/shard_map/ppermute | solution.py:739
  5.6 8.5 %copy-start.3 = (f32[1536]{0:T(1024)S(1)}, f32[1536]{0:T(1024)}, u32[]{:S(2)}) copy-start(f32[1536]{0:T(1024)} %param.12) | copy-start | bytes 18436
  10.8 12.0 %collective-permute-start.2 = (bf16[272,768]{1,0:T(8,128)(2,1)S(1)}, bf16[272,768]{1,0:T(8,128)(2,1)S(1)}, u32[]{:S(2)}, u32[]{:S(2)}) collective-permute-start(bf16[272,768]{1,0:T(8,128)(2,1)S(1)} %get-tuple-element.54.mine.encoded), channel_id=1, source_target_pairs={{0,1},{1,0},{2,3},{3,2},{4,5},{5,4},{6,7},{7,6},{8,9},{9,8},{10,11... | collective-permute-start | bytes 1253384 | tf_op jit(solution)/shard_map/ppermute | solution.py:714
  24.3 38.0 %copy-start.2 = (f32[4]{0:T(128)S(1)}, f32[4]{0:T(128)}, u32[]{:S(2)}) copy-start(f32[4]{0:T(128)} %param.14) | copy-start | bytes 52
  24.3 10.8 %collective-permute-start.3 = (bf16[128,384]{1,0:T(8,128)(2,1)S(1)}, bf16[128,384]{1,0:T(8,128)(2,1)S(1)}, u32[]{:S(2)}, u32[]{:S(2)}) collective-permute-start(bf16[128,384]{1,0:T(8,128)(2,1)S(1)} %get-tuple-element.59), channel_id=1, source_target_pairs={{0,32},{2,34},{4,36},{6,38},{8,40},{10,42},{12,44},{14,46},{16,48}... | collective-permute-start | bytes 294920 | tf_op jit(solution)/shard_map/ppermute | solution.py:718
  30.0 5.1 %collective-permute-start.4 = (bf16[128,384]{1,0:T(8,128)(2,1)S(1)}, bf16[128,384]{1,0:T(8,128)(2,1)S(1)}, u32[]{:S(2)}, u32[]{:S(2)}) collective-permute-start(bf16[128,384]{1,0:T(8,128)(2,1)S(1)} %get-tuple-element.60), channel_id=1, source_target_pairs={{0,96},{2,98},{4,100},{6,102},{8,104},{10,106},{12,108},{14,110},{... | collective-permute-start | bytes 294920 | tf_op jit(solution)/shard_map/ppermute | solution.py:718
  31.6 6.1 %collective-permute-start.5 = (bf16[128,384]{1,0:T(8,128)(2,1)S(1)}, bf16[128,384]{1,0:T(8,128)(2,1)S(1)}, u32[]{:S(2)}, u32[]{:S(2)}) collective-permute-start(bf16[128,384]{1,0:T(8,128)(2,1)S(1)} %get-tuple-element.61), channel_id=1, source_target_pairs={{0,64},{2,66},{4,68},{6,70},{8,72},{10,74},{12,76},{14,78},{16,80}... | collective-permute-start | bytes 294920 | tf_op jit(solution)/shard_map/ppermute | solution.py:718
  37.8 12.5 %collective-permute-start.6 = (bf16[512,384]{1,0:T(8,128)(2,1)S(1)}, bf16[512,384]{1,0:T(8,128)(2,1)S(1)}, u32[]{:S(2)}, u32[]{:S(2)}) collective-permute-start(bf16[512,384]{1,0:T(8,128)(2,1)S(1)} %constant_dynamic-update-slice_fusion.refs_0_), channel_id=1, source_target_pairs={{0,8},{2,10},{4,12},{6,14},{8,16},{10,18},{12,20},{14,22},{16,24},... | collective-permute-start | bytes 1179656 | tf_op jit(solution)/shard_map/ppermute | solution.py:718
  39.9 10.4 %collective-permute-start.7 = (bf16[512,384]{1,0:T(8,128)(2,1)S(1)}, bf16[512,384]{1,0:T(8,128)(2,1)S(1)}, u32[]{:S(2)}, u32[]{:S(2)}) collective-permute-start(bf16[512,384]{1,0:T(8,128)(2,1)S(1)} %constant_dynamic-update-slice_fusion.refs_0_), channel_id=1, source_target_pairs={{0,24},{2,26},{4,28},{6,30},{8,0},{10,2},{12,4},{14,6},{16,8},{18,... | collective-permute-start | bytes 1179656 | tf_op jit(solution)/shard_map/ppermute | solution.py:718
  42.9 5.9 %collective-permute-start.10 = (bf16[136,256]{1,0:T(8,128)(2,1)S(1)}, bf16[136,256]{1,0:T(8,128)(2,1)S(1)}, u32[]{:S(2)}, u32[]{:S(2)}) collective-permute-start(bf16[136,256]{1,0:T(8,128)(2,1)S(1)} %get-tuple-element.68), channel_id=1, source_target_pairs={{0,64},{2,66},{4,68},{6,70},{8,72},{10,74},{12,76},{14,78},{16,80}... | collective-permute-start | bytes 208904 | tf_op jit(solution)/shard_map/ppermute | solution.py:718
  44.8 5.5 %collective-permute-start.8 = (bf16[136,256]{1,0:T(8,128)(2,1)S(1)}, bf16[136,256]{1,0:T(8,128)(2,1)S(1)}, u32[]{:S(2)}, u32[]{:S(2)}) collective-permute-start(bf16[136,256]{1,0:T(8,128)(2,1)S(1)} %get-tuple-element.66), channel_id=1, source_target_pairs={{0,32},{2,34},{4,36},{6,38},{8,40},{10,42},{12,44},{14,46},{16,48}... | collective-permute-start | bytes 208904 | tf_op jit(solution)/shard_map/ppermute | solution.py:718
  45.4 4.9 %collective-permute-start.9 = (bf16[136,256]{1,0:T(8,128)(2,1)S(1)}, bf16[136,256]{1,0:T(8,128)(2,1)S(1)}, u32[]{:S(2)}, u32[]{:S(2)}) collective-permute-start(bf16[136,256]{1,0:T(8,128)(2,1)S(1)} %get-tuple-element.67), channel_id=1, source_target_pairs={{0,96},{2,98},{4,100},{6,102},{8,104},{10,106},{12,108},{14,110},{... | collective-permute-start | bytes 208904 | tf_op jit(solution)/shard_map/ppermute | solution.py:718
  48.8 4.8 %collective-permute-start.11 = (bf16[512,384]{1,0:T(8,128)(2,1)S(1)}, bf16[512,384]{1,0:T(8,128)(2,1)S(1)}, u32[]{:S(2)}, u32[]{:S(2)}) collective-permute-start(bf16[512,384]{1,0:T(8,128)(2,1)S(1)} %constant_dynamic-update-slice_fusion.refs_0_), channel_id=1, source_target_pairs={{0,2},{2,0},{4,6},{6,4},{8,10},{10,8},{12,14},{14,12},{16,18},{18,... | collective-permute-start | bytes 1179656 | tf_op jit(solution)/shard_map/ppermute | solution.py:718
  50.3 5.4 %collective-permute-start.12 = (bf16[512,384]{1,0:T(8,128)(2,1)S(1)}, bf16[512,384]{1,0:T(8,128)(2,1)S(1)}, u32[]{:S(2)}, u32[]{:S(2)}) collective-permute-start(bf16[512,384]{1,0:T(8,128)(2,1)S(1)} %collective-permute-done.6.refs_1_), channel_id=1, source_target_pairs={{0,2},{2,0},{4,6},{6,4},{8,10},{10,8},{12,14},{14,12},{16,18},{18,... | collective-permute-start | bytes 1179656 | tf_op jit(solution)/shard_map/ppermute | solution.py:718
  50.4 5.3 %collective-permute-start.13 = (bf16[512,384]{1,0:T(8,128)(2,1)S(1)}, bf16[512,384]{1,0:T(8,128)(2,1)S(1)}, u32[]{:S(2)}, u32[]{:S(2)}) collective-permute-start(bf16[512,384]{1,0:T(8,128)(2,1)S(1)} %collective-permute-done.7.refs_2_), channel_id=1, source_target_pairs={{0,2},{2,0},{4,6},{6,4},{8,10},{10,8},{12,14},{14,12},{16,18},{18,... | collective-permute-start | bytes 1179656 | tf_op jit(solution)/shard_map/ppermute | solution.py:718
  50.9 9.3 %collective-permute-start.16 = (bf16[544,256]{1,0:T(8,128)(2,1)S(1)}, bf16[544,256]{1,0:T(8,128)(2,1)S(1)}, u32[]{:S(2)}, u32[]{:S(2)}) collective-permute-start(bf16[544,256]{1,0:T(8,128)(2,1)S(1)} %constant_dynamic-update-slice_fusion.4.queries), channel_id=1, source_target_pairs={{0,4},{2,6},{4,0},{6,2},{8,12},{10,14},{12,8},{14,10},{16,20},{18,... | collective-permute-start | bytes 835592 | tf_op jit(solution)/shard_map/ppermute | solution.py:718
  52.4 7.9 %collective-permute-start.14 = (bf16[256,384]{1,0:T(8,128)(2,1)S(1)}, bf16[256,384]{1,0:T(8,128)(2,1)S(1)}, u32[]{:S(2)}, u32[]{:S(2)}) collective-permute-start(bf16[256,384]{1,0:T(8,128)(2,1)S(1)} %slice.6), channel_id=1, source_target_pairs={{0,8},{2,10},{4,12},{6,14},{8,16},{10,18},{12,20},{14,22},{16,24},... | collective-permute-start | bytes 589832 | tf_op jit(solution)/shard_map/ppermute | solution.py:718
  53.6 6.7 %collective-permute-start.15 = (bf16[256,384]{1,0:T(8,128)(2,1)S(1)}, bf16[256,384]{1,0:T(8,128)(2,1)S(1)}, u32[]{:S(2)}, u32[]{:S(2)}) collective-permute-start(bf16[256,384]{1,0:T(8,128)(2,1)S(1)} %slice.7), channel_id=1, source_target_pairs={{0,24},{2,26},{4,28},{6,30},{8,0},{10,2},{12,4},{14,6},{16,8},{18,... | collective-permute-start | bytes 589832 | tf_op jit(solution)/shard_map/ppermute | solution.py:718
  60.3 2.0 %collective-permute-start.17 = (bf16[512,384]{1,0:T(8,128)(2,1)S(1)}, bf16[512,384]{1,0:T(8,128)(2,1)S(1)}, u32[]{:S(2)}, u32[]{:S(2)}) collective-permute-start(bf16[512,384]{1,0:T(8,128)(2,1)S(1)} %constant_dynamic-update-slice_fusion.8.refs_6_), channel_id=1, source_target_pairs={{0,2},{2,0},{4,6},{6,4},{8,10},{10,8},{12,14},{14,12},{16,18},{18,... | collective-permute-start | bytes 1179656 | tf_op jit(solution)/shard_map/ppermute | solution.py:718
  62.3 22.8 %copy-start = (bf16[768,1536]{1,0:T(8,128)(2,1)S(1)}, bf16[768,1536]{1,0:T(8,128)(2,1)}, u32[]{:S(2)}) copy-start(bf16[768,1536]{1,0:T(8,128)(2,1)} %weight.6) | copy-start | bytes 7077892
  66.6 8.8 %collective-permute-start.18 = (bf16[544,256]{1,0:T(8,128)(2,1)S(1)}, bf16[544,256]{1,0:T(8,128)(2,1)S(1)}, u32[]{:S(2)}, u32[]{:S(2)}) collective-permute-start(bf16[544,256]{1,0:T(8,128)(2,1)S(1)} %get-tuple-element.79), channel_id=1, source_target_pairs={{0,4},{2,6},{4,0},{6,2},{8,12},{10,14},{12,8},{14,10},{16,20},{18,... | collective-permute-start | bytes 835592 | tf_op jit(solution)/shard_map/ppermute | solution.py:718
  67.5 25.5 %slice-start = ((s8[7077888]{0:T(1024)(128)(4,1)}), s8[4194304]{0:T(1024)(128)(4,1)S(1)}, s32[]{:S(2)}) async-start(s8[7077888]{0:T(1024)(128)(4,1)} %bitcast.2), calls=%async_computation | async-start | bytes 8388608
  67.5 25.5 %slice-start.1 = ((s8[7077888]{0:T(1024)(128)(4,1)}), s8[2883584]{0:T(1024)(128)(4,1)S(1)}, s32[]{:S(2)}) async-start(s8[7077888]{0:T(1024)(128)(4,1)} %bitcast.2), calls=%async_computation.1 | async-start | bytes 5767168
  76.0 5.2 %collective-permute-start.19 = (bf16[136,256]{1,0:T(8,128)(2,1)S(1)}, bf16[136,256]{1,0:T(8,128)(2,1)S(1)}, u32[]{:S(2)}, u32[]{:S(2)}) collective-permute-start(bf16[136,256]{1,0:T(8,128)(2,1)S(1)} %get-tuple-element.81), channel_id=1, source_target_pairs={{0,96},{2,98},{4,100},{6,102},{8,104},{10,106},{12,108},{14,110},{... | collective-permute-start | bytes 208904 | tf_op jit(solution)/shard_map/ppermute | solution.py:718
  78.6 5.9 %collective-permute-start.20 = (bf16[136,256]{1,0:T(8,128)(2,1)S(1)}, bf16[136,256]{1,0:T(8,128)(2,1)S(1)}, u32[]{:S(2)}, u32[]{:S(2)}) collective-permute-start(bf16[136,256]{1,0:T(8,128)(2,1)S(1)} %get-tuple-element.82), channel_id=1, source_target_pairs={{0,64},{2,66},{4,68},{6,70},{8,72},{10,74},{12,76},{14,78},{16,80}... | collective-permute-start | bytes 208904 | tf_op jit(solution)/shard_map/ppermute | solution.py:718
  79.0 6.1 %collective-permute-start.21 = (bf16[136,256]{1,0:T(8,128)(2,1)S(1)}, bf16[136,256]{1,0:T(8,128)(2,1)S(1)}, u32[]{:S(2)}, u32[]{:S(2)}) collective-permute-start(bf16[136,256]{1,0:T(8,128)(2,1)S(1)} %get-tuple-element.83), channel_id=1, source_target_pairs={{0,32},{2,34},{4,36},{6,38},{8,40},{10,42},{12,44},{14,46},{16,48}... | collective-permute-start | bytes 208904 | tf_op jit(solution)/shard_map/ppermute | solution.py:718
  85.6 7.4 %collective-permute-start.22 = (bf16[136,768]{1,0:T(8,128)(2,1)S(1)}, bf16[136,768]{1,0:T(8,128)(2,1)S(1)}, u32[]{:S(2)}, u32[]{:S(2)}) collective-permute-start(bf16[136,768]{1,0:T(8,128)(2,1)S(1)} %output.3), channel_id=1, source_target_pairs={{0,1},{1,0},{2,3},{3,2},{4,5},{5,4},{6,7},{7,6},{8,9},{9,8},{10,11... | collective-permute-start | bytes 626696 | tf_op jit(solution)/shard_map/ppermute | solution.py:714
  93.9 9.7 %collective-permute-start.24 = (bf16[272,512]{1,0:T(8,128)(2,1)S(1)}, bf16[272,512]{1,0:T(8,128)(2,1)S(1)}, u32[]{:S(2)}, u32[]{:S(2)}) collective-permute-start(bf16[272,512]{1,0:T(8,128)(2,1)S(1)} %get-tuple-element.87), channel_id=1, source_target_pairs={{0,1},{1,0},{2,3},{3,2},{4,5},{5,4},{6,7},{7,6},{8,9},{9,8},{10,11... | collective-permute-start | bytes 835592 | tf_op jit(solution)/shard_map/ppermute | solution.py:714
  97.4 6.2 %copy-start.1 = (bf16[256,1536]{1,0:T(8,128)(2,1)S(1)}, bf16[256,1536]{1,0:T(8,128)(2,1)}, u32[]{:S(2)}) copy-start(bf16[256,1536]{1,0:T(8,128)(2,1)} %grad.5) | copy-start | bytes 2359300
  98.5 8.4 %collective-permute-start.23 = (bf16[272,256]{1,0:T(8,128)(2,1)}, bf16[272,256]{1,0:T(8,128)(2,1)}, u32[]{:S(2)}, u32[]{:S(2)}) collective-permute-start(bf16[272,256]{1,0:T(8,128)(2,1)} %decode.2), channel_id=1, source_target_pairs={{0,1},{1,0},{2,3},{3,2},{4,5},{5,4},{6,7},{7,6},{8,9},{9,8},{10,11... | collective-permute-start | bytes 417800 | tf_op jit(solution)/shard_map/ppermute | solution.py:714
  105.0 8.4 %collective-permute-start.26 = (bf16[272,512]{1,0:T(8,128)(2,1)}, bf16[272,512]{1,0:T(8,128)(2,1)}, u32[]{:S(2)}, u32[]{:S(2)}) collective-permute-start(bf16[272,512]{1,0:T(8,128)(2,1)} %get-tuple-element.91.refs_0_), channel_id=1, source_target_pairs={{0,1},{1,0},{2,3},{3,2},{4,5},{5,4},{6,7},{7,6},{8,9},{9,8},{10,11... | collective-permute-start | bytes 835592 | tf_op jit(solution)/shard_map/ppermute | solution.py:714
  108.9 6.9 %collective-permute-start.25 = (bf16[272,256]{1,0:T(8,128)(2,1)}, bf16[272,256]{1,0:T(8,128)(2,1)}, u32[]{:S(2)}, u32[]{:S(2)}) collective-permute-start(bf16[272,256]{1,0:T(8,128)(2,1)} %get-tuple-element.90.refs_1_), channel_id=1, source_target_pairs={{0,1},{1,0},{2,3},{3,2},{4,5},{5,4},{6,7},{7,6},{8,9},{9,8},{10,11... | collective-permute-start | bytes 417800 | tf_op jit(solution)/shard_map/ppermute | solution.py:714

commit v14 on v13

--- a/solution.py
+++ b/solution.py
@@ -189,10 +189,8 @@
     )
 
 
-def encode_kernel(near, far, rows, stem, weight, ahead, encoded, loaded, embedded, halo, sem):
+def encode_kernel(near, far, rows, stem, weight, encoded, embedded, halo):
     ids = position()
-    copy = pltpu.make_async_copy(ahead, loaded, sem)
-    copy.start()
     feats = stem.shape[1]
     half = weight.shape[2]
     place = lax.broadcasted_iota(jnp.int32, (ROWS - OWN, 128), 0)
@@ -215,33 +213,43 @@
         encoded[:, at] = (mine + 0.5 * pre * (1.0 + gelu_tanh(pre))).astype(BF16)
 
     tiles(half // TILE, convolve)
-    copy.wait()
-
-
-def encode(near, far, rows, stem, weight, ahead):
+
+
+def encode(near, far, rows, stem, weight):
     half = weight.shape[2]
     feats = stem.shape[1]
     return pl.pallas_call(
         encode_kernel,
-        in_specs=[VM] * 5 + [HBM],
-        out_specs=[VM, VM],
-        out_shape=[shape((2 * ROWS, half), BF16), pltpu.VMEM(ahead.shape, BF16)],
+        in_specs=[VM] * 5,
+        out_specs=VM,
+        out_shape=shape((2 * ROWS, half), BF16),
         scratch_shapes=[
             pltpu.VMEM((2 * ROWS, feats), BF16),
             pltpu.VMEM((2 * (ROWS - OWN), feats), BF16),
-            pltpu.SemaphoreType.DMA(()),
         ],
         compiler_params=params(12),
         cost_estimate=cost(4 * OWN * weight.size, weight.size * 4),
         name="encode",
-    )(
-        near,
-        far,
-        near_memory(rows),
-        near_memory(stem),
-        near_memory(weight),
-        far_memory(ahead),
-    )
+    )(near, far, near_memory(rows), near_memory(stem), near_memory(weight))
+
+
+def fetch_kernel(source, target, sem):
+    copy = pltpu.make_async_copy(source, target, sem)
+    copy.start()
+    copy.wait()
+
+
+def fetch(value):
+    return pl.pallas_call(
+        fetch_kernel,
+        in_specs=[HBM],
+        out_specs=VM,
+        out_shape=pltpu.VMEM(value.shape, value.dtype),
+        scratch_shapes=[pltpu.SemaphoreType.DMA(())],
+        compiler_params=params(2),
+        cost_estimate=cost(10**5, value.size * 2),
+        name="fetch",
+    )(far_memory(value))
 
 
 def unpacked(both):
@@ -294,7 +302,7 @@
         compiler_params=params(12),
         cost_estimate=cost(2 * ROWS * weight.size * 2 // 3, weight.size * 2),
         name="project_keys",
-    )(mine, theirs, gain, weight)
+    )(mine, theirs, gain, near_memory(weight))
 
 
 def project_queries_kernel(normed, weight, q0, q1, q2, q3, packed):
@@ -739,9 +747,9 @@
     far = lax.ppermute(far, "seq", pairs + [(b, a) for a, b in pairs])
     halo = near, far
     rows, stem_weight, encoder_weight = load(codes, stem_weight, encoder_weight)
-    encoded, attention_weight = encode(
-        *halo, rows, stem_weight, encoder_weight, attention_weight
-    )
+    encoded = encode(*halo, rows, stem_weight, encoder_weight)
+    encoded, attention_weight = lax.optimization_barrier((encoded, attention_weight))
+    attention_weight = fetch(attention_weight)
     gain = norm_gain.reshape(1, feats)
     normed, *keyvals = project_keys(encoded, swap(encoded), gain, attention_weight)
 

time: 118 us -> 118 us (level)
  waiting for transfers between devices: 38.6 us -> 42.8 us
  starting transfers between devices: 43.4 us -> 39.8 us
  Pallas kernels: 34.8 us -> 33.5 us
    ppermute x20, starting transfers between devices: 28.8 us -> 25.2 us  [send(): return lax.ppermute(value, 'seq', moves(**step))]
    ppermute x20, waiting for transfers between devices: 21.3 us -> 23.9 us  [send(): return lax.ppermute(value, 'seq', moves(**step))]
    ppermute x6, waiting for transfers between devices: 17.3 us -> 18.9 us  [swap(): return lax.ppermute(value, 'head', [(0, 1), (1, 0)])]
    pallas_call x1 -> x2, Pallas kernels: 5.16 us -> 5.56 us  [the longest x1 3.02 us: fetch(): pl.pallas_call(fetch_kernel, in_specs=[HBM], out_specs=VM, out_shape=pltp...]
where the time goes in v14:
time: 118 us; the launch traced here: 117 us
  waiting for transfers between devices  42.8 us (36%)
  starting transfers between devices  39.8 us (34%)
  Pallas kernels  33.5 us (28%)
    ppermute x20, starting transfers between devices, send(): return lax.ppermute(value, 'seq', moves(**step))  25.2 us
    ppermute x20, waiting for transfers between devices, send(): return lax.ppermute(value, 'seq', moves(**step))  23.9 us
    ppermute x6, waiting for transfers between devices, swap(): return lax.ppermute(value, 'head', [(0, 1), (1, 0)])  18.9 us
    ppermute x6, starting transfers between devices, swap(): return lax.ppermute(value, 'head', [(0, 1), (1, 0)])  13.9 us
    pallas_call x2, Pallas kernels, attend(): pl.pallas_call(functools.partial(attend_kernel, len(pieces), len(inverses...  8.36 us
    pallas_call x3, Pallas kernels, backward(): pl.pallas_call(functools.partial(backward_kernel, mine, [first for first,...  5.09 us
    pallas_call x1, Pallas kernels, load(): pl.pallas_call(load_kernel, in_specs=[VM, HBM, HBM], out_specs=[VM] * 3,...  3.29 us
    pallas_call x1, Pallas kernels, fetch(): pl.pallas_call(fetch_kernel, in_specs=[HBM], out_specs=VM, out_shape=pltp...  3.02 us
  transfers between devices with their start and end apart: 27, of which 16 were waited for; matrix products, arithmetic and copies ran while one was open for 0% of the time, Pallas kernels for 16%

profile of v14, /device:TPU:0, one launch (start us, length us, event | category | flops | bytes accessed | tf_op | source)
XLA Modules:
  0.0 117.3 jit_solution(16891954179259401100)
XLA Ops:
  0.6 0.9 prepare.1
  1.5 0.1 collective-permute-start
  1.6 0.7 collective-permute-start.1
  2.3 0.0 copy-start.3
  2.3 3.3 %load.1 = (bf16[256,1536]{1,0:T(8,128)(2,1)S(1)}, bf16[256,1536]{1,0:T(8,128)(2,1)S(1)}, bf16[3,1536,768]{2,1,0:T(8,128)(2,1)S(1)}) custom-call(bf16[128,128]{1,0:T(8,128)(2,1)S(1)} %get-tuple-element.50.codes, bf16[256,1536]{1,0:T(8,128)(2,1)} %stems.1, bf16[3,1536,768]{2,1,0:T(8,128)(2,1)} %weights.1), custom_call_target="tpu_custom_call" | custom-call | flops 100000 | bytes 7077888 | tf_op jit(solution)/shard_map/load/pallas_call | solution.py:168
  5.6 0.0 collective-permute-done.near
  5.6 2.5 %encode.1.mine.encoded = bf16[272,768]{1,0:T(8,128)(2,1)S(1)} custom-call(bf16[8,1664]{1,0:T(8,128)(2,1)S(1)} %collective-permute-done.near, bf16[8,1664]{1,0:T(8,128)(2,1)S(1)} %collective-permute-done.1.far, bf16[256,1536]{1,0:T(8,128)(2,1)S(1)} %get-tuple-element.51.rows, bf16[256,1536]{1,0:T(8,128)(2,1)S(1)} %get-tuple-element.52.stem, ...), custom_call_target="tpu_custom_call" | custom-call | flops 1811939328 | bytes 14155776 | tf_op jit(solution)/shard_map/encode/pallas_call | solution.py:221
  8.2 3.4 %collective-permute-start.2 = (bf16[272,768]{1,0:T(8,128)(2,1)S(1)}, bf16[272,768]{1,0:T(8,128)(2,1)S(1)}, u32[]{:S(2)}, u32[]{:S(2)}) collective-permute-start(bf16[272,768]{1,0:T(8,128)(2,1)S(1)} %encode.1.mine.encoded), channel_id=1, source_target_pairs={{0,1},{1,0},{2,3},{3,2},{4,5},{5,4},{6,7},{7,6},{8,9},{9,8},{10,11... | collective-permute-start | bytes 1253384 | tf_op jit(solution)/shard_map/ppermute | solution.py:722
  11.5 3.0 %fetch.1.weight = bf16[3,1536,768]{2,1,0:T(8,128)(2,1)S(1)} custom-call(bf16[3,1536,768]{2,1,0:T(8,128)(2,1)} %source), custom_call_target="tpu_custom_call" | custom-call | flops 100000 | bytes 7077888 | tf_op jit(solution)/shard_map/fetch/pallas_call | solution.py:243
  14.6 6.2 %collective-permute-done.2.theirs = bf16[272,768]{1,0:T(8,128)(2,1)S(1)} collective-permute-done((bf16[272,768]{1,0:T(8,128)(2,1)S(1)}, bf16[272,768]{1,0:T(8,128)(2,1)S(1)}, u32[]{:S(2)}, u32[]{:S(2)}) %collective-permute-start.2) | collective-permute-done | bytes 417824 | tf_op jit(solution)/shard_map/ppermute | solution.py:722
  20.7 1.5 %project_keys.1 = (bf16[2,136,768]{2,1,0:T(8,128)(2,1)S(1)}, bf16[128,384]{1,0:T(8,128)(2,1)S(1)}, bf16[128,384]{1,0:T(8,128)(2,1)S(1)}, bf16[128,384]{1,0:T(8,128)(2,1)S(1)}, bf16[128,384]{1,0:T(8,128)(2,1)S(1)}) custom-call(bf16[272,768]{1,0:T(8,128)(2,1)S(1)} %encode.1.mine.encoded, bf16[272,768]{1,0:T(8,128)(2,1)S(1)} %collective-permute-done.2.theirs, ...), custom_call_target="tpu_custom_call" | custom-call | flops 641728512 | bytes 7077888 | tf_op jit(solution)/shard_map/project_keys/pallas_call | solution.py:296
  22.2 0.0 copy-start.2
  22.2 5.2 %collective-permute-start.3 = (bf16[128,384]{1,0:T(8,128)(2,1)S(1)}, bf16[128,384]{1,0:T(8,128)(2,1)S(1)}, u32[]{:S(2)}, u32[]{:S(2)}) collective-permute-start(bf16[128,384]{1,0:T(8,128)(2,1)S(1)} %get-tuple-element.59), channel_id=1, source_target_pairs={{0,32},{2,34},{4,36},{6,38},{8,40},{10,42},{12,44},{14,46},{16,48}... | collective-permute-start | bytes 294920 | tf_op jit(solution)/shard_map/ppermute | solution.py:726
  27.4 1.6 %collective-permute-start.4 = (bf16[128,384]{1,0:T(8,128)(2,1)S(1)}, bf16[128,384]{1,0:T(8,128)(2,1)S(1)}, u32[]{:S(2)}, u32[]{:S(2)}) collective-permute-start(bf16[128,384]{1,0:T(8,128)(2,1)S(1)} %get-tuple-element.60), channel_id=1, source_target_pairs={{0,96},{2,98},{4,100},{6,102},{8,104},{10,106},{12,108},{14,110},{... | collective-permute-start | bytes 294920 | tf_op jit(solution)/shard_map/ppermute | solution.py:726
  29.0 2.0 %collective-permute-start.5 = (bf16[128,384]{1,0:T(8,128)(2,1)S(1)}, bf16[128,384]{1,0:T(8,128)(2,1)S(1)}, u32[]{:S(2)}, u32[]{:S(2)}) collective-permute-start(bf16[128,384]{1,0:T(8,128)(2,1)S(1)} %get-tuple-element.61), channel_id=1, source_target_pairs={{0,64},{2,66},{4,68},{6,70},{8,72},{10,74},{12,76},{14,78},{16,80}... | collective-permute-start | bytes 294920 | tf_op jit(solution)/shard_map/ppermute | solution.py:726
  31.0 1.6 %collective-permute-done.3 = bf16[128,384]{1,0:T(8,128)(2,1)S(1)} collective-permute-done((bf16[128,384]{1,0:T(8,128)(2,1)S(1)}, bf16[128,384]{1,0:T(8,128)(2,1)S(1)}, u32[]{:S(2)}, u32[]{:S(2)}) %collective-permute-start.3) | collective-permute-done | bytes 98336 | tf_op jit(solution)/shard_map/ppermute | solution.py:726
  32.5 2.6 %collective-permute-done.5 = bf16[128,384]{1,0:T(8,128)(2,1)S(1)} collective-permute-done((bf16[128,384]{1,0:T(8,128)(2,1)S(1)}, bf16[128,384]{1,0:T(8,128)(2,1)S(1)}, u32[]{:S(2)}, u32[]{:S(2)}) %collective-permute-start.5) | collective-permute-done | bytes 98336 | tf_op jit(solution)/shard_map/ppermute | solution.py:726
  35.2 2.2 %collective-permute-start.6 = (bf16[512,384]{1,0:T(8,128)(2,1)S(1)}, bf16[512,384]{1,0:T(8,128)(2,1)S(1)}, u32[]{:S(2)}, u32[]{:S(2)}) collective-permute-start(bf16[512,384]{1,0:T(8,128)(2,1)S(1)} %constant_dynamic-update-slice_fusion.refs_0_), channel_id=1, source_target_pairs={{0,8},{2,10},{4,12},{6,14},{8,16},{10,18},{12,20},{14,22},{16,24},... | collective-permute-start | bytes 1179656 | tf_op jit(solution)/shard_map/ppermute | solution.py:726
  37.3 2.2 %collective-permute-start.7 = (bf16[512,384]{1,0:T(8,128)(2,1)S(1)}, bf16[512,384]{1,0:T(8,128)(2,1)S(1)}, u32[]{:S(2)}, u32[]{:S(2)}) collective-permute-start(bf16[512,384]{1,0:T(8,128)(2,1)S(1)} %constant_dynamic-update-slice_fusion.refs_0_), channel_id=1, source_target_pairs={{0,24},{2,26},{4,28},{6,30},{8,0},{10,2},{12,4},{14,6},{16,8},{18,... | collective-permute-start | bytes 1179656 | tf_op jit(solution)/shard_map/ppermute | solution.py:726
  39.5 0.7 project_queries.1
  40.3 0.4 collective-permute-start.8
  40.6 3.0 %collective-permute-start.9 = (bf16[136,256]{1,0:T(8,128)(2,1)S(1)}, bf16[136,256]{1,0:T(8,128)(2,1)S(1)}, u32[]{:S(2)}, u32[]{:S(2)}) collective-permute-start(bf16[136,256]{1,0:T(8,128)(2,1)S(1)} %get-tuple-element.67), channel_id=1, source_target_pairs={{0,96},{2,98},{4,100},{6,102},{8,104},{10,106},{12,108},{14,110},{... | collective-permute-start | bytes 208904 | tf_op jit(solution)/shard_map/ppermute | solution.py:726
  43.6 0.6 collective-permute-start.10
  44.2 2.4 %collective-permute-done.8 = bf16[136,256]{1,0:T(8,128)(2,1)S(1)} collective-permute-done((bf16[136,256]{1,0:T(8,128)(2,1)S(1)}, bf16[136,256]{1,0:T(8,128)(2,1)S(1)}, u32[]{:S(2)}, u32[]{:S(2)}) %collective-permute-start.8) | collective-permute-done | bytes 69664 | tf_op jit(solution)/shard_map/ppermute | solution.py:726
  46.6 2.8 %collective-permute-done.10 = bf16[136,256]{1,0:T(8,128)(2,1)S(1)} collective-permute-done((bf16[136,256]{1,0:T(8,128)(2,1)S(1)}, bf16[136,256]{1,0:T(8,128)(2,1)S(1)}, u32[]{:S(2)}, u32[]{:S(2)}) %collective-permute-start.10) | collective-permute-done | bytes 69664 | tf_op jit(solution)/shard_map/ppermute | solution.py:726
  49.4 0.5 collective-permute-start.13
  49.9 0.3 collective-permute-start.16
  50.3 0.8 collective-permute-start.14
  51.1 2.5 %collective-permute-start.15 = (bf16[256,384]{1,0:T(8,128)(2,1)S(1)}, bf16[256,384]{1,0:T(8,128)(2,1)S(1)}, u32[]{:S(2)}, u32[]{:S(2)}) collective-permute-start(bf16[256,384]{1,0:T(8,128)(2,1)S(1)} %slice.7), channel_id=1, source_target_pairs={{0,24},{2,26},{4,28},{6,30},{8,0},{10,2},{12,4},{14,6},{16,8},{18,... | collective-permute-start | bytes 589832 | tf_op jit(solution)/shard_map/ppermute | solution.py:726
  53.6 0.9 norms.1.refs_8_
  54.6 3.7 %collective-permute-done.14 = bf16[256,384]{1,0:T(8,128)(2,1)S(1)} collective-permute-done((bf16[256,384]{1,0:T(8,128)(2,1)S(1)}, bf16[256,384]{1,0:T(8,128)(2,1)S(1)}, u32[]{:S(2)}, u32[]{:S(2)}) %collective-permute-start.14) | collective-permute-done | bytes 196640 | tf_op jit(solution)/shard_map/ppermute | solution.py:726
  58.3 0.4 collective-permute-done.16.queries
  58.7 0.3 collective-permute-start.17
  59.0 1.7 %collective-permute-done.17.refs_7_ = bf16[512,384]{1,0:T(8,128)(2,1)S(1)} collective-permute-done((bf16[512,384]{1,0:T(8,128)(2,1)S(1)}, bf16[512,384]{1,0:T(8,128)(2,1)S(1)}, u32[]{:S(2)}, u32[]{:S(2)}) %collective-permute-start.17) | collective-permute-done | bytes 393248 | tf_op jit(solution)/shard_map/ppermute | solution.py:726
  60.7 4.3 %attend.2 = (bf16[544,256]{1,0:T(8,128)(2,1)S(1)}, f32[8,1024]{1,0:T(8,128)S(1)}) custom-call(f32[1,4]{1,0:T(1,128)S(1)} %bitcast.4, bf16[544,256]{1,0:T(8,128)(2,1)S(1)} %collective-permute-done.16.queries, bf16[512,384]{1,0:T(8,128)(2,1)S(1)} %constant_dynamic-update-slice_fusion.refs_0_, bf16[512,384]{1,0:T(8,128)(2,1)S(1)} %collective-permute-done.6.refs_1_, ...), custom_call_target="tpu_custom_call" | custom-call | flops 2281701376 | bytes 4456448 | tf_op jit(solution)/shard_map/attend/pallas_call | solution.py:473
  65.0 1.4 %collective-permute-start.18 = (bf16[544,256]{1,0:T(8,128)(2,1)S(1)}, bf16[544,256]{1,0:T(8,128)(2,1)S(1)}, u32[]{:S(2)}, u32[]{:S(2)}) collective-permute-start(bf16[544,256]{1,0:T(8,128)(2,1)S(1)} %get-tuple-element.79), channel_id=1, source_target_pairs={{0,4},{2,6},{4,0},{6,2},{8,12},{10,14},{12,8},{14,10},{16,20},{18,... | collective-permute-start | bytes 835592 | tf_op jit(solution)/shard_map/ppermute | solution.py:726
  66.5 4.0 %attend.3.a0 = bf16[544,256]{1,0:T(8,128)(2,1)S(1)} custom-call(f32[1,4]{1,0:T(1,128)S(1)} %bitcast.5, bf16[544,256]{1,0:T(8,128)(2,1)S(1)} %constant_dynamic-update-slice_fusion.4.queries, bf16[512,384]{1,0:T(8,128)(2,1)S(1)} %constant_dynamic-update-slice_fusion.refs_0_, bf16[512,384]{1,0:T(8,128)(2,1)S(1)} %collective-permute-done.6.refs_1_, ...), custom_call_target="tpu_custom_call" | custom-call | flops 2281701376 | bytes 4456448 | tf_op jit(solution)/shard_map/attend/pallas_call | solution.py:473
  70.5 3.3 %collective-permute-done.18.a1 = bf16[544,256]{1,0:T(8,128)(2,1)S(1)} collective-permute-done((bf16[544,256]{1,0:T(8,128)(2,1)S(1)}, bf16[544,256]{1,0:T(8,128)(2,1)S(1)}, u32[]{:S(2)}, u32[]{:S(2)}) %collective-permute-start.18) | collective-permute-done | bytes 278560 | tf_op jit(solution)/shard_map/ppermute | solution.py:726
  73.8 0.5 merge.1
  74.4 0.9 collective-permute-start.19
  75.2 1.2 %collective-permute-start.20 = (bf16[136,256]{1,0:T(8,128)(2,1)S(1)}, bf16[136,256]{1,0:T(8,128)(2,1)S(1)}, u32[]{:S(2)}, u32[]{:S(2)}) collective-permute-start(bf16[136,256]{1,0:T(8,128)(2,1)S(1)} %get-tuple-element.82), channel_id=1, source_target_pairs={{0,64},{2,66},{4,68},{6,70},{8,72},{10,74},{12,76},{14,78},{16,80}... | collective-permute-start | bytes 208904 | tf_op jit(solution)/shard_map/ppermute | solution.py:726
  76.4 0.2 collective-permute-start.21
  76.7 2.1 %collective-permute-done.19.a1 = bf16[136,256]{1,0:T(8,128)(2,1)S(1)} collective-permute-done((bf16[136,256]{1,0:T(8,128)(2,1)S(1)}, bf16[136,256]{1,0:T(8,128)(2,1)S(1)}, u32[]{:S(2)}, u32[]{:S(2)}) %collective-permute-start.19) | collective-permute-done | bytes 69664 | tf_op jit(solution)/shard_map/ppermute | solution.py:726
  78.7 2.7 %collective-permute-done.20.a2 = bf16[136,256]{1,0:T(8,128)(2,1)S(1)} collective-permute-done((bf16[136,256]{1,0:T(8,128)(2,1)S(1)}, bf16[136,256]{1,0:T(8,128)(2,1)S(1)}, u32[]{:S(2)}, u32[]{:S(2)}) %collective-permute-start.20) | collective-permute-done | bytes 69664 | tf_op jit(solution)/shard_map/ppermute | solution.py:726
  81.4 0.7 collective-permute-done.21.a3
  82.1 0.4 output.3
  82.5 3.2 %collective-permute-start.22 = (bf16[136,768]{1,0:T(8,128)(2,1)S(1)}, bf16[136,768]{1,0:T(8,128)(2,1)S(1)}, u32[]{:S(2)}, u32[]{:S(2)}) collective-permute-start(bf16[136,768]{1,0:T(8,128)(2,1)S(1)} %output.3), channel_id=1, source_target_pairs={{0,1},{1,0},{2,3},{3,2},{4,5},{5,4},{6,7},{7,6},{8,9},{9,8},{10,11... | collective-permute-start | bytes 626696 | tf_op jit(solution)/shard_map/ppermute | solution.py:722
  85.7 0.4 output.2.own
  86.1 3.8 %collective-permute-done.22.other = bf16[136,768]{1,0:T(8,128)(2,1)S(1)} collective-permute-done((bf16[136,768]{1,0:T(8,128)(2,1)S(1)}, bf16[136,768]{1,0:T(8,128)(2,1)S(1)}, u32[]{:S(2)}, u32[]{:S(2)}) %collective-permute-start.22) | collective-permute-done | bytes 208928 | tf_op jit(solution)/shard_map/ppermute | solution.py:722
  89.9 0.9 decode_first.1
  90.8 3.4 %collective-permute-start.24 = (bf16[272,512]{1,0:T(8,128)(2,1)S(1)}, bf16[272,512]{1,0:T(8,128)(2,1)S(1)}, u32[]{:S(2)}, u32[]{:S(2)}) collective-permute-start(bf16[272,512]{1,0:T(8,128)(2,1)S(1)} %get-tuple-element.87), channel_id=1, source_target_pairs={{0,1},{1,0},{2,3},{3,2},{4,5},{5,4},{6,7},{7,6},{8,9},{9,8},{10,11... | collective-permute-start | bytes 835592 | tf_op jit(solution)/shard_map/ppermute | solution.py:722
  94.3 1.2 decode.2
  95.4 0.4 collective-permute-start.23
  95.8 1.2 decode.3.own
  97.0 3.5 %collective-permute-done.24.other = bf16[272,512]{1,0:T(8,128)(2,1)S(1)} collective-permute-done((bf16[272,512]{1,0:T(8,128)(2,1)S(1)}, bf16[272,512]{1,0:T(8,128)(2,1)S(1)}, u32[]{:S(2)}, u32[]{:S(2)}) %collective-permute-start.24) | collective-permute-done | bytes 278560 | tf_op jit(solution)/shard_map/ppermute | solution.py:722
  100.6 0.6 slopes.2
  101.2 1.1 collective-permute-done.23.other
  102.3 2.0 %slopes.3 = (bf16[256,768]{1,0:T(8,128)(2,1)}, bf16[272,256]{1,0:T(8,128)(2,1)}, f32[128,256]{1,0:T(8,128)S(1)}) custom-call(f32[272,768]{1,0:T(8,128)S(1)} %decode.3.own, bf16[272,256]{1,0:T(8,128)(2,1)} %collective-permute-done.23.other, bf16[272,768]{1,0:T(8,128)(2,1)S(1)} %get-tuple-element.85.inputs, bf16[256,1536]{1,0:T(8,128)(2,1)S(1)} %copy-done.1, ...), custom_call_target="tpu_custom_call" | custom-call | flops 208896000000 | bytes 974848 | tf_op jit(solution)/shard_map/slopes/pallas_call | solution.py:639
  104.3 1.7 %collective-permute-start.25 = (bf16[272,256]{1,0:T(8,128)(2,1)}, bf16[272,256]{1,0:T(8,128)(2,1)}, u32[]{:S(2)}, u32[]{:S(2)}) collective-permute-start(bf16[272,256]{1,0:T(8,128)(2,1)} %get-tuple-element.90.refs_1_), channel_id=1, source_target_pairs={{0,1},{1,0},{2,3},{3,2},{4,5},{5,4},{6,7},{7,6},{8,9},{9,8},{10,11... | collective-permute-start | bytes 417800 | tf_op jit(solution)/shard_map/ppermute | solution.py:722
  106.0 1.8 %collective-permute-start.26 = (bf16[272,512]{1,0:T(8,128)(2,1)S(1)}, bf16[272,512]{1,0:T(8,128)(2,1)S(1)}, u32[]{:S(2)}, u32[]{:S(2)}) collective-permute-start(bf16[272,512]{1,0:T(8,128)(2,1)S(1)} %get-tuple-element.91.refs_0_), channel_id=1, source_target_pairs={{0,1},{1,0},{2,3},{3,2},{4,5},{5,4},{6,7},{7,6},{8,9},{9,8},{10,11... | collective-permute-start | bytes 835592 | tf_op jit(solution)/shard_map/ppermute | solution.py:722
  107.8 2.1 %backward.3.refs_1_ = f32[128,768]{1,0:T(8,128)S(1)} custom-call(bf16[272,512]{1,0:T(8,128)(2,1)S(1)} %get-tuple-element.91.refs_0_, bf16[272,256]{1,0:T(8,128)(2,1)} %get-tuple-element.90.refs_1_, f32[128,512]{1,0:T(8,128)S(1)} %get-tuple-element.92.refs_2_, f32[128,256]{1,0:T(8,128)S(1)} %get-tuple-element.93.refs_3_, bf16[3,768,1536]{2,1,0:T(8,128)(2,1)S(1)} %bitcast.3), custom_call_target="tpu_custom_call" | custom-call | flops 96259276800 | bytes 1253376 | tf_op jit(solution)/shard_map/backward/pallas_call | solution.py:698
  109.9 4.3 %collective-permute-done.26.refs_0_ = bf16[272,512]{1,0:T(8,128)(2,1)S(1)} collective-permute-done((bf16[272,512]{1,0:T(8,128)(2,1)S(1)}, bf16[272,512]{1,0:T(8,128)(2,1)S(1)}, u32[]{:S(2)}, u32[]{:S(2)}) %collective-permute-start.26) | collective-permute-done | bytes 278560 | tf_op jit(solution)/shard_map/ppermute | solution.py:722
  114.3 0.9 backward.4.refs_1_
  115.1 2.1 %backward.5 = bf16[128,768]{1,0:T(8,128)(2,1)} custom-call(bf16[272,256]{1,0:T(8,128)(2,1)} %collective-permute-done.25.refs_0_, f32[128,768]{1,0:T(8,128)S(1)} %backward.4.refs_1_, bf16[3,768,1536]{2,1,0:T(8,128)(2,1)S(1)} %bitcast.3), custom_call_target="tpu_custom_call" | custom-call | flops 32086425600 | bytes 417792 | tf_op jit(solution)/shard_map/backward/pallas_call | solution.py:698
  (36 shorter events, 0.2 us)
Async XLA Ops:
  1.5 4.1 %collective-permute-start = (bf16[8,1664]{1,0:T(8,128)(2,1)S(1)}, bf16[8,1664]{1,0:T(8,128)(2,1)S(1)}, u32[]{:S(2)}, u32[]{:S(2)}) collective-permute-start(bf16[8,1664]{1,0:T(8,128)(2,1)S(1)} %get-tuple-element.48), channel_id=1, source_target_pairs={{0,2},{2,0},{4,6},{6,4},{8,10},{10,8},{12,14},{14,12},{16,18},{18,... | collective-permute-start | bytes 79880 | tf_op jit(solution)/shard_map/ppermute | solution.py:726
  1.6 4.0 %collective-permute-start.1 = (bf16[8,1664]{1,0:T(8,128)(2,1)S(1)}, bf16[8,1664]{1,0:T(8,128)(2,1)S(1)}, u32[]{:S(2)}, u32[]{:S(2)}) collective-permute-start(bf16[8,1664]{1,0:T(8,128)(2,1)S(1)} %get-tuple-element.49), channel_id=1, source_target_pairs={{2,4},{6,8},{10,12},{14,16},{18,20},{22,24},{26,28},{30,32},{34,36... | collective-permute-start | bytes 79880 | tf_op jit(solution)/shard_map/ppermute | solution.py:747
  2.3 9.2 %copy-start.3 = (f32[1536]{0:T(1024)S(1)}, f32[1536]{0:T(1024)}, u32[]{:S(2)}) copy-start(f32[1536]{0:T(1024)} %param.12) | copy-start | bytes 18436
  8.2 12.6 %collective-permute-start.2 = (bf16[272,768]{1,0:T(8,128)(2,1)S(1)}, bf16[272,768]{1,0:T(8,128)(2,1)S(1)}, u32[]{:S(2)}, u32[]{:S(2)}) collective-permute-start(bf16[272,768]{1,0:T(8,128)(2,1)S(1)} %encode.1.mine.encoded), channel_id=1, source_target_pairs={{0,1},{1,0},{2,3},{3,2},{4,5},{5,4},{6,7},{7,6},{8,9},{9,8},{10,11... | collective-permute-start | bytes 1253384 | tf_op jit(solution)/shard_map/ppermute | solution.py:722
  22.2 38.5 %copy-start.2 = (f32[4]{0:T(128)S(1)}, f32[4]{0:T(128)}, u32[]{:S(2)}) copy-start(f32[4]{0:T(128)} %param.14) | copy-start | bytes 52
  22.2 10.3 %collective-permute-start.3 = (bf16[128,384]{1,0:T(8,128)(2,1)S(1)}, bf16[128,384]{1,0:T(8,128)(2,1)S(1)}, u32[]{:S(2)}, u32[]{:S(2)}) collective-permute-start(bf16[128,384]{1,0:T(8,128)(2,1)S(1)} %get-tuple-element.59), channel_id=1, source_target_pairs={{0,32},{2,34},{4,36},{6,38},{8,40},{10,42},{12,44},{14,46},{16,48}... | collective-permute-start | bytes 294920 | tf_op jit(solution)/shard_map/ppermute | solution.py:726
  27.4 5.1 %collective-permute-start.4 = (bf16[128,384]{1,0:T(8,128)(2,1)S(1)}, bf16[128,384]{1,0:T(8,128)(2,1)S(1)}, u32[]{:S(2)}, u32[]{:S(2)}) collective-permute-start(bf16[128,384]{1,0:T(8,128)(2,1)S(1)} %get-tuple-element.60), channel_id=1, source_target_pairs={{0,96},{2,98},{4,100},{6,102},{8,104},{10,106},{12,108},{14,110},{... | collective-permute-start | bytes 294920 | tf_op jit(solution)/shard_map/ppermute | solution.py:726
  29.0 6.1 %collective-permute-start.5 = (bf16[128,384]{1,0:T(8,128)(2,1)S(1)}, bf16[128,384]{1,0:T(8,128)(2,1)S(1)}, u32[]{:S(2)}, u32[]{:S(2)}) collective-permute-start(bf16[128,384]{1,0:T(8,128)(2,1)S(1)} %get-tuple-element.61), channel_id=1, source_target_pairs={{0,64},{2,66},{4,68},{6,70},{8,72},{10,74},{12,76},{14,78},{16,80}... | collective-permute-start | bytes 294920 | tf_op jit(solution)/shard_map/ppermute | solution.py:726
  35.2 14.2 %collective-permute-start.6 = (bf16[512,384]{1,0:T(8,128)(2,1)S(1)}, bf16[512,384]{1,0:T(8,128)(2,1)S(1)}, u32[]{:S(2)}, u32[]{:S(2)}) collective-permute-start(bf16[512,384]{1,0:T(8,128)(2,1)S(1)} %constant_dynamic-update-slice_fusion.refs_0_), channel_id=1, source_target_pairs={{0,8},{2,10},{4,12},{6,14},{8,16},{10,18},{12,20},{14,22},{16,24},... | collective-permute-start | bytes 1179656 | tf_op jit(solution)/shard_map/ppermute | solution.py:726
  37.3 12.1 %collective-permute-start.7 = (bf16[512,384]{1,0:T(8,128)(2,1)S(1)}, bf16[512,384]{1,0:T(8,128)(2,1)S(1)}, u32[]{:S(2)}, u32[]{:S(2)}) collective-permute-start(bf16[512,384]{1,0:T(8,128)(2,1)S(1)} %constant_dynamic-update-slice_fusion.refs_0_), channel_id=1, source_target_pairs={{0,24},{2,26},{4,28},{6,30},{8,0},{10,2},{12,4},{14,6},{16,8},{18,... | collective-permute-start | bytes 1179656 | tf_op jit(solution)/shard_map/ppermute | solution.py:726
  40.3 6.3 %collective-permute-start.8 = (bf16[136,256]{1,0:T(8,128)(2,1)S(1)}, bf16[136,256]{1,0:T(8,128)(2,1)S(1)}, u32[]{:S(2)}, u32[]{:S(2)}) collective-permute-start(bf16[136,256]{1,0:T(8,128)(2,1)S(1)} %get-tuple-element.66), channel_id=1, source_target_pairs={{0,32},{2,34},{4,36},{6,38},{8,40},{10,42},{12,44},{14,46},{16,48}... | collective-permute-start | bytes 208904 | tf_op jit(solution)/shard_map/ppermute | solution.py:726
  40.6 6.0 %collective-permute-start.9 = (bf16[136,256]{1,0:T(8,128)(2,1)S(1)}, bf16[136,256]{1,0:T(8,128)(2,1)S(1)}, u32[]{:S(2)}, u32[]{:S(2)}) collective-permute-start(bf16[136,256]{1,0:T(8,128)(2,1)S(1)} %get-tuple-element.67), channel_id=1, source_target_pairs={{0,96},{2,98},{4,100},{6,102},{8,104},{10,106},{12,108},{14,110},{... | collective-permute-start | bytes 208904 | tf_op jit(solution)/shard_map/ppermute | solution.py:726
  43.6 5.8 %collective-permute-start.10 = (bf16[136,256]{1,0:T(8,128)(2,1)S(1)}, bf16[136,256]{1,0:T(8,128)(2,1)S(1)}, u32[]{:S(2)}, u32[]{:S(2)}) collective-permute-start(bf16[136,256]{1,0:T(8,128)(2,1)S(1)} %get-tuple-element.68), channel_id=1, source_target_pairs={{0,64},{2,66},{4,68},{6,70},{8,72},{10,74},{12,76},{14,78},{16,80}... | collective-permute-start | bytes 208904 | tf_op jit(solution)/shard_map/ppermute | solution.py:726
  46.6 4.5 %collective-permute-start.11 = (bf16[512,384]{1,0:T(8,128)(2,1)S(1)}, bf16[512,384]{1,0:T(8,128)(2,1)S(1)}, u32[]{:S(2)}, u32[]{:S(2)}) collective-permute-start(bf16[512,384]{1,0:T(8,128)(2,1)S(1)} %constant_dynamic-update-slice_fusion.refs_0_), channel_id=1, source_target_pairs={{0,2},{2,0},{4,6},{6,4},{8,10},{10,8},{12,14},{14,12},{16,18},{18,... | collective-permute-start | bytes 1179656 | tf_op jit(solution)/shard_map/ppermute | solution.py:726
  49.4 4.2 %collective-permute-start.12 = (bf16[512,384]{1,0:T(8,128)(2,1)S(1)}, bf16[512,384]{1,0:T(8,128)(2,1)S(1)}, u32[]{:S(2)}, u32[]{:S(2)}) collective-permute-start(bf16[512,384]{1,0:T(8,128)(2,1)S(1)} %collective-permute-done.6.refs_1_), channel_id=1, source_target_pairs={{0,2},{2,0},{4,6},{6,4},{8,10},{10,8},{12,14},{14,12},{16,18},{18,... | collective-permute-start | bytes 1179656 | tf_op jit(solution)/shard_map/ppermute | solution.py:726
  49.4 4.2 %collective-permute-start.13 = (bf16[512,384]{1,0:T(8,128)(2,1)S(1)}, bf16[512,384]{1,0:T(8,128)(2,1)S(1)}, u32[]{:S(2)}, u32[]{:S(2)}) collective-permute-start(bf16[512,384]{1,0:T(8,128)(2,1)S(1)} %collective-permute-done.7.refs_2_), channel_id=1, source_target_pairs={{0,2},{2,0},{4,6},{6,4},{8,10},{10,8},{12,14},{14,12},{16,18},{18,... | collective-permute-start | bytes 1179656 | tf_op jit(solution)/shard_map/ppermute | solution.py:726
  49.9 8.7 %collective-permute-start.16 = (bf16[544,256]{1,0:T(8,128)(2,1)S(1)}, bf16[544,256]{1,0:T(8,128)(2,1)S(1)}, u32[]{:S(2)}, u32[]{:S(2)}) collective-permute-start(bf16[544,256]{1,0:T(8,128)(2,1)S(1)} %constant_dynamic-update-slice_fusion.4.queries), channel_id=1, source_target_pairs={{0,4},{2,6},{4,0},{6,2},{8,12},{10,14},{12,8},{14,10},{16,20},{18,... | collective-permute-start | bytes 835592 | tf_op jit(solution)/shard_map/ppermute | solution.py:726
  50.3 7.9 %collective-permute-start.14 = (bf16[256,384]{1,0:T(8,128)(2,1)S(1)}, bf16[256,384]{1,0:T(8,128)(2,1)S(1)}, u32[]{:S(2)}, u32[]{:S(2)}) collective-permute-start(bf16[256,384]{1,0:T(8,128)(2,1)S(1)} %slice.6), channel_id=1, source_target_pairs={{0,8},{2,10},{4,12},{6,14},{8,16},{10,18},{12,20},{14,22},{16,24},... | collective-permute-start | bytes 589832 | tf_op jit(solution)/shard_map/ppermute | solution.py:726
  51.1 7.1 %collective-permute-start.15 = (bf16[256,384]{1,0:T(8,128)(2,1)S(1)}, bf16[256,384]{1,0:T(8,128)(2,1)S(1)}, u32[]{:S(2)}, u32[]{:S(2)}) collective-permute-start(bf16[256,384]{1,0:T(8,128)(2,1)S(1)} %slice.7), channel_id=1, source_target_pairs={{0,24},{2,26},{4,28},{6,30},{8,0},{10,2},{12,4},{14,6},{16,8},{18,... | collective-permute-start | bytes 589832 | tf_op jit(solution)/shard_map/ppermute | solution.py:726
  58.7 2.0 %collective-permute-start.17 = (bf16[512,384]{1,0:T(8,128)(2,1)S(1)}, bf16[512,384]{1,0:T(8,128)(2,1)S(1)}, u32[]{:S(2)}, u32[]{:S(2)}) collective-permute-start(bf16[512,384]{1,0:T(8,128)(2,1)S(1)} %constant_dynamic-update-slice_fusion.8.refs_6_), channel_id=1, source_target_pairs={{0,2},{2,0},{4,6},{6,4},{8,10},{10,8},{12,14},{14,12},{16,18},{18,... | collective-permute-start | bytes 1179656 | tf_op jit(solution)/shard_map/ppermute | solution.py:726
  60.7 21.4 %copy-start = (bf16[768,1536]{1,0:T(8,128)(2,1)S(1)}, bf16[768,1536]{1,0:T(8,128)(2,1)}, u32[]{:S(2)}) copy-start(bf16[768,1536]{1,0:T(8,128)(2,1)} %weight.6) | copy-start | bytes 7077892
  65.0 8.8 %collective-permute-start.18 = (bf16[544,256]{1,0:T(8,128)(2,1)S(1)}, bf16[544,256]{1,0:T(8,128)(2,1)S(1)}, u32[]{:S(2)}, u32[]{:S(2)}) collective-permute-start(bf16[544,256]{1,0:T(8,128)(2,1)S(1)} %get-tuple-element.79), channel_id=1, source_target_pairs={{0,4},{2,6},{4,0},{6,2},{8,12},{10,14},{12,8},{14,10},{16,20},{18,... | collective-permute-start | bytes 835592 | tf_op jit(solution)/shard_map/ppermute | solution.py:726
  66.5 23.5 %slice-start = ((s8[7077888]{0:T(1024)(128)(4,1)}), s8[4194304]{0:T(1024)(128)(4,1)S(1)}, s32[]{:S(2)}) async-start(s8[7077888]{0:T(1024)(128)(4,1)} %bitcast.2), calls=%async_computation | async-start | bytes 8388608
  66.5 23.5 %slice-start.1 = ((s8[7077888]{0:T(1024)(128)(4,1)}), s8[2883584]{0:T(1024)(128)(4,1)S(1)}, s32[]{:S(2)}) async-start(s8[7077888]{0:T(1024)(128)(4,1)} %bitcast.2), calls=%async_computation.1 | async-start | bytes 5767168
  74.4 4.4 %collective-permute-start.19 = (bf16[136,256]{1,0:T(8,128)(2,1)S(1)}, bf16[136,256]{1,0:T(8,128)(2,1)S(1)}, u32[]{:S(2)}, u32[]{:S(2)}) collective-permute-start(bf16[136,256]{1,0:T(8,128)(2,1)S(1)} %get-tuple-element.81), channel_id=1, source_target_pairs={{0,96},{2,98},{4,100},{6,102},{8,104},{10,106},{12,108},{14,110},{... | collective-permute-start | bytes 208904 | tf_op jit(solution)/shard_map/ppermute | solution.py:726
  75.2 6.2 %collective-permute-start.20 = (bf16[136,256]{1,0:T(8,128)(2,1)S(1)}, bf16[136,256]{1,0:T(8,128)(2,1)S(1)}, u32[]{:S(2)}, u32[]{:S(2)}) collective-permute-start(bf16[136,256]{1,0:T(8,128)(2,1)S(1)} %get-tuple-element.82), channel_id=1, source_target_pairs={{0,64},{2,66},{4,68},{6,70},{8,72},{10,74},{12,76},{14,78},{16,80}... | collective-permute-start | bytes 208904 | tf_op jit(solution)/shard_map/ppermute | solution.py:726
  76.4 5.7 %collective-permute-start.21 = (bf16[136,256]{1,0:T(8,128)(2,1)S(1)}, bf16[136,256]{1,0:T(8,128)(2,1)S(1)}, u32[]{:S(2)}, u32[]{:S(2)}) collective-permute-start(bf16[136,256]{1,0:T(8,128)(2,1)S(1)} %get-tuple-element.83), channel_id=1, source_target_pairs={{0,32},{2,34},{4,36},{6,38},{8,40},{10,42},{12,44},{14,46},{16,48}... | collective-permute-start | bytes 208904 | tf_op jit(solution)/shard_map/ppermute | solution.py:726
  82.5 7.4 %collective-permute-start.22 = (bf16[136,768]{1,0:T(8,128)(2,1)S(1)}, bf16[136,768]{1,0:T(8,128)(2,1)S(1)}, u32[]{:S(2)}, u32[]{:S(2)}) collective-permute-start(bf16[136,768]{1,0:T(8,128)(2,1)S(1)} %output.3), channel_id=1, source_target_pairs={{0,1},{1,0},{2,3},{3,2},{4,5},{5,4},{6,7},{7,6},{8,9},{9,8},{10,11... | collective-permute-start | bytes 626696 | tf_op jit(solution)/shard_map/ppermute | solution.py:722
  90.8 9.7 %collective-permute-start.24 = (bf16[272,512]{1,0:T(8,128)(2,1)S(1)}, bf16[272,512]{1,0:T(8,128)(2,1)S(1)}, u32[]{:S(2)}, u32[]{:S(2)}) collective-permute-start(bf16[272,512]{1,0:T(8,128)(2,1)S(1)} %get-tuple-element.87), channel_id=1, source_target_pairs={{0,1},{1,0},{2,3},{3,2},{4,5},{5,4},{6,7},{7,6},{8,9},{9,8},{10,11... | collective-permute-start | bytes 835592 | tf_op jit(solution)/shard_map/ppermute | solution.py:722
  94.3 6.3 %copy-start.1 = (bf16[256,1536]{1,0:T(8,128)(2,1)S(1)}, bf16[256,1536]{1,0:T(8,128)(2,1)}, u32[]{:S(2)}) copy-start(bf16[256,1536]{1,0:T(8,128)(2,1)} %grad.5) | copy-start | bytes 2359300
  95.4 6.9 %collective-permute-start.23 = (bf16[272,256]{1,0:T(8,128)(2,1)}, bf16[272,256]{1,0:T(8,128)(2,1)}, u32[]{:S(2)}, u32[]{:S(2)}) collective-permute-start(bf16[272,256]{1,0:T(8,128)(2,1)} %decode.2), channel_id=1, source_target_pairs={{0,1},{1,0},{2,3},{3,2},{4,5},{5,4},{6,7},{7,6},{8,9},{9,8},{10,11... | collective-permute-start | bytes 417800 | tf_op jit(solution)/shard_map/ppermute | solution.py:722
  104.3 10.9 %collective-permute-start.25 = (bf16[272,256]{1,0:T(8,128)(2,1)}, bf16[272,256]{1,0:T(8,128)(2,1)}, u32[]{:S(2)}, u32[]{:S(2)}) collective-permute-start(bf16[272,256]{1,0:T(8,128)(2,1)} %get-tuple-element.90.refs_1_), channel_id=1, source_target_pairs={{0,1},{1,0},{2,3},{3,2},{4,5},{5,4},{6,7},{7,6},{8,9},{9,8},{10,11... | collective-permute-start | bytes 417800 | tf_op jit(solution)/shard_map/ppermute | solution.py:722
  106.0 8.3 %collective-permute-start.26 = (bf16[272,512]{1,0:T(8,128)(2,1)S(1)}, bf16[272,512]{1,0:T(8,128)(2,1)S(1)}, u32[]{:S(2)}, u32[]{:S(2)}) collective-permute-start(bf16[272,512]{1,0:T(8,128)(2,1)S(1)} %get-tuple-element.91.refs_0_), channel_id=1, source_target_pairs={{0,1},{1,0},{2,3},{3,2},{4,5},{5,4},{6,7},{7,6},{8,9},{9,8},{10,11... | collective-permute-start | bytes 835592 | tf_op jit(solution)/shard_map/ppermute | solution.py:722

commit v15 on v14

--- a/solution.py
+++ b/solution.py
@@ -571,7 +571,7 @@
         decode_first_kernel,
         in_specs=[VM] * 4,
         out_specs=[VM] * 2,
-        out_shape=[shape((2 * ROWS, half), BF16), shape((2 * ROWS, width), BF16)],
+        out_shape=[shape((2 * ROWS, half), BF16), pltpu.VMEM((2 * ROWS, width), BF16)],
         compiler_params=params(8),
         cost_estimate=cost(10**6, 10**4),
         name="decode_first",
@@ -590,7 +590,7 @@
         functools.partial(decode_kernel, mine, first),
         in_specs=[VM, VM],
         out_specs=VM,
-        out_shape=shape((2 * ROWS, width), dtype),
+        out_shape=pltpu.VMEM((2 * ROWS, width), dtype),
         compiler_params=params(8),
         cost_estimate=cost(10**6, 10**4),
         name="decode",
@@ -642,14 +642,14 @@
         out_specs=[VM] * 3,
         out_shape=[
             shape((2 * OWN, width + (first if done else 0)), BF16),
-            shape((2 * ROWS, width), BF16),
+            pltpu.VMEM((2 * ROWS, width), BF16),
             shape((OWN, width), F32),
         ],
         scratch_shapes=[pltpu.VMEM((width // 64, 2 * OWN, 128), F32)],
         compiler_params=params(8),
         cost_estimate=cost(100 * 30 * 1000 * other.size, 14 * other.size),
         name="slopes",
-    )(own, other, inputs, grad, near, far, *done)
+    )(own, near_memory(other), inputs, near_memory(grad), near, far, *done)
 
 
 def backward_kernel(mine, firsts, count, *refs):
@@ -701,9 +701,9 @@
         out_specs=VM,
         out_shape=shape((OWN, half), dtype),
         compiler_params=params(10),
-        cost_estimate=cost(100 * 2 * 3 * half * size, 6 * size),
+        cost_estimate=cost(1 * 2 * 3 * half * size, 6 * size),
         name="backward",
-    )(*[part for _, part in parts], *starts, weight)
+    )(*[near_memory(part) for _, part in parts], *starts, weight)
 
 
 def place(at):

time: 118 us -> 114 us (0.966)
  waiting for transfers between devices: 42.8 us -> 38.6 us
    ppermute x6, waiting for transfers between devices: 18.9 us -> 14.7 us  [swap(): return lax.ppermute(value, 'head', [(0, 1), (1, 0)])]
  transfers between devices with their start and end apart: 27 -> 27, of which waited for: 16 -> 16; matrix products, arithmetic and copies ran while one was open for 0% -> 0% of each run, Pallas kernels for 16% -> 19%
where the time goes in v15:
time: 114 us
  starting transfers between devices  39.7 us (35%)
  waiting for transfers between devices  38.6 us (34%)
  Pallas kernels  34.2 us (30%)
    ppermute x20, starting transfers between devices, send(): return lax.ppermute(value, 'seq', moves(**step))  25.2 us
    ppermute x20, waiting for transfers between devices, send(): return lax.ppermute(value, 'seq', moves(**step))  23.9 us
    ppermute x6, waiting for transfers between devices, swap(): return lax.ppermute(value, 'head', [(0, 1), (1, 0)])  14.7 us
    ppermute x6, starting transfers between devices, swap(): return lax.ppermute(value, 'head', [(0, 1), (1, 0)])  13.8 us
    pallas_call x2, Pallas kernels, attend(): pl.pallas_call(functools.partial(attend_kernel, len(pieces), len(inverses...  8.36 us
    pallas_call x3, Pallas kernels, backward(): pl.pallas_call(functools.partial(backward_kernel, mine, [first for first,...  5.17 us
    pallas_call x1, Pallas kernels, load(): pl.pallas_call(load_kernel, in_specs=[VM, HBM, HBM], out_specs=[VM] * 3,...  3.29 us
    pallas_call x2, Pallas kernels, slopes(): pl.pallas_call(functools.partial(slope_kernel, first), in_specs=[VM] * (6...  3.27 us
  transfers between devices with their start and end apart: 27, of which 16 were waited for; matrix products, arithmetic and copies ran while one was open for 0% of the time, Pallas kernels for 19%

profile of v15, /device:TPU:0, one launch (start us, length us, event | category | flops | bytes accessed | tf_op | source)
XLA Modules:
  0.0 113.6 jit_solution(8695964829058297408)
XLA Ops:
  0.6 0.9 prepare.1
  1.5 0.1 collective-permute-start
  1.6 0.7 collective-permute-start.1
  2.3 0.0 copy-start.3
  2.3 3.3 %load.1 = (bf16[256,1536]{1,0:T(8,128)(2,1)S(1)}, bf16[256,1536]{1,0:T(8,128)(2,1)S(1)}, bf16[3,1536,768]{2,1,0:T(8,128)(2,1)S(1)}) custom-call(bf16[128,128]{1,0:T(8,128)(2,1)S(1)} %get-tuple-element.50.codes, bf16[256,1536]{1,0:T(8,128)(2,1)} %stems.1, bf16[3,1536,768]{2,1,0:T(8,128)(2,1)} %weights.1), custom_call_target="tpu_custom_call" | custom-call | flops 100000 | bytes 7077888 | tf_op jit(solution)/shard_map/load/pallas_call | solution.py:168
  5.6 2.5 %encode.1.mine.encoded = bf16[272,768]{1,0:T(8,128)(2,1)S(1)} custom-call(bf16[8,1664]{1,0:T(8,128)(2,1)S(1)} %collective-permute-done.near, bf16[8,1664]{1,0:T(8,128)(2,1)S(1)} %collective-permute-done.1.far, bf16[256,1536]{1,0:T(8,128)(2,1)S(1)} %get-tuple-element.51.rows, bf16[256,1536]{1,0:T(8,128)(2,1)S(1)} %get-tuple-element.52.stem, ...), custom_call_target="tpu_custom_call" | custom-call | flops 1811939328 | bytes 14155776 | tf_op jit(solution)/shard_map/encode/pallas_call | solution.py:221
  8.2 3.4 %collective-permute-start.2 = (bf16[272,768]{1,0:T(8,128)(2,1)S(1)}, bf16[272,768]{1,0:T(8,128)(2,1)S(1)}, u32[]{:S(2)}, u32[]{:S(2)}) collective-permute-start(bf16[272,768]{1,0:T(8,128)(2,1)S(1)} %encode.1.mine.encoded), channel_id=1, source_target_pairs={{0,1},{1,0},{2,3},{3,2},{4,5},{5,4},{6,7},{7,6},{8,9},{9,8},{10,11... | collective-permute-start | bytes 1253384 | tf_op jit(solution)/shard_map/ppermute | solution.py:722
  11.5 3.0 %fetch.1.weight = bf16[3,1536,768]{2,1,0:T(8,128)(2,1)S(1)} custom-call(bf16[3,1536,768]{2,1,0:T(8,128)(2,1)} %source), custom_call_target="tpu_custom_call" | custom-call | flops 100000 | bytes 7077888 | tf_op jit(solution)/shard_map/fetch/pallas_call | solution.py:243
  14.6 6.2 %collective-permute-done.2.theirs = bf16[272,768]{1,0:T(8,128)(2,1)S(1)} collective-permute-done((bf16[272,768]{1,0:T(8,128)(2,1)S(1)}, bf16[272,768]{1,0:T(8,128)(2,1)S(1)}, u32[]{:S(2)}, u32[]{:S(2)}) %collective-permute-start.2) | collective-permute-done | bytes 417824 | tf_op jit(solution)/shard_map/ppermute | solution.py:722
  20.7 1.5 %project_keys.1 = (bf16[2,136,768]{2,1,0:T(8,128)(2,1)S(1)}, bf16[128,384]{1,0:T(8,128)(2,1)S(1)}, bf16[128,384]{1,0:T(8,128)(2,1)S(1)}, bf16[128,384]{1,0:T(8,128)(2,1)S(1)}, bf16[128,384]{1,0:T(8,128)(2,1)S(1)}) custom-call(bf16[272,768]{1,0:T(8,128)(2,1)S(1)} %encode.1.mine.encoded, bf16[272,768]{1,0:T(8,128)(2,1)S(1)} %collective-permute-done.2.theirs, ...), custom_call_target="tpu_custom_call" | custom-call | flops 641728512 | bytes 7077888 | tf_op jit(solution)/shard_map/project_keys/pallas_call | solution.py:296
  22.2 0.0 copy-start.2
  22.2 5.2 %collective-permute-start.3 = (bf16[128,384]{1,0:T(8,128)(2,1)S(1)}, bf16[128,384]{1,0:T(8,128)(2,1)S(1)}, u32[]{:S(2)}, u32[]{:S(2)}) collective-permute-start(bf16[128,384]{1,0:T(8,128)(2,1)S(1)} %get-tuple-element.59), channel_id=1, source_target_pairs={{0,32},{2,34},{4,36},{6,38},{8,40},{10,42},{12,44},{14,46},{16,48}... | collective-permute-start | bytes 294920 | tf_op jit(solution)/shard_map/ppermute | solution.py:726
  27.4 1.6 %collective-permute-start.4 = (bf16[128,384]{1,0:T(8,128)(2,1)S(1)}, bf16[128,384]{1,0:T(8,128)(2,1)S(1)}, u32[]{:S(2)}, u32[]{:S(2)}) collective-permute-start(bf16[128,384]{1,0:T(8,128)(2,1)S(1)} %get-tuple-element.60), channel_id=1, source_target_pairs={{0,96},{2,98},{4,100},{6,102},{8,104},{10,106},{12,108},{14,110},{... | collective-permute-start | bytes 294920 | tf_op jit(solution)/shard_map/ppermute | solution.py:726
  29.0 2.0 %collective-permute-start.5 = (bf16[128,384]{1,0:T(8,128)(2,1)S(1)}, bf16[128,384]{1,0:T(8,128)(2,1)S(1)}, u32[]{:S(2)}, u32[]{:S(2)}) collective-permute-start(bf16[128,384]{1,0:T(8,128)(2,1)S(1)} %get-tuple-element.61), channel_id=1, source_target_pairs={{0,64},{2,66},{4,68},{6,70},{8,72},{10,74},{12,76},{14,78},{16,80}... | collective-permute-start | bytes 294920 | tf_op jit(solution)/shard_map/ppermute | solution.py:726
  31.0 1.6 %collective-permute-done.3 = bf16[128,384]{1,0:T(8,128)(2,1)S(1)} collective-permute-done((bf16[128,384]{1,0:T(8,128)(2,1)S(1)}, bf16[128,384]{1,0:T(8,128)(2,1)S(1)}, u32[]{:S(2)}, u32[]{:S(2)}) %collective-permute-start.3) | collective-permute-done | bytes 98336 | tf_op jit(solution)/shard_map/ppermute | solution.py:726
  32.5 2.6 %collective-permute-done.5 = bf16[128,384]{1,0:T(8,128)(2,1)S(1)} collective-permute-done((bf16[128,384]{1,0:T(8,128)(2,1)S(1)}, bf16[128,384]{1,0:T(8,128)(2,1)S(1)}, u32[]{:S(2)}, u32[]{:S(2)}) %collective-permute-start.5) | collective-permute-done | bytes 98336 | tf_op jit(solution)/shard_map/ppermute | solution.py:726
  35.2 2.2 %collective-permute-start.6 = (bf16[512,384]{1,0:T(8,128)(2,1)S(1)}, bf16[512,384]{1,0:T(8,128)(2,1)S(1)}, u32[]{:S(2)}, u32[]{:S(2)}) collective-permute-start(bf16[512,384]{1,0:T(8,128)(2,1)S(1)} %constant_dynamic-update-slice_fusion.refs_0_), channel_id=1, source_target_pairs={{0,8},{2,10},{4,12},{6,14},{8,16},{10,18},{12,20},{14,22},{16,24},... | collective-permute-start | bytes 1179656 | tf_op jit(solution)/shard_map/ppermute | solution.py:726
  37.3 2.2 %collective-permute-start.7 = (bf16[512,384]{1,0:T(8,128)(2,1)S(1)}, bf16[512,384]{1,0:T(8,128)(2,1)S(1)}, u32[]{:S(2)}, u32[]{:S(2)}) collective-permute-start(bf16[512,384]{1,0:T(8,128)(2,1)S(1)} %constant_dynamic-update-slice_fusion.refs_0_), channel_id=1, source_target_pairs={{0,24},{2,26},{4,28},{6,30},{8,0},{10,2},{12,4},{14,6},{16,8},{18,... | collective-permute-start | bytes 1179656 | tf_op jit(solution)/shard_map/ppermute | solution.py:726
  39.5 0.7 project_queries.1
  40.3 0.4 collective-permute-start.8
  40.6 3.0 %collective-permute-start.9 = (bf16[136,256]{1,0:T(8,128)(2,1)S(1)}, bf16[136,256]{1,0:T(8,128)(2,1)S(1)}, u32[]{:S(2)}, u32[]{:S(2)}) collective-permute-start(bf16[136,256]{1,0:T(8,128)(2,1)S(1)} %get-tuple-element.67), channel_id=1, source_target_pairs={{0,96},{2,98},{4,100},{6,102},{8,104},{10,106},{12,108},{14,110},{... | collective-permute-start | bytes 208904 | tf_op jit(solution)/shard_map/ppermute | solution.py:726
  43.6 0.6 collective-permute-start.10
  44.2 2.4 %collective-permute-done.8 = bf16[136,256]{1,0:T(8,128)(2,1)S(1)} collective-permute-done((bf16[136,256]{1,0:T(8,128)(2,1)S(1)}, bf16[136,256]{1,0:T(8,128)(2,1)S(1)}, u32[]{:S(2)}, u32[]{:S(2)}) %collective-permute-start.8) | collective-permute-done | bytes 69664 | tf_op jit(solution)/shard_map/ppermute | solution.py:726
  46.6 2.8 %collective-permute-done.10 = bf16[136,256]{1,0:T(8,128)(2,1)S(1)} collective-permute-done((bf16[136,256]{1,0:T(8,128)(2,1)S(1)}, bf16[136,256]{1,0:T(8,128)(2,1)S(1)}, u32[]{:S(2)}, u32[]{:S(2)}) %collective-permute-start.10) | collective-permute-done | bytes 69664 | tf_op jit(solution)/shard_map/ppermute | solution.py:726
  49.4 0.5 collective-permute-start.13
  49.9 0.3 collective-permute-start.16
  50.3 0.8 collective-permute-start.14
  51.1 2.5 %collective-permute-start.15 = (bf16[256,384]{1,0:T(8,128)(2,1)S(1)}, bf16[256,384]{1,0:T(8,128)(2,1)S(1)}, u32[]{:S(2)}, u32[]{:S(2)}) collective-permute-start(bf16[256,384]{1,0:T(8,128)(2,1)S(1)} %slice.7), channel_id=1, source_target_pairs={{0,24},{2,26},{4,28},{6,30},{8,0},{10,2},{12,4},{14,6},{16,8},{18,... | collective-permute-start | bytes 589832 | tf_op jit(solution)/shard_map/ppermute | solution.py:726
  53.6 0.9 norms.1.refs_8_
  54.6 3.7 %collective-permute-done.14 = bf16[256,384]{1,0:T(8,128)(2,1)S(1)} collective-permute-done((bf16[256,384]{1,0:T(8,128)(2,1)S(1)}, bf16[256,384]{1,0:T(8,128)(2,1)S(1)}, u32[]{:S(2)}, u32[]{:S(2)}) %collective-permute-start.14) | collective-permute-done | bytes 196640 | tf_op jit(solution)/shard_map/ppermute | solution.py:726
  58.3 0.4 collective-permute-done.16.queries
  58.7 0.3 collective-permute-start.17
  59.0 1.7 %collective-permute-done.17.refs_7_ = bf16[512,384]{1,0:T(8,128)(2,1)S(1)} collective-permute-done((bf16[512,384]{1,0:T(8,128)(2,1)S(1)}, bf16[512,384]{1,0:T(8,128)(2,1)S(1)}, u32[]{:S(2)}, u32[]{:S(2)}) %collective-permute-start.17) | collective-permute-done | bytes 393248 | tf_op jit(solution)/shard_map/ppermute | solution.py:726
  60.7 4.3 %attend.2 = (bf16[544,256]{1,0:T(8,128)(2,1)S(1)}, f32[8,1024]{1,0:T(8,128)S(1)}) custom-call(f32[1,4]{1,0:T(1,128)S(1)} %bitcast.4, bf16[544,256]{1,0:T(8,128)(2,1)S(1)} %collective-permute-done.16.queries, bf16[512,384]{1,0:T(8,128)(2,1)S(1)} %constant_dynamic-update-slice_fusion.refs_0_, bf16[512,384]{1,0:T(8,128)(2,1)S(1)} %collective-permute-done.6.refs_1_, ...), custom_call_target="tpu_custom_call" | custom-call | flops 2281701376 | bytes 4456448 | tf_op jit(solution)/shard_map/attend/pallas_call | solution.py:473
  65.0 1.4 %collective-permute-start.18 = (bf16[544,256]{1,0:T(8,128)(2,1)S(1)}, bf16[544,256]{1,0:T(8,128)(2,1)S(1)}, u32[]{:S(2)}, u32[]{:S(2)}) collective-permute-start(bf16[544,256]{1,0:T(8,128)(2,1)S(1)} %get-tuple-element.79), channel_id=1, source_target_pairs={{0,4},{2,6},{4,0},{6,2},{8,12},{10,14},{12,8},{14,10},{16,20},{18,... | collective-permute-start | bytes 835592 | tf_op jit(solution)/shard_map/ppermute | solution.py:726
  66.5 4.0 %attend.3.a0 = bf16[544,256]{1,0:T(8,128)(2,1)S(1)} custom-call(f32[1,4]{1,0:T(1,128)S(1)} %bitcast.5, bf16[544,256]{1,0:T(8,128)(2,1)S(1)} %constant_dynamic-update-slice_fusion.4.queries, bf16[512,384]{1,0:T(8,128)(2,1)S(1)} %constant_dynamic-update-slice_fusion.refs_0_, bf16[512,384]{1,0:T(8,128)(2,1)S(1)} %collective-permute-done.6.refs_1_, ...), custom_call_target="tpu_custom_call" | custom-call | flops 2281701376 | bytes 4456448 | tf_op jit(solution)/shard_map/attend/pallas_call | solution.py:473
  70.5 3.3 %collective-permute-done.18.a1 = bf16[544,256]{1,0:T(8,128)(2,1)S(1)} collective-permute-done((bf16[544,256]{1,0:T(8,128)(2,1)S(1)}, bf16[544,256]{1,0:T(8,128)(2,1)S(1)}, u32[]{:S(2)}, u32[]{:S(2)}) %collective-permute-start.18) | collective-permute-done | bytes 278560 | tf_op jit(solution)/shard_map/ppermute | solution.py:726
  73.8 0.5 merge.1
  74.4 0.9 collective-permute-start.19
  75.2 1.2 %collective-permute-start.20 = (bf16[136,256]{1,0:T(8,128)(2,1)S(1)}, bf16[136,256]{1,0:T(8,128)(2,1)S(1)}, u32[]{:S(2)}, u32[]{:S(2)}) collective-permute-start(bf16[136,256]{1,0:T(8,128)(2,1)S(1)} %get-tuple-element.82), channel_id=1, source_target_pairs={{0,64},{2,66},{4,68},{6,70},{8,72},{10,74},{12,76},{14,78},{16,80}... | collective-permute-start | bytes 208904 | tf_op jit(solution)/shard_map/ppermute | solution.py:726
  76.4 0.2 collective-permute-start.21
  76.7 2.1 %collective-permute-done.19.a1 = bf16[136,256]{1,0:T(8,128)(2,1)S(1)} collective-permute-done((bf16[136,256]{1,0:T(8,128)(2,1)S(1)}, bf16[136,256]{1,0:T(8,128)(2,1)S(1)}, u32[]{:S(2)}, u32[]{:S(2)}) %collective-permute-start.19) | collective-permute-done | bytes 69664 | tf_op jit(solution)/shard_map/ppermute | solution.py:726
  78.7 2.7 %collective-permute-done.20.a2 = bf16[136,256]{1,0:T(8,128)(2,1)S(1)} collective-permute-done((bf16[136,256]{1,0:T(8,128)(2,1)S(1)}, bf16[136,256]{1,0:T(8,128)(2,1)S(1)}, u32[]{:S(2)}, u32[]{:S(2)}) %collective-permute-start.20) | collective-permute-done | bytes 69664 | tf_op jit(solution)/shard_map/ppermute | solution.py:726
  81.4 0.7 collective-permute-done.21.a3
  82.1 0.4 output.3
  82.5 3.2 %collective-permute-start.22 = (bf16[136,768]{1,0:T(8,128)(2,1)S(1)}, bf16[136,768]{1,0:T(8,128)(2,1)S(1)}, u32[]{:S(2)}, u32[]{:S(2)}) collective-permute-start(bf16[136,768]{1,0:T(8,128)(2,1)S(1)} %output.3), channel_id=1, source_target_pairs={{0,1},{1,0},{2,3},{3,2},{4,5},{5,4},{6,7},{7,6},{8,9},{9,8},{10,11... | collective-permute-start | bytes 626696 | tf_op jit(solution)/shard_map/ppermute | solution.py:722
  85.7 0.4 output.2.own
  86.1 3.8 %collective-permute-done.22.other = bf16[136,768]{1,0:T(8,128)(2,1)S(1)} collective-permute-done((bf16[136,768]{1,0:T(8,128)(2,1)S(1)}, bf16[136,768]{1,0:T(8,128)(2,1)S(1)}, u32[]{:S(2)}, u32[]{:S(2)}) %collective-permute-start.22) | collective-permute-done | bytes 208928 | tf_op jit(solution)/shard_map/ppermute | solution.py:722
  89.9 0.9 decode_first.1
  90.8 3.4 %collective-permute-start.24 = (bf16[272,512]{1,0:T(8,128)(2,1)S(1)}, bf16[272,512]{1,0:T(8,128)(2,1)S(1)}, u32[]{:S(2)}, u32[]{:S(2)}) collective-permute-start(bf16[272,512]{1,0:T(8,128)(2,1)S(1)} %get-tuple-element.87), channel_id=1, source_target_pairs={{0,1},{1,0},{2,3},{3,2},{4,5},{5,4},{6,7},{7,6},{8,9},{9,8},{10,11... | collective-permute-start | bytes 835592 | tf_op jit(solution)/shard_map/ppermute | solution.py:722
  94.3 1.2 %decode.2 = bf16[272,256]{1,0:T(8,128)(2,1)} custom-call(bf16[272,768]{1,0:T(8,128)(2,1)S(1)} %get-tuple-element.85.inputs, bf16[3,768,1536]{2,1,0:T(8,128)(2,1)S(1)} %bitcast.3), custom_call_target="tpu_custom_call" | custom-call | flops 1000000 | bytes 10000 | tf_op jit(solution)/shard_map/decode/pallas_call | solution.py:589
  95.4 0.4 collective-permute-start.23
  95.8 1.2 %decode.3.own = f32[272,768]{1,0:T(8,128)S(1)} custom-call(bf16[272,768]{1,0:T(8,128)(2,1)S(1)} %get-tuple-element.85.inputs, bf16[3,768,1536]{2,1,0:T(8,128)(2,1)S(1)} %bitcast.3), custom_call_target="tpu_custom_call" | custom-call | flops 1000000 | bytes 10000 | tf_op jit(solution)/shard_map/decode/pallas_call | solution.py:589
  97.0 3.8 %collective-permute-done.24.other = bf16[272,512]{1,0:T(8,128)(2,1)S(1)} collective-permute-done((bf16[272,512]{1,0:T(8,128)(2,1)S(1)}, bf16[272,512]{1,0:T(8,128)(2,1)S(1)}, u32[]{:S(2)}, u32[]{:S(2)}) %collective-permute-start.24) | collective-permute-done | bytes 278560 | tf_op jit(solution)/shard_map/ppermute | solution.py:722
  100.8 1.3 %slopes.2 = (bf16[256,512]{1,0:T(8,128)(2,1)S(1)}, bf16[272,512]{1,0:T(8,128)(2,1)}, f32[128,512]{1,0:T(8,128)S(1)}) custom-call(f32[272,768]{1,0:T(8,128)S(1)} %decode.3.own, bf16[272,512]{1,0:T(8,128)(2,1)S(1)} %collective-permute-done.24.other, bf16[272,768]{1,0:T(8,128)(2,1)S(1)} %get-tuple-element.85.inputs, bf16[256,1536]{1,0:T(8,128)(2,1)S(1)} %copy-done.1, ...), custom_call_target="tpu_custom_call" | custom-call | flops 417792000000 | bytes 1949696 | tf_op jit(solution)/shard_map/slopes/pallas_call | solution.py:639
  102.2 1.6 %collective-permute-start.26 = (bf16[272,512]{1,0:T(8,128)(2,1)}, bf16[272,512]{1,0:T(8,128)(2,1)}, u32[]{:S(2)}, u32[]{:S(2)}) collective-permute-start(bf16[272,512]{1,0:T(8,128)(2,1)} %get-tuple-element.91.refs_0_), channel_id=1, source_target_pairs={{0,1},{1,0},{2,3},{3,2},{4,5},{5,4},{6,7},{7,6},{8,9},{9,8},{10,11... | collective-permute-start | bytes 835592 | tf_op jit(solution)/shard_map/ppermute | solution.py:722
  103.8 0.1 collective-permute-done.23.other
  103.9 1.9 %slopes.3 = (bf16[256,768]{1,0:T(8,128)(2,1)}, bf16[272,256]{1,0:T(8,128)(2,1)S(1)}, f32[128,256]{1,0:T(8,128)S(1)}) custom-call(f32[272,768]{1,0:T(8,128)S(1)} %decode.3.own, bf16[272,256]{1,0:T(8,128)(2,1)} %collective-permute-done.23.other, bf16[272,768]{1,0:T(8,128)(2,1)S(1)} %get-tuple-element.85.inputs, bf16[256,1536]{1,0:T(8,128)(2,1)S(1)} %copy-done.1, ...), custom_call_target="tpu_custom_call" | custom-call | flops 208896000000 | bytes 974848 | tf_op jit(solution)/shard_map/slopes/pallas_call | solution.py:639
  105.9 1.8 %collective-permute-start.25 = (bf16[272,256]{1,0:T(8,128)(2,1)S(1)}, bf16[272,256]{1,0:T(8,128)(2,1)S(1)}, u32[]{:S(2)}, u32[]{:S(2)}) collective-permute-start(bf16[272,256]{1,0:T(8,128)(2,1)S(1)} %get-tuple-element.90.refs_1_), channel_id=1, source_target_pairs={{0,1},{1,0},{2,3},{3,2},{4,5},{5,4},{6,7},{7,6},{8,9},{9,8},{10,11... | collective-permute-start | bytes 417800 | tf_op jit(solution)/shard_map/ppermute | solution.py:722
  107.7 2.2 %backward.3.refs_1_ = f32[128,768]{1,0:T(8,128)S(1)} custom-call(bf16[272,512]{1,0:T(8,128)(2,1)} %get-tuple-element.91.refs_0_, bf16[272,256]{1,0:T(8,128)(2,1)S(1)} %get-tuple-element.90.refs_1_, f32[128,512]{1,0:T(8,128)S(1)} %get-tuple-element.92.refs_2_, f32[128,256]{1,0:T(8,128)S(1)} %get-tuple-element.93.refs_3_, bf16[3,768,1536]{2,1,0:T(8,128)(2,1)S(1)} %bitcast.3), custom_call_target="tpu_custom_call" | custom-call | flops 962592768 | bytes 1253376 | tf_op jit(solution)/shard_map/backward/pallas_call | solution.py:698
  109.8 0.7 collective-permute-done.26.refs_0_
  110.6 1.8 %backward.4.refs_1_ = f32[128,768]{1,0:T(8,128)S(1)} custom-call(bf16[272,512]{1,0:T(8,128)(2,1)} %collective-permute-done.26.refs_0_, f32[128,768]{1,0:T(8,128)S(1)} %backward.3.refs_1_, bf16[3,768,1536]{2,1,0:T(8,128)(2,1)S(1)} %bitcast.3), custom_call_target="tpu_custom_call" | custom-call | flops 641728512 | bytes 835584 | tf_op jit(solution)/shard_map/backward/pallas_call | solution.py:698
  112.4 0.0 collective-permute-done.25.refs_0_
  112.4 1.2 %backward.5 = bf16[128,768]{1,0:T(8,128)(2,1)} custom-call(bf16[272,256]{1,0:T(8,128)(2,1)S(1)} %collective-permute-done.25.refs_0_, f32[128,768]{1,0:T(8,128)S(1)} %backward.4.refs_1_, bf16[3,768,1536]{2,1,0:T(8,128)(2,1)S(1)} %bitcast.3), custom_call_target="tpu_custom_call" | custom-call | flops 320864256 | bytes 417792 | tf_op jit(solution)/shard_map/backward/pallas_call | solution.py:698
  (36 shorter events, 0.2 us)
Async XLA Ops:
  1.5 4.1 %collective-permute-start = (bf16[8,1664]{1,0:T(8,128)(2,1)S(1)}, bf16[8,1664]{1,0:T(8,128)(2,1)S(1)}, u32[]{:S(2)}, u32[]{:S(2)}) collective-permute-start(bf16[8,1664]{1,0:T(8,128)(2,1)S(1)} %get-tuple-element.48), channel_id=1, source_target_pairs={{0,2},{2,0},{4,6},{6,4},{8,10},{10,8},{12,14},{14,12},{16,18},{18,... | collective-permute-start | bytes 79880 | tf_op jit(solution)/shard_map/ppermute | solution.py:726
  1.6 4.0 %collective-permute-start.1 = (bf16[8,1664]{1,0:T(8,128)(2,1)S(1)}, bf16[8,1664]{1,0:T(8,128)(2,1)S(1)}, u32[]{:S(2)}, u32[]{:S(2)}) collective-permute-start(bf16[8,1664]{1,0:T(8,128)(2,1)S(1)} %get-tuple-element.49), channel_id=1, source_target_pairs={{2,4},{6,8},{10,12},{14,16},{18,20},{22,24},{26,28},{30,32},{34,36... | collective-permute-start | bytes 79880 | tf_op jit(solution)/shard_map/ppermute | solution.py:747
  2.3 9.2 %copy-start.3 = (f32[1536]{0:T(1024)S(1)}, f32[1536]{0:T(1024)}, u32[]{:S(2)}) copy-start(f32[1536]{0:T(1024)} %param.12) | copy-start | bytes 18436
  8.2 12.6 %collective-permute-start.2 = (bf16[272,768]{1,0:T(8,128)(2,1)S(1)}, bf16[272,768]{1,0:T(8,128)(2,1)S(1)}, u32[]{:S(2)}, u32[]{:S(2)}) collective-permute-start(bf16[272,768]{1,0:T(8,128)(2,1)S(1)} %encode.1.mine.encoded), channel_id=1, source_target_pairs={{0,1},{1,0},{2,3},{3,2},{4,5},{5,4},{6,7},{7,6},{8,9},{9,8},{10,11... | collective-permute-start | bytes 1253384 | tf_op jit(solution)/shard_map/ppermute | solution.py:722
  22.2 38.5 %copy-start.2 = (f32[4]{0:T(128)S(1)}, f32[4]{0:T(128)}, u32[]{:S(2)}) copy-start(f32[4]{0:T(128)} %param.14) | copy-start | bytes 52
  22.2 10.3 %collective-permute-start.3 = (bf16[128,384]{1,0:T(8,128)(2,1)S(1)}, bf16[128,384]{1,0:T(8,128)(2,1)S(1)}, u32[]{:S(2)}, u32[]{:S(2)}) collective-permute-start(bf16[128,384]{1,0:T(8,128)(2,1)S(1)} %get-tuple-element.59), channel_id=1, source_target_pairs={{0,32},{2,34},{4,36},{6,38},{8,40},{10,42},{12,44},{14,46},{16,48}... | collective-permute-start | bytes 294920 | tf_op jit(solution)/shard_map/ppermute | solution.py:726
  27.4 5.1 %collective-permute-start.4 = (bf16[128,384]{1,0:T(8,128)(2,1)S(1)}, bf16[128,384]{1,0:T(8,128)(2,1)S(1)}, u32[]{:S(2)}, u32[]{:S(2)}) collective-permute-start(bf16[128,384]{1,0:T(8,128)(2,1)S(1)} %get-tuple-element.60), channel_id=1, source_target_pairs={{0,96},{2,98},{4,100},{6,102},{8,104},{10,106},{12,108},{14,110},{... | collective-permute-start | bytes 294920 | tf_op jit(solution)/shard_map/ppermute | solution.py:726
  29.0 6.1 %collective-permute-start.5 = (bf16[128,384]{1,0:T(8,128)(2,1)S(1)}, bf16[128,384]{1,0:T(8,128)(2,1)S(1)}, u32[]{:S(2)}, u32[]{:S(2)}) collective-permute-start(bf16[128,384]{1,0:T(8,128)(2,1)S(1)} %get-tuple-element.61), channel_id=1, source_target_pairs={{0,64},{2,66},{4,68},{6,70},{8,72},{10,74},{12,76},{14,78},{16,80}... | collective-permute-start | bytes 294920 | tf_op jit(solution)/shard_map/ppermute | solution.py:726
  35.2 14.2 %collective-permute-start.6 = (bf16[512,384]{1,0:T(8,128)(2,1)S(1)}, bf16[512,384]{1,0:T(8,128)(2,1)S(1)}, u32[]{:S(2)}, u32[]{:S(2)}) collective-permute-start(bf16[512,384]{1,0:T(8,128)(2,1)S(1)} %constant_dynamic-update-slice_fusion.refs_0_), channel_id=1, source_target_pairs={{0,8},{2,10},{4,12},{6,14},{8,16},{10,18},{12,20},{14,22},{16,24},... | collective-permute-start | bytes 1179656 | tf_op jit(solution)/shard_map/ppermute | solution.py:726
  37.3 12.1 %collective-permute-start.7 = (bf16[512,384]{1,0:T(8,128)(2,1)S(1)}, bf16[512,384]{1,0:T(8,128)(2,1)S(1)}, u32[]{:S(2)}, u32[]{:S(2)}) collective-permute-start(bf16[512,384]{1,0:T(8,128)(2,1)S(1)} %constant_dynamic-update-slice_fusion.refs_0_), channel_id=1, source_target_pairs={{0,24},{2,26},{4,28},{6,30},{8,0},{10,2},{12,4},{14,6},{16,8},{18,... | collective-permute-start | bytes 1179656 | tf_op jit(solution)/shard_map/ppermute | solution.py:726
  40.3 6.3 %collective-permute-start.8 = (bf16[136,256]{1,0:T(8,128)(2,1)S(1)}, bf16[136,256]{1,0:T(8,128)(2,1)S(1)}, u32[]{:S(2)}, u32[]{:S(2)}) collective-permute-start(bf16[136,256]{1,0:T(8,128)(2,1)S(1)} %get-tuple-element.66), channel_id=1, source_target_pairs={{0,32},{2,34},{4,36},{6,38},{8,40},{10,42},{12,44},{14,46},{16,48}... | collective-permute-start | bytes 208904 | tf_op jit(solution)/shard_map/ppermute | solution.py:726
  40.6 6.0 %collective-permute-start.9 = (bf16[136,256]{1,0:T(8,128)(2,1)S(1)}, bf16[136,256]{1,0:T(8,128)(2,1)S(1)}, u32[]{:S(2)}, u32[]{:S(2)}) collective-permute-start(bf16[136,256]{1,0:T(8,128)(2,1)S(1)} %get-tuple-element.67), channel_id=1, source_target_pairs={{0,96},{2,98},{4,100},{6,102},{8,104},{10,106},{12,108},{14,110},{... | collective-permute-start | bytes 208904 | tf_op jit(solution)/shard_map/ppermute | solution.py:726
  43.6 5.8 %collective-permute-start.10 = (bf16[136,256]{1,0:T(8,128)(2,1)S(1)}, bf16[136,256]{1,0:T(8,128)(2,1)S(1)}, u32[]{:S(2)}, u32[]{:S(2)}) collective-permute-start(bf16[136,256]{1,0:T(8,128)(2,1)S(1)} %get-tuple-element.68), channel_id=1, source_target_pairs={{0,64},{2,66},{4,68},{6,70},{8,72},{10,74},{12,76},{14,78},{16,80}... | collective-permute-start | bytes 208904 | tf_op jit(solution)/shard_map/ppermute | solution.py:726
  46.6 4.5 %collective-permute-start.11 = (bf16[512,384]{1,0:T(8,128)(2,1)S(1)}, bf16[512,384]{1,0:T(8,128)(2,1)S(1)}, u32[]{:S(2)}, u32[]{:S(2)}) collective-permute-start(bf16[512,384]{1,0:T(8,128)(2,1)S(1)} %constant_dynamic-update-slice_fusion.refs_0_), channel_id=1, source_target_pairs={{0,2},{2,0},{4,6},{6,4},{8,10},{10,8},{12,14},{14,12},{16,18},{18,... | collective-permute-start | bytes 1179656 | tf_op jit(solution)/shard_map/ppermute | solution.py:726
  49.4 4.2 %collective-permute-start.12 = (bf16[512,384]{1,0:T(8,128)(2,1)S(1)}, bf16[512,384]{1,0:T(8,128)(2,1)S(1)}, u32[]{:S(2)}, u32[]{:S(2)}) collective-permute-start(bf16[512,384]{1,0:T(8,128)(2,1)S(1)} %collective-permute-done.6.refs_1_), channel_id=1, source_target_pairs={{0,2},{2,0},{4,6},{6,4},{8,10},{10,8},{12,14},{14,12},{16,18},{18,... | collective-permute-start | bytes 1179656 | tf_op jit(solution)/shard_map/ppermute | solution.py:726
  49.4 4.2 %collective-permute-start.13 = (bf16[512,384]{1,0:T(8,128)(2,1)S(1)}, bf16[512,384]{1,0:T(8,128)(2,1)S(1)}, u32[]{:S(2)}, u32[]{:S(2)}) collective-permute-start(bf16[512,384]{1,0:T(8,128)(2,1)S(1)} %collective-permute-done.7.refs_2_), channel_id=1, source_target_pairs={{0,2},{2,0},{4,6},{6,4},{8,10},{10,8},{12,14},{14,12},{16,18},{18,... | collective-permute-start | bytes 1179656 | tf_op jit(solution)/shard_map/ppermute | solution.py:726
  49.9 8.7 %collective-permute-start.16 = (bf16[544,256]{1,0:T(8,128)(2,1)S(1)}, bf16[544,256]{1,0:T(8,128)(2,1)S(1)}, u32[]{:S(2)}, u32[]{:S(2)}) collective-permute-start(bf16[544,256]{1,0:T(8,128)(2,1)S(1)} %constant_dynamic-update-slice_fusion.4.queries), channel_id=1, source_target_pairs={{0,4},{2,6},{4,0},{6,2},{8,12},{10,14},{12,8},{14,10},{16,20},{18,... | collective-permute-start | bytes 835592 | tf_op jit(solution)/shard_map/ppermute | solution.py:726
  50.3 7.9 %collective-permute-start.14 = (bf16[256,384]{1,0:T(8,128)(2,1)S(1)}, bf16[256,384]{1,0:T(8,128)(2,1)S(1)}, u32[]{:S(2)}, u32[]{:S(2)}) collective-permute-start(bf16[256,384]{1,0:T(8,128)(2,1)S(1)} %slice.6), channel_id=1, source_target_pairs={{0,8},{2,10},{4,12},{6,14},{8,16},{10,18},{12,20},{14,22},{16,24},... | collective-permute-start | bytes 589832 | tf_op jit(solution)/shard_map/ppermute | solution.py:726
  51.1 7.1 %collective-permute-start.15 = (bf16[256,384]{1,0:T(8,128)(2,1)S(1)}, bf16[256,384]{1,0:T(8,128)(2,1)S(1)}, u32[]{:S(2)}, u32[]{:S(2)}) collective-permute-start(bf16[256,384]{1,0:T(8,128)(2,1)S(1)} %slice.7), channel_id=1, source_target_pairs={{0,24},{2,26},{4,28},{6,30},{8,0},{10,2},{12,4},{14,6},{16,8},{18,... | collective-permute-start | bytes 589832 | tf_op jit(solution)/shard_map/ppermute | solution.py:726
  58.7 2.0 %collective-permute-start.17 = (bf16[512,384]{1,0:T(8,128)(2,1)S(1)}, bf16[512,384]{1,0:T(8,128)(2,1)S(1)}, u32[]{:S(2)}, u32[]{:S(2)}) collective-permute-start(bf16[512,384]{1,0:T(8,128)(2,1)S(1)} %constant_dynamic-update-slice_fusion.8.refs_6_), channel_id=1, source_target_pairs={{0,2},{2,0},{4,6},{6,4},{8,10},{10,8},{12,14},{14,12},{16,18},{18,... | collective-permute-start | bytes 1179656 | tf_op jit(solution)/shard_map/ppermute | solution.py:726
  60.7 21.4 %copy-start = (bf16[768,1536]{1,0:T(8,128)(2,1)S(1)}, bf16[768,1536]{1,0:T(8,128)(2,1)}, u32[]{:S(2)}) copy-start(bf16[768,1536]{1,0:T(8,128)(2,1)} %weight.6) | copy-start | bytes 7077892
  65.0 8.8 %collective-permute-start.18 = (bf16[544,256]{1,0:T(8,128)(2,1)S(1)}, bf16[544,256]{1,0:T(8,128)(2,1)S(1)}, u32[]{:S(2)}, u32[]{:S(2)}) collective-permute-start(bf16[544,256]{1,0:T(8,128)(2,1)S(1)} %get-tuple-element.79), channel_id=1, source_target_pairs={{0,4},{2,6},{4,0},{6,2},{8,12},{10,14},{12,8},{14,10},{16,20},{18,... | collective-permute-start | bytes 835592 | tf_op jit(solution)/shard_map/ppermute | solution.py:726
  66.5 23.5 %slice-start = ((s8[7077888]{0:T(1024)(128)(4,1)}), s8[4194304]{0:T(1024)(128)(4,1)S(1)}, s32[]{:S(2)}) async-start(s8[7077888]{0:T(1024)(128)(4,1)} %bitcast.2), calls=%async_computation | async-start | bytes 8388608
  66.5 23.5 %slice-start.1 = ((s8[7077888]{0:T(1024)(128)(4,1)}), s8[2883584]{0:T(1024)(128)(4,1)S(1)}, s32[]{:S(2)}) async-start(s8[7077888]{0:T(1024)(128)(4,1)} %bitcast.2), calls=%async_computation.1 | async-start | bytes 5767168
  74.4 4.4 %collective-permute-start.19 = (bf16[136,256]{1,0:T(8,128)(2,1)S(1)}, bf16[136,256]{1,0:T(8,128)(2,1)S(1)}, u32[]{:S(2)}, u32[]{:S(2)}) collective-permute-start(bf16[136,256]{1,0:T(8,128)(2,1)S(1)} %get-tuple-element.81), channel_id=1, source_target_pairs={{0,96},{2,98},{4,100},{6,102},{8,104},{10,106},{12,108},{14,110},{... | collective-permute-start | bytes 208904 | tf_op jit(solution)/shard_map/ppermute | solution.py:726
  75.2 6.2 %collective-permute-start.20 = (bf16[136,256]{1,0:T(8,128)(2,1)S(1)}, bf16[136,256]{1,0:T(8,128)(2,1)S(1)}, u32[]{:S(2)}, u32[]{:S(2)}) collective-permute-start(bf16[136,256]{1,0:T(8,128)(2,1)S(1)} %get-tuple-element.82), channel_id=1, source_target_pairs={{0,64},{2,66},{4,68},{6,70},{8,72},{10,74},{12,76},{14,78},{16,80}... | collective-permute-start | bytes 208904 | tf_op jit(solution)/shard_map/ppermute | solution.py:726
  76.4 5.7 %collective-permute-start.21 = (bf16[136,256]{1,0:T(8,128)(2,1)S(1)}, bf16[136,256]{1,0:T(8,128)(2,1)S(1)}, u32[]{:S(2)}, u32[]{:S(2)}) collective-permute-start(bf16[136,256]{1,0:T(8,128)(2,1)S(1)} %get-tuple-element.83), channel_id=1, source_target_pairs={{0,32},{2,34},{4,36},{6,38},{8,40},{10,42},{12,44},{14,46},{16,48}... | collective-permute-start | bytes 208904 | tf_op jit(solution)/shard_map/ppermute | solution.py:726
  82.5 7.4 %collective-permute-start.22 = (bf16[136,768]{1,0:T(8,128)(2,1)S(1)}, bf16[136,768]{1,0:T(8,128)(2,1)S(1)}, u32[]{:S(2)}, u32[]{:S(2)}) collective-permute-start(bf16[136,768]{1,0:T(8,128)(2,1)S(1)} %output.3), channel_id=1, source_target_pairs={{0,1},{1,0},{2,3},{3,2},{4,5},{5,4},{6,7},{7,6},{8,9},{9,8},{10,11... | collective-permute-start | bytes 626696 | tf_op jit(solution)/shard_map/ppermute | solution.py:722
  90.8 10.0 %collective-permute-start.24 = (bf16[272,512]{1,0:T(8,128)(2,1)S(1)}, bf16[272,512]{1,0:T(8,128)(2,1)S(1)}, u32[]{:S(2)}, u32[]{:S(2)}) collective-permute-start(bf16[272,512]{1,0:T(8,128)(2,1)S(1)} %get-tuple-element.87), channel_id=1, source_target_pairs={{0,1},{1,0},{2,3},{3,2},{4,5},{5,4},{6,7},{7,6},{8,9},{9,8},{10,11... | collective-permute-start | bytes 835592 | tf_op jit(solution)/shard_map/ppermute | solution.py:722
  94.3 6.6 %copy-start.1 = (bf16[256,1536]{1,0:T(8,128)(2,1)S(1)}, bf16[256,1536]{1,0:T(8,128)(2,1)}, u32[]{:S(2)}) copy-start(bf16[256,1536]{1,0:T(8,128)(2,1)} %grad.5) | copy-start | bytes 2359300
  95.4 8.5 %collective-permute-start.23 = (bf16[272,256]{1,0:T(8,128)(2,1)}, bf16[272,256]{1,0:T(8,128)(2,1)}, u32[]{:S(2)}, u32[]{:S(2)}) collective-permute-start(bf16[272,256]{1,0:T(8,128)(2,1)} %decode.2), channel_id=1, source_target_pairs={{0,1},{1,0},{2,3},{3,2},{4,5},{5,4},{6,7},{7,6},{8,9},{9,8},{10,11... | collective-permute-start | bytes 417800 | tf_op jit(solution)/shard_map/ppermute | solution.py:722
  102.2 8.4 %collective-permute-start.26 = (bf16[272,512]{1,0:T(8,128)(2,1)}, bf16[272,512]{1,0:T(8,128)(2,1)}, u32[]{:S(2)}, u32[]{:S(2)}) collective-permute-start(bf16[272,512]{1,0:T(8,128)(2,1)} %get-tuple-element.91.refs_0_), channel_id=1, source_target_pairs={{0,1},{1,0},{2,3},{3,2},{4,5},{5,4},{6,7},{7,6},{8,9},{9,8},{10,11... | collective-permute-start | bytes 835592 | tf_op jit(solution)/shard_map/ppermute | solution.py:722
  105.9 6.6 %collective-permute-start.25 = (bf16[272,256]{1,0:T(8,128)(2,1)S(1)}, bf16[272,256]{1,0:T(8,128)(2,1)S(1)}, u32[]{:S(2)}, u32[]{:S(2)}) collective-permute-start(bf16[272,256]{1,0:T(8,128)(2,1)S(1)} %get-tuple-element.90.refs_1_), channel_id=1, source_target_pairs={{0,1},{1,0},{2,3},{3,2},{4,5},{5,4},{6,7},{7,6},{8,9},{9,8},{10,11... | collective-permute-start | bytes 417800 | tf_op jit(solution)/shard_map/ppermute | solution.py:722

commit v16 on v15

--- a/solution.py
+++ b/solution.py
@@ -513,7 +513,7 @@
     def tile(i):
         at = lanes(side * half + i * TILE, TILE)
         total = None
-        for distance, ref in enumerate((a0, a1, a2, a3)):
+        for distance, ref in zip((0, 2, 1, 3), (a0, a1, a2, a3)):
             head = lax.rem(ids[1] + distance, 4)
             rows = weight[pl.ds(pl.multiple_of(head * HEAD, HEAD), HEAD), at]
             term = dot(ref[:, :HEAD], rows)
@@ -754,7 +754,7 @@
     normed, *keyvals = project_keys(encoded, swap(encoded), gain, attention_weight)
 
     def spread(blocks):
-        return [send(blocks[d], dx=d) for d in (1, 3, 2)]
+        return [send(blocks[d], dx=d) for d in (2, 1, 3)]
 
     def stacked(blocks):
         return jnp.concatenate(lax.optimization_barrier(blocks), axis=0)
@@ -779,7 +779,7 @@
     other = send(other, dy=1)
     own = attend(scale, queries, pieces, inverses=[inverse, later])[0]
     mixed = merge([own, other])
-    heads = [mixed[0], send(mixed[1], dx=-1), send(mixed[3], dx=-2), send(mixed[2], dx=-3)]
+    heads = [mixed[0], send(mixed[1], dx=-2), send(mixed[2], dx=-1), send(mixed[3], dx=-3)]
 
     sent = swap(output(heads, out_weight, False, BF16))
     kept = output(heads, out_weight, True, F32)

time: 114 us -> 115 us (level)
  starting transfers between devices: 39.7 us -> 43.5 us
  waiting for transfers between devices: 38.6 us -> 35.5 us
    ppermute x20, starting transfers between devices: 25.2 us -> 28.9 us  [send(): return lax.ppermute(value, 'seq', moves(**step))]
    ppermute x20, waiting for transfers between devices: 23.9 us -> 20.9 us  [send(): return lax.ppermute(value, 'seq', moves(**step))]
  transfers between devices with their start and end apart: 27 -> 27, of which waited for: 16 -> 17; matrix products, arithmetic and copies ran while one was open for 0% -> 0% of each run, Pallas kernels for 19% -> 19%
where the time goes in v16:
time: 115 us; the launch traced here: 114 us
  starting transfers between devices  43.5 us (38%)
  waiting for transfers between devices  35.5 us (31%)
  Pallas kernels  34.2 us (30%)
    ppermute x20, starting transfers between devices, send(): return lax.ppermute(value, 'seq', moves(**step))  28.9 us
    ppermute x20, waiting for transfers between devices, send(): return lax.ppermute(value, 'seq', moves(**step))  20.9 us
    ppermute x6, waiting for transfers between devices, swap(): return lax.ppermute(value, 'head', [(0, 1), (1, 0)])  14.5 us
    ppermute x6, starting transfers between devices, swap(): return lax.ppermute(value, 'head', [(0, 1), (1, 0)])  13.9 us
    pallas_call x2, Pallas kernels, attend(): pl.pallas_call(functools.partial(attend_kernel, len(pieces), len(inverses...  8.36 us
    pallas_call x3, Pallas kernels, backward(): pl.pallas_call(functools.partial(backward_kernel, mine, [first for first,...  5.19 us
    pallas_call x1, Pallas kernels, load(): pl.pallas_call(load_kernel, in_specs=[VM, HBM, HBM], out_specs=[VM] * 3,...  3.29 us
    pallas_call x2, Pallas kernels, slopes(): pl.pallas_call(functools.partial(slope_kernel, first), in_specs=[VM] * (6...  3.27 us
  transfers between devices with their start and end apart: 27, of which 17 were waited for; matrix products, arithmetic and copies ran while one was open for 0% of the time, Pallas kernels for 19%

profile of v16, /device:TPU:0, one launch (start us, length us, event | category | flops | bytes accessed | tf_op | source)
XLA Modules:
  0.0 114.3 jit_solution(13617475986384555411)
XLA Ops:
  0.6 0.9 prepare.1
  1.5 0.1 collective-permute-start
  1.6 0.7 collective-permute-start.1
  2.3 0.0 copy-start.3
  2.3 3.3 %load.1 = (bf16[256,1536]{1,0:T(8,128)(2,1)S(1)}, bf16[256,1536]{1,0:T(8,128)(2,1)S(1)}, bf16[3,1536,768]{2,1,0:T(8,128)(2,1)S(1)}) custom-call(bf16[128,128]{1,0:T(8,128)(2,1)S(1)} %get-tuple-element.50.codes, bf16[256,1536]{1,0:T(8,128)(2,1)} %stems.1, bf16[3,1536,768]{2,1,0:T(8,128)(2,1)} %weights.1), custom_call_target="tpu_custom_call" | custom-call | flops 100000 | bytes 7077888 | tf_op jit(solution)/shard_map/load/pallas_call | solution.py:168
  5.6 0.0 collective-permute-done.1.far
  5.6 2.5 %encode.1.mine.encoded = bf16[272,768]{1,0:T(8,128)(2,1)S(1)} custom-call(bf16[8,1664]{1,0:T(8,128)(2,1)S(1)} %collective-permute-done.near, bf16[8,1664]{1,0:T(8,128)(2,1)S(1)} %collective-permute-done.1.far, bf16[256,1536]{1,0:T(8,128)(2,1)S(1)} %get-tuple-element.51.rows, bf16[256,1536]{1,0:T(8,128)(2,1)S(1)} %get-tuple-element.52.stem, ...), custom_call_target="tpu_custom_call" | custom-call | flops 1811939328 | bytes 14155776 | tf_op jit(solution)/shard_map/encode/pallas_call | solution.py:221
  8.2 3.4 %collective-permute-start.2 = (bf16[272,768]{1,0:T(8,128)(2,1)S(1)}, bf16[272,768]{1,0:T(8,128)(2,1)S(1)}, u32[]{:S(2)}, u32[]{:S(2)}) collective-permute-start(bf16[272,768]{1,0:T(8,128)(2,1)S(1)} %encode.1.mine.encoded), channel_id=1, source_target_pairs={{0,1},{1,0},{2,3},{3,2},{4,5},{5,4},{6,7},{7,6},{8,9},{9,8},{10,11... | collective-permute-start | bytes 1253384 | tf_op jit(solution)/shard_map/ppermute | solution.py:722
  11.5 3.0 %fetch.1.weight = bf16[3,1536,768]{2,1,0:T(8,128)(2,1)S(1)} custom-call(bf16[3,1536,768]{2,1,0:T(8,128)(2,1)} %source), custom_call_target="tpu_custom_call" | custom-call | flops 100000 | bytes 7077888 | tf_op jit(solution)/shard_map/fetch/pallas_call | solution.py:243
  14.6 6.2 %collective-permute-done.2.theirs = bf16[272,768]{1,0:T(8,128)(2,1)S(1)} collective-permute-done((bf16[272,768]{1,0:T(8,128)(2,1)S(1)}, bf16[272,768]{1,0:T(8,128)(2,1)S(1)}, u32[]{:S(2)}, u32[]{:S(2)}) %collective-permute-start.2) | collective-permute-done | bytes 417824 | tf_op jit(solution)/shard_map/ppermute | solution.py:722
  20.7 1.5 %project_keys.1 = (bf16[2,136,768]{2,1,0:T(8,128)(2,1)S(1)}, bf16[128,384]{1,0:T(8,128)(2,1)S(1)}, bf16[128,384]{1,0:T(8,128)(2,1)S(1)}, bf16[128,384]{1,0:T(8,128)(2,1)S(1)}, bf16[128,384]{1,0:T(8,128)(2,1)S(1)}) custom-call(bf16[272,768]{1,0:T(8,128)(2,1)S(1)} %encode.1.mine.encoded, bf16[272,768]{1,0:T(8,128)(2,1)S(1)} %collective-permute-done.2.theirs, ...), custom_call_target="tpu_custom_call" | custom-call | flops 641728512 | bytes 7077888 | tf_op jit(solution)/shard_map/project_keys/pallas_call | solution.py:296
  22.2 0.0 copy-start.2
  22.2 6.7 %collective-permute-start.3 = (bf16[128,384]{1,0:T(8,128)(2,1)S(1)}, bf16[128,384]{1,0:T(8,128)(2,1)S(1)}, u32[]{:S(2)}, u32[]{:S(2)}) collective-permute-start(bf16[128,384]{1,0:T(8,128)(2,1)S(1)} %get-tuple-element.59), channel_id=1, source_target_pairs={{0,64},{2,66},{4,68},{6,70},{8,72},{10,74},{12,76},{14,78},{16,80}... | collective-permute-start | bytes 294920 | tf_op jit(solution)/shard_map/ppermute | solution.py:726
  28.9 0.8 collective-permute-start.4
  29.7 2.4 %collective-permute-start.5 = (bf16[128,384]{1,0:T(8,128)(2,1)S(1)}, bf16[128,384]{1,0:T(8,128)(2,1)S(1)}, u32[]{:S(2)}, u32[]{:S(2)}) collective-permute-start(bf16[128,384]{1,0:T(8,128)(2,1)S(1)} %get-tuple-element.61), channel_id=1, source_target_pairs={{0,96},{2,98},{4,100},{6,102},{8,104},{10,106},{12,108},{14,110},{... | collective-permute-start | bytes 294920 | tf_op jit(solution)/shard_map/ppermute | solution.py:726
  32.2 2.6 %collective-permute-done.4 = bf16[128,384]{1,0:T(8,128)(2,1)S(1)} collective-permute-done((bf16[128,384]{1,0:T(8,128)(2,1)S(1)}, bf16[128,384]{1,0:T(8,128)(2,1)S(1)}, u32[]{:S(2)}, u32[]{:S(2)}) %collective-permute-start.4) | collective-permute-done | bytes 98336 | tf_op jit(solution)/shard_map/ppermute | solution.py:726
  34.9 2.0 %collective-permute-start.6 = (bf16[512,384]{1,0:T(8,128)(2,1)S(1)}, bf16[512,384]{1,0:T(8,128)(2,1)S(1)}, u32[]{:S(2)}, u32[]{:S(2)}) collective-permute-start(bf16[512,384]{1,0:T(8,128)(2,1)S(1)} %constant_dynamic-update-slice_fusion.refs_0_), channel_id=1, source_target_pairs={{0,8},{2,10},{4,12},{6,14},{8,16},{10,18},{12,20},{14,22},{16,24},... | collective-permute-start | bytes 1179656 | tf_op jit(solution)/shard_map/ppermute | solution.py:726
  36.8 2.2 %collective-permute-start.7 = (bf16[512,384]{1,0:T(8,128)(2,1)S(1)}, bf16[512,384]{1,0:T(8,128)(2,1)S(1)}, u32[]{:S(2)}, u32[]{:S(2)}) collective-permute-start(bf16[512,384]{1,0:T(8,128)(2,1)S(1)} %constant_dynamic-update-slice_fusion.refs_0_), channel_id=1, source_target_pairs={{0,24},{2,26},{4,28},{6,30},{8,0},{10,2},{12,4},{14,6},{16,8},{18,... | collective-permute-start | bytes 1179656 | tf_op jit(solution)/shard_map/ppermute | solution.py:726
  39.1 0.7 project_queries.1
  39.8 1.5 %collective-permute-start.8 = (bf16[136,256]{1,0:T(8,128)(2,1)S(1)}, bf16[136,256]{1,0:T(8,128)(2,1)S(1)}, u32[]{:S(2)}, u32[]{:S(2)}) collective-permute-start(bf16[136,256]{1,0:T(8,128)(2,1)S(1)} %get-tuple-element.66), channel_id=1, source_target_pairs={{0,64},{2,66},{4,68},{6,70},{8,72},{10,74},{12,76},{14,78},{16,80}... | collective-permute-start | bytes 208904 | tf_op jit(solution)/shard_map/ppermute | solution.py:726
  41.3 2.6 %collective-permute-start.9 = (bf16[136,256]{1,0:T(8,128)(2,1)S(1)}, bf16[136,256]{1,0:T(8,128)(2,1)S(1)}, u32[]{:S(2)}, u32[]{:S(2)}) collective-permute-start(bf16[136,256]{1,0:T(8,128)(2,1)S(1)} %get-tuple-element.67), channel_id=1, source_target_pairs={{0,32},{2,34},{4,36},{6,38},{8,40},{10,42},{12,44},{14,46},{16,48}... | collective-permute-start | bytes 208904 | tf_op jit(solution)/shard_map/ppermute | solution.py:726
  44.0 0.6 collective-permute-start.10
  44.6 1.1 collective-permute-done.8
  45.7 1.2 %collective-permute-done.9 = bf16[136,256]{1,0:T(8,128)(2,1)S(1)} collective-permute-done((bf16[136,256]{1,0:T(8,128)(2,1)S(1)}, bf16[136,256]{1,0:T(8,128)(2,1)S(1)}, u32[]{:S(2)}, u32[]{:S(2)}) %collective-permute-start.9) | collective-permute-done | bytes 69664 | tf_op jit(solution)/shard_map/ppermute | solution.py:726
  46.9 1.4 %collective-permute-done.10 = bf16[136,256]{1,0:T(8,128)(2,1)S(1)} collective-permute-done((bf16[136,256]{1,0:T(8,128)(2,1)S(1)}, bf16[136,256]{1,0:T(8,128)(2,1)S(1)}, u32[]{:S(2)}, u32[]{:S(2)}) %collective-permute-start.10) | collective-permute-done | bytes 69664 | tf_op jit(solution)/shard_map/ppermute | solution.py:726
  48.3 0.5 collective-permute-start.13
  48.8 0.3 collective-permute-start.16
  49.2 1.2 %collective-permute-start.14 = (bf16[256,384]{1,0:T(8,128)(2,1)S(1)}, bf16[256,384]{1,0:T(8,128)(2,1)S(1)}, u32[]{:S(2)}, u32[]{:S(2)}) collective-permute-start(bf16[256,384]{1,0:T(8,128)(2,1)S(1)} %slice.6), channel_id=1, source_target_pairs={{0,8},{2,10},{4,12},{6,14},{8,16},{10,18},{12,20},{14,22},{16,24},... | collective-permute-start | bytes 589832 | tf_op jit(solution)/shard_map/ppermute | solution.py:726
  50.5 2.1 %collective-permute-start.15 = (bf16[256,384]{1,0:T(8,128)(2,1)S(1)}, bf16[256,384]{1,0:T(8,128)(2,1)S(1)}, u32[]{:S(2)}, u32[]{:S(2)}) collective-permute-start(bf16[256,384]{1,0:T(8,128)(2,1)S(1)} %slice.7), channel_id=1, source_target_pairs={{0,24},{2,26},{4,28},{6,30},{8,0},{10,2},{12,4},{14,6},{16,8},{18,... | collective-permute-start | bytes 589832 | tf_op jit(solution)/shard_map/ppermute | solution.py:726
  52.5 0.9 norms.1.refs_8_
  53.5 3.7 %collective-permute-done.14 = bf16[256,384]{1,0:T(8,128)(2,1)S(1)} collective-permute-done((bf16[256,384]{1,0:T(8,128)(2,1)S(1)}, bf16[256,384]{1,0:T(8,128)(2,1)S(1)}, u32[]{:S(2)}, u32[]{:S(2)}) %collective-permute-start.14) | collective-permute-done | bytes 196640 | tf_op jit(solution)/shard_map/ppermute | solution.py:726
  57.2 0.4 collective-permute-done.16.queries
  57.6 0.3 collective-permute-start.17
  57.9 1.7 %collective-permute-done.17.refs_7_ = bf16[512,384]{1,0:T(8,128)(2,1)S(1)} collective-permute-done((bf16[512,384]{1,0:T(8,128)(2,1)S(1)}, bf16[512,384]{1,0:T(8,128)(2,1)S(1)}, u32[]{:S(2)}, u32[]{:S(2)}) %collective-permute-start.17) | collective-permute-done | bytes 393248 | tf_op jit(solution)/shard_map/ppermute | solution.py:726
  59.6 4.3 %attend.2 = (bf16[544,256]{1,0:T(8,128)(2,1)S(1)}, f32[8,1024]{1,0:T(8,128)S(1)}) custom-call(f32[1,4]{1,0:T(1,128)S(1)} %bitcast.4, bf16[544,256]{1,0:T(8,128)(2,1)S(1)} %collective-permute-done.16.queries, bf16[512,384]{1,0:T(8,128)(2,1)S(1)} %constant_dynamic-update-slice_fusion.refs_0_, bf16[512,384]{1,0:T(8,128)(2,1)S(1)} %collective-permute-done.6.refs_1_, ...), custom_call_target="tpu_custom_call" | custom-call | flops 2281701376 | bytes 4456448 | tf_op jit(solution)/shard_map/attend/pallas_call | solution.py:473
  63.9 1.4 %collective-permute-start.18 = (bf16[544,256]{1,0:T(8,128)(2,1)S(1)}, bf16[544,256]{1,0:T(8,128)(2,1)S(1)}, u32[]{:S(2)}, u32[]{:S(2)}) collective-permute-start(bf16[544,256]{1,0:T(8,128)(2,1)S(1)} %get-tuple-element.79), channel_id=1, source_target_pairs={{0,4},{2,6},{4,0},{6,2},{8,12},{10,14},{12,8},{14,10},{16,20},{18,... | collective-permute-start | bytes 835592 | tf_op jit(solution)/shard_map/ppermute | solution.py:726
  65.4 4.0 %attend.3.a0 = bf16[544,256]{1,0:T(8,128)(2,1)S(1)} custom-call(f32[1,4]{1,0:T(1,128)S(1)} %bitcast.5, bf16[544,256]{1,0:T(8,128)(2,1)S(1)} %constant_dynamic-update-slice_fusion.4.queries, bf16[512,384]{1,0:T(8,128)(2,1)S(1)} %constant_dynamic-update-slice_fusion.refs_0_, bf16[512,384]{1,0:T(8,128)(2,1)S(1)} %collective-permute-done.6.refs_1_, ...), custom_call_target="tpu_custom_call" | custom-call | flops 2281701376 | bytes 4456448 | tf_op jit(solution)/shard_map/attend/pallas_call | solution.py:473
  69.4 3.3 %collective-permute-done.18.a1 = bf16[544,256]{1,0:T(8,128)(2,1)S(1)} collective-permute-done((bf16[544,256]{1,0:T(8,128)(2,1)S(1)}, bf16[544,256]{1,0:T(8,128)(2,1)S(1)}, u32[]{:S(2)}, u32[]{:S(2)}) %collective-permute-start.18) | collective-permute-done | bytes 278560 | tf_op jit(solution)/shard_map/ppermute | solution.py:726
  72.7 0.5 merge.1
  73.3 1.2 %collective-permute-start.19 = (bf16[136,256]{1,0:T(8,128)(2,1)S(1)}, bf16[136,256]{1,0:T(8,128)(2,1)S(1)}, u32[]{:S(2)}, u32[]{:S(2)}) collective-permute-start(bf16[136,256]{1,0:T(8,128)(2,1)S(1)} %get-tuple-element.81), channel_id=1, source_target_pairs={{0,64},{2,66},{4,68},{6,70},{8,72},{10,74},{12,76},{14,78},{16,80}... | collective-permute-start | bytes 208904 | tf_op jit(solution)/shard_map/ppermute | solution.py:726
  74.5 2.8 %collective-permute-start.20 = (bf16[136,256]{1,0:T(8,128)(2,1)S(1)}, bf16[136,256]{1,0:T(8,128)(2,1)S(1)}, u32[]{:S(2)}, u32[]{:S(2)}) collective-permute-start(bf16[136,256]{1,0:T(8,128)(2,1)S(1)} %get-tuple-element.82), channel_id=1, source_target_pairs={{0,96},{2,98},{4,100},{6,102},{8,104},{10,106},{12,108},{14,110},{... | collective-permute-start | bytes 208904 | tf_op jit(solution)/shard_map/ppermute | solution.py:726
  77.3 2.3 %collective-permute-done.19.a1 = bf16[136,256]{1,0:T(8,128)(2,1)S(1)} collective-permute-done((bf16[136,256]{1,0:T(8,128)(2,1)S(1)}, bf16[136,256]{1,0:T(8,128)(2,1)S(1)}, u32[]{:S(2)}, u32[]{:S(2)}) %collective-permute-start.19) | collective-permute-done | bytes 69664 | tf_op jit(solution)/shard_map/ppermute | solution.py:726
  79.6 0.5 collective-permute-done.20.a2
  80.1 2.8 %collective-permute-done.21.a3 = bf16[136,256]{1,0:T(8,128)(2,1)S(1)} collective-permute-done((bf16[136,256]{1,0:T(8,128)(2,1)S(1)}, bf16[136,256]{1,0:T(8,128)(2,1)S(1)}, u32[]{:S(2)}, u32[]{:S(2)}) %collective-permute-start.21) | collective-permute-done | bytes 69664 | tf_op jit(solution)/shard_map/ppermute | solution.py:726
  82.9 0.4 output.3
  83.3 3.3 %collective-permute-start.22 = (bf16[136,768]{1,0:T(8,128)(2,1)S(1)}, bf16[136,768]{1,0:T(8,128)(2,1)S(1)}, u32[]{:S(2)}, u32[]{:S(2)}) collective-permute-start(bf16[136,768]{1,0:T(8,128)(2,1)S(1)} %output.3), channel_id=1, source_target_pairs={{0,1},{1,0},{2,3},{3,2},{4,5},{5,4},{6,7},{7,6},{8,9},{9,8},{10,11... | collective-permute-start | bytes 626696 | tf_op jit(solution)/shard_map/ppermute | solution.py:722
  86.5 0.4 output.2.own
  86.9 3.7 %collective-permute-done.22.other = bf16[136,768]{1,0:T(8,128)(2,1)S(1)} collective-permute-done((bf16[136,768]{1,0:T(8,128)(2,1)S(1)}, bf16[136,768]{1,0:T(8,128)(2,1)S(1)}, u32[]{:S(2)}, u32[]{:S(2)}) %collective-permute-start.22) | collective-permute-done | bytes 208928 | tf_op jit(solution)/shard_map/ppermute | solution.py:722
  90.6 0.9 decode_first.1
  91.6 3.5 %collective-permute-start.24 = (bf16[272,512]{1,0:T(8,128)(2,1)S(1)}, bf16[272,512]{1,0:T(8,128)(2,1)S(1)}, u32[]{:S(2)}, u32[]{:S(2)}) collective-permute-start(bf16[272,512]{1,0:T(8,128)(2,1)S(1)} %get-tuple-element.87), channel_id=1, source_target_pairs={{0,1},{1,0},{2,3},{3,2},{4,5},{5,4},{6,7},{7,6},{8,9},{9,8},{10,11... | collective-permute-start | bytes 835592 | tf_op jit(solution)/shard_map/ppermute | solution.py:722
  95.0 1.2 %decode.2 = bf16[272,256]{1,0:T(8,128)(2,1)} custom-call(bf16[272,768]{1,0:T(8,128)(2,1)S(1)} %get-tuple-element.85.inputs, bf16[3,768,1536]{2,1,0:T(8,128)(2,1)S(1)} %bitcast.3), custom_call_target="tpu_custom_call" | custom-call | flops 1000000 | bytes 10000 | tf_op jit(solution)/shard_map/decode/pallas_call | solution.py:589
  96.2 0.3 collective-permute-start.23
  96.5 1.2 %decode.3.own = f32[272,768]{1,0:T(8,128)S(1)} custom-call(bf16[272,768]{1,0:T(8,128)(2,1)S(1)} %get-tuple-element.85.inputs, bf16[3,768,1536]{2,1,0:T(8,128)(2,1)S(1)} %bitcast.3), custom_call_target="tpu_custom_call" | custom-call | flops 1000000 | bytes 10000 | tf_op jit(solution)/shard_map/decode/pallas_call | solution.py:589
  97.7 3.7 %collective-permute-done.24.other = bf16[272,512]{1,0:T(8,128)(2,1)S(1)} collective-permute-done((bf16[272,512]{1,0:T(8,128)(2,1)S(1)}, bf16[272,512]{1,0:T(8,128)(2,1)S(1)}, u32[]{:S(2)}, u32[]{:S(2)}) %collective-permute-start.24) | collective-permute-done | bytes 278560 | tf_op jit(solution)/shard_map/ppermute | solution.py:722
  101.4 1.3 %slopes.2 = (bf16[256,512]{1,0:T(8,128)(2,1)S(1)}, bf16[272,512]{1,0:T(8,128)(2,1)}, f32[128,512]{1,0:T(8,128)S(1)}) custom-call(f32[272,768]{1,0:T(8,128)S(1)} %decode.3.own, bf16[272,512]{1,0:T(8,128)(2,1)S(1)} %collective-permute-done.24.other, bf16[272,768]{1,0:T(8,128)(2,1)S(1)} %get-tuple-element.85.inputs, bf16[256,1536]{1,0:T(8,128)(2,1)S(1)} %copy-done.1, ...), custom_call_target="tpu_custom_call" | custom-call | flops 417792000000 | bytes 1949696 | tf_op jit(solution)/shard_map/slopes/pallas_call | solution.py:639
  102.7 1.7 %collective-permute-start.26 = (bf16[272,512]{1,0:T(8,128)(2,1)}, bf16[272,512]{1,0:T(8,128)(2,1)}, u32[]{:S(2)}, u32[]{:S(2)}) collective-permute-start(bf16[272,512]{1,0:T(8,128)(2,1)} %get-tuple-element.91.refs_0_), channel_id=1, source_target_pairs={{0,1},{1,0},{2,3},{3,2},{4,5},{5,4},{6,7},{7,6},{8,9},{9,8},{10,11... | collective-permute-start | bytes 835592 | tf_op jit(solution)/shard_map/ppermute | solution.py:722
  104.5 0.1 collective-permute-done.23.other
  104.6 1.9 %slopes.3 = (bf16[256,768]{1,0:T(8,128)(2,1)}, bf16[272,256]{1,0:T(8,128)(2,1)S(1)}, f32[128,256]{1,0:T(8,128)S(1)}) custom-call(f32[272,768]{1,0:T(8,128)S(1)} %decode.3.own, bf16[272,256]{1,0:T(8,128)(2,1)} %collective-permute-done.23.other, bf16[272,768]{1,0:T(8,128)(2,1)S(1)} %get-tuple-element.85.inputs, bf16[256,1536]{1,0:T(8,128)(2,1)S(1)} %copy-done.1, ...), custom_call_target="tpu_custom_call" | custom-call | flops 208896000000 | bytes 974848 | tf_op jit(solution)/shard_map/slopes/pallas_call | solution.py:639
  106.5 1.7 %collective-permute-start.25 = (bf16[272,256]{1,0:T(8,128)(2,1)S(1)}, bf16[272,256]{1,0:T(8,128)(2,1)S(1)}, u32[]{:S(2)}, u32[]{:S(2)}) collective-permute-start(bf16[272,256]{1,0:T(8,128)(2,1)S(1)} %get-tuple-element.90.refs_1_), channel_id=1, source_target_pairs={{0,1},{1,0},{2,3},{3,2},{4,5},{5,4},{6,7},{7,6},{8,9},{9,8},{10,11... | collective-permute-start | bytes 417800 | tf_op jit(solution)/shard_map/ppermute | solution.py:722
  108.2 2.2 %backward.3.refs_1_ = f32[128,768]{1,0:T(8,128)S(1)} custom-call(bf16[272,512]{1,0:T(8,128)(2,1)} %get-tuple-element.91.refs_0_, bf16[272,256]{1,0:T(8,128)(2,1)S(1)} %get-tuple-element.90.refs_1_, f32[128,512]{1,0:T(8,128)S(1)} %get-tuple-element.92.refs_2_, f32[128,256]{1,0:T(8,128)S(1)} %get-tuple-element.93.refs_3_, bf16[3,768,1536]{2,1,0:T(8,128)(2,1)S(1)} %bitcast.3), custom_call_target="tpu_custom_call" | custom-call | flops 962592768 | bytes 1253376 | tf_op jit(solution)/shard_map/backward/pallas_call | solution.py:698
  110.4 0.7 collective-permute-done.26.refs_0_
  111.1 1.8 %backward.4.refs_1_ = f32[128,768]{1,0:T(8,128)S(1)} custom-call(bf16[272,512]{1,0:T(8,128)(2,1)} %collective-permute-done.26.refs_0_, f32[128,768]{1,0:T(8,128)S(1)} %backward.3.refs_1_, bf16[3,768,1536]{2,1,0:T(8,128)(2,1)S(1)} %bitcast.3), custom_call_target="tpu_custom_call" | custom-call | flops 641728512 | bytes 835584 | tf_op jit(solution)/shard_map/backward/pallas_call | solution.py:698
  112.9 0.1 collective-permute-done.25.refs_0_
  113.1 1.2 %backward.5 = bf16[128,768]{1,0:T(8,128)(2,1)} custom-call(bf16[272,256]{1,0:T(8,128)(2,1)S(1)} %collective-permute-done.25.refs_0_, f32[128,768]{1,0:T(8,128)S(1)} %backward.4.refs_1_, bf16[3,768,1536]{2,1,0:T(8,128)(2,1)S(1)} %bitcast.3), custom_call_target="tpu_custom_call" | custom-call | flops 320864256 | bytes 417792 | tf_op jit(solution)/shard_map/backward/pallas_call | solution.py:698
  (36 shorter events, 0.2 us)
Async XLA Ops:
  1.5 4.1 %collective-permute-start = (bf16[8,1664]{1,0:T(8,128)(2,1)S(1)}, bf16[8,1664]{1,0:T(8,128)(2,1)S(1)}, u32[]{:S(2)}, u32[]{:S(2)}) collective-permute-start(bf16[8,1664]{1,0:T(8,128)(2,1)S(1)} %get-tuple-element.48), channel_id=1, source_target_pairs={{0,2},{2,0},{4,6},{6,4},{8,10},{10,8},{12,14},{14,12},{16,18},{18,... | collective-permute-start | bytes 79880 | tf_op jit(solution)/shard_map/ppermute | solution.py:726
  1.6 4.0 %collective-permute-start.1 = (bf16[8,1664]{1,0:T(8,128)(2,1)S(1)}, bf16[8,1664]{1,0:T(8,128)(2,1)S(1)}, u32[]{:S(2)}, u32[]{:S(2)}) collective-permute-start(bf16[8,1664]{1,0:T(8,128)(2,1)S(1)} %get-tuple-element.49), channel_id=1, source_target_pairs={{2,4},{6,8},{10,12},{14,16},{18,20},{22,24},{26,28},{30,32},{34,36... | collective-permute-start | bytes 79880 | tf_op jit(solution)/shard_map/ppermute | solution.py:747
  2.3 9.2 %copy-start.3 = (f32[1536]{0:T(1024)S(1)}, f32[1536]{0:T(1024)}, u32[]{:S(2)}) copy-start(f32[1536]{0:T(1024)} %param.12) | copy-start | bytes 18436
  8.2 12.6 %collective-permute-start.2 = (bf16[272,768]{1,0:T(8,128)(2,1)S(1)}, bf16[272,768]{1,0:T(8,128)(2,1)S(1)}, u32[]{:S(2)}, u32[]{:S(2)}) collective-permute-start(bf16[272,768]{1,0:T(8,128)(2,1)S(1)} %encode.1.mine.encoded), channel_id=1, source_target_pairs={{0,1},{1,0},{2,3},{3,2},{4,5},{5,4},{6,7},{7,6},{8,9},{9,8},{10,11... | collective-permute-start | bytes 1253384 | tf_op jit(solution)/shard_map/ppermute | solution.py:722
  22.2 37.4 %copy-start.2 = (f32[4]{0:T(128)S(1)}, f32[4]{0:T(128)}, u32[]{:S(2)}) copy-start(f32[4]{0:T(128)} %param.14) | copy-start | bytes 52
  22.2 9.9 %collective-permute-start.3 = (bf16[128,384]{1,0:T(8,128)(2,1)S(1)}, bf16[128,384]{1,0:T(8,128)(2,1)S(1)}, u32[]{:S(2)}, u32[]{:S(2)}) collective-permute-start(bf16[128,384]{1,0:T(8,128)(2,1)S(1)} %get-tuple-element.59), channel_id=1, source_target_pairs={{0,64},{2,66},{4,68},{6,70},{8,72},{10,74},{12,76},{14,78},{16,80}... | collective-permute-start | bytes 294920 | tf_op jit(solution)/shard_map/ppermute | solution.py:726
  28.9 5.8 %collective-permute-start.4 = (bf16[128,384]{1,0:T(8,128)(2,1)S(1)}, bf16[128,384]{1,0:T(8,128)(2,1)S(1)}, u32[]{:S(2)}, u32[]{:S(2)}) collective-permute-start(bf16[128,384]{1,0:T(8,128)(2,1)S(1)} %get-tuple-element.60), channel_id=1, source_target_pairs={{0,32},{2,34},{4,36},{6,38},{8,40},{10,42},{12,44},{14,46},{16,48}... | collective-permute-start | bytes 294920 | tf_op jit(solution)/shard_map/ppermute | solution.py:726
  29.7 5.0 %collective-permute-start.5 = (bf16[128,384]{1,0:T(8,128)(2,1)S(1)}, bf16[128,384]{1,0:T(8,128)(2,1)S(1)}, u32[]{:S(2)}, u32[]{:S(2)}) collective-permute-start(bf16[128,384]{1,0:T(8,128)(2,1)S(1)} %get-tuple-element.61), channel_id=1, source_target_pairs={{0,96},{2,98},{4,100},{6,102},{8,104},{10,106},{12,108},{14,110},{... | collective-permute-start | bytes 294920 | tf_op jit(solution)/shard_map/ppermute | solution.py:726
  34.9 13.4 %collective-permute-start.6 = (bf16[512,384]{1,0:T(8,128)(2,1)S(1)}, bf16[512,384]{1,0:T(8,128)(2,1)S(1)}, u32[]{:S(2)}, u32[]{:S(2)}) collective-permute-start(bf16[512,384]{1,0:T(8,128)(2,1)S(1)} %constant_dynamic-update-slice_fusion.refs_0_), channel_id=1, source_target_pairs={{0,8},{2,10},{4,12},{6,14},{8,16},{10,18},{12,20},{14,22},{16,24},... | collective-permute-start | bytes 1179656 | tf_op jit(solution)/shard_map/ppermute | solution.py:726
  36.8 11.4 %collective-permute-start.7 = (bf16[512,384]{1,0:T(8,128)(2,1)S(1)}, bf16[512,384]{1,0:T(8,128)(2,1)S(1)}, u32[]{:S(2)}, u32[]{:S(2)}) collective-permute-start(bf16[512,384]{1,0:T(8,128)(2,1)S(1)} %constant_dynamic-update-slice_fusion.refs_0_), channel_id=1, source_target_pairs={{0,24},{2,26},{4,28},{6,30},{8,0},{10,2},{12,4},{14,6},{16,8},{18,... | collective-permute-start | bytes 1179656 | tf_op jit(solution)/shard_map/ppermute | solution.py:726
  39.8 5.9 %collective-permute-start.8 = (bf16[136,256]{1,0:T(8,128)(2,1)S(1)}, bf16[136,256]{1,0:T(8,128)(2,1)S(1)}, u32[]{:S(2)}, u32[]{:S(2)}) collective-permute-start(bf16[136,256]{1,0:T(8,128)(2,1)S(1)} %get-tuple-element.66), channel_id=1, source_target_pairs={{0,64},{2,66},{4,68},{6,70},{8,72},{10,74},{12,76},{14,78},{16,80}... | collective-permute-start | bytes 208904 | tf_op jit(solution)/shard_map/ppermute | solution.py:726
  41.3 5.5 %collective-permute-start.9 = (bf16[136,256]{1,0:T(8,128)(2,1)S(1)}, bf16[136,256]{1,0:T(8,128)(2,1)S(1)}, u32[]{:S(2)}, u32[]{:S(2)}) collective-permute-start(bf16[136,256]{1,0:T(8,128)(2,1)S(1)} %get-tuple-element.67), channel_id=1, source_target_pairs={{0,32},{2,34},{4,36},{6,38},{8,40},{10,42},{12,44},{14,46},{16,48}... | collective-permute-start | bytes 208904 | tf_op jit(solution)/shard_map/ppermute | solution.py:726
  44.0 4.3 %collective-permute-start.10 = (bf16[136,256]{1,0:T(8,128)(2,1)S(1)}, bf16[136,256]{1,0:T(8,128)(2,1)S(1)}, u32[]{:S(2)}, u32[]{:S(2)}) collective-permute-start(bf16[136,256]{1,0:T(8,128)(2,1)S(1)} %get-tuple-element.68), channel_id=1, source_target_pairs={{0,96},{2,98},{4,100},{6,102},{8,104},{10,106},{12,108},{14,110},{... | collective-permute-start | bytes 208904 | tf_op jit(solution)/shard_map/ppermute | solution.py:726
  45.7 4.8 %collective-permute-start.11 = (bf16[512,384]{1,0:T(8,128)(2,1)S(1)}, bf16[512,384]{1,0:T(8,128)(2,1)S(1)}, u32[]{:S(2)}, u32[]{:S(2)}) collective-permute-start(bf16[512,384]{1,0:T(8,128)(2,1)S(1)} %constant_dynamic-update-slice_fusion.refs_0_), channel_id=1, source_target_pairs={{0,2},{2,0},{4,6},{6,4},{8,10},{10,8},{12,14},{14,12},{16,18},{18,... | collective-permute-start | bytes 1179656 | tf_op jit(solution)/shard_map/ppermute | solution.py:726
  48.3 4.3 %collective-permute-start.12 = (bf16[512,384]{1,0:T(8,128)(2,1)S(1)}, bf16[512,384]{1,0:T(8,128)(2,1)S(1)}, u32[]{:S(2)}, u32[]{:S(2)}) collective-permute-start(bf16[512,384]{1,0:T(8,128)(2,1)S(1)} %collective-permute-done.6.refs_1_), channel_id=1, source_target_pairs={{0,2},{2,0},{4,6},{6,4},{8,10},{10,8},{12,14},{14,12},{16,18},{18,... | collective-permute-start | bytes 1179656 | tf_op jit(solution)/shard_map/ppermute | solution.py:726
  48.3 4.2 %collective-permute-start.13 = (bf16[512,384]{1,0:T(8,128)(2,1)S(1)}, bf16[512,384]{1,0:T(8,128)(2,1)S(1)}, u32[]{:S(2)}, u32[]{:S(2)}) collective-permute-start(bf16[512,384]{1,0:T(8,128)(2,1)S(1)} %collective-permute-done.7.refs_2_), channel_id=1, source_target_pairs={{0,2},{2,0},{4,6},{6,4},{8,10},{10,8},{12,14},{14,12},{16,18},{18,... | collective-permute-start | bytes 1179656 | tf_op jit(solution)/shard_map/ppermute | solution.py:726
  48.8 8.7 %collective-permute-start.16 = (bf16[544,256]{1,0:T(8,128)(2,1)S(1)}, bf16[544,256]{1,0:T(8,128)(2,1)S(1)}, u32[]{:S(2)}, u32[]{:S(2)}) collective-permute-start(bf16[544,256]{1,0:T(8,128)(2,1)S(1)} %constant_dynamic-update-slice_fusion.4.queries), channel_id=1, source_target_pairs={{0,4},{2,6},{4,0},{6,2},{8,12},{10,14},{12,8},{14,10},{16,20},{18,... | collective-permute-start | bytes 835592 | tf_op jit(solution)/shard_map/ppermute | solution.py:726
  49.2 7.9 %collective-permute-start.14 = (bf16[256,384]{1,0:T(8,128)(2,1)S(1)}, bf16[256,384]{1,0:T(8,128)(2,1)S(1)}, u32[]{:S(2)}, u32[]{:S(2)}) collective-permute-start(bf16[256,384]{1,0:T(8,128)(2,1)S(1)} %slice.6), channel_id=1, source_target_pairs={{0,8},{2,10},{4,12},{6,14},{8,16},{10,18},{12,20},{14,22},{16,24},... | collective-permute-start | bytes 589832 | tf_op jit(solution)/shard_map/ppermute | solution.py:726
  50.5 6.7 %collective-permute-start.15 = (bf16[256,384]{1,0:T(8,128)(2,1)S(1)}, bf16[256,384]{1,0:T(8,128)(2,1)S(1)}, u32[]{:S(2)}, u32[]{:S(2)}) collective-permute-start(bf16[256,384]{1,0:T(8,128)(2,1)S(1)} %slice.7), channel_id=1, source_target_pairs={{0,24},{2,26},{4,28},{6,30},{8,0},{10,2},{12,4},{14,6},{16,8},{18,... | collective-permute-start | bytes 589832 | tf_op jit(solution)/shard_map/ppermute | solution.py:726
  57.6 2.0 %collective-permute-start.17 = (bf16[512,384]{1,0:T(8,128)(2,1)S(1)}, bf16[512,384]{1,0:T(8,128)(2,1)S(1)}, u32[]{:S(2)}, u32[]{:S(2)}) collective-permute-start(bf16[512,384]{1,0:T(8,128)(2,1)S(1)} %constant_dynamic-update-slice_fusion.8.refs_6_), channel_id=1, source_target_pairs={{0,2},{2,0},{4,6},{6,4},{8,10},{10,8},{12,14},{14,12},{16,18},{18,... | collective-permute-start | bytes 1179656 | tf_op jit(solution)/shard_map/ppermute | solution.py:726
  59.6 23.2 %copy-start = (bf16[768,1536]{1,0:T(8,128)(2,1)S(1)}, bf16[768,1536]{1,0:T(8,128)(2,1)}, u32[]{:S(2)}) copy-start(bf16[768,1536]{1,0:T(8,128)(2,1)} %weight.6) | copy-start | bytes 7077892
  63.9 8.8 %collective-permute-start.18 = (bf16[544,256]{1,0:T(8,128)(2,1)S(1)}, bf16[544,256]{1,0:T(8,128)(2,1)S(1)}, u32[]{:S(2)}, u32[]{:S(2)}) collective-permute-start(bf16[544,256]{1,0:T(8,128)(2,1)S(1)} %get-tuple-element.79), channel_id=1, source_target_pairs={{0,4},{2,6},{4,0},{6,2},{8,12},{10,14},{12,8},{14,10},{16,20},{18,... | collective-permute-start | bytes 835592 | tf_op jit(solution)/shard_map/ppermute | solution.py:726
  65.4 25.3 %slice-start = ((s8[7077888]{0:T(1024)(128)(4,1)}), s8[4194304]{0:T(1024)(128)(4,1)S(1)}, s32[]{:S(2)}) async-start(s8[7077888]{0:T(1024)(128)(4,1)} %bitcast.2), calls=%async_computation | async-start | bytes 8388608
  65.4 25.3 %slice-start.1 = ((s8[7077888]{0:T(1024)(128)(4,1)}), s8[2883584]{0:T(1024)(128)(4,1)S(1)}, s32[]{:S(2)}) async-start(s8[7077888]{0:T(1024)(128)(4,1)} %bitcast.2), calls=%async_computation.1 | async-start | bytes 5767168
  73.3 6.3 %collective-permute-start.19 = (bf16[136,256]{1,0:T(8,128)(2,1)S(1)}, bf16[136,256]{1,0:T(8,128)(2,1)S(1)}, u32[]{:S(2)}, u32[]{:S(2)}) collective-permute-start(bf16[136,256]{1,0:T(8,128)(2,1)S(1)} %get-tuple-element.81), channel_id=1, source_target_pairs={{0,64},{2,66},{4,68},{6,70},{8,72},{10,74},{12,76},{14,78},{16,80}... | collective-permute-start | bytes 208904 | tf_op jit(solution)/shard_map/ppermute | solution.py:726
  74.5 5.6 %collective-permute-start.20 = (bf16[136,256]{1,0:T(8,128)(2,1)S(1)}, bf16[136,256]{1,0:T(8,128)(2,1)S(1)}, u32[]{:S(2)}, u32[]{:S(2)}) collective-permute-start(bf16[136,256]{1,0:T(8,128)(2,1)S(1)} %get-tuple-element.82), channel_id=1, source_target_pairs={{0,96},{2,98},{4,100},{6,102},{8,104},{10,106},{12,108},{14,110},{... | collective-permute-start | bytes 208904 | tf_op jit(solution)/shard_map/ppermute | solution.py:726
  77.3 5.5 %collective-permute-start.21 = (bf16[136,256]{1,0:T(8,128)(2,1)S(1)}, bf16[136,256]{1,0:T(8,128)(2,1)S(1)}, u32[]{:S(2)}, u32[]{:S(2)}) collective-permute-start(bf16[136,256]{1,0:T(8,128)(2,1)S(1)} %get-tuple-element.83), channel_id=1, source_target_pairs={{0,32},{2,34},{4,36},{6,38},{8,40},{10,42},{12,44},{14,46},{16,48}... | collective-permute-start | bytes 208904 | tf_op jit(solution)/shard_map/ppermute | solution.py:726
  83.3 7.4 %collective-permute-start.22 = (bf16[136,768]{1,0:T(8,128)(2,1)S(1)}, bf16[136,768]{1,0:T(8,128)(2,1)S(1)}, u32[]{:S(2)}, u32[]{:S(2)}) collective-permute-start(bf16[136,768]{1,0:T(8,128)(2,1)S(1)} %output.3), channel_id=1, source_target_pairs={{0,1},{1,0},{2,3},{3,2},{4,5},{5,4},{6,7},{7,6},{8,9},{9,8},{10,11... | collective-permute-start | bytes 626696 | tf_op jit(solution)/shard_map/ppermute | solution.py:722
  91.6 9.8 %collective-permute-start.24 = (bf16[272,512]{1,0:T(8,128)(2,1)S(1)}, bf16[272,512]{1,0:T(8,128)(2,1)S(1)}, u32[]{:S(2)}, u32[]{:S(2)}) collective-permute-start(bf16[272,512]{1,0:T(8,128)(2,1)S(1)} %get-tuple-element.87), channel_id=1, source_target_pairs={{0,1},{1,0},{2,3},{3,2},{4,5},{5,4},{6,7},{7,6},{8,9},{9,8},{10,11... | collective-permute-start | bytes 835592 | tf_op jit(solution)/shard_map/ppermute | solution.py:722
  95.0 6.3 %copy-start.1 = (bf16[256,1536]{1,0:T(8,128)(2,1)S(1)}, bf16[256,1536]{1,0:T(8,128)(2,1)}, u32[]{:S(2)}) copy-start(bf16[256,1536]{1,0:T(8,128)(2,1)} %grad.5) | copy-start | bytes 2359300
  96.2 8.4 %collective-permute-start.23 = (bf16[272,256]{1,0:T(8,128)(2,1)}, bf16[272,256]{1,0:T(8,128)(2,1)}, u32[]{:S(2)}, u32[]{:S(2)}) collective-permute-start(bf16[272,256]{1,0:T(8,128)(2,1)} %decode.2), channel_id=1, source_target_pairs={{0,1},{1,0},{2,3},{3,2},{4,5},{5,4},{6,7},{7,6},{8,9},{9,8},{10,11... | collective-permute-start | bytes 417800 | tf_op jit(solution)/shard_map/ppermute | solution.py:722
  102.7 8.4 %collective-permute-start.26 = (bf16[272,512]{1,0:T(8,128)(2,1)}, bf16[272,512]{1,0:T(8,128)(2,1)}, u32[]{:S(2)}, u32[]{:S(2)}) collective-permute-start(bf16[272,512]{1,0:T(8,128)(2,1)} %get-tuple-element.91.refs_0_), channel_id=1, source_target_pairs={{0,1},{1,0},{2,3},{3,2},{4,5},{5,4},{6,7},{7,6},{8,9},{9,8},{10,11... | collective-permute-start | bytes 835592 | tf_op jit(solution)/shard_map/ppermute | solution.py:722
  106.5 6.6 %collective-permute-start.25 = (bf16[272,256]{1,0:T(8,128)(2,1)S(1)}, bf16[272,256]{1,0:T(8,128)(2,1)S(1)}, u32[]{:S(2)}, u32[]{:S(2)}) collective-permute-start(bf16[272,256]{1,0:T(8,128)(2,1)S(1)} %get-tuple-element.90.refs_1_), channel_id=1, source_target_pairs={{0,1},{1,0},{2,3},{3,2},{4,5},{5,4},{6,7},{7,6},{8,9},{9,8},{10,11... | collective-permute-start | bytes 417800 | tf_op jit(solution)/shard_map/ppermute | solution.py:722
